TPU v7x, 32 devices: a whole 2x2x4 slice. The times are simulated.
32 devices in a mesh: dp: 8 (over z, core), seq: 4 (over y, x).
Axes of the slice: x: 2, y: 2, z: 4, core: 2. Of those that a mesh axis runs over, the one named last changes fastest.
Arguments:
- inputs: bfloat16 [8, 1024, 4096], P('dp', 'seq'), may hold values from -10 to 10
- weights: bfloat16 [4096, 768], P('dp'), may hold values from -0.09375 to 0.09375
- cotangent: bfloat16 [8, 1024, 512], P('dp', 'seq'), may hold values from -6 to 6
- doc_lengths: int32 [8, 8], P('dp'), may hold values from 1 to 512, 1024 in all within a row
- kept_flags: int32 [8, 8], P('dp'), may hold values 0 or 1
Outputs:
- attention: bfloat16 [8, 1024, 512], P('dp', 'seq')
- inputs_grad: bfloat16 [8, 1024, 4096], P('dp', 'seq')
- weights_grad: float32 [4096, 768], P(('dp', 'seq'))
All inputs are finite; a program needn't handle non-finite values. No bound on the sum of `kept_flags` on one device may be relied on, other than what follows from the above.
Results may differ from a plain program's by a relative error of at most 0.013.
Values may be sent and summed in bfloat16 or wider, within the bound.
No kernel may reach another device: no remote copies, remote signals or barrier semaphores. Data moves between devices by JAX's collectives and lax.ppermute only.
A program may use at most 128 MiB of HBM per device.

v0:
```python
import math

import jax
import jax.numpy as jnp
from jax import lax
from jax.sharding import PartitionSpec as P

HEAD_DIM = 128


def doc_tables(doc_row, flag_row, positions):
    doc_ends = jnp.cumsum(doc_row)
    doc_starts = doc_ends - doc_row
    inside = (positions[:, None] >= doc_starts[None, :]) & (positions[:, None] < doc_ends[None, :])
    start_of = jnp.sum(jnp.where(inside, doc_starts[None, :], 0), axis=1)
    keep_of = jnp.sum(jnp.where(inside, flag_row[None, :], 0), axis=1)
    return (start_of, keep_of)


def attend(query_rows, cot_rows, positions, start_of, keys, values):
    row_count, head_dim = query_rows.shape
    key_count = keys.shape[0]
    row_block = min(512, row_count)
    key_block = min(512, key_count)
    block_count = row_count // row_block
    softmax_scale = 1.0 / math.sqrt(head_dim)

    def scores(block_index, query_tile, pos_tile, start_tile):
        key_start = block_index * key_block
        key_tile = lax.dynamic_slice_in_dim(keys, key_start, key_block, 0)
        value_tile = lax.dynamic_slice_in_dim(values, key_start, key_block, 0)
        key_positions = key_start + lax.iota(jnp.int32, key_block)
        allowed = (key_positions[None, :] >= start_tile[:, None]) & (
            key_positions[None, :] <= pos_tile[:, None]
        )
        logits = (
            lax.dot_general(
                query_tile, key_tile, (((1,), (1,)), ((), ())), preferred_element_type=jnp.float32
            )
            * softmax_scale
        )
        return (key_tile, value_tile, allowed, logits)

    def one_block(carried, tiles_in):
        key_grads, value_grads = carried
        query_tile, cot_tile, pos_tile, start_tile = tiles_in
        key_first = 0
        key_last = key_count // key_block

        def statistics(block_index, running):
            running_max, row_mass = running
            _, _, allowed, logits = scores(block_index, query_tile, pos_tile, start_tile)
            masked = jnp.where(allowed, logits, -1e30)
            new_max = jnp.maximum(running_max, jnp.max(masked, axis=1))
            row_mass = row_mass * jnp.exp(running_max - new_max) + jnp.sum(
                jnp.where(allowed, jnp.exp(masked - new_max[:, None]), 0.0), axis=1
            )
            return (new_max, row_mass)

        start_state = (
            jnp.full((row_block,), -1e30, jnp.float32),
            jnp.zeros((row_block,), jnp.float32),
        )
        running_max, row_mass = lax.fori_loop(key_first, key_last, statistics, start_state)
        log_norm = running_max + jnp.log(row_mass)

        def forward(block_index, accumulated):
            _, value_tile, allowed, logits = scores(block_index, query_tile, pos_tile, start_tile)
            weights_half = jnp.where(allowed, jnp.exp(logits - log_norm[:, None]), 0.0).astype(
                jnp.bfloat16
            )
            return accumulated + jnp.dot(
                weights_half, value_tile, preferred_element_type=jnp.float32
            )

        accumulated = lax.fori_loop(
            key_first, key_last, forward, jnp.zeros((row_block, head_dim), jnp.float32)
        )
        out_tile = accumulated.astype(jnp.bfloat16)
        row_delta = jnp.sum(cot_tile.astype(jnp.float32) * out_tile.astype(jnp.float32), axis=1)

        def backward(block_index, running):
            grad_query, grad_keys, grad_values = running
            key_tile, value_tile, allowed, logits = scores(
                block_index, query_tile, pos_tile, start_tile
            )
            attn_weights = jnp.where(allowed, jnp.exp(logits - log_norm[:, None]), 0.0)
            weights_half = attn_weights.astype(jnp.bfloat16)
            weight_grads = lax.dot_general(
                cot_tile, value_tile, (((1,), (1,)), ((), ())), preferred_element_type=jnp.float32
            )
            score_grads = (attn_weights * (weight_grads - row_delta[:, None])).astype(jnp.bfloat16)
            grad_query = grad_query + jnp.dot(
                score_grads, key_tile, preferred_element_type=jnp.float32
            )
            key_start = block_index * key_block
            key_term = (
                lax.dot_general(
                    score_grads,
                    query_tile,
                    (((0,), (0,)), ((), ())),
                    preferred_element_type=jnp.float32,
                )
                * softmax_scale
            )
            value_term = lax.dot_general(
                weights_half, cot_tile, (((0,), (0,)), ((), ())), preferred_element_type=jnp.float32
            )
            grad_keys = lax.dynamic_update_slice_in_dim(
                grad_keys,
                lax.dynamic_slice_in_dim(grad_keys, key_start, key_block, 0) + key_term,
                key_start,
                0,
            )
            grad_values = lax.dynamic_update_slice_in_dim(
                grad_values,
                lax.dynamic_slice_in_dim(grad_values, key_start, key_block, 0) + value_term,
                key_start,
                0,
            )
            return (grad_query, grad_keys, grad_values)

        start_back = (jnp.zeros((row_block, head_dim), jnp.float32), key_grads, value_grads)
        grad_query, key_grads, value_grads = lax.fori_loop(
            key_first, key_last, backward, start_back
        )
        return (
            (key_grads, value_grads),
            (out_tile, (grad_query * softmax_scale).astype(jnp.bfloat16)),
        )

    tiles_in = (
        query_rows.reshape(block_count, row_block, head_dim),
        cot_rows.reshape(block_count, row_block, head_dim),
        positions.reshape(block_count, row_block),
        start_of.reshape(block_count, row_block),
    )
    start_grads = (
        jnp.zeros((key_count, head_dim), jnp.float32),
        jnp.zeros((key_count, head_dim), jnp.float32),
    )
    (key_grads, value_grads), (out_tiles, query_tiles) = lax.scan(one_block, start_grads, tiles_in)
    return (
        out_tiles.reshape(row_count, head_dim),
        query_tiles.reshape(row_count, head_dim),
        key_grads,
        value_grads,
    )


def shards(inputs, weights, cotangent, doc_lengths, kept_flags):
    seq_count = lax.axis_size("seq")
    tokens = inputs[0]
    local_count = tokens.shape[0]
    seq_length = local_count * seq_count
    head_dim = HEAD_DIM
    qwidth = cotangent.shape[2]
    heads_total = qwidth // head_dim
    heads_local = heads_total // seq_count
    local_width = heads_local * head_dim
    full_weights = lax.all_gather(weights, "dp", axis=0, tiled=True)
    projected = jnp.dot(tokens, full_weights, preferred_element_type=jnp.float32).astype(
        jnp.bfloat16
    )
    seq_index = lax.axis_index("seq")
    doc_row = doc_lengths[0]
    flag_row = kept_flags[0]
    token_positions = seq_index * local_count + lax.iota(jnp.int32, local_count)
    _, keep_of = doc_tables(doc_row, flag_row, token_positions)
    cot_rows = jnp.where(keep_of[:, None] > 0, cotangent[0], jnp.zeros_like(cotangent[0]))
    query_part = projected[:, :qwidth].reshape(local_count, seq_count, local_width)
    pair_part = jnp.broadcast_to(
        projected[:, None, qwidth:], (local_count, seq_count, 2 * head_dim)
    )
    cot_part = cot_rows.reshape(local_count, seq_count, local_width)
    packed = jnp.concatenate([query_part, pair_part, cot_part], axis=2)
    received = lax.all_to_all(packed, "seq", split_axis=1, concat_axis=0, tiled=True)
    received = received.reshape(seq_length, 2 * local_width + 2 * head_dim)
    query_rows = received[:, :local_width]
    keys = received[:, local_width : local_width + head_dim]
    values = received[:, local_width + head_dim : local_width + 2 * head_dim]
    head_cot = received[:, local_width + 2 * head_dim :]
    row_positions = lax.iota(jnp.int32, seq_length * heads_local) // heads_local
    row_starts, _ = doc_tables(doc_row, flag_row, row_positions)
    out_rows, query_grads, key_grads, value_grads = attend(
        query_rows, head_cot, row_positions, row_starts, keys, values
    )
    outgoing = jnp.concatenate([out_rows, query_grads], axis=1)
    outgoing = outgoing.reshape(seq_count, local_count, 1, 2 * local_width)
    returned = lax.all_to_all(outgoing, "seq", split_axis=0, concat_axis=2, tiled=True)
    returned = returned.reshape(local_count, seq_count, 2, local_width)
    attention = returned[:, :, 0, :].reshape(local_count, qwidth)
    query_local = returned[:, :, 1, :].reshape(local_count, qwidth)
    pair_grads = jnp.concatenate([key_grads, value_grads], axis=1)
    pair_local = lax.psum_scatter(pair_grads, "seq", scatter_dimension=0, tiled=True).astype(
        jnp.bfloat16
    )
    dprojected = jnp.concatenate([query_local, pair_local], axis=1)
    inputs_grad = lax.dot_general(
        dprojected, full_weights, (((1,), (1,)), ((), ())), preferred_element_type=jnp.float32
    ).astype(jnp.bfloat16)
    weights_grad = lax.psum_scatter(
        lax.dot_general(
            tokens, dprojected, (((0,), (0,)), ((), ())), preferred_element_type=jnp.float32
        ),
        ("dp", "seq"),
        scatter_dimension=0,
        tiled=True,
    )
    return (attention[None], inputs_grad[None], weights_grad)


def solution(mesh):
    in_specs = (
        P("dp", "seq", None),
        P("dp", None),
        P("dp", "seq", None),
        P("dp", None),
        P("dp", None),
    )
    out_specs = (P("dp", "seq", None), P("dp", "seq", None), P(("dp", "seq"), None))
    return jax.shard_map(shards, mesh=mesh, in_specs=in_specs, out_specs=out_specs, check_vma=False)
```

profile of v0, /device:TPU:0, one launch (start us, length us, event | category | flops | bytes accessed | tf_op | source)
XLA Modules:
  0.0 341.7 jit_solution(17219450601114746413)
XLA Ops:
  7.9 1.0 squeeze.22
  8.9 0.8 reduce-window.4
  11.3 65.9 %all-gather.2.cloned.1.call-done = bf16[4096,768]{1,0:T(8,128)(2,1)} async-done(((bf16[512,768]{1,0:T(8,128)(2,1)}), bf16[4096,768]{1,0:T(8,128)(2,1)}) %all-gather.2.cloned.1.call-update) | async-done | bytes 6291472 | tf_op jit(solution)/shard_map/all_gather | solution.py:161
  77.1 4.6 %fusion.51 = bf16[256,768]{1,0:T(8,128)(2,1)S(1)} fusion(bf16[4096,768]{1,0:T(8,128)(2,1)} %all-gather.2.cloned.1.call-done, bf16[1,256,4096]{2,1,0:T(8,128)(2,1)S(1)} %copy-done), kind=kOutput, calls=%fused_computation.73 | convolution fusion | flops 1610809344 | bytes 8781824 | tf_op jit(solution)/shard_map/dot_general | solution.py:162
  81.8 1.1 pad_maximum_fusion
  82.9 3.6 %all-to-all-start = ((bf16[256,4,512]{2,0,1:T(8,128)(2,1)}), bf16[256,4,512]{2,0,1:T(8,128)(2,1)S(1)}, u32[]{:S(2)}, u32[]{:S(2)}) async-start(bf16[256,4,512]{2,0,1:T(8,128)(2,1)} %pad_maximum_fusion), calls=%async_computation | async-start | bytes 2097152 | tf_op jit(solution)/shard_map/all_to_all | solution.py:177
  86.7 14.0 %all-to-all-done = bf16[256,4,512]{2,0,1:T(8,128)(2,1)S(1)} async-done(((bf16[256,4,512]{2,0,1:T(8,128)(2,1)}), bf16[256,4,512]{2,0,1:T(8,128)(2,1)S(1)}, u32[]{:S(2)}, u32[]{:S(2)}) %all-to-all-start) | async-done | bytes 1048608 | tf_op jit(solution)/shard_map/all_to_all | solution.py:177
  100.8 1.0 fusion.59
  101.8 0.8 broadcast.130
  102.6 38.7 %while.67 = (s32[]{:T(128)}, f32[1024,128]{1,0:T(8,128)}, f32[1024,128]{1,0:T(8,128)S(1)}, bf16[2,512,128]{2,1,0:T(8,128)(2,1)}, bf16[2,512,128]{2,1,0:T(8,128)(...) while((s32[]{:T(128)}, f32[1024,128]{1,0:T(8,128)}, ...), condition=%wide.region_13.14_spmd, body=%wide.region_3.13_spmd.sunk | while | flops 545460224 | bytes 17384184 | solution.py:142
  102.6 0.9 dynamic-slice_bitcast_fusion.4
  103.5 3.4 while.68
  103.6 1.3 fusion.95
  105.3 1.3 fusion.95
  106.9 3.3 while.69
  107.0 1.6 fusion.100
  108.6 1.6 fusion.100
  110.3 1.1 multiply_reduce_fusion.2
  111.5 8.8 %while.70 = (s32[]{:T(128)}, f32[512,128]{1,0:T(8,128)S(1)}, f32[1024,128]{1,0:T(8,128)}, f32[1024,128]{1,0:T(8,128)S(1)}, s32[512]{0:T(512)S(1)}, /*index=5*/s3...) while((s32[]{:T(128)}, f32[512,128]{1,0:T(8,128)S(1)}, ...), condition=%wide.region_12.12_spmd.clone, body=%wide.region_11.11_spmd.clone.sunk | while | flops 338493952 | bytes 11415845 | solution.py:124
  111.5 1.3 fusion.111
  113.5 1.3 convolution_add_fusion.3
  115.1 0.8 copy-done.2
  115.9 1.3 fusion.111
  117.9 1.3 convolution_add_fusion.3
  120.3 1.7 fusion.93
  122.0 0.9 dynamic-slice_bitcast_fusion.4
  122.9 3.4 while.68
  122.9 1.3 fusion.95
  124.6 1.3 fusion.95
  126.3 3.3 while.69
  126.3 1.6 fusion.100
  128.0 1.6 fusion.100
  129.7 1.1 multiply_reduce_fusion.2
  130.8 8.8 %while.70 = (s32[]{:T(128)}, f32[512,128]{1,0:T(8,128)S(1)}, f32[1024,128]{1,0:T(8,128)}, f32[1024,128]{1,0:T(8,128)S(1)}, s32[512]{0:T(512)S(1)}, /*index=5*/s3...) while((s32[]{:T(128)}, f32[512,128]{1,0:T(8,128)S(1)}, ...), condition=%wide.region_12.12_spmd.clone, body=%wide.region_11.11_spmd.clone.sunk | while | flops 338493952 | bytes 11415845 | solution.py:124
  130.9 1.4 fusion.111
  132.9 1.3 convolution_add_fusion.3
  135.3 1.3 fusion.111
  137.2 1.3 convolution_add_fusion.3
  139.6 1.7 fusion.93
  141.3 2.1 pad_maximum_fusion.1
  143.6 15.5 %all_to_all.30 = bf16[4,256,1,256]{3,1,2,0:T(8,128)(2,1)S(1)} all-to-all(bf16[4,256,1,256]{3,1,2,0:T(8,128)(2,1)S(1)} %maximum_bitcast_fusion), channel_id=1, replica_groups=mesh['dp'=8,'seq'=4] {'seq'}, dimensions={0} | all-to-all | bytes 1048576 | tf_op jit(solution)/shard_map/all_to_all | solution.py:190
  159.4 10.7 %reduce-scatter.3.cloned.1.call-done = f32[256,256]{1,0:T(8,128)} async-done(((f32[1024,256]{1,0:T(8,128)}), f32[256,256]{1,0:T(8,128)}) %reduce-scatter.3.cloned.1.call-update) | async-done | bytes 262160 | tf_op jit(solution)/shard_map/reduce_scatter | solution.py:195
  170.1 1.0 convert_element_type.43
  171.2 6.4 %convolution_bitcast_fusion = f32[4096,768]{0,1:T(8,128)} fusion(bf16[1,256,4096]{2,1,0:T(8,128)(2,1)S(1)} %copy-done, bf16[256,256]{0,1:T(8,128)(2,1)S(1)} %copy.33, bf16[256,512]{0,1:T(8,128)(2,1)S(1)} %bitcast.126), kind=kOutput, calls=%fused_computation.67 | convolution fusion | flops 1611399168 | bytes 15073280 | tf_op jit(solution)/shard_map/dot_general | solution.py:203
  177.5 0.8 copy.34
  178.4 6.0 %fusion.47 = bf16[1,256,4096]{2,1,0:T(8,128)(2,1)} fusion(bf16[4096,768]{1,0:T(8,128)(2,1)} %all-gather.2.cloned.1.call-done, bf16[256,256]{0,1:T(8,128)(2,1)S(1)} %copy.33, bf16[256,512]{0,1:T(8,128)(2,1)S(1)} %bitcast.127), kind=kOutput, calls=%fused_computation.69 | convolution fusion | flops 1612447744 | bytes 8781824 | tf_op jit(solution)/shard_map/dot_general | solution.py:199
  184.3 148.9 %reduce-scatter.5.cloned.1.call-done = f32[128,768]{0,1:T(8,128)} async-done(((f32[4096,768]{0,1:T(8,128)}), f32[128,768]{0,1:T(8,128)}) %reduce-scatter.5.cloned.1.call-update) | async-done | bytes 393232 | tf_op jit(solution)/shard_map/reduce_scatter | solution.py:202
  333.3 1.9 copy.35
  (103 shorter events, 10.4 us)
Async XLA Ops:
  7.2 70.0 %copy-start = (bf16[1,256,4096]{2,1,0:T(8,128)(2,1)S(1)}, bf16[1,256,4096]{2,1,0:T(8,128)(2,1)}, u32[]{:S(2)}) copy-start(bf16[1,256,4096]{2,1,0:T(8,128)(2,1)} %param.13) | copy-start | bytes 6291460
  7.2 70.0 %all-gather.2.cloned.1.call-start = ((), (), s32[]{:S(2)}) async-start(), calls=%async_computation.4 | async-start | bytes 7077888 | tf_op jit(solution)/shard_map/all_gather | solution.py:161
  82.9 17.8 %all-to-all-start = ((bf16[256,4,512]{2,0,1:T(8,128)(2,1)}), bf16[256,4,512]{2,0,1:T(8,128)(2,1)S(1)}, u32[]{:S(2)}, u32[]{:S(2)}) async-start(bf16[256,4,512]{2,0,1:T(8,128)(2,1)} %pad_maximum_fusion), calls=%async_computation | async-start | bytes 2097152 | tf_op jit(solution)/shard_map/all_to_all | solution.py:177
  86.6 83.5 %reduce-scatter.3.cloned.1.call-start = ((), (), s32[]{:S(2)}) async-start(), calls=%async_computation.5 | async-start | bytes 1310720 | tf_op jit(solution)/shard_map/reduce_scatter | solution.py:195
  110.3 1.2 copy-start.3
  112.9 1.9 copy-start.1
  115.1 0.8 copy-start.2
  117.2 1.9 copy-start.1
  119.5 0.8 copy-start.2
  129.7 1.2 copy-start.3
  132.2 1.9 copy-start.1
  134.5 0.8 copy-start.2
  136.6 1.9 copy-start.1
  138.8 0.8 copy-start.2
  141.3 2.2 copy-start.4
  141.3 2.2 copy-start.5
  143.5 189.8 %reduce-scatter.5.cloned.1.call-start = ((), (), s32[]{:S(2)}) async-start(), calls=%async_computation.6 | async-start | bytes 12976128 | tf_op jit(solution)/shard_map/reduce_scatter | solution.py:202
Sparse Core Ops, SparseCore 0:
  9.7 67.4 all-gather.1
  143.6 26.4 reduce-scatter.2
  177.7 155.5 reduce-scatter.4
where the time goes:
time: 343 us; the launch traced here: 342 us
  waiting for transfers between devices  240 us (70%)
  matrix products  42.7 us (12%)
  blocking collectives  15.5 us (5%)
  between operations  13.9 us (4%)
  other arithmetic  13.8 us (4%)
  local copies, waits for them, and re-layouts  11.1 us (3%)
  starting transfers between devices  3.73 us (1%)
    reduce_scatter x1, waiting for transfers between devices, shards(): lax.psum_scatter(lax.dot_general(tokens, dprojected, (((0,), (0,)), ((),...  149 us
    all_gather x1, waiting for transfers between devices, shards(): full_weights = lax.all_gather(weights, 'dp', axis=0, tiled=True)  65.9 us
    all_to_all x1, blocking collectives, shards(): lax.all_to_all(outgoing, 'seq', split_axis=0, concat_axis=2, tiled=True)  15.5 us
    all_to_all x1, waiting for transfers between devices, shards(): lax.all_to_all(packed, 'seq', split_axis=1, concat_axis=0, tiled=True)  14 us
    reduce_scatter x1, waiting for transfers between devices, shards(): lax.psum_scatter(pair_grads, 'seq', scatter_dimension=0, tiled=True)  10.7 us
    dot_general x8, matrix products, scores(): lax.dot_general(query_tile, key_tile, (((1,), (1,)), ((), ())), preferred...  10.5 us
  transfers between devices with their start and end apart: 4, of which 4 were waited for; matrix products, arithmetic and copies ran while one was open for 3% of the time, Pallas kernels for 0%

commit v1 on v0

v1 whole, which is shorter than its diff:
```python
import functools
import math

import jax
import jax.numpy as jnp
from jax import lax
from jax.experimental import pallas as pl
from jax.experimental.pallas import tpu as pltpu
from jax.sharding import PartitionSpec as P

HEAD_DIM = 128
PAIR = 2
CORES = 2
BF16 = jnp.bfloat16
F32 = jnp.float32
NT = (((1,), (1,)), ((), ()))
TN = (((0,), (0,)), ((), ()))
VMEM = pl.BlockSpec(memory_space=pltpu.VMEM)
SMEM = pl.BlockSpec(memory_space=pltpu.SMEM)


def dot(a, b, dims=(((1,), (0,)), ((), ()))):
    return lax.dot_general(a, b, dims, preferred_element_type=F32)


def swap_x(array):
    count = lax.axis_size("seq")
    return lax.ppermute(array, "seq", [(i, i ^ 1) for i in range(count)])


def shift_rest(array, step):
    count = lax.axis_size("seq")
    rest = count // PAIR
    pairs = [(i, PAIR * ((i // PAIR + step) % rest) + i % PAIR) for i in range(count)]
    return lax.ppermute(array, "seq", pairs)


def swap_core(array):
    count = lax.axis_size("dp")
    return lax.ppermute(array, "dp", [(i, i ^ 1) for i in range(count)])


def shift_chip(array, step):
    count = lax.axis_size("dp")
    chips = count // CORES
    pairs = [(i, CORES * ((i // CORES + step) % chips) + i % CORES) for i in range(count)]
    return lax.ppermute(array, "dp", pairs)


def shift_seq(array, step):
    count = lax.axis_size("seq")
    pairs = [(i, i + step) for i in range(count) if 0 <= i + step < count]
    return lax.ppermute(array, "seq", pairs)


def block_order(chips, rest, x):
    dp_index = lax.axis_index("dp")
    chip, core = dp_index // CORES, dp_index % CORES
    place = lax.axis_index("seq") // PAIR
    order = []
    for k in range(chips):
        for c in range(CORES):
            for j in range(rest):
                shard = CORES * ((chip - k + chips) % chips) + (core ^ c)
                order.append(shard * (PAIR * rest) + PAIR * ((place - j + rest) % rest) + x)
    return jnp.stack(order).astype(jnp.int32)


def copy_block(order_ref, in_ref, out_ref):
    out_ref[...] = in_ref[...]


def pick_blocks(tokens, order, width):
    rows, total = tokens.shape
    count = order.shape[0]
    if width % 128:
        blocks = tokens.reshape(rows, total // width, width)
        return jnp.take(blocks, order, axis=1).reshape(rows, count * width)
    return pl.pallas_call(
        copy_block,
        grid_spec=pltpu.PrefetchScalarGridSpec(
            num_scalar_prefetch=1,
            grid=(count,),
            in_specs=[pl.BlockSpec((rows, width), lambda i, order: (0, order[i]))],
            out_specs=pl.BlockSpec((rows, width), lambda i, order: (0, i)),
        ),
        out_shape=jax.ShapeDtypeStruct((rows, count * width), tokens.dtype),
        name="pick_blocks",
    )(order, tokens)


def place_block(half, where_ref, mine_ref, other_ref, out_ref):
    source = where_ref[pl.program_id(0)]

    @pl.when(source < half)
    def _():
        out_ref[...] = mine_ref[...]

    @pl.when(source >= half)
    def _():
        out_ref[...] = other_ref[...]


def place_blocks(mine, other, where, width):
    rows, total = mine.shape
    half = total // width
    if width % 128:
        blocks = jnp.concatenate([mine, other], axis=1).reshape(rows, 2 * half, width)
        return jnp.take(blocks, where, axis=1).reshape(rows, 2 * total)
    return pl.pallas_call(
        functools.partial(place_block, half),
        grid_spec=pltpu.PrefetchScalarGridSpec(
            num_scalar_prefetch=1,
            grid=(2 * half,),
            in_specs=[
                pl.BlockSpec((rows, width), lambda i, where: (0, jnp.minimum(where[i], half - 1))),
                pl.BlockSpec((rows, width), lambda i, where: (0, jnp.maximum(where[i] - half, 0))),
            ],
            out_specs=pl.BlockSpec((rows, width), lambda i, where: (0, i)),
        ),
        out_shape=jax.ShapeDtypeStruct((rows, 2 * total), mine.dtype),
        name="place_blocks",
    )(where, mine, other)


def attend_kernel(
    heads, back, place_ref, docs_ref, q_ref, cot_ref, *refs
):
    pair_refs, (out_ref, dq_ref, dpair_ref, dback_ref) = refs[: back + 1], refs[back + 1 :]
    rows = q_ref.shape[0]
    hd = HEAD_DIM
    scale = 1.0 / math.sqrt(hd)
    first = place_ref[0] * rows
    base = first - back * rows
    total = (back + 1) * rows

    row_pos = first + lax.broadcasted_iota(jnp.int32, (1, rows), 1)
    start_of = jnp.zeros((1, rows), jnp.int32)
    start = jnp.int32(0)
    for d in range(docs_ref.shape[0]):
        end = start + docs_ref[d]
        start_of = jnp.where((row_pos >= start) & (row_pos < end), start, start_of)
        start = end
    key_pos = base + lax.broadcasted_iota(jnp.int32, (total, rows), 0)
    allowed = (key_pos >= start_of) & (key_pos <= row_pos)

    pairs = [r[...] for r in pair_refs]
    keys = jnp.concatenate([p[:, :hd] for p in pairs], axis=0)
    values = jnp.concatenate([p[:, hd:] for p in pairs], axis=0)
    keys_t, values_t = keys.T, values.T
    dk = jnp.zeros((total, hd), F32)
    dv = jnp.zeros((total, hd), F32)
    for h in range(heads):
        cols = slice(h * hd, (h + 1) * hd)
        q, cot = q_ref[:, cols], cot_ref[:, cols]
        logits = jnp.where(allowed, dot(keys, q, NT) * scale, -1e30)
        top = jnp.max(logits, axis=0, keepdims=True)
        raised = jnp.exp(logits - top)
        probs = raised * (1.0 / jnp.sum(raised, axis=0, keepdims=True))
        probs_half = probs.astype(BF16)
        out_t = dot(values_t, probs_half).astype(BF16)
        cot_t = cot.T
        delta = jnp.sum(cot_t.astype(F32) * out_t.astype(F32), axis=0, keepdims=True)
        dscores = (probs * (dot(values, cot, NT) - delta)).astype(BF16)
        out_ref[:, cols] = out_t.T
        dq_ref[:, cols] = (dot(keys_t, dscores) * scale).astype(BF16).T
        dk += dot(dscores, q)
        dv += dot(probs_half, cot)
    both = jnp.concatenate([dk * scale, dv], axis=1)
    dpair_ref[...] = both[back * rows :]
    dback_ref[...] = both[: back * rows].astype(BF16)


def attend(place, docs, q, cot, pairs):
    rows, width = q.shape
    back = len(pairs) - 1
    two = 2 * HEAD_DIM
    return pl.pallas_call(
        functools.partial(attend_kernel, width // HEAD_DIM, back),
        in_specs=[SMEM, SMEM] + [VMEM] * (back + 3),
        out_specs=[VMEM] * 4,
        out_shape=[
            jax.ShapeDtypeStruct((rows, width), BF16),
            jax.ShapeDtypeStruct((rows, width), BF16),
            jax.ShapeDtypeStruct((rows, two), F32),
            jax.ShapeDtypeStruct((back * rows, two), BF16),
        ],
        compiler_params=pltpu.CompilerParams(vmem_limit_bytes=48 * 2**20),
        name="attend",
    )(place, docs, q, cot, *pairs)


def kept_rows(doc_row, flag_row, positions):
    ends = jnp.cumsum(doc_row)
    starts = ends - doc_row
    inside = (positions[:, None] >= starts[None, :]) & (positions[:, None] < ends[None, :])
    return jnp.sum(jnp.where(inside, flag_row[None, :], 0), axis=1)


def shards(inputs, weights, cotangent, doc_lengths, kept_flags):
    seq_count = lax.axis_size("seq")
    chips = lax.axis_size("dp") // CORES
    rest = seq_count // PAIR
    place = lax.axis_index("seq")
    x = place % PAIR
    tokens = inputs[0]
    local = tokens.shape[0]
    qwidth = cotangent.shape[2]
    shard_rows, cols = weights.shape
    width = shard_rows // seq_count
    back = -(-(local * seq_count // 2 - 1) // local)

    order_mine = block_order(chips, rest, x)
    order_other = block_order(chips, rest, 1 - x)
    tokens_other = swap_x(pick_blocks(tokens, order_other, width))
    tokens_mine = pick_blocks(tokens, order_mine, width)

    blocks = weights.reshape(seq_count, width, cols)

    def own_block(step):
        index = PAIR * ((place // PAIR - step + rest) % rest) + x
        return lax.dynamic_index_in_dim(blocks, index, 0, keepdims=False)

    groups = []
    for k in range(chips):
        if k == 0:
            here = [own_block(j) for j in range(rest)]
        else:
            first = shift_chip(own_block(0), k)
            here = [first] + [shift_rest(first, j) for j in range(1, rest)]
        here = jnp.concatenate(here, axis=0)
        groups += [here, swap_core(here)]
    weights_half = jnp.concatenate(groups, axis=0)

    partial_other = dot(tokens_other, weights_half).astype(BF16)
    pair_from = swap_x(partial_other[:, qwidth:])
    query_from = swap_x(partial_other[:, :qwidth])
    partial_mine = dot(tokens_mine, weights_half)
    pair = (partial_mine[:, qwidth:] + pair_from.astype(F32)).astype(BF16)
    query = (partial_mine[:, :qwidth] + query_from.astype(F32)).astype(BF16)

    doc_row, flag_row = doc_lengths[0], kept_flags[0]
    positions = place * local + lax.iota(jnp.int32, local)
    kept = kept_rows(doc_row, flag_row, positions)
    cot = jnp.where(kept[:, None] > 0, cotangent[0], jnp.zeros_like(cotangent[0]))

    pairs = [shift_seq(pair, j) for j in range(back, 0, -1)] + [pair]
    attention, dquery, dpair, dback = attend(place[None], doc_row, query, cot, pairs)

    dquery_other = swap_x(dquery)
    for j in range(1, back + 1):
        sent = dback[(back - j) * local : (back - j + 1) * local]
        dpair = dpair + shift_seq(sent, -j).astype(F32)
    dpair = dpair.astype(BF16)
    dpair_other = swap_x(dpair)

    dmine = jnp.concatenate([dquery, dpair], axis=1)
    dother = jnp.concatenate([dquery_other, dpair_other], axis=1)

    grad_from = swap_x(dot(dother, weights_half, NT).astype(BF16))
    grad_mine = dot(dmine, weights_half, NT).astype(BF16)
    order_all = jnp.concatenate([order_mine, order_other])
    where = jnp.zeros_like(order_all).at[order_all].set(lax.iota(jnp.int32, order_all.shape[0]))
    inputs_grad = place_blocks(grad_mine, grad_from, where, width)

    total = dot(tokens_mine, dmine, TN) + dot(tokens_other, dother, TN)
    total = total.reshape(chips, CORES, rest, width, cols)
    result = None
    for step in range(chips):
        k = (step + 1) % chips
        group = total[k, 0] + swap_core(total[k, 1].astype(BF16)).astype(F32)
        part = group[0]
        for j in range(1, rest):
            part = part + shift_rest(group[j].astype(BF16), -j).astype(F32)
        if k:
            part = shift_chip(part.astype(BF16), -k).astype(F32)
        result = part if result is None else result + part
    return (attention[None], inputs_grad[None], result)


def solution(mesh):
    in_specs = (
        P("dp", "seq", None),
        P("dp", None),
        P("dp", "seq", None),
        P("dp", None),
        P("dp", None),
    )
    out_specs = (P("dp", "seq", None), P("dp", "seq", None), P(("dp", "seq"), None))
    return jax.shard_map(shards, mesh=mesh, in_specs=in_specs, out_specs=out_specs, check_vma=False)
```

time: 343 us -> 154 us (0.45)
  waiting for transfers between devices: 240 us -> 30.8 us
  Pallas kernels: 0 us -> 43.1 us
  starting transfers between devices: 3.73 us -> 44 us
  matrix products: 42.7 us -> 11 us
  blocking collectives: 15.5 us -> 0 us
  between operations: 13.9 us -> 1.09 us
  other arithmetic: 13.8 us -> 4.61 us
  local copies, waits for them, and re-layouts: 11.1 us -> 16.7 us
    reduce_scatter x2 -> x0, waiting for transfers between devices: 160 us -> none  [the longest x1 149 us: shards(): lax.psum_scatter(lax.dot_general(tokens, dprojected, (((0,), (0,)), ((),...]
    all_gather x1 -> x0, waiting for transfers between devices: 65.9 us -> none  [shards(): full_weights = lax.all_gather(weights, 'dp', axis=0, tiled=True)]
    ppermute x0 -> x31, starting transfers between devices: none -> 44 us  [the longest x6 14.8 us: shift_chip(): return lax.ppermute(array, 'dp', pairs)]
    pallas_call x0 -> x4, Pallas kernels: none -> 43.1 us  [the longest x2 19.1 us: pick_blocks(): pl.pallas_call(copy_block, grid_spec=pltpu.PrefetchScalarGridSpec(num_sca...]
    dot_general x31 -> x6, matrix products: 42.7 us -> 11 us  [dot(): return lax.dot_general(a, b, dims, preferred_element_type=F32)]
    ppermute x0 -> x31, waiting for transfers between devices: none -> 30.8 us  [the longest x7 13.7 us: shift_rest(): return lax.ppermute(array, 'seq', pairs)]
    all_to_all x1 -> x0, blocking collectives: 15.5 us -> none  [shards(): lax.all_to_all(outgoing, 'seq', split_axis=0, concat_axis=2, tiled=True)]
    all_to_all x1 -> x0, waiting for transfers between devices: 14 us -> none  [shards(): lax.all_to_all(packed, 'seq', split_axis=1, concat_axis=0, tiled=True)]
  transfers between devices with their start and end apart: 4 -> 31, of which waited for: 4 -> 12; matrix products, arithmetic and copies ran while one was open for 3% -> 14% of each run, Pallas kernels for 0% -> 13%
where the time goes in v1:
time: 154 us; the launch traced here: 151 us
  starting transfers between devices  44 us (29%)
  Pallas kernels  43.1 us (28%)
  waiting for transfers between devices  30.8 us (20%)
  local copies, waits for them, and re-layouts  16.7 us (11%)
  matrix products  11 us (7%)
  other arithmetic  4.61 us (3%)
    pallas_call x2, Pallas kernels, pick_blocks(): pl.pallas_call(copy_block, grid_spec=pltpu.PrefetchScalarGridSpec(num_sca...  19.1 us
    pallas_call x1, Pallas kernels, place_blocks(): pl.pallas_call(functools.partial(place_block, half), grid_spec=pltpu.Pref...  17.7 us
    ppermute x6, starting transfers between devices, shift_chip(): return lax.ppermute(array, 'dp', pairs)  14.8 us
    ppermute x7, waiting for transfers between devices, shift_rest(): return lax.ppermute(array, 'seq', pairs)  13.7 us
    unnamed x28, local copies, waits for them, and re-layouts  13.2 us
    ppermute x6, starting transfers between devices, swap_x(): return lax.ppermute(array, 'seq', [(i, i ^ 1) for i in range(count)])  11.1 us
    dot_general x6, matrix products, dot(): return lax.dot_general(a, b, dims, preferred_element_type=F32)  11 us
    ppermute x4, starting transfers between devices, shift_seq(): return lax.ppermute(array, 'seq', pairs)  8.45 us
  transfers between devices with their start and end apart: 31, of which 12 were waited for; matrix products, arithmetic and copies ran while one was open for 14% of the time, Pallas kernels for 13%

profile of v1, /device:TPU:0, one launch (start us, length us, event | category | flops | bytes accessed | tf_op | source)
XLA Modules:
  0.0 151.3 jit_solution(7721705329061679243)
XLA Ops:
  0.7 1.7 %constant_dynamic-update-slice_fusion.11 = (bf16[2048,768]{1,0:T(8,128)(2,1)}, bf16[128,768]{1,0:T(8,128)(2,1)S(1)}) fusion(bf16[4,128,768]{2,1,0:T(8,128)(2,1)} %bitcast.164, s32[]{:T(128)S(6)} %select_n.215), kind=kLoop, calls=%fused_computation.61 | loop fusion | bytes 589828
  2.4 5.0 %collective-permute-start.7 = (bf16[128,768]{1,0:T(8,128)(2,1)S(1)}, bf16[128,768]{1,0:T(8,128)(2,1)S(1)}, u32[]{:S(2)}, u32[]{:S(2)}) collective-permute-start(bf16[128,768]{1,0:T(8,128)(2,1)S(1)} %get-tuple-element.14), channel_id=1, source_target_pairs={{0,24},{4,28},{8,0},{12,4},{16,8},{20,12},{24,16},{28,20},{1,25},{... | collective-permute-start | bytes 589832 | tf_op jit(solution)/shard_map/ppermute | solution.py:47
  7.5 1.0 collective-permute-start.1
  9.1 9.6 %pick_blocks.3 = bf16[256,2048]{1,0:T(8,128)(2,1)} custom-call(s32[16]{0:T(128)} %stack.135.order_ref, bf16[256,4096]{1,0:T(8,128)(2,1)} %bitcast.161), custom_call_target="tpu_custom_call" | custom-call | tf_op jit(solution)/shard_map/pick_blocks/pallas_call | solution.py:79
  18.6 1.5 collective-permute-start.10
  20.1 1.6 %constant_dynamic-update-slice_fusion.10 = (bf16[2048,768]{1,0:T(8,128)(2,1)}, bf16[128,768]{1,0:T(8,128)(2,1)S(1)}) fusion(bf16[2048,768]{1,0:T(8,128)(2,1)} %get-tuple-element.13, bf16[4,128,768]{2,1,0:T(8,128)(2,1)} %bitcast.165, s32[]{:T(128)S(6)} %select_n.216), kind=kLoop, calls=%fused_computation.60 | loop fusion | bytes 589828
  22.2 1.6 %collective-permute-start.8 = (bf16[128,768]{1,0:T(8,128)(2,1)S(1)}, bf16[128,768]{1,0:T(8,128)(2,1)S(1)}, u32[]{:S(2)}, u32[]{:S(2)}) collective-permute-start(bf16[128,768]{1,0:T(8,128)(2,1)S(1)} %collective-permute-done.7), channel_id=1, source_target_pairs={{0,2},{1,3},{2,0},{3,1},{4,6},{5,7},{6,4},{7,5},{8,10},{9,11},{10,... | collective-permute-start | bytes 589832 | tf_op jit(solution)/shard_map/ppermute | solution.py:35
  25.1 9.5 %pick_blocks.2 = bf16[256,2048]{1,0:T(8,128)(2,1)} custom-call(s32[16]{0:T(128)} %stack.118.order_ref, bf16[256,4096]{1,0:T(8,128)(2,1)} %bitcast.162), custom_call_target="tpu_custom_call" | custom-call | tf_op jit(solution)/shard_map/pick_blocks/pallas_call | solution.py:79
  34.6 1.5 %collective-permute-start.5 = (bf16[128,768]{1,0:T(8,128)(2,1)S(1)}, bf16[128,768]{1,0:T(8,128)(2,1)S(1)}, u32[]{:S(2)}, u32[]{:S(2)}) collective-permute-start(bf16[128,768]{1,0:T(8,128)(2,1)S(1)} %collective-permute-done.4), channel_id=1, source_target_pairs={{0,2},{1,3},{2,0},{3,1},{4,6},{5,7},{6,4},{7,5},{8,10},{9,11},{10,... | collective-permute-start | bytes 589832 | tf_op jit(solution)/shard_map/ppermute | solution.py:35
  36.8 4.5 %collective-permute-done.5 = bf16[128,768]{1,0:T(8,128)(2,1)S(1)} collective-permute-done((bf16[128,768]{1,0:T(8,128)(2,1)S(1)}, bf16[128,768]{1,0:T(8,128)(2,1)S(1)}, u32[]{:S(2)}, u32[]{:S(2)}) %collective-permute-start.5) | collective-permute-done | bytes 196640 | tf_op jit(solution)/shard_map/ppermute | solution.py:35
  41.5 0.8 constant_dynamic-update-slice_fusion.9
  43.6 0.8 constant_dynamic-update-slice_fusion.6
  45.9 0.8 constant_dynamic-update-slice_fusion.3
  48.9 3.0 %convolution_convert_fusion.2 = bf16[256,768]{1,0:T(8,128)(2,1)S(1)} fusion(bf16[256,2048]{1,0:T(8,128)(2,1)S(1)} %collective-permute-done.10, bf16[2048,768]{1,0:T(8,128)(2,1)} %constant_dynamic-update-slice_fusion), kind=kOutput, calls=%fused_computation.4 | convolution fusion | flops 805502976 | bytes 4587520 | tf_op jit(solution)/shard_map/dot_general | solution.py:23
  52.5 1.5 collective-permute-start.11
  54.0 1.0 fusion.25
  55.1 3.2 %collective-permute-done.12 = bf16[256,256]{1,0:T(8,128)(2,1)S(1)} collective-permute-done((bf16[256,256]{1,0:T(8,128)(2,1)S(1)}, bf16[256,256]{1,0:T(8,128)(2,1)S(1)}, u32[]{:S(2)}, u32[]{:S(2)}) %collective-permute-start.12) | collective-permute-done | bytes 131104 | tf_op jit(solution)/shard_map/ppermute | solution.py:28
  58.3 2.4 %collective-permute-start.14 = (bf16[256,256]{1,0:T(8,128)(2,1)S(1)}, bf16[256,256]{1,0:T(8,128)(2,1)S(1)}, u32[]{:S(2)}, u32[]{:S(2)}) collective-permute-start(bf16[256,256]{1,0:T(8,128)(2,1)S(1)} %fusion.13.refs_2_), channel_id=1, source_target_pairs={{0,1},{1,2},{2,3},{4,5},{5,6},{6,7},{8,9},{9,10},{10,11},{12,13},{... | collective-permute-start | bytes 393224 | tf_op jit(solution)/shard_map/ppermute | solution.py:53
  60.8 3.4 %collective-permute-start.13 = (bf16[256,256]{1,0:T(8,128)(2,1)S(1)}, bf16[256,256]{1,0:T(8,128)(2,1)S(1)}, u32[]{:S(2)}, u32[]{:S(2)}) collective-permute-start(bf16[256,256]{1,0:T(8,128)(2,1)S(1)} %fusion.13.refs_2_), channel_id=1, source_target_pairs={{0,2},{1,3},{4,6},{5,7},{8,10},{9,11},{12,14},{13,15},{16,18},{17,... | collective-permute-start | bytes 393224 | tf_op jit(solution)/shard_map/ppermute | solution.py:53
  64.4 3.7 %collective-permute-done.13.refs_0_ = bf16[256,256]{1,0:T(8,128)(2,1)S(1)} collective-permute-done((bf16[256,256]{1,0:T(8,128)(2,1)S(1)}, bf16[256,256]{1,0:T(8,128)(2,1)S(1)}, u32[]{:S(2)}, u32[]{:S(2)}) %collective-permute-start.13) | collective-permute-done | bytes 131104 | tf_op jit(solution)/shard_map/ppermute | solution.py:53
  68.1 6.3 %attend.1 = (bf16[256,512]{1,0:T(8,128)(2,1)}, bf16[256,512]{1,0:T(8,128)(2,1)S(1)}, f32[256,256]{1,0:T(8,128)S(1)}, bf16[512,256]{1,0:T(8,128)(2,1)S(1)}) custom-call(s32[1]{0:T(128)} %bitcast.place_ref, s32[8]{0:T(128)S(1)} %bitcast.158, bf16[256,512]{1,0:T(8,128)(2,1)S(1)} %fusion.4.q_ref, bf16[256,512]{1,0:T(8,128)(2,1)S(1)} %bitcast_select_fusion.cot_ref, ...), custom_call_target="tpu_custom_call" | custom-call | tf_op jit(solution)/shard_map/attend/pallas_call | solution.py:178
  74.4 1.3 collective-permute-start.15
  75.7 1.3 collective-permute-start.16
  77.0 2.7 %collective-permute-start.17 = (bf16[256,512]{1,0:T(8,128)(2,1)S(1)}, bf16[256,512]{1,0:T(8,128)(2,1)S(1)}, u32[]{:S(2)}, u32[]{:S(2)}) collective-permute-start(bf16[256,512]{1,0:T(8,128)(2,1)S(1)} %get-tuple-element.8), channel_id=1, source_target_pairs={{0,1},{1,0},{2,3},{3,2},{4,5},{5,4},{6,7},{7,6},{8,9},{9,8},{10,11... | collective-permute-start | bytes 786440 | tf_op jit(solution)/shard_map/ppermute | solution.py:28
  79.7 2.9 %collective-permute-done.15 = bf16[256,256]{1,0:T(8,128)(2,1)S(1)} collective-permute-done((bf16[256,256]{1,0:T(8,128)(2,1)S(1)}, bf16[256,256]{1,0:T(8,128)(2,1)S(1)}, u32[]{:S(2)}, u32[]{:S(2)}) %collective-permute-start.15) | collective-permute-done | bytes 131104 | tf_op jit(solution)/shard_map/ppermute | solution.py:53
  82.7 1.1 collective-permute-done.16
  83.8 3.0 %collective-permute-start.18 = (bf16[256,256]{1,0:T(8,128)(2,1)S(1)}, bf16[256,256]{1,0:T(8,128)(2,1)S(1)}, u32[]{:S(2)}, u32[]{:S(2)}) collective-permute-start(bf16[256,256]{1,0:T(8,128)(2,1)S(1)} %add_convert_fusion), channel_id=1, source_target_pairs={{0,1},{1,0},{2,3},{3,2},{4,5},{5,4},{6,7},{7,6},{8,9},{9,8},{10,11... | collective-permute-start | bytes 393224 | tf_op jit(solution)/shard_map/ppermute | solution.py:28
  87.4 3.2 %collective-permute-done.18 = bf16[256,256]{1,0:T(8,128)(2,1)S(1)} collective-permute-done((bf16[256,256]{1,0:T(8,128)(2,1)S(1)}, bf16[256,256]{1,0:T(8,128)(2,1)S(1)}, u32[]{:S(2)}, u32[]{:S(2)}) %collective-permute-start.18) | collective-permute-done | bytes 131104 | tf_op jit(solution)/shard_map/ppermute | solution.py:28
  90.6 1.0 fusion.26
  91.6 1.1 convolution_add_fusion
  93.1 2.2 %copy-done.1 = f32[2048,768]{1,0:T(8,128)} copy-done((f32[2048,768]{1,0:T(8,128)}, f32[2048,768]{1,0:T(8,128)S(1)}, u32[]{:S(2)}) %copy-start.1) | copy-done | bytes 6291480
  96.5 1.1 scatter_custom_fusion.where_ref
  97.7 2.9 %convolution_convert_fusion = bf16[256,2048]{1,0:T(8,128)(2,1)S(1)} fusion(bf16[256,768]{1,0:T(8,128)(2,1)S(1)} %constant_dynamic-update-slice_fusion.12, bf16[2048,768]{1,0:T(8,128)(2,1)} %constant_dynamic-update-slice_fusion), kind=kOutput, calls=%fused_computation.2 | convolution fusion | flops 805830656 | bytes 4587520 | tf_op jit(solution)/shard_map/dot_general | solution.py:23
  100.6 1.8 %collective-permute-start.19 = (bf16[256,2048]{1,0:T(8,128)(2,1)S(1)}, bf16[256,2048]{1,0:T(8,128)(2,1)S(1)}, u32[]{:S(2)}, u32[]{:S(2)}) collective-permute-start(bf16[256,2048]{1,0:T(8,128)(2,1)S(1)} %convolution_convert_fusion), channel_id=1, source_target_pairs={{0,1},{1,0},{2,3},{3,2},{4,5},{5,4},{6,7},{7,6},{8,9},{9,8},{10,11... | collective-permute-start | bytes 3145736 | tf_op jit(solution)/shard_map/ppermute | solution.py:28
  102.4 2.6 %fusion.3 = (f32[2,128,768]{2,1,0:T(8,128)S(1)}, f32[2,128,768]{2,1,0:T(8,128)S(1)}, f32[2,128,768]{2,1,0:T(8,128)S(1)}, f32[2,128,768]{2,1,0:T(8,128)S(1)}) fusion(f32[4,2,2,128,768]{4,3,2,1,0:T(8,128)} %bitcast.160, bf16[2,128,768]{2,1,0:T(8,128)(2,1)} %collective-permute-done.20, bf16[2,128,768]{2,1,0:T(8,128)(2,1)} %collective-permute-done.29, ...), kind=kLoop, calls=%fused_computation.12 | loop fusion | flops 1572864 | bytes 7864320 | tf_op jit(solution)/shard_map/add | solution.py:271
  105.9 1.3 collective-permute-start.27
  108.0 1.4 collective-permute-start.21
  109.3 3.6 %collective-permute-done.24 = bf16[128,768]{1,0:T(8,128)(2,1)S(1)} collective-permute-done((bf16[128,768]{1,0:T(8,128)(2,1)S(1)}, bf16[128,768]{1,0:T(8,128)(2,1)S(1)}, u32[]{:S(2)}, u32[]{:S(2)}) %collective-permute-start.24) | collective-permute-done | bytes 196640 | tf_op jit(solution)/shard_map/ppermute | solution.py:35
  113.0 3.3 %collective-permute-start.25 = (bf16[128,768]{1,0:T(8,128)(2,1)S(1)}, bf16[128,768]{1,0:T(8,128)(2,1)S(1)}, u32[]{:S(2)}, u32[]{:S(2)}) collective-permute-start(bf16[128,768]{1,0:T(8,128)(2,1)S(1)} %fusion.10), channel_id=1, source_target_pairs={{0,16},{4,20},{8,24},{12,28},{16,0},{20,4},{24,8},{28,12},{1,17},{... | collective-permute-start | bytes 589832 | tf_op jit(solution)/shard_map/ppermute | solution.py:47
  116.3 0.9 collective-permute-done.27
  117.2 2.5 %collective-permute-start.28 = (bf16[128,768]{1,0:T(8,128)(2,1)S(1)}, bf16[128,768]{1,0:T(8,128)(2,1)S(1)}, u32[]{:S(2)}, u32[]{:S(2)}) collective-permute-start(bf16[128,768]{1,0:T(8,128)(2,1)S(1)} %fusion.8), channel_id=1, source_target_pairs={{0,8},{4,12},{8,16},{12,20},{16,24},{20,28},{24,0},{28,4},{1,9},{5... | collective-permute-start | bytes 589832 | tf_op jit(solution)/shard_map/ppermute | solution.py:47
  119.8 4.7 %collective-permute-done.21 = bf16[128,768]{1,0:T(8,128)(2,1)S(1)} collective-permute-done((bf16[128,768]{1,0:T(8,128)(2,1)S(1)}, bf16[128,768]{1,0:T(8,128)(2,1)S(1)}, u32[]{:S(2)}, u32[]{:S(2)}) %collective-permute-start.21) | collective-permute-done | bytes 196640 | tf_op jit(solution)/shard_map/ppermute | solution.py:35
  124.5 2.9 %collective-permute-start.22 = (bf16[128,768]{1,0:T(8,128)(2,1)S(1)}, bf16[128,768]{1,0:T(8,128)(2,1)S(1)}, u32[]{:S(2)}, u32[]{:S(2)}) collective-permute-start(bf16[128,768]{1,0:T(8,128)(2,1)S(1)} %fusion.12), channel_id=1, source_target_pairs={{0,24},{4,28},{8,0},{12,4},{16,8},{20,12},{24,16},{28,20},{1,25},{... | collective-permute-start | bytes 589832 | tf_op jit(solution)/shard_map/ppermute | solution.py:47
  127.3 2.0 %convolution_convert_fusion.1.mine_ref = bf16[256,2048]{1,0:T(8,128)(2,1)} fusion(bf16[2048,768]{1,0:T(8,128)(2,1)S(1)} %copy-done.6, bf16[256,256]{1,0:T(8,128)(2,1)S(1)} %add_convert_fusion, bf16[256,512]{1,0:T(8,128)(2,1)S(1)} %get-tuple-element.8), kind=kOutput, calls=%fused_computation.3 | convolution fusion | flops 806617088 | bytes 4587520 | tf_op jit(solution)/shard_map/dot_general | solution.py:23
  129.3 2.4 %collective-permute-done.22 = bf16[128,768]{1,0:T(8,128)(2,1)S(1)} collective-permute-done((bf16[128,768]{1,0:T(8,128)(2,1)S(1)}, bf16[128,768]{1,0:T(8,128)(2,1)S(1)}, u32[]{:S(2)}, u32[]{:S(2)}) %collective-permute-start.22) | collective-permute-done | bytes 196640 | tf_op jit(solution)/shard_map/ppermute | solution.py:47
  131.8 0.9 fusion.6
  132.6 1.0 copy-done.3
  133.6 17.7 %place_blocks.1 = bf16[256,4096]{1,0:T(8,128)(2,1)} custom-call(s32[32]{0:T(128)} %scatter_custom_fusion.where_ref, bf16[256,2048]{1,0:T(8,128)(2,1)} %convolution_convert_fusion.1.mine_ref, bf16[256,2048]{1,0:T(8,128)(2,1)} %copy-done.3), custom_call_target="tpu_custom_call" | custom-call | tf_op jit(solution)/shard_map/place_blocks/pallas_call | solution.py:110
  (87 shorter events, 12.7 us)
Async XLA Ops:
  0.6 21.2 %copy-start = (s32[1,8]{1,0:T(1,128)S(1)}, s32[1,8]{1,0:T(1,128)}, u32[]{:S(2)}) copy-start(s32[1,8]{1,0:T(1,128)} %param.8) | copy-start | bytes 100
  0.6 21.4 %copy-start.7 = (s32[1,8]{1,0:T(1,128)S(1)}, s32[1,8]{1,0:T(1,128)}, u32[]{:S(2)}) copy-start(s32[1,8]{1,0:T(1,128)} %param.9) | copy-start | bytes 100
  0.7 23.6 %copy-start.4 = (bf16[1,256,512]{2,1,0:T(8,128)(2,1)S(1)}, bf16[1,256,512]{2,1,0:T(8,128)(2,1)}, u32[]{:S(2)}) copy-start(bf16[1,256,512]{2,1,0:T(8,128)(2,1)} %param.7) | copy-start | bytes 786436
  2.4 19.8 %collective-permute-start.7 = (bf16[128,768]{1,0:T(8,128)(2,1)S(1)}, bf16[128,768]{1,0:T(8,128)(2,1)S(1)}, u32[]{:S(2)}, u32[]{:S(2)}) collective-permute-start(bf16[128,768]{1,0:T(8,128)(2,1)S(1)} %get-tuple-element.14), channel_id=1, source_target_pairs={{0,24},{4,28},{8,0},{12,4},{16,8},{20,12},{24,16},{28,20},{1,25},{... | collective-permute-start | bytes 589832 | tf_op jit(solution)/shard_map/ppermute | solution.py:47
  7.4 27.2 %collective-permute-start.4 = (bf16[128,768]{1,0:T(8,128)(2,1)S(1)}, bf16[128,768]{1,0:T(8,128)(2,1)S(1)}, u32[]{:S(2)}, u32[]{:S(2)}) collective-permute-start(bf16[128,768]{1,0:T(8,128)(2,1)S(1)} %get-tuple-element.14), channel_id=1, source_target_pairs={{0,16},{4,20},{8,24},{12,28},{16,0},{20,4},{24,8},{28,12},{1,17},{... | collective-permute-start | bytes 589832 | tf_op jit(solution)/shard_map/ppermute | solution.py:47
  7.5 16.3 %collective-permute-start.1 = (bf16[128,768]{1,0:T(8,128)(2,1)S(1)}, bf16[128,768]{1,0:T(8,128)(2,1)S(1)}, u32[]{:S(2)}, u32[]{:S(2)}) collective-permute-start(bf16[128,768]{1,0:T(8,128)(2,1)S(1)} %get-tuple-element.14), channel_id=1, source_target_pairs={{0,8},{4,12},{8,16},{12,20},{16,24},{20,28},{24,0},{28,4},{1,9},{5... | collective-permute-start | bytes 589832 | tf_op jit(solution)/shard_map/ppermute | solution.py:47
  18.6 30.2 %collective-permute-start.10 = (bf16[256,2048]{1,0:T(8,128)(2,1)}, bf16[256,2048]{1,0:T(8,128)(2,1)S(1)}, u32[]{:S(2)}, u32[]{:S(2)}) collective-permute-start(bf16[256,2048]{1,0:T(8,128)(2,1)} %pick_blocks.3), channel_id=1, source_target_pairs={{0,1},{1,0},{2,3},{3,2},{4,5},{5,4},{6,7},{7,6},{8,9},{9,8},{10,11... | collective-permute-start | bytes 3145736 | tf_op jit(solution)/shard_map/ppermute | solution.py:28
  21.8 19.7 %collective-permute-start = (bf16[256,768]{1,0:T(8,128)(2,1)S(1)}, bf16[256,768]{1,0:T(8,128)(2,1)S(1)}, u32[]{:S(2)}, u32[]{:S(2)}) collective-permute-start(bf16[256,768]{1,0:T(8,128)(2,1)S(1)} %pad_maximum_fusion), channel_id=1, source_target_pairs={{0,4},{4,0},{8,12},{12,8},{16,20},{20,16},{24,28},{28,24},{1,5},{5... | collective-permute-start | bytes 1179656 | tf_op jit(solution)/shard_map/ppermute | solution.py:40
  22.2 14.0 %collective-permute-start.8 = (bf16[128,768]{1,0:T(8,128)(2,1)S(1)}, bf16[128,768]{1,0:T(8,128)(2,1)S(1)}, u32[]{:S(2)}, u32[]{:S(2)}) collective-permute-start(bf16[128,768]{1,0:T(8,128)(2,1)S(1)} %collective-permute-done.7), channel_id=1, source_target_pairs={{0,2},{1,3},{2,0},{3,1},{4,6},{5,7},{6,4},{7,5},{8,10},{9,11},{10,... | collective-permute-start | bytes 589832 | tf_op jit(solution)/shard_map/ppermute | solution.py:35
  23.8 12.5 %collective-permute-start.2 = (bf16[128,768]{1,0:T(8,128)(2,1)S(1)}, bf16[128,768]{1,0:T(8,128)(2,1)S(1)}, u32[]{:S(2)}, u32[]{:S(2)}) collective-permute-start(bf16[128,768]{1,0:T(8,128)(2,1)S(1)} %collective-permute-done.1), channel_id=1, source_target_pairs={{0,2},{1,3},{2,0},{3,1},{4,6},{5,7},{6,4},{7,5},{8,10},{9,11},{10,... | collective-permute-start | bytes 589832 | tf_op jit(solution)/shard_map/ppermute | solution.py:35
  34.6 6.7 %collective-permute-start.5 = (bf16[128,768]{1,0:T(8,128)(2,1)S(1)}, bf16[128,768]{1,0:T(8,128)(2,1)S(1)}, u32[]{:S(2)}, u32[]{:S(2)}) collective-permute-start(bf16[128,768]{1,0:T(8,128)(2,1)S(1)} %collective-permute-done.4), channel_id=1, source_target_pairs={{0,2},{1,3},{2,0},{3,1},{4,6},{5,7},{6,4},{7,5},{8,10},{9,11},{10,... | collective-permute-start | bytes 589832 | tf_op jit(solution)/shard_map/ppermute | solution.py:35
  36.2 11.9 %collective-permute-start.9 = (bf16[256,768]{1,0:T(8,128)(2,1)S(1)}, bf16[256,768]{1,0:T(8,128)(2,1)S(1)}, u32[]{:S(2)}, u32[]{:S(2)}) collective-permute-start(bf16[256,768]{1,0:T(8,128)(2,1)S(1)} %pad_maximum_fusion.3), channel_id=1, source_target_pairs={{0,4},{4,0},{8,12},{12,8},{16,20},{20,16},{24,28},{28,24},{1,5},{5... | collective-permute-start | bytes 1179656 | tf_op jit(solution)/shard_map/ppermute | solution.py:40
  36.3 7.3 %collective-permute-start.3 = (bf16[256,768]{1,0:T(8,128)(2,1)S(1)}, bf16[256,768]{1,0:T(8,128)(2,1)S(1)}, u32[]{:S(2)}, u32[]{:S(2)}) collective-permute-start(bf16[256,768]{1,0:T(8,128)(2,1)S(1)} %pad_maximum_fusion.1), channel_id=1, source_target_pairs={{0,4},{4,0},{8,12},{12,8},{16,20},{20,16},{24,28},{28,24},{1,5},{5... | collective-permute-start | bytes 1179656 | tf_op jit(solution)/shard_map/ppermute | solution.py:40
  41.4 4.5 %collective-permute-start.6 = (bf16[256,768]{1,0:T(8,128)(2,1)S(1)}, bf16[256,768]{1,0:T(8,128)(2,1)S(1)}, u32[]{:S(2)}, u32[]{:S(2)}) collective-permute-start(bf16[256,768]{1,0:T(8,128)(2,1)S(1)} %pad_maximum_fusion.2), channel_id=1, source_target_pairs={{0,4},{4,0},{8,12},{12,8},{16,20},{20,16},{24,28},{28,24},{1,5},{5... | collective-permute-start | bytes 1179656 | tf_op jit(solution)/shard_map/ppermute | solution.py:40
  48.9 5.2 %copy-start.2 = (bf16[256,2048]{1,0:T(8,128)(2,1)S(1)}, bf16[256,2048]{1,0:T(8,128)(2,1)}, u32[]{:S(2)}) copy-start(bf16[256,2048]{1,0:T(8,128)(2,1)} %pick_blocks.2) | copy-start | bytes 3145732
  48.9 5.2 %copy-start.5 = (bf16[2048,768]{1,0:T(8,128)(2,1)S(1)}, bf16[2048,768]{1,0:T(8,128)(2,1)}, u32[]{:S(2)}) copy-start(bf16[2048,768]{1,0:T(8,128)(2,1)} %constant_dynamic-update-slice_fusion) | copy-start | bytes 9437188
  51.9 6.4 %collective-permute-start.12 = (bf16[256,256]{1,0:T(8,128)(2,1)S(1)}, bf16[256,256]{1,0:T(8,128)(2,1)S(1)}, u32[]{:S(2)}, u32[]{:S(2)}) collective-permute-start(bf16[256,256]{1,0:T(8,128)(2,1)S(1)} %slice.99), channel_id=1, source_target_pairs={{0,1},{1,0},{2,3},{3,2},{4,5},{5,4},{6,7},{7,6},{8,9},{9,8},{10,11... | collective-permute-start | bytes 393224 | tf_op jit(solution)/shard_map/ppermute | solution.py:28
  52.5 11.7 %collective-permute-start.11 = (bf16[256,512]{1,0:T(8,128)(2,1)S(1)}, bf16[256,512]{1,0:T(8,128)(2,1)S(1)}, u32[]{:S(2)}, u32[]{:S(2)}) collective-permute-start(bf16[256,512]{1,0:T(8,128)(2,1)S(1)} %slice.97), channel_id=1, source_target_pairs={{0,1},{1,0},{2,3},{3,2},{4,5},{5,4},{6,7},{7,6},{8,9},{9,8},{10,11... | collective-permute-start | bytes 786440 | tf_op jit(solution)/shard_map/ppermute | solution.py:28
  58.3 6.0 %collective-permute-start.14 = (bf16[256,256]{1,0:T(8,128)(2,1)S(1)}, bf16[256,256]{1,0:T(8,128)(2,1)S(1)}, u32[]{:S(2)}, u32[]{:S(2)}) collective-permute-start(bf16[256,256]{1,0:T(8,128)(2,1)S(1)} %fusion.13.refs_2_), channel_id=1, source_target_pairs={{0,1},{1,2},{2,3},{4,5},{5,6},{6,7},{8,9},{9,10},{10,11},{12,13},{... | collective-permute-start | bytes 393224 | tf_op jit(solution)/shard_map/ppermute | solution.py:53
  60.8 7.3 %collective-permute-start.13 = (bf16[256,256]{1,0:T(8,128)(2,1)S(1)}, bf16[256,256]{1,0:T(8,128)(2,1)S(1)}, u32[]{:S(2)}, u32[]{:S(2)}) collective-permute-start(bf16[256,256]{1,0:T(8,128)(2,1)S(1)} %fusion.13.refs_2_), channel_id=1, source_target_pairs={{0,2},{1,3},{4,6},{5,7},{8,10},{9,11},{12,14},{13,15},{16,18},{17,... | collective-permute-start | bytes 393224 | tf_op jit(solution)/shard_map/ppermute | solution.py:53
  74.4 8.3 %collective-permute-start.15 = (bf16[256,256]{1,0:T(8,128)(2,1)S(1)}, bf16[256,256]{1,0:T(8,128)(2,1)S(1)}, u32[]{:S(2)}, u32[]{:S(2)}) collective-permute-start(bf16[256,256]{1,0:T(8,128)(2,1)S(1)} %get-tuple-element.23), channel_id=1, source_target_pairs={{1,0},{2,1},{3,2},{5,4},{6,5},{7,6},{9,8},{10,9},{11,10},{13,12},{... | collective-permute-start | bytes 393224 | tf_op jit(solution)/shard_map/ppermute | solution.py:53
  75.7 8.1 %collective-permute-start.16 = (bf16[256,256]{1,0:T(8,128)(2,1)S(1)}, bf16[256,256]{1,0:T(8,128)(2,1)S(1)}, u32[]{:S(2)}, u32[]{:S(2)}) collective-permute-start(bf16[256,256]{1,0:T(8,128)(2,1)S(1)} %get-tuple-element.24), channel_id=1, source_target_pairs={{2,0},{3,1},{6,4},{7,5},{10,8},{11,9},{14,12},{15,13},{18,16},{19,... | collective-permute-start | bytes 393224 | tf_op jit(solution)/shard_map/ppermute | solution.py:53
  77.0 10.3 %collective-permute-start.17 = (bf16[256,512]{1,0:T(8,128)(2,1)S(1)}, bf16[256,512]{1,0:T(8,128)(2,1)S(1)}, u32[]{:S(2)}, u32[]{:S(2)}) collective-permute-start(bf16[256,512]{1,0:T(8,128)(2,1)S(1)} %get-tuple-element.8), channel_id=1, source_target_pairs={{0,1},{1,0},{2,3},{3,2},{4,5},{5,4},{6,7},{7,6},{8,9},{9,8},{10,11... | collective-permute-start | bytes 786440 | tf_op jit(solution)/shard_map/ppermute | solution.py:28
  83.8 6.7 %collective-permute-start.18 = (bf16[256,256]{1,0:T(8,128)(2,1)S(1)}, bf16[256,256]{1,0:T(8,128)(2,1)S(1)}, u32[]{:S(2)}, u32[]{:S(2)}) collective-permute-start(bf16[256,256]{1,0:T(8,128)(2,1)S(1)} %add_convert_fusion), channel_id=1, source_target_pairs={{0,1},{1,0},{2,3},{3,2},{4,5},{5,4},{6,7},{7,6},{8,9},{9,8},{10,11... | collective-permute-start | bytes 393224 | tf_op jit(solution)/shard_map/ppermute | solution.py:28
  92.7 2.6 %copy-start.1 = (f32[2048,768]{1,0:T(8,128)}, f32[2048,768]{1,0:T(8,128)S(1)}, u32[]{:S(2)}) copy-start(f32[2048,768]{1,0:T(8,128)S(1)} %convolution_add_fusion) | copy-start | bytes 18874372
  95.4 7.0 %collective-permute-start.20 = (bf16[2,128,768]{2,1,0:T(8,128)(2,1)S(1)}, bf16[2,128,768]{2,1,0:T(8,128)(2,1)}, u32[]{:S(2)}, u32[]{:S(2)}) collective-permute-start(bf16[2,128,768]{2,1,0:T(8,128)(2,1)S(1)} %get-tuple-element.19), channel_id=1, source_target_pairs={{0,4},{4,0},{8,12},{12,8},{16,20},{20,16},{24,28},{28,24},{1,5},{5... | collective-permute-start | bytes 1179656 | tf_op jit(solution)/shard_map/ppermute | solution.py:40
  95.5 6.9 %collective-permute-start.29 = (bf16[2,128,768]{2,1,0:T(8,128)(2,1)S(1)}, bf16[2,128,768]{2,1,0:T(8,128)(2,1)}, u32[]{:S(2)}, u32[]{:S(2)}) collective-permute-start(bf16[2,128,768]{2,1,0:T(8,128)(2,1)S(1)} %get-tuple-element.20), channel_id=1, source_target_pairs={{0,4},{4,0},{8,12},{12,8},{16,20},{20,16},{24,28},{28,24},{1,5},{5... | collective-permute-start | bytes 1179656 | tf_op jit(solution)/shard_map/ppermute | solution.py:40
  96.0 6.4 %collective-permute-start.26 = (bf16[2,128,768]{2,1,0:T(8,128)(2,1)S(1)}, bf16[2,128,768]{2,1,0:T(8,128)(2,1)}, u32[]{:S(2)}, u32[]{:S(2)}) collective-permute-start(bf16[2,128,768]{2,1,0:T(8,128)(2,1)S(1)} %get-tuple-element.21), channel_id=1, source_target_pairs={{0,4},{4,0},{8,12},{12,8},{16,20},{20,16},{24,28},{28,24},{1,5},{5... | collective-permute-start | bytes 1179656 | tf_op jit(solution)/shard_map/ppermute | solution.py:40
  96.1 6.3 %collective-permute-start.23 = (bf16[2,128,768]{2,1,0:T(8,128)(2,1)S(1)}, bf16[2,128,768]{2,1,0:T(8,128)(2,1)}, u32[]{:S(2)}, u32[]{:S(2)}) collective-permute-start(bf16[2,128,768]{2,1,0:T(8,128)(2,1)S(1)} %get-tuple-element.22), channel_id=1, source_target_pairs={{0,4},{4,0},{8,12},{12,8},{16,20},{20,16},{24,28},{28,24},{1,5},{5... | collective-permute-start | bytes 1179656 | tf_op jit(solution)/shard_map/ppermute | solution.py:40
  100.6 32.0 %collective-permute-start.19 = (bf16[256,2048]{1,0:T(8,128)(2,1)S(1)}, bf16[256,2048]{1,0:T(8,128)(2,1)S(1)}, u32[]{:S(2)}, u32[]{:S(2)}) collective-permute-start(bf16[256,2048]{1,0:T(8,128)(2,1)S(1)} %convolution_convert_fusion), channel_id=1, source_target_pairs={{0,1},{1,0},{2,3},{3,2},{4,5},{5,4},{6,7},{7,6},{8,9},{9,8},{10,11... | collective-permute-start | bytes 3145736 | tf_op jit(solution)/shard_map/ppermute | solution.py:28
  105.0 22.3 %copy-start.6 = (bf16[2048,768]{1,0:T(8,128)(2,1)S(1)}, bf16[2048,768]{1,0:T(8,128)(2,1)}, u32[]{:S(2)}) copy-start(bf16[2048,768]{1,0:T(8,128)(2,1)} %constant_dynamic-update-slice_fusion) | copy-start | bytes 9437188
  105.1 7.9 %collective-permute-start.24 = (bf16[128,768]{1,0:T(8,128)(2,1)S(1)}, bf16[128,768]{1,0:T(8,128)(2,1)S(1)}, u32[]{:S(2)}, u32[]{:S(2)}) collective-permute-start(bf16[128,768]{1,0:T(8,128)(2,1)S(1)} %fusion.15), channel_id=1, source_target_pairs={{0,2},{1,3},{2,0},{3,1},{4,6},{5,7},{6,4},{7,5},{8,10},{9,11},{10,... | collective-permute-start | bytes 589832 | tf_op jit(solution)/shard_map/ppermute | solution.py:35
  105.9 11.3 %collective-permute-start.27 = (bf16[128,768]{1,0:T(8,128)(2,1)S(1)}, bf16[128,768]{1,0:T(8,128)(2,1)S(1)}, u32[]{:S(2)}, u32[]{:S(2)}) collective-permute-start(bf16[128,768]{1,0:T(8,128)(2,1)S(1)} %fusion.16), channel_id=1, source_target_pairs={{0,2},{1,3},{2,0},{3,1},{4,6},{5,7},{6,4},{7,5},{8,10},{9,11},{10,... | collective-permute-start | bytes 589832 | tf_op jit(solution)/shard_map/ppermute | solution.py:35
  107.2 22.1 %collective-permute-start.30 = (bf16[128,768]{1,0:T(8,128)(2,1)S(1)}, bf16[128,768]{1,0:T(8,128)(2,1)S(1)}, u32[]{:S(2)}, u32[]{:S(2)}) collective-permute-start(bf16[128,768]{1,0:T(8,128)(2,1)S(1)} %fusion.17), channel_id=1, source_target_pairs={{0,2},{1,3},{2,0},{3,1},{4,6},{5,7},{6,4},{7,5},{8,10},{9,11},{10,... | collective-permute-start | bytes 589832 | tf_op jit(solution)/shard_map/ppermute | solution.py:35
  108.0 16.5 %collective-permute-start.21 = (bf16[128,768]{1,0:T(8,128)(2,1)S(1)}, bf16[128,768]{1,0:T(8,128)(2,1)S(1)}, u32[]{:S(2)}, u32[]{:S(2)}) collective-permute-start(bf16[128,768]{1,0:T(8,128)(2,1)S(1)} %fusion.14), channel_id=1, source_target_pairs={{0,2},{1,3},{2,0},{3,1},{4,6},{5,7},{6,4},{7,5},{8,10},{9,11},{10,... | collective-permute-start | bytes 589832 | tf_op jit(solution)/shard_map/ppermute | solution.py:35
  113.0 16.3 %collective-permute-start.25 = (bf16[128,768]{1,0:T(8,128)(2,1)S(1)}, bf16[128,768]{1,0:T(8,128)(2,1)S(1)}, u32[]{:S(2)}, u32[]{:S(2)}) collective-permute-start(bf16[128,768]{1,0:T(8,128)(2,1)S(1)} %fusion.10), channel_id=1, source_target_pairs={{0,16},{4,20},{8,24},{12,28},{16,0},{20,4},{24,8},{28,12},{1,17},{... | collective-permute-start | bytes 589832 | tf_op jit(solution)/shard_map/ppermute | solution.py:47
  117.2 12.1 %collective-permute-start.28 = (bf16[128,768]{1,0:T(8,128)(2,1)S(1)}, bf16[128,768]{1,0:T(8,128)(2,1)S(1)}, u32[]{:S(2)}, u32[]{:S(2)}) collective-permute-start(bf16[128,768]{1,0:T(8,128)(2,1)S(1)} %fusion.8), channel_id=1, source_target_pairs={{0,8},{4,12},{8,16},{12,20},{16,24},{20,28},{24,0},{28,4},{1,9},{5... | collective-permute-start | bytes 589832 | tf_op jit(solution)/shard_map/ppermute | solution.py:47
  124.5 7.3 %collective-permute-start.22 = (bf16[128,768]{1,0:T(8,128)(2,1)S(1)}, bf16[128,768]{1,0:T(8,128)(2,1)S(1)}, u32[]{:S(2)}, u32[]{:S(2)}) collective-permute-start(bf16[128,768]{1,0:T(8,128)(2,1)S(1)} %fusion.12), channel_id=1, source_target_pairs={{0,24},{4,28},{8,0},{12,4},{16,8},{20,12},{24,16},{28,20},{1,25},{... | collective-permute-start | bytes 589832 | tf_op jit(solution)/shard_map/ppermute | solution.py:47
  132.6 1.0 copy-start.3

commit v2 on v1

--- a/solution.py
+++ b/solution.py
@@ -66,65 +66,174 @@
     return jnp.stack(order).astype(jnp.int32)
 
 
-def copy_block(order_ref, in_ref, out_ref):
-    out_ref[...] = in_ref[...]
-
-
-def pick_blocks(tokens, order, width):
+def lanes(index, width):
+    return pl.ds(pl.multiple_of(index * width, width), width)
+
+
+def split_kernel(width, mine_order, other_order, in_ref, mine_ref, other_ref):
+    for i in range(mine_order.shape[0]):
+        out = slice(i * width, (i + 1) * width)
+        other_ref[:, out] = in_ref[:, lanes(other_order[i], width)]
+        mine_ref[:, out] = in_ref[:, lanes(mine_order[i], width)]
+
+
+def split_tokens(tokens, mine_order, other_order, width):
     rows, total = tokens.shape
-    count = order.shape[0]
+    half = total // 2
     if width % 128:
         blocks = tokens.reshape(rows, total // width, width)
-        return jnp.take(blocks, order, axis=1).reshape(rows, count * width)
-    return pl.pallas_call(
-        copy_block,
+        take = lambda order: jnp.take(blocks, order, axis=1).reshape(rows, half)
+        return take(mine_order), take(other_order)
+    tile = min(rows, 64)
+    return pl.pallas_call(
+        functools.partial(split_kernel, width),
         grid_spec=pltpu.PrefetchScalarGridSpec(
-            num_scalar_prefetch=1,
-            grid=(count,),
-            in_specs=[pl.BlockSpec((rows, width), lambda i, order: (0, order[i]))],
-            out_specs=pl.BlockSpec((rows, width), lambda i, order: (0, i)),
+            num_scalar_prefetch=2,
+            grid=(rows // tile,),
+            in_specs=[pl.BlockSpec((tile, total), lambda i, *_: (i, 0))],
+            out_specs=[pl.BlockSpec((tile, half), lambda i, *_: (i, 0))] * 2,
         ),
-        out_shape=jax.ShapeDtypeStruct((rows, count * width), tokens.dtype),
-        name="pick_blocks",
-    )(order, tokens)
-
-
-def place_block(half, where_ref, mine_ref, other_ref, out_ref):
-    source = where_ref[pl.program_id(0)]
-
-    @pl.when(source < half)
-    def _():
-        out_ref[...] = mine_ref[...]
-
-    @pl.when(source >= half)
-    def _():
-        out_ref[...] = other_ref[...]
-
-
-def place_blocks(mine, other, where, width):
-    rows, total = mine.shape
-    half = total // width
-    if width % 128:
-        blocks = jnp.concatenate([mine, other], axis=1).reshape(rows, 2 * half, width)
-        return jnp.take(blocks, where, axis=1).reshape(rows, 2 * total)
-    return pl.pallas_call(
-        functools.partial(place_block, half),
-        grid_spec=pltpu.PrefetchScalarGridSpec(
-            num_scalar_prefetch=1,
-            grid=(2 * half,),
-            in_specs=[
-                pl.BlockSpec((rows, width), lambda i, where: (0, jnp.minimum(where[i], half - 1))),
-                pl.BlockSpec((rows, width), lambda i, where: (0, jnp.maximum(where[i] - half, 0))),
-            ],
-            out_specs=pl.BlockSpec((rows, width), lambda i, where: (0, i)),
-        ),
-        out_shape=jax.ShapeDtypeStruct((rows, 2 * total), mine.dtype),
-        name="place_blocks",
-    )(where, mine, other)
+        out_shape=[jax.ShapeDtypeStruct((rows, half), tokens.dtype)] * 2,
+        name="split_tokens",
+    )(mine_order, other_order, tokens)
+
+
+def place_kernel(width, order, half_ref, base_ref, out_ref, sems):
+    copies = []
+    for i in range(order.shape[0]):
+        source = half_ref.at[:, pl.ds(i * width, width)]
+        copies.append(pltpu.make_async_copy(source, out_ref.at[:, lanes(order[i], width)], sems.at[i]))
+    for copy in copies:
+        copy.start()
+    for copy in copies:
+        copy.wait()
+
+
+def place_half(base, half, order, width):
+    anywhere = pl.BlockSpec(memory_space=pl.ANY)
+    return pl.pallas_call(
+        functools.partial(place_kernel, width),
+        in_specs=[SMEM, anywhere, anywhere],
+        out_specs=anywhere,
+        out_shape=jax.ShapeDtypeStruct(base.shape, base.dtype),
+        scratch_shapes=[pltpu.SemaphoreType.DMA((order.shape[0],))],
+        input_output_aliases={2: 0},
+        name="place_half",
+    )(order, half, base)
+
+
+def group_rows(width, rest, own_ref, piece_refs, own_order, k):
+    if k == 0:
+        here = [own_ref[pl.ds(pl.multiple_of(own_order[j] * width, width), width), :] for j in range(rest)]
+        return jnp.concatenate(here + [piece_refs[0][...]], axis=0)
+    return jnp.concatenate([r[...] for r in piece_refs[1 + (k - 1) * (rest + 1) : 1 + k * (rest + 1)]], axis=0)
+
+
+def project_kernel(chips, rest, width, qwidth, own_order, tokens_ref, own_ref, *refs):
+    pieces, (query_ref, pair_ref) = refs[:-2], refs[-2:]
+    span = CORES * rest * width
+    total = None
+    for k in range(chips):
+        rows = group_rows(width, rest, own_ref, pieces, own_order, k)
+        term = dot(tokens_ref[:, k * span : (k + 1) * span], rows)
+        total = term if total is None else total + term
+    query_ref[...] = total[:, :qwidth].astype(query_ref.dtype)
+    pair_ref[...] = total[:, qwidth:].astype(pair_ref.dtype)
+
+
+def project(tokens, own_order, own, pieces, chips, rest, width, qwidth, kind):
+    rows, cols = tokens.shape[0], own.shape[1]
+    return pl.pallas_call(
+        functools.partial(project_kernel, chips, rest, width, qwidth),
+        in_specs=[SMEM] + [VMEM] * (2 + len(pieces)),
+        out_specs=[VMEM] * 2,
+        out_shape=[
+            jax.ShapeDtypeStruct((rows, qwidth), kind),
+            jax.ShapeDtypeStruct((rows, cols - qwidth), kind),
+        ],
+        compiler_params=pltpu.CompilerParams(vmem_limit_bytes=48 * 2**20),
+        name="project",
+    )(own_order, tokens, own, *pieces)
+
+
+def grad_kernel(chips, rest, width, scatter, own_order, order, dquery_ref, dpair_ref, own_ref, *refs):
+    pieces, out_ref = refs[:-1], refs[-1]
+    span = CORES * rest * width
+    grads = jnp.concatenate([dquery_ref[...], dpair_ref[...]], axis=1)
+    for k in range(chips):
+        rows = group_rows(width, rest, own_ref, pieces, own_order, k)
+        term = dot(grads, rows, NT).astype(BF16)
+        if scatter:
+            for i in range(CORES * rest):
+                place = lanes(order[k * CORES * rest + i], width)
+                out_ref[:, place] = term[:, i * width : (i + 1) * width]
+        else:
+            out_ref[:, k * span : (k + 1) * span] = term
+
+
+def width_grad(dquery, dpair, own_order, order, own, pieces, chips, rest, width, scatter):
+    rows = dquery.shape[0]
+    total = chips * CORES * rest * width * (PAIR if scatter else 1)
+    return pl.pallas_call(
+        functools.partial(grad_kernel, chips, rest, width, scatter),
+        in_specs=[SMEM, SMEM] + [VMEM] * (3 + len(pieces)),
+        out_specs=VMEM,
+        out_shape=jax.ShapeDtypeStruct((rows, total), BF16),
+        compiler_params=pltpu.CompilerParams(vmem_limit_bytes=48 * 2**20),
+        name="width_grad",
+    )(own_order, order, dquery, dpair, own, *pieces)
+
+
+def weight_kernel(span, tokens_ref, other_ref, dq_ref, dp_ref, dq_other_ref, dp_other_ref, keep_ref, send_ref):
+    mine = jnp.concatenate([dq_ref[...], dp_ref[...]], axis=1)
+    other = jnp.concatenate([dq_other_ref[...], dp_other_ref[...]], axis=1)
+    both = jnp.concatenate([mine, other], axis=0)
+    left = jnp.concatenate([tokens_ref[...], other_ref[...]], axis=0)
+    total = dot(left.T, both)
+    keep_ref[...] = total[: span // 2]
+    send_ref[...] = total[span // 2 :].astype(BF16)
+
+
+def weight_terms(tokens, other, k, span, grads):
+    rows = tokens.shape[0]
+    cols = grads[0].shape[1] + grads[1].shape[1]
+    column = pl.BlockSpec((rows, span), lambda i: (0, k))
+    whole = [pl.BlockSpec(g.shape, lambda i: (0, 0)) for g in grads]
+    return pl.pallas_call(
+        functools.partial(weight_kernel, span),
+        grid=(1,),
+        in_specs=[column, column] + whole,
+        out_specs=[pl.BlockSpec((span // 2, cols), lambda i: (0, 0))] * 2,
+        out_shape=[
+            jax.ShapeDtypeStruct((span // 2, cols), F32),
+            jax.ShapeDtypeStruct((span // 2, cols), BF16),
+        ],
+        compiler_params=pltpu.CompilerParams(vmem_limit_bytes=48 * 2**20),
+        name="weight_terms",
+    )(tokens, other, *grads)
+
+
+def core_sum_kernel(width, keep_ref, from_ref, mine_ref, *send_refs):
+    total = keep_ref[...] + from_ref[...].astype(F32)
+    mine_ref[...] = total[:width]
+    for j, ref in enumerate(send_refs, 1):
+        ref[...] = total[j * width : (j + 1) * width].astype(BF16)
+
+
+def core_sum(keep, received, rest, width):
+    cols = keep.shape[1]
+    return pl.pallas_call(
+        functools.partial(core_sum_kernel, width),
+        in_specs=[VMEM] * 2,
+        out_specs=[VMEM] * rest,
+        out_shape=[jax.ShapeDtypeStruct((width, cols), F32)]
+        + [jax.ShapeDtypeStruct((width, cols), BF16)] * (rest - 1),
+        name="core_sum",
+    )(keep, received)
 
 
 def attend_kernel(
-    heads, back, place_ref, docs_ref, q_ref, cot_ref, *refs
+    heads, back, place_ref, docs_ref, q_ref, q_from_ref, cot_ref, *refs
 ):
     pair_refs, (out_ref, dq_ref, dpair_ref, dback_ref) = refs[: back + 1], refs[back + 1 :]
     rows = q_ref.shape[0]
@@ -152,7 +261,8 @@
     dv = jnp.zeros((total, hd), F32)
     for h in range(heads):
         cols = slice(h * hd, (h + 1) * hd)
-        q, cot = q_ref[:, cols], cot_ref[:, cols]
+        q = (q_ref[:, cols] + q_from_ref[:, cols].astype(F32)).astype(BF16)
+        cot = cot_ref[:, cols]
         logits = jnp.where(allowed, dot(keys, q, NT) * scale, -1e30)
         top = jnp.max(logits, axis=0, keepdims=True)
         raised = jnp.exp(logits - top)
@@ -171,13 +281,13 @@
     dback_ref[...] = both[: back * rows].astype(BF16)
 
 
-def attend(place, docs, q, cot, pairs):
+def attend(place, docs, q, q_from, cot, pairs):
     rows, width = q.shape
     back = len(pairs) - 1
     two = 2 * HEAD_DIM
     return pl.pallas_call(
         functools.partial(attend_kernel, width // HEAD_DIM, back),
-        in_specs=[SMEM, SMEM] + [VMEM] * (back + 3),
+        in_specs=[SMEM, SMEM] + [VMEM] * (back + 4),
         out_specs=[VMEM] * 4,
         out_shape=[
             jax.ShapeDtypeStruct((rows, width), BF16),
@@ -187,7 +297,7 @@
         ],
         compiler_params=pltpu.CompilerParams(vmem_limit_bytes=48 * 2**20),
         name="attend",
-    )(place, docs, q, cot, *pairs)
+    )(place, docs, q, q_from, cot, *pairs)
 
 
 def kept_rows(doc_row, flag_row, positions):
@@ -212,32 +322,23 @@
 
     order_mine = block_order(chips, rest, x)
     order_other = block_order(chips, rest, 1 - x)
-    tokens_other = swap_x(pick_blocks(tokens, order_other, width))
-    tokens_mine = pick_blocks(tokens, order_mine, width)
+    tokens_mine, tokens_sent = split_tokens(tokens, order_mine, order_other, width)
+    tokens_other = swap_x(tokens_sent)
 
     blocks = weights.reshape(seq_count, width, cols)
-
-    def own_block(step):
-        index = PAIR * ((place // PAIR - step + rest) % rest) + x
-        return lax.dynamic_index_in_dim(blocks, index, 0, keepdims=False)
-
-    groups = []
-    for k in range(chips):
-        if k == 0:
-            here = [own_block(j) for j in range(rest)]
-        else:
-            first = shift_chip(own_block(0), k)
-            here = [first] + [shift_rest(first, j) for j in range(1, rest)]
-        here = jnp.concatenate(here, axis=0)
-        groups += [here, swap_core(here)]
-    weights_half = jnp.concatenate(groups, axis=0)
-
-    partial_other = dot(tokens_other, weights_half).astype(BF16)
-    pair_from = swap_x(partial_other[:, qwidth:])
-    query_from = swap_x(partial_other[:, :qwidth])
-    partial_mine = dot(tokens_mine, weights_half)
-    pair = (partial_mine[:, qwidth:] + pair_from.astype(F32)).astype(BF16)
-    query = (partial_mine[:, :qwidth] + query_from.astype(F32)).astype(BF16)
+    own_order = jnp.stack([PAIR * ((place // PAIR - j + rest) % rest) + x for j in range(rest)])
+    own_blocks = [lax.dynamic_index_in_dim(blocks, own_order[j], 0, keepdims=False) for j in range(rest)]
+    pieces = [swap_core(jnp.concatenate(own_blocks, axis=0))]
+    for k in range(1, chips):
+        first = shift_chip(own_blocks[0], k)
+        here = [first] + [shift_rest(first, j) for j in range(1, rest)]
+        pieces += here + [swap_core(jnp.concatenate(here, axis=0))]
+    weight_args = (weights, pieces, chips, rest, width)
+
+    query_sent, pair_sent = project(tokens_other, own_order, *weight_args, qwidth, BF16)
+    pair_from, query_from = swap_x(pair_sent), swap_x(query_sent)
+    query, pair = project(tokens_mine, own_order, *weight_args, qwidth, F32)
+    pair = (pair + pair_from.astype(F32)).astype(BF16)
 
     doc_row, flag_row = doc_lengths[0], kept_flags[0]
     positions = place * local + lax.iota(jnp.int32, local)
@@ -245,7 +346,7 @@
     cot = jnp.where(kept[:, None] > 0, cotangent[0], jnp.zeros_like(cotangent[0]))
 
     pairs = [shift_seq(pair, j) for j in range(back, 0, -1)] + [pair]
-    attention, dquery, dpair, dback = attend(place[None], doc_row, query, cot, pairs)
+    attention, dquery, dpair, dback = attend(place[None], doc_row, query, query_from, cot, pairs)
 
     dquery_other = swap_x(dquery)
     for j in range(1, back + 1):
@@ -254,27 +355,30 @@
     dpair = dpair.astype(BF16)
     dpair_other = swap_x(dpair)
 
-    dmine = jnp.concatenate([dquery, dpair], axis=1)
-    dother = jnp.concatenate([dquery_other, dpair_other], axis=1)
-
-    grad_from = swap_x(dot(dother, weights_half, NT).astype(BF16))
-    grad_mine = dot(dmine, weights_half, NT).astype(BF16)
-    order_all = jnp.concatenate([order_mine, order_other])
-    where = jnp.zeros_like(order_all).at[order_all].set(lax.iota(jnp.int32, order_all.shape[0]))
-    inputs_grad = place_blocks(grad_mine, grad_from, where, width)
-
-    total = dot(tokens_mine, dmine, TN) + dot(tokens_other, dother, TN)
-    total = total.reshape(chips, CORES, rest, width, cols)
+    span = CORES * rest * width
+    grads = (dquery, dpair, dquery_other, dpair_other)
     result = None
     for step in range(chips):
         k = (step + 1) % chips
-        group = total[k, 0] + swap_core(total[k, 1].astype(BF16)).astype(F32)
-        part = group[0]
+        keep, sent = weight_terms(tokens_mine, tokens_other, k, span, grads)
+        part, *sent = core_sum(keep, swap_core(sent), rest, width)
         for j in range(1, rest):
-            part = part + shift_rest(group[j].astype(BF16), -j).astype(F32)
+            part = part + shift_rest(sent[j - 1], -j).astype(F32)
         if k:
             part = shift_chip(part.astype(BF16), -k).astype(F32)
         result = part if result is None else result + part
+
+    grad_args = (own_order, order_mine, *weight_args)
+    grad_from = swap_x(width_grad(dquery_other, dpair_other, *grad_args, False))
+    if width % 128:
+        grad_mine = width_grad(dquery, dpair, *grad_args, False)
+        order_all = jnp.concatenate([order_mine, order_other])
+        where = jnp.zeros_like(order_all).at[order_all].set(lax.iota(jnp.int32, order_all.shape[0]))
+        both = jnp.concatenate([grad_mine, grad_from], axis=1).reshape(local, -1, width)
+        inputs_grad = jnp.take(both, where, axis=1).reshape(tokens.shape)
+    else:
+        base = width_grad(dquery, dpair, *grad_args, True)
+        inputs_grad = place_half(base, grad_from, order_other, width)
     return (attention[None], inputs_grad[None], result)
 
 

time: 154 us -> 172 us (1.12); the launches traced: 151 us -> 171 us
  Pallas kernels: 43.1 us -> 68.4 us
  matrix products: 11 us -> 0 us
  starting transfers between devices: 44 us -> 39.1 us
  other arithmetic: 4.61 us -> 8.81 us
  waiting for transfers between devices: 30.8 us -> 34.3 us
  local copies, waits for them, and re-layouts: 16.7 us -> 19.6 us
    pallas_call x3 -> x14, Pallas kernels: 36.8 us -> 62.1 us  [the longest x1 33.7 us: place_half(): pl.pallas_call(functools.partial(place_kernel, width), in_specs=[SMEM, an...]
    dot_general x6 -> x0, matrix products: 11 us -> none  [dot(): return lax.dot_general(a, b, dims, preferred_element_type=F32)]
    ppermute x6, waiting for transfers between devices: 2.43 us -> 10.6 us  [shift_chip(): return lax.ppermute(array, 'dp', pairs)]
    ppermute x7, waiting for transfers between devices: 13.7 us -> 6.56 us  [shift_rest(): return lax.ppermute(array, 'seq', pairs)]
    ppermute x6, starting transfers between devices: 14.8 us -> 9.88 us  [shift_chip(): return lax.ppermute(array, 'dp', pairs)]
    concatenate x4, other arithmetic: 0.11 us -> 4.18 us  [the longest x3 3.41 us: shards(): pieces += here + [swap_core(jnp.concatenate(here, axis=0))]]
    unnamed x28 -> x80, local copies, waits for them, and re-layouts: 13.2 us -> 17.2 us
    convert_element_type x3, other arithmetic: 0.11 us -> 3.24 us  [shards(): part = shift_chip(part.astype(BF16), -k).astype(F32)]
  transfers between devices with their start and end apart: 31 -> 31, of which waited for: 12 -> 11; matrix products, arithmetic and copies ran while one was open for 14% -> 6% of each run, Pallas kernels for 13% -> 15%
where the time goes in v2:
time: 172 us; the launch traced here: 171 us
  Pallas kernels  68.4 us (40%)
  starting transfers between devices  39.1 us (23%)
  waiting for transfers between devices  34.3 us (20%)
  local copies, waits for them, and re-layouts  19.6 us (11%)
  other arithmetic  8.81 us (5%)
    pallas_call x1, Pallas kernels, place_half(): pl.pallas_call(functools.partial(place_kernel, width), in_specs=[SMEM, an...  33.7 us
    unnamed x80, local copies, waits for them, and re-layouts  17.2 us
    ppermute x6, starting transfers between devices, swap_x(): return lax.ppermute(array, 'seq', [(i, i ^ 1) for i in range(count)])  10.8 us
    ppermute x6, waiting for transfers between devices, shift_chip(): return lax.ppermute(array, 'dp', pairs)  10.6 us
    ppermute x6, starting transfers between devices, shift_chip(): return lax.ppermute(array, 'dp', pairs)  9.88 us
    ppermute x4, starting transfers between devices, shift_seq(): return lax.ppermute(array, 'seq', pairs)  9.85 us
    ppermute x6, waiting for transfers between devices, swap_x(): return lax.ppermute(array, 'seq', [(i, i ^ 1) for i in range(count)])  9.13 us
    pallas_call x4, Pallas kernels, core_sum(): pl.pallas_call(functools.partial(core_sum_kernel, width), in_specs=[VMEM]...  8.47 us
  transfers between devices with their start and end apart: 31, of which 11 were waited for; matrix products, arithmetic and copies ran while one was open for 6% of the time, Pallas kernels for 15%

profile of v2, /device:TPU:0, one launch (start us, length us, event | category | flops | bytes accessed | tf_op | source)
XLA Modules:
  0.0 171.5 jit_solution(3988504176307306231)
XLA Ops:
  0.7 1.1 dynamic-slice_bitcast_fusion.1
  1.8 3.1 %collective-permute-start.1 = (bf16[128,768]{1,0:T(8,128)(2,1)S(1)}, bf16[128,768]{1,0:T(8,128)(2,1)S(1)}, u32[]{:S(2)}, u32[]{:S(2)}) collective-permute-start(bf16[128,768]{1,0:T(8,128)(2,1)S(1)} %get-tuple-element.55), channel_id=1, source_target_pairs={{0,8},{4,12},{8,16},{12,20},{16,24},{20,28},{24,0},{28,4},{1,9},{5... | collective-permute-start | bytes 589832 | tf_op jit(solution)/shard_map/ppermute | solution.py:47
  4.8 2.6 %collective-permute-start.4 = (bf16[128,768]{1,0:T(8,128)(2,1)S(1)}, bf16[128,768]{1,0:T(8,128)(2,1)S(1)}, u32[]{:S(2)}, u32[]{:S(2)}) collective-permute-start(bf16[128,768]{1,0:T(8,128)(2,1)S(1)} %get-tuple-element.55), channel_id=1, source_target_pairs={{0,16},{4,20},{8,24},{12,28},{16,0},{20,4},{24,8},{28,12},{1,17},{... | collective-permute-start | bytes 589832 | tf_op jit(solution)/shard_map/ppermute | solution.py:47
  7.4 1.3 collective-permute-start.7
  10.1 4.7 %split_tokens.1 = (bf16[256,2048]{1,0:T(8,128)(2,1)}, bf16[256,2048]{1,0:T(8,128)(2,1)}) custom-call(s32[16]{0:T(128)} %stack.130.mine_order.order, s32[16]{0:T(128)} %stack.147.other_order.order, bf16[256,4096]{1,0:T(8,128)(2,1)} %bitcast.59), custom_call_target="tpu_custom_call" | custom-call | tf_op jit(solution)/shard_map/split_tokens/pallas_call | solution.py:88
  14.8 1.6 collective-permute-start.10
  16.3 1.5 collective-permute-start.2
  18.6 1.7 collective-permute-done.4.refs_4_
  20.3 1.5 collective-permute-start.5
  23.8 4.3 %collective-permute-done.5.refs_5_ = bf16[128,768]{1,0:T(8,128)(2,1)S(1)} collective-permute-done((bf16[128,768]{1,0:T(8,128)(2,1)S(1)}, bf16[128,768]{1,0:T(8,128)(2,1)S(1)}, u32[]{:S(2)}, u32[]{:S(2)}) %collective-permute-start.5) | collective-permute-done | bytes 196640 | tf_op jit(solution)/shard_map/ppermute | solution.py:35
  29.0 2.3 %collective-permute-done.8.refs_8_ = bf16[128,768]{1,0:T(8,128)(2,1)S(1)} collective-permute-done((bf16[128,768]{1,0:T(8,128)(2,1)}, bf16[128,768]{1,0:T(8,128)(2,1)S(1)}, u32[]{:S(2)}, u32[]{:S(2)}) %collective-permute-start.8) | collective-permute-done | bytes 196640 | tf_op jit(solution)/shard_map/ppermute | solution.py:35
  31.3 1.8 %pad_maximum_fusion.3 = bf16[256,768]{1,0:T(8,128)(2,1)} fusion(bf16[128,768]{1,0:T(8,128)(2,1)S(1)} %collective-permute-done.8.refs_8_, bf16[128,768]{1,0:T(8,128)(2,1)} %collective-permute-done.7.refs_7_), kind=kLoop, calls=%fused_computation.3 | loop fusion | flops 786432 | bytes 786432 | tf_op jit(solution)/shard_map/concatenate | solution.py:335
  33.4 1.5 collective-permute-done.9.refs_9_
  35.0 4.2 %collective-permute-done.10.tokens_ref.other_ref = bf16[256,2048]{1,0:T(8,128)(2,1)S(1)} collective-permute-done((bf16[256,2048]{1,0:T(8,128)(2,1)}, bf16[256,2048]{1,0:T(8,128)(2,1)S(1)}, u32[]{:S(2)}, u32[]{:S(2)}) %collective-permute-start.10) | collective-permute-done | bytes 1048608 | tf_op jit(solution)/shard_map/ppermute | solution.py:28
  43.8 2.0 %project.3 = (bf16[256,512]{1,0:T(8,128)(2,1)S(1)}, bf16[256,256]{1,0:T(8,128)(2,1)S(1)}) custom-call(s32[2]{0:T(128)S(1)} %pad_add_fusion.own_order, bf16[256,2048]{1,0:T(8,128)(2,1)S(1)} %collective-permute-done.10.tokens_ref.other_ref, bf16[512,768]{1,0:T(8,128)(2,1)S(1)} %copy-done.1, bf16[256,768]{1,0:T(8,128)(2,1)S(1)} %collective-permute-done.refs_0_, ...), custom_call_target="tpu_custom_call" | custom-call | tf_op jit(solution)/shard_map/project/pallas_call | solution.py:146
  45.7 1.6 collective-permute-start.12
  47.3 2.0 %project.2 = (f32[256,512]{1,0:T(8,128)S(1)}, f32[256,256]{1,0:T(8,128)S(1)}) custom-call(s32[2]{0:T(128)S(1)} %pad_add_fusion.own_order, bf16[256,2048]{1,0:T(8,128)(2,1)S(1)} %copy-done, bf16[512,768]{1,0:T(8,128)(2,1)S(1)} %copy-done.1, bf16[256,768]{1,0:T(8,128)(2,1)S(1)} %collective-permute-done.refs_0_, bf16[128,768]{1,0:T(8,128)(2,1)S(1)} %copy-done.6, ...), custom_call_target="tpu_custom_call" | custom-call | tf_op jit(solution)/shard_map/project/pallas_call | solution.py:146
  49.9 1.9 %collective-permute-done.12 = bf16[256,256]{1,0:T(8,128)(2,1)S(1)} collective-permute-done((bf16[256,256]{1,0:T(8,128)(2,1)S(1)}, bf16[256,256]{1,0:T(8,128)(2,1)S(1)}, u32[]{:S(2)}, u32[]{:S(2)}) %collective-permute-start.12) | collective-permute-done | bytes 131104 | tf_op jit(solution)/shard_map/ppermute | solution.py:28
  51.9 3.4 %collective-permute-start.13 = (bf16[256,256]{1,0:T(8,128)(2,1)S(1)}, bf16[256,256]{1,0:T(8,128)(2,1)S(1)}, u32[]{:S(2)}, u32[]{:S(2)}) collective-permute-start(bf16[256,256]{1,0:T(8,128)(2,1)S(1)} %add_convert_fusion.4.refs_2_), channel_id=1, source_target_pairs={{0,2},{1,3},{4,6},{5,7},{8,10},{9,11},{12,14},{13,15},{16,18},{17,... | collective-permute-start | bytes 393224 | tf_op jit(solution)/shard_map/ppermute | solution.py:53
  55.3 3.7 %collective-permute-start.14 = (bf16[256,256]{1,0:T(8,128)(2,1)S(1)}, bf16[256,256]{1,0:T(8,128)(2,1)S(1)}, u32[]{:S(2)}, u32[]{:S(2)}) collective-permute-start(bf16[256,256]{1,0:T(8,128)(2,1)S(1)} %add_convert_fusion.4.refs_2_), channel_id=1, source_target_pairs={{0,1},{1,2},{2,3},{4,5},{5,6},{6,7},{8,9},{9,10},{10,11},{12,13},{... | collective-permute-start | bytes 393224 | tf_op jit(solution)/shard_map/ppermute | solution.py:53
  59.1 2.4 %collective-permute-done.14.refs_1_ = bf16[256,256]{1,0:T(8,128)(2,1)S(1)} collective-permute-done((bf16[256,256]{1,0:T(8,128)(2,1)S(1)}, bf16[256,256]{1,0:T(8,128)(2,1)S(1)}, u32[]{:S(2)}, u32[]{:S(2)}) %collective-permute-start.14) | collective-permute-done | bytes 131104 | tf_op jit(solution)/shard_map/ppermute | solution.py:53
  61.5 6.3 %attend.1 = (bf16[256,512]{1,0:T(8,128)(2,1)}, bf16[256,512]{1,0:T(8,128)(2,1)S(1)}, f32[256,256]{1,0:T(8,128)S(1)}, bf16[512,256]{1,0:T(8,128)(2,1)S(1)}) custom-call(s32[1]{0:T(128)} %bitcast.place_ref, s32[8]{0:T(128)S(1)} %bitcast.57, f32[256,512]{1,0:T(8,128)S(1)} %get-tuple-element.30.q_ref, bf16[256,512]{1,0:T(8,128)(2,1)S(1)} %collective-permute-done.11.q_from_ref, ...), custom_call_target="tpu_custom_call" | custom-call | tf_op jit(solution)/shard_map/attend/pallas_call | solution.py:288
  67.8 1.3 collective-permute-start.16
  69.1 1.5 collective-permute-start.17
  70.6 3.1 %collective-permute-start.15 = (bf16[256,512]{1,0:T(8,128)(2,1)S(1)}, bf16[256,512]{1,0:T(8,128)(2,1)S(1)}, u32[]{:S(2)}, u32[]{:S(2)}) collective-permute-start(bf16[256,512]{1,0:T(8,128)(2,1)S(1)} %get-tuple-element.36.dquery_ref.dq_ref), channel_id=1, source_target_pairs={{0,1},{1,0},{2,3},{3,2},{4,5},{5,4},{6,7},{7,6},{8,9},{9,8},{10,11... | collective-permute-start | bytes 786440 | tf_op jit(solution)/shard_map/ppermute | solution.py:28
  73.7 2.5 %collective-permute-done.16 = bf16[256,256]{1,0:T(8,128)(2,1)S(1)} collective-permute-done((bf16[256,256]{1,0:T(8,128)(2,1)S(1)}, bf16[256,256]{1,0:T(8,128)(2,1)S(1)}, u32[]{:S(2)}, u32[]{:S(2)}) %collective-permute-start.16) | collective-permute-done | bytes 131104 | tf_op jit(solution)/shard_map/ppermute | solution.py:53
  76.2 1.6 collective-permute-done.17
  77.9 2.0 %collective-permute-start.18 = (bf16[256,256]{1,0:T(8,128)(2,1)S(1)}, bf16[256,256]{1,0:T(8,128)(2,1)S(1)}, u32[]{:S(2)}, u32[]{:S(2)}) collective-permute-start(bf16[256,256]{1,0:T(8,128)(2,1)S(1)} %add_convert_fusion.3.dpair_ref.dp_ref), channel_id=1, source_target_pairs={{0,1},{1,0},{2,3},{3,2},{4,5},{5,4},{6,7},{7,6},{8,9},{9,8},{10,11... | collective-permute-start | bytes 393224 | tf_op jit(solution)/shard_map/ppermute | solution.py:28
  79.9 3.0 %collective-permute-done.18.dpair_ref.dp_other_ref = bf16[256,256]{1,0:T(8,128)(2,1)S(1)} collective-permute-done((bf16[256,256]{1,0:T(8,128)(2,1)S(1)}, bf16[256,256]{1,0:T(8,128)(2,1)S(1)}, u32[]{:S(2)}, u32[]{:S(2)}) %collective-permute-start.18) | collective-permute-done | bytes 131104 | tf_op jit(solution)/shard_map/ppermute | solution.py:28
  84.6 1.4 weight_terms.5
  87.3 1.4 weight_terms.6
  89.7 1.4 weight_terms.7
  93.2 2.1 %core_sum.4 = (f32[128,768]{1,0:T(8,128)}, bf16[128,768]{1,0:T(8,128)(2,1)}) custom-call(f32[256,768]{1,0:T(8,128)} %copy-done.33, bf16[256,768]{1,0:T(8,128)(2,1)} %copy-done.37), custom_call_target="tpu_custom_call" | custom-call | tf_op jit(solution)/shard_map/core_sum/pallas_call | solution.py:225
  95.3 1.0 copy-done.3
  101.9 2.9 %width_grad.2 = bf16[256,2048]{1,0:T(8,128)(2,1)} custom-call(s32[2]{0:T(128)S(1)} %pad_add_fusion.own_order, s32[16]{0:T(128)S(1)} %copy-done.34, bf16[256,512]{1,0:T(8,128)(2,1)S(1)} %collective-permute-done.15.dquery_ref.dq_other_ref, bf16[256,256]{1,0:T(8,128)(2,1)S(1)} %copy-done.29, bf16[512,768]{1,0:T(8,128)(2,1)S(1)} %copy-done.1, ...), custom_call_target="tpu_custom_call" | custom-call | tf_op jit(solution)/shard_map/width_grad/pallas_call | solution.py:177
  104.8 1.9 %collective-permute-start.19 = (bf16[256,2048]{1,0:T(8,128)(2,1)}, bf16[256,2048]{1,0:T(8,128)(2,1)}, u32[]{:S(2)}, u32[]{:S(2)}) collective-permute-start(bf16[256,2048]{1,0:T(8,128)(2,1)} %width_grad.2), channel_id=1, source_target_pairs={{0,1},{1,0},{2,3},{3,2},{4,5},{5,4},{6,7},{7,6},{8,9},{9,8},{10,11... | collective-permute-start | bytes 3145736 | tf_op jit(solution)/shard_map/ppermute | solution.py:28
  106.7 2.1 %core_sum.5 = (f32[128,768]{1,0:T(8,128)}, bf16[128,768]{1,0:T(8,128)(2,1)}) custom-call(f32[256,768]{1,0:T(8,128)} %copy-done.32, bf16[256,768]{1,0:T(8,128)(2,1)} %collective-permute-done.23.from_ref), custom_call_target="tpu_custom_call" | custom-call | tf_op jit(solution)/shard_map/core_sum/pallas_call | solution.py:225
  108.8 2.0 %collective-permute-start.24 = (bf16[128,768]{1,0:T(8,128)(2,1)}, bf16[128,768]{1,0:T(8,128)(2,1)}, u32[]{:S(2)}, u32[]{:S(2)}) collective-permute-start(bf16[128,768]{1,0:T(8,128)(2,1)} %get-tuple-element.46), channel_id=1, source_target_pairs={{0,2},{1,3},{2,0},{3,1},{4,6},{5,7},{6,4},{7,5},{8,10},{9,11},{10,... | collective-permute-start | bytes 589832 | tf_op jit(solution)/shard_map/ppermute | solution.py:35
  110.9 2.2 %core_sum.6 = (f32[128,768]{1,0:T(8,128)}, bf16[128,768]{1,0:T(8,128)(2,1)}) custom-call(f32[256,768]{1,0:T(8,128)} %copy-done.31, bf16[256,768]{1,0:T(8,128)(2,1)} %collective-permute-done.26.from_ref), custom_call_target="tpu_custom_call" | custom-call | tf_op jit(solution)/shard_map/core_sum/pallas_call | solution.py:225
  113.1 2.1 %core_sum.7 = (f32[128,768]{1,0:T(8,128)}, bf16[128,768]{1,0:T(8,128)(2,1)}) custom-call(f32[256,768]{1,0:T(8,128)} %copy-done.30, bf16[256,768]{1,0:T(8,128)(2,1)} %collective-permute-done.29.from_ref), custom_call_target="tpu_custom_call" | custom-call | tf_op jit(solution)/shard_map/core_sum/pallas_call | solution.py:225
  115.2 2.0 %collective-permute-start.30 = (bf16[128,768]{1,0:T(8,128)(2,1)}, bf16[128,768]{1,0:T(8,128)(2,1)S(1)}, u32[]{:S(2)}, u32[]{:S(2)}) collective-permute-start(bf16[128,768]{1,0:T(8,128)(2,1)} %get-tuple-element.54), channel_id=1, source_target_pairs={{0,2},{1,3},{2,0},{3,1},{4,6},{5,7},{6,4},{7,5},{8,10},{9,11},{10,... | collective-permute-start | bytes 589832 | tf_op jit(solution)/shard_map/ppermute | solution.py:35
  117.2 1.1 add_convert_fusion.2
  118.9 1.1 add_convert_fusion.1
  119.9 1.9 %collective-permute-start.25 = (bf16[128,768]{1,0:T(8,128)(2,1)S(1)}, bf16[128,768]{1,0:T(8,128)(2,1)S(1)}, u32[]{:S(2)}, u32[]{:S(2)}) collective-permute-start(bf16[128,768]{1,0:T(8,128)(2,1)S(1)} %add_convert_fusion.1), channel_id=1, source_target_pairs={{0,16},{4,20},{8,24},{12,28},{16,0},{20,4},{24,8},{28,12},{1,17},{... | collective-permute-start | bytes 589832 | tf_op jit(solution)/shard_map/ppermute | solution.py:47
  121.9 1.1 add_convert_fusion
  124.3 3.6 %width_grad.3.base_ref = bf16[256,4096]{1,0:T(8,128)(2,1)} custom-call(s32[2]{0:T(128)S(1)} %pad_add_fusion.own_order, s32[16]{0:T(128)S(1)} %copy-done.34, bf16[256,512]{1,0:T(8,128)(2,1)S(1)} %get-tuple-element.36.dquery_ref.dq_ref, bf16[256,256]{1,0:T(8,128)(2,1)S(1)} %copy-done.27, bf16[512,768]{1,0:T(8,128)(2,1)S(1)} %copy-done.1, ...), custom_call_target="tpu_custom_call" | custom-call | tf_op jit(solution)/shard_map/width_grad/pallas_call | solution.py:177
  127.8 8.9 %collective-permute-done.25 = bf16[128,768]{1,0:T(8,128)(2,1)S(1)} collective-permute-done((bf16[128,768]{1,0:T(8,128)(2,1)S(1)}, bf16[128,768]{1,0:T(8,128)(2,1)S(1)}, u32[]{:S(2)}, u32[]{:S(2)}) %collective-permute-start.25) | collective-permute-done | bytes 196640 | tf_op jit(solution)/shard_map/ppermute | solution.py:47
  137.6 33.7 %place_half.1 = bf16[256,4096]{1,0:T(8,128)(2,1)} custom-call(s32[16]{0:T(128)} %stack.147.other_order.order, bf16[256,2048]{1,0:T(8,128)(2,1)} %collective-permute-done.19.half_ref, bf16[256,4096]{1,0:T(8,128)(2,1)} %width_grad.3.base_ref), custom_call_target="tpu_custom_call", output_to_operand_aliasing={{}: (2, {})} | custom-call | tf_op jit(solution)/shard_map/place_half/pallas_call | solution.py:114
  (130 shorter events, 25.2 us)
Async XLA Ops:
  1.8 14.6 %collective-permute-start.1 = (bf16[128,768]{1,0:T(8,128)(2,1)S(1)}, bf16[128,768]{1,0:T(8,128)(2,1)S(1)}, u32[]{:S(2)}, u32[]{:S(2)}) collective-permute-start(bf16[128,768]{1,0:T(8,128)(2,1)S(1)} %get-tuple-element.55), channel_id=1, source_target_pairs={{0,8},{4,12},{8,16},{12,20},{16,24},{20,28},{24,0},{28,4},{1,9},{5... | collective-permute-start | bytes 589832 | tf_op jit(solution)/shard_map/ppermute | solution.py:47
  4.8 15.5 %collective-permute-start.4 = (bf16[128,768]{1,0:T(8,128)(2,1)S(1)}, bf16[128,768]{1,0:T(8,128)(2,1)S(1)}, u32[]{:S(2)}, u32[]{:S(2)}) collective-permute-start(bf16[128,768]{1,0:T(8,128)(2,1)S(1)} %get-tuple-element.55), channel_id=1, source_target_pairs={{0,16},{4,20},{8,24},{12,28},{16,0},{20,4},{24,8},{28,12},{1,17},{... | collective-permute-start | bytes 589832 | tf_op jit(solution)/shard_map/ppermute | solution.py:47
  7.4 14.4 %collective-permute-start.7 = (bf16[128,768]{1,0:T(8,128)(2,1)S(1)}, bf16[128,768]{1,0:T(8,128)(2,1)}, u32[]{:S(2)}, u32[]{:S(2)}) collective-permute-start(bf16[128,768]{1,0:T(8,128)(2,1)S(1)} %get-tuple-element.55), channel_id=1, source_target_pairs={{0,24},{4,28},{8,0},{12,4},{16,8},{20,12},{24,16},{28,20},{1,25},{... | collective-permute-start | bytes 589832 | tf_op jit(solution)/shard_map/ppermute | solution.py:47
  14.8 18.3 %copy-start.35 = (s32[1,8]{1,0:T(1,128)S(1)}, s32[1,8]{1,0:T(1,128)}, u32[]{:S(2)}) copy-start(s32[1,8]{1,0:T(1,128)} %param.8) | copy-start | bytes 100
  14.8 18.5 %copy-start.39 = (s32[1,8]{1,0:T(1,128)S(1)}, s32[1,8]{1,0:T(1,128)}, u32[]{:S(2)}) copy-start(s32[1,8]{1,0:T(1,128)} %param.9) | copy-start | bytes 100
  14.8 24.3 %copy-start.1 = (bf16[512,768]{1,0:T(8,128)(2,1)S(1)}, bf16[512,768]{1,0:T(8,128)(2,1)}, u32[]{:S(2)}) copy-start(bf16[512,768]{1,0:T(8,128)(2,1)} %own_ref.7) | copy-start | bytes 2359300
  14.8 24.3 %collective-permute-start.10 = (bf16[256,2048]{1,0:T(8,128)(2,1)}, bf16[256,2048]{1,0:T(8,128)(2,1)S(1)}, u32[]{:S(2)}, u32[]{:S(2)}) collective-permute-start(bf16[256,2048]{1,0:T(8,128)(2,1)} %get-tuple-element.31), channel_id=1, source_target_pairs={{0,1},{1,0},{2,3},{3,2},{4,5},{5,4},{6,7},{7,6},{8,9},{9,8},{10,11... | collective-permute-start | bytes 3145736 | tf_op jit(solution)/shard_map/ppermute | solution.py:28
  16.3 14.9 %copy-start.5 = (bf16[128,768]{1,0:T(8,128)(2,1)}, bf16[128,768]{1,0:T(8,128)(2,1)S(1)}, u32[]{:S(2)}) copy-start(bf16[128,768]{1,0:T(8,128)(2,1)S(1)} %collective-permute-done.1.refs_1_) | copy-start | bytes 589828
  16.3 6.0 %collective-permute-start.2 = (bf16[128,768]{1,0:T(8,128)(2,1)S(1)}, bf16[128,768]{1,0:T(8,128)(2,1)S(1)}, u32[]{:S(2)}, u32[]{:S(2)}) collective-permute-start(bf16[128,768]{1,0:T(8,128)(2,1)S(1)} %collective-permute-done.1.refs_1_), channel_id=1, source_target_pairs={{0,2},{1,3},{2,0},{3,1},{4,6},{5,7},{6,4},{7,5},{8,10},{9,11},{10,... | collective-permute-start | bytes 589832 | tf_op jit(solution)/shard_map/ppermute | solution.py:35
  18.6 14.8 %collective-permute-start = (bf16[256,768]{1,0:T(8,128)(2,1)}, bf16[256,768]{1,0:T(8,128)(2,1)S(1)}, u32[]{:S(2)}, u32[]{:S(2)}) collective-permute-start(bf16[256,768]{1,0:T(8,128)(2,1)} %pad_maximum_fusion), channel_id=1, source_target_pairs={{0,4},{4,0},{8,12},{12,8},{16,20},{20,16},{24,28},{28,24},{1,5},{5... | collective-permute-start | bytes 1179656 | tf_op jit(solution)/shard_map/ppermute | solution.py:40
  20.3 11.0 %copy-start.9 = (bf16[128,768]{1,0:T(8,128)(2,1)}, bf16[128,768]{1,0:T(8,128)(2,1)S(1)}, u32[]{:S(2)}) copy-start(bf16[128,768]{1,0:T(8,128)(2,1)S(1)} %collective-permute-done.4.refs_4_) | copy-start | bytes 589828
  20.3 7.8 %collective-permute-start.5 = (bf16[128,768]{1,0:T(8,128)(2,1)S(1)}, bf16[128,768]{1,0:T(8,128)(2,1)S(1)}, u32[]{:S(2)}, u32[]{:S(2)}) collective-permute-start(bf16[128,768]{1,0:T(8,128)(2,1)S(1)} %collective-permute-done.4.refs_4_), channel_id=1, source_target_pairs={{0,2},{1,3},{2,0},{3,1},{4,6},{5,7},{6,4},{7,5},{8,10},{9,11},{10,... | collective-permute-start | bytes 589832 | tf_op jit(solution)/shard_map/ppermute | solution.py:35
  21.8 9.4 %collective-permute-start.8 = (bf16[128,768]{1,0:T(8,128)(2,1)}, bf16[128,768]{1,0:T(8,128)(2,1)S(1)}, u32[]{:S(2)}, u32[]{:S(2)}) collective-permute-start(bf16[128,768]{1,0:T(8,128)(2,1)} %collective-permute-done.7.refs_7_), channel_id=1, source_target_pairs={{0,2},{1,3},{2,0},{3,1},{4,6},{5,7},{6,4},{7,5},{8,10},{9,11},{10,... | collective-permute-start | bytes 589832 | tf_op jit(solution)/shard_map/ppermute | solution.py:35
  23.8 9.6 %collective-permute-start.3 = (bf16[256,768]{1,0:T(8,128)(2,1)}, bf16[256,768]{1,0:T(8,128)(2,1)S(1)}, u32[]{:S(2)}, u32[]{:S(2)}) collective-permute-start(bf16[256,768]{1,0:T(8,128)(2,1)} %pad_maximum_fusion.1), channel_id=1, source_target_pairs={{0,4},{4,0},{8,12},{12,8},{16,20},{20,16},{24,28},{28,24},{1,5},{5... | collective-permute-start | bytes 1179656 | tf_op jit(solution)/shard_map/ppermute | solution.py:40
  29.0 4.5 %collective-permute-start.6 = (bf16[256,768]{1,0:T(8,128)(2,1)}, bf16[256,768]{1,0:T(8,128)(2,1)S(1)}, u32[]{:S(2)}, u32[]{:S(2)}) collective-permute-start(bf16[256,768]{1,0:T(8,128)(2,1)} %pad_maximum_fusion.2), channel_id=1, source_target_pairs={{0,4},{4,0},{8,12},{12,8},{16,20},{20,16},{24,28},{28,24},{1,5},{5... | collective-permute-start | bytes 1179656 | tf_op jit(solution)/shard_map/ppermute | solution.py:40
  33.0 1.9 %collective-permute-start.9 = (bf16[256,768]{1,0:T(8,128)(2,1)}, bf16[256,768]{1,0:T(8,128)(2,1)S(1)}, u32[]{:S(2)}, u32[]{:S(2)}) collective-permute-start(bf16[256,768]{1,0:T(8,128)(2,1)} %pad_maximum_fusion.3), channel_id=1, source_target_pairs={{0,4},{4,0},{8,12},{12,8},{16,20},{20,16},{24,28},{28,24},{1,5},{5... | collective-permute-start | bytes 1179656 | tf_op jit(solution)/shard_map/ppermute | solution.py:40
  33.4 13.9 %copy-start = (bf16[256,2048]{1,0:T(8,128)(2,1)S(1)}, bf16[256,2048]{1,0:T(8,128)(2,1)}, u32[]{:S(2)}) copy-start(bf16[256,2048]{1,0:T(8,128)(2,1)} %get-tuple-element.29.tokens_ref) | copy-start | bytes 3145732
  35.0 12.3 %copy-start.2 = (bf16[256,768]{1,0:T(8,128)(2,1)}, bf16[256,768]{1,0:T(8,128)(2,1)S(1)}, u32[]{:S(2)}) copy-start(bf16[256,768]{1,0:T(8,128)(2,1)S(1)} %collective-permute-done.9.refs_9_) | copy-start | bytes 1179652
  45.7 6.1 %collective-permute-start.12 = (bf16[256,256]{1,0:T(8,128)(2,1)S(1)}, bf16[256,256]{1,0:T(8,128)(2,1)S(1)}, u32[]{:S(2)}, u32[]{:S(2)}) collective-permute-start(bf16[256,256]{1,0:T(8,128)(2,1)S(1)} %get-tuple-element.34), channel_id=1, source_target_pairs={{0,1},{1,0},{2,3},{3,2},{4,5},{5,4},{6,7},{7,6},{8,9},{9,8},{10,11... | collective-permute-start | bytes 393224 | tf_op jit(solution)/shard_map/ppermute | solution.py:28
  47.3 11.7 %copy-start.38 = (bf16[1,256,512]{2,1,0:T(8,128)(2,1)S(1)}, bf16[1,256,512]{2,1,0:T(8,128)(2,1)}, u32[]{:S(2)}) copy-start(bf16[1,256,512]{2,1,0:T(8,128)(2,1)} %param.7) | copy-start | bytes 786436
  49.3 12.2 %collective-permute-start.11 = (bf16[256,512]{1,0:T(8,128)(2,1)S(1)}, bf16[256,512]{1,0:T(8,128)(2,1)S(1)}, u32[]{:S(2)}, u32[]{:S(2)}) collective-permute-start(bf16[256,512]{1,0:T(8,128)(2,1)S(1)} %get-tuple-element.32), channel_id=1, source_target_pairs={{0,1},{1,0},{2,3},{3,2},{4,5},{5,4},{6,7},{7,6},{8,9},{9,8},{10,11... | collective-permute-start | bytes 786440 | tf_op jit(solution)/shard_map/ppermute | solution.py:28
  51.9 7.2 %collective-permute-start.13 = (bf16[256,256]{1,0:T(8,128)(2,1)S(1)}, bf16[256,256]{1,0:T(8,128)(2,1)S(1)}, u32[]{:S(2)}, u32[]{:S(2)}) collective-permute-start(bf16[256,256]{1,0:T(8,128)(2,1)S(1)} %add_convert_fusion.4.refs_2_), channel_id=1, source_target_pairs={{0,2},{1,3},{4,6},{5,7},{8,10},{9,11},{12,14},{13,15},{16,18},{17,... | collective-permute-start | bytes 393224 | tf_op jit(solution)/shard_map/ppermute | solution.py:53
  55.3 6.2 %collective-permute-start.14 = (bf16[256,256]{1,0:T(8,128)(2,1)S(1)}, bf16[256,256]{1,0:T(8,128)(2,1)S(1)}, u32[]{:S(2)}, u32[]{:S(2)}) collective-permute-start(bf16[256,256]{1,0:T(8,128)(2,1)S(1)} %add_convert_fusion.4.refs_2_), channel_id=1, source_target_pairs={{0,1},{1,2},{2,3},{4,5},{5,6},{6,7},{8,9},{9,10},{10,11},{12,13},{... | collective-permute-start | bytes 393224 | tf_op jit(solution)/shard_map/ppermute | solution.py:53
  67.8 8.4 %collective-permute-start.16 = (bf16[256,256]{1,0:T(8,128)(2,1)S(1)}, bf16[256,256]{1,0:T(8,128)(2,1)S(1)}, u32[]{:S(2)}, u32[]{:S(2)}) collective-permute-start(bf16[256,256]{1,0:T(8,128)(2,1)S(1)} %get-tuple-element.57), channel_id=1, source_target_pairs={{1,0},{2,1},{3,2},{5,4},{6,5},{7,6},{9,8},{10,9},{11,10},{13,12},{... | collective-permute-start | bytes 393224 | tf_op jit(solution)/shard_map/ppermute | solution.py:53
  69.1 8.7 %collective-permute-start.17 = (bf16[256,256]{1,0:T(8,128)(2,1)S(1)}, bf16[256,256]{1,0:T(8,128)(2,1)S(1)}, u32[]{:S(2)}, u32[]{:S(2)}) collective-permute-start(bf16[256,256]{1,0:T(8,128)(2,1)S(1)} %get-tuple-element.58), channel_id=1, source_target_pairs={{2,0},{3,1},{6,4},{7,5},{10,8},{11,9},{14,12},{15,13},{18,16},{19,... | collective-permute-start | bytes 393224 | tf_op jit(solution)/shard_map/ppermute | solution.py:53
  70.6 12.4 %collective-permute-start.15 = (bf16[256,512]{1,0:T(8,128)(2,1)S(1)}, bf16[256,512]{1,0:T(8,128)(2,1)S(1)}, u32[]{:S(2)}, u32[]{:S(2)}) collective-permute-start(bf16[256,512]{1,0:T(8,128)(2,1)S(1)} %get-tuple-element.36.dquery_ref.dq_ref), channel_id=1, source_target_pairs={{0,1},{1,0},{2,3},{3,2},{4,5},{5,4},{6,7},{7,6},{8,9},{9,8},{10,11... | collective-permute-start | bytes 786440 | tf_op jit(solution)/shard_map/ppermute | solution.py:28
  77.9 11.8 %copy-start.26 = (bf16[256,256]{1,0:T(8,128)(2,1)}, bf16[256,256]{1,0:T(8,128)(2,1)S(1)}, u32[]{:S(2)}) copy-start(bf16[256,256]{1,0:T(8,128)(2,1)S(1)} %add_convert_fusion.3.dpair_ref.dp_ref) | copy-start | bytes 393220
  77.9 5.0 %collective-permute-start.18 = (bf16[256,256]{1,0:T(8,128)(2,1)S(1)}, bf16[256,256]{1,0:T(8,128)(2,1)S(1)}, u32[]{:S(2)}, u32[]{:S(2)}) collective-permute-start(bf16[256,256]{1,0:T(8,128)(2,1)S(1)} %add_convert_fusion.3.dpair_ref.dp_ref), channel_id=1, source_target_pairs={{0,1},{1,0},{2,3},{3,2},{4,5},{5,4},{6,7},{7,6},{8,9},{9,8},{10,11... | collective-permute-start | bytes 393224 | tf_op jit(solution)/shard_map/ppermute | solution.py:28
  83.0 6.7 %copy-start.28 = (bf16[256,256]{1,0:T(8,128)(2,1)}, bf16[256,256]{1,0:T(8,128)(2,1)S(1)}, u32[]{:S(2)}) copy-start(bf16[256,256]{1,0:T(8,128)(2,1)S(1)} %collective-permute-done.18.dpair_ref.dp_other_ref) | copy-start | bytes 393220
  84.6 7.9 %collective-permute-start.20 = (bf16[256,768]{1,0:T(8,128)(2,1)S(1)}, bf16[256,768]{1,0:T(8,128)(2,1)S(1)}, u32[]{:S(2)}, u32[]{:S(2)}) collective-permute-start(bf16[256,768]{1,0:T(8,128)(2,1)S(1)} %get-tuple-element.40), channel_id=1, source_target_pairs={{0,4},{4,0},{8,12},{12,8},{16,20},{20,16},{24,28},{28,24},{1,5},{5... | collective-permute-start | bytes 1179656 | tf_op jit(solution)/shard_map/ppermute | solution.py:40
  86.8 19.9 %collective-permute-start.23 = (bf16[256,768]{1,0:T(8,128)(2,1)}, bf16[256,768]{1,0:T(8,128)(2,1)}, u32[]{:S(2)}, u32[]{:S(2)}) collective-permute-start(bf16[256,768]{1,0:T(8,128)(2,1)} %get-tuple-element.44), channel_id=1, source_target_pairs={{0,4},{4,0},{8,12},{12,8},{16,20},{20,16},{24,28},{28,24},{1,5},{5... | collective-permute-start | bytes 1179656 | tf_op jit(solution)/shard_map/ppermute | solution.py:40
  89.7 21.2 %collective-permute-start.26 = (bf16[256,768]{1,0:T(8,128)(2,1)}, bf16[256,768]{1,0:T(8,128)(2,1)}, u32[]{:S(2)}, u32[]{:S(2)}) collective-permute-start(bf16[256,768]{1,0:T(8,128)(2,1)} %get-tuple-element.48), channel_id=1, source_target_pairs={{0,4},{4,0},{8,12},{12,8},{16,20},{20,16},{24,28},{28,24},{1,5},{5... | collective-permute-start | bytes 1179656 | tf_op jit(solution)/shard_map/ppermute | solution.py:40
  92.0 21.1 %collective-permute-start.29 = (bf16[256,768]{1,0:T(8,128)(2,1)}, bf16[256,768]{1,0:T(8,128)(2,1)}, u32[]{:S(2)}, u32[]{:S(2)}) collective-permute-start(bf16[256,768]{1,0:T(8,128)(2,1)} %get-tuple-element.52), channel_id=1, source_target_pairs={{0,4},{4,0},{8,12},{12,8},{16,20},{20,16},{24,28},{28,24},{1,5},{5... | collective-permute-start | bytes 1179656 | tf_op jit(solution)/shard_map/ppermute | solution.py:40
  95.3 21.9 %collective-permute-start.21 = (bf16[128,768]{1,0:T(8,128)(2,1)}, bf16[128,768]{1,0:T(8,128)(2,1)}, u32[]{:S(2)}, u32[]{:S(2)}) collective-permute-start(bf16[128,768]{1,0:T(8,128)(2,1)} %get-tuple-element.42), channel_id=1, source_target_pairs={{0,2},{1,3},{2,0},{3,1},{4,6},{5,7},{6,4},{7,5},{8,10},{9,11},{10,... | collective-permute-start | bytes 589832 | tf_op jit(solution)/shard_map/ppermute | solution.py:35
  104.8 32.8 %collective-permute-start.19 = (bf16[256,2048]{1,0:T(8,128)(2,1)}, bf16[256,2048]{1,0:T(8,128)(2,1)}, u32[]{:S(2)}, u32[]{:S(2)}) collective-permute-start(bf16[256,2048]{1,0:T(8,128)(2,1)} %width_grad.2), channel_id=1, source_target_pairs={{0,1},{1,0},{2,3},{3,2},{4,5},{5,4},{6,7},{7,6},{8,9},{9,8},{10,11... | collective-permute-start | bytes 3145736 | tf_op jit(solution)/shard_map/ppermute | solution.py:28
  108.8 10.0 %collective-permute-start.24 = (bf16[128,768]{1,0:T(8,128)(2,1)}, bf16[128,768]{1,0:T(8,128)(2,1)}, u32[]{:S(2)}, u32[]{:S(2)}) collective-permute-start(bf16[128,768]{1,0:T(8,128)(2,1)} %get-tuple-element.46), channel_id=1, source_target_pairs={{0,2},{1,3},{2,0},{3,1},{4,6},{5,7},{6,4},{7,5},{8,10},{9,11},{10,... | collective-permute-start | bytes 589832 | tf_op jit(solution)/shard_map/ppermute | solution.py:35
  110.9 12.5 %copy-start.4 = (bf16[256,768]{1,0:T(8,128)(2,1)S(1)}, bf16[256,768]{1,0:T(8,128)(2,1)}, u32[]{:S(2)}) copy-start(bf16[256,768]{1,0:T(8,128)(2,1)} %copy-done.2) | copy-start | bytes 1179652
  110.9 12.5 %copy-start.8 = (bf16[128,768]{1,0:T(8,128)(2,1)S(1)}, bf16[128,768]{1,0:T(8,128)(2,1)}, u32[]{:S(2)}) copy-start(bf16[128,768]{1,0:T(8,128)(2,1)} %copy-done.5) | copy-start | bytes 589828
  110.9 12.5 %copy-start.12 = (bf16[128,768]{1,0:T(8,128)(2,1)S(1)}, bf16[128,768]{1,0:T(8,128)(2,1)}, u32[]{:S(2)}) copy-start(bf16[128,768]{1,0:T(8,128)(2,1)} %copy-done.9) | copy-start | bytes 589828
  110.9 12.5 %copy-start.16 = (bf16[128,768]{1,0:T(8,128)(2,1)S(1)}, bf16[128,768]{1,0:T(8,128)(2,1)}, u32[]{:S(2)}) copy-start(bf16[128,768]{1,0:T(8,128)(2,1)} %copy-done.13) | copy-start | bytes 589828
  110.9 12.5 %copy-start.21 = (bf16[128,768]{1,0:T(8,128)(2,1)S(1)}, bf16[128,768]{1,0:T(8,128)(2,1)}, u32[]{:S(2)}) copy-start(bf16[128,768]{1,0:T(8,128)(2,1)} %copy-done.17) | copy-start | bytes 589828
  113.1 8.8 %collective-permute-start.27 = (bf16[128,768]{1,0:T(8,128)(2,1)}, bf16[128,768]{1,0:T(8,128)(2,1)}, u32[]{:S(2)}, u32[]{:S(2)}) collective-permute-start(bf16[128,768]{1,0:T(8,128)(2,1)} %get-tuple-element.50), channel_id=1, source_target_pairs={{0,2},{1,3},{2,0},{3,1},{4,6},{5,7},{6,4},{7,5},{8,10},{9,11},{10,... | collective-permute-start | bytes 589832 | tf_op jit(solution)/shard_map/ppermute | solution.py:35
  115.2 8.2 %copy-start.25 = (bf16[128,768]{1,0:T(8,128)(2,1)S(1)}, bf16[128,768]{1,0:T(8,128)(2,1)}, u32[]{:S(2)}) copy-start(bf16[128,768]{1,0:T(8,128)(2,1)} %copy-done.22) | copy-start | bytes 589828
  115.2 12.7 %collective-permute-start.30 = (bf16[128,768]{1,0:T(8,128)(2,1)}, bf16[128,768]{1,0:T(8,128)(2,1)S(1)}, u32[]{:S(2)}, u32[]{:S(2)}) collective-permute-start(bf16[128,768]{1,0:T(8,128)(2,1)} %get-tuple-element.54), channel_id=1, source_target_pairs={{0,2},{1,3},{2,0},{3,1},{4,6},{5,7},{6,4},{7,5},{8,10},{9,11},{10,... | collective-permute-start | bytes 589832 | tf_op jit(solution)/shard_map/ppermute | solution.py:35
  118.3 9.6 %collective-permute-start.22 = (bf16[128,768]{1,0:T(8,128)(2,1)S(1)}, bf16[128,768]{1,0:T(8,128)(2,1)S(1)}, u32[]{:S(2)}, u32[]{:S(2)}) collective-permute-start(bf16[128,768]{1,0:T(8,128)(2,1)S(1)} %add_convert_fusion.2), channel_id=1, source_target_pairs={{0,24},{4,28},{8,0},{12,4},{16,8},{20,12},{24,16},{28,20},{1,25},{... | collective-permute-start | bytes 589832 | tf_op jit(solution)/shard_map/ppermute | solution.py:47
  119.9 16.8 %collective-permute-start.25 = (bf16[128,768]{1,0:T(8,128)(2,1)S(1)}, bf16[128,768]{1,0:T(8,128)(2,1)S(1)}, u32[]{:S(2)}, u32[]{:S(2)}) collective-permute-start(bf16[128,768]{1,0:T(8,128)(2,1)S(1)} %add_convert_fusion.1), channel_id=1, source_target_pairs={{0,16},{4,20},{8,24},{12,28},{16,0},{20,4},{24,8},{28,12},{1,17},{... | collective-permute-start | bytes 589832 | tf_op jit(solution)/shard_map/ppermute | solution.py:47
  123.0 13.8 %collective-permute-start.28 = (bf16[128,768]{1,0:T(8,128)(2,1)S(1)}, bf16[128,768]{1,0:T(8,128)(2,1)S(1)}, u32[]{:S(2)}, u32[]{:S(2)}) collective-permute-start(bf16[128,768]{1,0:T(8,128)(2,1)S(1)} %add_convert_fusion), channel_id=1, source_target_pairs={{0,8},{4,12},{8,16},{12,20},{16,24},{20,28},{24,0},{28,4},{1,9},{5... | collective-permute-start | bytes 589832 | tf_op jit(solution)/shard_map/ppermute | solution.py:47
  124.3 12.5 %copy-start.36 = (f32[128,768]{1,0:T(8,128)S(1)}, f32[128,768]{1,0:T(8,128)}, u32[]{:S(2)}) copy-start(f32[128,768]{1,0:T(8,128)} %get-tuple-element.53) | copy-start | bytes 1179652
  (23 other events, 33.1 us)

commit v3 on v1

v3 whole, which is shorter than its diff:
```python
import functools
import math

import jax
import jax.numpy as jnp
from jax import lax
from jax.experimental import pallas as pl
from jax.experimental.pallas import tpu as pltpu
from jax.sharding import PartitionSpec as P

HEAD_DIM = 128
PAIR = 2
CORES = 2
BF16 = jnp.bfloat16
F32 = jnp.float32
NT = (((1,), (1,)), ((), ()))
TN = (((0,), (0,)), ((), ()))
VMEM = pl.BlockSpec(memory_space=pltpu.VMEM)
SMEM = pl.BlockSpec(memory_space=pltpu.SMEM)


def dot(a, b, dims=(((1,), (0,)), ((), ()))):
    return lax.dot_general(a, b, dims, preferred_element_type=F32)


def swap_x(array):
    count = lax.axis_size("seq")
    return lax.ppermute(array, "seq", [(i, i ^ 1) for i in range(count)])


def shift_rest(array, step):
    count = lax.axis_size("seq")
    rest = count // PAIR
    pairs = [(i, PAIR * ((i // PAIR + step) % rest) + i % PAIR) for i in range(count)]
    return lax.ppermute(array, "seq", pairs)


def swap_core(array):
    count = lax.axis_size("dp")
    return lax.ppermute(array, "dp", [(i, i ^ 1) for i in range(count)])


def shift_chip(array, step):
    count = lax.axis_size("dp")
    chips = count // CORES
    pairs = [(i, CORES * ((i // CORES + step) % chips) + i % CORES) for i in range(count)]
    return lax.ppermute(array, "dp", pairs)


def shift_seq(array, step):
    count = lax.axis_size("seq")
    pairs = [(i, i + step) for i in range(count) if 0 <= i + step < count]
    return lax.ppermute(array, "seq", pairs)


def block_order(chips, rest, flip):
    dp_index, place = lax.axis_index("dp"), lax.axis_index("seq")
    chip, core = dp_index // CORES, dp_index % CORES
    around, x = place // PAIR, (place + flip) % PAIR
    order = []
    for k in range(chips):
        for c in range(CORES):
            for j in range(rest):
                shard = CORES * ((chip - k + chips) % chips) + (core + c) % CORES
                order.append(shard * (PAIR * rest) + PAIR * ((around - j + rest) % rest) + x)
    return order


def lanes(index, width):
    return pl.ds(pl.multiple_of(index * width, width), width)


def split_kernel(chips, rest, width, in_ref, mine_ref, other_ref):
    mine, other = block_order(chips, rest, 0), block_order(chips, rest, 1)
    for i in range(len(mine)):
        out = slice(i * width, (i + 1) * width)
        other_ref[:, out] = in_ref[:, lanes(other[i], width)]
        mine_ref[:, out] = in_ref[:, lanes(mine[i], width)]


def split_tokens(tokens, chips, rest, width):
    rows, total = tokens.shape
    half = total // 2
    if width % 128:
        blocks = tokens.reshape(rows, total // width, width)
        orders = [jnp.stack(block_order(chips, rest, flip)) for flip in range(PAIR)]
        return [jnp.take(blocks, order, axis=1).reshape(rows, half) for order in orders]
    tile = min(rows, 128)
    return pl.pallas_call(
        functools.partial(split_kernel, chips, rest, width),
        grid=(rows // tile,),
        in_specs=[pl.BlockSpec((tile, total), lambda i: (i, 0))],
        out_specs=[pl.BlockSpec((tile, half), lambda i: (i, 0))] * 2,
        out_shape=[jax.ShapeDtypeStruct((rows, half), tokens.dtype)] * 2,
        name="split_tokens",
    )(tokens)


def merge_kernel(chips, rest, width, mine_ref, other_ref, out_ref):
    mine, other = block_order(chips, rest, 0), block_order(chips, rest, 1)
    for i in range(len(mine)):
        source = slice(i * width, (i + 1) * width)
        out_ref[:, lanes(mine[i], width)] = mine_ref[:, source]
        out_ref[:, lanes(other[i], width)] = other_ref[:, source]


def merge_halves(mine, other, chips, rest, width):
    rows, half = mine.shape
    if width % 128:
        order = jnp.stack(block_order(chips, rest, 0) + block_order(chips, rest, 1))
        where = jnp.zeros_like(order).at[order].set(lax.iota(order.dtype, order.shape[0]))
        blocks = jnp.concatenate([mine, other], axis=1).reshape(rows, order.shape[0], width)
        return jnp.take(blocks, where, axis=1).reshape(rows, 2 * half)
    tile = min(rows, 128)
    return pl.pallas_call(
        functools.partial(merge_kernel, chips, rest, width),
        grid=(rows // tile,),
        in_specs=[pl.BlockSpec((tile, half), lambda i: (i, 0))] * 2,
        out_specs=pl.BlockSpec((tile, 2 * half), lambda i: (i, 0)),
        out_shape=jax.ShapeDtypeStruct((rows, 2 * half), mine.dtype),
        name="merge_halves",
    )(mine, other)


def project_kernel(first, span, per, qwidth, has_sum, tokens_ref, *refs):
    if has_sum:
        sum_ref, refs = refs[0], refs[1:]
        total = sum_ref[...]
    else:
        total = None
    pieces = refs[:-2] if qwidth else refs[:-1]
    for g in range(len(pieces) // per):
        rows = jnp.concatenate([r[...] for r in pieces[g * per : (g + 1) * per]], axis=0)
        term = dot(tokens_ref[:, (first + g) * span : (first + g + 1) * span], rows)
        total = term if total is None else total + term
    if qwidth:
        query_ref, pair_ref = refs[-2:]
        query_ref[...] = total[:, :qwidth].astype(query_ref.dtype)
        pair_ref[...] = total[:, qwidth:].astype(pair_ref.dtype)
    else:
        refs[-1][...] = total


def project(tokens, groups, first, qwidth=0, kind=F32, so_far=None):
    rows = tokens.shape[0]
    cols = groups[0][0].shape[1]
    pieces = [piece for group in groups for piece in group]
    span = sum(piece.shape[0] for piece in groups[0])
    widths = [qwidth, cols - qwidth] if qwidth else [cols]
    sums = [] if so_far is None else [so_far]
    outs = pl.pallas_call(
        functools.partial(project_kernel, first, span, len(groups[0]), qwidth, len(sums)),
        in_specs=[VMEM] * (1 + len(sums) + len(pieces)),
        out_specs=[VMEM] * len(widths),
        out_shape=[jax.ShapeDtypeStruct((rows, w), kind) for w in widths],
        compiler_params=pltpu.CompilerParams(vmem_limit_bytes=48 * 2**20),
        name="project",
    )(tokens, *sums, *pieces)
    return outs if qwidth else outs[0]


def grad_kernel(span, per, dquery_ref, dpair_ref, *refs):
    pieces, out_ref = refs[:-1], refs[-1]
    grads = jnp.concatenate([dquery_ref[...], dpair_ref[...]], axis=1)
    for k in range(len(pieces) // per):
        rows = jnp.concatenate([r[...] for r in pieces[k * per : (k + 1) * per]], axis=0)
        out_ref[:, k * span : (k + 1) * span] = dot(grads, rows, NT).astype(BF16)


def width_grad(dquery, dpair, groups):
    rows = dquery.shape[0]
    pieces = [piece for group in groups for piece in group]
    span = sum(piece.shape[0] for piece in groups[0])
    return pl.pallas_call(
        functools.partial(grad_kernel, span, len(groups[0])),
        in_specs=[VMEM] * (2 + len(pieces)),
        out_specs=VMEM,
        out_shape=jax.ShapeDtypeStruct((rows, span * len(groups)), BF16),
        compiler_params=pltpu.CompilerParams(vmem_limit_bytes=48 * 2**20),
        name="width_grad",
    )(dquery, dpair, *pieces)


def weight_kernel(steps, span, tokens_ref, other_ref, dq_ref, dp_ref, dq_other_ref, dp_other_ref, keep_ref, send_ref):
    mine = jnp.concatenate([dq_ref[...], dp_ref[...]], axis=1)
    other = jnp.concatenate([dq_other_ref[...], dp_other_ref[...]], axis=1)
    both = jnp.concatenate([mine, other], axis=0)
    half = span // 2
    for i, k in enumerate(steps):
        cut = slice(k * span, (k + 1) * span)
        left = jnp.concatenate([tokens_ref[:, cut], other_ref[:, cut]], axis=0)
        total = dot(left.T, both).astype(BF16)
        keep_ref[i * half : (i + 1) * half, :] = total[:half]
        send_ref[i * half : (i + 1) * half, :] = total[half:]


def weight_terms(tokens, other, steps, span, grads):
    cols = grads[0].shape[1] + grads[1].shape[1]
    return pl.pallas_call(
        functools.partial(weight_kernel, steps, span),
        in_specs=[VMEM] * 6,
        out_specs=[VMEM] * 2,
        out_shape=[jax.ShapeDtypeStruct((len(steps) * span // 2, cols), BF16)] * 2,
        compiler_params=pltpu.CompilerParams(vmem_limit_bytes=48 * 2**20),
        name="weight_terms",
    )(tokens, other, *grads)


def core_sum_kernel(rest, width, keep_ref, from_ref, *out_refs):
    total = (keep_ref[...].astype(F32) + from_ref[...].astype(F32)).astype(BF16)
    for i in range(total.shape[0] // (rest * width)):
        for j in range(rest):
            source = (i * rest + j) * width
            out_refs[j][i * width : (i + 1) * width, :] = total[source : source + width]


def core_sum(keep, received, rest, width):
    rows, cols = keep.shape
    return pl.pallas_call(
        functools.partial(core_sum_kernel, rest, width),
        in_specs=[VMEM] * 2,
        out_specs=[VMEM] * rest,
        out_shape=[jax.ShapeDtypeStruct((rows // rest, cols), BF16)] * rest,
        name="core_sum",
    )(keep, received)


def sum_kernel(width, *refs):
    count = refs[0].shape[0] // width
    terms, outs = refs[:-count], refs[-count:]
    total = terms[0][...].astype(F32)
    for ref in terms[1:]:
        total = total + ref[...].astype(F32)
    for i, ref in enumerate(outs):
        ref[...] = total[i * width : (i + 1) * width].astype(ref.dtype)


def sum_terms(terms, width, kinds):
    cols = terms[0].shape[1]
    return pl.pallas_call(
        functools.partial(sum_kernel, width),
        in_specs=[VMEM] * len(terms),
        out_specs=[VMEM] * len(kinds),
        out_shape=[jax.ShapeDtypeStruct((width, cols), kind) for kind in kinds],
        name="sum_terms",
    )(*terms)


def attend_kernel(
    heads, back, docs_ref, q_ref, q_from_ref, cot_ref, *refs
):
    pair_refs, (out_ref, dq_ref, dpair_ref, dback_ref) = refs[: back + 1], refs[back + 1 :]
    rows = q_ref.shape[0]
    hd = HEAD_DIM
    scale = 1.0 / math.sqrt(hd)
    first = lax.axis_index("seq") * rows
    base = first - back * rows
    total = (back + 1) * rows

    row_pos = first + lax.broadcasted_iota(jnp.int32, (1, rows), 1)
    start_of = jnp.zeros((1, rows), jnp.int32)
    start = jnp.int32(0)
    for d in range(docs_ref.shape[0]):
        end = start + docs_ref[d]
        start_of = jnp.where((row_pos >= start) & (row_pos < end), start, start_of)
        start = end
    key_pos = base + lax.broadcasted_iota(jnp.int32, (total, rows), 0)
    allowed = (key_pos >= start_of) & (key_pos <= row_pos)

    pairs = [r[...] for r in pair_refs]
    keys = jnp.concatenate([p[:, :hd] for p in pairs], axis=0)
    values = jnp.concatenate([p[:, hd:] for p in pairs], axis=0)
    keys_t, values_t = keys.T, values.T
    dk = jnp.zeros((total, hd), F32)
    dv = jnp.zeros((total, hd), F32)
    for h in range(heads):
        cols = slice(h * hd, (h + 1) * hd)
        q = (q_ref[:, cols] + q_from_ref[:, cols].astype(F32)).astype(BF16)
        cot = cot_ref[:, cols]
        logits = jnp.where(allowed, dot(keys, q, NT) * scale, -1e30)
        top = jnp.max(logits, axis=0, keepdims=True)
        raised = jnp.exp(logits - top)
        probs = raised * (1.0 / jnp.sum(raised, axis=0, keepdims=True))
        probs_half = probs.astype(BF16)
        out_t = dot(values_t, probs_half).astype(BF16)
        cot_t = cot.T
        delta = jnp.sum(cot_t.astype(F32) * out_t.astype(F32), axis=0, keepdims=True)
        dscores = (probs * (dot(values, cot, NT) - delta)).astype(BF16)
        out_ref[:, cols] = out_t.T
        dq_ref[:, cols] = (dot(keys_t, dscores) * scale).astype(BF16).T
        dk += dot(dscores, q)
        dv += dot(probs_half, cot)
    both = jnp.concatenate([dk * scale, dv], axis=1)
    dpair_ref[...] = both[back * rows :]
    dback_ref[...] = both[: back * rows].astype(BF16)


def attend(docs, q, q_from, cot, pairs):
    rows, width = q.shape
    back = len(pairs) - 1
    two = 2 * HEAD_DIM
    return pl.pallas_call(
        functools.partial(attend_kernel, width // HEAD_DIM, back),
        in_specs=[SMEM] + [VMEM] * (back + 4),
        out_specs=[VMEM] * 4,
        out_shape=[
            jax.ShapeDtypeStruct((rows, width), BF16),
            jax.ShapeDtypeStruct((rows, width), BF16),
            jax.ShapeDtypeStruct((rows, two), F32),
            jax.ShapeDtypeStruct((back * rows, two), BF16),
        ],
        compiler_params=pltpu.CompilerParams(vmem_limit_bytes=48 * 2**20),
        name="attend",
    )(docs, q, q_from, cot, *pairs)


def kept_rows(doc_row, flag_row, positions):
    ends = jnp.cumsum(doc_row)
    starts = ends - doc_row
    inside = (positions[:, None] >= starts[None, :]) & (positions[:, None] < ends[None, :])
    return jnp.sum(jnp.where(inside, flag_row[None, :], 0), axis=1)


def shards(inputs, weights, cotangent, doc_lengths, kept_flags):
    seq_count = lax.axis_size("seq")
    chips = lax.axis_size("dp") // CORES
    rest = seq_count // PAIR
    place = lax.axis_index("seq")
    tokens = inputs[0]
    local = tokens.shape[0]
    qwidth = cotangent.shape[2]
    shard_rows, cols = weights.shape
    width = shard_rows // seq_count
    back = -(-(local * seq_count // 2 - 1) // local)

    tokens_mine, tokens_sent = split_tokens(tokens, chips, rest, width)
    tokens_other = swap_x(tokens_sent)

    blocks = weights.reshape(seq_count, width, cols)
    groups = []
    for k in range(chips):
        if k == 0:
            places = [PAIR * ((place // PAIR - j + rest) % rest) + place % PAIR for j in range(rest)]
            here = [lax.dynamic_index_in_dim(blocks, p, 0, keepdims=False) for p in places]
            own = here[0]
        else:
            first = shift_chip(own, k)
            here = [first] + [shift_rest(first, j) for j in range(1, rest)]
        groups.append(here + [swap_core(piece) for piece in here])

    early, late, last = groups[:-1], groups[-1:], chips - 1
    so_far = project(tokens_other, early, 0)
    query_sent, pair_sent = project(tokens_other, late, last, qwidth, BF16, so_far)
    pair_from, query_from = swap_x(pair_sent), swap_x(query_sent)
    so_far = project(tokens_mine, early, 0)
    query, pair = project(tokens_mine, late, last, qwidth, F32, so_far)
    pair = (pair + pair_from.astype(F32)).astype(BF16)

    doc_row, flag_row = doc_lengths[0], kept_flags[0]
    positions = place * local + lax.iota(jnp.int32, local)
    kept = kept_rows(doc_row, flag_row, positions)
    cot = jnp.where(kept[:, None] > 0, cotangent[0], jnp.zeros_like(cotangent[0]))

    pairs = [shift_seq(pair, j) for j in range(back, 0, -1)] + [pair]
    attention, dquery, dpair, dback = attend(doc_row, query, query_from, cot, pairs)

    dquery_other = swap_x(dquery)
    for j in range(1, back + 1):
        sent = dback[(back - j) * local : (back - j + 1) * local]
        dpair = dpair + shift_seq(sent, -j).astype(F32)
    dpair = dpair.astype(BF16)
    dpair_other = swap_x(dpair)

    span = CORES * rest * width
    grads = (dquery, dpair, dquery_other, dpair_other)
    order = sorted(range(chips), key=lambda k: (k == 0, -min(k, chips - k), k))
    finished = []
    for steps in (order[: chips // 2], order[chips // 2 :]):
        keep, sent = weight_terms(tokens_mine, tokens_other, steps, span, grads)
        kept_here, *sent = core_sum(keep, swap_core(sent), rest, width)
        terms = [kept_here] + [shift_rest(piece, -j) for j, piece in enumerate(sent, 1)]
        parts = sum_terms(terms, width, [BF16 if k else F32 for k in steps])
        finished += [shift_chip(part, -k) if k else part for k, part in zip(steps, parts)]
    (weights_grad,) = sum_terms(finished, width, [F32])

    grad_from = swap_x(width_grad(dquery_other, dpair_other, groups))
    inputs_grad = merge_halves(width_grad(dquery, dpair, groups), grad_from, chips, rest, width)
    return (attention[None], inputs_grad[None], weights_grad)


def solution(mesh):
    in_specs = (
        P("dp", "seq", None),
        P("dp", None),
        P("dp", "seq", None),
        P("dp", None),
        P("dp", None),
    )
    out_specs = (P("dp", "seq", None), P("dp", "seq", None), P(("dp", "seq"), None))
    return jax.shard_map(shards, mesh=mesh, in_specs=in_specs, out_specs=out_specs, check_vma=False)
```

time: 154 us -> 123 us (0.80)
  local copies, waits for them, and re-layouts: 16.7 us -> 2.85 us
  matrix products: 11 us -> 0 us
  waiting for transfers between devices: 30.8 us -> 40.3 us
  Pallas kernels: 43.1 us -> 35 us
  other arithmetic: 4.61 us -> 0.46 us
  starting transfers between devices: 44 us -> 41.7 us
    dot_general x6 -> x0, matrix products: 11 us -> none  [dot(): return lax.dot_general(a, b, dims, preferred_element_type=F32)]
    unnamed x28 -> x36, local copies, waits for them, and re-layouts: 13.2 us -> 2.8 us
    ppermute x6, waiting for transfers between devices: 2.43 us -> 11.9 us  [shift_chip(): return lax.ppermute(array, 'dp', pairs)]
    pallas_call x3 -> x15, Pallas kernels: 36.8 us -> 28.7 us  [the longest x3 6.04 us: sum_terms(): pl.pallas_call(functools.partial(sum_kernel, width), in_specs=[VMEM] * le...]
    add x2 -> x0, other arithmetic: 3.47 us -> none  [the longest x1 2.62 us: shards(): group = total[k, 0] + swap_core(total[k, 1].astype(BF16)).astype(F32)]
    ppermute x7 -> x5, waiting for transfers between devices: 13.7 us -> 16.2 us  [shift_rest(): return lax.ppermute(array, 'seq', pairs)]
    ppermute x6, waiting for transfers between devices: 6.77 us -> 4.61 us  [swap_x(): return lax.ppermute(array, 'seq', [(i, i ^ 1) for i in range(count)])]
    ppermute x7 -> x5, starting transfers between devices: 7.79 us -> 5.63 us  [shift_rest(): return lax.ppermute(array, 'seq', pairs)]
  transfers between devices with their start and end apart: 31 -> 31, of which waited for: 12 -> 13; matrix products, arithmetic and copies ran while one was open for 14% -> 0% of each run, Pallas kernels for 13% -> 18%
where the time goes in v3:
time: 123 us; the launch traced here: 121 us
  starting transfers between devices  41.7 us (34%)
  waiting for transfers between devices  40.3 us (33%)
  Pallas kernels  35 us (28%)
  local copies, waits for them, and re-layouts  2.85 us (2%)
    ppermute x5, waiting for transfers between devices, shift_rest(): return lax.ppermute(array, 'seq', pairs)  16.2 us
    ppermute x6, starting transfers between devices, shift_chip(): return lax.ppermute(array, 'dp', pairs)  13.6 us
    ppermute x6, starting transfers between devices, swap_x(): return lax.ppermute(array, 'seq', [(i, i ^ 1) for i in range(count)])  12.6 us
    ppermute x6, waiting for transfers between devices, shift_chip(): return lax.ppermute(array, 'dp', pairs)  11.9 us
    ppermute x4, starting transfers between devices, shift_seq(): return lax.ppermute(array, 'seq', pairs)  8.41 us
    ppermute x4, waiting for transfers between devices, shift_seq(): return lax.ppermute(array, 'seq', pairs)  7.11 us
    pallas_call x1, Pallas kernels, attend(): pl.pallas_call(functools.partial(attend_kernel, width // HEAD_DIM, back),...  6.31 us
    pallas_call x3, Pallas kernels, sum_terms(): pl.pallas_call(functools.partial(sum_kernel, width), in_specs=[VMEM] * le...  6.04 us
  transfers between devices with their start and end apart: 31, of which 13 were waited for; matrix products, arithmetic and copies ran while one was open for 0% of the time, Pallas kernels for 18%

profile of v3, /device:TPU:0, one launch (start us, length us, event | category | flops | bytes accessed | tf_op | source)
XLA Modules:
  0.0 121.2 jit_solution(10724310814528617514)
XLA Ops:
  0.7 2.9 %split_tokens.1 = (bf16[256,2048]{1,0:T(8,128)(2,1)}, bf16[256,2048]{1,0:T(8,128)(2,1)}) custom-call(bf16[256,4096]{1,0:T(8,128)(2,1)} %bitcast.22), custom_call_target="tpu_custom_call" | custom-call | tf_op jit(solution)/shard_map/split_tokens/pallas_call | solution.py:89
  3.6 2.9 %collective-permute-start.14 = (bf16[256,2048]{1,0:T(8,128)(2,1)}, bf16[256,2048]{1,0:T(8,128)(2,1)S(1)}, u32[]{:S(2)}, u32[]{:S(2)}) collective-permute-start(bf16[256,2048]{1,0:T(8,128)(2,1)} %get-tuple-element.27), channel_id=1, source_target_pairs={{0,1},{1,0},{2,3},{3,2},{4,5},{5,4},{6,7},{7,6},{8,9},{9,8},{10,11... | collective-permute-start | bytes 3145736 | tf_op jit(solution)/shard_map/ppermute | solution.py:28
  6.6 1.6 %collective-permute-start.2 = (bf16[128,768]{1,0:T(8,128)(2,1)S(1)}, bf16[128,768]{1,0:T(8,128)(2,1)S(1)}, u32[]{:S(2)}, u32[]{:S(2)}) collective-permute-start(bf16[128,768]{1,0:T(8,128)(2,1)S(1)} %get-tuple-element.48.refs_0_), channel_id=1, source_target_pairs={{0,8},{4,12},{8,16},{12,20},{16,24},{20,28},{24,0},{28,4},{1,9},{5... | collective-permute-start | bytes 589832 | tf_op jit(solution)/shard_map/ppermute | solution.py:47
  8.4 2.6 %collective-permute-start.6 = (bf16[128,768]{1,0:T(8,128)(2,1)S(1)}, bf16[128,768]{1,0:T(8,128)(2,1)S(1)}, u32[]{:S(2)}, u32[]{:S(2)}) collective-permute-start(bf16[128,768]{1,0:T(8,128)(2,1)S(1)} %get-tuple-element.48.refs_0_), channel_id=1, source_target_pairs={{0,16},{4,20},{8,24},{12,28},{16,0},{20,4},{24,8},{28,12},{1,17},{... | collective-permute-start | bytes 589832 | tf_op jit(solution)/shard_map/ppermute | solution.py:47
  11.0 1.4 %collective-permute-start.10 = (bf16[128,768]{1,0:T(8,128)(2,1)S(1)}, bf16[128,768]{1,0:T(8,128)(2,1)}, u32[]{:S(2)}, u32[]{:S(2)}) collective-permute-start(bf16[128,768]{1,0:T(8,128)(2,1)S(1)} %get-tuple-element.48.refs_0_), channel_id=1, source_target_pairs={{0,24},{4,28},{8,0},{12,4},{16,8},{20,12},{24,16},{28,20},{1,25},{... | collective-permute-start | bytes 589832 | tf_op jit(solution)/shard_map/ppermute | solution.py:47
  12.4 3.9 %collective-permute-done.2.refs_4_ = bf16[128,768]{1,0:T(8,128)(2,1)S(1)} collective-permute-done((bf16[128,768]{1,0:T(8,128)(2,1)S(1)}, bf16[128,768]{1,0:T(8,128)(2,1)S(1)}, u32[]{:S(2)}, u32[]{:S(2)}) %collective-permute-start.2) | collective-permute-done | bytes 196640 | tf_op jit(solution)/shard_map/ppermute | solution.py:47
  16.3 1.5 %collective-permute-start.3 = (bf16[128,768]{1,0:T(8,128)(2,1)S(1)}, bf16[128,768]{1,0:T(8,128)(2,1)S(1)}, u32[]{:S(2)}, u32[]{:S(2)}) collective-permute-start(bf16[128,768]{1,0:T(8,128)(2,1)S(1)} %collective-permute-done.2.refs_4_), channel_id=1, source_target_pairs={{0,2},{1,3},{2,0},{3,1},{4,6},{5,7},{6,4},{7,5},{8,10},{9,11},{10,... | collective-permute-start | bytes 589832 | tf_op jit(solution)/shard_map/ppermute | solution.py:35
  18.0 6.3 %collective-permute-done.6.refs_8_ = bf16[128,768]{1,0:T(8,128)(2,1)S(1)} collective-permute-done((bf16[128,768]{1,0:T(8,128)(2,1)S(1)}, bf16[128,768]{1,0:T(8,128)(2,1)S(1)}, u32[]{:S(2)}, u32[]{:S(2)}) %collective-permute-start.6) | collective-permute-done | bytes 196640 | tf_op jit(solution)/shard_map/ppermute | solution.py:47
  24.3 1.5 %collective-permute-start.7 = (bf16[128,768]{1,0:T(8,128)(2,1)S(1)}, bf16[128,768]{1,0:T(8,128)(2,1)S(1)}, u32[]{:S(2)}, u32[]{:S(2)}) collective-permute-start(bf16[128,768]{1,0:T(8,128)(2,1)S(1)} %collective-permute-done.6.refs_8_), channel_id=1, source_target_pairs={{0,2},{1,3},{2,0},{3,1},{4,6},{5,7},{6,4},{7,5},{8,10},{9,11},{10,... | collective-permute-start | bytes 589832 | tf_op jit(solution)/shard_map/ppermute | solution.py:35
  26.6 5.5 %collective-permute-done.7.refs_9_ = bf16[128,768]{1,0:T(8,128)(2,1)S(1)} collective-permute-done((bf16[128,768]{1,0:T(8,128)(2,1)S(1)}, bf16[128,768]{1,0:T(8,128)(2,1)S(1)}, u32[]{:S(2)}, u32[]{:S(2)}) %collective-permute-start.7) | collective-permute-done | bytes 196640 | tf_op jit(solution)/shard_map/ppermute | solution.py:35
  32.6 2.7 %collective-permute-done.11.refs_2_.refs_13_ = bf16[128,768]{1,0:T(8,128)(2,1)S(1)} collective-permute-done((bf16[128,768]{1,0:T(8,128)(2,1)}, bf16[128,768]{1,0:T(8,128)(2,1)S(1)}, u32[]{:S(2)}, u32[]{:S(2)}) %collective-permute-start.11) | collective-permute-done | bytes 196640 | tf_op jit(solution)/shard_map/ppermute | solution.py:35
  35.4 0.8 project.6.refs_0_
  36.8 1.4 %project.7 = (bf16[256,512]{1,0:T(8,128)(2,1)S(1)}, bf16[256,256]{1,0:T(8,128)(2,1)S(1)}) custom-call(bf16[256,2048]{1,0:T(8,128)(2,1)S(1)} %collective-permute-done.14.tokens_ref.other_ref, f32[256,768]{1,0:T(8,128)S(1)} %project.6.refs_0_, bf16[128,768]{1,0:T(8,128)(2,1)} %collective-permute-done.10.refs_1_.refs_12_, ...), custom_call_target="tpu_custom_call" | custom-call | tf_op jit(solution)/shard_map/project/pallas_call | solution.py:151
  39.6 1.3 %project.5 = (f32[256,512]{1,0:T(8,128)S(1)}, f32[256,256]{1,0:T(8,128)S(1)}) custom-call(bf16[256,2048]{1,0:T(8,128)(2,1)S(1)} %copy-done, f32[256,768]{1,0:T(8,128)S(1)} %project.4.refs_0_, bf16[128,768]{1,0:T(8,128)(2,1)} %collective-permute-done.10.refs_1_.refs_12_, bf16[128,768]{1,0:T(8,128)(2,1)S(1)} %collective-permute-done.11.refs_2_.refs_13_, ...), custom_call_target="tpu_custom_call" | custom-call | tf_op jit(solution)/shard_map/project/pallas_call | solution.py:151
  40.9 1.5 %collective-permute-start.15 = (bf16[256,512]{1,0:T(8,128)(2,1)S(1)}, bf16[256,512]{1,0:T(8,128)(2,1)S(1)}, u32[]{:S(2)}, u32[]{:S(2)}) collective-permute-start(bf16[256,512]{1,0:T(8,128)(2,1)S(1)} %get-tuple-element.28), channel_id=1, source_target_pairs={{0,1},{1,0},{2,3},{3,2},{4,5},{5,4},{6,7},{7,6},{8,9},{9,8},{10,11... | collective-permute-start | bytes 786440 | tf_op jit(solution)/shard_map/ppermute | solution.py:28
  42.5 1.6 %collective-permute-done.16 = bf16[256,256]{1,0:T(8,128)(2,1)S(1)} collective-permute-done((bf16[256,256]{1,0:T(8,128)(2,1)S(1)}, bf16[256,256]{1,0:T(8,128)(2,1)S(1)}, u32[]{:S(2)}, u32[]{:S(2)}) %collective-permute-start.16) | collective-permute-done | bytes 131104 | tf_op jit(solution)/shard_map/ppermute | solution.py:28
  44.2 3.4 %collective-permute-start.17 = (bf16[256,256]{1,0:T(8,128)(2,1)S(1)}, bf16[256,256]{1,0:T(8,128)(2,1)S(1)}, u32[]{:S(2)}, u32[]{:S(2)}) collective-permute-start(bf16[256,256]{1,0:T(8,128)(2,1)S(1)} %add_convert_fusion.1.refs_2_), channel_id=1, source_target_pairs={{0,2},{1,3},{4,6},{5,7},{8,10},{9,11},{12,14},{13,15},{16,18},{17,... | collective-permute-start | bytes 393224 | tf_op jit(solution)/shard_map/ppermute | solution.py:53
  47.6 2.2 %collective-permute-start.18 = (bf16[256,256]{1,0:T(8,128)(2,1)S(1)}, bf16[256,256]{1,0:T(8,128)(2,1)S(1)}, u32[]{:S(2)}, u32[]{:S(2)}) collective-permute-start(bf16[256,256]{1,0:T(8,128)(2,1)S(1)} %add_convert_fusion.1.refs_2_), channel_id=1, source_target_pairs={{0,1},{1,2},{2,3},{4,5},{5,6},{6,7},{8,9},{9,10},{10,11},{12,13},{... | collective-permute-start | bytes 393224 | tf_op jit(solution)/shard_map/ppermute | solution.py:53
  49.9 3.0 %collective-permute-done.17.refs_0_ = bf16[256,256]{1,0:T(8,128)(2,1)S(1)} collective-permute-done((bf16[256,256]{1,0:T(8,128)(2,1)S(1)}, bf16[256,256]{1,0:T(8,128)(2,1)S(1)}, u32[]{:S(2)}, u32[]{:S(2)}) %collective-permute-start.17) | collective-permute-done | bytes 131104 | tf_op jit(solution)/shard_map/ppermute | solution.py:53
  52.9 6.3 %attend.1 = (bf16[256,512]{1,0:T(8,128)(2,1)}, bf16[256,512]{1,0:T(8,128)(2,1)S(1)}, f32[256,256]{1,0:T(8,128)S(1)}, bf16[512,256]{1,0:T(8,128)(2,1)S(1)}) custom-call(s32[8]{0:T(128)S(1)} %bitcast.21, f32[256,512]{1,0:T(8,128)S(1)} %get-tuple-element.26.q_ref, bf16[256,512]{1,0:T(8,128)(2,1)S(1)} %collective-permute-done.15.q_from_ref, ...), custom_call_target="tpu_custom_call" | custom-call | tf_op jit(solution)/shard_map/attend/pallas_call | solution.py:302
  59.2 1.3 %collective-permute-start.20 = (bf16[256,256]{1,0:T(8,128)(2,1)S(1)}, bf16[256,256]{1,0:T(8,128)(2,1)S(1)}, u32[]{:S(2)}, u32[]{:S(2)}) collective-permute-start(bf16[256,256]{1,0:T(8,128)(2,1)S(1)} %get-tuple-element.50), channel_id=1, source_target_pairs={{2,0},{3,1},{6,4},{7,5},{10,8},{11,9},{14,12},{15,13},{18,16},{19,... | collective-permute-start | bytes 393224 | tf_op jit(solution)/shard_map/ppermute | solution.py:53
  60.5 1.5 %collective-permute-start.19 = (bf16[256,256]{1,0:T(8,128)(2,1)S(1)}, bf16[256,256]{1,0:T(8,128)(2,1)S(1)}, u32[]{:S(2)}, u32[]{:S(2)}) collective-permute-start(bf16[256,256]{1,0:T(8,128)(2,1)S(1)} %get-tuple-element.49), channel_id=1, source_target_pairs={{1,0},{2,1},{3,2},{5,4},{6,5},{7,6},{9,8},{10,9},{11,10},{13,12},{... | collective-permute-start | bytes 393224 | tf_op jit(solution)/shard_map/ppermute | solution.py:53
  62.0 2.7 %collective-permute-start.21 = (bf16[256,512]{1,0:T(8,128)(2,1)S(1)}, bf16[256,512]{1,0:T(8,128)(2,1)S(1)}, u32[]{:S(2)}, u32[]{:S(2)}) collective-permute-start(bf16[256,512]{1,0:T(8,128)(2,1)S(1)} %get-tuple-element.32.dquery_ref.dq_ref), channel_id=1, source_target_pairs={{0,1},{1,0},{2,3},{3,2},{4,5},{5,4},{6,7},{7,6},{8,9},{9,8},{10,11... | collective-permute-start | bytes 786440 | tf_op jit(solution)/shard_map/ppermute | solution.py:28
  64.7 1.4 %collective-permute-done.20 = bf16[256,256]{1,0:T(8,128)(2,1)S(1)} collective-permute-done((bf16[256,256]{1,0:T(8,128)(2,1)S(1)}, bf16[256,256]{1,0:T(8,128)(2,1)S(1)}, u32[]{:S(2)}, u32[]{:S(2)}) %collective-permute-start.20) | collective-permute-done | bytes 131104 | tf_op jit(solution)/shard_map/ppermute | solution.py:53
  66.1 2.8 %collective-permute-done.19 = bf16[256,256]{1,0:T(8,128)(2,1)S(1)} collective-permute-done((bf16[256,256]{1,0:T(8,128)(2,1)S(1)}, bf16[256,256]{1,0:T(8,128)(2,1)S(1)}, u32[]{:S(2)}, u32[]{:S(2)}) %collective-permute-start.19) | collective-permute-done | bytes 131104 | tf_op jit(solution)/shard_map/ppermute | solution.py:53
  68.9 2.8 %collective-permute-start.22 = (bf16[256,256]{1,0:T(8,128)(2,1)S(1)}, bf16[256,256]{1,0:T(8,128)(2,1)S(1)}, u32[]{:S(2)}, u32[]{:S(2)}) collective-permute-start(bf16[256,256]{1,0:T(8,128)(2,1)S(1)} %add_convert_fusion.dpair_ref.dp_ref), channel_id=1, source_target_pairs={{0,1},{1,0},{2,3},{3,2},{4,5},{5,4},{6,7},{7,6},{8,9},{9,8},{10,11... | collective-permute-start | bytes 393224 | tf_op jit(solution)/shard_map/ppermute | solution.py:28
  71.7 2.9 %collective-permute-done.22.dpair_ref.dp_other_ref = bf16[256,256]{1,0:T(8,128)(2,1)S(1)} collective-permute-done((bf16[256,256]{1,0:T(8,128)(2,1)S(1)}, bf16[256,256]{1,0:T(8,128)(2,1)S(1)}, u32[]{:S(2)}, u32[]{:S(2)}) %collective-permute-start.22) | collective-permute-done | bytes 131104 | tf_op jit(solution)/shard_map/ppermute | solution.py:28
  74.7 1.0 weight_terms.2
  75.7 0.9 copy-done.11
  76.6 1.9 %weight_terms.3 = (bf16[512,768]{1,0:T(8,128)(2,1)S(1)}, bf16[512,768]{1,0:T(8,128)(2,1)}) custom-call(bf16[256,2048]{1,0:T(8,128)(2,1)S(1)} %copy-done, bf16[256,2048]{1,0:T(8,128)(2,1)S(1)} %collective-permute-done.14.tokens_ref.other_ref, bf16[256,512]{1,0:T(8,128)(2,1)S(1)} %get-tuple-element.32.dquery_ref.dq_ref, ...), custom_call_target="tpu_custom_call" | custom-call | tf_op jit(solution)/shard_map/weight_terms/pallas_call | solution.py:199
  79.0 2.9 %width_grad.3 = bf16[256,2048]{1,0:T(8,128)(2,1)} custom-call(bf16[256,512]{1,0:T(8,128)(2,1)S(1)} %collective-permute-done.21.dquery_ref.dq_other_ref, bf16[256,256]{1,0:T(8,128)(2,1)S(1)} %collective-permute-done.22.dpair_ref.dp_other_ref, bf16[128,768]{1,0:T(8,128)(2,1)S(1)} %get-tuple-element.48.refs_0_, bf16[128,768]{1,0:T(8,128)(2,1)S(1)} %get-tuple-element.47.refs_1_, ...), custom_call_target="tpu_custom_call" | custom-call | tf_op jit(solution)/shard_map/width_grad/pallas_call | solution.py:174
  82.0 2.0 %collective-permute-start.23 = (bf16[256,2048]{1,0:T(8,128)(2,1)}, bf16[256,2048]{1,0:T(8,128)(2,1)}, u32[]{:S(2)}, u32[]{:S(2)}) collective-permute-start(bf16[256,2048]{1,0:T(8,128)(2,1)} %width_grad.3), channel_id=1, source_target_pairs={{0,1},{1,0},{2,3},{3,2},{4,5},{5,4},{6,7},{7,6},{8,9},{9,8},{10,11... | collective-permute-start | bytes 3145736 | tf_op jit(solution)/shard_map/ppermute | solution.py:28
  84.0 0.9 copy-done.13
  84.9 2.5 %core_sum.2 = (bf16[256,768]{1,0:T(8,128)(2,1)}, bf16[256,768]{1,0:T(8,128)(2,1)}) custom-call(bf16[512,768]{1,0:T(8,128)(2,1)} %copy-done.11, bf16[512,768]{1,0:T(8,128)(2,1)} %copy-done.13), custom_call_target="tpu_custom_call" | custom-call | tf_op jit(solution)/shard_map/core_sum/pallas_call | solution.py:219
  87.4 0.9 collective-permute-start.25
  88.3 2.4 %core_sum.3 = (bf16[256,768]{1,0:T(8,128)(2,1)}, bf16[256,768]{1,0:T(8,128)(2,1)}) custom-call(bf16[512,768]{1,0:T(8,128)(2,1)} %copy-done.10, bf16[512,768]{1,0:T(8,128)(2,1)} %collective-permute-done.28.from_ref), custom_call_target="tpu_custom_call" | custom-call | tf_op jit(solution)/shard_map/core_sum/pallas_call | solution.py:219
  90.7 1.1 collective-permute-start.29
  91.8 7.9 %collective-permute-done.25.refs_1_ = bf16[256,768]{1,0:T(8,128)(2,1)} collective-permute-done((bf16[256,768]{1,0:T(8,128)(2,1)}, bf16[256,768]{1,0:T(8,128)(2,1)}, u32[]{:S(2)}, u32[]{:S(2)}) %collective-permute-start.25) | collective-permute-done | bytes 393248 | tf_op jit(solution)/shard_map/ppermute | solution.py:35
  99.7 1.9 %sum_terms.3 = (bf16[128,768]{1,0:T(8,128)(2,1)}, bf16[128,768]{1,0:T(8,128)(2,1)}) custom-call(bf16[256,768]{1,0:T(8,128)(2,1)} %get-tuple-element.37.refs_0_, bf16[256,768]{1,0:T(8,128)(2,1)} %collective-permute-done.25.refs_1_), custom_call_target="tpu_custom_call" | custom-call | tf_op jit(solution)/shard_map/sum_terms/pallas_call | solution.py:240
  101.6 4.2 %collective-permute-start.26 = (bf16[128,768]{1,0:T(8,128)(2,1)}, bf16[128,768]{1,0:T(8,128)(2,1)S(1)}, u32[]{:S(2)}, u32[]{:S(2)}) collective-permute-start(bf16[128,768]{1,0:T(8,128)(2,1)} %get-tuple-element.39), channel_id=1, source_target_pairs={{0,16},{4,20},{8,24},{12,28},{16,0},{20,4},{24,8},{28,12},{1,17},{... | collective-permute-start | bytes 589832 | tf_op jit(solution)/shard_map/ppermute | solution.py:47
  105.8 1.2 %collective-permute-start.27 = (bf16[128,768]{1,0:T(8,128)(2,1)}, bf16[128,768]{1,0:T(8,128)(2,1)}, u32[]{:S(2)}, u32[]{:S(2)}) collective-permute-start(bf16[128,768]{1,0:T(8,128)(2,1)} %get-tuple-element.40), channel_id=1, source_target_pairs={{0,24},{4,28},{8,0},{12,4},{16,8},{20,12},{24,16},{28,20},{1,25},{... | collective-permute-start | bytes 589832 | tf_op jit(solution)/shard_map/ppermute | solution.py:47
  107.1 2.0 %sum_terms.4 = (bf16[128,768]{1,0:T(8,128)(2,1)}, f32[128,768]{1,0:T(8,128)}) custom-call(bf16[256,768]{1,0:T(8,128)(2,1)} %get-tuple-element.43.refs_0_, bf16[256,768]{1,0:T(8,128)(2,1)} %collective-permute-done.29.refs_1_), custom_call_target="tpu_custom_call" | custom-call | tf_op jit(solution)/shard_map/sum_terms/pallas_call | solution.py:240
  109.1 2.6 %collective-permute-start.30 = (bf16[128,768]{1,0:T(8,128)(2,1)}, bf16[128,768]{1,0:T(8,128)(2,1)}, u32[]{:S(2)}, u32[]{:S(2)}) collective-permute-start(bf16[128,768]{1,0:T(8,128)(2,1)} %get-tuple-element.45), channel_id=1, source_target_pairs={{0,8},{4,12},{8,16},{12,20},{16,24},{20,28},{24,0},{28,4},{1,9},{5... | collective-permute-start | bytes 589832 | tf_op jit(solution)/shard_map/ppermute | solution.py:47
  111.7 1.9 %width_grad.2.mine_ref = bf16[256,2048]{1,0:T(8,128)(2,1)S(1)} custom-call(bf16[256,512]{1,0:T(8,128)(2,1)S(1)} %copy-done.9, bf16[256,256]{1,0:T(8,128)(2,1)S(1)} %add_convert_fusion.dpair_ref.dp_ref, bf16[128,768]{1,0:T(8,128)(2,1)S(1)} %get-tuple-element.48.refs_0_, bf16[128,768]{1,0:T(8,128)(2,1)S(1)} %get-tuple-element.47.refs_1_, ...), custom_call_target="tpu_custom_call" | custom-call | tf_op jit(solution)/shard_map/width_grad/pallas_call | solution.py:174
  113.7 1.0 copy-done.1
  114.6 2.8 %merge_halves.1 = bf16[256,4096]{1,0:T(8,128)(2,1)} custom-call(bf16[256,2048]{1,0:T(8,128)(2,1)} %copy-done.1, bf16[256,2048]{1,0:T(8,128)(2,1)} %collective-permute-done.23.other_ref), custom_call_target="tpu_custom_call" | custom-call | tf_op jit(solution)/shard_map/merge_halves/pallas_call | solution.py:115
  117.4 1.7 %collective-permute-done.30.refs_2_ = bf16[128,768]{1,0:T(8,128)(2,1)} collective-permute-done((bf16[128,768]{1,0:T(8,128)(2,1)}, bf16[128,768]{1,0:T(8,128)(2,1)}, u32[]{:S(2)}, u32[]{:S(2)}) %collective-permute-start.30) | collective-permute-done | bytes 196640 | tf_op jit(solution)/shard_map/ppermute | solution.py:47
  119.1 2.1 %sum_terms.5 = f32[128,768]{1,0:T(8,128)} custom-call(bf16[128,768]{1,0:T(8,128)(2,1)} %copy-done.16, bf16[128,768]{1,0:T(8,128)(2,1)} %collective-permute-done.27.refs_1_, bf16[128,768]{1,0:T(8,128)(2,1)} %collective-permute-done.30.refs_2_, f32[128,768]{1,0:T(8,128)} %get-tuple-element.46.refs_3_), custom_call_target="tpu_custom_call" | custom-call | tf_op jit(solution)/shard_map/sum_terms/pallas_call | solution.py:240
  (76 shorter events, 4.6 us)
Async XLA Ops:
  0.6 5.9 %copy-start.15 = (bf16[512,768]{1,0:T(8,128)(2,1)S(1)}, bf16[512,768]{1,0:T(8,128)(2,1)}, u32[]{:S(2)}) copy-start(bf16[512,768]{1,0:T(8,128)(2,1)} %param.6) | copy-start | bytes 2359300
  0.6 17.2 %copy-start.12 = (s32[1,8]{1,0:T(1,128)S(1)}, s32[1,8]{1,0:T(1,128)}, u32[]{:S(2)}) copy-start(s32[1,8]{1,0:T(1,128)} %param.8) | copy-start | bytes 100
  0.7 34.7 %copy-start.17 = (s32[1,8]{1,0:T(1,128)S(1)}, s32[1,8]{1,0:T(1,128)}, u32[]{:S(2)}) copy-start(s32[1,8]{1,0:T(1,128)} %param.9) | copy-start | bytes 100
  3.6 31.9 %collective-permute-start.14 = (bf16[256,2048]{1,0:T(8,128)(2,1)}, bf16[256,2048]{1,0:T(8,128)(2,1)S(1)}, u32[]{:S(2)}, u32[]{:S(2)}) collective-permute-start(bf16[256,2048]{1,0:T(8,128)(2,1)} %get-tuple-element.27), channel_id=1, source_target_pairs={{0,1},{1,0},{2,3},{3,2},{4,5},{5,4},{6,7},{7,6},{8,9},{9,8},{10,11... | collective-permute-start | bytes 3145736 | tf_op jit(solution)/shard_map/ppermute | solution.py:28
  6.5 4.5 %collective-permute-start = (bf16[128,768]{1,0:T(8,128)(2,1)S(1)}, bf16[128,768]{1,0:T(8,128)(2,1)S(1)}, u32[]{:S(2)}, u32[]{:S(2)}) collective-permute-start(bf16[128,768]{1,0:T(8,128)(2,1)S(1)} %get-tuple-element.48.refs_0_), channel_id=1, source_target_pairs={{0,4},{4,0},{8,12},{12,8},{16,20},{20,16},{24,28},{28,24},{1,5},{5... | collective-permute-start | bytes 589832 | tf_op jit(solution)/shard_map/ppermute | solution.py:40
  6.6 9.7 %collective-permute-start.2 = (bf16[128,768]{1,0:T(8,128)(2,1)S(1)}, bf16[128,768]{1,0:T(8,128)(2,1)S(1)}, u32[]{:S(2)}, u32[]{:S(2)}) collective-permute-start(bf16[128,768]{1,0:T(8,128)(2,1)S(1)} %get-tuple-element.48.refs_0_), channel_id=1, source_target_pairs={{0,8},{4,12},{8,16},{12,20},{16,24},{20,28},{24,0},{28,4},{1,9},{5... | collective-permute-start | bytes 589832 | tf_op jit(solution)/shard_map/ppermute | solution.py:47
  8.2 9.8 %collective-permute-start.1 = (bf16[128,768]{1,0:T(8,128)(2,1)S(1)}, bf16[128,768]{1,0:T(8,128)(2,1)S(1)}, u32[]{:S(2)}, u32[]{:S(2)}) collective-permute-start(bf16[128,768]{1,0:T(8,128)(2,1)S(1)} %get-tuple-element.47.refs_1_), channel_id=1, source_target_pairs={{0,4},{4,0},{8,12},{12,8},{16,20},{20,16},{24,28},{28,24},{1,5},{5... | collective-permute-start | bytes 589832 | tf_op jit(solution)/shard_map/ppermute | solution.py:40
  8.4 15.9 %collective-permute-start.6 = (bf16[128,768]{1,0:T(8,128)(2,1)S(1)}, bf16[128,768]{1,0:T(8,128)(2,1)S(1)}, u32[]{:S(2)}, u32[]{:S(2)}) collective-permute-start(bf16[128,768]{1,0:T(8,128)(2,1)S(1)} %get-tuple-element.48.refs_0_), channel_id=1, source_target_pairs={{0,16},{4,20},{8,24},{12,28},{16,0},{20,4},{24,8},{28,12},{1,17},{... | collective-permute-start | bytes 589832 | tf_op jit(solution)/shard_map/ppermute | solution.py:47
  11.0 14.8 %collective-permute-start.10 = (bf16[128,768]{1,0:T(8,128)(2,1)S(1)}, bf16[128,768]{1,0:T(8,128)(2,1)}, u32[]{:S(2)}, u32[]{:S(2)}) collective-permute-start(bf16[128,768]{1,0:T(8,128)(2,1)S(1)} %get-tuple-element.48.refs_0_), channel_id=1, source_target_pairs={{0,24},{4,28},{8,0},{12,4},{16,8},{20,12},{24,16},{28,20},{1,25},{... | collective-permute-start | bytes 589832 | tf_op jit(solution)/shard_map/ppermute | solution.py:47
  16.3 9.5 %collective-permute-start.3 = (bf16[128,768]{1,0:T(8,128)(2,1)S(1)}, bf16[128,768]{1,0:T(8,128)(2,1)S(1)}, u32[]{:S(2)}, u32[]{:S(2)}) collective-permute-start(bf16[128,768]{1,0:T(8,128)(2,1)S(1)} %collective-permute-done.2.refs_4_), channel_id=1, source_target_pairs={{0,2},{1,3},{2,0},{3,1},{4,6},{5,7},{6,4},{7,5},{8,10},{9,11},{10,... | collective-permute-start | bytes 589832 | tf_op jit(solution)/shard_map/ppermute | solution.py:35
  18.0 8.4 %collective-permute-start.4 = (bf16[128,768]{1,0:T(8,128)(2,1)S(1)}, bf16[128,768]{1,0:T(8,128)(2,1)S(1)}, u32[]{:S(2)}, u32[]{:S(2)}) collective-permute-start(bf16[128,768]{1,0:T(8,128)(2,1)S(1)} %collective-permute-done.2.refs_4_), channel_id=1, source_target_pairs={{0,4},{4,0},{8,12},{12,8},{16,20},{20,16},{24,28},{28,24},{1,5},{5... | collective-permute-start | bytes 589832 | tf_op jit(solution)/shard_map/ppermute | solution.py:40
  24.3 7.8 %collective-permute-start.7 = (bf16[128,768]{1,0:T(8,128)(2,1)S(1)}, bf16[128,768]{1,0:T(8,128)(2,1)S(1)}, u32[]{:S(2)}, u32[]{:S(2)}) collective-permute-start(bf16[128,768]{1,0:T(8,128)(2,1)S(1)} %collective-permute-done.6.refs_8_), channel_id=1, source_target_pairs={{0,2},{1,3},{2,0},{3,1},{4,6},{5,7},{6,4},{7,5},{8,10},{9,11},{10,... | collective-permute-start | bytes 589832 | tf_op jit(solution)/shard_map/ppermute | solution.py:35
  25.8 6.2 %collective-permute-start.8 = (bf16[128,768]{1,0:T(8,128)(2,1)S(1)}, bf16[128,768]{1,0:T(8,128)(2,1)S(1)}, u32[]{:S(2)}, u32[]{:S(2)}) collective-permute-start(bf16[128,768]{1,0:T(8,128)(2,1)S(1)} %collective-permute-done.6.refs_8_), channel_id=1, source_target_pairs={{0,4},{4,0},{8,12},{12,8},{16,20},{20,16},{24,28},{28,24},{1,5},{5... | collective-permute-start | bytes 589832 | tf_op jit(solution)/shard_map/ppermute | solution.py:40
  25.8 9.5 %collective-permute-start.11 = (bf16[128,768]{1,0:T(8,128)(2,1)}, bf16[128,768]{1,0:T(8,128)(2,1)S(1)}, u32[]{:S(2)}, u32[]{:S(2)}) collective-permute-start(bf16[128,768]{1,0:T(8,128)(2,1)} %collective-permute-done.10.refs_1_.refs_12_), channel_id=1, source_target_pairs={{0,2},{1,3},{2,0},{3,1},{4,6},{5,7},{6,4},{7,5},{8,10},{9,11},{10,... | collective-permute-start | bytes 589832 | tf_op jit(solution)/shard_map/ppermute | solution.py:35
  26.4 9.9 %collective-permute-start.12 = (bf16[128,768]{1,0:T(8,128)(2,1)}, bf16[128,768]{1,0:T(8,128)(2,1)S(1)}, u32[]{:S(2)}, u32[]{:S(2)}) collective-permute-start(bf16[128,768]{1,0:T(8,128)(2,1)} %collective-permute-done.10.refs_1_.refs_12_), channel_id=1, source_target_pairs={{0,4},{4,0},{8,12},{12,8},{16,20},{20,16},{24,28},{28,24},{1,5},{5... | collective-permute-start | bytes 589832 | tf_op jit(solution)/shard_map/ppermute | solution.py:40
  32.1 3.4 %collective-permute-start.5 = (bf16[128,768]{1,0:T(8,128)(2,1)S(1)}, bf16[128,768]{1,0:T(8,128)(2,1)S(1)}, u32[]{:S(2)}, u32[]{:S(2)}) collective-permute-start(bf16[128,768]{1,0:T(8,128)(2,1)S(1)} %collective-permute-done.3.refs_5_), channel_id=1, source_target_pairs={{0,4},{4,0},{8,12},{12,8},{16,20},{20,16},{24,28},{28,24},{1,5},{5... | collective-permute-start | bytes 589832 | tf_op jit(solution)/shard_map/ppermute | solution.py:40
  32.1 3.4 %collective-permute-start.9 = (bf16[128,768]{1,0:T(8,128)(2,1)S(1)}, bf16[128,768]{1,0:T(8,128)(2,1)S(1)}, u32[]{:S(2)}, u32[]{:S(2)}) collective-permute-start(bf16[128,768]{1,0:T(8,128)(2,1)S(1)} %collective-permute-done.7.refs_9_), channel_id=1, source_target_pairs={{0,4},{4,0},{8,12},{12,8},{16,20},{20,16},{24,28},{28,24},{1,5},{5... | collective-permute-start | bytes 589832 | tf_op jit(solution)/shard_map/ppermute | solution.py:40
  35.3 43.7 %copy-start.2 = (bf16[128,768]{1,0:T(8,128)(2,1)}, bf16[128,768]{1,0:T(8,128)(2,1)S(1)}, u32[]{:S(2)}) copy-start(bf16[128,768]{1,0:T(8,128)(2,1)S(1)} %collective-permute-done.11.refs_2_.refs_13_) | copy-start | bytes 589828
  35.3 1.4 %collective-permute-start.13 = (bf16[128,768]{1,0:T(8,128)(2,1)S(1)}, bf16[128,768]{1,0:T(8,128)(2,1)S(1)}, u32[]{:S(2)}, u32[]{:S(2)}) collective-permute-start(bf16[128,768]{1,0:T(8,128)(2,1)S(1)} %collective-permute-done.11.refs_2_.refs_13_), channel_id=1, source_target_pairs={{0,4},{4,0},{8,12},{12,8},{16,20},{20,16},{24,28},{28,24},{1,5},{5... | collective-permute-start | bytes 589832 | tf_op jit(solution)/shard_map/ppermute | solution.py:40
  36.3 2.5 %copy-start = (bf16[256,2048]{1,0:T(8,128)(2,1)S(1)}, bf16[256,2048]{1,0:T(8,128)(2,1)}, u32[]{:S(2)}) copy-start(bf16[256,2048]{1,0:T(8,128)(2,1)} %get-tuple-element.25.tokens_ref) | copy-start | bytes 3145732
  36.3 42.8 %copy-start.4 = (bf16[128,768]{1,0:T(8,128)(2,1)}, bf16[128,768]{1,0:T(8,128)(2,1)S(1)}, u32[]{:S(2)}) copy-start(bf16[128,768]{1,0:T(8,128)(2,1)S(1)} %collective-permute-done.12.refs_3_.refs_14_) | copy-start | bytes 589828
  36.8 42.3 %copy-start.6 = (bf16[128,768]{1,0:T(8,128)(2,1)}, bf16[128,768]{1,0:T(8,128)(2,1)S(1)}, u32[]{:S(2)}) copy-start(bf16[128,768]{1,0:T(8,128)(2,1)S(1)} %collective-permute-done.13.refs_4_.refs_15_) | copy-start | bytes 589828
  38.1 6.0 %collective-permute-start.16 = (bf16[256,256]{1,0:T(8,128)(2,1)S(1)}, bf16[256,256]{1,0:T(8,128)(2,1)S(1)}, u32[]{:S(2)}, u32[]{:S(2)}) collective-permute-start(bf16[256,256]{1,0:T(8,128)(2,1)S(1)} %get-tuple-element.30), channel_id=1, source_target_pairs={{0,1},{1,0},{2,3},{3,2},{4,5},{5,4},{6,7},{7,6},{8,9},{9,8},{10,11... | collective-permute-start | bytes 393224 | tf_op jit(solution)/shard_map/ppermute | solution.py:28
  39.6 10.3 %copy-start.14 = (bf16[1,256,512]{2,1,0:T(8,128)(2,1)S(1)}, bf16[1,256,512]{2,1,0:T(8,128)(2,1)}, u32[]{:S(2)}) copy-start(bf16[1,256,512]{2,1,0:T(8,128)(2,1)} %param.7) | copy-start | bytes 786436
  40.9 12.0 %collective-permute-start.15 = (bf16[256,512]{1,0:T(8,128)(2,1)S(1)}, bf16[256,512]{1,0:T(8,128)(2,1)S(1)}, u32[]{:S(2)}, u32[]{:S(2)}) collective-permute-start(bf16[256,512]{1,0:T(8,128)(2,1)S(1)} %get-tuple-element.28), channel_id=1, source_target_pairs={{0,1},{1,0},{2,3},{3,2},{4,5},{5,4},{6,7},{7,6},{8,9},{9,8},{10,11... | collective-permute-start | bytes 786440 | tf_op jit(solution)/shard_map/ppermute | solution.py:28
  44.2 8.7 %collective-permute-start.17 = (bf16[256,256]{1,0:T(8,128)(2,1)S(1)}, bf16[256,256]{1,0:T(8,128)(2,1)S(1)}, u32[]{:S(2)}, u32[]{:S(2)}) collective-permute-start(bf16[256,256]{1,0:T(8,128)(2,1)S(1)} %add_convert_fusion.1.refs_2_), channel_id=1, source_target_pairs={{0,2},{1,3},{4,6},{5,7},{8,10},{9,11},{12,14},{13,15},{16,18},{17,... | collective-permute-start | bytes 393224 | tf_op jit(solution)/shard_map/ppermute | solution.py:53
  47.6 5.3 %collective-permute-start.18 = (bf16[256,256]{1,0:T(8,128)(2,1)S(1)}, bf16[256,256]{1,0:T(8,128)(2,1)S(1)}, u32[]{:S(2)}, u32[]{:S(2)}) collective-permute-start(bf16[256,256]{1,0:T(8,128)(2,1)S(1)} %add_convert_fusion.1.refs_2_), channel_id=1, source_target_pairs={{0,1},{1,2},{2,3},{4,5},{5,6},{6,7},{8,9},{9,10},{10,11},{12,13},{... | collective-permute-start | bytes 393224 | tf_op jit(solution)/shard_map/ppermute | solution.py:53
  59.2 19.3 %copy-start.8 = (bf16[256,512]{1,0:T(8,128)(2,1)}, bf16[256,512]{1,0:T(8,128)(2,1)S(1)}, u32[]{:S(2)}) copy-start(bf16[256,512]{1,0:T(8,128)(2,1)S(1)} %get-tuple-element.32.dquery_ref.dq_ref) | copy-start | bytes 786436
  59.2 6.9 %collective-permute-start.20 = (bf16[256,256]{1,0:T(8,128)(2,1)S(1)}, bf16[256,256]{1,0:T(8,128)(2,1)S(1)}, u32[]{:S(2)}, u32[]{:S(2)}) collective-permute-start(bf16[256,256]{1,0:T(8,128)(2,1)S(1)} %get-tuple-element.50), channel_id=1, source_target_pairs={{2,0},{3,1},{6,4},{7,5},{10,8},{11,9},{14,12},{15,13},{18,16},{19,... | collective-permute-start | bytes 393224 | tf_op jit(solution)/shard_map/ppermute | solution.py:53
  60.5 8.3 %collective-permute-start.19 = (bf16[256,256]{1,0:T(8,128)(2,1)S(1)}, bf16[256,256]{1,0:T(8,128)(2,1)S(1)}, u32[]{:S(2)}, u32[]{:S(2)}) collective-permute-start(bf16[256,256]{1,0:T(8,128)(2,1)S(1)} %get-tuple-element.49), channel_id=1, source_target_pairs={{1,0},{2,1},{3,2},{5,4},{6,5},{7,6},{9,8},{10,9},{11,10},{13,12},{... | collective-permute-start | bytes 393224 | tf_op jit(solution)/shard_map/ppermute | solution.py:53
  62.0 12.7 %collective-permute-start.21 = (bf16[256,512]{1,0:T(8,128)(2,1)S(1)}, bf16[256,512]{1,0:T(8,128)(2,1)S(1)}, u32[]{:S(2)}, u32[]{:S(2)}) collective-permute-start(bf16[256,512]{1,0:T(8,128)(2,1)S(1)} %get-tuple-element.32.dquery_ref.dq_ref), channel_id=1, source_target_pairs={{0,1},{1,0},{2,3},{3,2},{4,5},{5,4},{6,7},{7,6},{8,9},{9,8},{10,11... | collective-permute-start | bytes 786440 | tf_op jit(solution)/shard_map/ppermute | solution.py:28
  68.9 5.8 %collective-permute-start.22 = (bf16[256,256]{1,0:T(8,128)(2,1)S(1)}, bf16[256,256]{1,0:T(8,128)(2,1)S(1)}, u32[]{:S(2)}, u32[]{:S(2)}) collective-permute-start(bf16[256,256]{1,0:T(8,128)(2,1)S(1)} %add_convert_fusion.dpair_ref.dp_ref), channel_id=1, source_target_pairs={{0,1},{1,0},{2,3},{3,2},{4,5},{5,4},{6,7},{7,6},{8,9},{9,8},{10,11... | collective-permute-start | bytes 393224 | tf_op jit(solution)/shard_map/ppermute | solution.py:28
  75.7 0.9 copy-start.11
  76.6 7.4 %collective-permute-start.24 = (bf16[512,768]{1,0:T(8,128)(2,1)S(1)}, bf16[512,768]{1,0:T(8,128)(2,1)S(1)}, u32[]{:S(2)}, u32[]{:S(2)}) collective-permute-start(bf16[512,768]{1,0:T(8,128)(2,1)S(1)} %get-tuple-element.36), channel_id=1, source_target_pairs={{0,4},{4,0},{8,12},{12,8},{16,20},{20,16},{24,28},{28,24},{1,5},{5... | collective-permute-start | bytes 2359304 | tf_op jit(solution)/shard_map/ppermute | solution.py:40
  78.5 3.4 %copy-start.10 = (bf16[512,768]{1,0:T(8,128)(2,1)}, bf16[512,768]{1,0:T(8,128)(2,1)S(1)}, u32[]{:S(2)}) copy-start(bf16[512,768]{1,0:T(8,128)(2,1)S(1)} %get-tuple-element.41.keep_ref) | copy-start | bytes 2359300
  78.5 9.7 %collective-permute-start.28 = (bf16[512,768]{1,0:T(8,128)(2,1)}, bf16[512,768]{1,0:T(8,128)(2,1)}, u32[]{:S(2)}, u32[]{:S(2)}) collective-permute-start(bf16[512,768]{1,0:T(8,128)(2,1)} %get-tuple-element.42), channel_id=1, source_target_pairs={{0,4},{4,0},{8,12},{12,8},{16,20},{20,16},{24,28},{28,24},{1,5},{5... | collective-permute-start | bytes 2359304 | tf_op jit(solution)/shard_map/ppermute | solution.py:40
  82.0 32.7 %collective-permute-start.23 = (bf16[256,2048]{1,0:T(8,128)(2,1)}, bf16[256,2048]{1,0:T(8,128)(2,1)}, u32[]{:S(2)}, u32[]{:S(2)}) collective-permute-start(bf16[256,2048]{1,0:T(8,128)(2,1)} %width_grad.3), channel_id=1, source_target_pairs={{0,1},{1,0},{2,3},{3,2},{4,5},{5,4},{6,7},{7,6},{8,9},{9,8},{10,11... | collective-permute-start | bytes 3145736 | tf_op jit(solution)/shard_map/ppermute | solution.py:28
  84.9 26.8 %copy-start.3 = (bf16[128,768]{1,0:T(8,128)(2,1)S(1)}, bf16[128,768]{1,0:T(8,128)(2,1)}, u32[]{:S(2)}) copy-start(bf16[128,768]{1,0:T(8,128)(2,1)} %copy-done.2) | copy-start | bytes 589828
  84.9 26.8 %copy-start.5 = (bf16[128,768]{1,0:T(8,128)(2,1)S(1)}, bf16[128,768]{1,0:T(8,128)(2,1)}, u32[]{:S(2)}) copy-start(bf16[128,768]{1,0:T(8,128)(2,1)} %copy-done.4) | copy-start | bytes 589828
  84.9 26.8 %copy-start.7 = (bf16[128,768]{1,0:T(8,128)(2,1)S(1)}, bf16[128,768]{1,0:T(8,128)(2,1)}, u32[]{:S(2)}) copy-start(bf16[128,768]{1,0:T(8,128)(2,1)} %copy-done.6) | copy-start | bytes 589828
  84.9 26.8 %copy-start.9 = (bf16[256,512]{1,0:T(8,128)(2,1)S(1)}, bf16[256,512]{1,0:T(8,128)(2,1)}, u32[]{:S(2)}) copy-start(bf16[256,512]{1,0:T(8,128)(2,1)} %copy-done.8) | copy-start | bytes 786436
  87.4 12.3 %collective-permute-start.25 = (bf16[256,768]{1,0:T(8,128)(2,1)}, bf16[256,768]{1,0:T(8,128)(2,1)}, u32[]{:S(2)}, u32[]{:S(2)}) collective-permute-start(bf16[256,768]{1,0:T(8,128)(2,1)} %get-tuple-element.38), channel_id=1, source_target_pairs={{0,2},{1,3},{2,0},{3,1},{4,6},{5,7},{6,4},{7,5},{8,10},{9,11},{10,... | collective-permute-start | bytes 1179656 | tf_op jit(solution)/shard_map/ppermute | solution.py:35
  90.7 16.4 %collective-permute-start.29 = (bf16[256,768]{1,0:T(8,128)(2,1)}, bf16[256,768]{1,0:T(8,128)(2,1)}, u32[]{:S(2)}, u32[]{:S(2)}) collective-permute-start(bf16[256,768]{1,0:T(8,128)(2,1)} %get-tuple-element.44), channel_id=1, source_target_pairs={{0,2},{1,3},{2,0},{3,1},{4,6},{5,7},{6,4},{7,5},{8,10},{9,11},{10,... | collective-permute-start | bytes 1179656 | tf_op jit(solution)/shard_map/ppermute | solution.py:35
  101.6 15.8 %collective-permute-start.26 = (bf16[128,768]{1,0:T(8,128)(2,1)}, bf16[128,768]{1,0:T(8,128)(2,1)S(1)}, u32[]{:S(2)}, u32[]{:S(2)}) collective-permute-start(bf16[128,768]{1,0:T(8,128)(2,1)} %get-tuple-element.39), channel_id=1, source_target_pairs={{0,16},{4,20},{8,24},{12,28},{16,0},{20,4},{24,8},{28,12},{1,17},{... | collective-permute-start | bytes 589832 | tf_op jit(solution)/shard_map/ppermute | solution.py:47
  105.8 11.7 %collective-permute-start.27 = (bf16[128,768]{1,0:T(8,128)(2,1)}, bf16[128,768]{1,0:T(8,128)(2,1)}, u32[]{:S(2)}, u32[]{:S(2)}) collective-permute-start(bf16[128,768]{1,0:T(8,128)(2,1)} %get-tuple-element.40), channel_id=1, source_target_pairs={{0,24},{4,28},{8,0},{12,4},{16,8},{20,12},{24,16},{28,20},{1,25},{... | collective-permute-start | bytes 589832 | tf_op jit(solution)/shard_map/ppermute | solution.py:47
  109.1 10.0 %collective-permute-start.30 = (bf16[128,768]{1,0:T(8,128)(2,1)}, bf16[128,768]{1,0:T(8,128)(2,1)}, u32[]{:S(2)}, u32[]{:S(2)}) collective-permute-start(bf16[128,768]{1,0:T(8,128)(2,1)} %get-tuple-element.45), channel_id=1, source_target_pairs={{0,8},{4,12},{8,16},{12,20},{16,24},{20,28},{24,0},{28,4},{1,9},{5... | collective-permute-start | bytes 589832 | tf_op jit(solution)/shard_map/ppermute | solution.py:47
  113.6 1.0 copy-start.1
  117.4 1.7 %copy-start.16 = (bf16[128,768]{1,0:T(8,128)(2,1)}, bf16[128,768]{1,0:T(8,128)(2,1)S(1)}, u32[]{:S(2)}) copy-start(bf16[128,768]{1,0:T(8,128)(2,1)S(1)} %collective-permute-done.26.refs_0_) | copy-start | bytes 589828
  (1 other events, 0.9 us)

commit v4 on v3

--- a/solution.py
+++ b/solution.py
@@ -58,8 +58,8 @@
     chip, core = dp_index // CORES, dp_index % CORES
     around, x = place // PAIR, (place + flip) % PAIR
     order = []
-    for k in range(chips):
-        for c in range(CORES):
+    for c in range(CORES):
+        for k in range(chips):
             for j in range(rest):
                 shard = CORES * ((chip - k + chips) % chips) + (core + c) % CORES
                 order.append(shard * (PAIR * rest) + PAIR * ((around - j + rest) % rest) + x)
@@ -70,28 +70,29 @@
     return pl.ds(pl.multiple_of(index * width, width), width)
 
 
-def split_kernel(chips, rest, width, in_ref, mine_ref, other_ref):
-    mine, other = block_order(chips, rest, 0), block_order(chips, rest, 1)
-    for i in range(len(mine)):
-        out = slice(i * width, (i + 1) * width)
-        other_ref[:, out] = in_ref[:, lanes(other[i], width)]
-        mine_ref[:, out] = in_ref[:, lanes(mine[i], width)]
+def split_kernel(chips, rest, width, in_ref, *out_refs):
+    for flip in range(PAIR):
+        order = block_order(chips, rest, flip)
+        count = len(order) // CORES
+        for i, block in enumerate(order):
+            at = slice(i % count * width, (i % count + 1) * width)
+            out_refs[flip * CORES + i // count][:, at] = in_ref[:, lanes(block, width)]
 
 
 def split_tokens(tokens, chips, rest, width):
     rows, total = tokens.shape
-    half = total // 2
+    parts = PAIR * CORES
     if width % 128:
         blocks = tokens.reshape(rows, total // width, width)
-        orders = [jnp.stack(block_order(chips, rest, flip)) for flip in range(PAIR)]
-        return [jnp.take(blocks, order, axis=1).reshape(rows, half) for order in orders]
+        order = jnp.stack(block_order(chips, rest, 0) + block_order(chips, rest, 1))
+        return jnp.split(jnp.take(blocks, order, axis=1).reshape(rows, total), parts, axis=1)
     tile = min(rows, 128)
     return pl.pallas_call(
         functools.partial(split_kernel, chips, rest, width),
         grid=(rows // tile,),
         in_specs=[pl.BlockSpec((tile, total), lambda i: (i, 0))],
-        out_specs=[pl.BlockSpec((tile, half), lambda i: (i, 0))] * 2,
-        out_shape=[jax.ShapeDtypeStruct((rows, half), tokens.dtype)] * 2,
+        out_specs=[pl.BlockSpec((tile, total // parts), lambda i: (i, 0))] * parts,
+        out_shape=[jax.ShapeDtypeStruct((rows, total // parts), tokens.dtype)] * parts,
         name="split_tokens",
     )(tokens)
 
@@ -122,7 +123,7 @@
     )(mine, other)
 
 
-def project_kernel(first, span, per, qwidth, has_sum, tokens_ref, *refs):
+def project_kernel(span, per, qwidth, has_sum, tokens_ref, *refs):
     if has_sum:
         sum_ref, refs = refs[0], refs[1:]
         total = sum_ref[...]
@@ -131,7 +132,7 @@
     pieces = refs[:-2] if qwidth else refs[:-1]
     for g in range(len(pieces) // per):
         rows = jnp.concatenate([r[...] for r in pieces[g * per : (g + 1) * per]], axis=0)
-        term = dot(tokens_ref[:, (first + g) * span : (first + g + 1) * span], rows)
+        term = dot(tokens_ref[:, g * span : (g + 1) * span], rows)
         total = term if total is None else total + term
     if qwidth:
         query_ref, pair_ref = refs[-2:]
@@ -141,7 +142,7 @@
         refs[-1][...] = total
 
 
-def project(tokens, groups, first, qwidth=0, kind=F32, so_far=None):
+def project(tokens, groups, qwidth=0, kind=F32, so_far=None):
     rows = tokens.shape[0]
     cols = groups[0][0].shape[1]
     pieces = [piece for group in groups for piece in group]
@@ -149,7 +150,7 @@
     widths = [qwidth, cols - qwidth] if qwidth else [cols]
     sums = [] if so_far is None else [so_far]
     outs = pl.pallas_call(
-        functools.partial(project_kernel, first, span, len(groups[0]), qwidth, len(sums)),
+        functools.partial(project_kernel, span, len(groups[0]), qwidth, len(sums)),
         in_specs=[VMEM] * (1 + len(sums) + len(pieces)),
         out_specs=[VMEM] * len(widths),
         out_shape=[jax.ShapeDtypeStruct((rows, w), kind) for w in widths],
@@ -181,69 +182,32 @@
     )(dquery, dpair, *pieces)
 
 
-def weight_kernel(steps, span, tokens_ref, other_ref, dq_ref, dp_ref, dq_other_ref, dp_other_ref, keep_ref, send_ref):
-    mine = jnp.concatenate([dq_ref[...], dp_ref[...]], axis=1)
-    other = jnp.concatenate([dq_other_ref[...], dp_other_ref[...]], axis=1)
-    both = jnp.concatenate([mine, other], axis=0)
-    half = span // 2
+def weight_kernel(steps, rest, width, count, *refs):
+    tokens, dquery, dpair = refs[:count], refs[count : 2 * count], refs[2 * count : 3 * count]
+    outs = refs[3 * count :]
+    right = jnp.concatenate(
+        [jnp.concatenate([q[...], p[...]], axis=1) for q, p in zip(dquery, dpair)], axis=0
+    )
+    span = rest * width
     for i, k in enumerate(steps):
-        cut = slice(k * span, (k + 1) * span)
-        left = jnp.concatenate([tokens_ref[:, cut], other_ref[:, cut]], axis=0)
-        total = dot(left.T, both).astype(BF16)
-        keep_ref[i * half : (i + 1) * half, :] = total[:half]
-        send_ref[i * half : (i + 1) * half, :] = total[half:]
-
-
-def weight_terms(tokens, other, steps, span, grads):
-    cols = grads[0].shape[1] + grads[1].shape[1]
-    return pl.pallas_call(
-        functools.partial(weight_kernel, steps, span),
-        in_specs=[VMEM] * 6,
-        out_specs=[VMEM] * 2,
-        out_shape=[jax.ShapeDtypeStruct((len(steps) * span // 2, cols), BF16)] * 2,
+        left = jnp.concatenate([t[:, k * span : (k + 1) * span] for t in tokens], axis=0)
+        total = dot(left.T, right)
+        for j in range(rest):
+            out = outs[i * rest + j]
+            out[...] = total[j * width : (j + 1) * width].astype(out.dtype)
+
+
+def weight_terms(steps, rest, width, tokens, dquery, dpair):
+    cols = dquery[0].shape[1] + dpair[0].shape[1]
+    count = len(tokens)
+    return pl.pallas_call(
+        functools.partial(weight_kernel, steps, rest, width, count),
+        in_specs=[VMEM] * (3 * count),
+        out_specs=[VMEM] * (len(steps) * rest),
+        out_shape=[jax.ShapeDtypeStruct((width, cols), BF16 if j else F32) for _ in steps for j in range(rest)],
         compiler_params=pltpu.CompilerParams(vmem_limit_bytes=48 * 2**20),
         name="weight_terms",
-    )(tokens, other, *grads)
-
-
-def core_sum_kernel(rest, width, keep_ref, from_ref, *out_refs):
-    total = (keep_ref[...].astype(F32) + from_ref[...].astype(F32)).astype(BF16)
-    for i in range(total.shape[0] // (rest * width)):
-        for j in range(rest):
-            source = (i * rest + j) * width
-            out_refs[j][i * width : (i + 1) * width, :] = total[source : source + width]
-
-
-def core_sum(keep, received, rest, width):
-    rows, cols = keep.shape
-    return pl.pallas_call(
-        functools.partial(core_sum_kernel, rest, width),
-        in_specs=[VMEM] * 2,
-        out_specs=[VMEM] * rest,
-        out_shape=[jax.ShapeDtypeStruct((rows // rest, cols), BF16)] * rest,
-        name="core_sum",
-    )(keep, received)
-
-
-def sum_kernel(width, *refs):
-    count = refs[0].shape[0] // width
-    terms, outs = refs[:-count], refs[-count:]
-    total = terms[0][...].astype(F32)
-    for ref in terms[1:]:
-        total = total + ref[...].astype(F32)
-    for i, ref in enumerate(outs):
-        ref[...] = total[i * width : (i + 1) * width].astype(ref.dtype)
-
-
-def sum_terms(terms, width, kinds):
-    cols = terms[0].shape[1]
-    return pl.pallas_call(
-        functools.partial(sum_kernel, width),
-        in_specs=[VMEM] * len(terms),
-        out_specs=[VMEM] * len(kinds),
-        out_shape=[jax.ShapeDtypeStruct((width, cols), kind) for kind in kinds],
-        name="sum_terms",
-    )(*terms)
+    )(*tokens, *dquery, *dpair)
 
 
 def attend_kernel(
@@ -333,27 +297,22 @@
     width = shard_rows // seq_count
     back = -(-(local * seq_count // 2 - 1) // local)
 
-    tokens_mine, tokens_sent = split_tokens(tokens, chips, rest, width)
-    tokens_other = swap_x(tokens_sent)
+    mine_own, mine_across, *sent = split_tokens(tokens, chips, rest, width)
+    other_own, other_across = [swap_x(part) for part in sent]
 
     blocks = weights.reshape(seq_count, width, cols)
-    groups = []
-    for k in range(chips):
-        if k == 0:
-            places = [PAIR * ((place // PAIR - j + rest) % rest) + place % PAIR for j in range(rest)]
-            here = [lax.dynamic_index_in_dim(blocks, p, 0, keepdims=False) for p in places]
-            own = here[0]
-        else:
-            first = shift_chip(own, k)
-            here = [first] + [shift_rest(first, j) for j in range(1, rest)]
-        groups.append(here + [swap_core(piece) for piece in here])
-
-    early, late, last = groups[:-1], groups[-1:], chips - 1
-    so_far = project(tokens_other, early, 0)
-    query_sent, pair_sent = project(tokens_other, late, last, qwidth, BF16, so_far)
+    places = [PAIR * ((place // PAIR - j + rest) % rest) + place % PAIR for j in range(rest)]
+    groups_own = [[lax.dynamic_index_in_dim(blocks, p, 0, keepdims=False) for p in places]]
+    for k in range(1, chips):
+        first = shift_chip(groups_own[0][0], k)
+        groups_own.append([first] + [shift_rest(first, j) for j in range(1, rest)])
+    groups_across = [[swap_core(piece) for piece in group] for group in groups_own]
+
+    so_far = project(other_own, groups_own)
+    query_sent, pair_sent = project(other_across, groups_across, qwidth, BF16, so_far)
     pair_from, query_from = swap_x(pair_sent), swap_x(query_sent)
-    so_far = project(tokens_mine, early, 0)
-    query, pair = project(tokens_mine, late, last, qwidth, F32, so_far)
+    so_far = project(mine_own, groups_own)
+    query, pair = project(mine_across, groups_across, qwidth, F32, so_far)
     pair = (pair + pair_from.astype(F32)).astype(BF16)
 
     doc_row, flag_row = doc_lengths[0], kept_flags[0]
@@ -371,18 +330,21 @@
     dpair = dpair.astype(BF16)
     dpair_other = swap_x(dpair)
 
-    span = CORES * rest * width
-    grads = (dquery, dpair, dquery_other, dpair_other)
+    left = [mine_own, other_own, swap_core(mine_across), swap_core(other_across)]
+    right = [[mine, other, swap_core(mine), swap_core(other)] for mine, other in ((dquery, dquery_other), (dpair, dpair_other))]
     order = sorted(range(chips), key=lambda k: (k == 0, -min(k, chips - k), k))
-    finished = []
+    weights_grad = None
     for steps in (order[: chips // 2], order[chips // 2 :]):
-        keep, sent = weight_terms(tokens_mine, tokens_other, steps, span, grads)
-        kept_here, *sent = core_sum(keep, swap_core(sent), rest, width)
-        terms = [kept_here] + [shift_rest(piece, -j) for j, piece in enumerate(sent, 1)]
-        parts = sum_terms(terms, width, [BF16 if k else F32 for k in steps])
-        finished += [shift_chip(part, -k) if k else part for k, part in zip(steps, parts)]
-    (weights_grad,) = sum_terms(finished, width, [F32])
-
+        terms = weight_terms(steps, rest, width, left, *right)
+        for i, k in enumerate(steps):
+            part, *sent = terms[i * rest : (i + 1) * rest]
+            for j, piece in enumerate(sent, 1):
+                part = part + shift_rest(piece, -j).astype(F32)
+            if k:
+                part = shift_chip(part.astype(BF16), -k).astype(F32)
+            weights_grad = part if weights_grad is None else weights_grad + part
+
+    groups = groups_own + groups_across
     grad_from = swap_x(width_grad(dquery_other, dpair_other, groups))
     inputs_grad = merge_halves(width_grad(dquery, dpair, groups), grad_from, chips, rest, width)
     return (attention[None], inputs_grad[None], weights_grad)

time: 123 us -> 119 us (0.967)
  Pallas kernels: 35 us -> 18.4 us
  waiting for transfers between devices: 40.3 us -> 47.2 us
  starting transfers between devices: 41.7 us -> 47.3 us
    pallas_call x11 -> x6, Pallas kernels: 18.2 us -> 4.38 us  [the longest x4 2.33 us: project(): pl.pallas_call(functools.partial(project_kernel, span, len(groups[0]), qw...]
    pallas_call x2, Pallas kernels: 4.86 us -> 2.03 us  [width_grad(): pl.pallas_call(functools.partial(grad_kernel, span, len(groups[0])), in_s...]
    ppermute x6 -> x7, waiting for transfers between devices: 4.61 us -> 7.06 us  [swap_x(): return lax.ppermute(array, 'seq', [(i, i ^ 1) for i in range(count)])]
    ppermute x5 -> x7, waiting for transfers between devices: 16.2 us -> 18.6 us  [shift_rest(): return lax.ppermute(array, 'seq', pairs)]
    ppermute x5 -> x7, starting transfers between devices: 5.63 us -> 7.97 us  [shift_rest(): return lax.ppermute(array, 'seq', pairs)]
    ppermute x6, starting transfers between devices: 13.6 us -> 15.3 us  [shift_chip(): return lax.ppermute(array, 'dp', pairs)]
    ppermute x6, waiting for transfers between devices: 11.9 us -> 13.5 us  [shift_chip(): return lax.ppermute(array, 'dp', pairs)]
    ppermute x10 -> x14, waiting for transfers between devices: 0.49 us -> 1.76 us  [swap_core(): return lax.ppermute(array, 'dp', [(i, i ^ 1) for i in range(count)])]
  transfers between devices with their start and end apart: 31 -> 38, of which waited for: 13 -> 19; matrix products, arithmetic and copies ran while one was open for 0% -> 1% of each run, Pallas kernels for 18% -> 12%
where the time goes in v4:
time: 119 us; the launch traced here: 118 us
  starting transfers between devices  47.3 us (40%)
  waiting for transfers between devices  47.2 us (40%)
  Pallas kernels  18.4 us (15%)
  local copies, waits for them, and re-layouts  3.09 us (3%)
  other arithmetic  1.41 us (1%)
    ppermute x7, waiting for transfers between devices, shift_rest(): return lax.ppermute(array, 'seq', pairs)  18.6 us
    ppermute x6, starting transfers between devices, shift_chip(): return lax.ppermute(array, 'dp', pairs)  15.3 us
    ppermute x6, waiting for transfers between devices, shift_chip(): return lax.ppermute(array, 'dp', pairs)  13.5 us
    ppermute x7, starting transfers between devices, swap_x(): return lax.ppermute(array, 'seq', [(i, i ^ 1) for i in range(count)])  12.1 us
    ppermute x4, starting transfers between devices, shift_seq(): return lax.ppermute(array, 'seq', pairs)  9.57 us
    ppermute x7, starting transfers between devices, shift_rest(): return lax.ppermute(array, 'seq', pairs)  7.97 us
    ppermute x7, waiting for transfers between devices, swap_x(): return lax.ppermute(array, 'seq', [(i, i ^ 1) for i in range(count)])  7.06 us
    pallas_call x1, Pallas kernels, attend(): pl.pallas_call(functools.partial(attend_kernel, width // HEAD_DIM, back),...  6.31 us
  transfers between devices with their start and end apart: 38, of which 19 were waited for; matrix products, arithmetic and copies ran while one was open for 1% of the time, Pallas kernels for 12%

profile of v4, /device:TPU:0, one launch (start us, length us, event | category | flops | bytes accessed | tf_op | source)
XLA Modules:
  0.0 118.2 jit_solution(4055520994660922914)
XLA Ops:
  0.7 1.1 dynamic-slice_bitcast_fusion
  1.8 3.1 %collective-permute-start = (bf16[128,768]{1,0:T(8,128)(2,1)S(1)}, bf16[128,768]{1,0:T(8,128)(2,1)S(1)}, u32[]{:S(2)}, u32[]{:S(2)}) collective-permute-start(bf16[128,768]{1,0:T(8,128)(2,1)S(1)} %get-tuple-element.44.refs_0_), channel_id=1, source_target_pairs={{0,8},{4,12},{8,16},{12,20},{16,24},{20,28},{24,0},{28,4},{1,9},{5... | collective-permute-start | bytes 589832 | tf_op jit(solution)/shard_map/ppermute | solution.py:47
  4.8 2.6 %collective-permute-start.2 = (bf16[128,768]{1,0:T(8,128)(2,1)S(1)}, bf16[128,768]{1,0:T(8,128)(2,1)S(1)}, u32[]{:S(2)}, u32[]{:S(2)}) collective-permute-start(bf16[128,768]{1,0:T(8,128)(2,1)S(1)} %get-tuple-element.44.refs_0_), channel_id=1, source_target_pairs={{0,16},{4,20},{8,24},{12,28},{16,0},{20,4},{24,8},{28,12},{1,17},{... | collective-permute-start | bytes 589832 | tf_op jit(solution)/shard_map/ppermute | solution.py:47
  7.4 1.3 %collective-permute-start.4 = (bf16[128,768]{1,0:T(8,128)(2,1)S(1)}, bf16[128,768]{1,0:T(8,128)(2,1)S(1)}, u32[]{:S(2)}, u32[]{:S(2)}) collective-permute-start(bf16[128,768]{1,0:T(8,128)(2,1)S(1)} %get-tuple-element.44.refs_0_), channel_id=1, source_target_pairs={{0,24},{4,28},{8,0},{12,4},{16,8},{20,12},{24,16},{28,20},{1,25},{... | collective-permute-start | bytes 589832 | tf_op jit(solution)/shard_map/ppermute | solution.py:47
  8.8 2.8 %split_tokens.1 = (bf16[256,1024]{1,0:T(8,128)(2,1)}, bf16[256,1024]{1,0:T(8,128)(2,1)}, bf16[256,1024]{1,0:T(8,128)(2,1)}, bf16[256,1024]{1,0:T(8,128)(2,1)}) custom-call(bf16[256,4096]{1,0:T(8,128)(2,1)} %bitcast.22), custom_call_target="tpu_custom_call" | custom-call | tf_op jit(solution)/shard_map/split_tokens/pallas_call | solution.py:90
  11.6 1.5 %collective-permute-start.15 = (bf16[256,1024]{1,0:T(8,128)(2,1)}, bf16[256,1024]{1,0:T(8,128)(2,1)S(1)}, u32[]{:S(2)}, u32[]{:S(2)}) collective-permute-start(bf16[256,1024]{1,0:T(8,128)(2,1)} %get-tuple-element.27), channel_id=1, source_target_pairs={{0,1},{1,0},{2,3},{3,2},{4,5},{5,4},{6,7},{7,6},{8,9},{9,8},{10,11... | collective-permute-start | bytes 1572872 | tf_op jit(solution)/shard_map/ppermute | solution.py:28
  13.6 6.7 %collective-permute-done.2.refs_4_ = bf16[128,768]{1,0:T(8,128)(2,1)S(1)} collective-permute-done((bf16[128,768]{1,0:T(8,128)(2,1)S(1)}, bf16[128,768]{1,0:T(8,128)(2,1)S(1)}, u32[]{:S(2)}, u32[]{:S(2)}) %collective-permute-start.2) | collective-permute-done | bytes 196640 | tf_op jit(solution)/shard_map/ppermute | solution.py:47
  20.3 1.5 %collective-permute-start.1 = (bf16[128,768]{1,0:T(8,128)(2,1)S(1)}, bf16[128,768]{1,0:T(8,128)(2,1)S(1)}, u32[]{:S(2)}, u32[]{:S(2)}) collective-permute-start(bf16[128,768]{1,0:T(8,128)(2,1)S(1)} %collective-permute-done.refs_2_), channel_id=1, source_target_pairs={{0,2},{1,3},{2,0},{3,1},{4,6},{5,7},{6,4},{7,5},{8,10},{9,11},{10,... | collective-permute-start | bytes 589832 | tf_op jit(solution)/shard_map/ppermute | solution.py:35
  22.4 1.5 %collective-permute-start.14 = (bf16[256,1024]{1,0:T(8,128)(2,1)}, bf16[256,1024]{1,0:T(8,128)(2,1)S(1)}, u32[]{:S(2)}, u32[]{:S(2)}) collective-permute-start(bf16[256,1024]{1,0:T(8,128)(2,1)} %get-tuple-element.26), channel_id=1, source_target_pairs={{0,1},{1,0},{2,3},{3,2},{4,5},{5,4},{6,7},{7,6},{8,9},{9,8},{10,11... | collective-permute-start | bytes 1572872 | tf_op jit(solution)/shard_map/ppermute | solution.py:28
  24.0 4.1 %collective-permute-done.1.refs_3_ = bf16[128,768]{1,0:T(8,128)(2,1)S(1)} collective-permute-done((bf16[128,768]{1,0:T(8,128)(2,1)S(1)}, bf16[128,768]{1,0:T(8,128)(2,1)S(1)}, u32[]{:S(2)}, u32[]{:S(2)}) %collective-permute-start.1) | collective-permute-done | bytes 196640 | tf_op jit(solution)/shard_map/ppermute | solution.py:35
  28.1 3.2 %collective-permute-done.3.refs_5_ = bf16[128,768]{1,0:T(8,128)(2,1)S(1)} collective-permute-done((bf16[128,768]{1,0:T(8,128)(2,1)S(1)}, bf16[128,768]{1,0:T(8,128)(2,1)S(1)}, u32[]{:S(2)}, u32[]{:S(2)}) %collective-permute-start.3) | collective-permute-done | bytes 196640 | tf_op jit(solution)/shard_map/ppermute | solution.py:35
  31.3 1.5 %collective-permute-start.5 = (bf16[128,768]{1,0:T(8,128)(2,1)S(1)}, bf16[128,768]{1,0:T(8,128)(2,1)S(1)}, u32[]{:S(2)}, u32[]{:S(2)}) collective-permute-start(bf16[128,768]{1,0:T(8,128)(2,1)S(1)} %collective-permute-done.4.refs_6_), channel_id=1, source_target_pairs={{0,2},{1,3},{2,0},{3,1},{4,6},{5,7},{6,4},{7,5},{8,10},{9,11},{10,... | collective-permute-start | bytes 589832 | tf_op jit(solution)/shard_map/ppermute | solution.py:35
  32.8 4.4 %collective-permute-done.5.refs_7_ = bf16[128,768]{1,0:T(8,128)(2,1)S(1)} collective-permute-done((bf16[128,768]{1,0:T(8,128)(2,1)S(1)}, bf16[128,768]{1,0:T(8,128)(2,1)S(1)}, u32[]{:S(2)}, u32[]{:S(2)}) %collective-permute-start.5) | collective-permute-done | bytes 196640 | tf_op jit(solution)/shard_map/ppermute | solution.py:35
  39.4 0.6 project.7
  40.0 1.5 %collective-permute-start.17 = (bf16[256,256]{1,0:T(8,128)(2,1)S(1)}, bf16[256,256]{1,0:T(8,128)(2,1)S(1)}, u32[]{:S(2)}, u32[]{:S(2)}) collective-permute-start(bf16[256,256]{1,0:T(8,128)(2,1)S(1)} %get-tuple-element.30), channel_id=1, source_target_pairs={{0,1},{1,0},{2,3},{3,2},{4,5},{5,4},{6,7},{7,6},{8,9},{9,8},{10,11... | collective-permute-start | bytes 393224 | tf_op jit(solution)/shard_map/ppermute | solution.py:28
  42.1 0.6 collective-permute-start.16
  42.8 0.6 project.5
  43.4 3.0 %collective-permute-done.17 = bf16[256,256]{1,0:T(8,128)(2,1)S(1)} collective-permute-done((bf16[256,256]{1,0:T(8,128)(2,1)S(1)}, bf16[256,256]{1,0:T(8,128)(2,1)S(1)}, u32[]{:S(2)}, u32[]{:S(2)}) %collective-permute-start.17) | collective-permute-done | bytes 131104 | tf_op jit(solution)/shard_map/ppermute | solution.py:28
  46.4 3.4 %collective-permute-start.18 = (bf16[256,256]{1,0:T(8,128)(2,1)S(1)}, bf16[256,256]{1,0:T(8,128)(2,1)S(1)}, u32[]{:S(2)}, u32[]{:S(2)}) collective-permute-start(bf16[256,256]{1,0:T(8,128)(2,1)S(1)} %add_convert_fusion.4.refs_2_), channel_id=1, source_target_pairs={{0,2},{1,3},{4,6},{5,7},{8,10},{9,11},{12,14},{13,15},{16,18},{17,... | collective-permute-start | bytes 393224 | tf_op jit(solution)/shard_map/ppermute | solution.py:53
  49.8 3.4 %collective-permute-start.19 = (bf16[256,256]{1,0:T(8,128)(2,1)S(1)}, bf16[256,256]{1,0:T(8,128)(2,1)S(1)}, u32[]{:S(2)}, u32[]{:S(2)}) collective-permute-start(bf16[256,256]{1,0:T(8,128)(2,1)S(1)} %add_convert_fusion.4.refs_2_), channel_id=1, source_target_pairs={{0,1},{1,2},{2,3},{4,5},{5,6},{6,7},{8,9},{9,10},{10,11},{12,13},{... | collective-permute-start | bytes 393224 | tf_op jit(solution)/shard_map/ppermute | solution.py:53
  53.7 2.0 %collective-permute-done.19.refs_1_ = bf16[256,256]{1,0:T(8,128)(2,1)S(1)} collective-permute-done((bf16[256,256]{1,0:T(8,128)(2,1)S(1)}, bf16[256,256]{1,0:T(8,128)(2,1)S(1)}, u32[]{:S(2)}, u32[]{:S(2)}) %collective-permute-start.19) | collective-permute-done | bytes 131104 | tf_op jit(solution)/shard_map/ppermute | solution.py:53
  55.8 6.3 %attend.1 = (bf16[256,512]{1,0:T(8,128)(2,1)}, bf16[256,512]{1,0:T(8,128)(2,1)S(1)}, f32[256,256]{1,0:T(8,128)S(1)}, bf16[512,256]{1,0:T(8,128)(2,1)S(1)}) custom-call(s32[8]{0:T(128)S(1)} %bitcast.21, f32[256,512]{1,0:T(8,128)S(1)} %get-tuple-element.25.q_ref, bf16[256,512]{1,0:T(8,128)(2,1)S(1)} %collective-permute-done.16.q_from_ref, ...), custom_call_target="tpu_custom_call" | custom-call | tf_op jit(solution)/shard_map/attend/pallas_call | solution.py:266
  62.1 1.3 %collective-permute-start.21 = (bf16[256,256]{1,0:T(8,128)(2,1)S(1)}, bf16[256,256]{1,0:T(8,128)(2,1)S(1)}, u32[]{:S(2)}, u32[]{:S(2)}) collective-permute-start(bf16[256,256]{1,0:T(8,128)(2,1)S(1)} %get-tuple-element.46), channel_id=1, source_target_pairs={{2,0},{3,1},{6,4},{7,5},{10,8},{11,9},{14,12},{15,13},{18,16},{19,... | collective-permute-start | bytes 393224 | tf_op jit(solution)/shard_map/ppermute | solution.py:53
  63.4 1.5 %collective-permute-start.20 = (bf16[256,256]{1,0:T(8,128)(2,1)S(1)}, bf16[256,256]{1,0:T(8,128)(2,1)S(1)}, u32[]{:S(2)}, u32[]{:S(2)}) collective-permute-start(bf16[256,256]{1,0:T(8,128)(2,1)S(1)} %get-tuple-element.45), channel_id=1, source_target_pairs={{1,0},{2,1},{3,2},{5,4},{6,5},{7,6},{9,8},{10,9},{11,10},{13,12},{... | collective-permute-start | bytes 393224 | tf_op jit(solution)/shard_map/ppermute | solution.py:53
  64.9 3.1 %collective-permute-start.22 = (bf16[256,512]{1,0:T(8,128)(2,1)S(1)}, bf16[256,512]{1,0:T(8,128)(2,1)S(1)}, u32[]{:S(2)}, u32[]{:S(2)}) collective-permute-start(bf16[256,512]{1,0:T(8,128)(2,1)S(1)} %get-tuple-element.32.dquery_ref.refs_4_), channel_id=1, source_target_pairs={{0,1},{1,0},{2,3},{3,2},{4,5},{5,4},{6,7},{7,6},{8,9},{9,8},{10,11... | collective-permute-start | bytes 786440 | tf_op jit(solution)/shard_map/ppermute | solution.py:28
  68.1 0.9 collective-permute-done.21
  68.9 3.0 %collective-permute-done.20 = bf16[256,256]{1,0:T(8,128)(2,1)S(1)} collective-permute-done((bf16[256,256]{1,0:T(8,128)(2,1)S(1)}, bf16[256,256]{1,0:T(8,128)(2,1)S(1)}, u32[]{:S(2)}, u32[]{:S(2)}) %collective-permute-start.20) | collective-permute-done | bytes 131104 | tf_op jit(solution)/shard_map/ppermute | solution.py:53
  72.0 2.5 %collective-permute-start.23 = (bf16[256,256]{1,0:T(8,128)(2,1)S(1)}, bf16[256,256]{1,0:T(8,128)(2,1)S(1)}, u32[]{:S(2)}, u32[]{:S(2)}) collective-permute-start(bf16[256,256]{1,0:T(8,128)(2,1)S(1)} %add_convert_fusion.3.dpair_ref.refs_8_), channel_id=1, source_target_pairs={{0,1},{1,0},{2,3},{3,2},{4,5},{5,4},{6,7},{7,6},{8,9},{9,8},{10,11... | collective-permute-start | bytes 393224 | tf_op jit(solution)/shard_map/ppermute | solution.py:28
  74.6 3.0 %collective-permute-done.22.dquery_ref.refs_5_ = bf16[256,512]{1,0:T(8,128)(2,1)S(1)} collective-permute-done((bf16[256,512]{1,0:T(8,128)(2,1)S(1)}, bf16[256,512]{1,0:T(8,128)(2,1)S(1)}, u32[]{:S(2)}, u32[]{:S(2)}) %collective-permute-start.22) | collective-permute-done | bytes 262176 | tf_op jit(solution)/shard_map/ppermute | solution.py:28
  78.1 1.0 collective-permute-done.23.dpair_ref.refs_9_
  79.3 1.1 collective-permute-done.30.refs_11_
  80.5 1.0 weight_terms.3
  81.5 2.3 %collective-permute-start.35 = (bf16[128,768]{1,0:T(8,128)(2,1)S(1)}, bf16[128,768]{1,0:T(8,128)(2,1)S(1)}, u32[]{:S(2)}, u32[]{:S(2)}) collective-permute-start(bf16[128,768]{1,0:T(8,128)(2,1)S(1)} %get-tuple-element.40), channel_id=1, source_target_pairs={{0,2},{1,3},{2,0},{3,1},{4,6},{5,7},{6,4},{7,5},{8,10},{9,11},{10,... | collective-permute-start | bytes 589832 | tf_op jit(solution)/shard_map/ppermute | solution.py:35
  83.8 1.0 width_grad.3
  84.8 1.3 %collective-permute-start.24 = (bf16[256,2048]{1,0:T(8,128)(2,1)S(1)}, bf16[256,2048]{1,0:T(8,128)(2,1)S(1)}, u32[]{:S(2)}, u32[]{:S(2)}) collective-permute-start(bf16[256,2048]{1,0:T(8,128)(2,1)S(1)} %width_grad.3), channel_id=1, source_target_pairs={{0,1},{1,0},{2,3},{3,2},{4,5},{5,4},{6,7},{7,6},{8,9},{9,8},{10,11... | collective-permute-start | bytes 3145736 | tf_op jit(solution)/shard_map/ppermute | solution.py:28
  86.1 1.0 weight_terms.2
  87.2 2.1 %collective-permute-start.33 = (bf16[128,768]{1,0:T(8,128)(2,1)S(1)}, bf16[128,768]{1,0:T(8,128)(2,1)S(1)}, u32[]{:S(2)}, u32[]{:S(2)}) collective-permute-start(bf16[128,768]{1,0:T(8,128)(2,1)S(1)} %get-tuple-element.38), channel_id=1, source_target_pairs={{0,2},{1,3},{2,0},{3,1},{4,6},{5,7},{6,4},{7,5},{8,10},{9,11},{10,... | collective-permute-start | bytes 589832 | tf_op jit(solution)/shard_map/ppermute | solution.py:35
  89.5 1.8 %collective-permute-start.36 = (bf16[128,768]{1,0:T(8,128)(2,1)S(1)}, bf16[128,768]{1,0:T(8,128)(2,1)S(1)}, u32[]{:S(2)}, u32[]{:S(2)}) collective-permute-start(bf16[128,768]{1,0:T(8,128)(2,1)S(1)} %add_convert_fusion), channel_id=1, source_target_pairs={{0,8},{4,12},{8,16},{12,20},{16,24},{20,28},{24,0},{28,4},{1,9},{5... | collective-permute-start | bytes 589832 | tf_op jit(solution)/shard_map/ppermute | solution.py:47
  91.3 6.8 %collective-permute-done.33 = bf16[128,768]{1,0:T(8,128)(2,1)S(1)} collective-permute-done((bf16[128,768]{1,0:T(8,128)(2,1)S(1)}, bf16[128,768]{1,0:T(8,128)(2,1)S(1)}, u32[]{:S(2)}, u32[]{:S(2)}) %collective-permute-start.33) | collective-permute-done | bytes 196640 | tf_op jit(solution)/shard_map/ppermute | solution.py:35
  98.2 4.6 %collective-permute-start.34 = (bf16[128,768]{1,0:T(8,128)(2,1)S(1)}, bf16[128,768]{1,0:T(8,128)(2,1)S(1)}, u32[]{:S(2)}, u32[]{:S(2)}) collective-permute-start(bf16[128,768]{1,0:T(8,128)(2,1)S(1)} %add_convert_fusion.1), channel_id=1, source_target_pairs={{0,24},{4,28},{8,0},{12,4},{16,8},{20,12},{24,16},{28,20},{1,25},{... | collective-permute-start | bytes 589832 | tf_op jit(solution)/shard_map/ppermute | solution.py:47
  102.9 1.9 %collective-permute-start.32 = (bf16[128,768]{1,0:T(8,128)(2,1)S(1)}, bf16[128,768]{1,0:T(8,128)(2,1)S(1)}, u32[]{:S(2)}, u32[]{:S(2)}) collective-permute-start(bf16[128,768]{1,0:T(8,128)(2,1)S(1)} %add_convert_fusion.2), channel_id=1, source_target_pairs={{0,16},{4,20},{8,24},{12,28},{16,0},{20,4},{24,8},{28,12},{1,17},{... | collective-permute-start | bytes 589832 | tf_op jit(solution)/shard_map/ppermute | solution.py:47
  104.8 1.0 width_grad.2.mine_ref
  105.8 1.0 copy-done.1
  106.8 1.1 collective-permute-done.34
  107.9 5.7 %collective-permute-done.32 = bf16[128,768]{1,0:T(8,128)(2,1)S(1)} collective-permute-done((bf16[128,768]{1,0:T(8,128)(2,1)S(1)}, bf16[128,768]{1,0:T(8,128)(2,1)S(1)}, u32[]{:S(2)}, u32[]{:S(2)}) %collective-permute-start.32) | collective-permute-done | bytes 196640 | tf_op jit(solution)/shard_map/ppermute | solution.py:47
  113.6 0.9 add_add_fusion
  114.4 1.0 copy-done.4
  115.4 2.8 %merge_halves.1 = bf16[256,4096]{1,0:T(8,128)(2,1)} custom-call(bf16[256,2048]{1,0:T(8,128)(2,1)} %copy-done.1, bf16[256,2048]{1,0:T(8,128)(2,1)} %copy-done.4), custom_call_target="tpu_custom_call" | custom-call | tf_op jit(solution)/shard_map/merge_halves/pallas_call | solution.py:116
  (67 shorter events, 5.8 us)
Async XLA Ops:
  0.6 23.2 %copy-start.3 = (s32[1,8]{1,0:T(1,128)S(1)}, s32[1,8]{1,0:T(1,128)}, u32[]{:S(2)}) copy-start(s32[1,8]{1,0:T(1,128)} %param.8) | copy-start | bytes 100
  0.6 37.5 %copy-start.6 = (s32[1,8]{1,0:T(1,128)S(1)}, s32[1,8]{1,0:T(1,128)}, u32[]{:S(2)}) copy-start(s32[1,8]{1,0:T(1,128)} %param.9) | copy-start | bytes 100
  1.8 11.3 %collective-permute-start = (bf16[128,768]{1,0:T(8,128)(2,1)S(1)}, bf16[128,768]{1,0:T(8,128)(2,1)S(1)}, u32[]{:S(2)}, u32[]{:S(2)}) collective-permute-start(bf16[128,768]{1,0:T(8,128)(2,1)S(1)} %get-tuple-element.44.refs_0_), channel_id=1, source_target_pairs={{0,8},{4,12},{8,16},{12,20},{16,24},{20,28},{24,0},{28,4},{1,9},{5... | collective-permute-start | bytes 589832 | tf_op jit(solution)/shard_map/ppermute | solution.py:47
  4.8 15.5 %collective-permute-start.2 = (bf16[128,768]{1,0:T(8,128)(2,1)S(1)}, bf16[128,768]{1,0:T(8,128)(2,1)S(1)}, u32[]{:S(2)}, u32[]{:S(2)}) collective-permute-start(bf16[128,768]{1,0:T(8,128)(2,1)S(1)} %get-tuple-element.44.refs_0_), channel_id=1, source_target_pairs={{0,16},{4,20},{8,24},{12,28},{16,0},{20,4},{24,8},{28,12},{1,17},{... | collective-permute-start | bytes 589832 | tf_op jit(solution)/shard_map/ppermute | solution.py:47
  7.4 14.4 %collective-permute-start.4 = (bf16[128,768]{1,0:T(8,128)(2,1)S(1)}, bf16[128,768]{1,0:T(8,128)(2,1)S(1)}, u32[]{:S(2)}, u32[]{:S(2)}) collective-permute-start(bf16[128,768]{1,0:T(8,128)(2,1)S(1)} %get-tuple-element.44.refs_0_), channel_id=1, source_target_pairs={{0,24},{4,28},{8,0},{12,4},{16,8},{20,12},{24,16},{28,20},{1,25},{... | collective-permute-start | bytes 589832 | tf_op jit(solution)/shard_map/ppermute | solution.py:47
  11.6 27.3 %copy-start.2 = (bf16[256,1024]{1,0:T(8,128)(2,1)S(1)}, bf16[256,1024]{1,0:T(8,128)(2,1)}, u32[]{:S(2)}) copy-start(bf16[256,1024]{1,0:T(8,128)(2,1)} %get-tuple-element.23.tokens_ref) | copy-start | bytes 1572868
  11.6 26.1 %collective-permute-start.15 = (bf16[256,1024]{1,0:T(8,128)(2,1)}, bf16[256,1024]{1,0:T(8,128)(2,1)S(1)}, u32[]{:S(2)}, u32[]{:S(2)}) collective-permute-start(bf16[256,1024]{1,0:T(8,128)(2,1)} %get-tuple-element.27), channel_id=1, source_target_pairs={{0,1},{1,0},{2,3},{3,2},{4,5},{5,4},{6,7},{7,6},{8,9},{9,8},{10,11... | collective-permute-start | bytes 1572872 | tf_op jit(solution)/shard_map/ppermute | solution.py:28
  13.1 9.2 %collective-permute-start.6 = (bf16[128,768]{1,0:T(8,128)(2,1)S(1)}, bf16[128,768]{1,0:T(8,128)(2,1)S(1)}, u32[]{:S(2)}, u32[]{:S(2)}) collective-permute-start(bf16[128,768]{1,0:T(8,128)(2,1)S(1)} %get-tuple-element.44.refs_0_), channel_id=1, source_target_pairs={{0,4},{4,0},{8,12},{12,8},{16,20},{20,16},{24,28},{28,24},{1,5},{5... | collective-permute-start | bytes 589832 | tf_op jit(solution)/shard_map/ppermute | solution.py:40
  13.1 10.9 %collective-permute-start.7 = (bf16[128,768]{1,0:T(8,128)(2,1)S(1)}, bf16[128,768]{1,0:T(8,128)(2,1)S(1)}, u32[]{:S(2)}, u32[]{:S(2)}) collective-permute-start(bf16[128,768]{1,0:T(8,128)(2,1)S(1)} %get-tuple-element.43.refs_1_), channel_id=1, source_target_pairs={{0,4},{4,0},{8,12},{12,8},{16,20},{20,16},{24,28},{28,24},{1,5},{5... | collective-permute-start | bytes 589832 | tf_op jit(solution)/shard_map/ppermute | solution.py:40
  20.3 7.8 %collective-permute-start.1 = (bf16[128,768]{1,0:T(8,128)(2,1)S(1)}, bf16[128,768]{1,0:T(8,128)(2,1)S(1)}, u32[]{:S(2)}, u32[]{:S(2)}) collective-permute-start(bf16[128,768]{1,0:T(8,128)(2,1)S(1)} %collective-permute-done.refs_2_), channel_id=1, source_target_pairs={{0,2},{1,3},{2,0},{3,1},{4,6},{5,7},{6,4},{7,5},{8,10},{9,11},{10,... | collective-permute-start | bytes 589832 | tf_op jit(solution)/shard_map/ppermute | solution.py:35
  21.8 9.4 %collective-permute-start.3 = (bf16[128,768]{1,0:T(8,128)(2,1)S(1)}, bf16[128,768]{1,0:T(8,128)(2,1)S(1)}, u32[]{:S(2)}, u32[]{:S(2)}) collective-permute-start(bf16[128,768]{1,0:T(8,128)(2,1)S(1)} %collective-permute-done.2.refs_4_), channel_id=1, source_target_pairs={{0,2},{1,3},{2,0},{3,1},{4,6},{5,7},{6,4},{7,5},{8,10},{9,11},{10,... | collective-permute-start | bytes 589832 | tf_op jit(solution)/shard_map/ppermute | solution.py:35
  22.4 16.7 %collective-permute-start.14 = (bf16[256,1024]{1,0:T(8,128)(2,1)}, bf16[256,1024]{1,0:T(8,128)(2,1)S(1)}, u32[]{:S(2)}, u32[]{:S(2)}) collective-permute-start(bf16[256,1024]{1,0:T(8,128)(2,1)} %get-tuple-element.26), channel_id=1, source_target_pairs={{0,1},{1,0},{2,3},{3,2},{4,5},{5,4},{6,7},{7,6},{8,9},{9,8},{10,11... | collective-permute-start | bytes 1572872 | tf_op jit(solution)/shard_map/ppermute | solution.py:28
  24.0 13.1 %collective-permute-start.8 = (bf16[128,768]{1,0:T(8,128)(2,1)S(1)}, bf16[128,768]{1,0:T(8,128)(2,1)S(1)}, u32[]{:S(2)}, u32[]{:S(2)}) collective-permute-start(bf16[128,768]{1,0:T(8,128)(2,1)S(1)} %collective-permute-done.refs_2_), channel_id=1, source_target_pairs={{0,4},{4,0},{8,12},{12,8},{16,20},{20,16},{24,28},{28,24},{1,5},{5... | collective-permute-start | bytes 589832 | tf_op jit(solution)/shard_map/ppermute | solution.py:40
  28.1 9.6 %collective-permute-start.10 = (bf16[128,768]{1,0:T(8,128)(2,1)S(1)}, bf16[128,768]{1,0:T(8,128)(2,1)S(1)}, u32[]{:S(2)}, u32[]{:S(2)}) collective-permute-start(bf16[128,768]{1,0:T(8,128)(2,1)S(1)} %collective-permute-done.2.refs_4_), channel_id=1, source_target_pairs={{0,4},{4,0},{8,12},{12,8},{16,20},{20,16},{24,28},{28,24},{1,5},{5... | collective-permute-start | bytes 589832 | tf_op jit(solution)/shard_map/ppermute | solution.py:40
  31.3 5.9 %collective-permute-start.5 = (bf16[128,768]{1,0:T(8,128)(2,1)S(1)}, bf16[128,768]{1,0:T(8,128)(2,1)S(1)}, u32[]{:S(2)}, u32[]{:S(2)}) collective-permute-start(bf16[128,768]{1,0:T(8,128)(2,1)S(1)} %collective-permute-done.4.refs_6_), channel_id=1, source_target_pairs={{0,2},{1,3},{2,0},{3,1},{4,6},{5,7},{6,4},{7,5},{8,10},{9,11},{10,... | collective-permute-start | bytes 589832 | tf_op jit(solution)/shard_map/ppermute | solution.py:35
  37.1 1.7 %collective-permute-start.12 = (bf16[128,768]{1,0:T(8,128)(2,1)S(1)}, bf16[128,768]{1,0:T(8,128)(2,1)S(1)}, u32[]{:S(2)}, u32[]{:S(2)}) collective-permute-start(bf16[128,768]{1,0:T(8,128)(2,1)S(1)} %collective-permute-done.4.refs_6_), channel_id=1, source_target_pairs={{0,4},{4,0},{8,12},{12,8},{16,20},{20,16},{24,28},{28,24},{1,5},{5... | collective-permute-start | bytes 589832 | tf_op jit(solution)/shard_map/ppermute | solution.py:40
  37.1 1.9 %collective-permute-start.9 = (bf16[128,768]{1,0:T(8,128)(2,1)S(1)}, bf16[128,768]{1,0:T(8,128)(2,1)S(1)}, u32[]{:S(2)}, u32[]{:S(2)}) collective-permute-start(bf16[128,768]{1,0:T(8,128)(2,1)S(1)} %collective-permute-done.1.refs_3_), channel_id=1, source_target_pairs={{0,4},{4,0},{8,12},{12,8},{16,20},{20,16},{24,28},{28,24},{1,5},{5... | collective-permute-start | bytes 589832 | tf_op jit(solution)/shard_map/ppermute | solution.py:40
  37.6 1.5 %collective-permute-start.11 = (bf16[128,768]{1,0:T(8,128)(2,1)S(1)}, bf16[128,768]{1,0:T(8,128)(2,1)S(1)}, u32[]{:S(2)}, u32[]{:S(2)}) collective-permute-start(bf16[128,768]{1,0:T(8,128)(2,1)S(1)} %collective-permute-done.3.refs_5_), channel_id=1, source_target_pairs={{0,4},{4,0},{8,12},{12,8},{16,20},{20,16},{24,28},{28,24},{1,5},{5... | collective-permute-start | bytes 589832 | tf_op jit(solution)/shard_map/ppermute | solution.py:40
  37.7 1.7 %collective-permute-start.13 = (bf16[128,768]{1,0:T(8,128)(2,1)S(1)}, bf16[128,768]{1,0:T(8,128)(2,1)S(1)}, u32[]{:S(2)}, u32[]{:S(2)}) collective-permute-start(bf16[128,768]{1,0:T(8,128)(2,1)S(1)} %collective-permute-done.5.refs_7_), channel_id=1, source_target_pairs={{0,4},{4,0},{8,12},{12,8},{16,20},{20,16},{24,28},{28,24},{1,5},{5... | collective-permute-start | bytes 589832 | tf_op jit(solution)/shard_map/ppermute | solution.py:40
  38.8 2.7 %copy-start = (bf16[256,1024]{1,0:T(8,128)(2,1)S(1)}, bf16[256,1024]{1,0:T(8,128)(2,1)}, u32[]{:S(2)}) copy-start(bf16[256,1024]{1,0:T(8,128)(2,1)} %get-tuple-element.24.tokens_ref.refs_0_) | copy-start | bytes 1572868
  38.9 38.7 %collective-permute-start.25 = (bf16[256,1024]{1,0:T(8,128)(2,1)S(1)}, bf16[256,1024]{1,0:T(8,128)(2,1)S(1)}, u32[]{:S(2)}, u32[]{:S(2)}) collective-permute-start(bf16[256,1024]{1,0:T(8,128)(2,1)S(1)} %copy-done.2), channel_id=1, source_target_pairs={{0,4},{4,0},{8,12},{12,8},{16,20},{20,16},{24,28},{28,24},{1,5},{5... | collective-permute-start | bytes 1572872 | tf_op jit(solution)/shard_map/ppermute | solution.py:40
  40.0 6.4 %collective-permute-start.17 = (bf16[256,256]{1,0:T(8,128)(2,1)S(1)}, bf16[256,256]{1,0:T(8,128)(2,1)S(1)}, u32[]{:S(2)}, u32[]{:S(2)}) collective-permute-start(bf16[256,256]{1,0:T(8,128)(2,1)S(1)} %get-tuple-element.30), channel_id=1, source_target_pairs={{0,1},{1,0},{2,3},{3,2},{4,5},{5,4},{6,7},{7,6},{8,9},{9,8},{10,11... | collective-permute-start | bytes 393224 | tf_op jit(solution)/shard_map/ppermute | solution.py:28
  42.1 11.1 %copy-start.5 = (bf16[1,256,512]{2,1,0:T(8,128)(2,1)S(1)}, bf16[1,256,512]{2,1,0:T(8,128)(2,1)}, u32[]{:S(2)}) copy-start(bf16[1,256,512]{2,1,0:T(8,128)(2,1)} %param.7) | copy-start | bytes 786436
  42.1 11.2 %collective-permute-start.16 = (bf16[256,512]{1,0:T(8,128)(2,1)S(1)}, bf16[256,512]{1,0:T(8,128)(2,1)S(1)}, u32[]{:S(2)}, u32[]{:S(2)}) collective-permute-start(bf16[256,512]{1,0:T(8,128)(2,1)S(1)} %get-tuple-element.28), channel_id=1, source_target_pairs={{0,1},{1,0},{2,3},{3,2},{4,5},{5,4},{6,7},{7,6},{8,9},{9,8},{10,11... | collective-permute-start | bytes 786440 | tf_op jit(solution)/shard_map/ppermute | solution.py:28
  46.4 7.3 %collective-permute-start.18 = (bf16[256,256]{1,0:T(8,128)(2,1)S(1)}, bf16[256,256]{1,0:T(8,128)(2,1)S(1)}, u32[]{:S(2)}, u32[]{:S(2)}) collective-permute-start(bf16[256,256]{1,0:T(8,128)(2,1)S(1)} %add_convert_fusion.4.refs_2_), channel_id=1, source_target_pairs={{0,2},{1,3},{4,6},{5,7},{8,10},{9,11},{12,14},{13,15},{16,18},{17,... | collective-permute-start | bytes 393224 | tf_op jit(solution)/shard_map/ppermute | solution.py:53
  49.8 5.9 %collective-permute-start.19 = (bf16[256,256]{1,0:T(8,128)(2,1)S(1)}, bf16[256,256]{1,0:T(8,128)(2,1)S(1)}, u32[]{:S(2)}, u32[]{:S(2)}) collective-permute-start(bf16[256,256]{1,0:T(8,128)(2,1)S(1)} %add_convert_fusion.4.refs_2_), channel_id=1, source_target_pairs={{0,1},{1,2},{2,3},{4,5},{5,6},{6,7},{8,9},{9,10},{10,11},{12,13},{... | collective-permute-start | bytes 393224 | tf_op jit(solution)/shard_map/ppermute | solution.py:53
  62.1 6.9 %collective-permute-start.21 = (bf16[256,256]{1,0:T(8,128)(2,1)S(1)}, bf16[256,256]{1,0:T(8,128)(2,1)S(1)}, u32[]{:S(2)}, u32[]{:S(2)}) collective-permute-start(bf16[256,256]{1,0:T(8,128)(2,1)S(1)} %get-tuple-element.46), channel_id=1, source_target_pairs={{2,0},{3,1},{6,4},{7,5},{10,8},{11,9},{14,12},{15,13},{18,16},{19,... | collective-permute-start | bytes 393224 | tf_op jit(solution)/shard_map/ppermute | solution.py:53
  63.4 8.6 %collective-permute-start.20 = (bf16[256,256]{1,0:T(8,128)(2,1)S(1)}, bf16[256,256]{1,0:T(8,128)(2,1)S(1)}, u32[]{:S(2)}, u32[]{:S(2)}) collective-permute-start(bf16[256,256]{1,0:T(8,128)(2,1)S(1)} %get-tuple-element.45), channel_id=1, source_target_pairs={{1,0},{2,1},{3,2},{5,4},{6,5},{7,6},{9,8},{10,9},{11,10},{13,12},{... | collective-permute-start | bytes 393224 | tf_op jit(solution)/shard_map/ppermute | solution.py:53
  64.9 14.2 %collective-permute-start.26 = (bf16[256,1024]{1,0:T(8,128)(2,1)S(1)}, bf16[256,1024]{1,0:T(8,128)(2,1)S(1)}, u32[]{:S(2)}, u32[]{:S(2)}) collective-permute-start(bf16[256,1024]{1,0:T(8,128)(2,1)S(1)} %collective-permute-done.14.tokens_ref), channel_id=1, source_target_pairs={{0,4},{4,0},{8,12},{12,8},{16,20},{20,16},{24,28},{28,24},{1,5},{5... | collective-permute-start | bytes 1572872 | tf_op jit(solution)/shard_map/ppermute | solution.py:40
  64.9 12.7 %collective-permute-start.22 = (bf16[256,512]{1,0:T(8,128)(2,1)S(1)}, bf16[256,512]{1,0:T(8,128)(2,1)S(1)}, u32[]{:S(2)}, u32[]{:S(2)}) collective-permute-start(bf16[256,512]{1,0:T(8,128)(2,1)S(1)} %get-tuple-element.32.dquery_ref.refs_4_), channel_id=1, source_target_pairs={{0,1},{1,0},{2,3},{3,2},{4,5},{5,4},{6,7},{7,6},{8,9},{9,8},{10,11... | collective-permute-start | bytes 786440 | tf_op jit(solution)/shard_map/ppermute | solution.py:28
  68.9 10.4 %collective-permute-start.27 = (bf16[256,512]{1,0:T(8,128)(2,1)S(1)}, bf16[256,512]{1,0:T(8,128)(2,1)S(1)}, u32[]{:S(2)}, u32[]{:S(2)}) collective-permute-start(bf16[256,512]{1,0:T(8,128)(2,1)S(1)} %get-tuple-element.32.dquery_ref.refs_4_), channel_id=1, source_target_pairs={{0,4},{4,0},{8,12},{12,8},{16,20},{20,16},{24,28},{28,24},{1,5},{5... | collective-permute-start | bytes 786440 | tf_op jit(solution)/shard_map/ppermute | solution.py:40
  72.0 7.1 %collective-permute-start.23 = (bf16[256,256]{1,0:T(8,128)(2,1)S(1)}, bf16[256,256]{1,0:T(8,128)(2,1)S(1)}, u32[]{:S(2)}, u32[]{:S(2)}) collective-permute-start(bf16[256,256]{1,0:T(8,128)(2,1)S(1)} %add_convert_fusion.3.dpair_ref.refs_8_), channel_id=1, source_target_pairs={{0,1},{1,0},{2,3},{3,2},{4,5},{5,4},{6,7},{7,6},{8,9},{9,8},{10,11... | collective-permute-start | bytes 393224 | tf_op jit(solution)/shard_map/ppermute | solution.py:28
  77.6 2.8 %collective-permute-start.28 = (bf16[256,512]{1,0:T(8,128)(2,1)S(1)}, bf16[256,512]{1,0:T(8,128)(2,1)S(1)}, u32[]{:S(2)}, u32[]{:S(2)}) collective-permute-start(bf16[256,512]{1,0:T(8,128)(2,1)S(1)} %collective-permute-done.22.dquery_ref.refs_5_), channel_id=1, source_target_pairs={{0,4},{4,0},{8,12},{12,8},{16,20},{20,16},{24,28},{28,24},{1,5},{5... | collective-permute-start | bytes 786440 | tf_op jit(solution)/shard_map/ppermute | solution.py:40
  77.6 1.7 %collective-permute-start.29 = (bf16[256,256]{1,0:T(8,128)(2,1)S(1)}, bf16[256,256]{1,0:T(8,128)(2,1)S(1)}, u32[]{:S(2)}, u32[]{:S(2)}) collective-permute-start(bf16[256,256]{1,0:T(8,128)(2,1)S(1)} %add_convert_fusion.3.dpair_ref.refs_8_), channel_id=1, source_target_pairs={{0,4},{4,0},{8,12},{12,8},{16,20},{20,16},{24,28},{28,24},{1,5},{5... | collective-permute-start | bytes 393224 | tf_op jit(solution)/shard_map/ppermute | solution.py:40
  79.1 1.3 %collective-permute-start.30 = (bf16[256,256]{1,0:T(8,128)(2,1)S(1)}, bf16[256,256]{1,0:T(8,128)(2,1)S(1)}, u32[]{:S(2)}, u32[]{:S(2)}) collective-permute-start(bf16[256,256]{1,0:T(8,128)(2,1)S(1)} %collective-permute-done.23.dpair_ref.refs_9_), channel_id=1, source_target_pairs={{0,4},{4,0},{8,12},{12,8},{16,20},{20,16},{24,28},{28,24},{1,5},{5... | collective-permute-start | bytes 393224 | tf_op jit(solution)/shard_map/ppermute | solution.py:40
  81.5 8.0 %collective-permute-start.35 = (bf16[128,768]{1,0:T(8,128)(2,1)S(1)}, bf16[128,768]{1,0:T(8,128)(2,1)S(1)}, u32[]{:S(2)}, u32[]{:S(2)}) collective-permute-start(bf16[128,768]{1,0:T(8,128)(2,1)S(1)} %get-tuple-element.40), channel_id=1, source_target_pairs={{0,2},{1,3},{2,0},{3,1},{4,6},{5,7},{6,4},{7,5},{8,10},{9,11},{10,... | collective-permute-start | bytes 589832 | tf_op jit(solution)/shard_map/ppermute | solution.py:35
  84.8 29.6 %collective-permute-start.24 = (bf16[256,2048]{1,0:T(8,128)(2,1)S(1)}, bf16[256,2048]{1,0:T(8,128)(2,1)S(1)}, u32[]{:S(2)}, u32[]{:S(2)}) collective-permute-start(bf16[256,2048]{1,0:T(8,128)(2,1)S(1)} %width_grad.3), channel_id=1, source_target_pairs={{0,1},{1,0},{2,3},{3,2},{4,5},{5,4},{6,7},{7,6},{8,9},{9,8},{10,11... | collective-permute-start | bytes 3145736 | tf_op jit(solution)/shard_map/ppermute | solution.py:28
  86.1 20.7 %collective-permute-start.37 = (bf16[128,768]{1,0:T(8,128)(2,1)S(1)}, bf16[128,768]{1,0:T(8,128)(2,1)S(1)}, u32[]{:S(2)}, u32[]{:S(2)}) collective-permute-start(bf16[128,768]{1,0:T(8,128)(2,1)S(1)} %get-tuple-element.42), channel_id=1, source_target_pairs={{0,2},{1,3},{2,0},{3,1},{4,6},{5,7},{6,4},{7,5},{8,10},{9,11},{10,... | collective-permute-start | bytes 589832 | tf_op jit(solution)/shard_map/ppermute | solution.py:35
  87.2 11.0 %collective-permute-start.33 = (bf16[128,768]{1,0:T(8,128)(2,1)S(1)}, bf16[128,768]{1,0:T(8,128)(2,1)S(1)}, u32[]{:S(2)}, u32[]{:S(2)}) collective-permute-start(bf16[128,768]{1,0:T(8,128)(2,1)S(1)} %get-tuple-element.38), channel_id=1, source_target_pairs={{0,2},{1,3},{2,0},{3,1},{4,6},{5,7},{6,4},{7,5},{8,10},{9,11},{10,... | collective-permute-start | bytes 589832 | tf_op jit(solution)/shard_map/ppermute | solution.py:35
  89.2 13.6 %collective-permute-start.31 = (bf16[128,768]{1,0:T(8,128)(2,1)S(1)}, bf16[128,768]{1,0:T(8,128)(2,1)S(1)}, u32[]{:S(2)}, u32[]{:S(2)}) collective-permute-start(bf16[128,768]{1,0:T(8,128)(2,1)S(1)} %get-tuple-element.36), channel_id=1, source_target_pairs={{0,2},{1,3},{2,0},{3,1},{4,6},{5,7},{6,4},{7,5},{8,10},{9,11},{10,... | collective-permute-start | bytes 589832 | tf_op jit(solution)/shard_map/ppermute | solution.py:35
  89.5 17.3 %collective-permute-start.36 = (bf16[128,768]{1,0:T(8,128)(2,1)S(1)}, bf16[128,768]{1,0:T(8,128)(2,1)S(1)}, u32[]{:S(2)}, u32[]{:S(2)}) collective-permute-start(bf16[128,768]{1,0:T(8,128)(2,1)S(1)} %add_convert_fusion), channel_id=1, source_target_pairs={{0,8},{4,12},{8,16},{12,20},{16,24},{20,28},{24,0},{28,4},{1,9},{5... | collective-permute-start | bytes 589832 | tf_op jit(solution)/shard_map/ppermute | solution.py:47
  98.2 9.7 %collective-permute-start.34 = (bf16[128,768]{1,0:T(8,128)(2,1)S(1)}, bf16[128,768]{1,0:T(8,128)(2,1)S(1)}, u32[]{:S(2)}, u32[]{:S(2)}) collective-permute-start(bf16[128,768]{1,0:T(8,128)(2,1)S(1)} %add_convert_fusion.1), channel_id=1, source_target_pairs={{0,24},{4,28},{8,0},{12,4},{16,8},{20,12},{24,16},{28,20},{1,25},{... | collective-permute-start | bytes 589832 | tf_op jit(solution)/shard_map/ppermute | solution.py:47
  102.9 10.7 %collective-permute-start.32 = (bf16[128,768]{1,0:T(8,128)(2,1)S(1)}, bf16[128,768]{1,0:T(8,128)(2,1)S(1)}, u32[]{:S(2)}, u32[]{:S(2)}) collective-permute-start(bf16[128,768]{1,0:T(8,128)(2,1)S(1)} %add_convert_fusion.2), channel_id=1, source_target_pairs={{0,16},{4,20},{8,24},{12,28},{16,0},{20,4},{24,8},{28,12},{1,17},{... | collective-permute-start | bytes 589832 | tf_op jit(solution)/shard_map/ppermute | solution.py:47
  105.8 1.0 copy-start.1
  114.4 1.0 copy-start.4

commit v5 on v4

--- a/solution.py
+++ b/solution.py
@@ -70,60 +70,66 @@
     return pl.ds(pl.multiple_of(index * width, width), width)
 
 
-def split_kernel(chips, rest, width, in_ref, *out_refs):
+def split_kernel(chips, rest, width, in_ref, held_ref, *out_refs):
     for flip in range(PAIR):
-        order = block_order(chips, rest, flip)
-        count = len(order) // CORES
-        for i, block in enumerate(order):
-            at = slice(i % count * width, (i % count + 1) * width)
-            out_refs[flip * CORES + i // count][:, at] = in_ref[:, lanes(block, width)]
-
-
-def split_tokens(tokens, chips, rest, width):
+        for i, block in enumerate(block_order(chips, rest, flip)):
+            out_refs[flip][:, i * width : (i + 1) * width] = in_ref[:, lanes(block, width)]
+    out_refs[PAIR][...] = held_ref[...]
+
+
+def split_tokens(tokens, held, chips, rest, width):
     rows, total = tokens.shape
-    parts = PAIR * CORES
     if width % 128:
         blocks = tokens.reshape(rows, total // width, width)
         order = jnp.stack(block_order(chips, rest, 0) + block_order(chips, rest, 1))
-        return jnp.split(jnp.take(blocks, order, axis=1).reshape(rows, total), parts, axis=1)
+        return *jnp.split(jnp.take(blocks, order, axis=1).reshape(rows, total), PAIR, axis=1), held
     tile = min(rows, 128)
+    half = pl.BlockSpec((tile, total // PAIR), lambda i: (i, 0))
+    whole = pl.BlockSpec(held.shape, lambda i: (0, 0))
     return pl.pallas_call(
         functools.partial(split_kernel, chips, rest, width),
         grid=(rows // tile,),
-        in_specs=[pl.BlockSpec((tile, total), lambda i: (i, 0))],
-        out_specs=[pl.BlockSpec((tile, total // parts), lambda i: (i, 0))] * parts,
-        out_shape=[jax.ShapeDtypeStruct((rows, total // parts), tokens.dtype)] * parts,
+        in_specs=[pl.BlockSpec((tile, total), lambda i: (i, 0)), whole],
+        out_specs=[half] * PAIR + [whole],
+        out_shape=[jax.ShapeDtypeStruct((rows, total // PAIR), tokens.dtype)] * PAIR
+        + [jax.ShapeDtypeStruct(held.shape, held.dtype)],
         name="split_tokens",
-    )(tokens)
-
-
-def merge_kernel(chips, rest, width, mine_ref, other_ref, out_ref):
-    mine, other = block_order(chips, rest, 0), block_order(chips, rest, 1)
-    for i in range(len(mine)):
-        source = slice(i * width, (i + 1) * width)
-        out_ref[:, lanes(mine[i], width)] = mine_ref[:, source]
-        out_ref[:, lanes(other[i], width)] = other_ref[:, source]
+    )(tokens, held)
+
+
+def merge_kernel(chips, rest, width, mine_ref, other_ref, out_ref, sems):
+    copies = []
+    for flip, ref in enumerate((mine_ref, other_ref)):
+        for i, block in enumerate(block_order(chips, rest, flip)):
+            source = ref.at[:, pl.ds(i * width, width)]
+            target = out_ref.at[:, lanes(block, width)]
+            copies.append(pltpu.make_async_copy(source, target, sems.at[len(copies)]))
+    for copy in copies:
+        copy.start()
+    for copy in copies:
+        copy.wait()
 
 
 def merge_halves(mine, other, chips, rest, width):
     rows, half = mine.shape
+    count = PAIR * half // width
     if width % 128:
         order = jnp.stack(block_order(chips, rest, 0) + block_order(chips, rest, 1))
-        where = jnp.zeros_like(order).at[order].set(lax.iota(order.dtype, order.shape[0]))
-        blocks = jnp.concatenate([mine, other], axis=1).reshape(rows, order.shape[0], width)
-        return jnp.take(blocks, where, axis=1).reshape(rows, 2 * half)
-    tile = min(rows, 128)
+        where = jnp.zeros_like(order).at[order].set(lax.iota(order.dtype, count))
+        blocks = jnp.concatenate([mine, other], axis=1).reshape(rows, count, width)
+        return jnp.take(blocks, where, axis=1).reshape(rows, PAIR * half)
     return pl.pallas_call(
         functools.partial(merge_kernel, chips, rest, width),
-        grid=(rows // tile,),
-        in_specs=[pl.BlockSpec((tile, half), lambda i: (i, 0))] * 2,
-        out_specs=pl.BlockSpec((tile, 2 * half), lambda i: (i, 0)),
-        out_shape=jax.ShapeDtypeStruct((rows, 2 * half), mine.dtype),
+        in_specs=[VMEM] * 2,
+        out_specs=pl.BlockSpec(memory_space=pl.ANY),
+        out_shape=jax.ShapeDtypeStruct((rows, PAIR * half), mine.dtype),
+        scratch_shapes=[pltpu.SemaphoreType.DMA((count,))],
+        compiler_params=pltpu.CompilerParams(vmem_limit_bytes=48 * 2**20),
         name="merge_halves",
     )(mine, other)
 
 
-def project_kernel(span, per, qwidth, has_sum, tokens_ref, *refs):
+def project_kernel(first, span, per, qwidth, has_sum, tokens_ref, *refs):
     if has_sum:
         sum_ref, refs = refs[0], refs[1:]
         total = sum_ref[...]
@@ -132,7 +138,7 @@
     pieces = refs[:-2] if qwidth else refs[:-1]
     for g in range(len(pieces) // per):
         rows = jnp.concatenate([r[...] for r in pieces[g * per : (g + 1) * per]], axis=0)
-        term = dot(tokens_ref[:, g * span : (g + 1) * span], rows)
+        term = dot(tokens_ref[:, (first + g) * span : (first + g + 1) * span], rows)
         total = term if total is None else total + term
     if qwidth:
         query_ref, pair_ref = refs[-2:]
@@ -142,7 +148,7 @@
         refs[-1][...] = total
 
 
-def project(tokens, groups, qwidth=0, kind=F32, so_far=None):
+def project(tokens, groups, first=0, qwidth=0, kind=F32, so_far=None):
     rows = tokens.shape[0]
     cols = groups[0][0].shape[1]
     pieces = [piece for group in groups for piece in group]
@@ -150,7 +156,7 @@
     widths = [qwidth, cols - qwidth] if qwidth else [cols]
     sums = [] if so_far is None else [so_far]
     outs = pl.pallas_call(
-        functools.partial(project_kernel, span, len(groups[0]), qwidth, len(sums)),
+        functools.partial(project_kernel, first, span, len(groups[0]), qwidth, len(sums)),
         in_specs=[VMEM] * (1 + len(sums) + len(pieces)),
         out_specs=[VMEM] * len(widths),
         out_shape=[jax.ShapeDtypeStruct((rows, w), kind) for w in widths],
@@ -184,7 +190,7 @@
 
 def weight_kernel(steps, rest, width, count, *refs):
     tokens, dquery, dpair = refs[:count], refs[count : 2 * count], refs[2 * count : 3 * count]
-    outs = refs[3 * count :]
+    outs = refs[3 * count + 1 :]
     right = jnp.concatenate(
         [jnp.concatenate([q[...], p[...]], axis=1) for q, p in zip(dquery, dpair)], axis=0
     )
@@ -197,17 +203,17 @@
             out[...] = total[j * width : (j + 1) * width].astype(out.dtype)
 
 
-def weight_terms(steps, rest, width, tokens, dquery, dpair):
+def weight_terms(steps, rest, width, tokens, dquery, dpair, after):
     cols = dquery[0].shape[1] + dpair[0].shape[1]
     count = len(tokens)
     return pl.pallas_call(
         functools.partial(weight_kernel, steps, rest, width, count),
-        in_specs=[VMEM] * (3 * count),
+        in_specs=[VMEM] * (3 * count) + [pl.BlockSpec(memory_space=pl.ANY)],
         out_specs=[VMEM] * (len(steps) * rest),
         out_shape=[jax.ShapeDtypeStruct((width, cols), BF16 if j else F32) for _ in steps for j in range(rest)],
         compiler_params=pltpu.CompilerParams(vmem_limit_bytes=48 * 2**20),
         name="weight_terms",
-    )(*tokens, *dquery, *dpair)
+    )(*tokens, *dquery, *dpair, after)
 
 
 def attend_kernel(
@@ -297,22 +303,26 @@
     width = shard_rows // seq_count
     back = -(-(local * seq_count // 2 - 1) // local)
 
-    mine_own, mine_across, *sent = split_tokens(tokens, chips, rest, width)
-    other_own, other_across = [swap_x(part) for part in sent]
-
     blocks = weights.reshape(seq_count, width, cols)
     places = [PAIR * ((place // PAIR - j + rest) % rest) + place % PAIR for j in range(rest)]
     groups_own = [[lax.dynamic_index_in_dim(blocks, p, 0, keepdims=False) for p in places]]
+    own = groups_own[0][0]
+    farthest = chips // 2
+    arrived = {farthest: shift_chip(own, farthest)}
+
+    tokens_mine, tokens_sent, own = split_tokens(tokens, own, chips, rest, width)
+    tokens_other = swap_x(tokens_sent)
+
     for k in range(1, chips):
-        first = shift_chip(groups_own[0][0], k)
+        first = arrived[k] if k in arrived else shift_chip(own, k)
         groups_own.append([first] + [shift_rest(first, j) for j in range(1, rest)])
     groups_across = [[swap_core(piece) for piece in group] for group in groups_own]
 
-    so_far = project(other_own, groups_own)
-    query_sent, pair_sent = project(other_across, groups_across, qwidth, BF16, so_far)
+    so_far = project(tokens_other, groups_own)
+    query_sent, pair_sent = project(tokens_other, groups_across, chips, qwidth, BF16, so_far)
     pair_from, query_from = swap_x(pair_sent), swap_x(query_sent)
-    so_far = project(mine_own, groups_own)
-    query, pair = project(mine_across, groups_across, qwidth, F32, so_far)
+    so_far = project(tokens_mine, groups_own)
+    query, pair = project(tokens_mine, groups_across, chips, qwidth, F32, so_far)
     pair = (pair + pair_from.astype(F32)).astype(BF16)
 
     doc_row, flag_row = doc_lengths[0], kept_flags[0]
@@ -330,12 +340,18 @@
     dpair = dpair.astype(BF16)
     dpair_other = swap_x(dpair)
 
-    left = [mine_own, other_own, swap_core(mine_across), swap_core(other_across)]
+    groups = groups_own + groups_across
+    grad_sent = width_grad(dquery_other, dpair_other, groups)
+    grad_from = swap_x(grad_sent)
+
+    half = chips * rest * width
+    left = [tokens_mine, tokens_other, swap_core(tokens_mine[:, half:]), swap_core(tokens_other[:, half:])]
     right = [[mine, other, swap_core(mine), swap_core(other)] for mine, other in ((dquery, dquery_other), (dpair, dpair_other))]
     order = sorted(range(chips), key=lambda k: (k == 0, -min(k, chips - k), k))
-    weights_grad = None
+    weights_grad, after = None, grad_sent
     for steps in (order[: chips // 2], order[chips // 2 :]):
-        terms = weight_terms(steps, rest, width, left, *right)
+        terms = weight_terms(steps, rest, width, left, *right, after)
+        after = terms[-1]
         for i, k in enumerate(steps):
             part, *sent = terms[i * rest : (i + 1) * rest]
             for j, piece in enumerate(sent, 1):
@@ -344,8 +360,6 @@
                 part = shift_chip(part.astype(BF16), -k).astype(F32)
             weights_grad = part if weights_grad is None else weights_grad + part
 
-    groups = groups_own + groups_across
-    grad_from = swap_x(width_grad(dquery_other, dpair_other, groups))
     inputs_grad = merge_halves(width_grad(dquery, dpair, groups), grad_from, chips, rest, width)
     return (attention[None], inputs_grad[None], weights_grad)
 

time: 119 us -> 122 us (1.025)
  waiting for transfers between devices: 47.2 us -> 53.6 us
  starting transfers between devices: 47.3 us -> 44.8 us
    ppermute x6, waiting for transfers between devices: 13.5 us -> 18.3 us  [shift_chip(): return lax.ppermute(array, 'dp', pairs)]
    ppermute x7 -> x6, starting transfers between devices: 12.1 us -> 9.84 us  [swap_x(): return lax.ppermute(array, 'seq', [(i, i ^ 1) for i in range(count)])]
    ppermute x14, waiting for transfers between devices: 1.76 us -> 0.24 us  [swap_core(): return lax.ppermute(array, 'dp', [(i, i ^ 1) for i in range(count)])]
    ppermute x4, starting transfers between devices: 9.57 us -> 8.23 us  [shift_seq(): return lax.ppermute(array, 'seq', pairs)]
    ppermute x7, waiting for transfers between devices: 18.6 us -> 19.9 us  [shift_rest(): return lax.ppermute(array, 'seq', pairs)]
    ppermute x6, starting transfers between devices: 15.3 us -> 16.6 us  [shift_chip(): return lax.ppermute(array, 'dp', pairs)]
    pallas_call x5, Pallas kernels: 5.14 us -> 3.87 us  [the longest x4 2.3 us: project(): pl.pallas_call(functools.partial(project_kernel, first, span, len(groups[...]
    ppermute x7 -> x6, waiting for transfers between devices: 7.06 us -> 8.22 us  [swap_x(): return lax.ppermute(array, 'seq', [(i, i ^ 1) for i in range(count)])]
  transfers between devices with their start and end apart: 38 -> 37, of which waited for: 19 -> 16; matrix products, arithmetic and copies ran while one was open for 1% -> 2% of each run, Pallas kernels for 12% -> 9%
where the time goes in v5:
time: 122 us
  waiting for transfers between devices  53.6 us (44%)
  starting transfers between devices  44.8 us (37%)
  Pallas kernels  17.3 us (14%)
  local copies, waits for them, and re-layouts  3.86 us (3%)
  other arithmetic  1.46 us (1%)
    ppermute x7, waiting for transfers between devices, shift_rest(): return lax.ppermute(array, 'seq', pairs)  19.9 us
    ppermute x6, waiting for transfers between devices, shift_chip(): return lax.ppermute(array, 'dp', pairs)  18.3 us
    ppermute x6, starting transfers between devices, shift_chip(): return lax.ppermute(array, 'dp', pairs)  16.6 us
    ppermute x6, starting transfers between devices, swap_x(): return lax.ppermute(array, 'seq', [(i, i ^ 1) for i in range(count)])  9.84 us
    ppermute x7, starting transfers between devices, shift_rest(): return lax.ppermute(array, 'seq', pairs)  8.44 us
    ppermute x4, starting transfers between devices, shift_seq(): return lax.ppermute(array, 'seq', pairs)  8.23 us
    ppermute x6, waiting for transfers between devices, swap_x(): return lax.ppermute(array, 'seq', [(i, i ^ 1) for i in range(count)])  8.22 us
    ppermute x4, waiting for transfers between devices, shift_seq(): return lax.ppermute(array, 'seq', pairs)  6.9 us
  transfers between devices with their start and end apart: 37, of which 16 were waited for; matrix products, arithmetic and copies ran while one was open for 2% of the time, Pallas kernels for 9%

profile of v5, /device:TPU:0, one launch (start us, length us, event | category | flops | bytes accessed | tf_op | source)
XLA Modules:
  0.0 122.2 jit_solution(7209034049806208834)
XLA Ops:
  0.7 1.7 %dynamic-slice_bitcast_fusion = (bf16[128,768]{1,0:T(8,128)(2,1)S(1)}, bf16[128,768]{1,0:T(8,128)(2,1)}) fusion(bf16[4,128,768]{2,1,0:T(8,128)(2,1)} %bitcast.24, s32[]{:T(128)S(6)} %select_n.42, s32[]{:T(128)S(6)} %select_n.40), kind=kLoop, calls=%fused_computation.7 | loop fusion | bytes 786440 | tf_op jit(solution)/shard_map/jit(dynamic_index_in_dim)/squeeze | solution.py:308
  2.4 3.0 %split_tokens.1 = (bf16[256,2048]{1,0:T(8,128)(2,1)}, bf16[256,2048]{1,0:T(8,128)(2,1)}, bf16[128,768]{1,0:T(8,128)(2,1)}) custom-call(bf16[256,4096]{1,0:T(8,128)(2,1)} %bitcast.22, bf16[128,768]{1,0:T(8,128)(2,1)} %get-tuple-element.42.held_ref.refs_0_), custom_call_target="tpu_custom_call" | custom-call | tf_op jit(solution)/shard_map/split_tokens/pallas_call | solution.py:89
  5.4 3.0 %collective-permute-start.14 = (bf16[256,2048]{1,0:T(8,128)(2,1)}, bf16[256,2048]{1,0:T(8,128)(2,1)S(1)}, u32[]{:S(2)}, u32[]{:S(2)}) collective-permute-start(bf16[256,2048]{1,0:T(8,128)(2,1)} %get-tuple-element.25), channel_id=1, source_target_pairs={{0,1},{1,0},{2,3},{3,2},{4,5},{5,4},{6,7},{7,6},{8,9},{9,8},{10,11... | collective-permute-start | bytes 3145736 | tf_op jit(solution)/shard_map/ppermute | solution.py:28
  8.4 1.6 %collective-permute-start = (bf16[128,768]{1,0:T(8,128)(2,1)}, bf16[128,768]{1,0:T(8,128)(2,1)S(1)}, u32[]{:S(2)}, u32[]{:S(2)}) collective-permute-start(bf16[128,768]{1,0:T(8,128)(2,1)} %get-tuple-element.23), channel_id=1, source_target_pairs={{0,8},{4,12},{8,16},{12,20},{16,24},{20,28},{24,0},{28,4},{1,9},{5... | collective-permute-start | bytes 589832 | tf_op jit(solution)/shard_map/ppermute | solution.py:47
  10.0 2.6 %collective-permute-start.2 = (bf16[128,768]{1,0:T(8,128)(2,1)S(1)}, bf16[128,768]{1,0:T(8,128)(2,1)S(1)}, u32[]{:S(2)}, u32[]{:S(2)}) collective-permute-start(bf16[128,768]{1,0:T(8,128)(2,1)S(1)} %copy-done.1), channel_id=1, source_target_pairs={{0,16},{4,20},{8,24},{12,28},{16,0},{20,4},{24,8},{28,12},{1,17},{... | collective-permute-start | bytes 589832 | tf_op jit(solution)/shard_map/ppermute | solution.py:47
  12.6 1.3 %collective-permute-start.4 = (bf16[128,768]{1,0:T(8,128)(2,1)}, bf16[128,768]{1,0:T(8,128)(2,1)S(1)}, u32[]{:S(2)}, u32[]{:S(2)}) collective-permute-start(bf16[128,768]{1,0:T(8,128)(2,1)} %get-tuple-element.23), channel_id=1, source_target_pairs={{0,24},{4,28},{8,0},{12,4},{16,8},{20,12},{24,16},{28,20},{1,25},{... | collective-permute-start | bytes 589832 | tf_op jit(solution)/shard_map/ppermute | solution.py:47
  13.9 4.4 %collective-permute-done.refs_2_ = bf16[128,768]{1,0:T(8,128)(2,1)S(1)} collective-permute-done((bf16[128,768]{1,0:T(8,128)(2,1)}, bf16[128,768]{1,0:T(8,128)(2,1)S(1)}, u32[]{:S(2)}, u32[]{:S(2)}) %collective-permute-start) | collective-permute-done | bytes 196640 | tf_op jit(solution)/shard_map/ppermute | solution.py:47
  18.5 1.1 slice.14
  19.6 5.7 %collective-permute-done.2.refs_4_ = bf16[128,768]{1,0:T(8,128)(2,1)S(1)} collective-permute-done((bf16[128,768]{1,0:T(8,128)(2,1)S(1)}, bf16[128,768]{1,0:T(8,128)(2,1)S(1)}, u32[]{:S(2)}, u32[]{:S(2)}) %collective-permute-start.2) | collective-permute-done | bytes 196640 | tf_op jit(solution)/shard_map/ppermute | solution.py:47
  25.4 1.5 %collective-permute-start.1 = (bf16[128,768]{1,0:T(8,128)(2,1)S(1)}, bf16[128,768]{1,0:T(8,128)(2,1)S(1)}, u32[]{:S(2)}, u32[]{:S(2)}) collective-permute-start(bf16[128,768]{1,0:T(8,128)(2,1)S(1)} %collective-permute-done.refs_2_), channel_id=1, source_target_pairs={{0,2},{1,3},{2,0},{3,1},{4,6},{5,7},{6,4},{7,5},{8,10},{9,11},{10,... | collective-permute-start | bytes 589832 | tf_op jit(solution)/shard_map/ppermute | solution.py:35
  27.5 1.5 %collective-permute-start.5 = (bf16[128,768]{1,0:T(8,128)(2,1)S(1)}, bf16[128,768]{1,0:T(8,128)(2,1)S(1)}, u32[]{:S(2)}, u32[]{:S(2)}) collective-permute-start(bf16[128,768]{1,0:T(8,128)(2,1)S(1)} %collective-permute-done.4.refs_6_), channel_id=1, source_target_pairs={{0,2},{1,3},{2,0},{3,1},{4,6},{5,7},{6,4},{7,5},{8,10},{9,11},{10,... | collective-permute-start | bytes 589832 | tf_op jit(solution)/shard_map/ppermute | solution.py:35
  29.0 4.1 %collective-permute-done.1.refs_3_ = bf16[128,768]{1,0:T(8,128)(2,1)S(1)} collective-permute-done((bf16[128,768]{1,0:T(8,128)(2,1)S(1)}, bf16[128,768]{1,0:T(8,128)(2,1)S(1)}, u32[]{:S(2)}, u32[]{:S(2)}) %collective-permute-start.1) | collective-permute-done | bytes 196640 | tf_op jit(solution)/shard_map/ppermute | solution.py:35
  33.1 4.2 %collective-permute-done.3.refs_5_ = bf16[128,768]{1,0:T(8,128)(2,1)S(1)} collective-permute-done((bf16[128,768]{1,0:T(8,128)(2,1)S(1)}, bf16[128,768]{1,0:T(8,128)(2,1)S(1)}, u32[]{:S(2)}, u32[]{:S(2)}) %collective-permute-start.3) | collective-permute-done | bytes 196640 | tf_op jit(solution)/shard_map/ppermute | solution.py:35
  37.3 3.2 %collective-permute-done.5.refs_7_ = bf16[128,768]{1,0:T(8,128)(2,1)S(1)} collective-permute-done((bf16[128,768]{1,0:T(8,128)(2,1)S(1)}, bf16[128,768]{1,0:T(8,128)(2,1)S(1)}, u32[]{:S(2)}, u32[]{:S(2)}) %collective-permute-start.5) | collective-permute-done | bytes 196640 | tf_op jit(solution)/shard_map/ppermute | solution.py:35
  42.5 0.6 project.7
  43.1 0.6 collective-permute-start.16
  43.7 0.6 project.4.refs_0_
  44.3 0.6 project.5
  44.9 1.6 %collective-permute-start.15 = (bf16[256,512]{1,0:T(8,128)(2,1)S(1)}, bf16[256,512]{1,0:T(8,128)(2,1)S(1)}, u32[]{:S(2)}, u32[]{:S(2)}) collective-permute-start(bf16[256,512]{1,0:T(8,128)(2,1)S(1)} %get-tuple-element.26), channel_id=1, source_target_pairs={{0,1},{1,0},{2,3},{3,2},{4,5},{5,4},{6,7},{7,6},{8,9},{9,8},{10,11... | collective-permute-start | bytes 786440 | tf_op jit(solution)/shard_map/ppermute | solution.py:28
  46.4 3.1 %collective-permute-done.16 = bf16[256,256]{1,0:T(8,128)(2,1)S(1)} collective-permute-done((bf16[256,256]{1,0:T(8,128)(2,1)S(1)}, bf16[256,256]{1,0:T(8,128)(2,1)S(1)}, u32[]{:S(2)}, u32[]{:S(2)}) %collective-permute-start.16) | collective-permute-done | bytes 131104 | tf_op jit(solution)/shard_map/ppermute | solution.py:28
  49.5 3.4 %collective-permute-start.17 = (bf16[256,256]{1,0:T(8,128)(2,1)S(1)}, bf16[256,256]{1,0:T(8,128)(2,1)S(1)}, u32[]{:S(2)}, u32[]{:S(2)}) collective-permute-start(bf16[256,256]{1,0:T(8,128)(2,1)S(1)} %add_convert_fusion.4.refs_2_), channel_id=1, source_target_pairs={{0,2},{1,3},{4,6},{5,7},{8,10},{9,11},{12,14},{13,15},{16,18},{17,... | collective-permute-start | bytes 393224 | tf_op jit(solution)/shard_map/ppermute | solution.py:53
  53.0 2.0 %collective-permute-start.18 = (bf16[256,256]{1,0:T(8,128)(2,1)S(1)}, bf16[256,256]{1,0:T(8,128)(2,1)S(1)}, u32[]{:S(2)}, u32[]{:S(2)}) collective-permute-start(bf16[256,256]{1,0:T(8,128)(2,1)S(1)} %add_convert_fusion.4.refs_2_), channel_id=1, source_target_pairs={{0,1},{1,2},{2,3},{4,5},{5,6},{6,7},{8,9},{9,10},{10,11},{12,13},{... | collective-permute-start | bytes 393224 | tf_op jit(solution)/shard_map/ppermute | solution.py:53
  55.1 3.1 %collective-permute-done.17.refs_0_ = bf16[256,256]{1,0:T(8,128)(2,1)S(1)} collective-permute-done((bf16[256,256]{1,0:T(8,128)(2,1)S(1)}, bf16[256,256]{1,0:T(8,128)(2,1)S(1)}, u32[]{:S(2)}, u32[]{:S(2)}) %collective-permute-start.17) | collective-permute-done | bytes 131104 | tf_op jit(solution)/shard_map/ppermute | solution.py:53
  58.2 6.3 %attend.1 = (bf16[256,512]{1,0:T(8,128)(2,1)}, bf16[256,512]{1,0:T(8,128)(2,1)S(1)}, f32[256,256]{1,0:T(8,128)S(1)}, bf16[512,256]{1,0:T(8,128)(2,1)S(1)}) custom-call(s32[8]{0:T(128)S(1)} %bitcast.21, f32[256,512]{1,0:T(8,128)S(1)} %get-tuple-element.24.q_ref, bf16[256,512]{1,0:T(8,128)(2,1)S(1)} %collective-permute-done.15.q_from_ref, ...), custom_call_target="tpu_custom_call" | custom-call | tf_op jit(solution)/shard_map/attend/pallas_call | solution.py:272
  64.6 1.3 %collective-permute-start.20 = (bf16[256,256]{1,0:T(8,128)(2,1)S(1)}, bf16[256,256]{1,0:T(8,128)(2,1)S(1)}, u32[]{:S(2)}, u32[]{:S(2)}) collective-permute-start(bf16[256,256]{1,0:T(8,128)(2,1)S(1)} %get-tuple-element.44), channel_id=1, source_target_pairs={{2,0},{3,1},{6,4},{7,5},{10,8},{11,9},{14,12},{15,13},{18,16},{19,... | collective-permute-start | bytes 393224 | tf_op jit(solution)/shard_map/ppermute | solution.py:53
  65.9 1.5 %collective-permute-start.19 = (bf16[256,256]{1,0:T(8,128)(2,1)S(1)}, bf16[256,256]{1,0:T(8,128)(2,1)S(1)}, u32[]{:S(2)}, u32[]{:S(2)}) collective-permute-start(bf16[256,256]{1,0:T(8,128)(2,1)S(1)} %get-tuple-element.43), channel_id=1, source_target_pairs={{1,0},{2,1},{3,2},{5,4},{6,5},{7,6},{9,8},{10,9},{11,10},{13,12},{... | collective-permute-start | bytes 393224 | tf_op jit(solution)/shard_map/ppermute | solution.py:53
  67.5 2.7 %collective-permute-start.21 = (bf16[256,512]{1,0:T(8,128)(2,1)S(1)}, bf16[256,512]{1,0:T(8,128)(2,1)S(1)}, u32[]{:S(2)}, u32[]{:S(2)}) collective-permute-start(bf16[256,512]{1,0:T(8,128)(2,1)S(1)} %get-tuple-element.30.dquery_ref.refs_4_), channel_id=1, source_target_pairs={{0,1},{1,0},{2,3},{3,2},{4,5},{5,4},{6,7},{7,6},{8,9},{9,8},{10,11... | collective-permute-start | bytes 786440 | tf_op jit(solution)/shard_map/ppermute | solution.py:28
  70.2 1.2 %collective-permute-done.20 = bf16[256,256]{1,0:T(8,128)(2,1)S(1)} collective-permute-done((bf16[256,256]{1,0:T(8,128)(2,1)S(1)}, bf16[256,256]{1,0:T(8,128)(2,1)S(1)}, u32[]{:S(2)}, u32[]{:S(2)}) %collective-permute-start.20) | collective-permute-done | bytes 131104 | tf_op jit(solution)/shard_map/ppermute | solution.py:53
  71.4 2.6 %collective-permute-done.19 = bf16[256,256]{1,0:T(8,128)(2,1)S(1)} collective-permute-done((bf16[256,256]{1,0:T(8,128)(2,1)S(1)}, bf16[256,256]{1,0:T(8,128)(2,1)S(1)}, u32[]{:S(2)}, u32[]{:S(2)}) %collective-permute-start.19) | collective-permute-done | bytes 131104 | tf_op jit(solution)/shard_map/ppermute | solution.py:53
  74.0 1.4 %collective-permute-start.22 = (bf16[256,256]{1,0:T(8,128)(2,1)S(1)}, bf16[256,256]{1,0:T(8,128)(2,1)S(1)}, u32[]{:S(2)}, u32[]{:S(2)}) collective-permute-start(bf16[256,256]{1,0:T(8,128)(2,1)S(1)} %add_convert_fusion.3.dpair_ref.refs_8_), channel_id=1, source_target_pairs={{0,1},{1,0},{2,3},{3,2},{4,5},{5,4},{6,7},{7,6},{8,9},{9,8},{10,11... | collective-permute-start | bytes 393224 | tf_op jit(solution)/shard_map/ppermute | solution.py:28
  75.5 4.1 %collective-permute-done.21.dquery_ref.refs_5_ = bf16[256,512]{1,0:T(8,128)(2,1)S(1)} collective-permute-done((bf16[256,512]{1,0:T(8,128)(2,1)S(1)}, bf16[256,512]{1,0:T(8,128)(2,1)S(1)}, u32[]{:S(2)}, u32[]{:S(2)}) %collective-permute-start.21) | collective-permute-done | bytes 262176 | tf_op jit(solution)/shard_map/ppermute | solution.py:28
  80.1 1.0 collective-permute-done.22.dpair_ref.refs_9_
  81.1 1.0 width_grad.3.refs_12_
  82.2 1.0 copy-done.2
  83.2 1.0 weight_terms.2
  84.2 1.0 weight_terms.3
  85.3 2.7 %collective-permute-start.34 = (bf16[128,768]{1,0:T(8,128)(2,1)S(1)}, bf16[128,768]{1,0:T(8,128)(2,1)S(1)}, u32[]{:S(2)}, u32[]{:S(2)}) collective-permute-start(bf16[128,768]{1,0:T(8,128)(2,1)S(1)} %get-tuple-element.38), channel_id=1, source_target_pairs={{0,2},{1,3},{2,0},{3,1},{4,6},{5,7},{6,4},{7,5},{8,10},{9,11},{10,... | collective-permute-start | bytes 589832 | tf_op jit(solution)/shard_map/ppermute | solution.py:35
  88.7 1.9 %collective-permute-start.36 = (bf16[128,768]{1,0:T(8,128)(2,1)S(1)}, bf16[128,768]{1,0:T(8,128)(2,1)S(1)}, u32[]{:S(2)}, u32[]{:S(2)}) collective-permute-start(bf16[128,768]{1,0:T(8,128)(2,1)S(1)} %get-tuple-element.40), channel_id=1, source_target_pairs={{0,2},{1,3},{2,0},{3,1},{4,6},{5,7},{6,4},{7,5},{8,10},{9,11},{10,... | collective-permute-start | bytes 589832 | tf_op jit(solution)/shard_map/ppermute | solution.py:35
  90.7 3.1 %collective-permute-done.34 = bf16[128,768]{1,0:T(8,128)(2,1)S(1)} collective-permute-done((bf16[128,768]{1,0:T(8,128)(2,1)S(1)}, bf16[128,768]{1,0:T(8,128)(2,1)S(1)}, u32[]{:S(2)}, u32[]{:S(2)}) %collective-permute-start.34) | collective-permute-done | bytes 196640 | tf_op jit(solution)/shard_map/ppermute | solution.py:35
  93.8 2.3 %collective-permute-start.35 = (bf16[128,768]{1,0:T(8,128)(2,1)S(1)}, bf16[128,768]{1,0:T(8,128)(2,1)S(1)}, u32[]{:S(2)}, u32[]{:S(2)}) collective-permute-start(bf16[128,768]{1,0:T(8,128)(2,1)S(1)} %add_convert_fusion), channel_id=1, source_target_pairs={{0,8},{4,12},{8,16},{12,20},{16,24},{20,28},{24,0},{28,4},{1,9},{5... | collective-permute-start | bytes 589832 | tf_op jit(solution)/shard_map/ppermute | solution.py:47
  96.1 1.9 %collective-permute-done.32 = bf16[128,768]{1,0:T(8,128)(2,1)S(1)} collective-permute-done((bf16[128,768]{1,0:T(8,128)(2,1)S(1)}, bf16[128,768]{1,0:T(8,128)(2,1)S(1)}, u32[]{:S(2)}, u32[]{:S(2)}) %collective-permute-start.32) | collective-permute-done | bytes 196640 | tf_op jit(solution)/shard_map/ppermute | solution.py:35
  98.0 4.7 %collective-permute-start.33 = (bf16[128,768]{1,0:T(8,128)(2,1)S(1)}, bf16[128,768]{1,0:T(8,128)(2,1)S(1)}, u32[]{:S(2)}, u32[]{:S(2)}) collective-permute-start(bf16[128,768]{1,0:T(8,128)(2,1)S(1)} %add_convert_fusion.1), channel_id=1, source_target_pairs={{0,24},{4,28},{8,0},{12,4},{16,8},{20,12},{24,16},{28,20},{1,25},{... | collective-permute-start | bytes 589832 | tf_op jit(solution)/shard_map/ppermute | solution.py:47
  102.8 3.5 %collective-permute-done.30 = bf16[128,768]{1,0:T(8,128)(2,1)S(1)} collective-permute-done((bf16[128,768]{1,0:T(8,128)(2,1)S(1)}, bf16[128,768]{1,0:T(8,128)(2,1)S(1)}, u32[]{:S(2)}, u32[]{:S(2)}) %collective-permute-start.30) | collective-permute-done | bytes 196640 | tf_op jit(solution)/shard_map/ppermute | solution.py:35
  106.3 4.1 %collective-permute-start.31 = (bf16[128,768]{1,0:T(8,128)(2,1)S(1)}, bf16[128,768]{1,0:T(8,128)(2,1)S(1)}, u32[]{:S(2)}, u32[]{:S(2)}) collective-permute-start(bf16[128,768]{1,0:T(8,128)(2,1)S(1)} %add_convert_fusion.2), channel_id=1, source_target_pairs={{0,16},{4,20},{8,24},{12,28},{16,0},{20,4},{24,8},{28,12},{1,17},{... | collective-permute-start | bytes 589832 | tf_op jit(solution)/shard_map/ppermute | solution.py:47
  110.4 1.0 width_grad.2.mine_ref
  111.4 8.2 %collective-permute-done.31 = bf16[128,768]{1,0:T(8,128)(2,1)S(1)} collective-permute-done((bf16[128,768]{1,0:T(8,128)(2,1)S(1)}, bf16[128,768]{1,0:T(8,128)(2,1)S(1)}, u32[]{:S(2)}, u32[]{:S(2)}) %collective-permute-start.31) | collective-permute-done | bytes 196640 | tf_op jit(solution)/shard_map/ppermute | solution.py:47
  119.6 0.9 add_add_fusion
  120.5 1.6 %merge_halves.1 = bf16[256,4096]{1,0:T(8,128)(2,1)} custom-call(bf16[256,2048]{1,0:T(8,128)(2,1)S(1)} %width_grad.2.mine_ref, bf16[256,2048]{1,0:T(8,128)(2,1)S(1)} %collective-permute-done.23.other_ref), custom_call_target="tpu_custom_call" | custom-call | tf_op jit(solution)/shard_map/merge_halves/pallas_call | solution.py:121
  (67 shorter events, 4.5 us)
Async XLA Ops:
  0.6 17.7 %copy-start.4 = (s32[1,8]{1,0:T(1,128)S(1)}, s32[1,8]{1,0:T(1,128)}, u32[]{:S(2)}) copy-start(s32[1,8]{1,0:T(1,128)} %param.8) | copy-start | bytes 100
  0.7 40.4 %copy-start.6 = (s32[1,8]{1,0:T(1,128)S(1)}, s32[1,8]{1,0:T(1,128)}, u32[]{:S(2)}) copy-start(s32[1,8]{1,0:T(1,128)} %param.9) | copy-start | bytes 100
  2.4 7.5 %copy-start.1 = (bf16[128,768]{1,0:T(8,128)(2,1)S(1)}, bf16[128,768]{1,0:T(8,128)(2,1)}, u32[]{:S(2)}) copy-start(bf16[128,768]{1,0:T(8,128)(2,1)} %get-tuple-element.42.held_ref.refs_0_) | copy-start | bytes 589828
  5.4 35.6 %collective-permute-start.14 = (bf16[256,2048]{1,0:T(8,128)(2,1)}, bf16[256,2048]{1,0:T(8,128)(2,1)S(1)}, u32[]{:S(2)}, u32[]{:S(2)}) collective-permute-start(bf16[256,2048]{1,0:T(8,128)(2,1)} %get-tuple-element.25), channel_id=1, source_target_pairs={{0,1},{1,0},{2,3},{3,2},{4,5},{5,4},{6,7},{7,6},{8,9},{9,8},{10,11... | collective-permute-start | bytes 3145736 | tf_op jit(solution)/shard_map/ppermute | solution.py:28
  8.4 9.9 %collective-permute-start = (bf16[128,768]{1,0:T(8,128)(2,1)}, bf16[128,768]{1,0:T(8,128)(2,1)S(1)}, u32[]{:S(2)}, u32[]{:S(2)}) collective-permute-start(bf16[128,768]{1,0:T(8,128)(2,1)} %get-tuple-element.23), channel_id=1, source_target_pairs={{0,8},{4,12},{8,16},{12,20},{16,24},{20,28},{24,0},{28,4},{1,9},{5... | collective-permute-start | bytes 589832 | tf_op jit(solution)/shard_map/ppermute | solution.py:47
  10.0 15.4 %collective-permute-start.2 = (bf16[128,768]{1,0:T(8,128)(2,1)S(1)}, bf16[128,768]{1,0:T(8,128)(2,1)S(1)}, u32[]{:S(2)}, u32[]{:S(2)}) collective-permute-start(bf16[128,768]{1,0:T(8,128)(2,1)S(1)} %copy-done.1), channel_id=1, source_target_pairs={{0,16},{4,20},{8,24},{12,28},{16,0},{20,4},{24,8},{28,12},{1,17},{... | collective-permute-start | bytes 589832 | tf_op jit(solution)/shard_map/ppermute | solution.py:47
  12.6 14.3 %collective-permute-start.4 = (bf16[128,768]{1,0:T(8,128)(2,1)}, bf16[128,768]{1,0:T(8,128)(2,1)S(1)}, u32[]{:S(2)}, u32[]{:S(2)}) collective-permute-start(bf16[128,768]{1,0:T(8,128)(2,1)} %get-tuple-element.23), channel_id=1, source_target_pairs={{0,24},{4,28},{8,0},{12,4},{16,8},{20,12},{24,16},{28,20},{1,25},{... | collective-permute-start | bytes 589832 | tf_op jit(solution)/shard_map/ppermute | solution.py:47
  13.9 13.0 %collective-permute-start.6 = (bf16[128,768]{1,0:T(8,128)(2,1)S(1)}, bf16[128,768]{1,0:T(8,128)(2,1)S(1)}, u32[]{:S(2)}, u32[]{:S(2)}) collective-permute-start(bf16[128,768]{1,0:T(8,128)(2,1)S(1)} %copy-done.1), channel_id=1, source_target_pairs={{0,4},{4,0},{8,12},{12,8},{16,20},{20,16},{24,28},{28,24},{1,5},{5... | collective-permute-start | bytes 589832 | tf_op jit(solution)/shard_map/ppermute | solution.py:40
  18.3 9.1 %collective-permute-start.7 = (bf16[128,768]{1,0:T(8,128)(2,1)S(1)}, bf16[128,768]{1,0:T(8,128)(2,1)S(1)}, u32[]{:S(2)}, u32[]{:S(2)}) collective-permute-start(bf16[128,768]{1,0:T(8,128)(2,1)S(1)} %get-tuple-element.41.refs_1_), channel_id=1, source_target_pairs={{0,4},{4,0},{8,12},{12,8},{16,20},{20,16},{24,28},{28,24},{1,5},{5... | collective-permute-start | bytes 589832 | tf_op jit(solution)/shard_map/ppermute | solution.py:40
  25.4 7.8 %collective-permute-start.1 = (bf16[128,768]{1,0:T(8,128)(2,1)S(1)}, bf16[128,768]{1,0:T(8,128)(2,1)S(1)}, u32[]{:S(2)}, u32[]{:S(2)}) collective-permute-start(bf16[128,768]{1,0:T(8,128)(2,1)S(1)} %collective-permute-done.refs_2_), channel_id=1, source_target_pairs={{0,2},{1,3},{2,0},{3,1},{4,6},{5,7},{6,4},{7,5},{8,10},{9,11},{10,... | collective-permute-start | bytes 589832 | tf_op jit(solution)/shard_map/ppermute | solution.py:35
  26.9 13.6 %collective-permute-start.8 = (bf16[128,768]{1,0:T(8,128)(2,1)S(1)}, bf16[128,768]{1,0:T(8,128)(2,1)S(1)}, u32[]{:S(2)}, u32[]{:S(2)}) collective-permute-start(bf16[128,768]{1,0:T(8,128)(2,1)S(1)} %collective-permute-done.refs_2_), channel_id=1, source_target_pairs={{0,4},{4,0},{8,12},{12,8},{16,20},{20,16},{24,28},{28,24},{1,5},{5... | collective-permute-start | bytes 589832 | tf_op jit(solution)/shard_map/ppermute | solution.py:40
  26.9 10.5 %collective-permute-start.3 = (bf16[128,768]{1,0:T(8,128)(2,1)S(1)}, bf16[128,768]{1,0:T(8,128)(2,1)S(1)}, u32[]{:S(2)}, u32[]{:S(2)}) collective-permute-start(bf16[128,768]{1,0:T(8,128)(2,1)S(1)} %collective-permute-done.2.refs_4_), channel_id=1, source_target_pairs={{0,2},{1,3},{2,0},{3,1},{4,6},{5,7},{6,4},{7,5},{8,10},{9,11},{10,... | collective-permute-start | bytes 589832 | tf_op jit(solution)/shard_map/ppermute | solution.py:35
  27.5 13.0 %collective-permute-start.5 = (bf16[128,768]{1,0:T(8,128)(2,1)S(1)}, bf16[128,768]{1,0:T(8,128)(2,1)S(1)}, u32[]{:S(2)}, u32[]{:S(2)}) collective-permute-start(bf16[128,768]{1,0:T(8,128)(2,1)S(1)} %collective-permute-done.4.refs_6_), channel_id=1, source_target_pairs={{0,2},{1,3},{2,0},{3,1},{4,6},{5,7},{6,4},{7,5},{8,10},{9,11},{10,... | collective-permute-start | bytes 589832 | tf_op jit(solution)/shard_map/ppermute | solution.py:35
  33.1 8.7 %collective-permute-start.10 = (bf16[128,768]{1,0:T(8,128)(2,1)S(1)}, bf16[128,768]{1,0:T(8,128)(2,1)S(1)}, u32[]{:S(2)}, u32[]{:S(2)}) collective-permute-start(bf16[128,768]{1,0:T(8,128)(2,1)S(1)} %collective-permute-done.2.refs_4_), channel_id=1, source_target_pairs={{0,4},{4,0},{8,12},{12,8},{16,20},{20,16},{24,28},{28,24},{1,5},{5... | collective-permute-start | bytes 589832 | tf_op jit(solution)/shard_map/ppermute | solution.py:40
  37.3 5.0 %collective-permute-start.12 = (bf16[128,768]{1,0:T(8,128)(2,1)S(1)}, bf16[128,768]{1,0:T(8,128)(2,1)S(1)}, u32[]{:S(2)}, u32[]{:S(2)}) collective-permute-start(bf16[128,768]{1,0:T(8,128)(2,1)S(1)} %collective-permute-done.4.refs_6_), channel_id=1, source_target_pairs={{0,4},{4,0},{8,12},{12,8},{16,20},{20,16},{24,28},{28,24},{1,5},{5... | collective-permute-start | bytes 589832 | tf_op jit(solution)/shard_map/ppermute | solution.py:40
  40.5 1.8 %collective-permute-start.9 = (bf16[128,768]{1,0:T(8,128)(2,1)S(1)}, bf16[128,768]{1,0:T(8,128)(2,1)S(1)}, u32[]{:S(2)}, u32[]{:S(2)}) collective-permute-start(bf16[128,768]{1,0:T(8,128)(2,1)S(1)} %collective-permute-done.1.refs_3_), channel_id=1, source_target_pairs={{0,4},{4,0},{8,12},{12,8},{16,20},{20,16},{24,28},{28,24},{1,5},{5... | collective-permute-start | bytes 589832 | tf_op jit(solution)/shard_map/ppermute | solution.py:40
  40.5 1.8 %collective-permute-start.11 = (bf16[128,768]{1,0:T(8,128)(2,1)S(1)}, bf16[128,768]{1,0:T(8,128)(2,1)S(1)}, u32[]{:S(2)}, u32[]{:S(2)}) collective-permute-start(bf16[128,768]{1,0:T(8,128)(2,1)S(1)} %collective-permute-done.3.refs_5_), channel_id=1, source_target_pairs={{0,4},{4,0},{8,12},{12,8},{16,20},{20,16},{24,28},{28,24},{1,5},{5... | collective-permute-start | bytes 589832 | tf_op jit(solution)/shard_map/ppermute | solution.py:40
  41.0 1.5 %collective-permute-start.13 = (bf16[128,768]{1,0:T(8,128)(2,1)S(1)}, bf16[128,768]{1,0:T(8,128)(2,1)S(1)}, u32[]{:S(2)}, u32[]{:S(2)}) collective-permute-start(bf16[128,768]{1,0:T(8,128)(2,1)S(1)} %collective-permute-done.5.refs_7_), channel_id=1, source_target_pairs={{0,4},{4,0},{8,12},{12,8},{16,20},{20,16},{24,28},{28,24},{1,5},{5... | collective-permute-start | bytes 589832 | tf_op jit(solution)/shard_map/ppermute | solution.py:40
  41.8 1.9 %copy-start = (bf16[256,2048]{1,0:T(8,128)(2,1)S(1)}, bf16[256,2048]{1,0:T(8,128)(2,1)}, u32[]{:S(2)}) copy-start(bf16[256,2048]{1,0:T(8,128)(2,1)} %get-tuple-element.22.tokens_ref.refs_0_) | copy-start | bytes 3145732
  41.8 37.8 %collective-permute-start.24 = (bf16[256,1024]{1,0:T(8,128)(2,1)S(1)}, bf16[256,1024]{1,0:T(8,128)(2,1)S(1)}, u32[]{:S(2)}, u32[]{:S(2)}) collective-permute-start(bf16[256,1024]{1,0:T(8,128)(2,1)S(1)} %slice.14), channel_id=1, source_target_pairs={{0,4},{4,0},{8,12},{12,8},{16,20},{20,16},{24,28},{28,24},{1,5},{5... | collective-permute-start | bytes 1572872 | tf_op jit(solution)/shard_map/ppermute | solution.py:40
  43.1 6.4 %collective-permute-start.16 = (bf16[256,256]{1,0:T(8,128)(2,1)S(1)}, bf16[256,256]{1,0:T(8,128)(2,1)S(1)}, u32[]{:S(2)}, u32[]{:S(2)}) collective-permute-start(bf16[256,256]{1,0:T(8,128)(2,1)S(1)} %get-tuple-element.28), channel_id=1, source_target_pairs={{0,1},{1,0},{2,3},{3,2},{4,5},{5,4},{6,7},{7,6},{8,9},{9,8},{10,11... | collective-permute-start | bytes 393224 | tf_op jit(solution)/shard_map/ppermute | solution.py:28
  44.3 10.7 %copy-start.5 = (bf16[1,256,512]{2,1,0:T(8,128)(2,1)S(1)}, bf16[1,256,512]{2,1,0:T(8,128)(2,1)}, u32[]{:S(2)}) copy-start(bf16[1,256,512]{2,1,0:T(8,128)(2,1)} %param.7) | copy-start | bytes 786436
  44.9 13.3 %collective-permute-start.15 = (bf16[256,512]{1,0:T(8,128)(2,1)S(1)}, bf16[256,512]{1,0:T(8,128)(2,1)S(1)}, u32[]{:S(2)}, u32[]{:S(2)}) collective-permute-start(bf16[256,512]{1,0:T(8,128)(2,1)S(1)} %get-tuple-element.26), channel_id=1, source_target_pairs={{0,1},{1,0},{2,3},{3,2},{4,5},{5,4},{6,7},{7,6},{8,9},{9,8},{10,11... | collective-permute-start | bytes 786440 | tf_op jit(solution)/shard_map/ppermute | solution.py:28
  49.5 8.7 %collective-permute-start.17 = (bf16[256,256]{1,0:T(8,128)(2,1)S(1)}, bf16[256,256]{1,0:T(8,128)(2,1)S(1)}, u32[]{:S(2)}, u32[]{:S(2)}) collective-permute-start(bf16[256,256]{1,0:T(8,128)(2,1)S(1)} %add_convert_fusion.4.refs_2_), channel_id=1, source_target_pairs={{0,2},{1,3},{4,6},{5,7},{8,10},{9,11},{12,14},{13,15},{16,18},{17,... | collective-permute-start | bytes 393224 | tf_op jit(solution)/shard_map/ppermute | solution.py:53
  53.0 5.3 %collective-permute-start.18 = (bf16[256,256]{1,0:T(8,128)(2,1)S(1)}, bf16[256,256]{1,0:T(8,128)(2,1)S(1)}, u32[]{:S(2)}, u32[]{:S(2)}) collective-permute-start(bf16[256,256]{1,0:T(8,128)(2,1)S(1)} %add_convert_fusion.4.refs_2_), channel_id=1, source_target_pairs={{0,1},{1,2},{2,3},{4,5},{5,6},{6,7},{8,9},{9,10},{10,11},{12,13},{... | collective-permute-start | bytes 393224 | tf_op jit(solution)/shard_map/ppermute | solution.py:53
  64.6 6.9 %collective-permute-start.20 = (bf16[256,256]{1,0:T(8,128)(2,1)S(1)}, bf16[256,256]{1,0:T(8,128)(2,1)S(1)}, u32[]{:S(2)}, u32[]{:S(2)}) collective-permute-start(bf16[256,256]{1,0:T(8,128)(2,1)S(1)} %get-tuple-element.44), channel_id=1, source_target_pairs={{2,0},{3,1},{6,4},{7,5},{10,8},{11,9},{14,12},{15,13},{18,16},{19,... | collective-permute-start | bytes 393224 | tf_op jit(solution)/shard_map/ppermute | solution.py:53
  65.9 8.1 %collective-permute-start.19 = (bf16[256,256]{1,0:T(8,128)(2,1)S(1)}, bf16[256,256]{1,0:T(8,128)(2,1)S(1)}, u32[]{:S(2)}, u32[]{:S(2)}) collective-permute-start(bf16[256,256]{1,0:T(8,128)(2,1)S(1)} %get-tuple-element.43), channel_id=1, source_target_pairs={{1,0},{2,1},{3,2},{5,4},{6,5},{7,6},{9,8},{10,9},{11,10},{13,12},{... | collective-permute-start | bytes 393224 | tf_op jit(solution)/shard_map/ppermute | solution.py:53
  67.4 15.8 %collective-permute-start.25 = (bf16[256,1024]{1,0:T(8,128)(2,1)S(1)}, bf16[256,1024]{1,0:T(8,128)(2,1)S(1)}, u32[]{:S(2)}, u32[]{:S(2)}) collective-permute-start(bf16[256,1024]{1,0:T(8,128)(2,1)S(1)} %slice.16), channel_id=1, source_target_pairs={{0,4},{4,0},{8,12},{12,8},{16,20},{20,16},{24,28},{28,24},{1,5},{5... | collective-permute-start | bytes 1572872 | tf_op jit(solution)/shard_map/ppermute | solution.py:40
  67.5 12.1 %collective-permute-start.21 = (bf16[256,512]{1,0:T(8,128)(2,1)S(1)}, bf16[256,512]{1,0:T(8,128)(2,1)S(1)}, u32[]{:S(2)}, u32[]{:S(2)}) collective-permute-start(bf16[256,512]{1,0:T(8,128)(2,1)S(1)} %get-tuple-element.30.dquery_ref.refs_4_), channel_id=1, source_target_pairs={{0,1},{1,0},{2,3},{3,2},{4,5},{5,4},{6,7},{7,6},{8,9},{9,8},{10,11... | collective-permute-start | bytes 786440 | tf_op jit(solution)/shard_map/ppermute | solution.py:28
  71.4 11.7 %collective-permute-start.26 = (bf16[256,512]{1,0:T(8,128)(2,1)S(1)}, bf16[256,512]{1,0:T(8,128)(2,1)S(1)}, u32[]{:S(2)}, u32[]{:S(2)}) collective-permute-start(bf16[256,512]{1,0:T(8,128)(2,1)S(1)} %get-tuple-element.30.dquery_ref.refs_4_), channel_id=1, source_target_pairs={{0,4},{4,0},{8,12},{12,8},{16,20},{20,16},{24,28},{28,24},{1,5},{5... | collective-permute-start | bytes 786440 | tf_op jit(solution)/shard_map/ppermute | solution.py:40
  74.0 7.1 %collective-permute-start.22 = (bf16[256,256]{1,0:T(8,128)(2,1)S(1)}, bf16[256,256]{1,0:T(8,128)(2,1)S(1)}, u32[]{:S(2)}, u32[]{:S(2)}) collective-permute-start(bf16[256,256]{1,0:T(8,128)(2,1)S(1)} %add_convert_fusion.3.dpair_ref.refs_8_), channel_id=1, source_target_pairs={{0,1},{1,0},{2,3},{3,2},{4,5},{5,4},{6,7},{7,6},{8,9},{9,8},{10,11... | collective-permute-start | bytes 393224 | tf_op jit(solution)/shard_map/ppermute | solution.py:28
  79.6 3.6 %collective-permute-start.27 = (bf16[256,512]{1,0:T(8,128)(2,1)S(1)}, bf16[256,512]{1,0:T(8,128)(2,1)S(1)}, u32[]{:S(2)}, u32[]{:S(2)}) collective-permute-start(bf16[256,512]{1,0:T(8,128)(2,1)S(1)} %collective-permute-done.21.dquery_ref.refs_5_), channel_id=1, source_target_pairs={{0,4},{4,0},{8,12},{12,8},{16,20},{20,16},{24,28},{28,24},{1,5},{5... | collective-permute-start | bytes 786440 | tf_op jit(solution)/shard_map/ppermute | solution.py:40
  79.6 3.5 %collective-permute-start.28 = (bf16[256,256]{1,0:T(8,128)(2,1)S(1)}, bf16[256,256]{1,0:T(8,128)(2,1)S(1)}, u32[]{:S(2)}, u32[]{:S(2)}) collective-permute-start(bf16[256,256]{1,0:T(8,128)(2,1)S(1)} %add_convert_fusion.3.dpair_ref.refs_8_), channel_id=1, source_target_pairs={{0,4},{4,0},{8,12},{12,8},{16,20},{20,16},{24,28},{28,24},{1,5},{5... | collective-permute-start | bytes 393224 | tf_op jit(solution)/shard_map/ppermute | solution.py:40
  81.1 2.0 %collective-permute-start.29 = (bf16[256,256]{1,0:T(8,128)(2,1)S(1)}, bf16[256,256]{1,0:T(8,128)(2,1)S(1)}, u32[]{:S(2)}, u32[]{:S(2)}) collective-permute-start(bf16[256,256]{1,0:T(8,128)(2,1)S(1)} %collective-permute-done.22.dpair_ref.refs_9_), channel_id=1, source_target_pairs={{0,4},{4,0},{8,12},{12,8},{16,20},{20,16},{24,28},{28,24},{1,5},{5... | collective-permute-start | bytes 393224 | tf_op jit(solution)/shard_map/ppermute | solution.py:40
  82.2 1.0 copy-start.2
  84.2 3.8 %copy-start.3 = (bf16[256,2048]{1,0:T(8,128)(2,1)S(1)}, bf16[256,2048]{1,0:T(8,128)(2,1)}, u32[]{:S(2)}) copy-start(bf16[256,2048]{1,0:T(8,128)(2,1)} %copy-done.2) | copy-start | bytes 3145732
  85.3 8.5 %collective-permute-start.34 = (bf16[128,768]{1,0:T(8,128)(2,1)S(1)}, bf16[128,768]{1,0:T(8,128)(2,1)S(1)}, u32[]{:S(2)}, u32[]{:S(2)}) collective-permute-start(bf16[128,768]{1,0:T(8,128)(2,1)S(1)} %get-tuple-element.38), channel_id=1, source_target_pairs={{0,2},{1,3},{2,0},{3,1},{4,6},{5,7},{6,4},{7,5},{8,10},{9,11},{10,... | collective-permute-start | bytes 589832 | tf_op jit(solution)/shard_map/ppermute | solution.py:35
  88.0 32.4 %collective-permute-start.23 = (bf16[256,2048]{1,0:T(8,128)(2,1)S(1)}, bf16[256,2048]{1,0:T(8,128)(2,1)S(1)}, u32[]{:S(2)}, u32[]{:S(2)}) collective-permute-start(bf16[256,2048]{1,0:T(8,128)(2,1)S(1)} %copy-done.3), channel_id=1, source_target_pairs={{0,1},{1,0},{2,3},{3,2},{4,5},{5,4},{6,7},{7,6},{8,9},{9,8},{10,11... | collective-permute-start | bytes 3145736 | tf_op jit(solution)/shard_map/ppermute | solution.py:28
  88.6 9.4 %collective-permute-start.32 = (bf16[128,768]{1,0:T(8,128)(2,1)S(1)}, bf16[128,768]{1,0:T(8,128)(2,1)S(1)}, u32[]{:S(2)}, u32[]{:S(2)}) collective-permute-start(bf16[128,768]{1,0:T(8,128)(2,1)S(1)} %get-tuple-element.36.refs_12_), channel_id=1, source_target_pairs={{0,2},{1,3},{2,0},{3,1},{4,6},{5,7},{6,4},{7,5},{8,10},{9,11},{10,... | collective-permute-start | bytes 589832 | tf_op jit(solution)/shard_map/ppermute | solution.py:35
  88.7 22.7 %collective-permute-start.36 = (bf16[128,768]{1,0:T(8,128)(2,1)S(1)}, bf16[128,768]{1,0:T(8,128)(2,1)S(1)}, u32[]{:S(2)}, u32[]{:S(2)}) collective-permute-start(bf16[128,768]{1,0:T(8,128)(2,1)S(1)} %get-tuple-element.40), channel_id=1, source_target_pairs={{0,2},{1,3},{2,0},{3,1},{4,6},{5,7},{6,4},{7,5},{8,10},{9,11},{10,... | collective-permute-start | bytes 589832 | tf_op jit(solution)/shard_map/ppermute | solution.py:35
  90.6 15.6 %collective-permute-start.30 = (bf16[128,768]{1,0:T(8,128)(2,1)S(1)}, bf16[128,768]{1,0:T(8,128)(2,1)S(1)}, u32[]{:S(2)}, u32[]{:S(2)}) collective-permute-start(bf16[128,768]{1,0:T(8,128)(2,1)S(1)} %get-tuple-element.34), channel_id=1, source_target_pairs={{0,2},{1,3},{2,0},{3,1},{4,6},{5,7},{6,4},{7,5},{8,10},{9,11},{10,... | collective-permute-start | bytes 589832 | tf_op jit(solution)/shard_map/ppermute | solution.py:35
  93.8 17.6 %collective-permute-start.35 = (bf16[128,768]{1,0:T(8,128)(2,1)S(1)}, bf16[128,768]{1,0:T(8,128)(2,1)S(1)}, u32[]{:S(2)}, u32[]{:S(2)}) collective-permute-start(bf16[128,768]{1,0:T(8,128)(2,1)S(1)} %add_convert_fusion), channel_id=1, source_target_pairs={{0,8},{4,12},{8,16},{12,20},{16,24},{20,28},{24,0},{28,4},{1,9},{5... | collective-permute-start | bytes 589832 | tf_op jit(solution)/shard_map/ppermute | solution.py:47
  98.0 13.4 %collective-permute-start.33 = (bf16[128,768]{1,0:T(8,128)(2,1)S(1)}, bf16[128,768]{1,0:T(8,128)(2,1)S(1)}, u32[]{:S(2)}, u32[]{:S(2)}) collective-permute-start(bf16[128,768]{1,0:T(8,128)(2,1)S(1)} %add_convert_fusion.1), channel_id=1, source_target_pairs={{0,24},{4,28},{8,0},{12,4},{16,8},{20,12},{24,16},{28,20},{1,25},{... | collective-permute-start | bytes 589832 | tf_op jit(solution)/shard_map/ppermute | solution.py:47
  106.3 13.3 %collective-permute-start.31 = (bf16[128,768]{1,0:T(8,128)(2,1)S(1)}, bf16[128,768]{1,0:T(8,128)(2,1)S(1)}, u32[]{:S(2)}, u32[]{:S(2)}) collective-permute-start(bf16[128,768]{1,0:T(8,128)(2,1)S(1)} %add_convert_fusion.2), channel_id=1, source_target_pairs={{0,16},{4,20},{8,24},{12,28},{16,0},{20,4},{24,8},{28,12},{1,17},{... | collective-permute-start | bytes 589832 | tf_op jit(solution)/shard_map/ppermute | solution.py:47

commit v6 on v5

--- a/solution.py
+++ b/solution.py
@@ -70,31 +70,49 @@
     return pl.ds(pl.multiple_of(index * width, width), width)
 
 
-def split_kernel(chips, rest, width, in_ref, held_ref, *out_refs):
-    for flip in range(PAIR):
-        for i, block in enumerate(block_order(chips, rest, flip)):
-            out_refs[flip][:, i * width : (i + 1) * width] = in_ref[:, lanes(block, width)]
-    out_refs[PAIR][...] = held_ref[...]
-
-
-def split_tokens(tokens, held, chips, rest, width):
-    rows, total = tokens.shape
+def split_kernel(chips, rest, width, in_ref, weights_ref, *out_refs):
+    own_ref = out_refs[-1]
+    order = block_order(chips, rest, 0) + block_order(chips, rest, 1)
+    for ref in out_refs[:-1]:
+        for i in range(ref.shape[1] // width):
+            ref[:, i * width : (i + 1) * width] = in_ref[:, lanes(order.pop(0), width)]
+
+    @pl.when(pl.program_id(0) == 0)
+    def _():
+        own_ref[...] = weights_ref[lanes(lax.axis_index("seq"), width), :]
+
+
+def own_places(rest):
+    place = lax.axis_index("seq")
+    return [PAIR * ((place // PAIR - j + rest) % rest) + place % PAIR for j in range(rest)]
+
+
+def split_inputs(tokens, weights, chips, rest):
+    (rows, total), (shard, cols) = tokens.shape, weights.shape
+    width = shard // (PAIR * rest)
+    half = total // PAIR
+    few = half // 8
+    widths = [half // CORES] * CORES + [half - few, few]
     if width % 128:
         blocks = tokens.reshape(rows, total // width, width)
         order = jnp.stack(block_order(chips, rest, 0) + block_order(chips, rest, 1))
-        return *jnp.split(jnp.take(blocks, order, axis=1).reshape(rows, total), PAIR, axis=1), held
+        taken = jnp.take(blocks, order, axis=1).reshape(rows, total)
+        own = lax.dynamic_index_in_dim(weights.reshape(PAIR * rest, width, cols), lax.axis_index("seq"), 0, keepdims=False)
+        return *jnp.split(taken, [half // CORES, half, total - few], axis=1), own
     tile = min(rows, 128)
-    half = pl.BlockSpec((tile, total // PAIR), lambda i: (i, 0))
-    whole = pl.BlockSpec(held.shape, lambda i: (0, 0))
+    own = pl.BlockSpec((width, cols), lambda i: (0, 0))
     return pl.pallas_call(
         functools.partial(split_kernel, chips, rest, width),
         grid=(rows // tile,),
-        in_specs=[pl.BlockSpec((tile, total), lambda i: (i, 0)), whole],
-        out_specs=[half] * PAIR + [whole],
-        out_shape=[jax.ShapeDtypeStruct((rows, total // PAIR), tokens.dtype)] * PAIR
-        + [jax.ShapeDtypeStruct(held.shape, held.dtype)],
-        name="split_tokens",
-    )(tokens, held)
+        in_specs=[
+            pl.BlockSpec((tile, total), lambda i: (i, 0)),
+            pl.BlockSpec((shard, cols), lambda i: (0, 0)),
+        ],
+        out_specs=[pl.BlockSpec((tile, w), lambda i: (i, 0)) for w in widths] + [own],
+        out_shape=[jax.ShapeDtypeStruct((rows, w), tokens.dtype) for w in widths]
+        + [jax.ShapeDtypeStruct((width, cols), weights.dtype)],
+        name="split_inputs",
+    )(tokens, weights)
 
 
 def merge_kernel(chips, rest, width, mine_ref, other_ref, out_ref, sems):
@@ -124,54 +142,51 @@
         out_specs=pl.BlockSpec(memory_space=pl.ANY),
         out_shape=jax.ShapeDtypeStruct((rows, PAIR * half), mine.dtype),
         scratch_shapes=[pltpu.SemaphoreType.DMA((count,))],
-        compiler_params=pltpu.CompilerParams(vmem_limit_bytes=48 * 2**20),
+        compiler_params=pltpu.CompilerParams(vmem_limit_bytes=20 * 2**20),
         name="merge_halves",
     )(mine, other)
 
 
-def project_kernel(first, span, per, qwidth, has_sum, tokens_ref, *refs):
-    if has_sum:
-        sum_ref, refs = refs[0], refs[1:]
-        total = sum_ref[...]
-    else:
-        total = None
-    pieces = refs[:-2] if qwidth else refs[:-1]
+def cut(parts, first, step):
+    for part in parts:
+        if first < part.shape[1]:
+            return part[:, first : first + step]
+        first -= part.shape[1]
+
+
+def project_kernel(span, per, qwidth, count, *refs):
+    tokens, pieces, (query_ref, pair_ref) = refs[:count], refs[count:-2], refs[-2:]
+    total = None
     for g in range(len(pieces) // per):
         rows = jnp.concatenate([r[...] for r in pieces[g * per : (g + 1) * per]], axis=0)
-        term = dot(tokens_ref[:, (first + g) * span : (first + g + 1) * span], rows)
+        term = dot(cut(tokens, g * span, span), rows)
         total = term if total is None else total + term
-    if qwidth:
-        query_ref, pair_ref = refs[-2:]
-        query_ref[...] = total[:, :qwidth].astype(query_ref.dtype)
-        pair_ref[...] = total[:, qwidth:].astype(pair_ref.dtype)
-    else:
-        refs[-1][...] = total
-
-
-def project(tokens, groups, first=0, qwidth=0, kind=F32, so_far=None):
-    rows = tokens.shape[0]
+    query_ref[...] = total[:, :qwidth].astype(query_ref.dtype)
+    pair_ref[...] = total[:, qwidth:].astype(pair_ref.dtype)
+
+
+def project(tokens, groups, qwidth, kind):
+    rows = tokens[0].shape[0]
     cols = groups[0][0].shape[1]
     pieces = [piece for group in groups for piece in group]
     span = sum(piece.shape[0] for piece in groups[0])
-    widths = [qwidth, cols - qwidth] if qwidth else [cols]
-    sums = [] if so_far is None else [so_far]
-    outs = pl.pallas_call(
-        functools.partial(project_kernel, first, span, len(groups[0]), qwidth, len(sums)),
-        in_specs=[VMEM] * (1 + len(sums) + len(pieces)),
-        out_specs=[VMEM] * len(widths),
-        out_shape=[jax.ShapeDtypeStruct((rows, w), kind) for w in widths],
-        compiler_params=pltpu.CompilerParams(vmem_limit_bytes=48 * 2**20),
+    return pl.pallas_call(
+        functools.partial(project_kernel, span, len(groups[0]), qwidth, len(tokens)),
+        in_specs=[VMEM] * (len(tokens) + len(pieces)),
+        out_specs=[VMEM] * 2,
+        out_shape=[jax.ShapeDtypeStruct((rows, w), kind) for w in (qwidth, cols - qwidth)],
+        compiler_params=pltpu.CompilerParams(vmem_limit_bytes=20 * 2**20),
         name="project",
-    )(tokens, *sums, *pieces)
-    return outs if qwidth else outs[0]
+    )(*tokens, *pieces)
 
 
 def grad_kernel(span, per, dquery_ref, dpair_ref, *refs):
-    pieces, out_ref = refs[:-1], refs[-1]
+    pieces, (out_ref, mark_ref) = refs[:-2], refs[-2:]
     grads = jnp.concatenate([dquery_ref[...], dpair_ref[...]], axis=1)
     for k in range(len(pieces) // per):
         rows = jnp.concatenate([r[...] for r in pieces[k * per : (k + 1) * per]], axis=0)
         out_ref[:, k * span : (k + 1) * span] = dot(grads, rows, NT).astype(BF16)
+    mark_ref[...] = grads[:16, :128]
 
 
 def width_grad(dquery, dpair, groups):
@@ -181,39 +196,43 @@
     return pl.pallas_call(
         functools.partial(grad_kernel, span, len(groups[0])),
         in_specs=[VMEM] * (2 + len(pieces)),
-        out_specs=VMEM,
-        out_shape=jax.ShapeDtypeStruct((rows, span * len(groups)), BF16),
-        compiler_params=pltpu.CompilerParams(vmem_limit_bytes=48 * 2**20),
+        out_specs=[VMEM] * 2,
+        out_shape=[jax.ShapeDtypeStruct((rows, span * len(groups)), BF16), jax.ShapeDtypeStruct((16, 128), BF16)],
+        compiler_params=pltpu.CompilerParams(vmem_limit_bytes=20 * 2**20),
         name="width_grad",
     )(dquery, dpair, *pieces)
 
 
-def weight_kernel(steps, rest, width, count, *refs):
-    tokens, dquery, dpair = refs[:count], refs[count : 2 * count], refs[2 * count : 3 * count]
-    outs = refs[3 * count + 1 :]
-    right = jnp.concatenate(
-        [jnp.concatenate([q[...], p[...]], axis=1) for q, p in zip(dquery, dpair)], axis=0
-    )
+def weight_kernel(steps, rest, width, sources, grads, *refs):
+    tokens = []
+    for count, _ in sources:
+        tokens.append(refs[:count])
+        refs = refs[count:]
+    right = [jnp.concatenate([r[...] for r in refs[i : i + grads]], axis=1) for i in range(0, grads * len(sources), grads)]
+    right = jnp.concatenate(right, axis=0)
+    outs = refs[grads * len(sources) + 1 :]
     span = rest * width
     for i, k in enumerate(steps):
-        left = jnp.concatenate([t[:, k * span : (k + 1) * span] for t in tokens], axis=0)
+        left = jnp.concatenate([cut(t, first + k * span, span) for t, (_, first) in zip(tokens, sources)], axis=0)
         total = dot(left.T, right)
         for j in range(rest):
             out = outs[i * rest + j]
             out[...] = total[j * width : (j + 1) * width].astype(out.dtype)
 
 
-def weight_terms(steps, rest, width, tokens, dquery, dpair, after):
-    cols = dquery[0].shape[1] + dpair[0].shape[1]
-    count = len(tokens)
-    return pl.pallas_call(
-        functools.partial(weight_kernel, steps, rest, width, count),
-        in_specs=[VMEM] * (3 * count) + [pl.BlockSpec(memory_space=pl.ANY)],
+def weight_terms(steps, rest, width, tokens, grads, after):
+    cols = sum(g.shape[1] for g in grads[0])
+    sources = [(len(parts), first) for parts, first in tokens]
+    parts = [part for group, _ in tokens for part in group]
+    given = [g for group in grads for g in group]
+    return pl.pallas_call(
+        functools.partial(weight_kernel, steps, rest, width, sources, len(grads[0])),
+        in_specs=[VMEM] * (len(parts) + len(given) + 1),
         out_specs=[VMEM] * (len(steps) * rest),
         out_shape=[jax.ShapeDtypeStruct((width, cols), BF16 if j else F32) for _ in steps for j in range(rest)],
-        compiler_params=pltpu.CompilerParams(vmem_limit_bytes=48 * 2**20),
+        compiler_params=pltpu.CompilerParams(vmem_limit_bytes=20 * 2**20),
         name="weight_terms",
-    )(*tokens, *dquery, *dpair, after)
+    )(*parts, *given, after)
 
 
 def attend_kernel(
@@ -279,7 +298,7 @@
             jax.ShapeDtypeStruct((rows, two), F32),
             jax.ShapeDtypeStruct((back * rows, two), BF16),
         ],
-        compiler_params=pltpu.CompilerParams(vmem_limit_bytes=48 * 2**20),
+        compiler_params=pltpu.CompilerParams(vmem_limit_bytes=20 * 2**20),
         name="attend",
     )(docs, q, q_from, cot, *pairs)
 
@@ -303,26 +322,25 @@
     width = shard_rows // seq_count
     back = -(-(local * seq_count // 2 - 1) // local)
 
+    mine_own, mine_across, *sent, own = split_inputs(tokens, weights, chips, rest)
+    tokens_mine = [mine_own, mine_across]
+    tokens_other = [swap_x(part) for part in sent]
+
     blocks = weights.reshape(seq_count, width, cols)
-    places = [PAIR * ((place // PAIR - j + rest) % rest) + place % PAIR for j in range(rest)]
-    groups_own = [[lax.dynamic_index_in_dim(blocks, p, 0, keepdims=False) for p in places]]
-    own = groups_own[0][0]
-    farthest = chips // 2
-    arrived = {farthest: shift_chip(own, farthest)}
-
-    tokens_mine, tokens_sent, own = split_tokens(tokens, own, chips, rest, width)
-    tokens_other = swap_x(tokens_sent)
-
-    for k in range(1, chips):
-        first = arrived[k] if k in arrived else shift_chip(own, k)
-        groups_own.append([first] + [shift_rest(first, j) for j in range(1, rest)])
+    groups_own = [[lax.dynamic_index_in_dim(blocks, p, 0, keepdims=False) for p in own_places(rest)]]
+    arrived = {}
+    for k in sorted(range(1, chips), key=lambda k: (-abs(2 * k - chips), k)):
+        first = shift_chip(own, k)
+        if k == chips // 2:
+            first, arrived = lax.optimization_barrier((first, arrived))
+        arrived[k] = [first] + [shift_rest(first, j) for j in range(1, rest)]
+    groups_own += [arrived[k] for k in range(1, chips)]
     groups_across = [[swap_core(piece) for piece in group] for group in groups_own]
-
-    so_far = project(tokens_other, groups_own)
-    query_sent, pair_sent = project(tokens_other, groups_across, chips, qwidth, BF16, so_far)
+    groups = groups_own + groups_across
+
+    query_sent, pair_sent = project(tokens_other, groups, qwidth, BF16)
     pair_from, query_from = swap_x(pair_sent), swap_x(query_sent)
-    so_far = project(tokens_mine, groups_own)
-    query, pair = project(tokens_mine, groups_across, chips, qwidth, F32, so_far)
+    query, pair = project(tokens_mine, groups, qwidth, F32)
     pair = (pair + pair_from.astype(F32)).astype(BF16)
 
     doc_row, flag_row = doc_lengths[0], kept_flags[0]
@@ -340,17 +358,18 @@
     dpair = dpair.astype(BF16)
     dpair_other = swap_x(dpair)
 
-    groups = groups_own + groups_across
-    grad_sent = width_grad(dquery_other, dpair_other, groups)
+    grad_sent, after = width_grad(dquery_other, dpair_other, groups)
     grad_from = swap_x(grad_sent)
 
     half = chips * rest * width
-    left = [tokens_mine, tokens_other, swap_core(tokens_mine[:, half:]), swap_core(tokens_other[:, half:])]
-    right = [[mine, other, swap_core(mine), swap_core(other)] for mine, other in ((dquery, dquery_other), (dpair, dpair_other))]
+    across = [swap_core(part) for part in tokens_other]
+    left = [(tokens_mine, 0), (tokens_other, 0), ([swap_core(mine_across)], 0), (across, half)]
+    right = [[dquery, dpair], [dquery_other, dpair_other]]
+    right += [[swap_core(g) for g in group] for group in right]
     order = sorted(range(chips), key=lambda k: (k == 0, -min(k, chips - k), k))
-    weights_grad, after = None, grad_sent
+    parts = []
     for steps in (order[: chips // 2], order[chips // 2 :]):
-        terms = weight_terms(steps, rest, width, left, *right, after)
+        terms = weight_terms(steps, rest, width, left, right, after)
         after = terms[-1]
         for i, k in enumerate(steps):
             part, *sent = terms[i * rest : (i + 1) * rest]
@@ -358,9 +377,10 @@
                 part = part + shift_rest(piece, -j).astype(F32)
             if k:
                 part = shift_chip(part.astype(BF16), -k).astype(F32)
-            weights_grad = part if weights_grad is None else weights_grad + part
-
-    inputs_grad = merge_halves(width_grad(dquery, dpair, groups), grad_from, chips, rest, width)
+            parts.append(part)
+    weights_grad = functools.reduce(jnp.add, reversed(parts))
+
+    inputs_grad = merge_halves(width_grad(dquery, dpair, groups)[0], grad_from, chips, rest, width)
     return (attention[None], inputs_grad[None], weights_grad)
 
 

time: 122 us -> 107 us (0.88)
  waiting for transfers between devices: 53.6 us -> 42.6 us
  local copies, waits for them, and re-layouts: 3.86 us -> 0.07 us
    ppermute x7, waiting for transfers between devices: 19.9 us -> 6.88 us  [shift_rest(): return lax.ppermute(array, 'seq', pairs)]
    ppermute x6, starting transfers between devices: 16.6 us -> 11.6 us  [shift_chip(): return lax.ppermute(array, 'dp', pairs)]
    ppermute x6 -> x7, waiting for transfers between devices: 8.22 us -> 10.7 us  [swap_x(): return lax.ppermute(array, 'seq', [(i, i ^ 1) for i in range(count)])]
    ppermute x6 -> x7, starting transfers between devices: 9.84 us -> 11.9 us  [swap_x(): return lax.ppermute(array, 'seq', [(i, i ^ 1) for i in range(count)])]
    squeeze x1, local copies, waits for them, and re-layouts: 1.73 us -> 0.03 us  [shards(): lax.dynamic_index_in_dim(blocks, p, 0, keepdims=False)]
    ppermute x7, starting transfers between devices: 8.44 us -> 9.96 us  [shift_rest(): return lax.ppermute(array, 'seq', pairs)]
    pallas_call x7 -> x5, Pallas kernels: 7.36 us -> 7.26 us  [the longest x1 3.21 us: split_inputs(): pl.pallas_call(functools.partial(split_kernel, chips, rest, width), grid=...]
  transfers between devices with their start and end apart: 37 -> 39, of which waited for: 16 -> 19; matrix products, arithmetic and copies ran while one was open for 2% -> 1% of each run, Pallas kernels for 9% -> 11%
where the time goes in v6:
time: 107 us
  starting transfers between devices  44.4 us (41%)
  waiting for transfers between devices  42.6 us (40%)
  Pallas kernels  17.6 us (16%)
  other arithmetic  1.43 us (1%)
    ppermute x6, waiting for transfers between devices, shift_chip(): return lax.ppermute(array, 'dp', pairs)  17.7 us
    ppermute x7, starting transfers between devices, swap_x(): return lax.ppermute(array, 'seq', [(i, i ^ 1) for i in range(count)])  11.9 us
    ppermute x6, starting transfers between devices, shift_chip(): return lax.ppermute(array, 'dp', pairs)  11.6 us
    ppermute x7, waiting for transfers between devices, swap_x(): return lax.ppermute(array, 'seq', [(i, i ^ 1) for i in range(count)])  10.7 us
    ppermute x7, starting transfers between devices, shift_rest(): return lax.ppermute(array, 'seq', pairs)  9.96 us
    ppermute x4, starting transfers between devices, shift_seq(): return lax.ppermute(array, 'seq', pairs)  8.71 us
    ppermute x7, waiting for transfers between devices, shift_rest(): return lax.ppermute(array, 'seq', pairs)  6.88 us
    pallas_call x1, Pallas kernels, attend(): pl.pallas_call(functools.partial(attend_kernel, width // HEAD_DIM, back),...  6.31 us
  transfers between devices with their start and end apart: 39, of which 19 were waited for; matrix products, arithmetic and copies ran while one was open for 1% of the time, Pallas kernels for 11%

profile of v6, /device:TPU:0, one launch (start us, length us, event | category | flops | bytes accessed | tf_op | source)
XLA Modules:
  0.0 107.0 jit_solution(16668856449475878476)
XLA Ops:
  0.7 3.2 %split_inputs.1 = (bf16[256,1024]{1,0:T(8,128)(2,1)}, bf16[256,1024]{1,0:T(8,128)(2,1)}, bf16[256,1792]{1,0:T(8,128)(2,1)}, bf16[256,256]{1,0:T(8,128)(2,1)}, bf16[128,768]{1,0:T(8,128)(2,1)}) custom-call(bf16[256,4096]{1,0:T(8,128)(2,1)} %bitcast.22, bf16[512,768]{1,0:T(8,128)(2,1)} %weights_ref.1), custom_call_target="tpu_custom_call" | custom-call | tf_op jit(solution)/shard_map/split_inputs/pallas_call | solution.py:104
  3.9 3.1 %collective-permute-start.1 = (bf16[128,768]{1,0:T(8,128)(2,1)}, bf16[128,768]{1,0:T(8,128)(2,1)S(1)}, u32[]{:S(2)}, u32[]{:S(2)}) collective-permute-start(bf16[128,768]{1,0:T(8,128)(2,1)} %get-tuple-element.34), channel_id=1, source_target_pairs={{0,8},{4,12},{8,16},{12,20},{16,24},{20,28},{24,0},{28,4},{1,9},{5... | collective-permute-start | bytes 589832 | tf_op jit(solution)/shard_map/ppermute | solution.py:47
  7.0 2.1 %collective-permute-start.3 = (bf16[128,768]{1,0:T(8,128)(2,1)}, bf16[128,768]{1,0:T(8,128)(2,1)S(1)}, u32[]{:S(2)}, u32[]{:S(2)}) collective-permute-start(bf16[128,768]{1,0:T(8,128)(2,1)} %get-tuple-element.34), channel_id=1, source_target_pairs={{0,24},{4,28},{8,0},{12,4},{16,8},{20,12},{24,16},{28,20},{1,25},{... | collective-permute-start | bytes 589832 | tf_op jit(solution)/shard_map/ppermute | solution.py:47
  9.0 1.6 %collective-permute-start.14 = (bf16[256,1792]{1,0:T(8,128)(2,1)}, bf16[256,1792]{1,0:T(8,128)(2,1)S(1)}, u32[]{:S(2)}, u32[]{:S(2)}) collective-permute-start(bf16[256,1792]{1,0:T(8,128)(2,1)} %get-tuple-element.41), channel_id=1, source_target_pairs={{0,1},{1,0},{2,3},{3,2},{4,5},{5,4},{6,7},{7,6},{8,9},{9,8},{10,11... | collective-permute-start | bytes 2752520 | tf_op jit(solution)/shard_map/ppermute | solution.py:28
  10.7 0.8 collective-permute-start
  11.5 3.5 %collective-permute-done.1.refs_4_.refs_2_ = bf16[128,768]{1,0:T(8,128)(2,1)S(1)} collective-permute-done((bf16[128,768]{1,0:T(8,128)(2,1)}, bf16[128,768]{1,0:T(8,128)(2,1)S(1)}, u32[]{:S(2)}, u32[]{:S(2)}) %collective-permute-start.1) | collective-permute-done | bytes 196640 | tf_op jit(solution)/shard_map/ppermute | solution.py:47
  15.0 1.8 %collective-permute-start.2 = (bf16[128,768]{1,0:T(8,128)(2,1)S(1)}, bf16[128,768]{1,0:T(8,128)(2,1)S(1)}, u32[]{:S(2)}, u32[]{:S(2)}) collective-permute-start(bf16[128,768]{1,0:T(8,128)(2,1)S(1)} %collective-permute-done.1.refs_4_.refs_2_), channel_id=1, source_target_pairs={{0,2},{1,3},{2,0},{3,1},{4,6},{5,7},{6,4},{7,5},{8,10},{9,11},{10,... | collective-permute-start | bytes 589832 | tf_op jit(solution)/shard_map/ppermute | solution.py:35
  16.7 1.0 collective-permute-done.3.refs_8_.refs_6_
  17.7 1.5 %collective-permute-start.4 = (bf16[128,768]{1,0:T(8,128)(2,1)S(1)}, bf16[128,768]{1,0:T(8,128)(2,1)S(1)}, u32[]{:S(2)}, u32[]{:S(2)}) collective-permute-start(bf16[128,768]{1,0:T(8,128)(2,1)S(1)} %collective-permute-done.3.refs_8_.refs_6_), channel_id=1, source_target_pairs={{0,2},{1,3},{2,0},{3,1},{4,6},{5,7},{6,4},{7,5},{8,10},{9,11},{10,... | collective-permute-start | bytes 589832 | tf_op jit(solution)/shard_map/ppermute | solution.py:35
  19.4 7.4 %collective-permute-done.refs_6_.refs_4_ = bf16[128,768]{1,0:T(8,128)(2,1)S(1)} collective-permute-done((bf16[128,768]{1,0:T(8,128)(2,1)}, bf16[128,768]{1,0:T(8,128)(2,1)S(1)}, u32[]{:S(2)}, u32[]{:S(2)}) %collective-permute-start) | collective-permute-done | bytes 196640 | tf_op jit(solution)/shard_map/ppermute | solution.py:47
  26.7 1.5 %collective-permute-start.15 = (bf16[256,256]{1,0:T(8,128)(2,1)}, bf16[256,256]{1,0:T(8,128)(2,1)S(1)}, u32[]{:S(2)}, u32[]{:S(2)}) collective-permute-start(bf16[256,256]{1,0:T(8,128)(2,1)} %get-tuple-element.42), channel_id=1, source_target_pairs={{0,1},{1,0},{2,3},{3,2},{4,5},{5,4},{6,7},{7,6},{8,9},{9,8},{10,11... | collective-permute-start | bytes 393224 | tf_op jit(solution)/shard_map/ppermute | solution.py:28
  28.4 1.6 %collective-permute-start.5 = (bf16[128,768]{1,0:T(8,128)(2,1)S(1)}, bf16[128,768]{1,0:T(8,128)(2,1)S(1)}, u32[]{:S(2)}, u32[]{:S(2)}) collective-permute-start(bf16[128,768]{1,0:T(8,128)(2,1)S(1)} %collective-permute-done.refs_6_.refs_4_), channel_id=1, source_target_pairs={{0,2},{1,3},{2,0},{3,1},{4,6},{5,7},{6,4},{7,5},{8,10},{9,11},{10,... | collective-permute-start | bytes 589832 | tf_op jit(solution)/shard_map/ppermute | solution.py:35
  30.0 3.9 %collective-permute-done.15.refs_1_.refs_3_ = bf16[256,256]{1,0:T(8,128)(2,1)S(1)} collective-permute-done((bf16[256,256]{1,0:T(8,128)(2,1)}, bf16[256,256]{1,0:T(8,128)(2,1)S(1)}, u32[]{:S(2)}, u32[]{:S(2)}) %collective-permute-start.15) | collective-permute-done | bytes 131104 | tf_op jit(solution)/shard_map/ppermute | solution.py:28
  34.5 1.3 %collective-permute-done.5.refs_7_.refs_5_ = bf16[128,768]{1,0:T(8,128)(2,1)S(1)} collective-permute-done((bf16[128,768]{1,0:T(8,128)(2,1)S(1)}, bf16[128,768]{1,0:T(8,128)(2,1)S(1)}, u32[]{:S(2)}, u32[]{:S(2)}) %collective-permute-start.5) | collective-permute-done | bytes 196640 | tf_op jit(solution)/shard_map/ppermute | solution.py:35
  37.7 1.0 project.3
  38.7 0.8 collective-permute-start.17
  39.6 1.0 project.2
  40.6 1.3 %collective-permute-start.16 = (bf16[256,512]{1,0:T(8,128)(2,1)S(1)}, bf16[256,512]{1,0:T(8,128)(2,1)S(1)}, u32[]{:S(2)}, u32[]{:S(2)}) collective-permute-start(bf16[256,512]{1,0:T(8,128)(2,1)S(1)} %get-tuple-element.43), channel_id=1, source_target_pairs={{0,1},{1,0},{2,3},{3,2},{4,5},{5,4},{6,7},{7,6},{8,9},{9,8},{10,11... | collective-permute-start | bytes 786440 | tf_op jit(solution)/shard_map/ppermute | solution.py:28
  41.9 3.2 %collective-permute-done.17 = bf16[256,256]{1,0:T(8,128)(2,1)S(1)} collective-permute-done((bf16[256,256]{1,0:T(8,128)(2,1)S(1)}, bf16[256,256]{1,0:T(8,128)(2,1)S(1)}, u32[]{:S(2)}, u32[]{:S(2)}) %collective-permute-start.17) | collective-permute-done | bytes 131104 | tf_op jit(solution)/shard_map/ppermute | solution.py:28
  45.2 3.4 %collective-permute-start.18 = (bf16[256,256]{1,0:T(8,128)(2,1)S(1)}, bf16[256,256]{1,0:T(8,128)(2,1)S(1)}, u32[]{:S(2)}, u32[]{:S(2)}) collective-permute-start(bf16[256,256]{1,0:T(8,128)(2,1)S(1)} %add_convert_fusion.4.refs_2_), channel_id=1, source_target_pairs={{0,2},{1,3},{4,6},{5,7},{8,10},{9,11},{12,14},{13,15},{16,18},{17,... | collective-permute-start | bytes 393224 | tf_op jit(solution)/shard_map/ppermute | solution.py:53
  48.6 2.7 %collective-permute-start.19 = (bf16[256,256]{1,0:T(8,128)(2,1)S(1)}, bf16[256,256]{1,0:T(8,128)(2,1)S(1)}, u32[]{:S(2)}, u32[]{:S(2)}) collective-permute-start(bf16[256,256]{1,0:T(8,128)(2,1)S(1)} %add_convert_fusion.4.refs_2_), channel_id=1, source_target_pairs={{0,1},{1,2},{2,3},{4,5},{5,6},{6,7},{8,9},{9,10},{10,11},{12,13},{... | collective-permute-start | bytes 393224 | tf_op jit(solution)/shard_map/ppermute | solution.py:53
  51.4 2.4 %collective-permute-done.18.refs_0_ = bf16[256,256]{1,0:T(8,128)(2,1)S(1)} collective-permute-done((bf16[256,256]{1,0:T(8,128)(2,1)S(1)}, bf16[256,256]{1,0:T(8,128)(2,1)S(1)}, u32[]{:S(2)}, u32[]{:S(2)}) %collective-permute-start.18) | collective-permute-done | bytes 131104 | tf_op jit(solution)/shard_map/ppermute | solution.py:53
  53.9 6.3 %attend.1 = (bf16[256,512]{1,0:T(8,128)(2,1)}, bf16[256,512]{1,0:T(8,128)(2,1)S(1)}, f32[256,256]{1,0:T(8,128)S(1)}, bf16[512,256]{1,0:T(8,128)(2,1)S(1)}) custom-call(s32[8]{0:T(128)S(1)} %bitcast.21, f32[256,512]{1,0:T(8,128)S(1)} %get-tuple-element.40.q_ref, bf16[256,512]{1,0:T(8,128)(2,1)S(1)} %collective-permute-done.16.q_from_ref, ...), custom_call_target="tpu_custom_call" | custom-call | tf_op jit(solution)/shard_map/attend/pallas_call | solution.py:291
  60.2 1.3 %collective-permute-start.21 = (bf16[256,256]{1,0:T(8,128)(2,1)S(1)}, bf16[256,256]{1,0:T(8,128)(2,1)S(1)}, u32[]{:S(2)}, u32[]{:S(2)}) collective-permute-start(bf16[256,256]{1,0:T(8,128)(2,1)S(1)} %get-tuple-element.64), channel_id=1, source_target_pairs={{2,0},{3,1},{6,4},{7,5},{10,8},{11,9},{14,12},{15,13},{18,16},{19,... | collective-permute-start | bytes 393224 | tf_op jit(solution)/shard_map/ppermute | solution.py:53
  61.5 1.3 %collective-permute-start.20 = (bf16[256,256]{1,0:T(8,128)(2,1)S(1)}, bf16[256,256]{1,0:T(8,128)(2,1)S(1)}, u32[]{:S(2)}, u32[]{:S(2)}) collective-permute-start(bf16[256,256]{1,0:T(8,128)(2,1)S(1)} %get-tuple-element.63), channel_id=1, source_target_pairs={{1,0},{2,1},{3,2},{5,4},{6,5},{7,6},{9,8},{10,9},{11,10},{13,12},{... | collective-permute-start | bytes 393224 | tf_op jit(solution)/shard_map/ppermute | solution.py:53
  62.8 3.1 %collective-permute-start.22 = (bf16[256,512]{1,0:T(8,128)(2,1)S(1)}, bf16[256,512]{1,0:T(8,128)(2,1)S(1)}, u32[]{:S(2)}, u32[]{:S(2)}) collective-permute-start(bf16[256,512]{1,0:T(8,128)(2,1)S(1)} %get-tuple-element.47.dquery_ref.refs_7_), channel_id=1, source_target_pairs={{0,1},{1,0},{2,3},{3,2},{4,5},{5,4},{6,7},{7,6},{8,9},{9,8},{10,11... | collective-permute-start | bytes 786440 | tf_op jit(solution)/shard_map/ppermute | solution.py:28
  65.9 1.2 %collective-permute-done.21 = bf16[256,256]{1,0:T(8,128)(2,1)S(1)} collective-permute-done((bf16[256,256]{1,0:T(8,128)(2,1)S(1)}, bf16[256,256]{1,0:T(8,128)(2,1)S(1)}, u32[]{:S(2)}, u32[]{:S(2)}) %collective-permute-start.21) | collective-permute-done | bytes 131104 | tf_op jit(solution)/shard_map/ppermute | solution.py:53
  67.1 2.5 %collective-permute-done.20 = bf16[256,256]{1,0:T(8,128)(2,1)S(1)} collective-permute-done((bf16[256,256]{1,0:T(8,128)(2,1)S(1)}, bf16[256,256]{1,0:T(8,128)(2,1)S(1)}, u32[]{:S(2)}, u32[]{:S(2)}) %collective-permute-start.20) | collective-permute-done | bytes 131104 | tf_op jit(solution)/shard_map/ppermute | solution.py:53
  69.6 2.7 %collective-permute-start.23 = (bf16[256,256]{1,0:T(8,128)(2,1)S(1)}, bf16[256,256]{1,0:T(8,128)(2,1)S(1)}, u32[]{:S(2)}, u32[]{:S(2)}) collective-permute-start(bf16[256,256]{1,0:T(8,128)(2,1)S(1)} %add_convert_fusion.3.dpair_ref.refs_8_), channel_id=1, source_target_pairs={{0,1},{1,0},{2,3},{3,2},{4,5},{5,4},{6,7},{7,6},{8,9},{9,8},{10,11... | collective-permute-start | bytes 393224 | tf_op jit(solution)/shard_map/ppermute | solution.py:28
  72.9 3.6 %collective-permute-done.23.dpair_ref.refs_10_ = bf16[256,256]{1,0:T(8,128)(2,1)S(1)} collective-permute-done((bf16[256,256]{1,0:T(8,128)(2,1)S(1)}, bf16[256,256]{1,0:T(8,128)(2,1)S(1)}, u32[]{:S(2)}, u32[]{:S(2)}) %collective-permute-start.23) | collective-permute-done | bytes 131104 | tf_op jit(solution)/shard_map/ppermute | solution.py:28
  76.5 1.0 width_grad.3
  77.8 1.0 weight_terms.2
  78.9 1.1 %collective-permute-start.37 = (bf16[128,768]{1,0:T(8,128)(2,1)S(1)}, bf16[128,768]{1,0:T(8,128)(2,1)S(1)}, u32[]{:S(2)}, u32[]{:S(2)}) collective-permute-start(bf16[128,768]{1,0:T(8,128)(2,1)S(1)} %get-tuple-element.60), channel_id=1, source_target_pairs={{0,2},{1,3},{2,0},{3,1},{4,6},{5,7},{6,4},{7,5},{8,10},{9,11},{10,... | collective-permute-start | bytes 589832 | tf_op jit(solution)/shard_map/ppermute | solution.py:35
  80.0 0.8 collective-permute-start.24
  80.8 1.9 %collective-permute-start.35 = (bf16[128,768]{1,0:T(8,128)(2,1)S(1)}, bf16[128,768]{1,0:T(8,128)(2,1)S(1)}, u32[]{:S(2)}, u32[]{:S(2)}) collective-permute-start(bf16[128,768]{1,0:T(8,128)(2,1)S(1)} %get-tuple-element.53.refs_15_), channel_id=1, source_target_pairs={{0,2},{1,3},{2,0},{3,1},{4,6},{5,7},{6,4},{7,5},{8,10},{9,11},{10,... | collective-permute-start | bytes 589832 | tf_op jit(solution)/shard_map/ppermute | solution.py:35
  82.7 1.0 weight_terms.3
  84.0 1.9 %collective-permute-start.32 = (bf16[128,768]{1,0:T(8,128)(2,1)S(1)}, bf16[128,768]{1,0:T(8,128)(2,1)S(1)}, u32[]{:S(2)}, u32[]{:S(2)}) collective-permute-start(bf16[128,768]{1,0:T(8,128)(2,1)S(1)} %get-tuple-element.55), channel_id=1, source_target_pairs={{0,2},{1,3},{2,0},{3,1},{4,6},{5,7},{6,4},{7,5},{8,10},{9,11},{10,... | collective-permute-start | bytes 589832 | tf_op jit(solution)/shard_map/ppermute | solution.py:35
  85.8 0.8 collective-permute-done.37
  86.7 2.9 %collective-permute-start.38 = (bf16[128,768]{1,0:T(8,128)(2,1)S(1)}, bf16[128,768]{1,0:T(8,128)(2,1)S(1)}, u32[]{:S(2)}, u32[]{:S(2)}) collective-permute-start(bf16[128,768]{1,0:T(8,128)(2,1)S(1)} %add_convert_fusion), channel_id=1, source_target_pairs={{0,16},{4,20},{8,24},{12,28},{16,0},{20,4},{24,8},{28,12},{1,17},{... | collective-permute-start | bytes 589832 | tf_op jit(solution)/shard_map/ppermute | solution.py:47
  89.6 1.3 %collective-permute-done.35 = bf16[128,768]{1,0:T(8,128)(2,1)S(1)} collective-permute-done((bf16[128,768]{1,0:T(8,128)(2,1)S(1)}, bf16[128,768]{1,0:T(8,128)(2,1)S(1)}, u32[]{:S(2)}, u32[]{:S(2)}) %collective-permute-start.35) | collective-permute-done | bytes 196640 | tf_op jit(solution)/shard_map/ppermute | solution.py:35
  90.9 1.7 %collective-permute-start.36 = (bf16[128,768]{1,0:T(8,128)(2,1)S(1)}, bf16[128,768]{1,0:T(8,128)(2,1)S(1)}, u32[]{:S(2)}, u32[]{:S(2)}) collective-permute-start(bf16[128,768]{1,0:T(8,128)(2,1)S(1)} %add_convert_fusion.1), channel_id=1, source_target_pairs={{0,24},{4,28},{8,0},{12,4},{16,8},{20,12},{24,16},{28,20},{1,25},{... | collective-permute-start | bytes 589832 | tf_op jit(solution)/shard_map/ppermute | solution.py:47
  92.7 2.4 %collective-permute-done.33 = bf16[128,768]{1,0:T(8,128)(2,1)S(1)} collective-permute-done((bf16[128,768]{1,0:T(8,128)(2,1)S(1)}, bf16[128,768]{1,0:T(8,128)(2,1)S(1)}, u32[]{:S(2)}, u32[]{:S(2)}) %collective-permute-start.33) | collective-permute-done | bytes 196640 | tf_op jit(solution)/shard_map/ppermute | solution.py:35
  95.2 1.0 collective-permute-start.34
  96.2 1.4 %width_grad.2 = (bf16[256,2048]{1,0:T(8,128)(2,1)S(1)}, bf16[16,128]{1,0:T(8,128)(2,1)}) custom-call(bf16[256,512]{1,0:T(8,128)(2,1)S(1)} %get-tuple-element.47.dquery_ref.refs_7_, bf16[256,256]{1,0:T(8,128)(2,1)S(1)} %add_convert_fusion.3.dpair_ref.refs_8_, bf16[128,768]{1,0:T(8,128)(2,1)S(1)} %get-tuple-element.62.refs_2_.refs_0_, ...), custom_call_target="tpu_custom_call" | custom-call | tf_op jit(solution)/shard_map/width_grad/pallas_call | solution.py:196
  97.6 1.0 collective-permute-done.32
  98.6 5.9 %collective-permute-done.36 = bf16[128,768]{1,0:T(8,128)(2,1)S(1)} collective-permute-done((bf16[128,768]{1,0:T(8,128)(2,1)S(1)}, bf16[128,768]{1,0:T(8,128)(2,1)S(1)}, u32[]{:S(2)}, u32[]{:S(2)}) %collective-permute-start.36) | collective-permute-done | bytes 196640 | tf_op jit(solution)/shard_map/ppermute | solution.py:47
  104.5 0.9 convert_add_fusion
  105.4 1.6 %merge_halves.1 = bf16[256,4096]{1,0:T(8,128)(2,1)} custom-call(bf16[256,2048]{1,0:T(8,128)(2,1)S(1)} %get-tuple-element.50.mine_ref, bf16[256,2048]{1,0:T(8,128)(2,1)S(1)} %collective-permute-done.24.other_ref), custom_call_target="tpu_custom_call" | custom-call | tf_op jit(solution)/shard_map/merge_halves/pallas_call | solution.py:139
  (65 shorter events, 4.3 us)
Async XLA Ops:
  0.6 18.6 %copy-start.3 = (bf16[512,768]{1,0:T(8,128)(2,1)S(1)}, bf16[512,768]{1,0:T(8,128)(2,1)}, u32[]{:S(2)}) copy-start(bf16[512,768]{1,0:T(8,128)(2,1)} %weights_ref.1) | copy-start | bytes 2359300
  0.6 27.6 %copy-start.2 = (s32[1,8]{1,0:T(1,128)S(1)}, s32[1,8]{1,0:T(1,128)}, u32[]{:S(2)}) copy-start(s32[1,8]{1,0:T(1,128)} %param.8) | copy-start | bytes 100
  0.7 35.7 %copy-start.5 = (s32[1,8]{1,0:T(1,128)S(1)}, s32[1,8]{1,0:T(1,128)}, u32[]{:S(2)}) copy-start(s32[1,8]{1,0:T(1,128)} %param.9) | copy-start | bytes 100
  3.9 11.1 %collective-permute-start.1 = (bf16[128,768]{1,0:T(8,128)(2,1)}, bf16[128,768]{1,0:T(8,128)(2,1)S(1)}, u32[]{:S(2)}, u32[]{:S(2)}) collective-permute-start(bf16[128,768]{1,0:T(8,128)(2,1)} %get-tuple-element.34), channel_id=1, source_target_pairs={{0,8},{4,12},{8,16},{12,20},{16,24},{20,28},{24,0},{28,4},{1,9},{5... | collective-permute-start | bytes 589832 | tf_op jit(solution)/shard_map/ppermute | solution.py:47
  7.0 10.8 %collective-permute-start.3 = (bf16[128,768]{1,0:T(8,128)(2,1)}, bf16[128,768]{1,0:T(8,128)(2,1)S(1)}, u32[]{:S(2)}, u32[]{:S(2)}) collective-permute-start(bf16[128,768]{1,0:T(8,128)(2,1)} %get-tuple-element.34), channel_id=1, source_target_pairs={{0,24},{4,28},{8,0},{12,4},{16,8},{20,12},{24,16},{28,20},{1,25},{... | collective-permute-start | bytes 589832 | tf_op jit(solution)/shard_map/ppermute | solution.py:47
  9.0 28.7 %collective-permute-start.14 = (bf16[256,1792]{1,0:T(8,128)(2,1)}, bf16[256,1792]{1,0:T(8,128)(2,1)S(1)}, u32[]{:S(2)}, u32[]{:S(2)}) collective-permute-start(bf16[256,1792]{1,0:T(8,128)(2,1)} %get-tuple-element.41), channel_id=1, source_target_pairs={{0,1},{1,0},{2,3},{3,2},{4,5},{5,4},{6,7},{7,6},{8,9},{9,8},{10,11... | collective-permute-start | bytes 2752520 | tf_op jit(solution)/shard_map/ppermute | solution.py:28
  10.7 16.0 %collective-permute-start = (bf16[128,768]{1,0:T(8,128)(2,1)}, bf16[128,768]{1,0:T(8,128)(2,1)S(1)}, u32[]{:S(2)}, u32[]{:S(2)}) collective-permute-start(bf16[128,768]{1,0:T(8,128)(2,1)} %get-tuple-element.34), channel_id=1, source_target_pairs={{0,16},{4,20},{8,24},{12,28},{16,0},{20,4},{24,8},{28,12},{1,17},{... | collective-permute-start | bytes 589832 | tf_op jit(solution)/shard_map/ppermute | solution.py:47
  15.0 13.4 %collective-permute-start.2 = (bf16[128,768]{1,0:T(8,128)(2,1)S(1)}, bf16[128,768]{1,0:T(8,128)(2,1)S(1)}, u32[]{:S(2)}, u32[]{:S(2)}) collective-permute-start(bf16[128,768]{1,0:T(8,128)(2,1)S(1)} %collective-permute-done.1.refs_4_.refs_2_), channel_id=1, source_target_pairs={{0,2},{1,3},{2,0},{3,1},{4,6},{5,7},{6,4},{7,5},{8,10},{9,11},{10,... | collective-permute-start | bytes 589832 | tf_op jit(solution)/shard_map/ppermute | solution.py:35
  17.7 10.7 %collective-permute-start.4 = (bf16[128,768]{1,0:T(8,128)(2,1)S(1)}, bf16[128,768]{1,0:T(8,128)(2,1)S(1)}, u32[]{:S(2)}, u32[]{:S(2)}) collective-permute-start(bf16[128,768]{1,0:T(8,128)(2,1)S(1)} %collective-permute-done.3.refs_8_.refs_6_), channel_id=1, source_target_pairs={{0,2},{1,3},{2,0},{3,1},{4,6},{5,7},{6,4},{7,5},{8,10},{9,11},{10,... | collective-permute-start | bytes 589832 | tf_op jit(solution)/shard_map/ppermute | solution.py:35
  19.3 14.6 %collective-permute-start.6 = (bf16[128,768]{1,0:T(8,128)(2,1)S(1)}, bf16[128,768]{1,0:T(8,128)(2,1)S(1)}, u32[]{:S(2)}, u32[]{:S(2)}) collective-permute-start(bf16[128,768]{1,0:T(8,128)(2,1)S(1)} %get-tuple-element.62.refs_2_.refs_0_), channel_id=1, source_target_pairs={{0,4},{4,0},{8,12},{12,8},{16,20},{20,16},{24,28},{28,24},{1,5},{5... | collective-permute-start | bytes 589832 | tf_op jit(solution)/shard_map/ppermute | solution.py:40
  26.7 7.1 %collective-permute-start.15 = (bf16[256,256]{1,0:T(8,128)(2,1)}, bf16[256,256]{1,0:T(8,128)(2,1)S(1)}, u32[]{:S(2)}, u32[]{:S(2)}) collective-permute-start(bf16[256,256]{1,0:T(8,128)(2,1)} %get-tuple-element.42), channel_id=1, source_target_pairs={{0,1},{1,0},{2,3},{3,2},{4,5},{5,4},{6,7},{7,6},{8,9},{9,8},{10,11... | collective-permute-start | bytes 393224 | tf_op jit(solution)/shard_map/ppermute | solution.py:28
  28.4 6.0 %collective-permute-start.7 = (bf16[128,768]{1,0:T(8,128)(2,1)S(1)}, bf16[128,768]{1,0:T(8,128)(2,1)S(1)}, u32[]{:S(2)}, u32[]{:S(2)}) collective-permute-start(bf16[128,768]{1,0:T(8,128)(2,1)S(1)} %get-tuple-element.61.refs_3_.refs_1_), channel_id=1, source_target_pairs={{0,4},{4,0},{8,12},{12,8},{16,20},{20,16},{24,28},{28,24},{1,5},{5... | collective-permute-start | bytes 589832 | tf_op jit(solution)/shard_map/ppermute | solution.py:40
  28.4 7.3 %collective-permute-start.5 = (bf16[128,768]{1,0:T(8,128)(2,1)S(1)}, bf16[128,768]{1,0:T(8,128)(2,1)S(1)}, u32[]{:S(2)}, u32[]{:S(2)}) collective-permute-start(bf16[128,768]{1,0:T(8,128)(2,1)S(1)} %collective-permute-done.refs_6_.refs_4_), channel_id=1, source_target_pairs={{0,2},{1,3},{2,0},{3,1},{4,6},{5,7},{6,4},{7,5},{8,10},{9,11},{10,... | collective-permute-start | bytes 589832 | tf_op jit(solution)/shard_map/ppermute | solution.py:35
  33.9 1.9 %collective-permute-start.8 = (bf16[128,768]{1,0:T(8,128)(2,1)S(1)}, bf16[128,768]{1,0:T(8,128)(2,1)S(1)}, u32[]{:S(2)}, u32[]{:S(2)}) collective-permute-start(bf16[128,768]{1,0:T(8,128)(2,1)S(1)} %collective-permute-done.1.refs_4_.refs_2_), channel_id=1, source_target_pairs={{0,4},{4,0},{8,12},{12,8},{16,20},{20,16},{24,28},{28,24},{1,5},{5... | collective-permute-start | bytes 589832 | tf_op jit(solution)/shard_map/ppermute | solution.py:40
  33.9 2.4 %collective-permute-start.9 = (bf16[128,768]{1,0:T(8,128)(2,1)S(1)}, bf16[128,768]{1,0:T(8,128)(2,1)S(1)}, u32[]{:S(2)}, u32[]{:S(2)}) collective-permute-start(bf16[128,768]{1,0:T(8,128)(2,1)S(1)} %collective-permute-done.2.refs_5_.refs_3_), channel_id=1, source_target_pairs={{0,4},{4,0},{8,12},{12,8},{16,20},{20,16},{24,28},{28,24},{1,5},{5... | collective-permute-start | bytes 589832 | tf_op jit(solution)/shard_map/ppermute | solution.py:40
  34.4 2.0 %collective-permute-start.10 = (bf16[128,768]{1,0:T(8,128)(2,1)S(1)}, bf16[128,768]{1,0:T(8,128)(2,1)S(1)}, u32[]{:S(2)}, u32[]{:S(2)}) collective-permute-start(bf16[128,768]{1,0:T(8,128)(2,1)S(1)} %collective-permute-done.refs_6_.refs_4_), channel_id=1, source_target_pairs={{0,4},{4,0},{8,12},{12,8},{16,20},{20,16},{24,28},{28,24},{1,5},{5... | collective-permute-start | bytes 589832 | tf_op jit(solution)/shard_map/ppermute | solution.py:40
  35.7 1.4 %collective-permute-start.12 = (bf16[128,768]{1,0:T(8,128)(2,1)S(1)}, bf16[128,768]{1,0:T(8,128)(2,1)S(1)}, u32[]{:S(2)}, u32[]{:S(2)}) collective-permute-start(bf16[128,768]{1,0:T(8,128)(2,1)S(1)} %collective-permute-done.3.refs_8_.refs_6_), channel_id=1, source_target_pairs={{0,4},{4,0},{8,12},{12,8},{16,20},{20,16},{24,28},{28,24},{1,5},{5... | collective-permute-start | bytes 589832 | tf_op jit(solution)/shard_map/ppermute | solution.py:40
  35.7 1.7 %collective-permute-start.13 = (bf16[128,768]{1,0:T(8,128)(2,1)S(1)}, bf16[128,768]{1,0:T(8,128)(2,1)S(1)}, u32[]{:S(2)}, u32[]{:S(2)}) collective-permute-start(bf16[128,768]{1,0:T(8,128)(2,1)S(1)} %collective-permute-done.4.refs_9_.refs_7_), channel_id=1, source_target_pairs={{0,4},{4,0},{8,12},{12,8},{16,20},{20,16},{24,28},{28,24},{1,5},{5... | collective-permute-start | bytes 589832 | tf_op jit(solution)/shard_map/ppermute | solution.py:40
  36.3 1.5 %collective-permute-start.11 = (bf16[128,768]{1,0:T(8,128)(2,1)S(1)}, bf16[128,768]{1,0:T(8,128)(2,1)S(1)}, u32[]{:S(2)}, u32[]{:S(2)}) collective-permute-start(bf16[128,768]{1,0:T(8,128)(2,1)S(1)} %collective-permute-done.5.refs_7_.refs_5_), channel_id=1, source_target_pairs={{0,4},{4,0},{8,12},{12,8},{16,20},{20,16},{24,28},{28,24},{1,5},{5... | collective-permute-start | bytes 589832 | tf_op jit(solution)/shard_map/ppermute | solution.py:40
  36.4 3.2 %copy-start = (bf16[256,1024]{1,0:T(8,128)(2,1)S(1)}, bf16[256,1024]{1,0:T(8,128)(2,1)}, u32[]{:S(2)}) copy-start(bf16[256,1024]{1,0:T(8,128)(2,1)} %get-tuple-element.32.refs_0_) | copy-start | bytes 1572868
  36.4 3.2 %copy-start.1 = (bf16[256,1024]{1,0:T(8,128)(2,1)S(1)}, bf16[256,1024]{1,0:T(8,128)(2,1)}, u32[]{:S(2)}) copy-start(bf16[256,1024]{1,0:T(8,128)(2,1)} %get-tuple-element.33.refs_1_) | copy-start | bytes 1572868
  36.4 36.1 %collective-permute-start.25 = (bf16[256,1024]{1,0:T(8,128)(2,1)}, bf16[256,1024]{1,0:T(8,128)(2,1)S(1)}, u32[]{:S(2)}, u32[]{:S(2)}) collective-permute-start(bf16[256,1024]{1,0:T(8,128)(2,1)} %get-tuple-element.33.refs_1_), channel_id=1, source_target_pairs={{0,4},{4,0},{8,12},{12,8},{16,20},{20,16},{24,28},{28,24},{1,5},{5... | collective-permute-start | bytes 1572872 | tf_op jit(solution)/shard_map/ppermute | solution.py:40
  38.7 6.4 %collective-permute-start.17 = (bf16[256,256]{1,0:T(8,128)(2,1)S(1)}, bf16[256,256]{1,0:T(8,128)(2,1)S(1)}, u32[]{:S(2)}, u32[]{:S(2)}) collective-permute-start(bf16[256,256]{1,0:T(8,128)(2,1)S(1)} %get-tuple-element.45), channel_id=1, source_target_pairs={{0,1},{1,0},{2,3},{3,2},{4,5},{5,4},{6,7},{7,6},{8,9},{9,8},{10,11... | collective-permute-start | bytes 393224 | tf_op jit(solution)/shard_map/ppermute | solution.py:28
  39.6 11.7 %copy-start.4 = (bf16[1,256,512]{2,1,0:T(8,128)(2,1)S(1)}, bf16[1,256,512]{2,1,0:T(8,128)(2,1)}, u32[]{:S(2)}) copy-start(bf16[1,256,512]{2,1,0:T(8,128)(2,1)} %param.7) | copy-start | bytes 786436
  40.6 13.3 %collective-permute-start.16 = (bf16[256,512]{1,0:T(8,128)(2,1)S(1)}, bf16[256,512]{1,0:T(8,128)(2,1)S(1)}, u32[]{:S(2)}, u32[]{:S(2)}) collective-permute-start(bf16[256,512]{1,0:T(8,128)(2,1)S(1)} %get-tuple-element.43), channel_id=1, source_target_pairs={{0,1},{1,0},{2,3},{3,2},{4,5},{5,4},{6,7},{7,6},{8,9},{9,8},{10,11... | collective-permute-start | bytes 786440 | tf_op jit(solution)/shard_map/ppermute | solution.py:28
  41.9 35.9 %collective-permute-start.26 = (bf16[256,1792]{1,0:T(8,128)(2,1)S(1)}, bf16[256,1792]{1,0:T(8,128)(2,1)S(1)}, u32[]{:S(2)}, u32[]{:S(2)}) collective-permute-start(bf16[256,1792]{1,0:T(8,128)(2,1)S(1)} %collective-permute-done.14.refs_0_.refs_2_), channel_id=1, source_target_pairs={{0,4},{4,0},{8,12},{12,8},{16,20},{20,16},{24,28},{28,24},{1,5},{5... | collective-permute-start | bytes 2752520 | tf_op jit(solution)/shard_map/ppermute | solution.py:40
  45.2 8.7 %collective-permute-start.18 = (bf16[256,256]{1,0:T(8,128)(2,1)S(1)}, bf16[256,256]{1,0:T(8,128)(2,1)S(1)}, u32[]{:S(2)}, u32[]{:S(2)}) collective-permute-start(bf16[256,256]{1,0:T(8,128)(2,1)S(1)} %add_convert_fusion.4.refs_2_), channel_id=1, source_target_pairs={{0,2},{1,3},{4,6},{5,7},{8,10},{9,11},{12,14},{13,15},{16,18},{17,... | collective-permute-start | bytes 393224 | tf_op jit(solution)/shard_map/ppermute | solution.py:53
  48.6 5.3 %collective-permute-start.19 = (bf16[256,256]{1,0:T(8,128)(2,1)S(1)}, bf16[256,256]{1,0:T(8,128)(2,1)S(1)}, u32[]{:S(2)}, u32[]{:S(2)}) collective-permute-start(bf16[256,256]{1,0:T(8,128)(2,1)S(1)} %add_convert_fusion.4.refs_2_), channel_id=1, source_target_pairs={{0,1},{1,2},{2,3},{4,5},{5,6},{6,7},{8,9},{9,10},{10,11},{12,13},{... | collective-permute-start | bytes 393224 | tf_op jit(solution)/shard_map/ppermute | solution.py:53
  60.2 6.9 %collective-permute-start.21 = (bf16[256,256]{1,0:T(8,128)(2,1)S(1)}, bf16[256,256]{1,0:T(8,128)(2,1)S(1)}, u32[]{:S(2)}, u32[]{:S(2)}) collective-permute-start(bf16[256,256]{1,0:T(8,128)(2,1)S(1)} %get-tuple-element.64), channel_id=1, source_target_pairs={{2,0},{3,1},{6,4},{7,5},{10,8},{11,9},{14,12},{15,13},{18,16},{19,... | collective-permute-start | bytes 393224 | tf_op jit(solution)/shard_map/ppermute | solution.py:53
  61.5 8.0 %collective-permute-start.20 = (bf16[256,256]{1,0:T(8,128)(2,1)S(1)}, bf16[256,256]{1,0:T(8,128)(2,1)S(1)}, u32[]{:S(2)}, u32[]{:S(2)}) collective-permute-start(bf16[256,256]{1,0:T(8,128)(2,1)S(1)} %get-tuple-element.63), channel_id=1, source_target_pairs={{1,0},{2,1},{3,2},{5,4},{6,5},{7,6},{9,8},{10,9},{11,10},{13,12},{... | collective-permute-start | bytes 393224 | tf_op jit(solution)/shard_map/ppermute | solution.py:53
  62.8 9.6 %collective-permute-start.22 = (bf16[256,512]{1,0:T(8,128)(2,1)S(1)}, bf16[256,512]{1,0:T(8,128)(2,1)S(1)}, u32[]{:S(2)}, u32[]{:S(2)}) collective-permute-start(bf16[256,512]{1,0:T(8,128)(2,1)S(1)} %get-tuple-element.47.dquery_ref.refs_7_), channel_id=1, source_target_pairs={{0,1},{1,0},{2,3},{3,2},{4,5},{5,4},{6,7},{7,6},{8,9},{9,8},{10,11... | collective-permute-start | bytes 786440 | tf_op jit(solution)/shard_map/ppermute | solution.py:28
  67.1 2.5 %collective-permute-start.27 = (bf16[256,256]{1,0:T(8,128)(2,1)S(1)}, bf16[256,256]{1,0:T(8,128)(2,1)S(1)}, u32[]{:S(2)}, u32[]{:S(2)}) collective-permute-start(bf16[256,256]{1,0:T(8,128)(2,1)S(1)} %collective-permute-done.15.refs_1_.refs_3_), channel_id=1, source_target_pairs={{0,4},{4,0},{8,12},{12,8},{16,20},{20,16},{24,28},{28,24},{1,5},{5... | collective-permute-start | bytes 393224 | tf_op jit(solution)/shard_map/ppermute | solution.py:40
  69.5 8.0 %collective-permute-start.28 = (bf16[256,512]{1,0:T(8,128)(2,1)S(1)}, bf16[256,512]{1,0:T(8,128)(2,1)S(1)}, u32[]{:S(2)}, u32[]{:S(2)}) collective-permute-start(bf16[256,512]{1,0:T(8,128)(2,1)S(1)} %get-tuple-element.47.dquery_ref.refs_7_), channel_id=1, source_target_pairs={{0,4},{4,0},{8,12},{12,8},{16,20},{20,16},{24,28},{28,24},{1,5},{5... | collective-permute-start | bytes 786440 | tf_op jit(solution)/shard_map/ppermute | solution.py:40
  69.6 6.9 %collective-permute-start.23 = (bf16[256,256]{1,0:T(8,128)(2,1)S(1)}, bf16[256,256]{1,0:T(8,128)(2,1)S(1)}, u32[]{:S(2)}, u32[]{:S(2)}) collective-permute-start(bf16[256,256]{1,0:T(8,128)(2,1)S(1)} %add_convert_fusion.3.dpair_ref.refs_8_), channel_id=1, source_target_pairs={{0,1},{1,0},{2,3},{3,2},{4,5},{5,4},{6,7},{7,6},{8,9},{9,8},{10,11... | collective-permute-start | bytes 393224 | tf_op jit(solution)/shard_map/ppermute | solution.py:28
  72.4 5.5 %collective-permute-start.30 = (bf16[256,512]{1,0:T(8,128)(2,1)S(1)}, bf16[256,512]{1,0:T(8,128)(2,1)S(1)}, u32[]{:S(2)}, u32[]{:S(2)}) collective-permute-start(bf16[256,512]{1,0:T(8,128)(2,1)S(1)} %collective-permute-done.22.dquery_ref.refs_9_), channel_id=1, source_target_pairs={{0,4},{4,0},{8,12},{12,8},{16,20},{20,16},{24,28},{28,24},{1,5},{5... | collective-permute-start | bytes 786440 | tf_op jit(solution)/shard_map/ppermute | solution.py:40
  72.5 5.0 %collective-permute-start.29 = (bf16[256,256]{1,0:T(8,128)(2,1)S(1)}, bf16[256,256]{1,0:T(8,128)(2,1)S(1)}, u32[]{:S(2)}, u32[]{:S(2)}) collective-permute-start(bf16[256,256]{1,0:T(8,128)(2,1)S(1)} %add_convert_fusion.3.dpair_ref.refs_8_), channel_id=1, source_target_pairs={{0,4},{4,0},{8,12},{12,8},{16,20},{20,16},{24,28},{28,24},{1,5},{5... | collective-permute-start | bytes 393224 | tf_op jit(solution)/shard_map/ppermute | solution.py:40
  76.5 1.3 %collective-permute-start.31 = (bf16[256,256]{1,0:T(8,128)(2,1)S(1)}, bf16[256,256]{1,0:T(8,128)(2,1)S(1)}, u32[]{:S(2)}, u32[]{:S(2)}) collective-permute-start(bf16[256,256]{1,0:T(8,128)(2,1)S(1)} %collective-permute-done.23.dpair_ref.refs_10_), channel_id=1, source_target_pairs={{0,4},{4,0},{8,12},{12,8},{16,20},{20,16},{24,28},{28,24},{1,5},{5... | collective-permute-start | bytes 393224 | tf_op jit(solution)/shard_map/ppermute | solution.py:40
  78.9 7.8 %collective-permute-start.37 = (bf16[128,768]{1,0:T(8,128)(2,1)S(1)}, bf16[128,768]{1,0:T(8,128)(2,1)S(1)}, u32[]{:S(2)}, u32[]{:S(2)}) collective-permute-start(bf16[128,768]{1,0:T(8,128)(2,1)S(1)} %get-tuple-element.60), channel_id=1, source_target_pairs={{0,2},{1,3},{2,0},{3,1},{4,6},{5,7},{6,4},{7,5},{8,10},{9,11},{10,... | collective-permute-start | bytes 589832 | tf_op jit(solution)/shard_map/ppermute | solution.py:35
  80.0 25.4 %collective-permute-start.24 = (bf16[256,2048]{1,0:T(8,128)(2,1)S(1)}, bf16[256,2048]{1,0:T(8,128)(2,1)S(1)}, u32[]{:S(2)}, u32[]{:S(2)}) collective-permute-start(bf16[256,2048]{1,0:T(8,128)(2,1)S(1)} %get-tuple-element.51), channel_id=1, source_target_pairs={{0,1},{1,0},{2,3},{3,2},{4,5},{5,4},{6,7},{7,6},{8,9},{9,8},{10,11... | collective-permute-start | bytes 3145736 | tf_op jit(solution)/shard_map/ppermute | solution.py:28
  80.8 10.1 %collective-permute-start.35 = (bf16[128,768]{1,0:T(8,128)(2,1)S(1)}, bf16[128,768]{1,0:T(8,128)(2,1)S(1)}, u32[]{:S(2)}, u32[]{:S(2)}) collective-permute-start(bf16[128,768]{1,0:T(8,128)(2,1)S(1)} %get-tuple-element.53.refs_15_), channel_id=1, source_target_pairs={{0,2},{1,3},{2,0},{3,1},{4,6},{5,7},{6,4},{7,5},{8,10},{9,11},{10,... | collective-permute-start | bytes 589832 | tf_op jit(solution)/shard_map/ppermute | solution.py:35
  83.8 11.4 %collective-permute-start.33 = (bf16[128,768]{1,0:T(8,128)(2,1)S(1)}, bf16[128,768]{1,0:T(8,128)(2,1)S(1)}, u32[]{:S(2)}, u32[]{:S(2)}) collective-permute-start(bf16[128,768]{1,0:T(8,128)(2,1)S(1)} %get-tuple-element.57), channel_id=1, source_target_pairs={{0,2},{1,3},{2,0},{3,1},{4,6},{5,7},{6,4},{7,5},{8,10},{9,11},{10,... | collective-permute-start | bytes 589832 | tf_op jit(solution)/shard_map/ppermute | solution.py:35
  84.0 14.7 %collective-permute-start.32 = (bf16[128,768]{1,0:T(8,128)(2,1)S(1)}, bf16[128,768]{1,0:T(8,128)(2,1)S(1)}, u32[]{:S(2)}, u32[]{:S(2)}) collective-permute-start(bf16[128,768]{1,0:T(8,128)(2,1)S(1)} %get-tuple-element.55), channel_id=1, source_target_pairs={{0,2},{1,3},{2,0},{3,1},{4,6},{5,7},{6,4},{7,5},{8,10},{9,11},{10,... | collective-permute-start | bytes 589832 | tf_op jit(solution)/shard_map/ppermute | solution.py:35
  86.7 11.9 %collective-permute-start.38 = (bf16[128,768]{1,0:T(8,128)(2,1)S(1)}, bf16[128,768]{1,0:T(8,128)(2,1)S(1)}, u32[]{:S(2)}, u32[]{:S(2)}) collective-permute-start(bf16[128,768]{1,0:T(8,128)(2,1)S(1)} %add_convert_fusion), channel_id=1, source_target_pairs={{0,16},{4,20},{8,24},{12,28},{16,0},{20,4},{24,8},{28,12},{1,17},{... | collective-permute-start | bytes 589832 | tf_op jit(solution)/shard_map/ppermute | solution.py:47
  90.9 13.6 %collective-permute-start.36 = (bf16[128,768]{1,0:T(8,128)(2,1)S(1)}, bf16[128,768]{1,0:T(8,128)(2,1)S(1)}, u32[]{:S(2)}, u32[]{:S(2)}) collective-permute-start(bf16[128,768]{1,0:T(8,128)(2,1)S(1)} %add_convert_fusion.1), channel_id=1, source_target_pairs={{0,24},{4,28},{8,0},{12,4},{16,8},{20,12},{24,16},{28,20},{1,25},{... | collective-permute-start | bytes 589832 | tf_op jit(solution)/shard_map/ppermute | solution.py:47
  95.2 9.4 %collective-permute-start.34 = (bf16[128,768]{1,0:T(8,128)(2,1)S(1)}, bf16[128,768]{1,0:T(8,128)(2,1)S(1)}, u32[]{:S(2)}, u32[]{:S(2)}) collective-permute-start(bf16[128,768]{1,0:T(8,128)(2,1)S(1)} %add_convert_fusion.2), channel_id=1, source_target_pairs={{0,8},{4,12},{8,16},{12,20},{16,24},{20,28},{24,0},{28,4},{1,9},{5... | collective-permute-start | bytes 589832 | tf_op jit(solution)/shard_map/ppermute | solution.py:47

commit v7 on v6

--- a/solution.py
+++ b/solution.py
@@ -53,72 +53,70 @@
     return lax.ppermute(array, "seq", pairs)
 
 
-def block_order(chips, rest, flip):
+def block_order(chips, rest, flip, steps):
     dp_index, place = lax.axis_index("dp"), lax.axis_index("seq")
     chip, core = dp_index // CORES, dp_index % CORES
     around, x = place // PAIR, (place + flip) % PAIR
     order = []
     for c in range(CORES):
-        for k in range(chips):
+        for k in steps:
             for j in range(rest):
                 shard = CORES * ((chip - k + chips) % chips) + (core + c) % CORES
                 order.append(shard * (PAIR * rest) + PAIR * ((around - j + rest) % rest) + x)
     return order
 
 
+def whole_order(chips, rest):
+    far = range(1, chips)
+    return [block_order(chips, rest, flip, steps) for flip, steps in ((0, range(chips)), (1, far), (1, range(1)))]
+
+
+def split_order(chips, rest):
+    mine, *others = whole_order(chips, rest)
+    half = len(mine) // CORES
+    return [mine[:half], mine[half:], *others]
+
+
 def lanes(index, width):
     return pl.ds(pl.multiple_of(index * width, width), width)
 
 
-def split_kernel(chips, rest, width, in_ref, weights_ref, *out_refs):
-    own_ref = out_refs[-1]
-    order = block_order(chips, rest, 0) + block_order(chips, rest, 1)
-    for ref in out_refs[:-1]:
-        for i in range(ref.shape[1] // width):
-            ref[:, i * width : (i + 1) * width] = in_ref[:, lanes(order.pop(0), width)]
-
-    @pl.when(pl.program_id(0) == 0)
-    def _():
-        own_ref[...] = weights_ref[lanes(lax.axis_index("seq"), width), :]
-
-
-def own_places(rest):
+def split_kernel(chips, rest, width, tokens_ref, *out_refs):
+    for ref, order in zip(out_refs, split_order(chips, rest)):
+        for i, block in enumerate(order):
+            ref[:, i * width : (i + 1) * width] = tokens_ref[:, lanes(block, width)]
+
+
+def own_places(rest, flip):
     place = lax.axis_index("seq")
-    return [PAIR * ((place // PAIR - j + rest) % rest) + place % PAIR for j in range(rest)]
-
-
-def split_inputs(tokens, weights, chips, rest):
-    (rows, total), (shard, cols) = tokens.shape, weights.shape
-    width = shard // (PAIR * rest)
+    return [PAIR * ((place // PAIR - j + rest) % rest) + (place + flip) % PAIR for j in range(rest)]
+
+
+def split_tokens(tokens, chips, rest, width):
+    rows, total = tokens.shape
     half = total // PAIR
-    few = half // 8
-    widths = [half // CORES] * CORES + [half - few, few]
+    near = half // chips
+    widths = [half // CORES] * CORES + [half - near, near]
     if width % 128:
-        blocks = tokens.reshape(rows, total // width, width)
-        order = jnp.stack(block_order(chips, rest, 0) + block_order(chips, rest, 1))
-        taken = jnp.take(blocks, order, axis=1).reshape(rows, total)
-        own = lax.dynamic_index_in_dim(weights.reshape(PAIR * rest, width, cols), lax.axis_index("seq"), 0, keepdims=False)
-        return *jnp.split(taken, [half // CORES, half, total - few], axis=1), own
+        order = jnp.stack(sum(whole_order(chips, rest), []))
+        taken = jnp.take(tokens.reshape(rows, total // width, width), order, axis=1).reshape(rows, total)
+        return jnp.split(taken, [half // CORES, half, total - near], axis=1)
     tile = min(rows, 128)
-    own = pl.BlockSpec((width, cols), lambda i: (0, 0))
     return pl.pallas_call(
         functools.partial(split_kernel, chips, rest, width),
         grid=(rows // tile,),
-        in_specs=[
-            pl.BlockSpec((tile, total), lambda i: (i, 0)),
-            pl.BlockSpec((shard, cols), lambda i: (0, 0)),
-        ],
-        out_specs=[pl.BlockSpec((tile, w), lambda i: (i, 0)) for w in widths] + [own],
-        out_shape=[jax.ShapeDtypeStruct((rows, w), tokens.dtype) for w in widths]
-        + [jax.ShapeDtypeStruct((width, cols), weights.dtype)],
-        name="split_inputs",
-    )(tokens, weights)
-
-
-def merge_kernel(chips, rest, width, mine_ref, other_ref, out_ref, sems):
+        in_specs=[pl.BlockSpec((tile, total), lambda i: (i, 0))],
+        out_specs=[pl.BlockSpec((tile, w), lambda i: (i, 0)) for w in widths],
+        out_shape=[jax.ShapeDtypeStruct((rows, w), tokens.dtype) for w in widths],
+        name="split_tokens",
+    )(tokens)
+
+
+def merge_kernel(chips, rest, width, *refs):
+    in_refs, out_ref, sems = refs[:-2], refs[-2], refs[-1]
     copies = []
-    for flip, ref in enumerate((mine_ref, other_ref)):
-        for i, block in enumerate(block_order(chips, rest, flip)):
+    for ref, order in zip(in_refs, whole_order(chips, rest)):
+        for i, block in enumerate(order):
             source = ref.at[:, pl.ds(i * width, width)]
             target = out_ref.at[:, lanes(block, width)]
             copies.append(pltpu.make_async_copy(source, target, sems.at[len(copies)]))
@@ -128,23 +126,24 @@
         copy.wait()
 
 
-def merge_halves(mine, other, chips, rest, width):
-    rows, half = mine.shape
-    count = PAIR * half // width
+def merge_parts(parts, chips, rest, width):
+    rows = parts[0].shape[0]
+    total = sum(part.shape[1] for part in parts)
+    count = total // width
     if width % 128:
-        order = jnp.stack(block_order(chips, rest, 0) + block_order(chips, rest, 1))
+        order = jnp.stack(sum(whole_order(chips, rest), []))
         where = jnp.zeros_like(order).at[order].set(lax.iota(order.dtype, count))
-        blocks = jnp.concatenate([mine, other], axis=1).reshape(rows, count, width)
-        return jnp.take(blocks, where, axis=1).reshape(rows, PAIR * half)
+        blocks = jnp.concatenate(parts, axis=1).reshape(rows, count, width)
+        return jnp.take(blocks, where, axis=1).reshape(rows, total)
     return pl.pallas_call(
         functools.partial(merge_kernel, chips, rest, width),
-        in_specs=[VMEM] * 2,
+        in_specs=[VMEM] * len(parts),
         out_specs=pl.BlockSpec(memory_space=pl.ANY),
-        out_shape=jax.ShapeDtypeStruct((rows, PAIR * half), mine.dtype),
+        out_shape=jax.ShapeDtypeStruct((rows, total), BF16),
         scratch_shapes=[pltpu.SemaphoreType.DMA((count,))],
         compiler_params=pltpu.CompilerParams(vmem_limit_bytes=20 * 2**20),
-        name="merge_halves",
-    )(mine, other)
+        name="merge_parts",
+    )(*parts)
 
 
 def cut(parts, first, step):
@@ -180,53 +179,64 @@
     )(*tokens, *pieces)
 
 
-def grad_kernel(span, per, dquery_ref, dpair_ref, *refs):
-    pieces, (out_ref, mark_ref) = refs[:-2], refs[-2:]
+def grad_kernel(span, counts, dquery_ref, dpair_ref, *refs):
+    pieces, outs, mark_ref = refs[: -len(counts) - 1], refs[-len(counts) - 1 : -1], refs[-1]
     grads = jnp.concatenate([dquery_ref[...], dpair_ref[...]], axis=1)
-    for k in range(len(pieces) // per):
-        rows = jnp.concatenate([r[...] for r in pieces[k * per : (k + 1) * per]], axis=0)
-        out_ref[:, k * span : (k + 1) * span] = dot(grads, rows, NT).astype(BF16)
+    per = len(pieces) // sum(counts)
+    for out_ref, count in zip(outs, counts):
+        for i in range(count):
+            rows = jnp.concatenate([r[...] for r in pieces[:per]], axis=0)
+            pieces = pieces[per:]
+            out_ref[:, i * span : (i + 1) * span] = dot(grads, rows, NT).astype(BF16)
     mark_ref[...] = grads[:16, :128]
 
 
-def width_grad(dquery, dpair, groups):
+def width_grad(dquery, dpair, parts):
     rows = dquery.shape[0]
-    pieces = [piece for group in groups for piece in group]
-    span = sum(piece.shape[0] for piece in groups[0])
-    return pl.pallas_call(
-        functools.partial(grad_kernel, span, len(groups[0])),
+    pieces = [piece for groups in parts for group in groups for piece in group]
+    span = sum(piece.shape[0] for piece in parts[0][0])
+    counts = [len(groups) for groups in parts]
+    return pl.pallas_call(
+        functools.partial(grad_kernel, span, counts),
         in_specs=[VMEM] * (2 + len(pieces)),
-        out_specs=[VMEM] * 2,
-        out_shape=[jax.ShapeDtypeStruct((rows, span * len(groups)), BF16), jax.ShapeDtypeStruct((16, 128), BF16)],
+        out_specs=[VMEM] * (len(parts) + 1),
+        out_shape=[jax.ShapeDtypeStruct((rows, span * count), BF16) for count in counts]
+        + [jax.ShapeDtypeStruct((16, 128), BF16)],
         compiler_params=pltpu.CompilerParams(vmem_limit_bytes=20 * 2**20),
         name="width_grad",
     )(dquery, dpair, *pieces)
 
 
-def weight_kernel(steps, rest, width, sources, grads, *refs):
-    tokens = []
-    for count, _ in sources:
-        tokens.append(refs[:count])
-        refs = refs[count:]
-    right = [jnp.concatenate([r[...] for r in refs[i : i + grads]], axis=1) for i in range(0, grads * len(sources), grads)]
-    right = jnp.concatenate(right, axis=0)
+def weight_kernel(steps, rest, width, chips, sources, grads, *refs):
+    tokens, refs = refs[: sum(sources)], refs[sum(sources) :]
+    rights = [jnp.concatenate([r[...] for r in refs[i : i + grads]], axis=1) for i in range(0, grads * len(sources), grads)]
+    right = jnp.concatenate(rights, axis=0)
     outs = refs[grads * len(sources) + 1 :]
     span = rest * width
     for i, k in enumerate(steps):
-        left = jnp.concatenate([cut(t, first + k * span, span) for t, (_, first) in zip(tokens, sources)], axis=0)
-        total = dot(left.T, right)
+        left, at = [], 0
+        for core, count in enumerate(sources):
+            parts, at = tokens[at : at + count], at + count
+            if count == 1:
+                left.append(parts[0][:, k * span : (k + 1) * span])
+            else:
+                far, near = parts
+                across = core // CORES
+                first = across if k == 0 else across * (chips - 1) + k - 1
+                left.append((far if k else near)[:, first * span : (first + 1) * span])
+        total = dot(jnp.concatenate(left, axis=0).T, right)
         for j in range(rest):
             out = outs[i * rest + j]
             out[...] = total[j * width : (j + 1) * width].astype(out.dtype)
 
 
-def weight_terms(steps, rest, width, tokens, grads, after):
+def weight_terms(steps, rest, width, chips, tokens, grads, after):
     cols = sum(g.shape[1] for g in grads[0])
-    sources = [(len(parts), first) for parts, first in tokens]
-    parts = [part for group, _ in tokens for part in group]
+    sources = [len(parts) for parts in tokens]
+    parts = [part for group in tokens for part in group]
     given = [g for group in grads for g in group]
     return pl.pallas_call(
-        functools.partial(weight_kernel, steps, rest, width, sources, len(grads[0])),
+        functools.partial(weight_kernel, steps, rest, width, chips, sources, len(grads[0])),
         in_specs=[VMEM] * (len(parts) + len(given) + 1),
         out_specs=[VMEM] * (len(steps) * rest),
         out_shape=[jax.ShapeDtypeStruct((width, cols), BF16 if j else F32) for _ in steps for j in range(rest)],
@@ -322,25 +332,35 @@
     width = shard_rows // seq_count
     back = -(-(local * seq_count // 2 - 1) // local)
 
-    mine_own, mine_across, *sent, own = split_inputs(tokens, weights, chips, rest)
-    tokens_mine = [mine_own, mine_across]
-    tokens_other = [swap_x(part) for part in sent]
-
-    blocks = weights.reshape(seq_count, width, cols)
-    groups_own = [[lax.dynamic_index_in_dim(blocks, p, 0, keepdims=False) for p in own_places(rest)]]
+    own = lax.dynamic_slice_in_dim(weights, place * width, width, 0)
+    mine_own, mine_across, sent, near = split_tokens(tokens, chips, rest, width)
+
+    blocks, near = lax.optimization_barrier((weights, near))
+    blocks = blocks.reshape(seq_count, width, cols)
+    groups_own, groups_near = [
+        [[lax.dynamic_index_in_dim(blocks, p, 0, keepdims=False) for p in own_places(rest, flip)]] for flip in range(PAIR)
+    ]
     arrived = {}
     for k in sorted(range(1, chips), key=lambda k: (-abs(2 * k - chips), k)):
         first = shift_chip(own, k)
+        if not arrived:
+            first, sent = lax.optimization_barrier((first, sent))
         if k == chips // 2:
             first, arrived = lax.optimization_barrier((first, arrived))
         arrived[k] = [first] + [shift_rest(first, j) for j in range(1, rest)]
+    far_other = swap_x(sent)
     groups_own += [arrived[k] for k in range(1, chips)]
+    last = groups_own[chips // 2]
+    last[-1], far_other = lax.optimization_barrier((last[-1], far_other))
     groups_across = [[swap_core(piece) for piece in group] for group in groups_own]
+    groups_near.append([swap_core(piece) for piece in groups_near[0]])
     groups = groups_own + groups_across
-
-    query_sent, pair_sent = project(tokens_other, groups, qwidth, BF16)
+    groups_far = groups_own[1:] + groups_across[1:]
+
+    query_sent, pair_sent = project([far_other], groups_far, qwidth, BF16)
+    query_sent, near_other = lax.optimization_barrier((query_sent, swap_x(near)))
     pair_from, query_from = swap_x(pair_sent), swap_x(query_sent)
-    query, pair = project(tokens_mine, groups, qwidth, F32)
+    query, pair = project([mine_own, mine_across, near], groups + groups_near, qwidth, F32)
     pair = (pair + pair_from.astype(F32)).astype(BF16)
 
     doc_row, flag_row = doc_lengths[0], kept_flags[0]
@@ -358,19 +378,17 @@
     dpair = dpair.astype(BF16)
     dpair_other = swap_x(dpair)
 
-    grad_sent, after = width_grad(dquery_other, dpair_other, groups)
-    grad_from = swap_x(grad_sent)
-
-    half = chips * rest * width
-    across = [swap_core(part) for part in tokens_other]
-    left = [(tokens_mine, 0), (tokens_other, 0), ([swap_core(mine_across)], 0), (across, half)]
+    left = [[mine_own], [far_other, near_other]]
+    left += [[swap_core(mine_across)], [swap_core(far_other), swap_core(near_other)]]
     right = [[dquery, dpair], [dquery_other, dpair_other]]
     right += [[swap_core(g) for g in group] for group in right]
     order = sorted(range(chips), key=lambda k: (k == 0, -min(k, chips - k), k))
-    parts = []
+    parts, after = [], dpair
     for steps in (order[: chips // 2], order[chips // 2 :]):
-        terms = weight_terms(steps, rest, width, left, right, after)
-        after = terms[-1]
+        terms = weight_terms(steps, rest, width, chips, left, right, after)
+        if not parts:
+            grad_sent, after = width_grad(dquery_other, dpair_other, [groups_far])
+            grad_from = swap_x(grad_sent)
         for i, k in enumerate(steps):
             part, *sent = terms[i * rest : (i + 1) * rest]
             for j, piece in enumerate(sent, 1):
@@ -380,7 +398,8 @@
             parts.append(part)
     weights_grad = functools.reduce(jnp.add, reversed(parts))
 
-    inputs_grad = merge_halves(width_grad(dquery, dpair, groups)[0], grad_from, chips, rest, width)
+    grad_mine, grad_near, _ = width_grad(dquery, dpair, [groups, groups_near])
+    inputs_grad = merge_parts([grad_mine, grad_from, grad_near], chips, rest, width)
     return (attention[None], inputs_grad[None], weights_grad)
 
 

time: 107 us -> 104 us (0.972)
  waiting for transfers between devices: 42.6 us -> 38.6 us
    ppermute x7, waiting for transfers between devices: 10.7 us -> 6.75 us  [swap_x(): return lax.ppermute(array, 'seq', [(i, i ^ 1) for i in range(count)])]
    ppermute x7, starting transfers between devices: 11.9 us -> 9.91 us  [swap_x(): return lax.ppermute(array, 'seq', [(i, i ^ 1) for i in range(count)])]
    ppermute x4, starting transfers between devices: 8.71 us -> 10.1 us  [shift_seq(): return lax.ppermute(array, 'seq', pairs)]
    ppermute x6, waiting for transfers between devices: 17.7 us -> 16.4 us  [shift_chip(): return lax.ppermute(array, 'dp', pairs)]
    ppermute x15 -> x17, starting transfers between devices: 2.27 us -> 2.81 us  [swap_core(): return lax.ppermute(array, 'dp', [(i, i ^ 1) for i in range(count)])]
  transfers between devices with their start and end apart: 39 -> 41, of which waited for: 19 -> 20; matrix products, arithmetic and copies ran while one was open for 1% -> 1% of each run, Pallas kernels for 11% -> 14%
where the time goes in v7:
time: 104 us
  starting transfers between devices  45 us (43%)
  waiting for transfers between devices  38.6 us (37%)
  Pallas kernels  17.1 us (16%)
  other arithmetic  1.44 us (1%)
  local copies, waits for them, and re-layouts  1.13 us (1%)
    ppermute x6, waiting for transfers between devices, shift_chip(): return lax.ppermute(array, 'dp', pairs)  16.4 us
    ppermute x6, starting transfers between devices, shift_chip(): return lax.ppermute(array, 'dp', pairs)  12 us
    ppermute x7, starting transfers between devices, shift_rest(): return lax.ppermute(array, 'seq', pairs)  10.2 us
    ppermute x4, starting transfers between devices, shift_seq(): return lax.ppermute(array, 'seq', pairs)  10.1 us
    ppermute x7, starting transfers between devices, swap_x(): return lax.ppermute(array, 'seq', [(i, i ^ 1) for i in range(count)])  9.91 us
    ppermute x7, waiting for transfers between devices, shift_rest(): return lax.ppermute(array, 'seq', pairs)  7.46 us
    ppermute x7, waiting for transfers between devices, swap_x(): return lax.ppermute(array, 'seq', [(i, i ^ 1) for i in range(count)])  6.75 us
    pallas_call x1, Pallas kernels, attend(): pl.pallas_call(functools.partial(attend_kernel, width // HEAD_DIM, back),...  6.31 us
  transfers between devices with their start and end apart: 41, of which 20 were waited for; matrix products, arithmetic and copies ran while one was open for 1% of the time, Pallas kernels for 14%

profile of v7, /device:TPU:0, one launch (start us, length us, event | category | flops | bytes accessed | tf_op | source)
XLA Modules:
  0.0 104.2 jit_solution(8913947262054369433)
XLA Ops:
  0.7 1.0 constant_dynamic-slice_fusion
  1.7 3.1 %collective-permute-start.1 = (bf16[128,768]{1,0:T(8,128)(2,1)S(1)}, bf16[128,768]{1,0:T(8,128)(2,1)S(1)}, u32[]{:S(2)}, u32[]{:S(2)}) collective-permute-start(bf16[128,768]{1,0:T(8,128)(2,1)S(1)} %constant_dynamic-slice_fusion), channel_id=1, source_target_pairs={{0,8},{4,12},{8,16},{12,20},{16,24},{20,28},{24,0},{28,4},{1,9},{5... | collective-permute-start | bytes 589832 | tf_op jit(solution)/shard_map/ppermute | solution.py:47
  4.8 2.8 %split_tokens.1 = (bf16[256,1024]{1,0:T(8,128)(2,1)}, bf16[256,1024]{1,0:T(8,128)(2,1)}, bf16[256,1536]{1,0:T(8,128)(2,1)}, bf16[256,512]{1,0:T(8,128)(2,1)}) custom-call(bf16[256,4096]{1,0:T(8,128)(2,1)} %bitcast.26), custom_call_target="tpu_custom_call" | custom-call | tf_op jit(solution)/shard_map/split_tokens/pallas_call | solution.py:105
  7.6 4.1 %collective-permute-done.1.refs_5_.refs_1_.refs_2_.refs_0_ = bf16[128,768]{1,0:T(8,128)(2,1)S(1)} collective-permute-done((bf16[128,768]{1,0:T(8,128)(2,1)S(1)}, bf16[128,768]{1,0:T(8,128)(2,1)S(1)}, u32[]{:S(2)}, u32[]{:S(2)}) %collective-permute-start.1) | collective-permute-done | bytes 196640 | tf_op jit(solution)/shard_map/ppermute | solution.py:47
  11.7 1.5 %collective-permute-start.6 = (bf16[256,1536]{1,0:T(8,128)(2,1)}, bf16[256,1536]{1,0:T(8,128)(2,1)S(1)}, u32[]{:S(2)}, u32[]{:S(2)}) collective-permute-start(bf16[256,1536]{1,0:T(8,128)(2,1)} %get-tuple-element.50), channel_id=1, source_target_pairs={{0,1},{1,0},{2,3},{3,2},{4,5},{5,4},{6,7},{7,6},{8,9},{9,8},{10,11... | collective-permute-start | bytes 2359304 | tf_op jit(solution)/shard_map/ppermute | solution.py:28
  13.2 1.7 %collective-permute-start.3 = (bf16[128,768]{1,0:T(8,128)(2,1)S(1)}, bf16[128,768]{1,0:T(8,128)(2,1)S(1)}, u32[]{:S(2)}, u32[]{:S(2)}) collective-permute-start(bf16[128,768]{1,0:T(8,128)(2,1)S(1)} %constant_dynamic-slice_fusion), channel_id=1, source_target_pairs={{0,24},{4,28},{8,0},{12,4},{16,8},{20,12},{24,16},{28,20},{1,25},{... | collective-permute-start | bytes 589832 | tf_op jit(solution)/shard_map/ppermute | solution.py:47
  14.9 1.5 %collective-permute-start.2 = (bf16[128,768]{1,0:T(8,128)(2,1)S(1)}, bf16[128,768]{1,0:T(8,128)(2,1)S(1)}, u32[]{:S(2)}, u32[]{:S(2)}) collective-permute-start(bf16[128,768]{1,0:T(8,128)(2,1)S(1)} %collective-permute-done.1.refs_5_.refs_1_.refs_2_.refs_0_), channel_id=1, source_target_pairs={{0,2},{1,3},{2,0},{3,1},{4,6},{5,7},{6,4},{7,5},{8,10},{9,11},{10,... | collective-permute-start | bytes 589832 | tf_op jit(solution)/shard_map/ppermute | solution.py:35
  16.4 3.6 %collective-permute-done.3.refs_9_.refs_5_.refs_6_.refs_4_ = bf16[128,768]{1,0:T(8,128)(2,1)S(1)} collective-permute-done((bf16[128,768]{1,0:T(8,128)(2,1)S(1)}, bf16[128,768]{1,0:T(8,128)(2,1)S(1)}, u32[]{:S(2)}, u32[]{:S(2)}) %collective-permute-start.3) | collective-permute-done | bytes 196640 | tf_op jit(solution)/shard_map/ppermute | solution.py:47
  20.1 1.5 %collective-permute-start.4 = (bf16[128,768]{1,0:T(8,128)(2,1)S(1)}, bf16[128,768]{1,0:T(8,128)(2,1)S(1)}, u32[]{:S(2)}, u32[]{:S(2)}) collective-permute-start(bf16[128,768]{1,0:T(8,128)(2,1)S(1)} %collective-permute-done.3.refs_9_.refs_5_.refs_6_.refs_4_), channel_id=1, source_target_pairs={{0,2},{1,3},{2,0},{3,1},{4,6},{5,7},{6,4},{7,5},{8,10},{9,11},{10,... | collective-permute-start | bytes 589832 | tf_op jit(solution)/shard_map/ppermute | solution.py:35
  21.6 0.5 collective-permute-start.17
  22.3 4.1 %collective-permute-done.refs_7_.refs_3_.refs_4_.refs_2_ = bf16[128,768]{1,0:T(8,128)(2,1)S(1)} collective-permute-done((bf16[128,768]{1,0:T(8,128)(2,1)S(1)}, bf16[128,768]{1,0:T(8,128)(2,1)S(1)}, u32[]{:S(2)}, u32[]{:S(2)}) %collective-permute-start) | collective-permute-done | bytes 196640 | tf_op jit(solution)/shard_map/ppermute | solution.py:47
  26.4 1.5 %collective-permute-start.5 = (bf16[128,768]{1,0:T(8,128)(2,1)S(1)}, bf16[128,768]{1,0:T(8,128)(2,1)S(1)}, u32[]{:S(2)}, u32[]{:S(2)}) collective-permute-start(bf16[128,768]{1,0:T(8,128)(2,1)S(1)} %collective-permute-done.refs_7_.refs_3_.refs_4_.refs_2_), channel_id=1, source_target_pairs={{0,2},{1,3},{2,0},{3,1},{4,6},{5,7},{6,4},{7,5},{8,10},{9,11},{10,... | collective-permute-start | bytes 589832 | tf_op jit(solution)/shard_map/ppermute | solution.py:35
  28.0 0.5 collective-permute-start.10
  28.5 3.7 %collective-permute-done.5.refs_8_.refs_4_.refs_5_.refs_3_ = bf16[128,768]{1,0:T(8,128)(2,1)S(1)} collective-permute-done((bf16[128,768]{1,0:T(8,128)(2,1)S(1)}, bf16[128,768]{1,0:T(8,128)(2,1)S(1)}, u32[]{:S(2)}, u32[]{:S(2)}) %collective-permute-start.5) | collective-permute-done | bytes 196640 | tf_op jit(solution)/shard_map/ppermute | solution.py:35
  34.7 0.8 project.3
  35.4 0.8 collective-permute-done.17.refs_2_
  36.2 1.2 %collective-permute-start.19 = (bf16[256,256]{1,0:T(8,128)(2,1)S(1)}, bf16[256,256]{1,0:T(8,128)(2,1)S(1)}, u32[]{:S(2)}, u32[]{:S(2)}) collective-permute-start(bf16[256,256]{1,0:T(8,128)(2,1)S(1)} %get-tuple-element.59), channel_id=1, source_target_pairs={{0,1},{1,0},{2,3},{3,2},{4,5},{5,4},{6,7},{7,6},{8,9},{9,8},{10,11... | collective-permute-start | bytes 393224 | tf_op jit(solution)/shard_map/ppermute | solution.py:28
  37.6 0.8 collective-permute-start.18
  38.5 1.2 %project.2 = (f32[256,512]{1,0:T(8,128)S(1)}, f32[256,256]{1,0:T(8,128)S(1)}) custom-call(bf16[256,1024]{1,0:T(8,128)(2,1)S(1)} %copy-done, bf16[256,1024]{1,0:T(8,128)(2,1)S(1)} %copy-done.1, bf16[256,512]{1,0:T(8,128)(2,1)S(1)} %copy-done.2, bf16[128,768]{1,0:T(8,128)(2,1)S(1)} %get-tuple-element.80.refs_3_.refs_0_, ...), custom_call_target="tpu_custom_call" | custom-call | tf_op jit(solution)/shard_map/project/pallas_call | solution.py:172
  39.7 2.1 %collective-permute-done.19 = bf16[256,256]{1,0:T(8,128)(2,1)S(1)} collective-permute-done((bf16[256,256]{1,0:T(8,128)(2,1)S(1)}, bf16[256,256]{1,0:T(8,128)(2,1)S(1)}, u32[]{:S(2)}, u32[]{:S(2)}) %collective-permute-start.19) | collective-permute-done | bytes 131104 | tf_op jit(solution)/shard_map/ppermute | solution.py:28
  41.8 3.4 %collective-permute-start.20 = (bf16[256,256]{1,0:T(8,128)(2,1)S(1)}, bf16[256,256]{1,0:T(8,128)(2,1)S(1)}, u32[]{:S(2)}, u32[]{:S(2)}) collective-permute-start(bf16[256,256]{1,0:T(8,128)(2,1)S(1)} %add_convert_fusion.4.refs_2_), channel_id=1, source_target_pairs={{0,2},{1,3},{4,6},{5,7},{8,10},{9,11},{12,14},{13,15},{16,18},{17,... | collective-permute-start | bytes 393224 | tf_op jit(solution)/shard_map/ppermute | solution.py:53
  45.2 4.1 %collective-permute-start.21 = (bf16[256,256]{1,0:T(8,128)(2,1)S(1)}, bf16[256,256]{1,0:T(8,128)(2,1)S(1)}, u32[]{:S(2)}, u32[]{:S(2)}) collective-permute-start(bf16[256,256]{1,0:T(8,128)(2,1)S(1)} %add_convert_fusion.4.refs_2_), channel_id=1, source_target_pairs={{0,1},{1,2},{2,3},{4,5},{5,6},{6,7},{8,9},{9,10},{10,11},{12,13},{... | collective-permute-start | bytes 393224 | tf_op jit(solution)/shard_map/ppermute | solution.py:53
  49.5 2.3 %collective-permute-done.21.refs_1_ = bf16[256,256]{1,0:T(8,128)(2,1)S(1)} collective-permute-done((bf16[256,256]{1,0:T(8,128)(2,1)S(1)}, bf16[256,256]{1,0:T(8,128)(2,1)S(1)}, u32[]{:S(2)}, u32[]{:S(2)}) %collective-permute-start.21) | collective-permute-done | bytes 131104 | tf_op jit(solution)/shard_map/ppermute | solution.py:53
  51.8 6.3 %attend.1 = (bf16[256,512]{1,0:T(8,128)(2,1)}, bf16[256,512]{1,0:T(8,128)(2,1)S(1)}, f32[256,256]{1,0:T(8,128)S(1)}, bf16[512,256]{1,0:T(8,128)(2,1)S(1)}) custom-call(s32[8]{0:T(128)S(1)} %bitcast.25, f32[256,512]{1,0:T(8,128)S(1)} %get-tuple-element.54.q_ref, bf16[256,512]{1,0:T(8,128)(2,1)S(1)} %collective-permute-done.18.q_from_ref, ...), custom_call_target="tpu_custom_call" | custom-call | tf_op jit(solution)/shard_map/attend/pallas_call | solution.py:301
  58.1 1.3 %collective-permute-start.23 = (bf16[256,256]{1,0:T(8,128)(2,1)S(1)}, bf16[256,256]{1,0:T(8,128)(2,1)S(1)}, u32[]{:S(2)}, u32[]{:S(2)}) collective-permute-start(bf16[256,256]{1,0:T(8,128)(2,1)S(1)} %get-tuple-element.82), channel_id=1, source_target_pairs={{2,0},{3,1},{6,4},{7,5},{10,8},{11,9},{14,12},{15,13},{18,16},{19,... | collective-permute-start | bytes 393224 | tf_op jit(solution)/shard_map/ppermute | solution.py:53
  59.4 1.3 %collective-permute-start.22 = (bf16[256,256]{1,0:T(8,128)(2,1)S(1)}, bf16[256,256]{1,0:T(8,128)(2,1)S(1)}, u32[]{:S(2)}, u32[]{:S(2)}) collective-permute-start(bf16[256,256]{1,0:T(8,128)(2,1)S(1)} %get-tuple-element.81), channel_id=1, source_target_pairs={{1,0},{2,1},{3,2},{5,4},{6,5},{7,6},{9,8},{10,9},{11,10},{13,12},{... | collective-permute-start | bytes 393224 | tf_op jit(solution)/shard_map/ppermute | solution.py:53
  60.7 3.1 %collective-permute-start.24 = (bf16[256,512]{1,0:T(8,128)(2,1)S(1)}, bf16[256,512]{1,0:T(8,128)(2,1)S(1)}, u32[]{:S(2)}, u32[]{:S(2)}) collective-permute-start(bf16[256,512]{1,0:T(8,128)(2,1)S(1)} %get-tuple-element.61.dquery_ref.refs_6_), channel_id=1, source_target_pairs={{0,1},{1,0},{2,3},{3,2},{4,5},{5,4},{6,7},{7,6},{8,9},{9,8},{10,11... | collective-permute-start | bytes 786440 | tf_op jit(solution)/shard_map/ppermute | solution.py:28
  63.8 1.1 %collective-permute-done.23 = bf16[256,256]{1,0:T(8,128)(2,1)S(1)} collective-permute-done((bf16[256,256]{1,0:T(8,128)(2,1)S(1)}, bf16[256,256]{1,0:T(8,128)(2,1)S(1)}, u32[]{:S(2)}, u32[]{:S(2)}) %collective-permute-start.23) | collective-permute-done | bytes 131104 | tf_op jit(solution)/shard_map/ppermute | solution.py:53
  65.0 2.8 %collective-permute-done.22 = bf16[256,256]{1,0:T(8,128)(2,1)S(1)} collective-permute-done((bf16[256,256]{1,0:T(8,128)(2,1)S(1)}, bf16[256,256]{1,0:T(8,128)(2,1)S(1)}, u32[]{:S(2)}, u32[]{:S(2)}) %collective-permute-start.22) | collective-permute-done | bytes 131104 | tf_op jit(solution)/shard_map/ppermute | solution.py:53
  67.8 2.3 %collective-permute-start.25 = (bf16[256,256]{1,0:T(8,128)(2,1)S(1)}, bf16[256,256]{1,0:T(8,128)(2,1)S(1)}, u32[]{:S(2)}, u32[]{:S(2)}) collective-permute-start(bf16[256,256]{1,0:T(8,128)(2,1)S(1)} %add_convert_fusion.3.dpair_ref.refs_7_.refs_14_), channel_id=1, source_target_pairs={{0,1},{1,0},{2,3},{3,2},{4,5},{5,4},{6,7},{7,6},{8,9},{9,8},{10,11... | collective-permute-start | bytes 393224 | tf_op jit(solution)/shard_map/ppermute | solution.py:28
  70.5 0.5 collective-permute-start.31
  71.0 3.2 %collective-permute-done.25.dpair_ref.refs_9_ = bf16[256,256]{1,0:T(8,128)(2,1)S(1)} collective-permute-done((bf16[256,256]{1,0:T(8,128)(2,1)S(1)}, bf16[256,256]{1,0:T(8,128)(2,1)S(1)}, u32[]{:S(2)}, u32[]{:S(2)}) %collective-permute-start.25) | collective-permute-done | bytes 131104 | tf_op jit(solution)/shard_map/ppermute | solution.py:28
  74.3 1.3 %collective-permute-done.33.refs_13_ = bf16[256,256]{1,0:T(8,128)(2,1)S(1)} collective-permute-done((bf16[256,256]{1,0:T(8,128)(2,1)S(1)}, bf16[256,256]{1,0:T(8,128)(2,1)S(1)}, u32[]{:S(2)}, u32[]{:S(2)}) %collective-permute-start.33) | collective-permute-done | bytes 131104 | tf_op jit(solution)/shard_map/ppermute | solution.py:40
  75.6 1.0 weight_terms.3
  76.6 1.9 %collective-permute-start.39 = (bf16[128,768]{1,0:T(8,128)(2,1)S(1)}, bf16[128,768]{1,0:T(8,128)(2,1)S(1)}, u32[]{:S(2)}, u32[]{:S(2)}) collective-permute-start(bf16[128,768]{1,0:T(8,128)(2,1)S(1)} %get-tuple-element.76), channel_id=1, source_target_pairs={{0,2},{1,3},{2,0},{3,1},{4,6},{5,7},{6,4},{7,5},{8,10},{9,11},{10,... | collective-permute-start | bytes 589832 | tf_op jit(solution)/shard_map/ppermute | solution.py:35
  78.6 0.8 width_grad.3
  79.7 1.6 %collective-permute-start.37 = (bf16[128,768]{1,0:T(8,128)(2,1)S(1)}, bf16[128,768]{1,0:T(8,128)(2,1)S(1)}, u32[]{:S(2)}, u32[]{:S(2)}) collective-permute-start(bf16[128,768]{1,0:T(8,128)(2,1)S(1)} %get-tuple-element.74), channel_id=1, source_target_pairs={{0,2},{1,3},{2,0},{3,1},{4,6},{5,7},{6,4},{7,5},{8,10},{9,11},{10,... | collective-permute-start | bytes 589832 | tf_op jit(solution)/shard_map/ppermute | solution.py:35
  81.3 1.0 weight_terms.2
  82.9 1.6 %collective-permute-start.34 = (bf16[128,768]{1,0:T(8,128)(2,1)S(1)}, bf16[128,768]{1,0:T(8,128)(2,1)S(1)}, u32[]{:S(2)}, u32[]{:S(2)}) collective-permute-start(bf16[128,768]{1,0:T(8,128)(2,1)S(1)} %get-tuple-element.70), channel_id=1, source_target_pairs={{0,2},{1,3},{2,0},{3,1},{4,6},{5,7},{6,4},{7,5},{8,10},{9,11},{10,... | collective-permute-start | bytes 589832 | tf_op jit(solution)/shard_map/ppermute | solution.py:35
  84.5 1.9 %collective-permute-start.40 = (bf16[128,768]{1,0:T(8,128)(2,1)S(1)}, bf16[128,768]{1,0:T(8,128)(2,1)S(1)}, u32[]{:S(2)}, u32[]{:S(2)}) collective-permute-start(bf16[128,768]{1,0:T(8,128)(2,1)S(1)} %add_convert_fusion), channel_id=1, source_target_pairs={{0,16},{4,20},{8,24},{12,28},{16,0},{20,4},{24,8},{28,12},{1,17},{... | collective-permute-start | bytes 589832 | tf_op jit(solution)/shard_map/ppermute | solution.py:47
  86.4 2.3 %collective-permute-done.37 = bf16[128,768]{1,0:T(8,128)(2,1)S(1)} collective-permute-done((bf16[128,768]{1,0:T(8,128)(2,1)S(1)}, bf16[128,768]{1,0:T(8,128)(2,1)S(1)}, u32[]{:S(2)}, u32[]{:S(2)}) %collective-permute-start.37) | collective-permute-done | bytes 196640 | tf_op jit(solution)/shard_map/ppermute | solution.py:35
  88.7 2.6 %collective-permute-start.38 = (bf16[128,768]{1,0:T(8,128)(2,1)S(1)}, bf16[128,768]{1,0:T(8,128)(2,1)S(1)}, u32[]{:S(2)}, u32[]{:S(2)}) collective-permute-start(bf16[128,768]{1,0:T(8,128)(2,1)S(1)} %add_convert_fusion.1), channel_id=1, source_target_pairs={{0,24},{4,28},{8,0},{12,4},{16,8},{20,12},{24,16},{28,20},{1,25},{... | collective-permute-start | bytes 589832 | tf_op jit(solution)/shard_map/ppermute | solution.py:47
  91.3 1.5 %collective-permute-done.35 = bf16[128,768]{1,0:T(8,128)(2,1)S(1)} collective-permute-done((bf16[128,768]{1,0:T(8,128)(2,1)S(1)}, bf16[128,768]{1,0:T(8,128)(2,1)S(1)}, u32[]{:S(2)}, u32[]{:S(2)}) %collective-permute-start.35) | collective-permute-done | bytes 196640 | tf_op jit(solution)/shard_map/ppermute | solution.py:35
  92.9 2.7 %collective-permute-start.36 = (bf16[128,768]{1,0:T(8,128)(2,1)S(1)}, bf16[128,768]{1,0:T(8,128)(2,1)S(1)}, u32[]{:S(2)}, u32[]{:S(2)}) collective-permute-start(bf16[128,768]{1,0:T(8,128)(2,1)S(1)} %add_convert_fusion.2), channel_id=1, source_target_pairs={{0,8},{4,12},{8,16},{12,20},{16,24},{20,28},{24,0},{28,4},{1,9},{5... | collective-permute-start | bytes 589832 | tf_op jit(solution)/shard_map/ppermute | solution.py:47
  95.6 1.6 %width_grad.2 = (bf16[256,2048]{1,0:T(8,128)(2,1)S(1)}, bf16[256,512]{1,0:T(8,128)(2,1)S(1)}, bf16[16,128]{1,0:T(8,128)(2,1)}) custom-call(bf16[256,512]{1,0:T(8,128)(2,1)S(1)} %get-tuple-element.61.dquery_ref.refs_6_, bf16[256,256]{1,0:T(8,128)(2,1)S(1)} %add_convert_fusion.3.dpair_ref.refs_7_.refs_14_, ...), custom_call_target="tpu_custom_call" | custom-call | tf_op jit(solution)/shard_map/width_grad/pallas_call | solution.py:199
  97.9 3.9 %collective-permute-done.36 = bf16[128,768]{1,0:T(8,128)(2,1)S(1)} collective-permute-done((bf16[128,768]{1,0:T(8,128)(2,1)S(1)}, bf16[128,768]{1,0:T(8,128)(2,1)S(1)}, u32[]{:S(2)}, u32[]{:S(2)}) %collective-permute-start.36) | collective-permute-done | bytes 196640 | tf_op jit(solution)/shard_map/ppermute | solution.py:47
  101.8 0.9 convert_add_fusion
  102.6 1.6 %merge_parts.1 = bf16[256,4096]{1,0:T(8,128)(2,1)} custom-call(bf16[256,2048]{1,0:T(8,128)(2,1)S(1)} %get-tuple-element.64.refs_0_, bf16[256,1536]{1,0:T(8,128)(2,1)S(1)} %collective-permute-done.26.refs_1_, bf16[256,512]{1,0:T(8,128)(2,1)S(1)} %get-tuple-element.66.refs_2_), custom_call_target="tpu_custom_call" | custom-call | tf_op jit(solution)/shard_map/merge_parts/pallas_call | solution.py:138
  (72 shorter events, 5.2 us)
Async XLA Ops:
  0.6 32.6 %copy-start.4 = (bf16[512,768]{1,0:T(8,128)(2,1)S(1)}, bf16[512,768]{1,0:T(8,128)(2,1)}, u32[]{:S(2)}) copy-start(bf16[512,768]{1,0:T(8,128)(2,1)} %param.6) | copy-start | bytes 2359300
  0.6 21.5 %copy-start.3 = (s32[1,8]{1,0:T(1,128)S(1)}, s32[1,8]{1,0:T(1,128)}, u32[]{:S(2)}) copy-start(s32[1,8]{1,0:T(1,128)} %param.8) | copy-start | bytes 100
  0.7 32.5 %copy-start.6 = (s32[1,8]{1,0:T(1,128)S(1)}, s32[1,8]{1,0:T(1,128)}, u32[]{:S(2)}) copy-start(s32[1,8]{1,0:T(1,128)} %param.9) | copy-start | bytes 100
  1.7 10.0 %collective-permute-start.1 = (bf16[128,768]{1,0:T(8,128)(2,1)S(1)}, bf16[128,768]{1,0:T(8,128)(2,1)S(1)}, u32[]{:S(2)}, u32[]{:S(2)}) collective-permute-start(bf16[128,768]{1,0:T(8,128)(2,1)S(1)} %constant_dynamic-slice_fusion), channel_id=1, source_target_pairs={{0,8},{4,12},{8,16},{12,20},{16,24},{20,28},{24,0},{28,4},{1,9},{5... | collective-permute-start | bytes 589832 | tf_op jit(solution)/shard_map/ppermute | solution.py:47
  11.7 20.7 %collective-permute-start.6 = (bf16[256,1536]{1,0:T(8,128)(2,1)}, bf16[256,1536]{1,0:T(8,128)(2,1)S(1)}, u32[]{:S(2)}, u32[]{:S(2)}) collective-permute-start(bf16[256,1536]{1,0:T(8,128)(2,1)} %get-tuple-element.50), channel_id=1, source_target_pairs={{0,1},{1,0},{2,3},{3,2},{4,5},{5,4},{6,7},{7,6},{8,9},{9,8},{10,11... | collective-permute-start | bytes 2359304 | tf_op jit(solution)/shard_map/ppermute | solution.py:28
  13.2 6.9 %collective-permute-start.3 = (bf16[128,768]{1,0:T(8,128)(2,1)S(1)}, bf16[128,768]{1,0:T(8,128)(2,1)S(1)}, u32[]{:S(2)}, u32[]{:S(2)}) collective-permute-start(bf16[128,768]{1,0:T(8,128)(2,1)S(1)} %constant_dynamic-slice_fusion), channel_id=1, source_target_pairs={{0,24},{4,28},{8,0},{12,4},{16,8},{20,12},{24,16},{28,20},{1,25},{... | collective-permute-start | bytes 589832 | tf_op jit(solution)/shard_map/ppermute | solution.py:47
  14.9 11.5 %collective-permute-start = (bf16[128,768]{1,0:T(8,128)(2,1)S(1)}, bf16[128,768]{1,0:T(8,128)(2,1)S(1)}, u32[]{:S(2)}, u32[]{:S(2)}) collective-permute-start(bf16[128,768]{1,0:T(8,128)(2,1)S(1)} %constant_dynamic-slice_fusion), channel_id=1, source_target_pairs={{0,16},{4,20},{8,24},{12,28},{16,0},{20,4},{24,8},{28,12},{1,17},{... | collective-permute-start | bytes 589832 | tf_op jit(solution)/shard_map/ppermute | solution.py:47
  14.9 11.5 %collective-permute-start.2 = (bf16[128,768]{1,0:T(8,128)(2,1)S(1)}, bf16[128,768]{1,0:T(8,128)(2,1)S(1)}, u32[]{:S(2)}, u32[]{:S(2)}) collective-permute-start(bf16[128,768]{1,0:T(8,128)(2,1)S(1)} %collective-permute-done.1.refs_5_.refs_1_.refs_2_.refs_0_), channel_id=1, source_target_pairs={{0,2},{1,3},{2,0},{3,1},{4,6},{5,7},{6,4},{7,5},{8,10},{9,11},{10,... | collective-permute-start | bytes 589832 | tf_op jit(solution)/shard_map/ppermute | solution.py:35
  20.1 6.4 %collective-permute-start.4 = (bf16[128,768]{1,0:T(8,128)(2,1)S(1)}, bf16[128,768]{1,0:T(8,128)(2,1)S(1)}, u32[]{:S(2)}, u32[]{:S(2)}) collective-permute-start(bf16[128,768]{1,0:T(8,128)(2,1)S(1)} %collective-permute-done.3.refs_9_.refs_5_.refs_6_.refs_4_), channel_id=1, source_target_pairs={{0,2},{1,3},{2,0},{3,1},{4,6},{5,7},{6,4},{7,5},{8,10},{9,11},{10,... | collective-permute-start | bytes 589832 | tf_op jit(solution)/shard_map/ppermute | solution.py:35
  21.6 14.6 %collective-permute-start.17 = (bf16[256,512]{1,0:T(8,128)(2,1)}, bf16[256,512]{1,0:T(8,128)(2,1)S(1)}, u32[]{:S(2)}, u32[]{:S(2)}) collective-permute-start(bf16[256,512]{1,0:T(8,128)(2,1)} %get-tuple-element.43.refs_2_), channel_id=1, source_target_pairs={{0,1},{1,0},{2,3},{3,2},{4,5},{5,4},{6,7},{7,6},{8,9},{9,8},{10,11... | collective-permute-start | bytes 786440 | tf_op jit(solution)/shard_map/ppermute | solution.py:28
  26.4 5.7 %collective-permute-start.5 = (bf16[128,768]{1,0:T(8,128)(2,1)S(1)}, bf16[128,768]{1,0:T(8,128)(2,1)S(1)}, u32[]{:S(2)}, u32[]{:S(2)}) collective-permute-start(bf16[128,768]{1,0:T(8,128)(2,1)S(1)} %collective-permute-done.refs_7_.refs_3_.refs_4_.refs_2_), channel_id=1, source_target_pairs={{0,2},{1,3},{2,0},{3,1},{4,6},{5,7},{6,4},{7,5},{8,10},{9,11},{10,... | collective-permute-start | bytes 589832 | tf_op jit(solution)/shard_map/ppermute | solution.py:35
  28.0 4.7 %collective-permute-start.9 = (bf16[128,768]{1,0:T(8,128)(2,1)S(1)}, bf16[128,768]{1,0:T(8,128)(2,1)S(1)}, u32[]{:S(2)}, u32[]{:S(2)}) collective-permute-start(bf16[128,768]{1,0:T(8,128)(2,1)S(1)} %collective-permute-done.1.refs_5_.refs_1_.refs_2_.refs_0_), channel_id=1, source_target_pairs={{0,4},{4,0},{8,12},{12,8},{16,20},{20,16},{24,28},{28,24},{1,5},{5... | collective-permute-start | bytes 589832 | tf_op jit(solution)/shard_map/ppermute | solution.py:40
  28.0 4.9 %collective-permute-start.10 = (bf16[128,768]{1,0:T(8,128)(2,1)S(1)}, bf16[128,768]{1,0:T(8,128)(2,1)S(1)}, u32[]{:S(2)}, u32[]{:S(2)}) collective-permute-start(bf16[128,768]{1,0:T(8,128)(2,1)S(1)} %collective-permute-done.2.refs_6_.refs_2_.refs_3_.refs_1_), channel_id=1, source_target_pairs={{0,4},{4,0},{8,12},{12,8},{16,20},{20,16},{24,28},{28,24},{1,5},{5... | collective-permute-start | bytes 589832 | tf_op jit(solution)/shard_map/ppermute | solution.py:40
  32.1 1.4 %collective-permute-start.11 = (bf16[128,768]{1,0:T(8,128)(2,1)S(1)}, bf16[128,768]{1,0:T(8,128)(2,1)S(1)}, u32[]{:S(2)}, u32[]{:S(2)}) collective-permute-start(bf16[128,768]{1,0:T(8,128)(2,1)S(1)} %collective-permute-done.refs_7_.refs_3_.refs_4_.refs_2_), channel_id=1, source_target_pairs={{0,4},{4,0},{8,12},{12,8},{16,20},{20,16},{24,28},{28,24},{1,5},{5... | collective-permute-start | bytes 589832 | tf_op jit(solution)/shard_map/ppermute | solution.py:40
  32.4 1.5 %collective-permute-start.13 = (bf16[128,768]{1,0:T(8,128)(2,1)S(1)}, bf16[128,768]{1,0:T(8,128)(2,1)S(1)}, u32[]{:S(2)}, u32[]{:S(2)}) collective-permute-start(bf16[128,768]{1,0:T(8,128)(2,1)S(1)} %collective-permute-done.3.refs_9_.refs_5_.refs_6_.refs_4_), channel_id=1, source_target_pairs={{0,4},{4,0},{8,12},{12,8},{16,20},{20,16},{24,28},{28,24},{1,5},{5... | collective-permute-start | bytes 589832 | tf_op jit(solution)/shard_map/ppermute | solution.py:40
  32.7 1.5 %collective-permute-start.14 = (bf16[128,768]{1,0:T(8,128)(2,1)S(1)}, bf16[128,768]{1,0:T(8,128)(2,1)S(1)}, u32[]{:S(2)}, u32[]{:S(2)}) collective-permute-start(bf16[128,768]{1,0:T(8,128)(2,1)S(1)} %collective-permute-done.4.refs_10_.refs_6_.refs_7_.refs_5_), channel_id=1, source_target_pairs={{0,4},{4,0},{8,12},{12,8},{16,20},{20,16},{24,28},{28,24},{1,5},{5... | collective-permute-start | bytes 589832 | tf_op jit(solution)/shard_map/ppermute | solution.py:40
  32.9 1.5 %collective-permute-start.12 = (bf16[128,768]{1,0:T(8,128)(2,1)S(1)}, bf16[128,768]{1,0:T(8,128)(2,1)S(1)}, u32[]{:S(2)}, u32[]{:S(2)}) collective-permute-start(bf16[128,768]{1,0:T(8,128)(2,1)S(1)} %collective-permute-done.5.refs_8_.refs_4_.refs_5_.refs_3_), channel_id=1, source_target_pairs={{0,4},{4,0},{8,12},{12,8},{16,20},{20,16},{24,28},{28,24},{1,5},{5... | collective-permute-start | bytes 589832 | tf_op jit(solution)/shard_map/ppermute | solution.py:40
  33.3 4.2 %copy-start.1 = (bf16[256,1024]{1,0:T(8,128)(2,1)S(1)}, bf16[256,1024]{1,0:T(8,128)(2,1)}, u32[]{:S(2)}) copy-start(bf16[256,1024]{1,0:T(8,128)(2,1)} %get-tuple-element.41.refs_1_) | copy-start | bytes 1572868
  33.3 5.2 %copy-start = (bf16[256,1024]{1,0:T(8,128)(2,1)S(1)}, bf16[256,1024]{1,0:T(8,128)(2,1)}, u32[]{:S(2)}) copy-start(bf16[256,1024]{1,0:T(8,128)(2,1)} %get-tuple-element.40.refs_0_) | copy-start | bytes 1572868
  33.3 5.2 %copy-start.2 = (bf16[256,512]{1,0:T(8,128)(2,1)S(1)}, bf16[256,512]{1,0:T(8,128)(2,1)}, u32[]{:S(2)}) copy-start(bf16[256,512]{1,0:T(8,128)(2,1)} %get-tuple-element.43.refs_2_) | copy-start | bytes 786436
  33.6 3.9 %collective-permute-start.7 = (bf16[128,768]{1,0:T(8,128)(2,1)S(1)}, bf16[128,768]{1,0:T(8,128)(2,1)S(1)}, u32[]{:S(2)}, u32[]{:S(2)}) collective-permute-start(bf16[128,768]{1,0:T(8,128)(2,1)S(1)} %get-tuple-element.80.refs_3_.refs_0_), channel_id=1, source_target_pairs={{0,4},{4,0},{8,12},{12,8},{16,20},{20,16},{24,28},{28,24},{1,5},{5... | collective-permute-start | bytes 589832 | tf_op jit(solution)/shard_map/ppermute | solution.py:40
  33.9 3.7 %collective-permute-start.8 = (bf16[128,768]{1,0:T(8,128)(2,1)S(1)}, bf16[128,768]{1,0:T(8,128)(2,1)S(1)}, u32[]{:S(2)}, u32[]{:S(2)}) collective-permute-start(bf16[128,768]{1,0:T(8,128)(2,1)S(1)} %get-tuple-element.79.refs_4_.refs_1_), channel_id=1, source_target_pairs={{0,4},{4,0},{8,12},{12,8},{16,20},{20,16},{24,28},{28,24},{1,5},{5... | collective-permute-start | bytes 589832 | tf_op jit(solution)/shard_map/ppermute | solution.py:40
  34.1 4.3 %collective-permute-start.15 = (bf16[128,768]{1,0:T(8,128)(2,1)S(1)}, bf16[128,768]{1,0:T(8,128)(2,1)S(1)}, u32[]{:S(2)}, u32[]{:S(2)}) collective-permute-start(bf16[128,768]{1,0:T(8,128)(2,1)S(1)} %get-tuple-element.78.refs_19_.refs_16_), channel_id=1, source_target_pairs={{0,4},{4,0},{8,12},{12,8},{16,20},{20,16},{24,28},{28,24},{1,5},{5... | collective-permute-start | bytes 589832 | tf_op jit(solution)/shard_map/ppermute | solution.py:40
  34.4 4.0 %collective-permute-start.16 = (bf16[128,768]{1,0:T(8,128)(2,1)S(1)}, bf16[128,768]{1,0:T(8,128)(2,1)S(1)}, u32[]{:S(2)}, u32[]{:S(2)}) collective-permute-start(bf16[128,768]{1,0:T(8,128)(2,1)S(1)} %get-tuple-element.77.refs_20_.refs_17_), channel_id=1, source_target_pairs={{0,4},{4,0},{8,12},{12,8},{16,20},{20,16},{24,28},{28,24},{1,5},{5... | collective-permute-start | bytes 589832 | tf_op jit(solution)/shard_map/ppermute | solution.py:40
  36.2 5.5 %collective-permute-start.19 = (bf16[256,256]{1,0:T(8,128)(2,1)S(1)}, bf16[256,256]{1,0:T(8,128)(2,1)S(1)}, u32[]{:S(2)}, u32[]{:S(2)}) collective-permute-start(bf16[256,256]{1,0:T(8,128)(2,1)S(1)} %get-tuple-element.59), channel_id=1, source_target_pairs={{0,1},{1,0},{2,3},{3,2},{4,5},{5,4},{6,7},{7,6},{8,9},{9,8},{10,11... | collective-permute-start | bytes 393224 | tf_op jit(solution)/shard_map/ppermute | solution.py:28
  37.5 30.3 %collective-permute-start.27 = (bf16[256,1024]{1,0:T(8,128)(2,1)S(1)}, bf16[256,1024]{1,0:T(8,128)(2,1)S(1)}, u32[]{:S(2)}, u32[]{:S(2)}) collective-permute-start(bf16[256,1024]{1,0:T(8,128)(2,1)S(1)} %copy-done.1), channel_id=1, source_target_pairs={{0,4},{4,0},{8,12},{12,8},{16,20},{20,16},{24,28},{28,24},{1,5},{5... | collective-permute-start | bytes 1572872 | tf_op jit(solution)/shard_map/ppermute | solution.py:40
  37.6 14.2 %collective-permute-start.18 = (bf16[256,512]{1,0:T(8,128)(2,1)S(1)}, bf16[256,512]{1,0:T(8,128)(2,1)S(1)}, u32[]{:S(2)}, u32[]{:S(2)}) collective-permute-start(bf16[256,512]{1,0:T(8,128)(2,1)S(1)} %get-tuple-element.57), channel_id=1, source_target_pairs={{0,1},{1,0},{2,3},{3,2},{4,5},{5,4},{6,7},{7,6},{8,9},{9,8},{10,11... | collective-permute-start | bytes 786440 | tf_op jit(solution)/shard_map/ppermute | solution.py:28
  38.5 10.8 %copy-start.5 = (bf16[1,256,512]{2,1,0:T(8,128)(2,1)S(1)}, bf16[1,256,512]{2,1,0:T(8,128)(2,1)}, u32[]{:S(2)}) copy-start(bf16[1,256,512]{2,1,0:T(8,128)(2,1)} %param.7) | copy-start | bytes 786436
  41.8 7.7 %collective-permute-start.20 = (bf16[256,256]{1,0:T(8,128)(2,1)S(1)}, bf16[256,256]{1,0:T(8,128)(2,1)S(1)}, u32[]{:S(2)}, u32[]{:S(2)}) collective-permute-start(bf16[256,256]{1,0:T(8,128)(2,1)S(1)} %add_convert_fusion.4.refs_2_), channel_id=1, source_target_pairs={{0,2},{1,3},{4,6},{5,7},{8,10},{9,11},{12,14},{13,15},{16,18},{17,... | collective-permute-start | bytes 393224 | tf_op jit(solution)/shard_map/ppermute | solution.py:53
  45.2 6.6 %collective-permute-start.21 = (bf16[256,256]{1,0:T(8,128)(2,1)S(1)}, bf16[256,256]{1,0:T(8,128)(2,1)S(1)}, u32[]{:S(2)}, u32[]{:S(2)}) collective-permute-start(bf16[256,256]{1,0:T(8,128)(2,1)S(1)} %add_convert_fusion.4.refs_2_), channel_id=1, source_target_pairs={{0,1},{1,2},{2,3},{4,5},{5,6},{6,7},{8,9},{9,10},{10,11},{12,13},{... | collective-permute-start | bytes 393224 | tf_op jit(solution)/shard_map/ppermute | solution.py:53
  49.4 24.9 %collective-permute-start.28 = (bf16[256,1536]{1,0:T(8,128)(2,1)S(1)}, bf16[256,1536]{1,0:T(8,128)(2,1)S(1)}, u32[]{:S(2)}, u32[]{:S(2)}) collective-permute-start(bf16[256,1536]{1,0:T(8,128)(2,1)S(1)} %collective-permute-done.6.refs_0_.refs_1_), channel_id=1, source_target_pairs={{0,4},{4,0},{8,12},{12,8},{16,20},{20,16},{24,28},{28,24},{1,5},{5... | collective-permute-start | bytes 2359304 | tf_op jit(solution)/shard_map/ppermute | solution.py:40
  58.1 6.9 %collective-permute-start.23 = (bf16[256,256]{1,0:T(8,128)(2,1)S(1)}, bf16[256,256]{1,0:T(8,128)(2,1)S(1)}, u32[]{:S(2)}, u32[]{:S(2)}) collective-permute-start(bf16[256,256]{1,0:T(8,128)(2,1)S(1)} %get-tuple-element.82), channel_id=1, source_target_pairs={{2,0},{3,1},{6,4},{7,5},{10,8},{11,9},{14,12},{15,13},{18,16},{19,... | collective-permute-start | bytes 393224 | tf_op jit(solution)/shard_map/ppermute | solution.py:53
  59.4 8.3 %collective-permute-start.22 = (bf16[256,256]{1,0:T(8,128)(2,1)S(1)}, bf16[256,256]{1,0:T(8,128)(2,1)S(1)}, u32[]{:S(2)}, u32[]{:S(2)}) collective-permute-start(bf16[256,256]{1,0:T(8,128)(2,1)S(1)} %get-tuple-element.81), channel_id=1, source_target_pairs={{1,0},{2,1},{3,2},{5,4},{6,5},{7,6},{9,8},{10,9},{11,10},{13,12},{... | collective-permute-start | bytes 393224 | tf_op jit(solution)/shard_map/ppermute | solution.py:53
  60.7 9.8 %collective-permute-start.24 = (bf16[256,512]{1,0:T(8,128)(2,1)S(1)}, bf16[256,512]{1,0:T(8,128)(2,1)S(1)}, u32[]{:S(2)}, u32[]{:S(2)}) collective-permute-start(bf16[256,512]{1,0:T(8,128)(2,1)S(1)} %get-tuple-element.61.dquery_ref.refs_6_), channel_id=1, source_target_pairs={{0,1},{1,0},{2,3},{3,2},{4,5},{5,4},{6,7},{7,6},{8,9},{9,8},{10,11... | collective-permute-start | bytes 786440 | tf_op jit(solution)/shard_map/ppermute | solution.py:28
  65.0 5.6 %collective-permute-start.29 = (bf16[256,512]{1,0:T(8,128)(2,1)S(1)}, bf16[256,512]{1,0:T(8,128)(2,1)S(1)}, u32[]{:S(2)}, u32[]{:S(2)}) collective-permute-start(bf16[256,512]{1,0:T(8,128)(2,1)S(1)} %collective-permute-done.17.refs_2_), channel_id=1, source_target_pairs={{0,4},{4,0},{8,12},{12,8},{16,20},{20,16},{24,28},{28,24},{1,5},{5... | collective-permute-start | bytes 786440 | tf_op jit(solution)/shard_map/ppermute | solution.py:40
  67.7 6.5 %collective-permute-start.30 = (bf16[256,512]{1,0:T(8,128)(2,1)S(1)}, bf16[256,512]{1,0:T(8,128)(2,1)S(1)}, u32[]{:S(2)}, u32[]{:S(2)}) collective-permute-start(bf16[256,512]{1,0:T(8,128)(2,1)S(1)} %get-tuple-element.61.dquery_ref.refs_6_), channel_id=1, source_target_pairs={{0,4},{4,0},{8,12},{12,8},{16,20},{20,16},{24,28},{28,24},{1,5},{5... | collective-permute-start | bytes 786440 | tf_op jit(solution)/shard_map/ppermute | solution.py:40
  67.8 6.5 %collective-permute-start.25 = (bf16[256,256]{1,0:T(8,128)(2,1)S(1)}, bf16[256,256]{1,0:T(8,128)(2,1)S(1)}, u32[]{:S(2)}, u32[]{:S(2)}) collective-permute-start(bf16[256,256]{1,0:T(8,128)(2,1)S(1)} %add_convert_fusion.3.dpair_ref.refs_7_.refs_14_), channel_id=1, source_target_pairs={{0,1},{1,0},{2,3},{3,2},{4,5},{5,4},{6,7},{7,6},{8,9},{9,8},{10,11... | collective-permute-start | bytes 393224 | tf_op jit(solution)/shard_map/ppermute | solution.py:28
  70.5 5.1 %collective-permute-start.32 = (bf16[256,512]{1,0:T(8,128)(2,1)S(1)}, bf16[256,512]{1,0:T(8,128)(2,1)S(1)}, u32[]{:S(2)}, u32[]{:S(2)}) collective-permute-start(bf16[256,512]{1,0:T(8,128)(2,1)S(1)} %collective-permute-done.24.dquery_ref.refs_8_), channel_id=1, source_target_pairs={{0,4},{4,0},{8,12},{12,8},{16,20},{20,16},{24,28},{28,24},{1,5},{5... | collective-permute-start | bytes 786440 | tf_op jit(solution)/shard_map/ppermute | solution.py:40
  70.5 3.7 %collective-permute-start.31 = (bf16[256,256]{1,0:T(8,128)(2,1)S(1)}, bf16[256,256]{1,0:T(8,128)(2,1)S(1)}, u32[]{:S(2)}, u32[]{:S(2)}) collective-permute-start(bf16[256,256]{1,0:T(8,128)(2,1)S(1)} %add_convert_fusion.3.dpair_ref.refs_7_.refs_14_), channel_id=1, source_target_pairs={{0,4},{4,0},{8,12},{12,8},{16,20},{20,16},{24,28},{28,24},{1,5},{5... | collective-permute-start | bytes 393224 | tf_op jit(solution)/shard_map/ppermute | solution.py:40
  74.3 1.3 %collective-permute-start.33 = (bf16[256,256]{1,0:T(8,128)(2,1)S(1)}, bf16[256,256]{1,0:T(8,128)(2,1)S(1)}, u32[]{:S(2)}, u32[]{:S(2)}) collective-permute-start(bf16[256,256]{1,0:T(8,128)(2,1)S(1)} %collective-permute-done.25.dpair_ref.refs_9_), channel_id=1, source_target_pairs={{0,4},{4,0},{8,12},{12,8},{16,20},{20,16},{24,28},{28,24},{1,5},{5... | collective-permute-start | bytes 393224 | tf_op jit(solution)/shard_map/ppermute | solution.py:40
  76.6 7.8 %collective-permute-start.39 = (bf16[128,768]{1,0:T(8,128)(2,1)S(1)}, bf16[128,768]{1,0:T(8,128)(2,1)S(1)}, u32[]{:S(2)}, u32[]{:S(2)}) collective-permute-start(bf16[128,768]{1,0:T(8,128)(2,1)S(1)} %get-tuple-element.76), channel_id=1, source_target_pairs={{0,2},{1,3},{2,0},{3,1},{4,6},{5,7},{6,4},{7,5},{8,10},{9,11},{10,... | collective-permute-start | bytes 589832 | tf_op jit(solution)/shard_map/ppermute | solution.py:35
  79.4 23.2 %collective-permute-start.26 = (bf16[256,1536]{1,0:T(8,128)(2,1)S(1)}, bf16[256,1536]{1,0:T(8,128)(2,1)S(1)}, u32[]{:S(2)}, u32[]{:S(2)}) collective-permute-start(bf16[256,1536]{1,0:T(8,128)(2,1)S(1)} %get-tuple-element.65), channel_id=1, source_target_pairs={{0,1},{1,0},{2,3},{3,2},{4,5},{5,4},{6,7},{7,6},{8,9},{9,8},{10,11... | collective-permute-start | bytes 2359304 | tf_op jit(solution)/shard_map/ppermute | solution.py:28
  79.7 8.9 %collective-permute-start.37 = (bf16[128,768]{1,0:T(8,128)(2,1)S(1)}, bf16[128,768]{1,0:T(8,128)(2,1)S(1)}, u32[]{:S(2)}, u32[]{:S(2)}) collective-permute-start(bf16[128,768]{1,0:T(8,128)(2,1)S(1)} %get-tuple-element.74), channel_id=1, source_target_pairs={{0,2},{1,3},{2,0},{3,1},{4,6},{5,7},{6,4},{7,5},{8,10},{9,11},{10,... | collective-permute-start | bytes 589832 | tf_op jit(solution)/shard_map/ppermute | solution.py:35
  82.4 10.5 %collective-permute-start.35 = (bf16[128,768]{1,0:T(8,128)(2,1)S(1)}, bf16[128,768]{1,0:T(8,128)(2,1)S(1)}, u32[]{:S(2)}, u32[]{:S(2)}) collective-permute-start(bf16[128,768]{1,0:T(8,128)(2,1)S(1)} %get-tuple-element.72), channel_id=1, source_target_pairs={{0,2},{1,3},{2,0},{3,1},{4,6},{5,7},{6,4},{7,5},{8,10},{9,11},{10,... | collective-permute-start | bytes 589832 | tf_op jit(solution)/shard_map/ppermute | solution.py:35
  82.9 14.4 %collective-permute-start.34 = (bf16[128,768]{1,0:T(8,128)(2,1)S(1)}, bf16[128,768]{1,0:T(8,128)(2,1)S(1)}, u32[]{:S(2)}, u32[]{:S(2)}) collective-permute-start(bf16[128,768]{1,0:T(8,128)(2,1)S(1)} %get-tuple-element.70), channel_id=1, source_target_pairs={{0,2},{1,3},{2,0},{3,1},{4,6},{5,7},{6,4},{7,5},{8,10},{9,11},{10,... | collective-permute-start | bytes 589832 | tf_op jit(solution)/shard_map/ppermute | solution.py:35
  84.5 12.9 %collective-permute-start.40 = (bf16[128,768]{1,0:T(8,128)(2,1)S(1)}, bf16[128,768]{1,0:T(8,128)(2,1)S(1)}, u32[]{:S(2)}, u32[]{:S(2)}) collective-permute-start(bf16[128,768]{1,0:T(8,128)(2,1)S(1)} %add_convert_fusion), channel_id=1, source_target_pairs={{0,16},{4,20},{8,24},{12,28},{16,0},{20,4},{24,8},{28,12},{1,17},{... | collective-permute-start | bytes 589832 | tf_op jit(solution)/shard_map/ppermute | solution.py:47
  88.7 9.2 %collective-permute-start.38 = (bf16[128,768]{1,0:T(8,128)(2,1)S(1)}, bf16[128,768]{1,0:T(8,128)(2,1)S(1)}, u32[]{:S(2)}, u32[]{:S(2)}) collective-permute-start(bf16[128,768]{1,0:T(8,128)(2,1)S(1)} %add_convert_fusion.1), channel_id=1, source_target_pairs={{0,24},{4,28},{8,0},{12,4},{16,8},{20,12},{24,16},{28,20},{1,25},{... | collective-permute-start | bytes 589832 | tf_op jit(solution)/shard_map/ppermute | solution.py:47
  92.9 8.9 %collective-permute-start.36 = (bf16[128,768]{1,0:T(8,128)(2,1)S(1)}, bf16[128,768]{1,0:T(8,128)(2,1)S(1)}, u32[]{:S(2)}, u32[]{:S(2)}) collective-permute-start(bf16[128,768]{1,0:T(8,128)(2,1)S(1)} %add_convert_fusion.2), channel_id=1, source_target_pairs={{0,8},{4,12},{8,16},{12,20},{16,24},{20,28},{24,0},{28,4},{1,9},{5... | collective-permute-start | bytes 589832 | tf_op jit(solution)/shard_map/ppermute | solution.py:47

commit v8 on v7

--- a/solution.py
+++ b/solution.py
@@ -245,15 +245,12 @@
     )(*parts, *given, after)
 
 
-def attend_kernel(
-    heads, back, docs_ref, q_ref, q_from_ref, cot_ref, *refs
-):
+def attend_kernel(heads, back, docs_ref, q_ref, q_from_ref, cot_ref, *refs):
     pair_refs, (out_ref, dq_ref, dpair_ref, dback_ref) = refs[: back + 1], refs[back + 1 :]
     rows = q_ref.shape[0]
     hd = HEAD_DIM
     scale = 1.0 / math.sqrt(hd)
     first = lax.axis_index("seq") * rows
-    base = first - back * rows
     total = (back + 1) * rows
 
     row_pos = first + lax.broadcasted_iota(jnp.int32, (1, rows), 1)
@@ -263,33 +260,56 @@
         end = start + docs_ref[d]
         start_of = jnp.where((row_pos >= start) & (row_pos < end), start, start_of)
         start = end
-    key_pos = base + lax.broadcasted_iota(jnp.int32, (total, rows), 0)
-    allowed = (key_pos >= start_of) & (key_pos <= row_pos)
+    key_pos = first - back * rows + lax.broadcasted_iota(jnp.int32, (total, rows), 0)
+    shut = jnp.where((key_pos >= start_of) & (key_pos <= row_pos), 0.0, -1e30)
 
     pairs = [r[...] for r in pair_refs]
     keys = jnp.concatenate([p[:, :hd] for p in pairs], axis=0)
     values = jnp.concatenate([p[:, hd:] for p in pairs], axis=0)
     keys_t, values_t = keys.T, values.T
-    dk = jnp.zeros((total, hd), F32)
-    dv = jnp.zeros((total, hd), F32)
+    sums = [jnp.zeros((total, hd), F32), jnp.zeros((total, hd), F32)]
+    cols = [slice(h * hd, (h + 1) * hd) for h in range(heads)]
+    state = {}
+
+    def products(h):
+        q = (q_ref[:, cols[h]] + q_from_ref[:, cols[h]].astype(F32)).astype(BF16)
+        cot = cot_ref[:, cols[h]]
+        state[h] = [q, cot, dot(keys, q, NT), dot(values, cot, NT)]
+
+    def softmax(h):
+        logits = state[h][2] * (scale * math.log2(math.e)) + shut
+        raised = jnp.exp2(logits - jnp.max(logits, axis=0, keepdims=True))
+        probs = raised * (1.0 / jnp.sum(raised, axis=0, keepdims=True))
+        state[h][2] = probs
+        state[h].append(probs.astype(BF16))
+
+    def outputs(h):
+        _, cot, _, _, probs_half = state[h]
+        out_t = dot(values_t, probs_half).astype(BF16)
+        out_ref[:, cols[h]] = out_t.T
+        state[h].append(jnp.sum(cot.T.astype(F32) * out_t.astype(F32), axis=0, keepdims=True))
+
+    def score_grads(h):
+        _, _, probs, dprobs, _, delta = state[h]
+        state[h][3] = (probs * (dprobs - delta)).astype(BF16)
+
+    def grads(h):
+        q, cot, _, dscores, probs_half, _ = state.pop(h)
+        dq_ref[:, cols[h]] = (dot(keys_t, dscores) * scale).astype(BF16).T
+        sums[0] = sums[0] + dot(dscores, q)
+        sums[1] = sums[1] + dot(probs_half, cot)
+
+    products(0)
     for h in range(heads):
-        cols = slice(h * hd, (h + 1) * hd)
-        q = (q_ref[:, cols] + q_from_ref[:, cols].astype(F32)).astype(BF16)
-        cot = cot_ref[:, cols]
-        logits = jnp.where(allowed, dot(keys, q, NT) * scale, -1e30)
-        top = jnp.max(logits, axis=0, keepdims=True)
-        raised = jnp.exp(logits - top)
-        probs = raised * (1.0 / jnp.sum(raised, axis=0, keepdims=True))
-        probs_half = probs.astype(BF16)
-        out_t = dot(values_t, probs_half).astype(BF16)
-        cot_t = cot.T
-        delta = jnp.sum(cot_t.astype(F32) * out_t.astype(F32), axis=0, keepdims=True)
-        dscores = (probs * (dot(values, cot, NT) - delta)).astype(BF16)
-        out_ref[:, cols] = out_t.T
-        dq_ref[:, cols] = (dot(keys_t, dscores) * scale).astype(BF16).T
-        dk += dot(dscores, q)
-        dv += dot(probs_half, cot)
-    both = jnp.concatenate([dk * scale, dv], axis=1)
+        softmax(h)
+        if h + 1 < heads:
+            products(h + 1)
+        outputs(h)
+        if h:
+            grads(h - 1)
+        score_grads(h)
+    grads(heads - 1)
+    both = jnp.concatenate([sums[0] * scale, sums[1]], axis=1)
     dpair_ref[...] = both[back * rows :]
     dback_ref[...] = both[: back * rows].astype(BF16)
 

time: 104 us -> 102 us (0.981)
  Pallas kernels: 17.1 us -> 14.9 us
    pallas_call x1, Pallas kernels: 6.31 us -> 4.1 us  [attend(): pl.pallas_call(functools.partial(attend_kernel, width // HEAD_DIM, back),...]
  transfers between devices with their start and end apart: 41 -> 41, of which waited for: 20 -> 20; matrix products, arithmetic and copies ran while one was open for 1% -> 1% of each run, Pallas kernels for 14% -> 12%
where the time goes in v8:
time: 102 us
  starting transfers between devices  45 us (44%)
  waiting for transfers between devices  38.6 us (38%)
  Pallas kernels  14.9 us (15%)
  other arithmetic  1.44 us (1%)
  local copies, waits for them, and re-layouts  1.13 us (1%)
    ppermute x6, waiting for transfers between devices, shift_chip(): return lax.ppermute(array, 'dp', pairs)  16.4 us
    ppermute x6, starting transfers between devices, shift_chip(): return lax.ppermute(array, 'dp', pairs)  12 us
    ppermute x7, starting transfers between devices, shift_rest(): return lax.ppermute(array, 'seq', pairs)  10.2 us
    ppermute x4, starting transfers between devices, shift_seq(): return lax.ppermute(array, 'seq', pairs)  10.1 us
    ppermute x7, starting transfers between devices, swap_x(): return lax.ppermute(array, 'seq', [(i, i ^ 1) for i in range(count)])  9.91 us
    ppermute x7, waiting for transfers between devices, shift_rest(): return lax.ppermute(array, 'seq', pairs)  7.46 us
    ppermute x7, waiting for transfers between devices, swap_x(): return lax.ppermute(array, 'seq', [(i, i ^ 1) for i in range(count)])  6.75 us
    ppermute x4, waiting for transfers between devices, shift_seq(): return lax.ppermute(array, 'seq', pairs)  6.16 us
  transfers between devices with their start and end apart: 41, of which 20 were waited for; matrix products, arithmetic and copies ran while one was open for 1% of the time, Pallas kernels for 12%

profile of v8, /device:TPU:0, one launch (start us, length us, event | category | flops | bytes accessed | tf_op | source)
XLA Modules:
  0.0 102.0 jit_solution(11977778239610154905)
XLA Ops:
  0.7 1.0 constant_dynamic-slice_fusion
  1.7 3.1 %collective-permute-start.1 = (bf16[128,768]{1,0:T(8,128)(2,1)S(1)}, bf16[128,768]{1,0:T(8,128)(2,1)S(1)}, u32[]{:S(2)}, u32[]{:S(2)}) collective-permute-start(bf16[128,768]{1,0:T(8,128)(2,1)S(1)} %constant_dynamic-slice_fusion), channel_id=1, source_target_pairs={{0,8},{4,12},{8,16},{12,20},{16,24},{20,28},{24,0},{28,4},{1,9},{5... | collective-permute-start | bytes 589832 | tf_op jit(solution)/shard_map/ppermute | solution.py:47
  4.8 2.8 %split_tokens.1 = (bf16[256,1024]{1,0:T(8,128)(2,1)}, bf16[256,1024]{1,0:T(8,128)(2,1)}, bf16[256,1536]{1,0:T(8,128)(2,1)}, bf16[256,512]{1,0:T(8,128)(2,1)}) custom-call(bf16[256,4096]{1,0:T(8,128)(2,1)} %bitcast.26), custom_call_target="tpu_custom_call" | custom-call | tf_op jit(solution)/shard_map/split_tokens/pallas_call | solution.py:105
  7.6 4.1 %collective-permute-done.1.refs_5_.refs_1_.refs_2_.refs_0_ = bf16[128,768]{1,0:T(8,128)(2,1)S(1)} collective-permute-done((bf16[128,768]{1,0:T(8,128)(2,1)S(1)}, bf16[128,768]{1,0:T(8,128)(2,1)S(1)}, u32[]{:S(2)}, u32[]{:S(2)}) %collective-permute-start.1) | collective-permute-done | bytes 196640 | tf_op jit(solution)/shard_map/ppermute | solution.py:47
  11.7 1.5 %collective-permute-start.6 = (bf16[256,1536]{1,0:T(8,128)(2,1)}, bf16[256,1536]{1,0:T(8,128)(2,1)S(1)}, u32[]{:S(2)}, u32[]{:S(2)}) collective-permute-start(bf16[256,1536]{1,0:T(8,128)(2,1)} %get-tuple-element.50), channel_id=1, source_target_pairs={{0,1},{1,0},{2,3},{3,2},{4,5},{5,4},{6,7},{7,6},{8,9},{9,8},{10,11... | collective-permute-start | bytes 2359304 | tf_op jit(solution)/shard_map/ppermute | solution.py:28
  13.2 1.7 %collective-permute-start.3 = (bf16[128,768]{1,0:T(8,128)(2,1)S(1)}, bf16[128,768]{1,0:T(8,128)(2,1)S(1)}, u32[]{:S(2)}, u32[]{:S(2)}) collective-permute-start(bf16[128,768]{1,0:T(8,128)(2,1)S(1)} %constant_dynamic-slice_fusion), channel_id=1, source_target_pairs={{0,24},{4,28},{8,0},{12,4},{16,8},{20,12},{24,16},{28,20},{1,25},{... | collective-permute-start | bytes 589832 | tf_op jit(solution)/shard_map/ppermute | solution.py:47
  14.9 1.5 %collective-permute-start.2 = (bf16[128,768]{1,0:T(8,128)(2,1)S(1)}, bf16[128,768]{1,0:T(8,128)(2,1)S(1)}, u32[]{:S(2)}, u32[]{:S(2)}) collective-permute-start(bf16[128,768]{1,0:T(8,128)(2,1)S(1)} %collective-permute-done.1.refs_5_.refs_1_.refs_2_.refs_0_), channel_id=1, source_target_pairs={{0,2},{1,3},{2,0},{3,1},{4,6},{5,7},{6,4},{7,5},{8,10},{9,11},{10,... | collective-permute-start | bytes 589832 | tf_op jit(solution)/shard_map/ppermute | solution.py:35
  16.4 3.6 %collective-permute-done.3.refs_9_.refs_5_.refs_6_.refs_4_ = bf16[128,768]{1,0:T(8,128)(2,1)S(1)} collective-permute-done((bf16[128,768]{1,0:T(8,128)(2,1)S(1)}, bf16[128,768]{1,0:T(8,128)(2,1)S(1)}, u32[]{:S(2)}, u32[]{:S(2)}) %collective-permute-start.3) | collective-permute-done | bytes 196640 | tf_op jit(solution)/shard_map/ppermute | solution.py:47
  20.1 1.5 %collective-permute-start.4 = (bf16[128,768]{1,0:T(8,128)(2,1)S(1)}, bf16[128,768]{1,0:T(8,128)(2,1)S(1)}, u32[]{:S(2)}, u32[]{:S(2)}) collective-permute-start(bf16[128,768]{1,0:T(8,128)(2,1)S(1)} %collective-permute-done.3.refs_9_.refs_5_.refs_6_.refs_4_), channel_id=1, source_target_pairs={{0,2},{1,3},{2,0},{3,1},{4,6},{5,7},{6,4},{7,5},{8,10},{9,11},{10,... | collective-permute-start | bytes 589832 | tf_op jit(solution)/shard_map/ppermute | solution.py:35
  21.6 0.5 collective-permute-start.17
  22.3 4.1 %collective-permute-done.refs_7_.refs_3_.refs_4_.refs_2_ = bf16[128,768]{1,0:T(8,128)(2,1)S(1)} collective-permute-done((bf16[128,768]{1,0:T(8,128)(2,1)S(1)}, bf16[128,768]{1,0:T(8,128)(2,1)S(1)}, u32[]{:S(2)}, u32[]{:S(2)}) %collective-permute-start) | collective-permute-done | bytes 196640 | tf_op jit(solution)/shard_map/ppermute | solution.py:47
  26.4 1.5 %collective-permute-start.5 = (bf16[128,768]{1,0:T(8,128)(2,1)S(1)}, bf16[128,768]{1,0:T(8,128)(2,1)S(1)}, u32[]{:S(2)}, u32[]{:S(2)}) collective-permute-start(bf16[128,768]{1,0:T(8,128)(2,1)S(1)} %collective-permute-done.refs_7_.refs_3_.refs_4_.refs_2_), channel_id=1, source_target_pairs={{0,2},{1,3},{2,0},{3,1},{4,6},{5,7},{6,4},{7,5},{8,10},{9,11},{10,... | collective-permute-start | bytes 589832 | tf_op jit(solution)/shard_map/ppermute | solution.py:35
  28.0 0.5 collective-permute-start.10
  28.5 3.7 %collective-permute-done.5.refs_8_.refs_4_.refs_5_.refs_3_ = bf16[128,768]{1,0:T(8,128)(2,1)S(1)} collective-permute-done((bf16[128,768]{1,0:T(8,128)(2,1)S(1)}, bf16[128,768]{1,0:T(8,128)(2,1)S(1)}, u32[]{:S(2)}, u32[]{:S(2)}) %collective-permute-start.5) | collective-permute-done | bytes 196640 | tf_op jit(solution)/shard_map/ppermute | solution.py:35
  34.7 0.8 project.3
  35.4 0.8 collective-permute-done.17.refs_2_
  36.2 1.2 %collective-permute-start.19 = (bf16[256,256]{1,0:T(8,128)(2,1)S(1)}, bf16[256,256]{1,0:T(8,128)(2,1)S(1)}, u32[]{:S(2)}, u32[]{:S(2)}) collective-permute-start(bf16[256,256]{1,0:T(8,128)(2,1)S(1)} %get-tuple-element.59), channel_id=1, source_target_pairs={{0,1},{1,0},{2,3},{3,2},{4,5},{5,4},{6,7},{7,6},{8,9},{9,8},{10,11... | collective-permute-start | bytes 393224 | tf_op jit(solution)/shard_map/ppermute | solution.py:28
  37.6 0.8 collective-permute-start.18
  38.5 1.2 %project.2 = (f32[256,512]{1,0:T(8,128)S(1)}, f32[256,256]{1,0:T(8,128)S(1)}) custom-call(bf16[256,1024]{1,0:T(8,128)(2,1)S(1)} %copy-done, bf16[256,1024]{1,0:T(8,128)(2,1)S(1)} %copy-done.1, bf16[256,512]{1,0:T(8,128)(2,1)S(1)} %copy-done.2, bf16[128,768]{1,0:T(8,128)(2,1)S(1)} %get-tuple-element.80.refs_3_.refs_0_, ...), custom_call_target="tpu_custom_call" | custom-call | tf_op jit(solution)/shard_map/project/pallas_call | solution.py:172
  39.7 2.1 %collective-permute-done.19 = bf16[256,256]{1,0:T(8,128)(2,1)S(1)} collective-permute-done((bf16[256,256]{1,0:T(8,128)(2,1)S(1)}, bf16[256,256]{1,0:T(8,128)(2,1)S(1)}, u32[]{:S(2)}, u32[]{:S(2)}) %collective-permute-start.19) | collective-permute-done | bytes 131104 | tf_op jit(solution)/shard_map/ppermute | solution.py:28
  41.8 3.4 %collective-permute-start.20 = (bf16[256,256]{1,0:T(8,128)(2,1)S(1)}, bf16[256,256]{1,0:T(8,128)(2,1)S(1)}, u32[]{:S(2)}, u32[]{:S(2)}) collective-permute-start(bf16[256,256]{1,0:T(8,128)(2,1)S(1)} %add_convert_fusion.4.refs_2_), channel_id=1, source_target_pairs={{0,2},{1,3},{4,6},{5,7},{8,10},{9,11},{12,14},{13,15},{16,18},{17,... | collective-permute-start | bytes 393224 | tf_op jit(solution)/shard_map/ppermute | solution.py:53
  45.2 4.1 %collective-permute-start.21 = (bf16[256,256]{1,0:T(8,128)(2,1)S(1)}, bf16[256,256]{1,0:T(8,128)(2,1)S(1)}, u32[]{:S(2)}, u32[]{:S(2)}) collective-permute-start(bf16[256,256]{1,0:T(8,128)(2,1)S(1)} %add_convert_fusion.4.refs_2_), channel_id=1, source_target_pairs={{0,1},{1,2},{2,3},{4,5},{5,6},{6,7},{8,9},{9,10},{10,11},{12,13},{... | collective-permute-start | bytes 393224 | tf_op jit(solution)/shard_map/ppermute | solution.py:53
  49.5 2.3 %collective-permute-done.21.refs_1_ = bf16[256,256]{1,0:T(8,128)(2,1)S(1)} collective-permute-done((bf16[256,256]{1,0:T(8,128)(2,1)S(1)}, bf16[256,256]{1,0:T(8,128)(2,1)S(1)}, u32[]{:S(2)}, u32[]{:S(2)}) %collective-permute-start.21) | collective-permute-done | bytes 131104 | tf_op jit(solution)/shard_map/ppermute | solution.py:53
  51.8 4.1 %attend.1 = (bf16[256,512]{1,0:T(8,128)(2,1)}, bf16[256,512]{1,0:T(8,128)(2,1)S(1)}, f32[256,256]{1,0:T(8,128)S(1)}, bf16[512,256]{1,0:T(8,128)(2,1)S(1)}) custom-call(s32[8]{0:T(128)S(1)} %bitcast.25, f32[256,512]{1,0:T(8,128)S(1)} %get-tuple-element.54.q_ref, bf16[256,512]{1,0:T(8,128)(2,1)S(1)} %collective-permute-done.18.q_from_ref, ...), custom_call_target="tpu_custom_call" | custom-call | tf_op jit(solution)/shard_map/attend/pallas_call | solution.py:321
  55.9 1.3 %collective-permute-start.23 = (bf16[256,256]{1,0:T(8,128)(2,1)S(1)}, bf16[256,256]{1,0:T(8,128)(2,1)S(1)}, u32[]{:S(2)}, u32[]{:S(2)}) collective-permute-start(bf16[256,256]{1,0:T(8,128)(2,1)S(1)} %get-tuple-element.82), channel_id=1, source_target_pairs={{2,0},{3,1},{6,4},{7,5},{10,8},{11,9},{14,12},{15,13},{18,16},{19,... | collective-permute-start | bytes 393224 | tf_op jit(solution)/shard_map/ppermute | solution.py:53
  57.2 1.3 %collective-permute-start.22 = (bf16[256,256]{1,0:T(8,128)(2,1)S(1)}, bf16[256,256]{1,0:T(8,128)(2,1)S(1)}, u32[]{:S(2)}, u32[]{:S(2)}) collective-permute-start(bf16[256,256]{1,0:T(8,128)(2,1)S(1)} %get-tuple-element.81), channel_id=1, source_target_pairs={{1,0},{2,1},{3,2},{5,4},{6,5},{7,6},{9,8},{10,9},{11,10},{13,12},{... | collective-permute-start | bytes 393224 | tf_op jit(solution)/shard_map/ppermute | solution.py:53
  58.5 3.1 %collective-permute-start.24 = (bf16[256,512]{1,0:T(8,128)(2,1)S(1)}, bf16[256,512]{1,0:T(8,128)(2,1)S(1)}, u32[]{:S(2)}, u32[]{:S(2)}) collective-permute-start(bf16[256,512]{1,0:T(8,128)(2,1)S(1)} %get-tuple-element.61.dquery_ref.refs_6_), channel_id=1, source_target_pairs={{0,1},{1,0},{2,3},{3,2},{4,5},{5,4},{6,7},{7,6},{8,9},{9,8},{10,11... | collective-permute-start | bytes 786440 | tf_op jit(solution)/shard_map/ppermute | solution.py:28
  61.6 1.1 %collective-permute-done.23 = bf16[256,256]{1,0:T(8,128)(2,1)S(1)} collective-permute-done((bf16[256,256]{1,0:T(8,128)(2,1)S(1)}, bf16[256,256]{1,0:T(8,128)(2,1)S(1)}, u32[]{:S(2)}, u32[]{:S(2)}) %collective-permute-start.23) | collective-permute-done | bytes 131104 | tf_op jit(solution)/shard_map/ppermute | solution.py:53
  62.8 2.8 %collective-permute-done.22 = bf16[256,256]{1,0:T(8,128)(2,1)S(1)} collective-permute-done((bf16[256,256]{1,0:T(8,128)(2,1)S(1)}, bf16[256,256]{1,0:T(8,128)(2,1)S(1)}, u32[]{:S(2)}, u32[]{:S(2)}) %collective-permute-start.22) | collective-permute-done | bytes 131104 | tf_op jit(solution)/shard_map/ppermute | solution.py:53
  65.6 2.3 %collective-permute-start.25 = (bf16[256,256]{1,0:T(8,128)(2,1)S(1)}, bf16[256,256]{1,0:T(8,128)(2,1)S(1)}, u32[]{:S(2)}, u32[]{:S(2)}) collective-permute-start(bf16[256,256]{1,0:T(8,128)(2,1)S(1)} %add_convert_fusion.3.dpair_ref.refs_7_.refs_14_), channel_id=1, source_target_pairs={{0,1},{1,0},{2,3},{3,2},{4,5},{5,4},{6,7},{7,6},{8,9},{9,8},{10,11... | collective-permute-start | bytes 393224 | tf_op jit(solution)/shard_map/ppermute | solution.py:28
  68.3 0.5 collective-permute-start.31
  68.8 3.2 %collective-permute-done.25.dpair_ref.refs_9_ = bf16[256,256]{1,0:T(8,128)(2,1)S(1)} collective-permute-done((bf16[256,256]{1,0:T(8,128)(2,1)S(1)}, bf16[256,256]{1,0:T(8,128)(2,1)S(1)}, u32[]{:S(2)}, u32[]{:S(2)}) %collective-permute-start.25) | collective-permute-done | bytes 131104 | tf_op jit(solution)/shard_map/ppermute | solution.py:28
  72.1 1.3 %collective-permute-done.33.refs_13_ = bf16[256,256]{1,0:T(8,128)(2,1)S(1)} collective-permute-done((bf16[256,256]{1,0:T(8,128)(2,1)S(1)}, bf16[256,256]{1,0:T(8,128)(2,1)S(1)}, u32[]{:S(2)}, u32[]{:S(2)}) %collective-permute-start.33) | collective-permute-done | bytes 131104 | tf_op jit(solution)/shard_map/ppermute | solution.py:40
  73.4 1.0 %weight_terms.3 = (f32[128,768]{1,0:T(8,128)S(1)}, bf16[128,768]{1,0:T(8,128)(2,1)S(1)}, f32[128,768]{1,0:T(8,128)S(1)}, bf16[128,768]{1,0:T(8,128)(2,1)S(1)}) custom-call(bf16[256,1024]{1,0:T(8,128)(2,1)S(1)} %copy-done, bf16[256,1536]{1,0:T(8,128)(2,1)S(1)} %collective-permute-done.6.refs_0_.refs_1_, bf16[256,512]{1,0:T(8,128)(2,1)S(1)} %collective-permute-done.17.refs_2_, ...), custom_call_target="tpu_custom_call" | custom-call | tf_op jit(solution)/shard_map/weight_terms/pallas_call | solution.py:238
  74.4 1.9 %collective-permute-start.39 = (bf16[128,768]{1,0:T(8,128)(2,1)S(1)}, bf16[128,768]{1,0:T(8,128)(2,1)S(1)}, u32[]{:S(2)}, u32[]{:S(2)}) collective-permute-start(bf16[128,768]{1,0:T(8,128)(2,1)S(1)} %get-tuple-element.76), channel_id=1, source_target_pairs={{0,2},{1,3},{2,0},{3,1},{4,6},{5,7},{6,4},{7,5},{8,10},{9,11},{10,... | collective-permute-start | bytes 589832 | tf_op jit(solution)/shard_map/ppermute | solution.py:35
  76.4 0.8 width_grad.3
  77.5 1.6 %collective-permute-start.37 = (bf16[128,768]{1,0:T(8,128)(2,1)S(1)}, bf16[128,768]{1,0:T(8,128)(2,1)S(1)}, u32[]{:S(2)}, u32[]{:S(2)}) collective-permute-start(bf16[128,768]{1,0:T(8,128)(2,1)S(1)} %get-tuple-element.74), channel_id=1, source_target_pairs={{0,2},{1,3},{2,0},{3,1},{4,6},{5,7},{6,4},{7,5},{8,10},{9,11},{10,... | collective-permute-start | bytes 589832 | tf_op jit(solution)/shard_map/ppermute | solution.py:35
  79.1 1.0 %weight_terms.2 = (f32[128,768]{1,0:T(8,128)S(1)}, bf16[128,768]{1,0:T(8,128)(2,1)S(1)}, f32[128,768]{1,0:T(8,128)S(1)}, bf16[128,768]{1,0:T(8,128)(2,1)S(1)}) custom-call(bf16[256,1024]{1,0:T(8,128)(2,1)S(1)} %copy-done, bf16[256,1536]{1,0:T(8,128)(2,1)S(1)} %collective-permute-done.6.refs_0_.refs_1_, bf16[256,512]{1,0:T(8,128)(2,1)S(1)} %collective-permute-done.17.refs_2_, ...), custom_call_target="tpu_custom_call" | custom-call | tf_op jit(solution)/shard_map/weight_terms/pallas_call | solution.py:238
  80.6 1.6 %collective-permute-start.34 = (bf16[128,768]{1,0:T(8,128)(2,1)S(1)}, bf16[128,768]{1,0:T(8,128)(2,1)S(1)}, u32[]{:S(2)}, u32[]{:S(2)}) collective-permute-start(bf16[128,768]{1,0:T(8,128)(2,1)S(1)} %get-tuple-element.70), channel_id=1, source_target_pairs={{0,2},{1,3},{2,0},{3,1},{4,6},{5,7},{6,4},{7,5},{8,10},{9,11},{10,... | collective-permute-start | bytes 589832 | tf_op jit(solution)/shard_map/ppermute | solution.py:35
  82.3 1.9 %collective-permute-start.40 = (bf16[128,768]{1,0:T(8,128)(2,1)S(1)}, bf16[128,768]{1,0:T(8,128)(2,1)S(1)}, u32[]{:S(2)}, u32[]{:S(2)}) collective-permute-start(bf16[128,768]{1,0:T(8,128)(2,1)S(1)} %add_convert_fusion), channel_id=1, source_target_pairs={{0,16},{4,20},{8,24},{12,28},{16,0},{20,4},{24,8},{28,12},{1,17},{... | collective-permute-start | bytes 589832 | tf_op jit(solution)/shard_map/ppermute | solution.py:47
  84.2 2.3 %collective-permute-done.37 = bf16[128,768]{1,0:T(8,128)(2,1)S(1)} collective-permute-done((bf16[128,768]{1,0:T(8,128)(2,1)S(1)}, bf16[128,768]{1,0:T(8,128)(2,1)S(1)}, u32[]{:S(2)}, u32[]{:S(2)}) %collective-permute-start.37) | collective-permute-done | bytes 196640 | tf_op jit(solution)/shard_map/ppermute | solution.py:35
  86.5 2.6 %collective-permute-start.38 = (bf16[128,768]{1,0:T(8,128)(2,1)S(1)}, bf16[128,768]{1,0:T(8,128)(2,1)S(1)}, u32[]{:S(2)}, u32[]{:S(2)}) collective-permute-start(bf16[128,768]{1,0:T(8,128)(2,1)S(1)} %add_convert_fusion.1), channel_id=1, source_target_pairs={{0,24},{4,28},{8,0},{12,4},{16,8},{20,12},{24,16},{28,20},{1,25},{... | collective-permute-start | bytes 589832 | tf_op jit(solution)/shard_map/ppermute | solution.py:47
  89.1 1.5 %collective-permute-done.35 = bf16[128,768]{1,0:T(8,128)(2,1)S(1)} collective-permute-done((bf16[128,768]{1,0:T(8,128)(2,1)S(1)}, bf16[128,768]{1,0:T(8,128)(2,1)S(1)}, u32[]{:S(2)}, u32[]{:S(2)}) %collective-permute-start.35) | collective-permute-done | bytes 196640 | tf_op jit(solution)/shard_map/ppermute | solution.py:35
  90.7 2.7 %collective-permute-start.36 = (bf16[128,768]{1,0:T(8,128)(2,1)S(1)}, bf16[128,768]{1,0:T(8,128)(2,1)S(1)}, u32[]{:S(2)}, u32[]{:S(2)}) collective-permute-start(bf16[128,768]{1,0:T(8,128)(2,1)S(1)} %add_convert_fusion.2), channel_id=1, source_target_pairs={{0,8},{4,12},{8,16},{12,20},{16,24},{20,28},{24,0},{28,4},{1,9},{5... | collective-permute-start | bytes 589832 | tf_op jit(solution)/shard_map/ppermute | solution.py:47
  93.4 1.6 %width_grad.2 = (bf16[256,2048]{1,0:T(8,128)(2,1)S(1)}, bf16[256,512]{1,0:T(8,128)(2,1)S(1)}, bf16[16,128]{1,0:T(8,128)(2,1)}) custom-call(bf16[256,512]{1,0:T(8,128)(2,1)S(1)} %get-tuple-element.61.dquery_ref.refs_6_, bf16[256,256]{1,0:T(8,128)(2,1)S(1)} %add_convert_fusion.3.dpair_ref.refs_7_.refs_14_, ...), custom_call_target="tpu_custom_call" | custom-call | tf_op jit(solution)/shard_map/width_grad/pallas_call | solution.py:199
  95.7 3.9 %collective-permute-done.36 = bf16[128,768]{1,0:T(8,128)(2,1)S(1)} collective-permute-done((bf16[128,768]{1,0:T(8,128)(2,1)S(1)}, bf16[128,768]{1,0:T(8,128)(2,1)S(1)}, u32[]{:S(2)}, u32[]{:S(2)}) %collective-permute-start.36) | collective-permute-done | bytes 196640 | tf_op jit(solution)/shard_map/ppermute | solution.py:47
  99.5 0.9 convert_add_fusion
  100.4 1.6 %merge_parts.1 = bf16[256,4096]{1,0:T(8,128)(2,1)} custom-call(bf16[256,2048]{1,0:T(8,128)(2,1)S(1)} %get-tuple-element.64.refs_0_, bf16[256,1536]{1,0:T(8,128)(2,1)S(1)} %collective-permute-done.26.refs_1_, bf16[256,512]{1,0:T(8,128)(2,1)S(1)} %get-tuple-element.66.refs_2_), custom_call_target="tpu_custom_call" | custom-call | tf_op jit(solution)/shard_map/merge_parts/pallas_call | solution.py:138
  (72 shorter events, 5.1 us)
Async XLA Ops:
  0.6 32.6 %copy-start.4 = (bf16[512,768]{1,0:T(8,128)(2,1)S(1)}, bf16[512,768]{1,0:T(8,128)(2,1)}, u32[]{:S(2)}) copy-start(bf16[512,768]{1,0:T(8,128)(2,1)} %param.6) | copy-start | bytes 2359300
  0.6 21.5 %copy-start.3 = (s32[1,8]{1,0:T(1,128)S(1)}, s32[1,8]{1,0:T(1,128)}, u32[]{:S(2)}) copy-start(s32[1,8]{1,0:T(1,128)} %param.8) | copy-start | bytes 100
  0.7 32.5 %copy-start.6 = (s32[1,8]{1,0:T(1,128)S(1)}, s32[1,8]{1,0:T(1,128)}, u32[]{:S(2)}) copy-start(s32[1,8]{1,0:T(1,128)} %param.9) | copy-start | bytes 100
  1.7 10.0 %collective-permute-start.1 = (bf16[128,768]{1,0:T(8,128)(2,1)S(1)}, bf16[128,768]{1,0:T(8,128)(2,1)S(1)}, u32[]{:S(2)}, u32[]{:S(2)}) collective-permute-start(bf16[128,768]{1,0:T(8,128)(2,1)S(1)} %constant_dynamic-slice_fusion), channel_id=1, source_target_pairs={{0,8},{4,12},{8,16},{12,20},{16,24},{20,28},{24,0},{28,4},{1,9},{5... | collective-permute-start | bytes 589832 | tf_op jit(solution)/shard_map/ppermute | solution.py:47
  11.7 20.7 %collective-permute-start.6 = (bf16[256,1536]{1,0:T(8,128)(2,1)}, bf16[256,1536]{1,0:T(8,128)(2,1)S(1)}, u32[]{:S(2)}, u32[]{:S(2)}) collective-permute-start(bf16[256,1536]{1,0:T(8,128)(2,1)} %get-tuple-element.50), channel_id=1, source_target_pairs={{0,1},{1,0},{2,3},{3,2},{4,5},{5,4},{6,7},{7,6},{8,9},{9,8},{10,11... | collective-permute-start | bytes 2359304 | tf_op jit(solution)/shard_map/ppermute | solution.py:28
  13.2 6.9 %collective-permute-start.3 = (bf16[128,768]{1,0:T(8,128)(2,1)S(1)}, bf16[128,768]{1,0:T(8,128)(2,1)S(1)}, u32[]{:S(2)}, u32[]{:S(2)}) collective-permute-start(bf16[128,768]{1,0:T(8,128)(2,1)S(1)} %constant_dynamic-slice_fusion), channel_id=1, source_target_pairs={{0,24},{4,28},{8,0},{12,4},{16,8},{20,12},{24,16},{28,20},{1,25},{... | collective-permute-start | bytes 589832 | tf_op jit(solution)/shard_map/ppermute | solution.py:47
  14.9 11.5 %collective-permute-start = (bf16[128,768]{1,0:T(8,128)(2,1)S(1)}, bf16[128,768]{1,0:T(8,128)(2,1)S(1)}, u32[]{:S(2)}, u32[]{:S(2)}) collective-permute-start(bf16[128,768]{1,0:T(8,128)(2,1)S(1)} %constant_dynamic-slice_fusion), channel_id=1, source_target_pairs={{0,16},{4,20},{8,24},{12,28},{16,0},{20,4},{24,8},{28,12},{1,17},{... | collective-permute-start | bytes 589832 | tf_op jit(solution)/shard_map/ppermute | solution.py:47
  14.9 11.5 %collective-permute-start.2 = (bf16[128,768]{1,0:T(8,128)(2,1)S(1)}, bf16[128,768]{1,0:T(8,128)(2,1)S(1)}, u32[]{:S(2)}, u32[]{:S(2)}) collective-permute-start(bf16[128,768]{1,0:T(8,128)(2,1)S(1)} %collective-permute-done.1.refs_5_.refs_1_.refs_2_.refs_0_), channel_id=1, source_target_pairs={{0,2},{1,3},{2,0},{3,1},{4,6},{5,7},{6,4},{7,5},{8,10},{9,11},{10,... | collective-permute-start | bytes 589832 | tf_op jit(solution)/shard_map/ppermute | solution.py:35
  20.1 6.4 %collective-permute-start.4 = (bf16[128,768]{1,0:T(8,128)(2,1)S(1)}, bf16[128,768]{1,0:T(8,128)(2,1)S(1)}, u32[]{:S(2)}, u32[]{:S(2)}) collective-permute-start(bf16[128,768]{1,0:T(8,128)(2,1)S(1)} %collective-permute-done.3.refs_9_.refs_5_.refs_6_.refs_4_), channel_id=1, source_target_pairs={{0,2},{1,3},{2,0},{3,1},{4,6},{5,7},{6,4},{7,5},{8,10},{9,11},{10,... | collective-permute-start | bytes 589832 | tf_op jit(solution)/shard_map/ppermute | solution.py:35
  21.6 14.6 %collective-permute-start.17 = (bf16[256,512]{1,0:T(8,128)(2,1)}, bf16[256,512]{1,0:T(8,128)(2,1)S(1)}, u32[]{:S(2)}, u32[]{:S(2)}) collective-permute-start(bf16[256,512]{1,0:T(8,128)(2,1)} %get-tuple-element.43.refs_2_), channel_id=1, source_target_pairs={{0,1},{1,0},{2,3},{3,2},{4,5},{5,4},{6,7},{7,6},{8,9},{9,8},{10,11... | collective-permute-start | bytes 786440 | tf_op jit(solution)/shard_map/ppermute | solution.py:28
  26.4 5.7 %collective-permute-start.5 = (bf16[128,768]{1,0:T(8,128)(2,1)S(1)}, bf16[128,768]{1,0:T(8,128)(2,1)S(1)}, u32[]{:S(2)}, u32[]{:S(2)}) collective-permute-start(bf16[128,768]{1,0:T(8,128)(2,1)S(1)} %collective-permute-done.refs_7_.refs_3_.refs_4_.refs_2_), channel_id=1, source_target_pairs={{0,2},{1,3},{2,0},{3,1},{4,6},{5,7},{6,4},{7,5},{8,10},{9,11},{10,... | collective-permute-start | bytes 589832 | tf_op jit(solution)/shard_map/ppermute | solution.py:35
  28.0 4.7 %collective-permute-start.9 = (bf16[128,768]{1,0:T(8,128)(2,1)S(1)}, bf16[128,768]{1,0:T(8,128)(2,1)S(1)}, u32[]{:S(2)}, u32[]{:S(2)}) collective-permute-start(bf16[128,768]{1,0:T(8,128)(2,1)S(1)} %collective-permute-done.1.refs_5_.refs_1_.refs_2_.refs_0_), channel_id=1, source_target_pairs={{0,4},{4,0},{8,12},{12,8},{16,20},{20,16},{24,28},{28,24},{1,5},{5... | collective-permute-start | bytes 589832 | tf_op jit(solution)/shard_map/ppermute | solution.py:40
  28.0 4.9 %collective-permute-start.10 = (bf16[128,768]{1,0:T(8,128)(2,1)S(1)}, bf16[128,768]{1,0:T(8,128)(2,1)S(1)}, u32[]{:S(2)}, u32[]{:S(2)}) collective-permute-start(bf16[128,768]{1,0:T(8,128)(2,1)S(1)} %collective-permute-done.2.refs_6_.refs_2_.refs_3_.refs_1_), channel_id=1, source_target_pairs={{0,4},{4,0},{8,12},{12,8},{16,20},{20,16},{24,28},{28,24},{1,5},{5... | collective-permute-start | bytes 589832 | tf_op jit(solution)/shard_map/ppermute | solution.py:40
  32.1 1.4 %collective-permute-start.11 = (bf16[128,768]{1,0:T(8,128)(2,1)S(1)}, bf16[128,768]{1,0:T(8,128)(2,1)S(1)}, u32[]{:S(2)}, u32[]{:S(2)}) collective-permute-start(bf16[128,768]{1,0:T(8,128)(2,1)S(1)} %collective-permute-done.refs_7_.refs_3_.refs_4_.refs_2_), channel_id=1, source_target_pairs={{0,4},{4,0},{8,12},{12,8},{16,20},{20,16},{24,28},{28,24},{1,5},{5... | collective-permute-start | bytes 589832 | tf_op jit(solution)/shard_map/ppermute | solution.py:40
  32.4 1.5 %collective-permute-start.13 = (bf16[128,768]{1,0:T(8,128)(2,1)S(1)}, bf16[128,768]{1,0:T(8,128)(2,1)S(1)}, u32[]{:S(2)}, u32[]{:S(2)}) collective-permute-start(bf16[128,768]{1,0:T(8,128)(2,1)S(1)} %collective-permute-done.3.refs_9_.refs_5_.refs_6_.refs_4_), channel_id=1, source_target_pairs={{0,4},{4,0},{8,12},{12,8},{16,20},{20,16},{24,28},{28,24},{1,5},{5... | collective-permute-start | bytes 589832 | tf_op jit(solution)/shard_map/ppermute | solution.py:40
  32.7 1.5 %collective-permute-start.14 = (bf16[128,768]{1,0:T(8,128)(2,1)S(1)}, bf16[128,768]{1,0:T(8,128)(2,1)S(1)}, u32[]{:S(2)}, u32[]{:S(2)}) collective-permute-start(bf16[128,768]{1,0:T(8,128)(2,1)S(1)} %collective-permute-done.4.refs_10_.refs_6_.refs_7_.refs_5_), channel_id=1, source_target_pairs={{0,4},{4,0},{8,12},{12,8},{16,20},{20,16},{24,28},{28,24},{1,5},{5... | collective-permute-start | bytes 589832 | tf_op jit(solution)/shard_map/ppermute | solution.py:40
  32.9 1.5 %collective-permute-start.12 = (bf16[128,768]{1,0:T(8,128)(2,1)S(1)}, bf16[128,768]{1,0:T(8,128)(2,1)S(1)}, u32[]{:S(2)}, u32[]{:S(2)}) collective-permute-start(bf16[128,768]{1,0:T(8,128)(2,1)S(1)} %collective-permute-done.5.refs_8_.refs_4_.refs_5_.refs_3_), channel_id=1, source_target_pairs={{0,4},{4,0},{8,12},{12,8},{16,20},{20,16},{24,28},{28,24},{1,5},{5... | collective-permute-start | bytes 589832 | tf_op jit(solution)/shard_map/ppermute | solution.py:40
  33.3 4.2 %copy-start.1 = (bf16[256,1024]{1,0:T(8,128)(2,1)S(1)}, bf16[256,1024]{1,0:T(8,128)(2,1)}, u32[]{:S(2)}) copy-start(bf16[256,1024]{1,0:T(8,128)(2,1)} %get-tuple-element.41.refs_1_) | copy-start | bytes 1572868
  33.3 5.2 %copy-start = (bf16[256,1024]{1,0:T(8,128)(2,1)S(1)}, bf16[256,1024]{1,0:T(8,128)(2,1)}, u32[]{:S(2)}) copy-start(bf16[256,1024]{1,0:T(8,128)(2,1)} %get-tuple-element.40.refs_0_) | copy-start | bytes 1572868
  33.3 5.2 %copy-start.2 = (bf16[256,512]{1,0:T(8,128)(2,1)S(1)}, bf16[256,512]{1,0:T(8,128)(2,1)}, u32[]{:S(2)}) copy-start(bf16[256,512]{1,0:T(8,128)(2,1)} %get-tuple-element.43.refs_2_) | copy-start | bytes 786436
  33.6 3.9 %collective-permute-start.7 = (bf16[128,768]{1,0:T(8,128)(2,1)S(1)}, bf16[128,768]{1,0:T(8,128)(2,1)S(1)}, u32[]{:S(2)}, u32[]{:S(2)}) collective-permute-start(bf16[128,768]{1,0:T(8,128)(2,1)S(1)} %get-tuple-element.80.refs_3_.refs_0_), channel_id=1, source_target_pairs={{0,4},{4,0},{8,12},{12,8},{16,20},{20,16},{24,28},{28,24},{1,5},{5... | collective-permute-start | bytes 589832 | tf_op jit(solution)/shard_map/ppermute | solution.py:40
  33.9 3.7 %collective-permute-start.8 = (bf16[128,768]{1,0:T(8,128)(2,1)S(1)}, bf16[128,768]{1,0:T(8,128)(2,1)S(1)}, u32[]{:S(2)}, u32[]{:S(2)}) collective-permute-start(bf16[128,768]{1,0:T(8,128)(2,1)S(1)} %get-tuple-element.79.refs_4_.refs_1_), channel_id=1, source_target_pairs={{0,4},{4,0},{8,12},{12,8},{16,20},{20,16},{24,28},{28,24},{1,5},{5... | collective-permute-start | bytes 589832 | tf_op jit(solution)/shard_map/ppermute | solution.py:40
  34.1 4.3 %collective-permute-start.15 = (bf16[128,768]{1,0:T(8,128)(2,1)S(1)}, bf16[128,768]{1,0:T(8,128)(2,1)S(1)}, u32[]{:S(2)}, u32[]{:S(2)}) collective-permute-start(bf16[128,768]{1,0:T(8,128)(2,1)S(1)} %get-tuple-element.78.refs_19_.refs_16_), channel_id=1, source_target_pairs={{0,4},{4,0},{8,12},{12,8},{16,20},{20,16},{24,28},{28,24},{1,5},{5... | collective-permute-start | bytes 589832 | tf_op jit(solution)/shard_map/ppermute | solution.py:40
  34.4 4.0 %collective-permute-start.16 = (bf16[128,768]{1,0:T(8,128)(2,1)S(1)}, bf16[128,768]{1,0:T(8,128)(2,1)S(1)}, u32[]{:S(2)}, u32[]{:S(2)}) collective-permute-start(bf16[128,768]{1,0:T(8,128)(2,1)S(1)} %get-tuple-element.77.refs_20_.refs_17_), channel_id=1, source_target_pairs={{0,4},{4,0},{8,12},{12,8},{16,20},{20,16},{24,28},{28,24},{1,5},{5... | collective-permute-start | bytes 589832 | tf_op jit(solution)/shard_map/ppermute | solution.py:40
  36.2 5.5 %collective-permute-start.19 = (bf16[256,256]{1,0:T(8,128)(2,1)S(1)}, bf16[256,256]{1,0:T(8,128)(2,1)S(1)}, u32[]{:S(2)}, u32[]{:S(2)}) collective-permute-start(bf16[256,256]{1,0:T(8,128)(2,1)S(1)} %get-tuple-element.59), channel_id=1, source_target_pairs={{0,1},{1,0},{2,3},{3,2},{4,5},{5,4},{6,7},{7,6},{8,9},{9,8},{10,11... | collective-permute-start | bytes 393224 | tf_op jit(solution)/shard_map/ppermute | solution.py:28
  37.5 28.1 %collective-permute-start.27 = (bf16[256,1024]{1,0:T(8,128)(2,1)S(1)}, bf16[256,1024]{1,0:T(8,128)(2,1)S(1)}, u32[]{:S(2)}, u32[]{:S(2)}) collective-permute-start(bf16[256,1024]{1,0:T(8,128)(2,1)S(1)} %copy-done.1), channel_id=1, source_target_pairs={{0,4},{4,0},{8,12},{12,8},{16,20},{20,16},{24,28},{28,24},{1,5},{5... | collective-permute-start | bytes 1572872 | tf_op jit(solution)/shard_map/ppermute | solution.py:40
  37.6 14.2 %collective-permute-start.18 = (bf16[256,512]{1,0:T(8,128)(2,1)S(1)}, bf16[256,512]{1,0:T(8,128)(2,1)S(1)}, u32[]{:S(2)}, u32[]{:S(2)}) collective-permute-start(bf16[256,512]{1,0:T(8,128)(2,1)S(1)} %get-tuple-element.57), channel_id=1, source_target_pairs={{0,1},{1,0},{2,3},{3,2},{4,5},{5,4},{6,7},{7,6},{8,9},{9,8},{10,11... | collective-permute-start | bytes 786440 | tf_op jit(solution)/shard_map/ppermute | solution.py:28
  38.5 10.8 %copy-start.5 = (bf16[1,256,512]{2,1,0:T(8,128)(2,1)S(1)}, bf16[1,256,512]{2,1,0:T(8,128)(2,1)}, u32[]{:S(2)}) copy-start(bf16[1,256,512]{2,1,0:T(8,128)(2,1)} %param.7) | copy-start | bytes 786436
  41.8 7.7 %collective-permute-start.20 = (bf16[256,256]{1,0:T(8,128)(2,1)S(1)}, bf16[256,256]{1,0:T(8,128)(2,1)S(1)}, u32[]{:S(2)}, u32[]{:S(2)}) collective-permute-start(bf16[256,256]{1,0:T(8,128)(2,1)S(1)} %add_convert_fusion.4.refs_2_), channel_id=1, source_target_pairs={{0,2},{1,3},{4,6},{5,7},{8,10},{9,11},{12,14},{13,15},{16,18},{17,... | collective-permute-start | bytes 393224 | tf_op jit(solution)/shard_map/ppermute | solution.py:53
  45.2 6.6 %collective-permute-start.21 = (bf16[256,256]{1,0:T(8,128)(2,1)S(1)}, bf16[256,256]{1,0:T(8,128)(2,1)S(1)}, u32[]{:S(2)}, u32[]{:S(2)}) collective-permute-start(bf16[256,256]{1,0:T(8,128)(2,1)S(1)} %add_convert_fusion.4.refs_2_), channel_id=1, source_target_pairs={{0,1},{1,2},{2,3},{4,5},{5,6},{6,7},{8,9},{9,10},{10,11},{12,13},{... | collective-permute-start | bytes 393224 | tf_op jit(solution)/shard_map/ppermute | solution.py:53
  49.4 22.7 %collective-permute-start.28 = (bf16[256,1536]{1,0:T(8,128)(2,1)S(1)}, bf16[256,1536]{1,0:T(8,128)(2,1)S(1)}, u32[]{:S(2)}, u32[]{:S(2)}) collective-permute-start(bf16[256,1536]{1,0:T(8,128)(2,1)S(1)} %collective-permute-done.6.refs_0_.refs_1_), channel_id=1, source_target_pairs={{0,4},{4,0},{8,12},{12,8},{16,20},{20,16},{24,28},{28,24},{1,5},{5... | collective-permute-start | bytes 2359304 | tf_op jit(solution)/shard_map/ppermute | solution.py:40
  55.9 6.9 %collective-permute-start.23 = (bf16[256,256]{1,0:T(8,128)(2,1)S(1)}, bf16[256,256]{1,0:T(8,128)(2,1)S(1)}, u32[]{:S(2)}, u32[]{:S(2)}) collective-permute-start(bf16[256,256]{1,0:T(8,128)(2,1)S(1)} %get-tuple-element.82), channel_id=1, source_target_pairs={{2,0},{3,1},{6,4},{7,5},{10,8},{11,9},{14,12},{15,13},{18,16},{19,... | collective-permute-start | bytes 393224 | tf_op jit(solution)/shard_map/ppermute | solution.py:53
  57.2 8.3 %collective-permute-start.22 = (bf16[256,256]{1,0:T(8,128)(2,1)S(1)}, bf16[256,256]{1,0:T(8,128)(2,1)S(1)}, u32[]{:S(2)}, u32[]{:S(2)}) collective-permute-start(bf16[256,256]{1,0:T(8,128)(2,1)S(1)} %get-tuple-element.81), channel_id=1, source_target_pairs={{1,0},{2,1},{3,2},{5,4},{6,5},{7,6},{9,8},{10,9},{11,10},{13,12},{... | collective-permute-start | bytes 393224 | tf_op jit(solution)/shard_map/ppermute | solution.py:53
  58.5 9.8 %collective-permute-start.24 = (bf16[256,512]{1,0:T(8,128)(2,1)S(1)}, bf16[256,512]{1,0:T(8,128)(2,1)S(1)}, u32[]{:S(2)}, u32[]{:S(2)}) collective-permute-start(bf16[256,512]{1,0:T(8,128)(2,1)S(1)} %get-tuple-element.61.dquery_ref.refs_6_), channel_id=1, source_target_pairs={{0,1},{1,0},{2,3},{3,2},{4,5},{5,4},{6,7},{7,6},{8,9},{9,8},{10,11... | collective-permute-start | bytes 786440 | tf_op jit(solution)/shard_map/ppermute | solution.py:28
  62.8 5.6 %collective-permute-start.29 = (bf16[256,512]{1,0:T(8,128)(2,1)S(1)}, bf16[256,512]{1,0:T(8,128)(2,1)S(1)}, u32[]{:S(2)}, u32[]{:S(2)}) collective-permute-start(bf16[256,512]{1,0:T(8,128)(2,1)S(1)} %collective-permute-done.17.refs_2_), channel_id=1, source_target_pairs={{0,4},{4,0},{8,12},{12,8},{16,20},{20,16},{24,28},{28,24},{1,5},{5... | collective-permute-start | bytes 786440 | tf_op jit(solution)/shard_map/ppermute | solution.py:40
  65.5 6.5 %collective-permute-start.30 = (bf16[256,512]{1,0:T(8,128)(2,1)S(1)}, bf16[256,512]{1,0:T(8,128)(2,1)S(1)}, u32[]{:S(2)}, u32[]{:S(2)}) collective-permute-start(bf16[256,512]{1,0:T(8,128)(2,1)S(1)} %get-tuple-element.61.dquery_ref.refs_6_), channel_id=1, source_target_pairs={{0,4},{4,0},{8,12},{12,8},{16,20},{20,16},{24,28},{28,24},{1,5},{5... | collective-permute-start | bytes 786440 | tf_op jit(solution)/shard_map/ppermute | solution.py:40
  65.6 6.5 %collective-permute-start.25 = (bf16[256,256]{1,0:T(8,128)(2,1)S(1)}, bf16[256,256]{1,0:T(8,128)(2,1)S(1)}, u32[]{:S(2)}, u32[]{:S(2)}) collective-permute-start(bf16[256,256]{1,0:T(8,128)(2,1)S(1)} %add_convert_fusion.3.dpair_ref.refs_7_.refs_14_), channel_id=1, source_target_pairs={{0,1},{1,0},{2,3},{3,2},{4,5},{5,4},{6,7},{7,6},{8,9},{9,8},{10,11... | collective-permute-start | bytes 393224 | tf_op jit(solution)/shard_map/ppermute | solution.py:28
  68.3 5.1 %collective-permute-start.32 = (bf16[256,512]{1,0:T(8,128)(2,1)S(1)}, bf16[256,512]{1,0:T(8,128)(2,1)S(1)}, u32[]{:S(2)}, u32[]{:S(2)}) collective-permute-start(bf16[256,512]{1,0:T(8,128)(2,1)S(1)} %collective-permute-done.24.dquery_ref.refs_8_), channel_id=1, source_target_pairs={{0,4},{4,0},{8,12},{12,8},{16,20},{20,16},{24,28},{28,24},{1,5},{5... | collective-permute-start | bytes 786440 | tf_op jit(solution)/shard_map/ppermute | solution.py:40
  68.3 3.7 %collective-permute-start.31 = (bf16[256,256]{1,0:T(8,128)(2,1)S(1)}, bf16[256,256]{1,0:T(8,128)(2,1)S(1)}, u32[]{:S(2)}, u32[]{:S(2)}) collective-permute-start(bf16[256,256]{1,0:T(8,128)(2,1)S(1)} %add_convert_fusion.3.dpair_ref.refs_7_.refs_14_), channel_id=1, source_target_pairs={{0,4},{4,0},{8,12},{12,8},{16,20},{20,16},{24,28},{28,24},{1,5},{5... | collective-permute-start | bytes 393224 | tf_op jit(solution)/shard_map/ppermute | solution.py:40
  72.0 1.3 %collective-permute-start.33 = (bf16[256,256]{1,0:T(8,128)(2,1)S(1)}, bf16[256,256]{1,0:T(8,128)(2,1)S(1)}, u32[]{:S(2)}, u32[]{:S(2)}) collective-permute-start(bf16[256,256]{1,0:T(8,128)(2,1)S(1)} %collective-permute-done.25.dpair_ref.refs_9_), channel_id=1, source_target_pairs={{0,4},{4,0},{8,12},{12,8},{16,20},{20,16},{24,28},{28,24},{1,5},{5... | collective-permute-start | bytes 393224 | tf_op jit(solution)/shard_map/ppermute | solution.py:40
  74.4 7.8 %collective-permute-start.39 = (bf16[128,768]{1,0:T(8,128)(2,1)S(1)}, bf16[128,768]{1,0:T(8,128)(2,1)S(1)}, u32[]{:S(2)}, u32[]{:S(2)}) collective-permute-start(bf16[128,768]{1,0:T(8,128)(2,1)S(1)} %get-tuple-element.76), channel_id=1, source_target_pairs={{0,2},{1,3},{2,0},{3,1},{4,6},{5,7},{6,4},{7,5},{8,10},{9,11},{10,... | collective-permute-start | bytes 589832 | tf_op jit(solution)/shard_map/ppermute | solution.py:35
  77.2 23.2 %collective-permute-start.26 = (bf16[256,1536]{1,0:T(8,128)(2,1)S(1)}, bf16[256,1536]{1,0:T(8,128)(2,1)S(1)}, u32[]{:S(2)}, u32[]{:S(2)}) collective-permute-start(bf16[256,1536]{1,0:T(8,128)(2,1)S(1)} %get-tuple-element.65), channel_id=1, source_target_pairs={{0,1},{1,0},{2,3},{3,2},{4,5},{5,4},{6,7},{7,6},{8,9},{9,8},{10,11... | collective-permute-start | bytes 2359304 | tf_op jit(solution)/shard_map/ppermute | solution.py:28
  77.5 8.9 %collective-permute-start.37 = (bf16[128,768]{1,0:T(8,128)(2,1)S(1)}, bf16[128,768]{1,0:T(8,128)(2,1)S(1)}, u32[]{:S(2)}, u32[]{:S(2)}) collective-permute-start(bf16[128,768]{1,0:T(8,128)(2,1)S(1)} %get-tuple-element.74), channel_id=1, source_target_pairs={{0,2},{1,3},{2,0},{3,1},{4,6},{5,7},{6,4},{7,5},{8,10},{9,11},{10,... | collective-permute-start | bytes 589832 | tf_op jit(solution)/shard_map/ppermute | solution.py:35
  80.2 10.5 %collective-permute-start.35 = (bf16[128,768]{1,0:T(8,128)(2,1)S(1)}, bf16[128,768]{1,0:T(8,128)(2,1)S(1)}, u32[]{:S(2)}, u32[]{:S(2)}) collective-permute-start(bf16[128,768]{1,0:T(8,128)(2,1)S(1)} %get-tuple-element.72), channel_id=1, source_target_pairs={{0,2},{1,3},{2,0},{3,1},{4,6},{5,7},{6,4},{7,5},{8,10},{9,11},{10,... | collective-permute-start | bytes 589832 | tf_op jit(solution)/shard_map/ppermute | solution.py:35
  80.6 14.4 %collective-permute-start.34 = (bf16[128,768]{1,0:T(8,128)(2,1)S(1)}, bf16[128,768]{1,0:T(8,128)(2,1)S(1)}, u32[]{:S(2)}, u32[]{:S(2)}) collective-permute-start(bf16[128,768]{1,0:T(8,128)(2,1)S(1)} %get-tuple-element.70), channel_id=1, source_target_pairs={{0,2},{1,3},{2,0},{3,1},{4,6},{5,7},{6,4},{7,5},{8,10},{9,11},{10,... | collective-permute-start | bytes 589832 | tf_op jit(solution)/shard_map/ppermute | solution.py:35
  82.3 12.9 %collective-permute-start.40 = (bf16[128,768]{1,0:T(8,128)(2,1)S(1)}, bf16[128,768]{1,0:T(8,128)(2,1)S(1)}, u32[]{:S(2)}, u32[]{:S(2)}) collective-permute-start(bf16[128,768]{1,0:T(8,128)(2,1)S(1)} %add_convert_fusion), channel_id=1, source_target_pairs={{0,16},{4,20},{8,24},{12,28},{16,0},{20,4},{24,8},{28,12},{1,17},{... | collective-permute-start | bytes 589832 | tf_op jit(solution)/shard_map/ppermute | solution.py:47
  86.5 9.2 %collective-permute-start.38 = (bf16[128,768]{1,0:T(8,128)(2,1)S(1)}, bf16[128,768]{1,0:T(8,128)(2,1)S(1)}, u32[]{:S(2)}, u32[]{:S(2)}) collective-permute-start(bf16[128,768]{1,0:T(8,128)(2,1)S(1)} %add_convert_fusion.1), channel_id=1, source_target_pairs={{0,24},{4,28},{8,0},{12,4},{16,8},{20,12},{24,16},{28,20},{1,25},{... | collective-permute-start | bytes 589832 | tf_op jit(solution)/shard_map/ppermute | solution.py:47
  90.7 8.9 %collective-permute-start.36 = (bf16[128,768]{1,0:T(8,128)(2,1)S(1)}, bf16[128,768]{1,0:T(8,128)(2,1)S(1)}, u32[]{:S(2)}, u32[]{:S(2)}) collective-permute-start(bf16[128,768]{1,0:T(8,128)(2,1)S(1)} %add_convert_fusion.2), channel_id=1, source_target_pairs={{0,8},{4,12},{8,16},{12,20},{16,24},{20,28},{24,0},{28,4},{1,9},{5... | collective-permute-start | bytes 589832 | tf_op jit(solution)/shard_map/ppermute | solution.py:47

commit v9 on v8

--- a/solution.py
+++ b/solution.py
@@ -112,21 +112,27 @@
     )(tokens)
 
 
-def merge_kernel(chips, rest, width, *refs):
-    in_refs, out_ref, sems = refs[:-2], refs[-2], refs[-1]
+def finish_kernel(chips, rest, width, *refs):
+    part_refs, term_refs, (out_ref, sum_ref, total_ref, sems) = refs[:3], refs[3:-4], refs[-4:]
     copies = []
-    for ref, order in zip(in_refs, whole_order(chips, rest)):
+    for ref, order in zip(part_refs, whole_order(chips, rest)):
         for i, block in enumerate(order):
             source = ref.at[:, pl.ds(i * width, width)]
             target = out_ref.at[:, lanes(block, width)]
             copies.append(pltpu.make_async_copy(source, target, sems.at[len(copies)]))
     for copy in copies:
         copy.start()
+    total = term_refs[0][...].astype(F32)
+    for ref in term_refs[1:]:
+        total = total + ref[...].astype(F32)
+    total_ref[...] = total
+    copies.append(pltpu.make_async_copy(total_ref, sum_ref, sems.at[len(copies)]))
+    copies[-1].start()
     for copy in copies:
         copy.wait()
 
 
-def merge_parts(parts, chips, rest, width):
+def finish(parts, terms, chips, rest, width):
     rows = parts[0].shape[0]
     total = sum(part.shape[1] for part in parts)
     count = total // width
@@ -134,16 +140,20 @@
         order = jnp.stack(sum(whole_order(chips, rest), []))
         where = jnp.zeros_like(order).at[order].set(lax.iota(order.dtype, count))
         blocks = jnp.concatenate(parts, axis=1).reshape(rows, count, width)
-        return jnp.take(blocks, where, axis=1).reshape(rows, total)
-    return pl.pallas_call(
-        functools.partial(merge_kernel, chips, rest, width),
-        in_specs=[VMEM] * len(parts),
-        out_specs=pl.BlockSpec(memory_space=pl.ANY),
-        out_shape=jax.ShapeDtypeStruct((rows, total), BF16),
-        scratch_shapes=[pltpu.SemaphoreType.DMA((count,))],
+        summed = functools.reduce(jnp.add, [term.astype(F32) for term in terms])
+        return jnp.take(blocks, where, axis=1).reshape(rows, total), summed
+    return pl.pallas_call(
+        functools.partial(finish_kernel, chips, rest, width),
+        in_specs=[VMEM] * (len(parts) + len(terms)),
+        out_specs=[pl.BlockSpec(memory_space=pl.ANY)] * 2,
+        out_shape=[
+            jax.ShapeDtypeStruct((rows, total), BF16),
+            jax.ShapeDtypeStruct(terms[0].shape, F32),
+        ],
+        scratch_shapes=[pltpu.VMEM(terms[0].shape, F32), pltpu.SemaphoreType.DMA((count + 1,))],
         compiler_params=pltpu.CompilerParams(vmem_limit_bytes=20 * 2**20),
-        name="merge_parts",
-    )(*parts)
+        name="finish",
+    )(*parts, *terms)
 
 
 def cut(parts, first, step):
@@ -411,15 +421,15 @@
             grad_from = swap_x(grad_sent)
         for i, k in enumerate(steps):
             part, *sent = terms[i * rest : (i + 1) * rest]
-            for j, piece in enumerate(sent, 1):
-                part = part + shift_rest(piece, -j).astype(F32)
+            received = [shift_rest(piece, -j) for j, piece in enumerate(sent, 1)]
             if k:
-                part = shift_chip(part.astype(BF16), -k).astype(F32)
-            parts.append(part)
-    weights_grad = functools.reduce(jnp.add, reversed(parts))
+                part = functools.reduce(jnp.add, [term.astype(F32) for term in received], part)
+                parts.append(shift_chip(part.astype(BF16), -k))
+            else:
+                parts += [part, *received]
 
     grad_mine, grad_near, _ = width_grad(dquery, dpair, [groups, groups_near])
-    inputs_grad = merge_parts([grad_mine, grad_from, grad_near], chips, rest, width)
+    inputs_grad, weights_grad = finish([grad_mine, grad_from, grad_near], parts, chips, rest, width)
     return (attention[None], inputs_grad[None], weights_grad)
 
 

time: 102 us -> 101 us (level)
  no operation moved by 1% of the time
where the time goes in v9:
time: 101 us
  starting transfers between devices  45 us (45%)
  waiting for transfers between devices  38.6 us (38%)
  Pallas kernels  15.1 us (15%)
  local copies, waits for them, and re-layouts  1.13 us (1%)
    ppermute x6, waiting for transfers between devices, shift_chip(): return lax.ppermute(array, 'dp', pairs)  16.4 us
    ppermute x6, starting transfers between devices, shift_chip(): return lax.ppermute(array, 'dp', pairs)  12 us
    ppermute x7, starting transfers between devices, shift_rest(): return lax.ppermute(array, 'seq', pairs)  10.2 us
    ppermute x4, starting transfers between devices, shift_seq(): return lax.ppermute(array, 'seq', pairs)  10.1 us
    ppermute x7, starting transfers between devices, swap_x(): return lax.ppermute(array, 'seq', [(i, i ^ 1) for i in range(count)])  9.91 us
    ppermute x7, waiting for transfers between devices, shift_rest(): return lax.ppermute(array, 'seq', pairs)  7.47 us
    ppermute x7, waiting for transfers between devices, swap_x(): return lax.ppermute(array, 'seq', [(i, i ^ 1) for i in range(count)])  6.75 us
    ppermute x4, waiting for transfers between devices, shift_seq(): return lax.ppermute(array, 'seq', pairs)  6.16 us
  transfers between devices with their start and end apart: 41, of which 20 were waited for; matrix products, arithmetic and copies ran while one was open for 1% of the time, Pallas kernels for 12%

profile of v9, /device:TPU:0, one launch (start us, length us, event | category | flops | bytes accessed | tf_op | source)
XLA Modules:
  0.0 101.3 jit_solution(17913350790811459937)
XLA Ops:
  0.7 1.0 constant_dynamic-slice_fusion
  1.7 3.1 %collective-permute-start.1 = (bf16[128,768]{1,0:T(8,128)(2,1)S(1)}, bf16[128,768]{1,0:T(8,128)(2,1)S(1)}, u32[]{:S(2)}, u32[]{:S(2)}) collective-permute-start(bf16[128,768]{1,0:T(8,128)(2,1)S(1)} %constant_dynamic-slice_fusion), channel_id=1, source_target_pairs={{0,8},{4,12},{8,16},{12,20},{16,24},{20,28},{24,0},{28,4},{1,9},{5... | collective-permute-start | bytes 589832 | tf_op jit(solution)/shard_map/ppermute | solution.py:47
  4.8 2.8 %split_tokens.1 = (bf16[256,1024]{1,0:T(8,128)(2,1)}, bf16[256,1024]{1,0:T(8,128)(2,1)}, bf16[256,1536]{1,0:T(8,128)(2,1)}, bf16[256,512]{1,0:T(8,128)(2,1)}) custom-call(bf16[256,4096]{1,0:T(8,128)(2,1)} %bitcast.26), custom_call_target="tpu_custom_call" | custom-call | tf_op jit(solution)/shard_map/split_tokens/pallas_call | solution.py:105
  7.6 4.1 %collective-permute-done.1.refs_5_.refs_1_.refs_2_.refs_0_ = bf16[128,768]{1,0:T(8,128)(2,1)S(1)} collective-permute-done((bf16[128,768]{1,0:T(8,128)(2,1)S(1)}, bf16[128,768]{1,0:T(8,128)(2,1)S(1)}, u32[]{:S(2)}, u32[]{:S(2)}) %collective-permute-start.1) | collective-permute-done | bytes 196640 | tf_op jit(solution)/shard_map/ppermute | solution.py:47
  11.7 1.5 %collective-permute-start.6 = (bf16[256,1536]{1,0:T(8,128)(2,1)}, bf16[256,1536]{1,0:T(8,128)(2,1)S(1)}, u32[]{:S(2)}, u32[]{:S(2)}) collective-permute-start(bf16[256,1536]{1,0:T(8,128)(2,1)} %get-tuple-element.52), channel_id=1, source_target_pairs={{0,1},{1,0},{2,3},{3,2},{4,5},{5,4},{6,7},{7,6},{8,9},{9,8},{10,11... | collective-permute-start | bytes 2359304 | tf_op jit(solution)/shard_map/ppermute | solution.py:28
  13.2 1.7 %collective-permute-start.3 = (bf16[128,768]{1,0:T(8,128)(2,1)S(1)}, bf16[128,768]{1,0:T(8,128)(2,1)S(1)}, u32[]{:S(2)}, u32[]{:S(2)}) collective-permute-start(bf16[128,768]{1,0:T(8,128)(2,1)S(1)} %constant_dynamic-slice_fusion), channel_id=1, source_target_pairs={{0,24},{4,28},{8,0},{12,4},{16,8},{20,12},{24,16},{28,20},{1,25},{... | collective-permute-start | bytes 589832 | tf_op jit(solution)/shard_map/ppermute | solution.py:47
  14.9 1.5 %collective-permute-start.2 = (bf16[128,768]{1,0:T(8,128)(2,1)S(1)}, bf16[128,768]{1,0:T(8,128)(2,1)S(1)}, u32[]{:S(2)}, u32[]{:S(2)}) collective-permute-start(bf16[128,768]{1,0:T(8,128)(2,1)S(1)} %collective-permute-done.1.refs_5_.refs_1_.refs_2_.refs_0_), channel_id=1, source_target_pairs={{0,2},{1,3},{2,0},{3,1},{4,6},{5,7},{6,4},{7,5},{8,10},{9,11},{10,... | collective-permute-start | bytes 589832 | tf_op jit(solution)/shard_map/ppermute | solution.py:35
  16.4 3.6 %collective-permute-done.3.refs_9_.refs_5_.refs_6_.refs_4_ = bf16[128,768]{1,0:T(8,128)(2,1)S(1)} collective-permute-done((bf16[128,768]{1,0:T(8,128)(2,1)S(1)}, bf16[128,768]{1,0:T(8,128)(2,1)S(1)}, u32[]{:S(2)}, u32[]{:S(2)}) %collective-permute-start.3) | collective-permute-done | bytes 196640 | tf_op jit(solution)/shard_map/ppermute | solution.py:47
  20.1 1.5 %collective-permute-start.4 = (bf16[128,768]{1,0:T(8,128)(2,1)S(1)}, bf16[128,768]{1,0:T(8,128)(2,1)S(1)}, u32[]{:S(2)}, u32[]{:S(2)}) collective-permute-start(bf16[128,768]{1,0:T(8,128)(2,1)S(1)} %collective-permute-done.3.refs_9_.refs_5_.refs_6_.refs_4_), channel_id=1, source_target_pairs={{0,2},{1,3},{2,0},{3,1},{4,6},{5,7},{6,4},{7,5},{8,10},{9,11},{10,... | collective-permute-start | bytes 589832 | tf_op jit(solution)/shard_map/ppermute | solution.py:35
  21.6 0.5 collective-permute-start.17
  22.3 4.1 %collective-permute-done.refs_7_.refs_3_.refs_4_.refs_2_ = bf16[128,768]{1,0:T(8,128)(2,1)S(1)} collective-permute-done((bf16[128,768]{1,0:T(8,128)(2,1)S(1)}, bf16[128,768]{1,0:T(8,128)(2,1)S(1)}, u32[]{:S(2)}, u32[]{:S(2)}) %collective-permute-start) | collective-permute-done | bytes 196640 | tf_op jit(solution)/shard_map/ppermute | solution.py:47
  26.4 1.5 %collective-permute-start.5 = (bf16[128,768]{1,0:T(8,128)(2,1)S(1)}, bf16[128,768]{1,0:T(8,128)(2,1)S(1)}, u32[]{:S(2)}, u32[]{:S(2)}) collective-permute-start(bf16[128,768]{1,0:T(8,128)(2,1)S(1)} %collective-permute-done.refs_7_.refs_3_.refs_4_.refs_2_), channel_id=1, source_target_pairs={{0,2},{1,3},{2,0},{3,1},{4,6},{5,7},{6,4},{7,5},{8,10},{9,11},{10,... | collective-permute-start | bytes 589832 | tf_op jit(solution)/shard_map/ppermute | solution.py:35
  28.0 0.5 collective-permute-start.10
  28.5 3.7 %collective-permute-done.5.refs_8_.refs_4_.refs_5_.refs_3_ = bf16[128,768]{1,0:T(8,128)(2,1)S(1)} collective-permute-done((bf16[128,768]{1,0:T(8,128)(2,1)S(1)}, bf16[128,768]{1,0:T(8,128)(2,1)S(1)}, u32[]{:S(2)}, u32[]{:S(2)}) %collective-permute-start.5) | collective-permute-done | bytes 196640 | tf_op jit(solution)/shard_map/ppermute | solution.py:35
  34.7 0.8 project.3
  35.4 0.8 collective-permute-done.17.refs_2_
  36.2 1.2 %collective-permute-start.19 = (bf16[256,256]{1,0:T(8,128)(2,1)S(1)}, bf16[256,256]{1,0:T(8,128)(2,1)S(1)}, u32[]{:S(2)}, u32[]{:S(2)}) collective-permute-start(bf16[256,256]{1,0:T(8,128)(2,1)S(1)} %get-tuple-element.61), channel_id=1, source_target_pairs={{0,1},{1,0},{2,3},{3,2},{4,5},{5,4},{6,7},{7,6},{8,9},{9,8},{10,11... | collective-permute-start | bytes 393224 | tf_op jit(solution)/shard_map/ppermute | solution.py:28
  37.6 0.8 collective-permute-start.18
  38.5 1.2 %project.2 = (f32[256,512]{1,0:T(8,128)S(1)}, f32[256,256]{1,0:T(8,128)S(1)}) custom-call(bf16[256,1024]{1,0:T(8,128)(2,1)S(1)} %copy-done, bf16[256,1024]{1,0:T(8,128)(2,1)S(1)} %copy-done.1, bf16[256,512]{1,0:T(8,128)(2,1)S(1)} %copy-done.2, bf16[128,768]{1,0:T(8,128)(2,1)S(1)} %get-tuple-element.84.refs_3_.refs_0_, ...), custom_call_target="tpu_custom_call" | custom-call | tf_op jit(solution)/shard_map/project/pallas_call | solution.py:182
  39.7 2.1 %collective-permute-done.19 = bf16[256,256]{1,0:T(8,128)(2,1)S(1)} collective-permute-done((bf16[256,256]{1,0:T(8,128)(2,1)S(1)}, bf16[256,256]{1,0:T(8,128)(2,1)S(1)}, u32[]{:S(2)}, u32[]{:S(2)}) %collective-permute-start.19) | collective-permute-done | bytes 131104 | tf_op jit(solution)/shard_map/ppermute | solution.py:28
  41.8 3.4 %collective-permute-start.20 = (bf16[256,256]{1,0:T(8,128)(2,1)S(1)}, bf16[256,256]{1,0:T(8,128)(2,1)S(1)}, u32[]{:S(2)}, u32[]{:S(2)}) collective-permute-start(bf16[256,256]{1,0:T(8,128)(2,1)S(1)} %add_convert_fusion.4.refs_2_), channel_id=1, source_target_pairs={{0,2},{1,3},{4,6},{5,7},{8,10},{9,11},{12,14},{13,15},{16,18},{17,... | collective-permute-start | bytes 393224 | tf_op jit(solution)/shard_map/ppermute | solution.py:53
  45.2 4.1 %collective-permute-start.21 = (bf16[256,256]{1,0:T(8,128)(2,1)S(1)}, bf16[256,256]{1,0:T(8,128)(2,1)S(1)}, u32[]{:S(2)}, u32[]{:S(2)}) collective-permute-start(bf16[256,256]{1,0:T(8,128)(2,1)S(1)} %add_convert_fusion.4.refs_2_), channel_id=1, source_target_pairs={{0,1},{1,2},{2,3},{4,5},{5,6},{6,7},{8,9},{9,10},{10,11},{12,13},{... | collective-permute-start | bytes 393224 | tf_op jit(solution)/shard_map/ppermute | solution.py:53
  49.5 2.3 %collective-permute-done.21.refs_1_ = bf16[256,256]{1,0:T(8,128)(2,1)S(1)} collective-permute-done((bf16[256,256]{1,0:T(8,128)(2,1)S(1)}, bf16[256,256]{1,0:T(8,128)(2,1)S(1)}, u32[]{:S(2)}, u32[]{:S(2)}) %collective-permute-start.21) | collective-permute-done | bytes 131104 | tf_op jit(solution)/shard_map/ppermute | solution.py:53
  51.8 4.1 %attend.1 = (bf16[256,512]{1,0:T(8,128)(2,1)}, bf16[256,512]{1,0:T(8,128)(2,1)S(1)}, f32[256,256]{1,0:T(8,128)S(1)}, bf16[512,256]{1,0:T(8,128)(2,1)S(1)}) custom-call(s32[8]{0:T(128)S(1)} %bitcast.25, f32[256,512]{1,0:T(8,128)S(1)} %get-tuple-element.56.q_ref, bf16[256,512]{1,0:T(8,128)(2,1)S(1)} %collective-permute-done.18.q_from_ref, ...), custom_call_target="tpu_custom_call" | custom-call | tf_op jit(solution)/shard_map/attend/pallas_call | solution.py:331
  55.9 1.3 %collective-permute-start.23 = (bf16[256,256]{1,0:T(8,128)(2,1)S(1)}, bf16[256,256]{1,0:T(8,128)(2,1)S(1)}, u32[]{:S(2)}, u32[]{:S(2)}) collective-permute-start(bf16[256,256]{1,0:T(8,128)(2,1)S(1)} %get-tuple-element.86), channel_id=1, source_target_pairs={{2,0},{3,1},{6,4},{7,5},{10,8},{11,9},{14,12},{15,13},{18,16},{19,... | collective-permute-start | bytes 393224 | tf_op jit(solution)/shard_map/ppermute | solution.py:53
  57.2 1.3 %collective-permute-start.22 = (bf16[256,256]{1,0:T(8,128)(2,1)S(1)}, bf16[256,256]{1,0:T(8,128)(2,1)S(1)}, u32[]{:S(2)}, u32[]{:S(2)}) collective-permute-start(bf16[256,256]{1,0:T(8,128)(2,1)S(1)} %get-tuple-element.85), channel_id=1, source_target_pairs={{1,0},{2,1},{3,2},{5,4},{6,5},{7,6},{9,8},{10,9},{11,10},{13,12},{... | collective-permute-start | bytes 393224 | tf_op jit(solution)/shard_map/ppermute | solution.py:53
  58.5 3.1 %collective-permute-start.24 = (bf16[256,512]{1,0:T(8,128)(2,1)S(1)}, bf16[256,512]{1,0:T(8,128)(2,1)S(1)}, u32[]{:S(2)}, u32[]{:S(2)}) collective-permute-start(bf16[256,512]{1,0:T(8,128)(2,1)S(1)} %get-tuple-element.63.dquery_ref.refs_6_), channel_id=1, source_target_pairs={{0,1},{1,0},{2,3},{3,2},{4,5},{5,4},{6,7},{7,6},{8,9},{9,8},{10,11... | collective-permute-start | bytes 786440 | tf_op jit(solution)/shard_map/ppermute | solution.py:28
  61.6 1.1 %collective-permute-done.23 = bf16[256,256]{1,0:T(8,128)(2,1)S(1)} collective-permute-done((bf16[256,256]{1,0:T(8,128)(2,1)S(1)}, bf16[256,256]{1,0:T(8,128)(2,1)S(1)}, u32[]{:S(2)}, u32[]{:S(2)}) %collective-permute-start.23) | collective-permute-done | bytes 131104 | tf_op jit(solution)/shard_map/ppermute | solution.py:53
  62.8 2.8 %collective-permute-done.22 = bf16[256,256]{1,0:T(8,128)(2,1)S(1)} collective-permute-done((bf16[256,256]{1,0:T(8,128)(2,1)S(1)}, bf16[256,256]{1,0:T(8,128)(2,1)S(1)}, u32[]{:S(2)}, u32[]{:S(2)}) %collective-permute-start.22) | collective-permute-done | bytes 131104 | tf_op jit(solution)/shard_map/ppermute | solution.py:53
  65.6 2.3 %collective-permute-start.25 = (bf16[256,256]{1,0:T(8,128)(2,1)S(1)}, bf16[256,256]{1,0:T(8,128)(2,1)S(1)}, u32[]{:S(2)}, u32[]{:S(2)}) collective-permute-start(bf16[256,256]{1,0:T(8,128)(2,1)S(1)} %add_convert_fusion.3.dpair_ref.refs_7_.refs_14_), channel_id=1, source_target_pairs={{0,1},{1,0},{2,3},{3,2},{4,5},{5,4},{6,7},{7,6},{8,9},{9,8},{10,11... | collective-permute-start | bytes 393224 | tf_op jit(solution)/shard_map/ppermute | solution.py:28
  68.3 0.5 collective-permute-start.31
  68.8 3.2 %collective-permute-done.25.dpair_ref.refs_9_ = bf16[256,256]{1,0:T(8,128)(2,1)S(1)} collective-permute-done((bf16[256,256]{1,0:T(8,128)(2,1)S(1)}, bf16[256,256]{1,0:T(8,128)(2,1)S(1)}, u32[]{:S(2)}, u32[]{:S(2)}) %collective-permute-start.25) | collective-permute-done | bytes 131104 | tf_op jit(solution)/shard_map/ppermute | solution.py:28
  72.1 1.3 %collective-permute-done.33.refs_13_ = bf16[256,256]{1,0:T(8,128)(2,1)S(1)} collective-permute-done((bf16[256,256]{1,0:T(8,128)(2,1)S(1)}, bf16[256,256]{1,0:T(8,128)(2,1)S(1)}, u32[]{:S(2)}, u32[]{:S(2)}) %collective-permute-start.33) | collective-permute-done | bytes 131104 | tf_op jit(solution)/shard_map/ppermute | solution.py:40
  73.4 1.0 %weight_terms.2 = (f32[128,768]{1,0:T(8,128)S(1)}, bf16[128,768]{1,0:T(8,128)(2,1)S(1)}, f32[128,768]{1,0:T(8,128)S(1)}, bf16[128,768]{1,0:T(8,128)(2,1)S(1)}) custom-call(bf16[256,1024]{1,0:T(8,128)(2,1)S(1)} %copy-done, bf16[256,1536]{1,0:T(8,128)(2,1)S(1)} %collective-permute-done.6.refs_0_.refs_1_, bf16[256,512]{1,0:T(8,128)(2,1)S(1)} %collective-permute-done.17.refs_2_, ...), custom_call_target="tpu_custom_call" | custom-call | tf_op jit(solution)/shard_map/weight_terms/pallas_call | solution.py:248
  74.4 1.9 %collective-permute-start.34 = (bf16[128,768]{1,0:T(8,128)(2,1)S(1)}, bf16[128,768]{1,0:T(8,128)(2,1)S(1)}, u32[]{:S(2)}, u32[]{:S(2)}) collective-permute-start(bf16[128,768]{1,0:T(8,128)(2,1)S(1)} %get-tuple-element.71), channel_id=1, source_target_pairs={{0,2},{1,3},{2,0},{3,1},{4,6},{5,7},{6,4},{7,5},{8,10},{9,11},{10,... | collective-permute-start | bytes 589832 | tf_op jit(solution)/shard_map/ppermute | solution.py:35
  76.4 0.8 width_grad.3
  77.5 1.6 %collective-permute-start.36 = (bf16[128,768]{1,0:T(8,128)(2,1)S(1)}, bf16[128,768]{1,0:T(8,128)(2,1)S(1)}, u32[]{:S(2)}, u32[]{:S(2)}) collective-permute-start(bf16[128,768]{1,0:T(8,128)(2,1)S(1)} %get-tuple-element.73), channel_id=1, source_target_pairs={{0,2},{1,3},{2,0},{3,1},{4,6},{5,7},{6,4},{7,5},{8,10},{9,11},{10,... | collective-permute-start | bytes 589832 | tf_op jit(solution)/shard_map/ppermute | solution.py:35
  79.1 1.0 %weight_terms.3 = (f32[128,768]{1,0:T(8,128)S(1)}, bf16[128,768]{1,0:T(8,128)(2,1)S(1)}, f32[128,768]{1,0:T(8,128)S(1)}, bf16[128,768]{1,0:T(8,128)(2,1)S(1)}) custom-call(bf16[256,1024]{1,0:T(8,128)(2,1)S(1)} %copy-done, bf16[256,1536]{1,0:T(8,128)(2,1)S(1)} %collective-permute-done.6.refs_0_.refs_1_, bf16[256,512]{1,0:T(8,128)(2,1)S(1)} %collective-permute-done.17.refs_2_, ...), custom_call_target="tpu_custom_call" | custom-call | tf_op jit(solution)/shard_map/weight_terms/pallas_call | solution.py:248
  80.2 0.5 collective-permute-start.38
  80.6 1.6 %collective-permute-start.40 = (bf16[128,768]{1,0:T(8,128)(2,1)S(1)}, bf16[128,768]{1,0:T(8,128)(2,1)S(1)}, u32[]{:S(2)}, u32[]{:S(2)}) collective-permute-start(bf16[128,768]{1,0:T(8,128)(2,1)S(1)} %get-tuple-element.78), channel_id=1, source_target_pairs={{0,2},{1,3},{2,0},{3,1},{4,6},{5,7},{6,4},{7,5},{8,10},{9,11},{10,... | collective-permute-start | bytes 589832 | tf_op jit(solution)/shard_map/ppermute | solution.py:35
  82.3 1.9 %collective-permute-start.35 = (bf16[128,768]{1,0:T(8,128)(2,1)S(1)}, bf16[128,768]{1,0:T(8,128)(2,1)S(1)}, u32[]{:S(2)}, u32[]{:S(2)}) collective-permute-start(bf16[128,768]{1,0:T(8,128)(2,1)S(1)} %add_convert_fusion.2), channel_id=1, source_target_pairs={{0,16},{4,20},{8,24},{12,28},{16,0},{20,4},{24,8},{28,12},{1,17},{... | collective-permute-start | bytes 589832 | tf_op jit(solution)/shard_map/ppermute | solution.py:47
  84.2 2.3 %collective-permute-done.36 = bf16[128,768]{1,0:T(8,128)(2,1)S(1)} collective-permute-done((bf16[128,768]{1,0:T(8,128)(2,1)S(1)}, bf16[128,768]{1,0:T(8,128)(2,1)S(1)}, u32[]{:S(2)}, u32[]{:S(2)}) %collective-permute-start.36) | collective-permute-done | bytes 196640 | tf_op jit(solution)/shard_map/ppermute | solution.py:35
  86.5 2.6 %collective-permute-start.37 = (bf16[128,768]{1,0:T(8,128)(2,1)S(1)}, bf16[128,768]{1,0:T(8,128)(2,1)S(1)}, u32[]{:S(2)}, u32[]{:S(2)}) collective-permute-start(bf16[128,768]{1,0:T(8,128)(2,1)S(1)} %add_convert_fusion.1), channel_id=1, source_target_pairs={{0,24},{4,28},{8,0},{12,4},{16,8},{20,12},{24,16},{28,20},{1,25},{... | collective-permute-start | bytes 589832 | tf_op jit(solution)/shard_map/ppermute | solution.py:47
  89.1 1.5 %collective-permute-done.38 = bf16[128,768]{1,0:T(8,128)(2,1)S(1)} collective-permute-done((bf16[128,768]{1,0:T(8,128)(2,1)S(1)}, bf16[128,768]{1,0:T(8,128)(2,1)S(1)}, u32[]{:S(2)}, u32[]{:S(2)}) %collective-permute-start.38) | collective-permute-done | bytes 196640 | tf_op jit(solution)/shard_map/ppermute | solution.py:35
  90.7 2.7 %collective-permute-start.39 = (bf16[128,768]{1,0:T(8,128)(2,1)S(1)}, bf16[128,768]{1,0:T(8,128)(2,1)S(1)}, u32[]{:S(2)}, u32[]{:S(2)}) collective-permute-start(bf16[128,768]{1,0:T(8,128)(2,1)S(1)} %add_convert_fusion), channel_id=1, source_target_pairs={{0,8},{4,12},{8,16},{12,20},{16,24},{20,28},{24,0},{28,4},{1,9},{5... | collective-permute-start | bytes 589832 | tf_op jit(solution)/shard_map/ppermute | solution.py:47
  93.4 1.6 %width_grad.2 = (bf16[256,2048]{1,0:T(8,128)(2,1)S(1)}, bf16[256,512]{1,0:T(8,128)(2,1)S(1)}, bf16[16,128]{1,0:T(8,128)(2,1)}) custom-call(bf16[256,512]{1,0:T(8,128)(2,1)S(1)} %get-tuple-element.63.dquery_ref.refs_6_, bf16[256,256]{1,0:T(8,128)(2,1)S(1)} %add_convert_fusion.3.dpair_ref.refs_7_.refs_14_, ...), custom_call_target="tpu_custom_call" | custom-call | tf_op jit(solution)/shard_map/width_grad/pallas_call | solution.py:209
  95.7 3.9 %collective-permute-done.39.refs_5_ = bf16[128,768]{1,0:T(8,128)(2,1)S(1)} collective-permute-done((bf16[128,768]{1,0:T(8,128)(2,1)S(1)}, bf16[128,768]{1,0:T(8,128)(2,1)S(1)}, u32[]{:S(2)}, u32[]{:S(2)}) %collective-permute-start.39) | collective-permute-done | bytes 196640 | tf_op jit(solution)/shard_map/ppermute | solution.py:47
  99.5 1.7 %finish.1 = (bf16[256,4096]{1,0:T(8,128)(2,1)}, f32[128,768]{1,0:T(8,128)}) custom-call(bf16[256,2048]{1,0:T(8,128)(2,1)S(1)} %get-tuple-element.66.refs_0_, bf16[256,1536]{1,0:T(8,128)(2,1)S(1)} %collective-permute-done.26.refs_1_, bf16[256,512]{1,0:T(8,128)(2,1)S(1)} %get-tuple-element.68.refs_2_, bf16[128,768]{1,0:T(8,128)(2,1)S(1)} %collective-permute-done.35.refs_3_, ...), custom_call_target="tpu_custom_call" | custom-call | tf_op jit(solution)/shard_map/finish/pallas_call | solution.py:145
  (71 shorter events, 4.6 us)
Async XLA Ops:
  0.6 32.6 %copy-start.4 = (bf16[512,768]{1,0:T(8,128)(2,1)S(1)}, bf16[512,768]{1,0:T(8,128)(2,1)}, u32[]{:S(2)}) copy-start(bf16[512,768]{1,0:T(8,128)(2,1)} %param.6) | copy-start | bytes 2359300
  0.6 21.5 %copy-start.3 = (s32[1,8]{1,0:T(1,128)S(1)}, s32[1,8]{1,0:T(1,128)}, u32[]{:S(2)}) copy-start(s32[1,8]{1,0:T(1,128)} %param.8) | copy-start | bytes 100
  0.7 32.5 %copy-start.6 = (s32[1,8]{1,0:T(1,128)S(1)}, s32[1,8]{1,0:T(1,128)}, u32[]{:S(2)}) copy-start(s32[1,8]{1,0:T(1,128)} %param.9) | copy-start | bytes 100
  1.7 10.0 %collective-permute-start.1 = (bf16[128,768]{1,0:T(8,128)(2,1)S(1)}, bf16[128,768]{1,0:T(8,128)(2,1)S(1)}, u32[]{:S(2)}, u32[]{:S(2)}) collective-permute-start(bf16[128,768]{1,0:T(8,128)(2,1)S(1)} %constant_dynamic-slice_fusion), channel_id=1, source_target_pairs={{0,8},{4,12},{8,16},{12,20},{16,24},{20,28},{24,0},{28,4},{1,9},{5... | collective-permute-start | bytes 589832 | tf_op jit(solution)/shard_map/ppermute | solution.py:47
  11.7 20.7 %collective-permute-start.6 = (bf16[256,1536]{1,0:T(8,128)(2,1)}, bf16[256,1536]{1,0:T(8,128)(2,1)S(1)}, u32[]{:S(2)}, u32[]{:S(2)}) collective-permute-start(bf16[256,1536]{1,0:T(8,128)(2,1)} %get-tuple-element.52), channel_id=1, source_target_pairs={{0,1},{1,0},{2,3},{3,2},{4,5},{5,4},{6,7},{7,6},{8,9},{9,8},{10,11... | collective-permute-start | bytes 2359304 | tf_op jit(solution)/shard_map/ppermute | solution.py:28
  13.2 6.9 %collective-permute-start.3 = (bf16[128,768]{1,0:T(8,128)(2,1)S(1)}, bf16[128,768]{1,0:T(8,128)(2,1)S(1)}, u32[]{:S(2)}, u32[]{:S(2)}) collective-permute-start(bf16[128,768]{1,0:T(8,128)(2,1)S(1)} %constant_dynamic-slice_fusion), channel_id=1, source_target_pairs={{0,24},{4,28},{8,0},{12,4},{16,8},{20,12},{24,16},{28,20},{1,25},{... | collective-permute-start | bytes 589832 | tf_op jit(solution)/shard_map/ppermute | solution.py:47
  14.9 11.5 %collective-permute-start = (bf16[128,768]{1,0:T(8,128)(2,1)S(1)}, bf16[128,768]{1,0:T(8,128)(2,1)S(1)}, u32[]{:S(2)}, u32[]{:S(2)}) collective-permute-start(bf16[128,768]{1,0:T(8,128)(2,1)S(1)} %constant_dynamic-slice_fusion), channel_id=1, source_target_pairs={{0,16},{4,20},{8,24},{12,28},{16,0},{20,4},{24,8},{28,12},{1,17},{... | collective-permute-start | bytes 589832 | tf_op jit(solution)/shard_map/ppermute | solution.py:47
  14.9 11.5 %collective-permute-start.2 = (bf16[128,768]{1,0:T(8,128)(2,1)S(1)}, bf16[128,768]{1,0:T(8,128)(2,1)S(1)}, u32[]{:S(2)}, u32[]{:S(2)}) collective-permute-start(bf16[128,768]{1,0:T(8,128)(2,1)S(1)} %collective-permute-done.1.refs_5_.refs_1_.refs_2_.refs_0_), channel_id=1, source_target_pairs={{0,2},{1,3},{2,0},{3,1},{4,6},{5,7},{6,4},{7,5},{8,10},{9,11},{10,... | collective-permute-start | bytes 589832 | tf_op jit(solution)/shard_map/ppermute | solution.py:35
  20.1 6.4 %collective-permute-start.4 = (bf16[128,768]{1,0:T(8,128)(2,1)S(1)}, bf16[128,768]{1,0:T(8,128)(2,1)S(1)}, u32[]{:S(2)}, u32[]{:S(2)}) collective-permute-start(bf16[128,768]{1,0:T(8,128)(2,1)S(1)} %collective-permute-done.3.refs_9_.refs_5_.refs_6_.refs_4_), channel_id=1, source_target_pairs={{0,2},{1,3},{2,0},{3,1},{4,6},{5,7},{6,4},{7,5},{8,10},{9,11},{10,... | collective-permute-start | bytes 589832 | tf_op jit(solution)/shard_map/ppermute | solution.py:35
  21.6 14.6 %collective-permute-start.17 = (bf16[256,512]{1,0:T(8,128)(2,1)}, bf16[256,512]{1,0:T(8,128)(2,1)S(1)}, u32[]{:S(2)}, u32[]{:S(2)}) collective-permute-start(bf16[256,512]{1,0:T(8,128)(2,1)} %get-tuple-element.45.refs_2_), channel_id=1, source_target_pairs={{0,1},{1,0},{2,3},{3,2},{4,5},{5,4},{6,7},{7,6},{8,9},{9,8},{10,11... | collective-permute-start | bytes 786440 | tf_op jit(solution)/shard_map/ppermute | solution.py:28
  26.4 5.7 %collective-permute-start.5 = (bf16[128,768]{1,0:T(8,128)(2,1)S(1)}, bf16[128,768]{1,0:T(8,128)(2,1)S(1)}, u32[]{:S(2)}, u32[]{:S(2)}) collective-permute-start(bf16[128,768]{1,0:T(8,128)(2,1)S(1)} %collective-permute-done.refs_7_.refs_3_.refs_4_.refs_2_), channel_id=1, source_target_pairs={{0,2},{1,3},{2,0},{3,1},{4,6},{5,7},{6,4},{7,5},{8,10},{9,11},{10,... | collective-permute-start | bytes 589832 | tf_op jit(solution)/shard_map/ppermute | solution.py:35
  28.0 4.7 %collective-permute-start.9 = (bf16[128,768]{1,0:T(8,128)(2,1)S(1)}, bf16[128,768]{1,0:T(8,128)(2,1)S(1)}, u32[]{:S(2)}, u32[]{:S(2)}) collective-permute-start(bf16[128,768]{1,0:T(8,128)(2,1)S(1)} %collective-permute-done.1.refs_5_.refs_1_.refs_2_.refs_0_), channel_id=1, source_target_pairs={{0,4},{4,0},{8,12},{12,8},{16,20},{20,16},{24,28},{28,24},{1,5},{5... | collective-permute-start | bytes 589832 | tf_op jit(solution)/shard_map/ppermute | solution.py:40
  28.0 4.9 %collective-permute-start.10 = (bf16[128,768]{1,0:T(8,128)(2,1)S(1)}, bf16[128,768]{1,0:T(8,128)(2,1)S(1)}, u32[]{:S(2)}, u32[]{:S(2)}) collective-permute-start(bf16[128,768]{1,0:T(8,128)(2,1)S(1)} %collective-permute-done.2.refs_6_.refs_2_.refs_3_.refs_1_), channel_id=1, source_target_pairs={{0,4},{4,0},{8,12},{12,8},{16,20},{20,16},{24,28},{28,24},{1,5},{5... | collective-permute-start | bytes 589832 | tf_op jit(solution)/shard_map/ppermute | solution.py:40
  32.1 1.4 %collective-permute-start.11 = (bf16[128,768]{1,0:T(8,128)(2,1)S(1)}, bf16[128,768]{1,0:T(8,128)(2,1)S(1)}, u32[]{:S(2)}, u32[]{:S(2)}) collective-permute-start(bf16[128,768]{1,0:T(8,128)(2,1)S(1)} %collective-permute-done.refs_7_.refs_3_.refs_4_.refs_2_), channel_id=1, source_target_pairs={{0,4},{4,0},{8,12},{12,8},{16,20},{20,16},{24,28},{28,24},{1,5},{5... | collective-permute-start | bytes 589832 | tf_op jit(solution)/shard_map/ppermute | solution.py:40
  32.4 1.5 %collective-permute-start.13 = (bf16[128,768]{1,0:T(8,128)(2,1)S(1)}, bf16[128,768]{1,0:T(8,128)(2,1)S(1)}, u32[]{:S(2)}, u32[]{:S(2)}) collective-permute-start(bf16[128,768]{1,0:T(8,128)(2,1)S(1)} %collective-permute-done.3.refs_9_.refs_5_.refs_6_.refs_4_), channel_id=1, source_target_pairs={{0,4},{4,0},{8,12},{12,8},{16,20},{20,16},{24,28},{28,24},{1,5},{5... | collective-permute-start | bytes 589832 | tf_op jit(solution)/shard_map/ppermute | solution.py:40
  32.7 1.5 %collective-permute-start.14 = (bf16[128,768]{1,0:T(8,128)(2,1)S(1)}, bf16[128,768]{1,0:T(8,128)(2,1)S(1)}, u32[]{:S(2)}, u32[]{:S(2)}) collective-permute-start(bf16[128,768]{1,0:T(8,128)(2,1)S(1)} %collective-permute-done.4.refs_10_.refs_6_.refs_7_.refs_5_), channel_id=1, source_target_pairs={{0,4},{4,0},{8,12},{12,8},{16,20},{20,16},{24,28},{28,24},{1,5},{5... | collective-permute-start | bytes 589832 | tf_op jit(solution)/shard_map/ppermute | solution.py:40
  32.9 1.5 %collective-permute-start.12 = (bf16[128,768]{1,0:T(8,128)(2,1)S(1)}, bf16[128,768]{1,0:T(8,128)(2,1)S(1)}, u32[]{:S(2)}, u32[]{:S(2)}) collective-permute-start(bf16[128,768]{1,0:T(8,128)(2,1)S(1)} %collective-permute-done.5.refs_8_.refs_4_.refs_5_.refs_3_), channel_id=1, source_target_pairs={{0,4},{4,0},{8,12},{12,8},{16,20},{20,16},{24,28},{28,24},{1,5},{5... | collective-permute-start | bytes 589832 | tf_op jit(solution)/shard_map/ppermute | solution.py:40
  33.3 4.2 %copy-start.1 = (bf16[256,1024]{1,0:T(8,128)(2,1)S(1)}, bf16[256,1024]{1,0:T(8,128)(2,1)}, u32[]{:S(2)}) copy-start(bf16[256,1024]{1,0:T(8,128)(2,1)} %get-tuple-element.43.refs_1_) | copy-start | bytes 1572868
  33.3 5.2 %copy-start = (bf16[256,1024]{1,0:T(8,128)(2,1)S(1)}, bf16[256,1024]{1,0:T(8,128)(2,1)}, u32[]{:S(2)}) copy-start(bf16[256,1024]{1,0:T(8,128)(2,1)} %get-tuple-element.42.refs_0_) | copy-start | bytes 1572868
  33.3 5.2 %copy-start.2 = (bf16[256,512]{1,0:T(8,128)(2,1)S(1)}, bf16[256,512]{1,0:T(8,128)(2,1)}, u32[]{:S(2)}) copy-start(bf16[256,512]{1,0:T(8,128)(2,1)} %get-tuple-element.45.refs_2_) | copy-start | bytes 786436
  33.6 3.9 %collective-permute-start.7 = (bf16[128,768]{1,0:T(8,128)(2,1)S(1)}, bf16[128,768]{1,0:T(8,128)(2,1)S(1)}, u32[]{:S(2)}, u32[]{:S(2)}) collective-permute-start(bf16[128,768]{1,0:T(8,128)(2,1)S(1)} %get-tuple-element.84.refs_3_.refs_0_), channel_id=1, source_target_pairs={{0,4},{4,0},{8,12},{12,8},{16,20},{20,16},{24,28},{28,24},{1,5},{5... | collective-permute-start | bytes 589832 | tf_op jit(solution)/shard_map/ppermute | solution.py:40
  33.9 3.7 %collective-permute-start.8 = (bf16[128,768]{1,0:T(8,128)(2,1)S(1)}, bf16[128,768]{1,0:T(8,128)(2,1)S(1)}, u32[]{:S(2)}, u32[]{:S(2)}) collective-permute-start(bf16[128,768]{1,0:T(8,128)(2,1)S(1)} %get-tuple-element.83.refs_4_.refs_1_), channel_id=1, source_target_pairs={{0,4},{4,0},{8,12},{12,8},{16,20},{20,16},{24,28},{28,24},{1,5},{5... | collective-permute-start | bytes 589832 | tf_op jit(solution)/shard_map/ppermute | solution.py:40
  34.1 4.3 %collective-permute-start.15 = (bf16[128,768]{1,0:T(8,128)(2,1)S(1)}, bf16[128,768]{1,0:T(8,128)(2,1)S(1)}, u32[]{:S(2)}, u32[]{:S(2)}) collective-permute-start(bf16[128,768]{1,0:T(8,128)(2,1)S(1)} %get-tuple-element.82.refs_19_.refs_16_), channel_id=1, source_target_pairs={{0,4},{4,0},{8,12},{12,8},{16,20},{20,16},{24,28},{28,24},{1,5},{5... | collective-permute-start | bytes 589832 | tf_op jit(solution)/shard_map/ppermute | solution.py:40
  34.4 4.0 %collective-permute-start.16 = (bf16[128,768]{1,0:T(8,128)(2,1)S(1)}, bf16[128,768]{1,0:T(8,128)(2,1)S(1)}, u32[]{:S(2)}, u32[]{:S(2)}) collective-permute-start(bf16[128,768]{1,0:T(8,128)(2,1)S(1)} %get-tuple-element.81.refs_20_.refs_17_), channel_id=1, source_target_pairs={{0,4},{4,0},{8,12},{12,8},{16,20},{20,16},{24,28},{28,24},{1,5},{5... | collective-permute-start | bytes 589832 | tf_op jit(solution)/shard_map/ppermute | solution.py:40
  36.2 5.5 %collective-permute-start.19 = (bf16[256,256]{1,0:T(8,128)(2,1)S(1)}, bf16[256,256]{1,0:T(8,128)(2,1)S(1)}, u32[]{:S(2)}, u32[]{:S(2)}) collective-permute-start(bf16[256,256]{1,0:T(8,128)(2,1)S(1)} %get-tuple-element.61), channel_id=1, source_target_pairs={{0,1},{1,0},{2,3},{3,2},{4,5},{5,4},{6,7},{7,6},{8,9},{9,8},{10,11... | collective-permute-start | bytes 393224 | tf_op jit(solution)/shard_map/ppermute | solution.py:28
  37.5 28.1 %collective-permute-start.27 = (bf16[256,1024]{1,0:T(8,128)(2,1)S(1)}, bf16[256,1024]{1,0:T(8,128)(2,1)S(1)}, u32[]{:S(2)}, u32[]{:S(2)}) collective-permute-start(bf16[256,1024]{1,0:T(8,128)(2,1)S(1)} %copy-done.1), channel_id=1, source_target_pairs={{0,4},{4,0},{8,12},{12,8},{16,20},{20,16},{24,28},{28,24},{1,5},{5... | collective-permute-start | bytes 1572872 | tf_op jit(solution)/shard_map/ppermute | solution.py:40
  37.6 14.2 %collective-permute-start.18 = (bf16[256,512]{1,0:T(8,128)(2,1)S(1)}, bf16[256,512]{1,0:T(8,128)(2,1)S(1)}, u32[]{:S(2)}, u32[]{:S(2)}) collective-permute-start(bf16[256,512]{1,0:T(8,128)(2,1)S(1)} %get-tuple-element.59), channel_id=1, source_target_pairs={{0,1},{1,0},{2,3},{3,2},{4,5},{5,4},{6,7},{7,6},{8,9},{9,8},{10,11... | collective-permute-start | bytes 786440 | tf_op jit(solution)/shard_map/ppermute | solution.py:28
  38.5 10.8 %copy-start.5 = (bf16[1,256,512]{2,1,0:T(8,128)(2,1)S(1)}, bf16[1,256,512]{2,1,0:T(8,128)(2,1)}, u32[]{:S(2)}) copy-start(bf16[1,256,512]{2,1,0:T(8,128)(2,1)} %param.7) | copy-start | bytes 786436
  41.8 7.7 %collective-permute-start.20 = (bf16[256,256]{1,0:T(8,128)(2,1)S(1)}, bf16[256,256]{1,0:T(8,128)(2,1)S(1)}, u32[]{:S(2)}, u32[]{:S(2)}) collective-permute-start(bf16[256,256]{1,0:T(8,128)(2,1)S(1)} %add_convert_fusion.4.refs_2_), channel_id=1, source_target_pairs={{0,2},{1,3},{4,6},{5,7},{8,10},{9,11},{12,14},{13,15},{16,18},{17,... | collective-permute-start | bytes 393224 | tf_op jit(solution)/shard_map/ppermute | solution.py:53
  45.2 6.6 %collective-permute-start.21 = (bf16[256,256]{1,0:T(8,128)(2,1)S(1)}, bf16[256,256]{1,0:T(8,128)(2,1)S(1)}, u32[]{:S(2)}, u32[]{:S(2)}) collective-permute-start(bf16[256,256]{1,0:T(8,128)(2,1)S(1)} %add_convert_fusion.4.refs_2_), channel_id=1, source_target_pairs={{0,1},{1,2},{2,3},{4,5},{5,6},{6,7},{8,9},{9,10},{10,11},{12,13},{... | collective-permute-start | bytes 393224 | tf_op jit(solution)/shard_map/ppermute | solution.py:53
  49.4 22.7 %collective-permute-start.28 = (bf16[256,1536]{1,0:T(8,128)(2,1)S(1)}, bf16[256,1536]{1,0:T(8,128)(2,1)S(1)}, u32[]{:S(2)}, u32[]{:S(2)}) collective-permute-start(bf16[256,1536]{1,0:T(8,128)(2,1)S(1)} %collective-permute-done.6.refs_0_.refs_1_), channel_id=1, source_target_pairs={{0,4},{4,0},{8,12},{12,8},{16,20},{20,16},{24,28},{28,24},{1,5},{5... | collective-permute-start | bytes 2359304 | tf_op jit(solution)/shard_map/ppermute | solution.py:40
  55.9 6.9 %collective-permute-start.23 = (bf16[256,256]{1,0:T(8,128)(2,1)S(1)}, bf16[256,256]{1,0:T(8,128)(2,1)S(1)}, u32[]{:S(2)}, u32[]{:S(2)}) collective-permute-start(bf16[256,256]{1,0:T(8,128)(2,1)S(1)} %get-tuple-element.86), channel_id=1, source_target_pairs={{2,0},{3,1},{6,4},{7,5},{10,8},{11,9},{14,12},{15,13},{18,16},{19,... | collective-permute-start | bytes 393224 | tf_op jit(solution)/shard_map/ppermute | solution.py:53
  57.2 8.3 %collective-permute-start.22 = (bf16[256,256]{1,0:T(8,128)(2,1)S(1)}, bf16[256,256]{1,0:T(8,128)(2,1)S(1)}, u32[]{:S(2)}, u32[]{:S(2)}) collective-permute-start(bf16[256,256]{1,0:T(8,128)(2,1)S(1)} %get-tuple-element.85), channel_id=1, source_target_pairs={{1,0},{2,1},{3,2},{5,4},{6,5},{7,6},{9,8},{10,9},{11,10},{13,12},{... | collective-permute-start | bytes 393224 | tf_op jit(solution)/shard_map/ppermute | solution.py:53
  58.5 9.8 %collective-permute-start.24 = (bf16[256,512]{1,0:T(8,128)(2,1)S(1)}, bf16[256,512]{1,0:T(8,128)(2,1)S(1)}, u32[]{:S(2)}, u32[]{:S(2)}) collective-permute-start(bf16[256,512]{1,0:T(8,128)(2,1)S(1)} %get-tuple-element.63.dquery_ref.refs_6_), channel_id=1, source_target_pairs={{0,1},{1,0},{2,3},{3,2},{4,5},{5,4},{6,7},{7,6},{8,9},{9,8},{10,11... | collective-permute-start | bytes 786440 | tf_op jit(solution)/shard_map/ppermute | solution.py:28
  62.8 5.6 %collective-permute-start.29 = (bf16[256,512]{1,0:T(8,128)(2,1)S(1)}, bf16[256,512]{1,0:T(8,128)(2,1)S(1)}, u32[]{:S(2)}, u32[]{:S(2)}) collective-permute-start(bf16[256,512]{1,0:T(8,128)(2,1)S(1)} %collective-permute-done.17.refs_2_), channel_id=1, source_target_pairs={{0,4},{4,0},{8,12},{12,8},{16,20},{20,16},{24,28},{28,24},{1,5},{5... | collective-permute-start | bytes 786440 | tf_op jit(solution)/shard_map/ppermute | solution.py:40
  65.5 6.5 %collective-permute-start.30 = (bf16[256,512]{1,0:T(8,128)(2,1)S(1)}, bf16[256,512]{1,0:T(8,128)(2,1)S(1)}, u32[]{:S(2)}, u32[]{:S(2)}) collective-permute-start(bf16[256,512]{1,0:T(8,128)(2,1)S(1)} %get-tuple-element.63.dquery_ref.refs_6_), channel_id=1, source_target_pairs={{0,4},{4,0},{8,12},{12,8},{16,20},{20,16},{24,28},{28,24},{1,5},{5... | collective-permute-start | bytes 786440 | tf_op jit(solution)/shard_map/ppermute | solution.py:40
  65.6 6.5 %collective-permute-start.25 = (bf16[256,256]{1,0:T(8,128)(2,1)S(1)}, bf16[256,256]{1,0:T(8,128)(2,1)S(1)}, u32[]{:S(2)}, u32[]{:S(2)}) collective-permute-start(bf16[256,256]{1,0:T(8,128)(2,1)S(1)} %add_convert_fusion.3.dpair_ref.refs_7_.refs_14_), channel_id=1, source_target_pairs={{0,1},{1,0},{2,3},{3,2},{4,5},{5,4},{6,7},{7,6},{8,9},{9,8},{10,11... | collective-permute-start | bytes 393224 | tf_op jit(solution)/shard_map/ppermute | solution.py:28
  68.3 5.1 %collective-permute-start.32 = (bf16[256,512]{1,0:T(8,128)(2,1)S(1)}, bf16[256,512]{1,0:T(8,128)(2,1)S(1)}, u32[]{:S(2)}, u32[]{:S(2)}) collective-permute-start(bf16[256,512]{1,0:T(8,128)(2,1)S(1)} %collective-permute-done.24.dquery_ref.refs_8_), channel_id=1, source_target_pairs={{0,4},{4,0},{8,12},{12,8},{16,20},{20,16},{24,28},{28,24},{1,5},{5... | collective-permute-start | bytes 786440 | tf_op jit(solution)/shard_map/ppermute | solution.py:40
  68.3 3.7 %collective-permute-start.31 = (bf16[256,256]{1,0:T(8,128)(2,1)S(1)}, bf16[256,256]{1,0:T(8,128)(2,1)S(1)}, u32[]{:S(2)}, u32[]{:S(2)}) collective-permute-start(bf16[256,256]{1,0:T(8,128)(2,1)S(1)} %add_convert_fusion.3.dpair_ref.refs_7_.refs_14_), channel_id=1, source_target_pairs={{0,4},{4,0},{8,12},{12,8},{16,20},{20,16},{24,28},{28,24},{1,5},{5... | collective-permute-start | bytes 393224 | tf_op jit(solution)/shard_map/ppermute | solution.py:40
  72.0 1.3 %collective-permute-start.33 = (bf16[256,256]{1,0:T(8,128)(2,1)S(1)}, bf16[256,256]{1,0:T(8,128)(2,1)S(1)}, u32[]{:S(2)}, u32[]{:S(2)}) collective-permute-start(bf16[256,256]{1,0:T(8,128)(2,1)S(1)} %collective-permute-done.25.dpair_ref.refs_9_), channel_id=1, source_target_pairs={{0,4},{4,0},{8,12},{12,8},{16,20},{20,16},{24,28},{28,24},{1,5},{5... | collective-permute-start | bytes 393224 | tf_op jit(solution)/shard_map/ppermute | solution.py:40
  74.4 7.8 %collective-permute-start.34 = (bf16[128,768]{1,0:T(8,128)(2,1)S(1)}, bf16[128,768]{1,0:T(8,128)(2,1)S(1)}, u32[]{:S(2)}, u32[]{:S(2)}) collective-permute-start(bf16[128,768]{1,0:T(8,128)(2,1)S(1)} %get-tuple-element.71), channel_id=1, source_target_pairs={{0,2},{1,3},{2,0},{3,1},{4,6},{5,7},{6,4},{7,5},{8,10},{9,11},{10,... | collective-permute-start | bytes 589832 | tf_op jit(solution)/shard_map/ppermute | solution.py:35
  77.2 22.4 %collective-permute-start.26 = (bf16[256,1536]{1,0:T(8,128)(2,1)S(1)}, bf16[256,1536]{1,0:T(8,128)(2,1)S(1)}, u32[]{:S(2)}, u32[]{:S(2)}) collective-permute-start(bf16[256,1536]{1,0:T(8,128)(2,1)S(1)} %get-tuple-element.67), channel_id=1, source_target_pairs={{0,1},{1,0},{2,3},{3,2},{4,5},{5,4},{6,7},{7,6},{8,9},{9,8},{10,11... | collective-permute-start | bytes 2359304 | tf_op jit(solution)/shard_map/ppermute | solution.py:28
  77.5 8.9 %collective-permute-start.36 = (bf16[128,768]{1,0:T(8,128)(2,1)S(1)}, bf16[128,768]{1,0:T(8,128)(2,1)S(1)}, u32[]{:S(2)}, u32[]{:S(2)}) collective-permute-start(bf16[128,768]{1,0:T(8,128)(2,1)S(1)} %get-tuple-element.73), channel_id=1, source_target_pairs={{0,2},{1,3},{2,0},{3,1},{4,6},{5,7},{6,4},{7,5},{8,10},{9,11},{10,... | collective-permute-start | bytes 589832 | tf_op jit(solution)/shard_map/ppermute | solution.py:35
  80.2 10.5 %collective-permute-start.38 = (bf16[128,768]{1,0:T(8,128)(2,1)S(1)}, bf16[128,768]{1,0:T(8,128)(2,1)S(1)}, u32[]{:S(2)}, u32[]{:S(2)}) collective-permute-start(bf16[128,768]{1,0:T(8,128)(2,1)S(1)} %get-tuple-element.76), channel_id=1, source_target_pairs={{0,2},{1,3},{2,0},{3,1},{4,6},{5,7},{6,4},{7,5},{8,10},{9,11},{10,... | collective-permute-start | bytes 589832 | tf_op jit(solution)/shard_map/ppermute | solution.py:35
  80.6 14.4 %collective-permute-start.40 = (bf16[128,768]{1,0:T(8,128)(2,1)S(1)}, bf16[128,768]{1,0:T(8,128)(2,1)S(1)}, u32[]{:S(2)}, u32[]{:S(2)}) collective-permute-start(bf16[128,768]{1,0:T(8,128)(2,1)S(1)} %get-tuple-element.78), channel_id=1, source_target_pairs={{0,2},{1,3},{2,0},{3,1},{4,6},{5,7},{6,4},{7,5},{8,10},{9,11},{10,... | collective-permute-start | bytes 589832 | tf_op jit(solution)/shard_map/ppermute | solution.py:35
  82.3 12.9 %collective-permute-start.35 = (bf16[128,768]{1,0:T(8,128)(2,1)S(1)}, bf16[128,768]{1,0:T(8,128)(2,1)S(1)}, u32[]{:S(2)}, u32[]{:S(2)}) collective-permute-start(bf16[128,768]{1,0:T(8,128)(2,1)S(1)} %add_convert_fusion.2), channel_id=1, source_target_pairs={{0,16},{4,20},{8,24},{12,28},{16,0},{20,4},{24,8},{28,12},{1,17},{... | collective-permute-start | bytes 589832 | tf_op jit(solution)/shard_map/ppermute | solution.py:47
  86.5 9.2 %collective-permute-start.37 = (bf16[128,768]{1,0:T(8,128)(2,1)S(1)}, bf16[128,768]{1,0:T(8,128)(2,1)S(1)}, u32[]{:S(2)}, u32[]{:S(2)}) collective-permute-start(bf16[128,768]{1,0:T(8,128)(2,1)S(1)} %add_convert_fusion.1), channel_id=1, source_target_pairs={{0,24},{4,28},{8,0},{12,4},{16,8},{20,12},{24,16},{28,20},{1,25},{... | collective-permute-start | bytes 589832 | tf_op jit(solution)/shard_map/ppermute | solution.py:47
  90.7 8.8 %collective-permute-start.39 = (bf16[128,768]{1,0:T(8,128)(2,1)S(1)}, bf16[128,768]{1,0:T(8,128)(2,1)S(1)}, u32[]{:S(2)}, u32[]{:S(2)}) collective-permute-start(bf16[128,768]{1,0:T(8,128)(2,1)S(1)} %add_convert_fusion), channel_id=1, source_target_pairs={{0,8},{4,12},{8,16},{12,20},{16,24},{20,28},{24,0},{28,4},{1,9},{5... | collective-permute-start | bytes 589832 | tf_op jit(solution)/shard_map/ppermute | solution.py:47

commit v10 on v9

--- a/solution.py
+++ b/solution.py
@@ -388,7 +388,6 @@
     groups_far = groups_own[1:] + groups_across[1:]
 
     query_sent, pair_sent = project([far_other], groups_far, qwidth, BF16)
-    query_sent, near_other = lax.optimization_barrier((query_sent, swap_x(near)))
     pair_from, query_from = swap_x(pair_sent), swap_x(query_sent)
     query, pair = project([mine_own, mine_across, near], groups + groups_near, qwidth, F32)
     pair = (pair + pair_from.astype(F32)).astype(BF16)
@@ -398,10 +397,13 @@
     kept = kept_rows(doc_row, flag_row, positions)
     cot = jnp.where(kept[:, None] > 0, cotangent[0], jnp.zeros_like(cotangent[0]))
 
+    near, _ = lax.optimization_barrier((near, pair))
+    near_other = swap_x(near)
     pairs = [shift_seq(pair, j) for j in range(back, 0, -1)] + [pair]
     attention, dquery, dpair, dback = attend(doc_row, query, query_from, cot, pairs)
 
-    dquery_other = swap_x(dquery)
+    dquery_sent, near_other = lax.optimization_barrier((dquery, near_other))
+    dquery_other = swap_x(dquery_sent)
     for j in range(1, back + 1):
         sent = dback[(back - j) * local : (back - j + 1) * local]
         dpair = dpair + shift_seq(sent, -j).astype(F32)

time: 101 us -> 101 us (level)
  waiting for transfers between devices: 38.6 us -> 35.2 us
  starting transfers between devices: 45 us -> 47.9 us
    ppermute x6, starting transfers between devices: 12 us -> 15.7 us  [shift_chip(): return lax.ppermute(array, 'dp', pairs)]
    ppermute x7, waiting for transfers between devices: 7.47 us -> 4.72 us  [shift_rest(): return lax.ppermute(array, 'seq', pairs)]
    ppermute x4, starting transfers between devices: 10.1 us -> 8.46 us  [shift_seq(): return lax.ppermute(array, 'seq', pairs)]
    ppermute x7, starting transfers between devices: 9.91 us -> 11.1 us  [swap_x(): return lax.ppermute(array, 'seq', [(i, i ^ 1) for i in range(count)])]
    ppermute x7, waiting for transfers between devices: 6.75 us -> 5.63 us  [swap_x(): return lax.ppermute(array, 'seq', [(i, i ^ 1) for i in range(count)])]
  transfers between devices with their start and end apart: 41 -> 41, of which waited for: 20 -> 18; matrix products, arithmetic and copies ran while one was open for 1% -> 1% of each run, Pallas kernels for 12% -> 12%
where the time goes in v10:
time: 101 us
  starting transfers between devices  47.9 us (47%)
  waiting for transfers between devices  35.2 us (35%)
  Pallas kernels  15 us (15%)
  local copies, waits for them, and re-layouts  1.13 us (1%)
    ppermute x6, waiting for transfers between devices, shift_chip(): return lax.ppermute(array, 'dp', pairs)  17.3 us
    ppermute x6, starting transfers between devices, shift_chip(): return lax.ppermute(array, 'dp', pairs)  15.7 us
    ppermute x7, starting transfers between devices, swap_x(): return lax.ppermute(array, 'seq', [(i, i ^ 1) for i in range(count)])  11.1 us
    ppermute x7, starting transfers between devices, shift_rest(): return lax.ppermute(array, 'seq', pairs)  9.47 us
    ppermute x4, starting transfers between devices, shift_seq(): return lax.ppermute(array, 'seq', pairs)  8.46 us
    ppermute x4, waiting for transfers between devices, shift_seq(): return lax.ppermute(array, 'seq', pairs)  6.42 us
    ppermute x7, waiting for transfers between devices, swap_x(): return lax.ppermute(array, 'seq', [(i, i ^ 1) for i in range(count)])  5.63 us
    ppermute x7, waiting for transfers between devices, shift_rest(): return lax.ppermute(array, 'seq', pairs)  4.72 us
  transfers between devices with their start and end apart: 41, of which 18 were waited for; matrix products, arithmetic and copies ran while one was open for 1% of the time, Pallas kernels for 12%

profile of v10, /device:TPU:0, one launch (start us, length us, event | category | flops | bytes accessed | tf_op | source)
XLA Modules:
  0.0 100.8 jit_solution(16648300365755085481)
XLA Ops:
  0.7 1.0 %constant_dynamic-slice_fusion = bf16[128,768]{1,0:T(8,128)(2,1)S(1)} fusion(bf16[512,768]{1,0:T(8,128)(2,1)} %param.6, s32[]{:T(128)S(6)} %select_n.64), kind=kLoop, calls=%fused_computation.11 | loop fusion | bytes 393220 | tf_op jit(solution)/shard_map/dynamic_slice | solution.py:365
  1.7 3.1 %collective-permute-start.1 = (bf16[128,768]{1,0:T(8,128)(2,1)S(1)}, bf16[128,768]{1,0:T(8,128)(2,1)S(1)}, u32[]{:S(2)}, u32[]{:S(2)}) collective-permute-start(bf16[128,768]{1,0:T(8,128)(2,1)S(1)} %constant_dynamic-slice_fusion), channel_id=1, source_target_pairs={{0,8},{4,12},{8,16},{12,20},{16,24},{20,28},{24,0},{28,4},{1,9},{5... | collective-permute-start | bytes 589832 | tf_op jit(solution)/shard_map/ppermute | solution.py:47
  4.8 2.8 %split_tokens.1 = (bf16[256,1024]{1,0:T(8,128)(2,1)}, bf16[256,1024]{1,0:T(8,128)(2,1)}, bf16[256,1536]{1,0:T(8,128)(2,1)}, bf16[256,512]{1,0:T(8,128)(2,1)}) custom-call(bf16[256,4096]{1,0:T(8,128)(2,1)} %bitcast.26), custom_call_target="tpu_custom_call" | custom-call | tf_op jit(solution)/shard_map/split_tokens/pallas_call | solution.py:105
  7.6 4.1 %collective-permute-done.1.refs_5_.refs_1_.refs_2_.refs_0_ = bf16[128,768]{1,0:T(8,128)(2,1)S(1)} collective-permute-done((bf16[128,768]{1,0:T(8,128)(2,1)S(1)}, bf16[128,768]{1,0:T(8,128)(2,1)S(1)}, u32[]{:S(2)}, u32[]{:S(2)}) %collective-permute-start.1) | collective-permute-done | bytes 196640 | tf_op jit(solution)/shard_map/ppermute | solution.py:47
  11.7 1.5 %collective-permute-start.6 = (bf16[256,1536]{1,0:T(8,128)(2,1)}, bf16[256,1536]{1,0:T(8,128)(2,1)S(1)}, u32[]{:S(2)}, u32[]{:S(2)}) collective-permute-start(bf16[256,1536]{1,0:T(8,128)(2,1)} %get-tuple-element.53), channel_id=1, source_target_pairs={{0,1},{1,0},{2,3},{3,2},{4,5},{5,4},{6,7},{7,6},{8,9},{9,8},{10,11... | collective-permute-start | bytes 2359304 | tf_op jit(solution)/shard_map/ppermute | solution.py:28
  13.2 1.7 %collective-permute-start.3 = (bf16[128,768]{1,0:T(8,128)(2,1)S(1)}, bf16[128,768]{1,0:T(8,128)(2,1)S(1)}, u32[]{:S(2)}, u32[]{:S(2)}) collective-permute-start(bf16[128,768]{1,0:T(8,128)(2,1)S(1)} %constant_dynamic-slice_fusion), channel_id=1, source_target_pairs={{0,24},{4,28},{8,0},{12,4},{16,8},{20,12},{24,16},{28,20},{1,25},{... | collective-permute-start | bytes 589832 | tf_op jit(solution)/shard_map/ppermute | solution.py:47
  14.9 1.5 %collective-permute-start.2 = (bf16[128,768]{1,0:T(8,128)(2,1)S(1)}, bf16[128,768]{1,0:T(8,128)(2,1)S(1)}, u32[]{:S(2)}, u32[]{:S(2)}) collective-permute-start(bf16[128,768]{1,0:T(8,128)(2,1)S(1)} %collective-permute-done.1.refs_5_.refs_1_.refs_2_.refs_0_), channel_id=1, source_target_pairs={{0,2},{1,3},{2,0},{3,1},{4,6},{5,7},{6,4},{7,5},{8,10},{9,11},{10,... | collective-permute-start | bytes 589832 | tf_op jit(solution)/shard_map/ppermute | solution.py:35
  16.4 3.6 %collective-permute-done.3.refs_9_.refs_5_.refs_6_.refs_4_ = bf16[128,768]{1,0:T(8,128)(2,1)S(1)} collective-permute-done((bf16[128,768]{1,0:T(8,128)(2,1)S(1)}, bf16[128,768]{1,0:T(8,128)(2,1)S(1)}, u32[]{:S(2)}, u32[]{:S(2)}) %collective-permute-start.3) | collective-permute-done | bytes 196640 | tf_op jit(solution)/shard_map/ppermute | solution.py:47
  20.1 1.5 %collective-permute-start.4 = (bf16[128,768]{1,0:T(8,128)(2,1)S(1)}, bf16[128,768]{1,0:T(8,128)(2,1)S(1)}, u32[]{:S(2)}, u32[]{:S(2)}) collective-permute-start(bf16[128,768]{1,0:T(8,128)(2,1)S(1)} %collective-permute-done.3.refs_9_.refs_5_.refs_6_.refs_4_), channel_id=1, source_target_pairs={{0,2},{1,3},{2,0},{3,1},{4,6},{5,7},{6,4},{7,5},{8,10},{9,11},{10,... | collective-permute-start | bytes 589832 | tf_op jit(solution)/shard_map/ppermute | solution.py:35
  21.8 4.6 %collective-permute-done.refs_7_.refs_3_.refs_4_.refs_2_ = bf16[128,768]{1,0:T(8,128)(2,1)S(1)} collective-permute-done((bf16[128,768]{1,0:T(8,128)(2,1)S(1)}, bf16[128,768]{1,0:T(8,128)(2,1)S(1)}, u32[]{:S(2)}, u32[]{:S(2)}) %collective-permute-start) | collective-permute-done | bytes 196640 | tf_op jit(solution)/shard_map/ppermute | solution.py:47
  26.4 1.5 %collective-permute-start.5 = (bf16[128,768]{1,0:T(8,128)(2,1)S(1)}, bf16[128,768]{1,0:T(8,128)(2,1)S(1)}, u32[]{:S(2)}, u32[]{:S(2)}) collective-permute-start(bf16[128,768]{1,0:T(8,128)(2,1)S(1)} %collective-permute-done.refs_7_.refs_3_.refs_4_.refs_2_), channel_id=1, source_target_pairs={{0,2},{1,3},{2,0},{3,1},{4,6},{5,7},{6,4},{7,5},{8,10},{9,11},{10,... | collective-permute-start | bytes 589832 | tf_op jit(solution)/shard_map/ppermute | solution.py:35
  28.0 0.5 collective-permute-start.11
  28.5 3.7 %collective-permute-done.5.refs_8_.refs_4_.refs_5_.refs_3_ = bf16[128,768]{1,0:T(8,128)(2,1)S(1)} collective-permute-done((bf16[128,768]{1,0:T(8,128)(2,1)S(1)}, bf16[128,768]{1,0:T(8,128)(2,1)S(1)}, u32[]{:S(2)}, u32[]{:S(2)}) %collective-permute-start.5) | collective-permute-done | bytes 196640 | tf_op jit(solution)/shard_map/ppermute | solution.py:35
  32.1 0.5 collective-permute-start.14
  34.1 0.8 project.3
  34.9 0.6 collective-permute-start.18
  35.7 1.5 %collective-permute-start.17 = (bf16[256,512]{1,0:T(8,128)(2,1)S(1)}, bf16[256,512]{1,0:T(8,128)(2,1)S(1)}, u32[]{:S(2)}, u32[]{:S(2)}) collective-permute-start(bf16[256,512]{1,0:T(8,128)(2,1)S(1)} %get-tuple-element.59), channel_id=1, source_target_pairs={{0,1},{1,0},{2,3},{3,2},{4,5},{5,4},{6,7},{7,6},{8,9},{9,8},{10,11... | collective-permute-start | bytes 786440 | tf_op jit(solution)/shard_map/ppermute | solution.py:28
  37.2 1.2 %project.2 = (f32[256,512]{1,0:T(8,128)S(1)}, f32[256,256]{1,0:T(8,128)S(1)}) custom-call(bf16[256,1024]{1,0:T(8,128)(2,1)S(1)} %copy-done, bf16[256,1024]{1,0:T(8,128)(2,1)S(1)} %copy-done.1, bf16[256,512]{1,0:T(8,128)(2,1)S(1)} %copy-done.2, bf16[128,768]{1,0:T(8,128)(2,1)S(1)} %get-tuple-element.86.refs_3_.refs_0_, ...), custom_call_target="tpu_custom_call" | custom-call | tf_op jit(solution)/shard_map/project/pallas_call | solution.py:182
  38.4 2.9 %collective-permute-done.18 = bf16[256,256]{1,0:T(8,128)(2,1)S(1)} collective-permute-done((bf16[256,256]{1,0:T(8,128)(2,1)S(1)}, bf16[256,256]{1,0:T(8,128)(2,1)S(1)}, u32[]{:S(2)}, u32[]{:S(2)}) %collective-permute-start.18) | collective-permute-done | bytes 131104 | tf_op jit(solution)/shard_map/ppermute | solution.py:28
  41.3 3.4 %collective-permute-start.19 = (bf16[256,256]{1,0:T(8,128)(2,1)S(1)}, bf16[256,256]{1,0:T(8,128)(2,1)S(1)}, u32[]{:S(2)}, u32[]{:S(2)}) collective-permute-start(bf16[256,256]{1,0:T(8,128)(2,1)S(1)} %add_convert_fusion.4.refs_2_), channel_id=1, source_target_pairs={{0,2},{1,3},{4,6},{5,7},{8,10},{9,11},{12,14},{13,15},{16,18},{17,... | collective-permute-start | bytes 393224 | tf_op jit(solution)/shard_map/ppermute | solution.py:53
  44.8 2.4 %collective-permute-start.20 = (bf16[256,256]{1,0:T(8,128)(2,1)S(1)}, bf16[256,256]{1,0:T(8,128)(2,1)S(1)}, u32[]{:S(2)}, u32[]{:S(2)}) collective-permute-start(bf16[256,256]{1,0:T(8,128)(2,1)S(1)} %add_convert_fusion.4.refs_2_), channel_id=1, source_target_pairs={{0,1},{1,2},{2,3},{4,5},{5,6},{6,7},{8,9},{9,10},{10,11},{12,13},{... | collective-permute-start | bytes 393224 | tf_op jit(solution)/shard_map/ppermute | solution.py:53
  47.4 2.6 %collective-permute-done.19.refs_0_ = bf16[256,256]{1,0:T(8,128)(2,1)S(1)} collective-permute-done((bf16[256,256]{1,0:T(8,128)(2,1)S(1)}, bf16[256,256]{1,0:T(8,128)(2,1)S(1)}, u32[]{:S(2)}, u32[]{:S(2)}) %collective-permute-start.19) | collective-permute-done | bytes 131104 | tf_op jit(solution)/shard_map/ppermute | solution.py:53
  50.1 0.9 collective-permute-done.20.refs_1_
  51.0 4.1 %attend.1 = (bf16[256,512]{1,0:T(8,128)(2,1)}, bf16[256,512]{1,0:T(8,128)(2,1)S(1)}, f32[256,256]{1,0:T(8,128)S(1)}, bf16[512,256]{1,0:T(8,128)(2,1)S(1)}) custom-call(s32[8]{0:T(128)S(1)} %bitcast.25, f32[256,512]{1,0:T(8,128)S(1)} %get-tuple-element.57.q_ref, bf16[256,512]{1,0:T(8,128)(2,1)S(1)} %collective-permute-done.17.q_from_ref, ...), custom_call_target="tpu_custom_call" | custom-call | tf_op jit(solution)/shard_map/attend/pallas_call | solution.py:331
  55.2 1.3 %collective-permute-start.22 = (bf16[256,256]{1,0:T(8,128)(2,1)S(1)}, bf16[256,256]{1,0:T(8,128)(2,1)S(1)}, u32[]{:S(2)}, u32[]{:S(2)}) collective-permute-start(bf16[256,256]{1,0:T(8,128)(2,1)S(1)} %get-tuple-element.88), channel_id=1, source_target_pairs={{2,0},{3,1},{6,4},{7,5},{10,8},{11,9},{14,12},{15,13},{18,16},{19,... | collective-permute-start | bytes 393224 | tf_op jit(solution)/shard_map/ppermute | solution.py:53
  56.5 1.3 %collective-permute-start.21 = (bf16[256,256]{1,0:T(8,128)(2,1)S(1)}, bf16[256,256]{1,0:T(8,128)(2,1)S(1)}, u32[]{:S(2)}, u32[]{:S(2)}) collective-permute-start(bf16[256,256]{1,0:T(8,128)(2,1)S(1)} %get-tuple-element.87), channel_id=1, source_target_pairs={{1,0},{2,1},{3,2},{5,4},{6,5},{7,6},{9,8},{10,9},{11,10},{13,12},{... | collective-permute-start | bytes 393224 | tf_op jit(solution)/shard_map/ppermute | solution.py:53
  57.8 3.2 %collective-permute-start.24 = (bf16[256,512]{1,0:T(8,128)(2,1)S(1)}, bf16[256,512]{1,0:T(8,128)(2,1)S(1)}, u32[]{:S(2)}, u32[]{:S(2)}) collective-permute-start(bf16[256,512]{1,0:T(8,128)(2,1)S(1)} %get-tuple-element.68.dquery_ref.refs_6_), channel_id=1, source_target_pairs={{0,1},{1,0},{2,3},{3,2},{4,5},{5,4},{6,7},{7,6},{8,9},{9,8},{10,11... | collective-permute-start | bytes 786440 | tf_op jit(solution)/shard_map/ppermute | solution.py:28
  60.9 1.1 %collective-permute-done.22 = bf16[256,256]{1,0:T(8,128)(2,1)S(1)} collective-permute-done((bf16[256,256]{1,0:T(8,128)(2,1)S(1)}, bf16[256,256]{1,0:T(8,128)(2,1)S(1)}, u32[]{:S(2)}, u32[]{:S(2)}) %collective-permute-start.22) | collective-permute-done | bytes 131104 | tf_op jit(solution)/shard_map/ppermute | solution.py:53
  62.0 1.8 %collective-permute-done.21 = bf16[256,256]{1,0:T(8,128)(2,1)S(1)} collective-permute-done((bf16[256,256]{1,0:T(8,128)(2,1)S(1)}, bf16[256,256]{1,0:T(8,128)(2,1)S(1)}, u32[]{:S(2)}, u32[]{:S(2)}) %collective-permute-start.21) | collective-permute-done | bytes 131104 | tf_op jit(solution)/shard_map/ppermute | solution.py:53
  63.8 3.0 %collective-permute-start.25 = (bf16[256,256]{1,0:T(8,128)(2,1)S(1)}, bf16[256,256]{1,0:T(8,128)(2,1)S(1)}, u32[]{:S(2)}, u32[]{:S(2)}) collective-permute-start(bf16[256,256]{1,0:T(8,128)(2,1)S(1)} %add_convert_fusion.3.dpair_ref.refs_7_.refs_14_), channel_id=1, source_target_pairs={{0,1},{1,0},{2,3},{3,2},{4,5},{5,4},{6,7},{7,6},{8,9},{9,8},{10,11... | collective-permute-start | bytes 393224 | tf_op jit(solution)/shard_map/ppermute | solution.py:28
  67.3 2.4 %collective-permute-done.25.dpair_ref.refs_9_ = bf16[256,256]{1,0:T(8,128)(2,1)S(1)} collective-permute-done((bf16[256,256]{1,0:T(8,128)(2,1)S(1)}, bf16[256,256]{1,0:T(8,128)(2,1)S(1)}, u32[]{:S(2)}, u32[]{:S(2)}) %collective-permute-start.25) | collective-permute-done | bytes 131104 | tf_op jit(solution)/shard_map/ppermute | solution.py:28
  69.8 0.5 collective-permute-start.33
  70.3 0.8 collective-permute-done.31.refs_11_
  71.3 1.0 %weight_terms.2 = (f32[128,768]{1,0:T(8,128)S(1)}, bf16[128,768]{1,0:T(8,128)(2,1)S(1)}, f32[128,768]{1,0:T(8,128)S(1)}, bf16[128,768]{1,0:T(8,128)(2,1)S(1)}) custom-call(bf16[256,1024]{1,0:T(8,128)(2,1)S(1)} %copy-done, bf16[256,1536]{1,0:T(8,128)(2,1)S(1)} %collective-permute-done.6.refs_0_.refs_1_, bf16[256,512]{1,0:T(8,128)(2,1)S(1)} %collective-permute-done.23.refs_2_, ...), custom_call_target="tpu_custom_call" | custom-call | tf_op jit(solution)/shard_map/weight_terms/pallas_call | solution.py:248
  72.3 1.9 %collective-permute-start.34 = (bf16[128,768]{1,0:T(8,128)(2,1)S(1)}, bf16[128,768]{1,0:T(8,128)(2,1)S(1)}, u32[]{:S(2)}, u32[]{:S(2)}) collective-permute-start(bf16[128,768]{1,0:T(8,128)(2,1)S(1)} %get-tuple-element.73), channel_id=1, source_target_pairs={{0,2},{1,3},{2,0},{3,1},{4,6},{5,7},{6,4},{7,5},{8,10},{9,11},{10,... | collective-permute-start | bytes 589832 | tf_op jit(solution)/shard_map/ppermute | solution.py:35
  74.2 0.8 width_grad.3
  75.0 1.4 %collective-permute-start.26 = (bf16[256,1536]{1,0:T(8,128)(2,1)S(1)}, bf16[256,1536]{1,0:T(8,128)(2,1)S(1)}, u32[]{:S(2)}, u32[]{:S(2)}) collective-permute-start(bf16[256,1536]{1,0:T(8,128)(2,1)S(1)} %get-tuple-element.69), channel_id=1, source_target_pairs={{0,1},{1,0},{2,3},{3,2},{4,5},{5,4},{6,7},{7,6},{8,9},{9,8},{10,11... | collective-permute-start | bytes 2359304 | tf_op jit(solution)/shard_map/ppermute | solution.py:28
  76.4 0.9 collective-permute-start.36
  77.3 1.0 %weight_terms.3 = (f32[128,768]{1,0:T(8,128)S(1)}, bf16[128,768]{1,0:T(8,128)(2,1)S(1)}, f32[128,768]{1,0:T(8,128)S(1)}, bf16[128,768]{1,0:T(8,128)(2,1)S(1)}) custom-call(bf16[256,1024]{1,0:T(8,128)(2,1)S(1)} %copy-done, bf16[256,1536]{1,0:T(8,128)(2,1)S(1)} %collective-permute-done.6.refs_0_.refs_1_, bf16[256,512]{1,0:T(8,128)(2,1)S(1)} %collective-permute-done.23.refs_2_, ...), custom_call_target="tpu_custom_call" | custom-call | tf_op jit(solution)/shard_map/weight_terms/pallas_call | solution.py:248
  78.4 1.2 %collective-permute-start.38 = (bf16[128,768]{1,0:T(8,128)(2,1)S(1)}, bf16[128,768]{1,0:T(8,128)(2,1)S(1)}, u32[]{:S(2)}, u32[]{:S(2)}) collective-permute-start(bf16[128,768]{1,0:T(8,128)(2,1)S(1)} %get-tuple-element.78), channel_id=1, source_target_pairs={{0,2},{1,3},{2,0},{3,1},{4,6},{5,7},{6,4},{7,5},{8,10},{9,11},{10,... | collective-permute-start | bytes 589832 | tf_op jit(solution)/shard_map/ppermute | solution.py:35
  79.5 0.9 collective-permute-start.40
  80.5 3.1 %collective-permute-start.35 = (bf16[128,768]{1,0:T(8,128)(2,1)S(1)}, bf16[128,768]{1,0:T(8,128)(2,1)S(1)}, u32[]{:S(2)}, u32[]{:S(2)}) collective-permute-start(bf16[128,768]{1,0:T(8,128)(2,1)S(1)} %add_convert_fusion.2), channel_id=1, source_target_pairs={{0,16},{4,20},{8,24},{12,28},{16,0},{20,4},{24,8},{28,12},{1,17},{... | collective-permute-start | bytes 589832 | tf_op jit(solution)/shard_map/ppermute | solution.py:47
  83.6 0.7 collective-permute-done.36
  84.4 3.9 %collective-permute-start.37 = (bf16[128,768]{1,0:T(8,128)(2,1)S(1)}, bf16[128,768]{1,0:T(8,128)(2,1)S(1)}, u32[]{:S(2)}, u32[]{:S(2)}) collective-permute-start(bf16[128,768]{1,0:T(8,128)(2,1)S(1)} %add_convert_fusion.1), channel_id=1, source_target_pairs={{0,24},{4,28},{8,0},{12,4},{16,8},{20,12},{24,16},{28,20},{1,25},{... | collective-permute-start | bytes 589832 | tf_op jit(solution)/shard_map/ppermute | solution.py:47
  88.6 3.9 %collective-permute-start.39 = (bf16[128,768]{1,0:T(8,128)(2,1)S(1)}, bf16[128,768]{1,0:T(8,128)(2,1)S(1)}, u32[]{:S(2)}, u32[]{:S(2)}) collective-permute-start(bf16[128,768]{1,0:T(8,128)(2,1)S(1)} %add_convert_fusion), channel_id=1, source_target_pairs={{0,8},{4,12},{8,16},{12,20},{16,24},{20,28},{24,0},{28,4},{1,9},{5... | collective-permute-start | bytes 589832 | tf_op jit(solution)/shard_map/ppermute | solution.py:47
  92.5 1.6 %width_grad.2 = (bf16[256,2048]{1,0:T(8,128)(2,1)S(1)}, bf16[256,512]{1,0:T(8,128)(2,1)S(1)}, bf16[16,128]{1,0:T(8,128)(2,1)}) custom-call(bf16[256,512]{1,0:T(8,128)(2,1)S(1)} %get-tuple-element.68.dquery_ref.refs_6_, bf16[256,256]{1,0:T(8,128)(2,1)S(1)} %add_convert_fusion.3.dpair_ref.refs_7_.refs_14_, ...), custom_call_target="tpu_custom_call" | custom-call | tf_op jit(solution)/shard_map/width_grad/pallas_call | solution.py:209
  94.5 4.6 %collective-permute-done.39.refs_5_ = bf16[128,768]{1,0:T(8,128)(2,1)S(1)} collective-permute-done((bf16[128,768]{1,0:T(8,128)(2,1)S(1)}, bf16[128,768]{1,0:T(8,128)(2,1)S(1)}, u32[]{:S(2)}, u32[]{:S(2)}) %collective-permute-start.39) | collective-permute-done | bytes 196640 | tf_op jit(solution)/shard_map/ppermute | solution.py:47
  99.0 1.7 %finish.1 = (bf16[256,4096]{1,0:T(8,128)(2,1)}, f32[128,768]{1,0:T(8,128)}) custom-call(bf16[256,2048]{1,0:T(8,128)(2,1)S(1)} %get-tuple-element.66.refs_0_, bf16[256,1536]{1,0:T(8,128)(2,1)S(1)} %collective-permute-done.26.refs_1_, bf16[256,512]{1,0:T(8,128)(2,1)S(1)} %get-tuple-element.70.refs_2_, bf16[128,768]{1,0:T(8,128)(2,1)S(1)} %collective-permute-done.35.refs_3_, ...), custom_call_target="tpu_custom_call" | custom-call | tf_op jit(solution)/shard_map/finish/pallas_call | solution.py:145
  (71 shorter events, 3.6 us)
Async XLA Ops:
  0.6 32.2 %copy-start.4 = (bf16[512,768]{1,0:T(8,128)(2,1)S(1)}, bf16[512,768]{1,0:T(8,128)(2,1)}, u32[]{:S(2)}) copy-start(bf16[512,768]{1,0:T(8,128)(2,1)} %param.6) | copy-start | bytes 2359300
  0.6 21.0 %copy-start.3 = (s32[1,8]{1,0:T(1,128)S(1)}, s32[1,8]{1,0:T(1,128)}, u32[]{:S(2)}) copy-start(s32[1,8]{1,0:T(1,128)} %param.8) | copy-start | bytes 100
  0.7 32.1 %copy-start.6 = (s32[1,8]{1,0:T(1,128)S(1)}, s32[1,8]{1,0:T(1,128)}, u32[]{:S(2)}) copy-start(s32[1,8]{1,0:T(1,128)} %param.9) | copy-start | bytes 100
  1.7 10.0 %collective-permute-start.1 = (bf16[128,768]{1,0:T(8,128)(2,1)S(1)}, bf16[128,768]{1,0:T(8,128)(2,1)S(1)}, u32[]{:S(2)}, u32[]{:S(2)}) collective-permute-start(bf16[128,768]{1,0:T(8,128)(2,1)S(1)} %constant_dynamic-slice_fusion), channel_id=1, source_target_pairs={{0,8},{4,12},{8,16},{12,20},{16,24},{20,28},{24,0},{28,4},{1,9},{5... | collective-permute-start | bytes 589832 | tf_op jit(solution)/shard_map/ppermute | solution.py:47
  11.7 20.5 %collective-permute-start.6 = (bf16[256,1536]{1,0:T(8,128)(2,1)}, bf16[256,1536]{1,0:T(8,128)(2,1)S(1)}, u32[]{:S(2)}, u32[]{:S(2)}) collective-permute-start(bf16[256,1536]{1,0:T(8,128)(2,1)} %get-tuple-element.53), channel_id=1, source_target_pairs={{0,1},{1,0},{2,3},{3,2},{4,5},{5,4},{6,7},{7,6},{8,9},{9,8},{10,11... | collective-permute-start | bytes 2359304 | tf_op jit(solution)/shard_map/ppermute | solution.py:28
  13.2 6.9 %collective-permute-start.3 = (bf16[128,768]{1,0:T(8,128)(2,1)S(1)}, bf16[128,768]{1,0:T(8,128)(2,1)S(1)}, u32[]{:S(2)}, u32[]{:S(2)}) collective-permute-start(bf16[128,768]{1,0:T(8,128)(2,1)S(1)} %constant_dynamic-slice_fusion), channel_id=1, source_target_pairs={{0,24},{4,28},{8,0},{12,4},{16,8},{20,12},{24,16},{28,20},{1,25},{... | collective-permute-start | bytes 589832 | tf_op jit(solution)/shard_map/ppermute | solution.py:47
  14.9 11.5 %collective-permute-start = (bf16[128,768]{1,0:T(8,128)(2,1)S(1)}, bf16[128,768]{1,0:T(8,128)(2,1)S(1)}, u32[]{:S(2)}, u32[]{:S(2)}) collective-permute-start(bf16[128,768]{1,0:T(8,128)(2,1)S(1)} %constant_dynamic-slice_fusion), channel_id=1, source_target_pairs={{0,16},{4,20},{8,24},{12,28},{16,0},{20,4},{24,8},{28,12},{1,17},{... | collective-permute-start | bytes 589832 | tf_op jit(solution)/shard_map/ppermute | solution.py:47
  14.9 11.5 %collective-permute-start.2 = (bf16[128,768]{1,0:T(8,128)(2,1)S(1)}, bf16[128,768]{1,0:T(8,128)(2,1)S(1)}, u32[]{:S(2)}, u32[]{:S(2)}) collective-permute-start(bf16[128,768]{1,0:T(8,128)(2,1)S(1)} %collective-permute-done.1.refs_5_.refs_1_.refs_2_.refs_0_), channel_id=1, source_target_pairs={{0,2},{1,3},{2,0},{3,1},{4,6},{5,7},{6,4},{7,5},{8,10},{9,11},{10,... | collective-permute-start | bytes 589832 | tf_op jit(solution)/shard_map/ppermute | solution.py:35
  20.1 6.4 %collective-permute-start.4 = (bf16[128,768]{1,0:T(8,128)(2,1)S(1)}, bf16[128,768]{1,0:T(8,128)(2,1)S(1)}, u32[]{:S(2)}, u32[]{:S(2)}) collective-permute-start(bf16[128,768]{1,0:T(8,128)(2,1)S(1)} %collective-permute-done.3.refs_9_.refs_5_.refs_6_.refs_4_), channel_id=1, source_target_pairs={{0,2},{1,3},{2,0},{3,1},{4,6},{5,7},{6,4},{7,5},{8,10},{9,11},{10,... | collective-permute-start | bytes 589832 | tf_op jit(solution)/shard_map/ppermute | solution.py:35
  26.4 5.7 %collective-permute-start.5 = (bf16[128,768]{1,0:T(8,128)(2,1)S(1)}, bf16[128,768]{1,0:T(8,128)(2,1)S(1)}, u32[]{:S(2)}, u32[]{:S(2)}) collective-permute-start(bf16[128,768]{1,0:T(8,128)(2,1)S(1)} %collective-permute-done.refs_7_.refs_3_.refs_4_.refs_2_), channel_id=1, source_target_pairs={{0,2},{1,3},{2,0},{3,1},{4,6},{5,7},{6,4},{7,5},{8,10},{9,11},{10,... | collective-permute-start | bytes 589832 | tf_op jit(solution)/shard_map/ppermute | solution.py:35
  28.0 4.7 %collective-permute-start.9 = (bf16[128,768]{1,0:T(8,128)(2,1)S(1)}, bf16[128,768]{1,0:T(8,128)(2,1)S(1)}, u32[]{:S(2)}, u32[]{:S(2)}) collective-permute-start(bf16[128,768]{1,0:T(8,128)(2,1)S(1)} %collective-permute-done.1.refs_5_.refs_1_.refs_2_.refs_0_), channel_id=1, source_target_pairs={{0,4},{4,0},{8,12},{12,8},{16,20},{20,16},{24,28},{28,24},{1,5},{5... | collective-permute-start | bytes 589832 | tf_op jit(solution)/shard_map/ppermute | solution.py:40
  28.0 5.5 %collective-permute-start.11 = (bf16[128,768]{1,0:T(8,128)(2,1)S(1)}, bf16[128,768]{1,0:T(8,128)(2,1)S(1)}, u32[]{:S(2)}, u32[]{:S(2)}) collective-permute-start(bf16[128,768]{1,0:T(8,128)(2,1)S(1)} %collective-permute-done.refs_7_.refs_3_.refs_4_.refs_2_), channel_id=1, source_target_pairs={{0,4},{4,0},{8,12},{12,8},{16,20},{20,16},{24,28},{28,24},{1,5},{5... | collective-permute-start | bytes 589832 | tf_op jit(solution)/shard_map/ppermute | solution.py:40
  28.5 4.5 %collective-permute-start.10 = (bf16[128,768]{1,0:T(8,128)(2,1)S(1)}, bf16[128,768]{1,0:T(8,128)(2,1)S(1)}, u32[]{:S(2)}, u32[]{:S(2)}) collective-permute-start(bf16[128,768]{1,0:T(8,128)(2,1)S(1)} %collective-permute-done.2.refs_6_.refs_2_.refs_3_.refs_1_), channel_id=1, source_target_pairs={{0,4},{4,0},{8,12},{12,8},{16,20},{20,16},{24,28},{28,24},{1,5},{5... | collective-permute-start | bytes 589832 | tf_op jit(solution)/shard_map/ppermute | solution.py:40
  32.1 1.4 %collective-permute-start.13 = (bf16[128,768]{1,0:T(8,128)(2,1)S(1)}, bf16[128,768]{1,0:T(8,128)(2,1)S(1)}, u32[]{:S(2)}, u32[]{:S(2)}) collective-permute-start(bf16[128,768]{1,0:T(8,128)(2,1)S(1)} %collective-permute-done.3.refs_9_.refs_5_.refs_6_.refs_4_), channel_id=1, source_target_pairs={{0,4},{4,0},{8,12},{12,8},{16,20},{20,16},{24,28},{28,24},{1,5},{5... | collective-permute-start | bytes 589832 | tf_op jit(solution)/shard_map/ppermute | solution.py:40
  32.1 1.8 %collective-permute-start.14 = (bf16[128,768]{1,0:T(8,128)(2,1)S(1)}, bf16[128,768]{1,0:T(8,128)(2,1)S(1)}, u32[]{:S(2)}, u32[]{:S(2)}) collective-permute-start(bf16[128,768]{1,0:T(8,128)(2,1)S(1)} %collective-permute-done.4.refs_10_.refs_6_.refs_7_.refs_5_), channel_id=1, source_target_pairs={{0,4},{4,0},{8,12},{12,8},{16,20},{20,16},{24,28},{28,24},{1,5},{5... | collective-permute-start | bytes 589832 | tf_op jit(solution)/shard_map/ppermute | solution.py:40
  32.7 1.5 %collective-permute-start.12 = (bf16[128,768]{1,0:T(8,128)(2,1)S(1)}, bf16[128,768]{1,0:T(8,128)(2,1)S(1)}, u32[]{:S(2)}, u32[]{:S(2)}) collective-permute-start(bf16[128,768]{1,0:T(8,128)(2,1)S(1)} %collective-permute-done.5.refs_8_.refs_4_.refs_5_.refs_3_), channel_id=1, source_target_pairs={{0,4},{4,0},{8,12},{12,8},{16,20},{20,16},{24,28},{28,24},{1,5},{5... | collective-permute-start | bytes 589832 | tf_op jit(solution)/shard_map/ppermute | solution.py:40
  32.8 2.7 %copy-start.1 = (bf16[256,1024]{1,0:T(8,128)(2,1)S(1)}, bf16[256,1024]{1,0:T(8,128)(2,1)}, u32[]{:S(2)}) copy-start(bf16[256,1024]{1,0:T(8,128)(2,1)} %get-tuple-element.44.refs_1_) | copy-start | bytes 1572868
  32.8 4.4 %copy-start = (bf16[256,1024]{1,0:T(8,128)(2,1)S(1)}, bf16[256,1024]{1,0:T(8,128)(2,1)}, u32[]{:S(2)}) copy-start(bf16[256,1024]{1,0:T(8,128)(2,1)} %get-tuple-element.43.refs_0_) | copy-start | bytes 1572868
  32.8 4.4 %copy-start.2 = (bf16[256,512]{1,0:T(8,128)(2,1)S(1)}, bf16[256,512]{1,0:T(8,128)(2,1)}, u32[]{:S(2)}) copy-start(bf16[256,512]{1,0:T(8,128)(2,1)} %get-tuple-element.67.refs_2_) | copy-start | bytes 786436
  32.9 2.6 %collective-permute-start.7 = (bf16[128,768]{1,0:T(8,128)(2,1)S(1)}, bf16[128,768]{1,0:T(8,128)(2,1)S(1)}, u32[]{:S(2)}, u32[]{:S(2)}) collective-permute-start(bf16[128,768]{1,0:T(8,128)(2,1)S(1)} %get-tuple-element.86.refs_3_.refs_0_), channel_id=1, source_target_pairs={{0,4},{4,0},{8,12},{12,8},{16,20},{20,16},{24,28},{28,24},{1,5},{5... | collective-permute-start | bytes 589832 | tf_op jit(solution)/shard_map/ppermute | solution.py:40
  33.4 2.2 %collective-permute-start.8 = (bf16[128,768]{1,0:T(8,128)(2,1)S(1)}, bf16[128,768]{1,0:T(8,128)(2,1)S(1)}, u32[]{:S(2)}, u32[]{:S(2)}) collective-permute-start(bf16[128,768]{1,0:T(8,128)(2,1)S(1)} %get-tuple-element.85.refs_4_.refs_1_), channel_id=1, source_target_pairs={{0,4},{4,0},{8,12},{12,8},{16,20},{20,16},{24,28},{28,24},{1,5},{5... | collective-permute-start | bytes 589832 | tf_op jit(solution)/shard_map/ppermute | solution.py:40
  33.6 3.6 %collective-permute-start.15 = (bf16[128,768]{1,0:T(8,128)(2,1)S(1)}, bf16[128,768]{1,0:T(8,128)(2,1)S(1)}, u32[]{:S(2)}, u32[]{:S(2)}) collective-permute-start(bf16[128,768]{1,0:T(8,128)(2,1)S(1)} %get-tuple-element.84.refs_19_.refs_16_), channel_id=1, source_target_pairs={{0,4},{4,0},{8,12},{12,8},{16,20},{20,16},{24,28},{28,24},{1,5},{5... | collective-permute-start | bytes 589832 | tf_op jit(solution)/shard_map/ppermute | solution.py:40
  34.0 3.2 %collective-permute-start.16 = (bf16[128,768]{1,0:T(8,128)(2,1)S(1)}, bf16[128,768]{1,0:T(8,128)(2,1)S(1)}, u32[]{:S(2)}, u32[]{:S(2)}) collective-permute-start(bf16[128,768]{1,0:T(8,128)(2,1)S(1)} %get-tuple-element.83.refs_20_.refs_17_), channel_id=1, source_target_pairs={{0,4},{4,0},{8,12},{12,8},{16,20},{20,16},{24,28},{28,24},{1,5},{5... | collective-permute-start | bytes 589832 | tf_op jit(solution)/shard_map/ppermute | solution.py:40
  34.9 6.4 %collective-permute-start.18 = (bf16[256,256]{1,0:T(8,128)(2,1)S(1)}, bf16[256,256]{1,0:T(8,128)(2,1)S(1)}, u32[]{:S(2)}, u32[]{:S(2)}) collective-permute-start(bf16[256,256]{1,0:T(8,128)(2,1)S(1)} %get-tuple-element.61), channel_id=1, source_target_pairs={{0,1},{1,0},{2,3},{3,2},{4,5},{5,4},{6,7},{7,6},{8,9},{9,8},{10,11... | collective-permute-start | bytes 393224 | tf_op jit(solution)/shard_map/ppermute | solution.py:28
  35.6 31.3 %collective-permute-start.27 = (bf16[256,1024]{1,0:T(8,128)(2,1)S(1)}, bf16[256,1024]{1,0:T(8,128)(2,1)S(1)}, u32[]{:S(2)}, u32[]{:S(2)}) collective-permute-start(bf16[256,1024]{1,0:T(8,128)(2,1)S(1)} %copy-done.1), channel_id=1, source_target_pairs={{0,4},{4,0},{8,12},{12,8},{16,20},{20,16},{24,28},{28,24},{1,5},{5... | collective-permute-start | bytes 1572872 | tf_op jit(solution)/shard_map/ppermute | solution.py:40
  35.7 15.4 %collective-permute-start.17 = (bf16[256,512]{1,0:T(8,128)(2,1)S(1)}, bf16[256,512]{1,0:T(8,128)(2,1)S(1)}, u32[]{:S(2)}, u32[]{:S(2)}) collective-permute-start(bf16[256,512]{1,0:T(8,128)(2,1)S(1)} %get-tuple-element.59), channel_id=1, source_target_pairs={{0,1},{1,0},{2,3},{3,2},{4,5},{5,4},{6,7},{7,6},{8,9},{9,8},{10,11... | collective-permute-start | bytes 786440 | tf_op jit(solution)/shard_map/ppermute | solution.py:28
  37.2 10.0 %copy-start.5 = (bf16[1,256,512]{2,1,0:T(8,128)(2,1)S(1)}, bf16[1,256,512]{2,1,0:T(8,128)(2,1)}, u32[]{:S(2)}) copy-start(bf16[1,256,512]{2,1,0:T(8,128)(2,1)} %param.7) | copy-start | bytes 786436
  41.3 8.7 %collective-permute-start.19 = (bf16[256,256]{1,0:T(8,128)(2,1)S(1)}, bf16[256,256]{1,0:T(8,128)(2,1)S(1)}, u32[]{:S(2)}, u32[]{:S(2)}) collective-permute-start(bf16[256,256]{1,0:T(8,128)(2,1)S(1)} %add_convert_fusion.4.refs_2_), channel_id=1, source_target_pairs={{0,2},{1,3},{4,6},{5,7},{8,10},{9,11},{12,14},{13,15},{16,18},{17,... | collective-permute-start | bytes 393224 | tf_op jit(solution)/shard_map/ppermute | solution.py:53
  44.8 6.2 %collective-permute-start.20 = (bf16[256,256]{1,0:T(8,128)(2,1)S(1)}, bf16[256,256]{1,0:T(8,128)(2,1)S(1)}, u32[]{:S(2)}, u32[]{:S(2)}) collective-permute-start(bf16[256,256]{1,0:T(8,128)(2,1)S(1)} %add_convert_fusion.4.refs_2_), channel_id=1, source_target_pairs={{0,1},{1,2},{2,3},{4,5},{5,6},{6,7},{8,9},{9,10},{10,11},{12,13},{... | collective-permute-start | bytes 393224 | tf_op jit(solution)/shard_map/ppermute | solution.py:53
  47.4 23.8 %collective-permute-start.28 = (bf16[256,1536]{1,0:T(8,128)(2,1)S(1)}, bf16[256,1536]{1,0:T(8,128)(2,1)S(1)}, u32[]{:S(2)}, u32[]{:S(2)}) collective-permute-start(bf16[256,1536]{1,0:T(8,128)(2,1)S(1)} %collective-permute-done.6.refs_0_.refs_1_), channel_id=1, source_target_pairs={{0,4},{4,0},{8,12},{12,8},{16,20},{20,16},{24,28},{28,24},{1,5},{5... | collective-permute-start | bytes 2359304 | tf_op jit(solution)/shard_map/ppermute | solution.py:40
  50.1 7.7 %collective-permute-start.23 = (bf16[256,512]{1,0:T(8,128)(2,1)S(1)}, bf16[256,512]{1,0:T(8,128)(2,1)S(1)}, u32[]{:S(2)}, u32[]{:S(2)}) collective-permute-start(bf16[256,512]{1,0:T(8,128)(2,1)S(1)} %copy-done.2), channel_id=1, source_target_pairs={{0,1},{1,0},{2,3},{3,2},{4,5},{5,4},{6,7},{7,6},{8,9},{9,8},{10,11... | collective-permute-start | bytes 786440 | tf_op jit(solution)/shard_map/ppermute | solution.py:28
  55.2 6.9 %collective-permute-start.22 = (bf16[256,256]{1,0:T(8,128)(2,1)S(1)}, bf16[256,256]{1,0:T(8,128)(2,1)S(1)}, u32[]{:S(2)}, u32[]{:S(2)}) collective-permute-start(bf16[256,256]{1,0:T(8,128)(2,1)S(1)} %get-tuple-element.88), channel_id=1, source_target_pairs={{2,0},{3,1},{6,4},{7,5},{10,8},{11,9},{14,12},{15,13},{18,16},{19,... | collective-permute-start | bytes 393224 | tf_op jit(solution)/shard_map/ppermute | solution.py:53
  56.5 7.3 %collective-permute-start.21 = (bf16[256,256]{1,0:T(8,128)(2,1)S(1)}, bf16[256,256]{1,0:T(8,128)(2,1)S(1)}, u32[]{:S(2)}, u32[]{:S(2)}) collective-permute-start(bf16[256,256]{1,0:T(8,128)(2,1)S(1)} %get-tuple-element.87), channel_id=1, source_target_pairs={{1,0},{2,1},{3,2},{5,4},{6,5},{7,6},{9,8},{10,9},{11,10},{13,12},{... | collective-permute-start | bytes 393224 | tf_op jit(solution)/shard_map/ppermute | solution.py:53
  57.8 9.4 %collective-permute-start.24 = (bf16[256,512]{1,0:T(8,128)(2,1)S(1)}, bf16[256,512]{1,0:T(8,128)(2,1)S(1)}, u32[]{:S(2)}, u32[]{:S(2)}) collective-permute-start(bf16[256,512]{1,0:T(8,128)(2,1)S(1)} %get-tuple-element.68.dquery_ref.refs_6_), channel_id=1, source_target_pairs={{0,1},{1,0},{2,3},{3,2},{4,5},{5,4},{6,7},{7,6},{8,9},{9,8},{10,11... | collective-permute-start | bytes 786440 | tf_op jit(solution)/shard_map/ppermute | solution.py:28
  62.0 7.8 %collective-permute-start.30 = (bf16[256,512]{1,0:T(8,128)(2,1)S(1)}, bf16[256,512]{1,0:T(8,128)(2,1)S(1)}, u32[]{:S(2)}, u32[]{:S(2)}) collective-permute-start(bf16[256,512]{1,0:T(8,128)(2,1)S(1)} %get-tuple-element.68.dquery_ref.refs_6_), channel_id=1, source_target_pairs={{0,4},{4,0},{8,12},{12,8},{16,20},{20,16},{24,28},{28,24},{1,5},{5... | collective-permute-start | bytes 786440 | tf_op jit(solution)/shard_map/ppermute | solution.py:40
  63.8 5.9 %collective-permute-start.25 = (bf16[256,256]{1,0:T(8,128)(2,1)S(1)}, bf16[256,256]{1,0:T(8,128)(2,1)S(1)}, u32[]{:S(2)}, u32[]{:S(2)}) collective-permute-start(bf16[256,256]{1,0:T(8,128)(2,1)S(1)} %add_convert_fusion.3.dpair_ref.refs_7_.refs_14_), channel_id=1, source_target_pairs={{0,1},{1,0},{2,3},{3,2},{4,5},{5,4},{6,7},{7,6},{8,9},{9,8},{10,11... | collective-permute-start | bytes 393224 | tf_op jit(solution)/shard_map/ppermute | solution.py:28
  66.8 4.3 %collective-permute-start.29 = (bf16[256,512]{1,0:T(8,128)(2,1)S(1)}, bf16[256,512]{1,0:T(8,128)(2,1)S(1)}, u32[]{:S(2)}, u32[]{:S(2)}) collective-permute-start(bf16[256,512]{1,0:T(8,128)(2,1)S(1)} %collective-permute-done.23.refs_2_), channel_id=1, source_target_pairs={{0,4},{4,0},{8,12},{12,8},{16,20},{20,16},{24,28},{28,24},{1,5},{5... | collective-permute-start | bytes 786440 | tf_op jit(solution)/shard_map/ppermute | solution.py:40
  67.1 4.2 %collective-permute-start.32 = (bf16[256,512]{1,0:T(8,128)(2,1)S(1)}, bf16[256,512]{1,0:T(8,128)(2,1)S(1)}, u32[]{:S(2)}, u32[]{:S(2)}) collective-permute-start(bf16[256,512]{1,0:T(8,128)(2,1)S(1)} %collective-permute-done.24.dquery_ref.refs_8_), channel_id=1, source_target_pairs={{0,4},{4,0},{8,12},{12,8},{16,20},{20,16},{24,28},{28,24},{1,5},{5... | collective-permute-start | bytes 786440 | tf_op jit(solution)/shard_map/ppermute | solution.py:40
  69.8 1.3 %collective-permute-start.31 = (bf16[256,256]{1,0:T(8,128)(2,1)S(1)}, bf16[256,256]{1,0:T(8,128)(2,1)S(1)}, u32[]{:S(2)}, u32[]{:S(2)}) collective-permute-start(bf16[256,256]{1,0:T(8,128)(2,1)S(1)} %add_convert_fusion.3.dpair_ref.refs_7_.refs_14_), channel_id=1, source_target_pairs={{0,4},{4,0},{8,12},{12,8},{16,20},{20,16},{24,28},{28,24},{1,5},{5... | collective-permute-start | bytes 393224 | tf_op jit(solution)/shard_map/ppermute | solution.py:40
  69.8 1.5 %collective-permute-start.33 = (bf16[256,256]{1,0:T(8,128)(2,1)S(1)}, bf16[256,256]{1,0:T(8,128)(2,1)S(1)}, u32[]{:S(2)}, u32[]{:S(2)}) collective-permute-start(bf16[256,256]{1,0:T(8,128)(2,1)S(1)} %collective-permute-done.25.dpair_ref.refs_9_), channel_id=1, source_target_pairs={{0,4},{4,0},{8,12},{12,8},{16,20},{20,16},{24,28},{28,24},{1,5},{5... | collective-permute-start | bytes 393224 | tf_op jit(solution)/shard_map/ppermute | solution.py:40
  72.3 8.1 %collective-permute-start.34 = (bf16[128,768]{1,0:T(8,128)(2,1)S(1)}, bf16[128,768]{1,0:T(8,128)(2,1)S(1)}, u32[]{:S(2)}, u32[]{:S(2)}) collective-permute-start(bf16[128,768]{1,0:T(8,128)(2,1)S(1)} %get-tuple-element.73), channel_id=1, source_target_pairs={{0,2},{1,3},{2,0},{3,1},{4,6},{5,7},{6,4},{7,5},{8,10},{9,11},{10,... | collective-permute-start | bytes 589832 | tf_op jit(solution)/shard_map/ppermute | solution.py:35
  75.0 24.0 %collective-permute-start.26 = (bf16[256,1536]{1,0:T(8,128)(2,1)S(1)}, bf16[256,1536]{1,0:T(8,128)(2,1)S(1)}, u32[]{:S(2)}, u32[]{:S(2)}) collective-permute-start(bf16[256,1536]{1,0:T(8,128)(2,1)S(1)} %get-tuple-element.69), channel_id=1, source_target_pairs={{0,1},{1,0},{2,3},{3,2},{4,5},{5,4},{6,7},{7,6},{8,9},{9,8},{10,11... | collective-permute-start | bytes 2359304 | tf_op jit(solution)/shard_map/ppermute | solution.py:28
  76.4 7.9 %collective-permute-start.36 = (bf16[128,768]{1,0:T(8,128)(2,1)S(1)}, bf16[128,768]{1,0:T(8,128)(2,1)S(1)}, u32[]{:S(2)}, u32[]{:S(2)}) collective-permute-start(bf16[128,768]{1,0:T(8,128)(2,1)S(1)} %get-tuple-element.75), channel_id=1, source_target_pairs={{0,2},{1,3},{2,0},{3,1},{4,6},{5,7},{6,4},{7,5},{8,10},{9,11},{10,... | collective-permute-start | bytes 589832 | tf_op jit(solution)/shard_map/ppermute | solution.py:35
  78.4 10.2 %collective-permute-start.38 = (bf16[128,768]{1,0:T(8,128)(2,1)S(1)}, bf16[128,768]{1,0:T(8,128)(2,1)S(1)}, u32[]{:S(2)}, u32[]{:S(2)}) collective-permute-start(bf16[128,768]{1,0:T(8,128)(2,1)S(1)} %get-tuple-element.78), channel_id=1, source_target_pairs={{0,2},{1,3},{2,0},{3,1},{4,6},{5,7},{6,4},{7,5},{8,10},{9,11},{10,... | collective-permute-start | bytes 589832 | tf_op jit(solution)/shard_map/ppermute | solution.py:35
  79.5 14.6 %collective-permute-start.40 = (bf16[128,768]{1,0:T(8,128)(2,1)S(1)}, bf16[128,768]{1,0:T(8,128)(2,1)S(1)}, u32[]{:S(2)}, u32[]{:S(2)}) collective-permute-start(bf16[128,768]{1,0:T(8,128)(2,1)S(1)} %get-tuple-element.80), channel_id=1, source_target_pairs={{0,2},{1,3},{2,0},{3,1},{4,6},{5,7},{6,4},{7,5},{8,10},{9,11},{10,... | collective-permute-start | bytes 589832 | tf_op jit(solution)/shard_map/ppermute | solution.py:35
  80.5 13.6 %collective-permute-start.35 = (bf16[128,768]{1,0:T(8,128)(2,1)S(1)}, bf16[128,768]{1,0:T(8,128)(2,1)S(1)}, u32[]{:S(2)}, u32[]{:S(2)}) collective-permute-start(bf16[128,768]{1,0:T(8,128)(2,1)S(1)} %add_convert_fusion.2), channel_id=1, source_target_pairs={{0,16},{4,20},{8,24},{12,28},{16,0},{20,4},{24,8},{28,12},{1,17},{... | collective-permute-start | bytes 589832 | tf_op jit(solution)/shard_map/ppermute | solution.py:47
  84.4 10.1 %collective-permute-start.37 = (bf16[128,768]{1,0:T(8,128)(2,1)S(1)}, bf16[128,768]{1,0:T(8,128)(2,1)S(1)}, u32[]{:S(2)}, u32[]{:S(2)}) collective-permute-start(bf16[128,768]{1,0:T(8,128)(2,1)S(1)} %add_convert_fusion.1), channel_id=1, source_target_pairs={{0,24},{4,28},{8,0},{12,4},{16,8},{20,12},{24,16},{28,20},{1,25},{... | collective-permute-start | bytes 589832 | tf_op jit(solution)/shard_map/ppermute | solution.py:47
  88.6 10.5 %collective-permute-start.39 = (bf16[128,768]{1,0:T(8,128)(2,1)S(1)}, bf16[128,768]{1,0:T(8,128)(2,1)S(1)}, u32[]{:S(2)}, u32[]{:S(2)}) collective-permute-start(bf16[128,768]{1,0:T(8,128)(2,1)S(1)} %add_convert_fusion), channel_id=1, source_target_pairs={{0,8},{4,12},{8,16},{12,20},{16,24},{20,28},{24,0},{28,4},{1,9},{5... | collective-permute-start | bytes 589832 | tf_op jit(solution)/shard_map/ppermute | solution.py:47

commit v11 on v10

--- a/solution.py
+++ b/solution.py
@@ -163,27 +163,27 @@
         first -= part.shape[1]
 
 
-def project_kernel(span, per, qwidth, count, *refs):
-    tokens, pieces, (query_ref, pair_ref) = refs[:count], refs[count:-2], refs[-2:]
+def project_kernel(span, per, cuts, count, *refs):
+    tokens, pieces, out_refs = refs[:count], refs[count : -len(cuts)], refs[-len(cuts) :]
+    low, high = cuts[0][0], cuts[-1][1]
     total = None
     for g in range(len(pieces) // per):
-        rows = jnp.concatenate([r[...] for r in pieces[g * per : (g + 1) * per]], axis=0)
+        rows = jnp.concatenate([r[:, low:high] for r in pieces[g * per : (g + 1) * per]], axis=0)
         term = dot(cut(tokens, g * span, span), rows)
         total = term if total is None else total + term
-    query_ref[...] = total[:, :qwidth].astype(query_ref.dtype)
-    pair_ref[...] = total[:, qwidth:].astype(pair_ref.dtype)
-
-
-def project(tokens, groups, qwidth, kind):
+    for (first, end), ref in zip(cuts, out_refs):
+        ref[...] = total[:, first - low : end - low].astype(ref.dtype)
+
+
+def project(tokens, groups, cuts, kind):
     rows = tokens[0].shape[0]
-    cols = groups[0][0].shape[1]
     pieces = [piece for group in groups for piece in group]
     span = sum(piece.shape[0] for piece in groups[0])
     return pl.pallas_call(
-        functools.partial(project_kernel, span, len(groups[0]), qwidth, len(tokens)),
+        functools.partial(project_kernel, span, len(groups[0]), cuts, len(tokens)),
         in_specs=[VMEM] * (len(tokens) + len(pieces)),
-        out_specs=[VMEM] * 2,
-        out_shape=[jax.ShapeDtypeStruct((rows, w), kind) for w in (qwidth, cols - qwidth)],
+        out_specs=[VMEM] * len(cuts),
+        out_shape=[jax.ShapeDtypeStruct((rows, end - first), kind) for first, end in cuts],
         compiler_params=pltpu.CompilerParams(vmem_limit_bytes=20 * 2**20),
         name="project",
     )(*tokens, *pieces)
@@ -387,9 +387,11 @@
     groups = groups_own + groups_across
     groups_far = groups_own[1:] + groups_across[1:]
 
-    query_sent, pair_sent = project([far_other], groups_far, qwidth, BF16)
+    query_cut, pair_cut = (0, qwidth), (qwidth, cols)
+    (pair_sent,) = project([far_other], groups_far, [pair_cut], BF16)
+    (query_sent,) = project([far_other], groups_far, [query_cut], BF16)
     pair_from, query_from = swap_x(pair_sent), swap_x(query_sent)
-    query, pair = project([mine_own, mine_across, near], groups + groups_near, qwidth, F32)
+    query, pair = project([mine_own, mine_across, near], groups + groups_near, [query_cut, pair_cut], F32)
     pair = (pair + pair_from.astype(F32)).astype(BF16)
 
     doc_row, flag_row = doc_lengths[0], kept_flags[0]
@@ -416,7 +418,7 @@
     right += [[swap_core(g) for g in group] for group in right]
     order = sorted(range(chips), key=lambda k: (k == 0, -min(k, chips - k), k))
     parts, after = [], dpair
-    for steps in (order[: chips // 2], order[chips // 2 :]):
+    for steps in (order[:1], order[1:]):
         terms = weight_terms(steps, rest, width, chips, left, right, after)
         if not parts:
             grad_sent, after = width_grad(dquery_other, dpair_other, [groups_far])

time: 101 us -> 100 us (0.990)
    ppermute x7, waiting for transfers between devices: 4.72 us -> 5.74 us  [shift_rest(): return lax.ppermute(array, 'seq', pairs)]
    pallas_call x2 -> x3, Pallas kernels: 1.97 us -> 2.15 us  [project(): pl.pallas_call(functools.partial(project_kernel, span, len(groups[0]), cu...]
  transfers between devices with their start and end apart: 41 -> 41, of which waited for: 18 -> 17; matrix products, arithmetic and copies ran while one was open for 1% -> 1% of each run, Pallas kernels for 12% -> 13%
where the time goes in v11:
time: 100 us
  starting transfers between devices  47.1 us (47%)
  waiting for transfers between devices  35 us (35%)
  Pallas kernels  15.3 us (15%)
  local copies, waits for them, and re-layouts  1.12 us (1%)
    ppermute x6, waiting for transfers between devices, shift_chip(): return lax.ppermute(array, 'dp', pairs)  16.4 us
    ppermute x6, starting transfers between devices, shift_chip(): return lax.ppermute(array, 'dp', pairs)  15.6 us
    ppermute x7, starting transfers between devices, swap_x(): return lax.ppermute(array, 'seq', [(i, i ^ 1) for i in range(count)])  10.6 us
    ppermute x7, starting transfers between devices, shift_rest(): return lax.ppermute(array, 'seq', pairs)  9.84 us
    ppermute x4, starting transfers between devices, shift_seq(): return lax.ppermute(array, 'seq', pairs)  8.18 us
    ppermute x4, waiting for transfers between devices, shift_seq(): return lax.ppermute(array, 'seq', pairs)  6.44 us
    ppermute x7, waiting for transfers between devices, shift_rest(): return lax.ppermute(array, 'seq', pairs)  5.74 us
    ppermute x7, waiting for transfers between devices, swap_x(): return lax.ppermute(array, 'seq', [(i, i ^ 1) for i in range(count)])  5.23 us
  transfers between devices with their start and end apart: 41, of which 17 were waited for; matrix products, arithmetic and copies ran while one was open for 1% of the time, Pallas kernels for 13%

profile of v11, /device:TPU:0, one launch (start us, length us, event | category | flops | bytes accessed | tf_op | source)
XLA Modules:
  0.0 100.0 jit_solution(12960428038746271938)
XLA Ops:
  0.7 1.0 %constant_dynamic-slice_fusion = bf16[128,768]{1,0:T(8,128)(2,1)S(1)} fusion(bf16[512,768]{1,0:T(8,128)(2,1)} %param.6, s32[]{:T(128)S(6)} %select_n.64), kind=kLoop, calls=%fused_computation.11 | loop fusion | bytes 393220 | tf_op jit(solution)/shard_map/dynamic_slice | solution.py:365
  1.7 3.1 %collective-permute-start.1 = (bf16[128,768]{1,0:T(8,128)(2,1)S(1)}, bf16[128,768]{1,0:T(8,128)(2,1)S(1)}, u32[]{:S(2)}, u32[]{:S(2)}) collective-permute-start(bf16[128,768]{1,0:T(8,128)(2,1)S(1)} %constant_dynamic-slice_fusion), channel_id=1, source_target_pairs={{0,8},{4,12},{8,16},{12,20},{16,24},{20,28},{24,0},{28,4},{1,9},{5... | collective-permute-start | bytes 589832 | tf_op jit(solution)/shard_map/ppermute | solution.py:47
  4.8 2.8 %split_tokens.1 = (bf16[256,1024]{1,0:T(8,128)(2,1)}, bf16[256,1024]{1,0:T(8,128)(2,1)}, bf16[256,1536]{1,0:T(8,128)(2,1)}, bf16[256,512]{1,0:T(8,128)(2,1)}) custom-call(bf16[256,4096]{1,0:T(8,128)(2,1)} %bitcast.26), custom_call_target="tpu_custom_call" | custom-call | tf_op jit(solution)/shard_map/split_tokens/pallas_call | solution.py:105
  7.6 4.1 %collective-permute-done.1.refs_5_.refs_1_.refs_2_.refs_0_ = bf16[128,768]{1,0:T(8,128)(2,1)S(1)} collective-permute-done((bf16[128,768]{1,0:T(8,128)(2,1)S(1)}, bf16[128,768]{1,0:T(8,128)(2,1)S(1)}, u32[]{:S(2)}, u32[]{:S(2)}) %collective-permute-start.1) | collective-permute-done | bytes 196640 | tf_op jit(solution)/shard_map/ppermute | solution.py:47
  11.7 1.5 %collective-permute-start.6 = (bf16[256,1536]{1,0:T(8,128)(2,1)}, bf16[256,1536]{1,0:T(8,128)(2,1)S(1)}, u32[]{:S(2)}, u32[]{:S(2)}) collective-permute-start(bf16[256,1536]{1,0:T(8,128)(2,1)} %get-tuple-element.51), channel_id=1, source_target_pairs={{0,1},{1,0},{2,3},{3,2},{4,5},{5,4},{6,7},{7,6},{8,9},{9,8},{10,11... | collective-permute-start | bytes 2359304 | tf_op jit(solution)/shard_map/ppermute | solution.py:28
  13.2 1.7 %collective-permute-start.3 = (bf16[128,768]{1,0:T(8,128)(2,1)S(1)}, bf16[128,768]{1,0:T(8,128)(2,1)S(1)}, u32[]{:S(2)}, u32[]{:S(2)}) collective-permute-start(bf16[128,768]{1,0:T(8,128)(2,1)S(1)} %constant_dynamic-slice_fusion), channel_id=1, source_target_pairs={{0,24},{4,28},{8,0},{12,4},{16,8},{20,12},{24,16},{28,20},{1,25},{... | collective-permute-start | bytes 589832 | tf_op jit(solution)/shard_map/ppermute | solution.py:47
  14.9 1.5 %collective-permute-start.2 = (bf16[128,768]{1,0:T(8,128)(2,1)S(1)}, bf16[128,768]{1,0:T(8,128)(2,1)S(1)}, u32[]{:S(2)}, u32[]{:S(2)}) collective-permute-start(bf16[128,768]{1,0:T(8,128)(2,1)S(1)} %collective-permute-done.1.refs_5_.refs_1_.refs_2_.refs_0_), channel_id=1, source_target_pairs={{0,2},{1,3},{2,0},{3,1},{4,6},{5,7},{6,4},{7,5},{8,10},{9,11},{10,... | collective-permute-start | bytes 589832 | tf_op jit(solution)/shard_map/ppermute | solution.py:35
  16.4 3.6 %collective-permute-done.3.refs_9_.refs_5_.refs_6_.refs_4_ = bf16[128,768]{1,0:T(8,128)(2,1)S(1)} collective-permute-done((bf16[128,768]{1,0:T(8,128)(2,1)S(1)}, bf16[128,768]{1,0:T(8,128)(2,1)S(1)}, u32[]{:S(2)}, u32[]{:S(2)}) %collective-permute-start.3) | collective-permute-done | bytes 196640 | tf_op jit(solution)/shard_map/ppermute | solution.py:47
  20.1 1.5 %collective-permute-start.4 = (bf16[128,768]{1,0:T(8,128)(2,1)S(1)}, bf16[128,768]{1,0:T(8,128)(2,1)S(1)}, u32[]{:S(2)}, u32[]{:S(2)}) collective-permute-start(bf16[128,768]{1,0:T(8,128)(2,1)S(1)} %collective-permute-done.3.refs_9_.refs_5_.refs_6_.refs_4_), channel_id=1, source_target_pairs={{0,2},{1,3},{2,0},{3,1},{4,6},{5,7},{6,4},{7,5},{8,10},{9,11},{10,... | collective-permute-start | bytes 589832 | tf_op jit(solution)/shard_map/ppermute | solution.py:35
  21.8 4.6 %collective-permute-done.refs_7_.refs_3_.refs_4_.refs_2_ = bf16[128,768]{1,0:T(8,128)(2,1)S(1)} collective-permute-done((bf16[128,768]{1,0:T(8,128)(2,1)S(1)}, bf16[128,768]{1,0:T(8,128)(2,1)S(1)}, u32[]{:S(2)}, u32[]{:S(2)}) %collective-permute-start) | collective-permute-done | bytes 196640 | tf_op jit(solution)/shard_map/ppermute | solution.py:47
  26.4 1.5 %collective-permute-start.5 = (bf16[128,768]{1,0:T(8,128)(2,1)S(1)}, bf16[128,768]{1,0:T(8,128)(2,1)S(1)}, u32[]{:S(2)}, u32[]{:S(2)}) collective-permute-start(bf16[128,768]{1,0:T(8,128)(2,1)S(1)} %collective-permute-done.refs_7_.refs_3_.refs_4_.refs_2_), channel_id=1, source_target_pairs={{0,2},{1,3},{2,0},{3,1},{4,6},{5,7},{6,4},{7,5},{8,10},{9,11},{10,... | collective-permute-start | bytes 589832 | tf_op jit(solution)/shard_map/ppermute | solution.py:35
  28.0 0.5 collective-permute-start.11
  28.5 3.7 %collective-permute-done.5.refs_8_.refs_4_.refs_5_.refs_3_ = bf16[128,768]{1,0:T(8,128)(2,1)S(1)} collective-permute-done((bf16[128,768]{1,0:T(8,128)(2,1)S(1)}, bf16[128,768]{1,0:T(8,128)(2,1)S(1)}, u32[]{:S(2)}, u32[]{:S(2)}) %collective-permute-start.5) | collective-permute-done | bytes 196640 | tf_op jit(solution)/shard_map/ppermute | solution.py:35
  32.1 0.5 collective-permute-start.14
  34.6 0.6 collective-permute-start.18
  35.2 0.6 project.4
  35.9 1.5 %collective-permute-start.17 = (bf16[256,512]{1,0:T(8,128)(2,1)S(1)}, bf16[256,512]{1,0:T(8,128)(2,1)S(1)}, u32[]{:S(2)}, u32[]{:S(2)}) collective-permute-start(bf16[256,512]{1,0:T(8,128)(2,1)S(1)} %project.4), channel_id=1, source_target_pairs={{0,1},{1,0},{2,3},{3,2},{4,5},{5,4},{6,7},{7,6},{8,9},{9,8},{10,11... | collective-permute-start | bytes 786440 | tf_op jit(solution)/shard_map/ppermute | solution.py:28
  37.4 1.2 %project.3 = (f32[256,512]{1,0:T(8,128)S(1)}, f32[256,256]{1,0:T(8,128)S(1)}) custom-call(bf16[256,1024]{1,0:T(8,128)(2,1)S(1)} %copy-done, bf16[256,1024]{1,0:T(8,128)(2,1)S(1)} %copy-done.1, bf16[256,512]{1,0:T(8,128)(2,1)S(1)} %copy-done.2, bf16[128,768]{1,0:T(8,128)(2,1)S(1)} %get-tuple-element.82.refs_3_.refs_0_, ...), custom_call_target="tpu_custom_call" | custom-call | tf_op jit(solution)/shard_map/project/pallas_call | solution.py:182
  38.7 2.3 %collective-permute-done.18 = bf16[256,256]{1,0:T(8,128)(2,1)S(1)} collective-permute-done((bf16[256,256]{1,0:T(8,128)(2,1)S(1)}, bf16[256,256]{1,0:T(8,128)(2,1)S(1)}, u32[]{:S(2)}, u32[]{:S(2)}) %collective-permute-start.18) | collective-permute-done | bytes 131104 | tf_op jit(solution)/shard_map/ppermute | solution.py:28
  41.0 3.4 %collective-permute-start.19 = (bf16[256,256]{1,0:T(8,128)(2,1)S(1)}, bf16[256,256]{1,0:T(8,128)(2,1)S(1)}, u32[]{:S(2)}, u32[]{:S(2)}) collective-permute-start(bf16[256,256]{1,0:T(8,128)(2,1)S(1)} %add_convert_fusion.4.refs_2_), channel_id=1, source_target_pairs={{0,2},{1,3},{4,6},{5,7},{8,10},{9,11},{12,14},{13,15},{16,18},{17,... | collective-permute-start | bytes 393224 | tf_op jit(solution)/shard_map/ppermute | solution.py:53
  44.4 2.2 %collective-permute-start.20 = (bf16[256,256]{1,0:T(8,128)(2,1)S(1)}, bf16[256,256]{1,0:T(8,128)(2,1)S(1)}, u32[]{:S(2)}, u32[]{:S(2)}) collective-permute-start(bf16[256,256]{1,0:T(8,128)(2,1)S(1)} %add_convert_fusion.4.refs_2_), channel_id=1, source_target_pairs={{0,1},{1,2},{2,3},{4,5},{5,6},{6,7},{8,9},{9,10},{10,11},{12,13},{... | collective-permute-start | bytes 393224 | tf_op jit(solution)/shard_map/ppermute | solution.py:53
  46.8 2.9 %collective-permute-done.19.refs_0_ = bf16[256,256]{1,0:T(8,128)(2,1)S(1)} collective-permute-done((bf16[256,256]{1,0:T(8,128)(2,1)S(1)}, bf16[256,256]{1,0:T(8,128)(2,1)S(1)}, u32[]{:S(2)}, u32[]{:S(2)}) %collective-permute-start.19) | collective-permute-done | bytes 131104 | tf_op jit(solution)/shard_map/ppermute | solution.py:53
  50.2 4.1 %attend.1 = (bf16[256,512]{1,0:T(8,128)(2,1)}, bf16[256,512]{1,0:T(8,128)(2,1)S(1)}, f32[256,256]{1,0:T(8,128)S(1)}, bf16[512,256]{1,0:T(8,128)(2,1)S(1)}) custom-call(s32[8]{0:T(128)S(1)} %bitcast.25, f32[256,512]{1,0:T(8,128)S(1)} %get-tuple-element.55.q_ref, bf16[256,512]{1,0:T(8,128)(2,1)S(1)} %collective-permute-done.17.q_from_ref, ...), custom_call_target="tpu_custom_call" | custom-call | tf_op jit(solution)/shard_map/attend/pallas_call | solution.py:331
  54.3 1.3 %collective-permute-start.22 = (bf16[256,256]{1,0:T(8,128)(2,1)S(1)}, bf16[256,256]{1,0:T(8,128)(2,1)S(1)}, u32[]{:S(2)}, u32[]{:S(2)}) collective-permute-start(bf16[256,256]{1,0:T(8,128)(2,1)S(1)} %get-tuple-element.84), channel_id=1, source_target_pairs={{2,0},{3,1},{6,4},{7,5},{10,8},{11,9},{14,12},{15,13},{18,16},{19,... | collective-permute-start | bytes 393224 | tf_op jit(solution)/shard_map/ppermute | solution.py:53
  55.6 1.3 %collective-permute-start.21 = (bf16[256,256]{1,0:T(8,128)(2,1)S(1)}, bf16[256,256]{1,0:T(8,128)(2,1)S(1)}, u32[]{:S(2)}, u32[]{:S(2)}) collective-permute-start(bf16[256,256]{1,0:T(8,128)(2,1)S(1)} %get-tuple-element.83), channel_id=1, source_target_pairs={{1,0},{2,1},{3,2},{5,4},{6,5},{7,6},{9,8},{10,9},{11,10},{13,12},{... | collective-permute-start | bytes 393224 | tf_op jit(solution)/shard_map/ppermute | solution.py:53
  56.9 3.2 %collective-permute-start.24 = (bf16[256,512]{1,0:T(8,128)(2,1)S(1)}, bf16[256,512]{1,0:T(8,128)(2,1)S(1)}, u32[]{:S(2)}, u32[]{:S(2)}) collective-permute-start(bf16[256,512]{1,0:T(8,128)(2,1)S(1)} %get-tuple-element.64.dquery_ref.refs_6_), channel_id=1, source_target_pairs={{0,1},{1,0},{2,3},{3,2},{4,5},{5,4},{6,7},{7,6},{8,9},{9,8},{10,11... | collective-permute-start | bytes 786440 | tf_op jit(solution)/shard_map/ppermute | solution.py:28
  60.1 1.1 %collective-permute-done.22 = bf16[256,256]{1,0:T(8,128)(2,1)S(1)} collective-permute-done((bf16[256,256]{1,0:T(8,128)(2,1)S(1)}, bf16[256,256]{1,0:T(8,128)(2,1)S(1)}, u32[]{:S(2)}, u32[]{:S(2)}) %collective-permute-start.22) | collective-permute-done | bytes 131104 | tf_op jit(solution)/shard_map/ppermute | solution.py:53
  61.2 2.0 %collective-permute-done.21 = bf16[256,256]{1,0:T(8,128)(2,1)S(1)} collective-permute-done((bf16[256,256]{1,0:T(8,128)(2,1)S(1)}, bf16[256,256]{1,0:T(8,128)(2,1)S(1)}, u32[]{:S(2)}, u32[]{:S(2)}) %collective-permute-start.21) | collective-permute-done | bytes 131104 | tf_op jit(solution)/shard_map/ppermute | solution.py:53
  63.2 2.8 %collective-permute-start.25 = (bf16[256,256]{1,0:T(8,128)(2,1)S(1)}, bf16[256,256]{1,0:T(8,128)(2,1)S(1)}, u32[]{:S(2)}, u32[]{:S(2)}) collective-permute-start(bf16[256,256]{1,0:T(8,128)(2,1)S(1)} %add_convert_fusion.3.dpair_ref.refs_7_.refs_14_), channel_id=1, source_target_pairs={{0,1},{1,0},{2,3},{3,2},{4,5},{5,4},{6,7},{7,6},{8,9},{9,8},{10,11... | collective-permute-start | bytes 393224 | tf_op jit(solution)/shard_map/ppermute | solution.py:28
  66.0 0.7 collective-permute-done.24.dquery_ref.refs_8_
  66.7 2.2 %collective-permute-done.25.dpair_ref.refs_9_ = bf16[256,256]{1,0:T(8,128)(2,1)S(1)} collective-permute-done((bf16[256,256]{1,0:T(8,128)(2,1)S(1)}, bf16[256,256]{1,0:T(8,128)(2,1)S(1)}, u32[]{:S(2)}, u32[]{:S(2)}) %collective-permute-start.25) | collective-permute-done | bytes 131104 | tf_op jit(solution)/shard_map/ppermute | solution.py:28
  68.9 0.5 collective-permute-start.33
  69.5 0.8 collective-permute-done.31.refs_11_
  70.5 0.6 weight_terms.2
  71.1 2.3 %collective-permute-start.34 = (bf16[128,768]{1,0:T(8,128)(2,1)S(1)}, bf16[128,768]{1,0:T(8,128)(2,1)S(1)}, u32[]{:S(2)}, u32[]{:S(2)}) collective-permute-start(bf16[128,768]{1,0:T(8,128)(2,1)S(1)} %get-tuple-element.69), channel_id=1, source_target_pairs={{0,2},{1,3},{2,0},{3,1},{4,6},{5,7},{6,4},{7,5},{8,10},{9,11},{10,... | collective-permute-start | bytes 589832 | tf_op jit(solution)/shard_map/ppermute | solution.py:35
  73.4 0.8 width_grad.3
  74.2 1.0 collective-permute-start.26
  75.2 1.5 %weight_terms.3 = (f32[128,768]{1,0:T(8,128)S(1)}, bf16[128,768]{1,0:T(8,128)(2,1)S(1)}, f32[128,768]{1,0:T(8,128)S(1)}, bf16[128,768]{1,0:T(8,128)(2,1)S(1)}, f...) custom-call(bf16[256,1024]{1,0:T(8,128)(2,1)S(1)} %copy-done, ...), custom_call_target="tpu_custom_call" | custom-call | tf_op jit(solution)/shard_map/weight_terms/pallas_call | solution.py:248
  76.7 1.0 collective-permute-start.36
  77.6 1.1 %collective-permute-start.38 = (bf16[128,768]{1,0:T(8,128)(2,1)S(1)}, bf16[128,768]{1,0:T(8,128)(2,1)S(1)}, u32[]{:S(2)}, u32[]{:S(2)}) collective-permute-start(bf16[128,768]{1,0:T(8,128)(2,1)S(1)} %get-tuple-element.74), channel_id=1, source_target_pairs={{0,2},{1,3},{2,0},{3,1},{4,6},{5,7},{6,4},{7,5},{8,10},{9,11},{10,... | collective-permute-start | bytes 589832 | tf_op jit(solution)/shard_map/ppermute | solution.py:35
  78.7 0.9 collective-permute-start.40
  79.7 3.1 %collective-permute-start.35 = (bf16[128,768]{1,0:T(8,128)(2,1)S(1)}, bf16[128,768]{1,0:T(8,128)(2,1)S(1)}, u32[]{:S(2)}, u32[]{:S(2)}) collective-permute-start(bf16[128,768]{1,0:T(8,128)(2,1)S(1)} %add_convert_fusion.2), channel_id=1, source_target_pairs={{0,16},{4,20},{8,24},{12,28},{16,0},{20,4},{24,8},{28,12},{1,17},{... | collective-permute-start | bytes 589832 | tf_op jit(solution)/shard_map/ppermute | solution.py:47
  82.8 1.7 %collective-permute-done.36 = bf16[128,768]{1,0:T(8,128)(2,1)S(1)} collective-permute-done((bf16[128,768]{1,0:T(8,128)(2,1)S(1)}, bf16[128,768]{1,0:T(8,128)(2,1)S(1)}, u32[]{:S(2)}, u32[]{:S(2)}) %collective-permute-start.36) | collective-permute-done | bytes 196640 | tf_op jit(solution)/shard_map/ppermute | solution.py:35
  84.6 3.8 %collective-permute-start.37 = (bf16[128,768]{1,0:T(8,128)(2,1)S(1)}, bf16[128,768]{1,0:T(8,128)(2,1)S(1)}, u32[]{:S(2)}, u32[]{:S(2)}) collective-permute-start(bf16[128,768]{1,0:T(8,128)(2,1)S(1)} %add_convert_fusion.1), channel_id=1, source_target_pairs={{0,24},{4,28},{8,0},{12,4},{16,8},{20,12},{24,16},{28,20},{1,25},{... | collective-permute-start | bytes 589832 | tf_op jit(solution)/shard_map/ppermute | solution.py:47
  88.8 3.9 %collective-permute-start.39 = (bf16[128,768]{1,0:T(8,128)(2,1)S(1)}, bf16[128,768]{1,0:T(8,128)(2,1)S(1)}, u32[]{:S(2)}, u32[]{:S(2)}) collective-permute-start(bf16[128,768]{1,0:T(8,128)(2,1)S(1)} %add_convert_fusion), channel_id=1, source_target_pairs={{0,8},{4,12},{8,16},{12,20},{16,24},{20,28},{24,0},{28,4},{1,9},{5... | collective-permute-start | bytes 589832 | tf_op jit(solution)/shard_map/ppermute | solution.py:47
  92.7 1.6 %width_grad.2 = (bf16[256,2048]{1,0:T(8,128)(2,1)S(1)}, bf16[256,512]{1,0:T(8,128)(2,1)S(1)}, bf16[16,128]{1,0:T(8,128)(2,1)}) custom-call(bf16[256,512]{1,0:T(8,128)(2,1)S(1)} %get-tuple-element.64.dquery_ref.refs_6_, bf16[256,256]{1,0:T(8,128)(2,1)S(1)} %add_convert_fusion.3.dpair_ref.refs_7_.refs_14_, ...), custom_call_target="tpu_custom_call" | custom-call | tf_op jit(solution)/shard_map/width_grad/pallas_call | solution.py:209
  94.3 4.0 %collective-permute-done.39.refs_5_ = bf16[128,768]{1,0:T(8,128)(2,1)S(1)} collective-permute-done((bf16[128,768]{1,0:T(8,128)(2,1)S(1)}, bf16[128,768]{1,0:T(8,128)(2,1)S(1)}, u32[]{:S(2)}, u32[]{:S(2)}) %collective-permute-start.39) | collective-permute-done | bytes 196640 | tf_op jit(solution)/shard_map/ppermute | solution.py:47
  98.3 1.7 %finish.1 = (bf16[256,4096]{1,0:T(8,128)(2,1)}, f32[128,768]{1,0:T(8,128)}) custom-call(bf16[256,2048]{1,0:T(8,128)(2,1)S(1)} %get-tuple-element.62.refs_0_, bf16[256,1536]{1,0:T(8,128)(2,1)S(1)} %collective-permute-done.26.refs_1_, bf16[256,512]{1,0:T(8,128)(2,1)S(1)} %get-tuple-element.66.refs_2_, bf16[128,768]{1,0:T(8,128)(2,1)S(1)} %collective-permute-done.35.refs_3_, ...), custom_call_target="tpu_custom_call" | custom-call | tf_op jit(solution)/shard_map/finish/pallas_call | solution.py:145
  (72 shorter events, 3.6 us)
Async XLA Ops:
  0.6 32.2 %copy-start.4 = (bf16[512,768]{1,0:T(8,128)(2,1)S(1)}, bf16[512,768]{1,0:T(8,128)(2,1)}, u32[]{:S(2)}) copy-start(bf16[512,768]{1,0:T(8,128)(2,1)} %param.6) | copy-start | bytes 2359300
  0.6 21.0 %copy-start.3 = (s32[1,8]{1,0:T(1,128)S(1)}, s32[1,8]{1,0:T(1,128)}, u32[]{:S(2)}) copy-start(s32[1,8]{1,0:T(1,128)} %param.8) | copy-start | bytes 100
  0.7 32.1 %copy-start.6 = (s32[1,8]{1,0:T(1,128)S(1)}, s32[1,8]{1,0:T(1,128)}, u32[]{:S(2)}) copy-start(s32[1,8]{1,0:T(1,128)} %param.9) | copy-start | bytes 100
  1.7 10.0 %collective-permute-start.1 = (bf16[128,768]{1,0:T(8,128)(2,1)S(1)}, bf16[128,768]{1,0:T(8,128)(2,1)S(1)}, u32[]{:S(2)}, u32[]{:S(2)}) collective-permute-start(bf16[128,768]{1,0:T(8,128)(2,1)S(1)} %constant_dynamic-slice_fusion), channel_id=1, source_target_pairs={{0,8},{4,12},{8,16},{12,20},{16,24},{20,28},{24,0},{28,4},{1,9},{5... | collective-permute-start | bytes 589832 | tf_op jit(solution)/shard_map/ppermute | solution.py:47
  11.7 20.5 %collective-permute-start.6 = (bf16[256,1536]{1,0:T(8,128)(2,1)}, bf16[256,1536]{1,0:T(8,128)(2,1)S(1)}, u32[]{:S(2)}, u32[]{:S(2)}) collective-permute-start(bf16[256,1536]{1,0:T(8,128)(2,1)} %get-tuple-element.51), channel_id=1, source_target_pairs={{0,1},{1,0},{2,3},{3,2},{4,5},{5,4},{6,7},{7,6},{8,9},{9,8},{10,11... | collective-permute-start | bytes 2359304 | tf_op jit(solution)/shard_map/ppermute | solution.py:28
  13.2 6.9 %collective-permute-start.3 = (bf16[128,768]{1,0:T(8,128)(2,1)S(1)}, bf16[128,768]{1,0:T(8,128)(2,1)S(1)}, u32[]{:S(2)}, u32[]{:S(2)}) collective-permute-start(bf16[128,768]{1,0:T(8,128)(2,1)S(1)} %constant_dynamic-slice_fusion), channel_id=1, source_target_pairs={{0,24},{4,28},{8,0},{12,4},{16,8},{20,12},{24,16},{28,20},{1,25},{... | collective-permute-start | bytes 589832 | tf_op jit(solution)/shard_map/ppermute | solution.py:47
  14.9 11.5 %collective-permute-start = (bf16[128,768]{1,0:T(8,128)(2,1)S(1)}, bf16[128,768]{1,0:T(8,128)(2,1)S(1)}, u32[]{:S(2)}, u32[]{:S(2)}) collective-permute-start(bf16[128,768]{1,0:T(8,128)(2,1)S(1)} %constant_dynamic-slice_fusion), channel_id=1, source_target_pairs={{0,16},{4,20},{8,24},{12,28},{16,0},{20,4},{24,8},{28,12},{1,17},{... | collective-permute-start | bytes 589832 | tf_op jit(solution)/shard_map/ppermute | solution.py:47
  14.9 11.5 %collective-permute-start.2 = (bf16[128,768]{1,0:T(8,128)(2,1)S(1)}, bf16[128,768]{1,0:T(8,128)(2,1)S(1)}, u32[]{:S(2)}, u32[]{:S(2)}) collective-permute-start(bf16[128,768]{1,0:T(8,128)(2,1)S(1)} %collective-permute-done.1.refs_5_.refs_1_.refs_2_.refs_0_), channel_id=1, source_target_pairs={{0,2},{1,3},{2,0},{3,1},{4,6},{5,7},{6,4},{7,5},{8,10},{9,11},{10,... | collective-permute-start | bytes 589832 | tf_op jit(solution)/shard_map/ppermute | solution.py:35
  20.1 6.4 %collective-permute-start.4 = (bf16[128,768]{1,0:T(8,128)(2,1)S(1)}, bf16[128,768]{1,0:T(8,128)(2,1)S(1)}, u32[]{:S(2)}, u32[]{:S(2)}) collective-permute-start(bf16[128,768]{1,0:T(8,128)(2,1)S(1)} %collective-permute-done.3.refs_9_.refs_5_.refs_6_.refs_4_), channel_id=1, source_target_pairs={{0,2},{1,3},{2,0},{3,1},{4,6},{5,7},{6,4},{7,5},{8,10},{9,11},{10,... | collective-permute-start | bytes 589832 | tf_op jit(solution)/shard_map/ppermute | solution.py:35
  26.4 5.7 %collective-permute-start.5 = (bf16[128,768]{1,0:T(8,128)(2,1)S(1)}, bf16[128,768]{1,0:T(8,128)(2,1)S(1)}, u32[]{:S(2)}, u32[]{:S(2)}) collective-permute-start(bf16[128,768]{1,0:T(8,128)(2,1)S(1)} %collective-permute-done.refs_7_.refs_3_.refs_4_.refs_2_), channel_id=1, source_target_pairs={{0,2},{1,3},{2,0},{3,1},{4,6},{5,7},{6,4},{7,5},{8,10},{9,11},{10,... | collective-permute-start | bytes 589832 | tf_op jit(solution)/shard_map/ppermute | solution.py:35
  28.0 4.7 %collective-permute-start.9 = (bf16[128,768]{1,0:T(8,128)(2,1)S(1)}, bf16[128,768]{1,0:T(8,128)(2,1)S(1)}, u32[]{:S(2)}, u32[]{:S(2)}) collective-permute-start(bf16[128,768]{1,0:T(8,128)(2,1)S(1)} %collective-permute-done.1.refs_5_.refs_1_.refs_2_.refs_0_), channel_id=1, source_target_pairs={{0,4},{4,0},{8,12},{12,8},{16,20},{20,16},{24,28},{28,24},{1,5},{5... | collective-permute-start | bytes 589832 | tf_op jit(solution)/shard_map/ppermute | solution.py:40
  28.0 5.4 %collective-permute-start.11 = (bf16[128,768]{1,0:T(8,128)(2,1)S(1)}, bf16[128,768]{1,0:T(8,128)(2,1)S(1)}, u32[]{:S(2)}, u32[]{:S(2)}) collective-permute-start(bf16[128,768]{1,0:T(8,128)(2,1)S(1)} %collective-permute-done.refs_7_.refs_3_.refs_4_.refs_2_), channel_id=1, source_target_pairs={{0,4},{4,0},{8,12},{12,8},{16,20},{20,16},{24,28},{28,24},{1,5},{5... | collective-permute-start | bytes 589832 | tf_op jit(solution)/shard_map/ppermute | solution.py:40
  28.5 4.4 %collective-permute-start.10 = (bf16[128,768]{1,0:T(8,128)(2,1)S(1)}, bf16[128,768]{1,0:T(8,128)(2,1)S(1)}, u32[]{:S(2)}, u32[]{:S(2)}) collective-permute-start(bf16[128,768]{1,0:T(8,128)(2,1)S(1)} %collective-permute-done.2.refs_6_.refs_2_.refs_3_.refs_1_), channel_id=1, source_target_pairs={{0,4},{4,0},{8,12},{12,8},{16,20},{20,16},{24,28},{28,24},{1,5},{5... | collective-permute-start | bytes 589832 | tf_op jit(solution)/shard_map/ppermute | solution.py:40
  32.1 1.4 %collective-permute-start.13 = (bf16[128,768]{1,0:T(8,128)(2,1)S(1)}, bf16[128,768]{1,0:T(8,128)(2,1)S(1)}, u32[]{:S(2)}, u32[]{:S(2)}) collective-permute-start(bf16[128,768]{1,0:T(8,128)(2,1)S(1)} %collective-permute-done.3.refs_9_.refs_5_.refs_6_.refs_4_), channel_id=1, source_target_pairs={{0,4},{4,0},{8,12},{12,8},{16,20},{20,16},{24,28},{28,24},{1,5},{5... | collective-permute-start | bytes 589832 | tf_op jit(solution)/shard_map/ppermute | solution.py:40
  32.1 1.8 %collective-permute-start.14 = (bf16[128,768]{1,0:T(8,128)(2,1)S(1)}, bf16[128,768]{1,0:T(8,128)(2,1)S(1)}, u32[]{:S(2)}, u32[]{:S(2)}) collective-permute-start(bf16[128,768]{1,0:T(8,128)(2,1)S(1)} %collective-permute-done.4.refs_10_.refs_6_.refs_7_.refs_5_), channel_id=1, source_target_pairs={{0,4},{4,0},{8,12},{12,8},{16,20},{20,16},{24,28},{28,24},{1,5},{5... | collective-permute-start | bytes 589832 | tf_op jit(solution)/shard_map/ppermute | solution.py:40
  32.7 1.5 %collective-permute-start.12 = (bf16[128,768]{1,0:T(8,128)(2,1)S(1)}, bf16[128,768]{1,0:T(8,128)(2,1)S(1)}, u32[]{:S(2)}, u32[]{:S(2)}) collective-permute-start(bf16[128,768]{1,0:T(8,128)(2,1)S(1)} %collective-permute-done.5.refs_8_.refs_4_.refs_5_.refs_3_), channel_id=1, source_target_pairs={{0,4},{4,0},{8,12},{12,8},{16,20},{20,16},{24,28},{28,24},{1,5},{5... | collective-permute-start | bytes 589832 | tf_op jit(solution)/shard_map/ppermute | solution.py:40
  32.9 2.9 %collective-permute-start.7 = (bf16[128,768]{1,0:T(8,128)(2,1)S(1)}, bf16[128,768]{1,0:T(8,128)(2,1)S(1)}, u32[]{:S(2)}, u32[]{:S(2)}) collective-permute-start(bf16[128,768]{1,0:T(8,128)(2,1)S(1)} %get-tuple-element.82.refs_3_.refs_0_), channel_id=1, source_target_pairs={{0,4},{4,0},{8,12},{12,8},{16,20},{20,16},{24,28},{28,24},{1,5},{5... | collective-permute-start | bytes 589832 | tf_op jit(solution)/shard_map/ppermute | solution.py:40
  33.4 2.5 %collective-permute-start.8 = (bf16[128,768]{1,0:T(8,128)(2,1)S(1)}, bf16[128,768]{1,0:T(8,128)(2,1)S(1)}, u32[]{:S(2)}, u32[]{:S(2)}) collective-permute-start(bf16[128,768]{1,0:T(8,128)(2,1)S(1)} %get-tuple-element.81.refs_4_.refs_1_), channel_id=1, source_target_pairs={{0,4},{4,0},{8,12},{12,8},{16,20},{20,16},{24,28},{28,24},{1,5},{5... | collective-permute-start | bytes 589832 | tf_op jit(solution)/shard_map/ppermute | solution.py:40
  33.6 3.8 %collective-permute-start.15 = (bf16[128,768]{1,0:T(8,128)(2,1)S(1)}, bf16[128,768]{1,0:T(8,128)(2,1)S(1)}, u32[]{:S(2)}, u32[]{:S(2)}) collective-permute-start(bf16[128,768]{1,0:T(8,128)(2,1)S(1)} %get-tuple-element.80.refs_19_.refs_16_), channel_id=1, source_target_pairs={{0,4},{4,0},{8,12},{12,8},{16,20},{20,16},{24,28},{28,24},{1,5},{5... | collective-permute-start | bytes 589832 | tf_op jit(solution)/shard_map/ppermute | solution.py:40
  33.9 3.5 %collective-permute-start.16 = (bf16[128,768]{1,0:T(8,128)(2,1)S(1)}, bf16[128,768]{1,0:T(8,128)(2,1)S(1)}, u32[]{:S(2)}, u32[]{:S(2)}) collective-permute-start(bf16[128,768]{1,0:T(8,128)(2,1)S(1)} %get-tuple-element.79.refs_20_.refs_17_), channel_id=1, source_target_pairs={{0,4},{4,0},{8,12},{12,8},{16,20},{20,16},{24,28},{28,24},{1,5},{5... | collective-permute-start | bytes 589832 | tf_op jit(solution)/shard_map/ppermute | solution.py:40
  34.5 1.2 %copy-start.1 = (bf16[256,1024]{1,0:T(8,128)(2,1)S(1)}, bf16[256,1024]{1,0:T(8,128)(2,1)}, u32[]{:S(2)}) copy-start(bf16[256,1024]{1,0:T(8,128)(2,1)} %get-tuple-element.42.refs_1_) | copy-start | bytes 1572868
  34.5 2.9 %copy-start = (bf16[256,1024]{1,0:T(8,128)(2,1)S(1)}, bf16[256,1024]{1,0:T(8,128)(2,1)}, u32[]{:S(2)}) copy-start(bf16[256,1024]{1,0:T(8,128)(2,1)} %get-tuple-element.41.refs_0_) | copy-start | bytes 1572868
  34.5 2.9 %copy-start.2 = (bf16[256,512]{1,0:T(8,128)(2,1)S(1)}, bf16[256,512]{1,0:T(8,128)(2,1)}, u32[]{:S(2)}) copy-start(bf16[256,512]{1,0:T(8,128)(2,1)} %get-tuple-element.63.refs_2_) | copy-start | bytes 786436
  34.6 6.4 %collective-permute-start.18 = (bf16[256,256]{1,0:T(8,128)(2,1)S(1)}, bf16[256,256]{1,0:T(8,128)(2,1)S(1)}, u32[]{:S(2)}, u32[]{:S(2)}) collective-permute-start(bf16[256,256]{1,0:T(8,128)(2,1)S(1)} %project.5), channel_id=1, source_target_pairs={{0,1},{1,0},{2,3},{3,2},{4,5},{5,4},{6,7},{7,6},{8,9},{9,8},{10,11... | collective-permute-start | bytes 393224 | tf_op jit(solution)/shard_map/ppermute | solution.py:28
  35.8 30.2 %collective-permute-start.27 = (bf16[256,1024]{1,0:T(8,128)(2,1)S(1)}, bf16[256,1024]{1,0:T(8,128)(2,1)S(1)}, u32[]{:S(2)}, u32[]{:S(2)}) collective-permute-start(bf16[256,1024]{1,0:T(8,128)(2,1)S(1)} %copy-done.1), channel_id=1, source_target_pairs={{0,4},{4,0},{8,12},{12,8},{16,20},{20,16},{24,28},{28,24},{1,5},{5... | collective-permute-start | bytes 1572872 | tf_op jit(solution)/shard_map/ppermute | solution.py:40
  35.9 14.3 %collective-permute-start.17 = (bf16[256,512]{1,0:T(8,128)(2,1)S(1)}, bf16[256,512]{1,0:T(8,128)(2,1)S(1)}, u32[]{:S(2)}, u32[]{:S(2)}) collective-permute-start(bf16[256,512]{1,0:T(8,128)(2,1)S(1)} %project.4), channel_id=1, source_target_pairs={{0,1},{1,0},{2,3},{3,2},{4,5},{5,4},{6,7},{7,6},{8,9},{9,8},{10,11... | collective-permute-start | bytes 786440 | tf_op jit(solution)/shard_map/ppermute | solution.py:28
  37.4 9.2 %copy-start.5 = (bf16[1,256,512]{2,1,0:T(8,128)(2,1)S(1)}, bf16[1,256,512]{2,1,0:T(8,128)(2,1)}, u32[]{:S(2)}) copy-start(bf16[1,256,512]{2,1,0:T(8,128)(2,1)} %param.7) | copy-start | bytes 786436
  41.0 8.7 %collective-permute-start.19 = (bf16[256,256]{1,0:T(8,128)(2,1)S(1)}, bf16[256,256]{1,0:T(8,128)(2,1)S(1)}, u32[]{:S(2)}, u32[]{:S(2)}) collective-permute-start(bf16[256,256]{1,0:T(8,128)(2,1)S(1)} %add_convert_fusion.4.refs_2_), channel_id=1, source_target_pairs={{0,2},{1,3},{4,6},{5,7},{8,10},{9,11},{12,14},{13,15},{16,18},{17,... | collective-permute-start | bytes 393224 | tf_op jit(solution)/shard_map/ppermute | solution.py:53
  44.4 5.8 %collective-permute-start.20 = (bf16[256,256]{1,0:T(8,128)(2,1)S(1)}, bf16[256,256]{1,0:T(8,128)(2,1)S(1)}, u32[]{:S(2)}, u32[]{:S(2)}) collective-permute-start(bf16[256,256]{1,0:T(8,128)(2,1)S(1)} %add_convert_fusion.4.refs_2_), channel_id=1, source_target_pairs={{0,1},{1,2},{2,3},{4,5},{5,6},{6,7},{8,9},{9,10},{10,11},{12,13},{... | collective-permute-start | bytes 393224 | tf_op jit(solution)/shard_map/ppermute | solution.py:53
  46.7 23.6 %collective-permute-start.28 = (bf16[256,1536]{1,0:T(8,128)(2,1)S(1)}, bf16[256,1536]{1,0:T(8,128)(2,1)S(1)}, u32[]{:S(2)}, u32[]{:S(2)}) collective-permute-start(bf16[256,1536]{1,0:T(8,128)(2,1)S(1)} %collective-permute-done.6.refs_0_.refs_1_), channel_id=1, source_target_pairs={{0,4},{4,0},{8,12},{12,8},{16,20},{20,16},{24,28},{28,24},{1,5},{5... | collective-permute-start | bytes 2359304 | tf_op jit(solution)/shard_map/ppermute | solution.py:40
  49.7 7.2 %collective-permute-start.23 = (bf16[256,512]{1,0:T(8,128)(2,1)S(1)}, bf16[256,512]{1,0:T(8,128)(2,1)S(1)}, u32[]{:S(2)}, u32[]{:S(2)}) collective-permute-start(bf16[256,512]{1,0:T(8,128)(2,1)S(1)} %copy-done.2), channel_id=1, source_target_pairs={{0,1},{1,0},{2,3},{3,2},{4,5},{5,4},{6,7},{7,6},{8,9},{9,8},{10,11... | collective-permute-start | bytes 786440 | tf_op jit(solution)/shard_map/ppermute | solution.py:28
  54.3 6.9 %collective-permute-start.22 = (bf16[256,256]{1,0:T(8,128)(2,1)S(1)}, bf16[256,256]{1,0:T(8,128)(2,1)S(1)}, u32[]{:S(2)}, u32[]{:S(2)}) collective-permute-start(bf16[256,256]{1,0:T(8,128)(2,1)S(1)} %get-tuple-element.84), channel_id=1, source_target_pairs={{2,0},{3,1},{6,4},{7,5},{10,8},{11,9},{14,12},{15,13},{18,16},{19,... | collective-permute-start | bytes 393224 | tf_op jit(solution)/shard_map/ppermute | solution.py:53
  55.6 7.5 %collective-permute-start.21 = (bf16[256,256]{1,0:T(8,128)(2,1)S(1)}, bf16[256,256]{1,0:T(8,128)(2,1)S(1)}, u32[]{:S(2)}, u32[]{:S(2)}) collective-permute-start(bf16[256,256]{1,0:T(8,128)(2,1)S(1)} %get-tuple-element.83), channel_id=1, source_target_pairs={{1,0},{2,1},{3,2},{5,4},{6,5},{7,6},{9,8},{10,9},{11,10},{13,12},{... | collective-permute-start | bytes 393224 | tf_op jit(solution)/shard_map/ppermute | solution.py:53
  56.9 9.8 %collective-permute-start.24 = (bf16[256,512]{1,0:T(8,128)(2,1)S(1)}, bf16[256,512]{1,0:T(8,128)(2,1)S(1)}, u32[]{:S(2)}, u32[]{:S(2)}) collective-permute-start(bf16[256,512]{1,0:T(8,128)(2,1)S(1)} %get-tuple-element.64.dquery_ref.refs_6_), channel_id=1, source_target_pairs={{0,1},{1,0},{2,3},{3,2},{4,5},{5,4},{6,7},{7,6},{8,9},{9,8},{10,11... | collective-permute-start | bytes 786440 | tf_op jit(solution)/shard_map/ppermute | solution.py:28
  61.2 7.8 %collective-permute-start.30 = (bf16[256,512]{1,0:T(8,128)(2,1)S(1)}, bf16[256,512]{1,0:T(8,128)(2,1)S(1)}, u32[]{:S(2)}, u32[]{:S(2)}) collective-permute-start(bf16[256,512]{1,0:T(8,128)(2,1)S(1)} %get-tuple-element.64.dquery_ref.refs_6_), channel_id=1, source_target_pairs={{0,4},{4,0},{8,12},{12,8},{16,20},{20,16},{24,28},{28,24},{1,5},{5... | collective-permute-start | bytes 786440 | tf_op jit(solution)/shard_map/ppermute | solution.py:40
  63.2 5.7 %collective-permute-start.25 = (bf16[256,256]{1,0:T(8,128)(2,1)S(1)}, bf16[256,256]{1,0:T(8,128)(2,1)S(1)}, u32[]{:S(2)}, u32[]{:S(2)}) collective-permute-start(bf16[256,256]{1,0:T(8,128)(2,1)S(1)} %add_convert_fusion.3.dpair_ref.refs_7_.refs_14_), channel_id=1, source_target_pairs={{0,1},{1,0},{2,3},{3,2},{4,5},{5,4},{6,7},{7,6},{8,9},{9,8},{10,11... | collective-permute-start | bytes 393224 | tf_op jit(solution)/shard_map/ppermute | solution.py:28
  66.0 4.3 %collective-permute-start.29 = (bf16[256,512]{1,0:T(8,128)(2,1)S(1)}, bf16[256,512]{1,0:T(8,128)(2,1)S(1)}, u32[]{:S(2)}, u32[]{:S(2)}) collective-permute-start(bf16[256,512]{1,0:T(8,128)(2,1)S(1)} %collective-permute-done.23.refs_2_), channel_id=1, source_target_pairs={{0,4},{4,0},{8,12},{12,8},{16,20},{20,16},{24,28},{28,24},{1,5},{5... | collective-permute-start | bytes 786440 | tf_op jit(solution)/shard_map/ppermute | solution.py:40
  66.7 3.8 %collective-permute-start.32 = (bf16[256,512]{1,0:T(8,128)(2,1)S(1)}, bf16[256,512]{1,0:T(8,128)(2,1)S(1)}, u32[]{:S(2)}, u32[]{:S(2)}) collective-permute-start(bf16[256,512]{1,0:T(8,128)(2,1)S(1)} %collective-permute-done.24.dquery_ref.refs_8_), channel_id=1, source_target_pairs={{0,4},{4,0},{8,12},{12,8},{16,20},{20,16},{24,28},{28,24},{1,5},{5... | collective-permute-start | bytes 786440 | tf_op jit(solution)/shard_map/ppermute | solution.py:40
  68.9 1.3 %collective-permute-start.31 = (bf16[256,256]{1,0:T(8,128)(2,1)S(1)}, bf16[256,256]{1,0:T(8,128)(2,1)S(1)}, u32[]{:S(2)}, u32[]{:S(2)}) collective-permute-start(bf16[256,256]{1,0:T(8,128)(2,1)S(1)} %add_convert_fusion.3.dpair_ref.refs_7_.refs_14_), channel_id=1, source_target_pairs={{0,4},{4,0},{8,12},{12,8},{16,20},{20,16},{24,28},{28,24},{1,5},{5... | collective-permute-start | bytes 393224 | tf_op jit(solution)/shard_map/ppermute | solution.py:40
  68.9 1.5 %collective-permute-start.33 = (bf16[256,256]{1,0:T(8,128)(2,1)S(1)}, bf16[256,256]{1,0:T(8,128)(2,1)S(1)}, u32[]{:S(2)}, u32[]{:S(2)}) collective-permute-start(bf16[256,256]{1,0:T(8,128)(2,1)S(1)} %collective-permute-done.25.dpair_ref.refs_9_), channel_id=1, source_target_pairs={{0,4},{4,0},{8,12},{12,8},{16,20},{20,16},{24,28},{28,24},{1,5},{5... | collective-permute-start | bytes 393224 | tf_op jit(solution)/shard_map/ppermute | solution.py:40
  71.1 8.5 %collective-permute-start.34 = (bf16[128,768]{1,0:T(8,128)(2,1)S(1)}, bf16[128,768]{1,0:T(8,128)(2,1)S(1)}, u32[]{:S(2)}, u32[]{:S(2)}) collective-permute-start(bf16[128,768]{1,0:T(8,128)(2,1)S(1)} %get-tuple-element.69), channel_id=1, source_target_pairs={{0,2},{1,3},{2,0},{3,1},{4,6},{5,7},{6,4},{7,5},{8,10},{9,11},{10,... | collective-permute-start | bytes 589832 | tf_op jit(solution)/shard_map/ppermute | solution.py:35
  74.2 24.1 %collective-permute-start.26 = (bf16[256,1536]{1,0:T(8,128)(2,1)S(1)}, bf16[256,1536]{1,0:T(8,128)(2,1)S(1)}, u32[]{:S(2)}, u32[]{:S(2)}) collective-permute-start(bf16[256,1536]{1,0:T(8,128)(2,1)S(1)} %get-tuple-element.65), channel_id=1, source_target_pairs={{0,1},{1,0},{2,3},{3,2},{4,5},{5,4},{6,7},{7,6},{8,9},{9,8},{10,11... | collective-permute-start | bytes 2359304 | tf_op jit(solution)/shard_map/ppermute | solution.py:28
  76.7 7.9 %collective-permute-start.36 = (bf16[128,768]{1,0:T(8,128)(2,1)S(1)}, bf16[128,768]{1,0:T(8,128)(2,1)S(1)}, u32[]{:S(2)}, u32[]{:S(2)}) collective-permute-start(bf16[128,768]{1,0:T(8,128)(2,1)S(1)} %get-tuple-element.72), channel_id=1, source_target_pairs={{0,2},{1,3},{2,0},{3,1},{4,6},{5,7},{6,4},{7,5},{8,10},{9,11},{10,... | collective-permute-start | bytes 589832 | tf_op jit(solution)/shard_map/ppermute | solution.py:35
  77.6 11.1 %collective-permute-start.38 = (bf16[128,768]{1,0:T(8,128)(2,1)S(1)}, bf16[128,768]{1,0:T(8,128)(2,1)S(1)}, u32[]{:S(2)}, u32[]{:S(2)}) collective-permute-start(bf16[128,768]{1,0:T(8,128)(2,1)S(1)} %get-tuple-element.74), channel_id=1, source_target_pairs={{0,2},{1,3},{2,0},{3,1},{4,6},{5,7},{6,4},{7,5},{8,10},{9,11},{10,... | collective-permute-start | bytes 589832 | tf_op jit(solution)/shard_map/ppermute | solution.py:35
  78.7 15.6 %collective-permute-start.40 = (bf16[128,768]{1,0:T(8,128)(2,1)S(1)}, bf16[128,768]{1,0:T(8,128)(2,1)S(1)}, u32[]{:S(2)}, u32[]{:S(2)}) collective-permute-start(bf16[128,768]{1,0:T(8,128)(2,1)S(1)} %get-tuple-element.76), channel_id=1, source_target_pairs={{0,2},{1,3},{2,0},{3,1},{4,6},{5,7},{6,4},{7,5},{8,10},{9,11},{10,... | collective-permute-start | bytes 589832 | tf_op jit(solution)/shard_map/ppermute | solution.py:35
  79.7 14.6 %collective-permute-start.35 = (bf16[128,768]{1,0:T(8,128)(2,1)S(1)}, bf16[128,768]{1,0:T(8,128)(2,1)S(1)}, u32[]{:S(2)}, u32[]{:S(2)}) collective-permute-start(bf16[128,768]{1,0:T(8,128)(2,1)S(1)} %add_convert_fusion.2), channel_id=1, source_target_pairs={{0,16},{4,20},{8,24},{12,28},{16,0},{20,4},{24,8},{28,12},{1,17},{... | collective-permute-start | bytes 589832 | tf_op jit(solution)/shard_map/ppermute | solution.py:47
  84.6 9.7 %collective-permute-start.37 = (bf16[128,768]{1,0:T(8,128)(2,1)S(1)}, bf16[128,768]{1,0:T(8,128)(2,1)S(1)}, u32[]{:S(2)}, u32[]{:S(2)}) collective-permute-start(bf16[128,768]{1,0:T(8,128)(2,1)S(1)} %add_convert_fusion.1), channel_id=1, source_target_pairs={{0,24},{4,28},{8,0},{12,4},{16,8},{20,12},{24,16},{28,20},{1,25},{... | collective-permute-start | bytes 589832 | tf_op jit(solution)/shard_map/ppermute | solution.py:47
  88.8 9.5 %collective-permute-start.39 = (bf16[128,768]{1,0:T(8,128)(2,1)S(1)}, bf16[128,768]{1,0:T(8,128)(2,1)S(1)}, u32[]{:S(2)}, u32[]{:S(2)}) collective-permute-start(bf16[128,768]{1,0:T(8,128)(2,1)S(1)} %add_convert_fusion), channel_id=1, source_target_pairs={{0,8},{4,12},{8,16},{12,20},{16,24},{20,28},{24,0},{28,4},{1,9},{5... | collective-permute-start | bytes 589832 | tf_op jit(solution)/shard_map/ppermute | solution.py:47

commit v12 on v11

--- a/solution.py
+++ b/solution.py
@@ -217,7 +217,7 @@
     )(dquery, dpair, *pieces)
 
 
-def weight_kernel(steps, rest, width, chips, sources, grads, *refs):
+def weight_kernel(steps, whole, rest, width, chips, sources, grads, *refs):
     tokens, refs = refs[: sum(sources)], refs[sum(sources) :]
     rights = [jnp.concatenate([r[...] for r in refs[i : i + grads]], axis=1) for i in range(0, grads * len(sources), grads)]
     right = jnp.concatenate(rights, axis=0)
@@ -235,21 +235,29 @@
                 first = across if k == 0 else across * (chips - 1) + k - 1
                 left.append((far if k else near)[:, first * span : (first + 1) * span])
         total = dot(jnp.concatenate(left, axis=0).T, right)
-        for j in range(rest):
-            out = outs[i * rest + j]
-            out[...] = total[j * width : (j + 1) * width].astype(out.dtype)
-
-
-def weight_terms(steps, rest, width, chips, tokens, grads, after):
+        here = 1 if k == whole else rest
+        rows = total.shape[0] // here
+        for j in range(here):
+            outs[j][...] = total[j * rows : (j + 1) * rows].astype(outs[j].dtype)
+        outs = outs[here:]
+
+
+def weight_terms(steps, whole, rest, width, chips, tokens, grads, after):
     cols = sum(g.shape[1] for g in grads[0])
     sources = [len(parts) for parts in tokens]
     parts = [part for group in tokens for part in group]
     given = [g for group in grads for g in group]
-    return pl.pallas_call(
-        functools.partial(weight_kernel, steps, rest, width, chips, sources, len(grads[0])),
+    shapes = []
+    for k in steps:
+        if k == whole:
+            shapes.append(jax.ShapeDtypeStruct((rest * width, cols), BF16))
+        else:
+            shapes += [jax.ShapeDtypeStruct((width, cols), BF16 if j else F32) for j in range(rest)]
+    return pl.pallas_call(
+        functools.partial(weight_kernel, steps, whole, rest, width, chips, sources, len(grads[0])),
         in_specs=[VMEM] * (len(parts) + len(given) + 1),
-        out_specs=[VMEM] * (len(steps) * rest),
-        out_shape=[jax.ShapeDtypeStruct((width, cols), BF16 if j else F32) for _ in steps for j in range(rest)],
+        out_specs=[VMEM] * len(shapes),
+        out_shape=shapes,
         compiler_params=pltpu.CompilerParams(vmem_limit_bytes=20 * 2**20),
         name="weight_terms",
     )(*parts, *given, after)
@@ -315,9 +323,9 @@
         if h + 1 < heads:
             products(h + 1)
         outputs(h)
+        score_grads(h)
         if h:
             grads(h - 1)
-        score_grads(h)
     grads(heads - 1)
     both = jnp.concatenate([sums[0] * scale, sums[1]], axis=1)
     dpair_ref[...] = both[back * rows :]
@@ -399,7 +407,7 @@
     kept = kept_rows(doc_row, flag_row, positions)
     cot = jnp.where(kept[:, None] > 0, cotangent[0], jnp.zeros_like(cotangent[0]))
 
-    near, _ = lax.optimization_barrier((near, pair))
+    near, _ = lax.optimization_barrier((near, pair_from))
     near_other = swap_x(near)
     pairs = [shift_seq(pair, j) for j in range(back, 0, -1)] + [pair]
     attention, dquery, dpair, dback = attend(doc_row, query, query_from, cot, pairs)
@@ -417,20 +425,28 @@
     right = [[dquery, dpair], [dquery_other, dpair_other]]
     right += [[swap_core(g) for g in group] for group in right]
     order = sorted(range(chips), key=lambda k: (k == 0, -min(k, chips - k), k))
-    parts, after = [], dpair
-    for steps in (order[:1], order[1:]):
-        terms = weight_terms(steps, rest, width, chips, left, right, after)
-        if not parts:
+    whole = chips - 1
+    steps_left = [k for k in order if k != whole]
+    parts, after, joined = [], dpair, None
+    for steps in ([whole, steps_left[0]], steps_left[1:]):
+        terms = weight_terms(steps, whole, rest, width, chips, left, right, after)
+        if joined is None:
+            joined, terms = shift_chip(terms[0], -whole), terms[1:]
+            steps = steps[1:]
             grad_sent, after = width_grad(dquery_other, dpair_other, [groups_far])
             grad_from = swap_x(grad_sent)
         for i, k in enumerate(steps):
             part, *sent = terms[i * rest : (i + 1) * rest]
+            if k == 0:
+                extra = [joined[j * width : (j + 1) * width].astype(F32) for j in range(rest)]
+                part = part + extra[0]
+                sent = [(piece.astype(F32) + more).astype(BF16) for piece, more in zip(sent, extra[1:])]
             received = [shift_rest(piece, -j) for j, piece in enumerate(sent, 1)]
             if k:
                 part = functools.reduce(jnp.add, [term.astype(F32) for term in received], part)
                 parts.append(shift_chip(part.astype(BF16), -k))
             else:
-                parts += [part, *received]
+                parts = [*received, part, *parts]
 
     grad_mine, grad_near, _ = width_grad(dquery, dpair, [groups, groups_near])
     inputs_grad, weights_grad = finish([grad_mine, grad_from, grad_near], parts, chips, rest, width)

time: 100 us -> 101 us (1.010); the launches traced: 100 us -> 98.8 us
  starting transfers between devices: 47.1 us -> 40.3 us
  waiting for transfers between devices: 35 us -> 40.6 us
    ppermute x6, starting transfers between devices: 15.6 us -> 9.87 us  [shift_chip(): return lax.ppermute(array, 'dp', pairs)]
    ppermute x6, waiting for transfers between devices: 16.4 us -> 19.5 us  [shift_chip(): return lax.ppermute(array, 'dp', pairs)]
    ppermute x7 -> x6, waiting for transfers between devices: 5.74 us -> 8.21 us  [shift_rest(): return lax.ppermute(array, 'seq', pairs)]
    ppermute x7 -> x6, starting transfers between devices: 9.84 us -> 8.81 us  [shift_rest(): return lax.ppermute(array, 'seq', pairs)]
  transfers between devices with their start and end apart: 41 -> 40, of which waited for: 17 -> 18; matrix products, arithmetic and copies ran while one was open for 1% -> 1% of each run, Pallas kernels for 13% -> 13%
where the time goes in v12:
time: 101 us; the launch traced here: 98.8 us
  waiting for transfers between devices  40.6 us (40%)
  starting transfers between devices  40.3 us (40%)
  Pallas kernels  15.2 us (15%)
  local copies, waits for them, and re-layouts  1.12 us (1%)
    ppermute x6, waiting for transfers between devices, shift_chip(): return lax.ppermute(array, 'dp', pairs)  19.5 us
    ppermute x7, starting transfers between devices, swap_x(): return lax.ppermute(array, 'seq', [(i, i ^ 1) for i in range(count)])  10.6 us
    ppermute x6, starting transfers between devices, shift_chip(): return lax.ppermute(array, 'dp', pairs)  9.87 us
    ppermute x6, starting transfers between devices, shift_rest(): return lax.ppermute(array, 'seq', pairs)  8.81 us
    ppermute x6, waiting for transfers between devices, shift_rest(): return lax.ppermute(array, 'seq', pairs)  8.21 us
    ppermute x4, starting transfers between devices, shift_seq(): return lax.ppermute(array, 'seq', pairs)  8.18 us
    ppermute x4, waiting for transfers between devices, shift_seq(): return lax.ppermute(array, 'seq', pairs)  6.43 us
    ppermute x7, waiting for transfers between devices, swap_x(): return lax.ppermute(array, 'seq', [(i, i ^ 1) for i in range(count)])  5.25 us
  transfers between devices with their start and end apart: 40, of which 18 were waited for; matrix products, arithmetic and copies ran while one was open for 1% of the time, Pallas kernels for 13%

profile of v12, /device:TPU:0, one launch (start us, length us, event | category | flops | bytes accessed | tf_op | source)
XLA Modules:
  0.0 98.8 jit_solution(3693450607728083747)
XLA Ops:
  0.7 1.0 %constant_dynamic-slice_fusion = bf16[128,768]{1,0:T(8,128)(2,1)S(1)} fusion(bf16[512,768]{1,0:T(8,128)(2,1)} %param.6, s32[]{:T(128)S(6)} %select_n.64), kind=kLoop, calls=%fused_computation.12 | loop fusion | bytes 393220 | tf_op jit(solution)/shard_map/dynamic_slice | solution.py:373
  1.7 3.1 %collective-permute-start.1 = (bf16[128,768]{1,0:T(8,128)(2,1)S(1)}, bf16[128,768]{1,0:T(8,128)(2,1)S(1)}, u32[]{:S(2)}, u32[]{:S(2)}) collective-permute-start(bf16[128,768]{1,0:T(8,128)(2,1)S(1)} %constant_dynamic-slice_fusion), channel_id=1, source_target_pairs={{0,8},{4,12},{8,16},{12,20},{16,24},{20,28},{24,0},{28,4},{1,9},{5... | collective-permute-start | bytes 589832 | tf_op jit(solution)/shard_map/ppermute | solution.py:47
  4.8 2.8 %split_tokens.1 = (bf16[256,1024]{1,0:T(8,128)(2,1)}, bf16[256,1024]{1,0:T(8,128)(2,1)}, bf16[256,1536]{1,0:T(8,128)(2,1)}, bf16[256,512]{1,0:T(8,128)(2,1)}) custom-call(bf16[256,4096]{1,0:T(8,128)(2,1)} %bitcast.26), custom_call_target="tpu_custom_call" | custom-call | tf_op jit(solution)/shard_map/split_tokens/pallas_call | solution.py:105
  7.6 4.1 %collective-permute-done.1.refs_5_.refs_1_.refs_2_.refs_0_ = bf16[128,768]{1,0:T(8,128)(2,1)S(1)} collective-permute-done((bf16[128,768]{1,0:T(8,128)(2,1)S(1)}, bf16[128,768]{1,0:T(8,128)(2,1)S(1)}, u32[]{:S(2)}, u32[]{:S(2)}) %collective-permute-start.1) | collective-permute-done | bytes 196640 | tf_op jit(solution)/shard_map/ppermute | solution.py:47
  11.7 1.5 %collective-permute-start.6 = (bf16[256,1536]{1,0:T(8,128)(2,1)}, bf16[256,1536]{1,0:T(8,128)(2,1)S(1)}, u32[]{:S(2)}, u32[]{:S(2)}) collective-permute-start(bf16[256,1536]{1,0:T(8,128)(2,1)} %get-tuple-element.50), channel_id=1, source_target_pairs={{0,1},{1,0},{2,3},{3,2},{4,5},{5,4},{6,7},{7,6},{8,9},{9,8},{10,11... | collective-permute-start | bytes 2359304 | tf_op jit(solution)/shard_map/ppermute | solution.py:28
  13.2 1.7 %collective-permute-start.3 = (bf16[128,768]{1,0:T(8,128)(2,1)S(1)}, bf16[128,768]{1,0:T(8,128)(2,1)S(1)}, u32[]{:S(2)}, u32[]{:S(2)}) collective-permute-start(bf16[128,768]{1,0:T(8,128)(2,1)S(1)} %constant_dynamic-slice_fusion), channel_id=1, source_target_pairs={{0,24},{4,28},{8,0},{12,4},{16,8},{20,12},{24,16},{28,20},{1,25},{... | collective-permute-start | bytes 589832 | tf_op jit(solution)/shard_map/ppermute | solution.py:47
  14.9 1.5 %collective-permute-start.2 = (bf16[128,768]{1,0:T(8,128)(2,1)S(1)}, bf16[128,768]{1,0:T(8,128)(2,1)S(1)}, u32[]{:S(2)}, u32[]{:S(2)}) collective-permute-start(bf16[128,768]{1,0:T(8,128)(2,1)S(1)} %collective-permute-done.1.refs_5_.refs_1_.refs_2_.refs_0_), channel_id=1, source_target_pairs={{0,2},{1,3},{2,0},{3,1},{4,6},{5,7},{6,4},{7,5},{8,10},{9,11},{10,... | collective-permute-start | bytes 589832 | tf_op jit(solution)/shard_map/ppermute | solution.py:35
  16.4 3.6 %collective-permute-done.3.refs_9_.refs_5_.refs_6_.refs_4_ = bf16[128,768]{1,0:T(8,128)(2,1)S(1)} collective-permute-done((bf16[128,768]{1,0:T(8,128)(2,1)S(1)}, bf16[128,768]{1,0:T(8,128)(2,1)S(1)}, u32[]{:S(2)}, u32[]{:S(2)}) %collective-permute-start.3) | collective-permute-done | bytes 196640 | tf_op jit(solution)/shard_map/ppermute | solution.py:47
  20.1 1.5 %collective-permute-start.4 = (bf16[128,768]{1,0:T(8,128)(2,1)S(1)}, bf16[128,768]{1,0:T(8,128)(2,1)S(1)}, u32[]{:S(2)}, u32[]{:S(2)}) collective-permute-start(bf16[128,768]{1,0:T(8,128)(2,1)S(1)} %collective-permute-done.3.refs_9_.refs_5_.refs_6_.refs_4_), channel_id=1, source_target_pairs={{0,2},{1,3},{2,0},{3,1},{4,6},{5,7},{6,4},{7,5},{8,10},{9,11},{10,... | collective-permute-start | bytes 589832 | tf_op jit(solution)/shard_map/ppermute | solution.py:35
  21.8 4.6 %collective-permute-done.refs_7_.refs_3_.refs_4_.refs_2_ = bf16[128,768]{1,0:T(8,128)(2,1)S(1)} collective-permute-done((bf16[128,768]{1,0:T(8,128)(2,1)S(1)}, bf16[128,768]{1,0:T(8,128)(2,1)S(1)}, u32[]{:S(2)}, u32[]{:S(2)}) %collective-permute-start) | collective-permute-done | bytes 196640 | tf_op jit(solution)/shard_map/ppermute | solution.py:47
  26.4 1.5 %collective-permute-start.5 = (bf16[128,768]{1,0:T(8,128)(2,1)S(1)}, bf16[128,768]{1,0:T(8,128)(2,1)S(1)}, u32[]{:S(2)}, u32[]{:S(2)}) collective-permute-start(bf16[128,768]{1,0:T(8,128)(2,1)S(1)} %collective-permute-done.refs_7_.refs_3_.refs_4_.refs_2_), channel_id=1, source_target_pairs={{0,2},{1,3},{2,0},{3,1},{4,6},{5,7},{6,4},{7,5},{8,10},{9,11},{10,... | collective-permute-start | bytes 589832 | tf_op jit(solution)/shard_map/ppermute | solution.py:35
  28.0 0.5 collective-permute-start.11
  28.5 3.7 %collective-permute-done.5.refs_8_.refs_4_.refs_5_.refs_3_ = bf16[128,768]{1,0:T(8,128)(2,1)S(1)} collective-permute-done((bf16[128,768]{1,0:T(8,128)(2,1)S(1)}, bf16[128,768]{1,0:T(8,128)(2,1)S(1)}, u32[]{:S(2)}, u32[]{:S(2)}) %collective-permute-start.5) | collective-permute-done | bytes 196640 | tf_op jit(solution)/shard_map/ppermute | solution.py:35
  32.1 0.5 collective-permute-start.14
  32.9 0.5 collective-permute-start.7
  34.6 0.6 collective-permute-start.18
  35.2 0.6 project.4
  35.9 1.5 %collective-permute-start.17 = (bf16[256,512]{1,0:T(8,128)(2,1)S(1)}, bf16[256,512]{1,0:T(8,128)(2,1)S(1)}, u32[]{:S(2)}, u32[]{:S(2)}) collective-permute-start(bf16[256,512]{1,0:T(8,128)(2,1)S(1)} %project.4), channel_id=1, source_target_pairs={{0,1},{1,0},{2,3},{3,2},{4,5},{5,4},{6,7},{7,6},{8,9},{9,8},{10,11... | collective-permute-start | bytes 786440 | tf_op jit(solution)/shard_map/ppermute | solution.py:28
  37.4 1.2 %project.3 = (f32[256,512]{1,0:T(8,128)S(1)}, f32[256,256]{1,0:T(8,128)S(1)}) custom-call(bf16[256,1024]{1,0:T(8,128)(2,1)S(1)} %copy-done, bf16[256,1024]{1,0:T(8,128)(2,1)S(1)} %copy-done.1, bf16[256,512]{1,0:T(8,128)(2,1)S(1)} %copy-done.2, bf16[128,768]{1,0:T(8,128)(2,1)S(1)} %get-tuple-element.80.refs_3_.refs_0_, ...), custom_call_target="tpu_custom_call" | custom-call | tf_op jit(solution)/shard_map/project/pallas_call | solution.py:182
  38.6 2.3 %collective-permute-done.18 = bf16[256,256]{1,0:T(8,128)(2,1)S(1)} collective-permute-done((bf16[256,256]{1,0:T(8,128)(2,1)S(1)}, bf16[256,256]{1,0:T(8,128)(2,1)S(1)}, u32[]{:S(2)}, u32[]{:S(2)}) %collective-permute-start.18) | collective-permute-done | bytes 131104 | tf_op jit(solution)/shard_map/ppermute | solution.py:28
  41.0 3.4 %collective-permute-start.19 = (bf16[256,256]{1,0:T(8,128)(2,1)S(1)}, bf16[256,256]{1,0:T(8,128)(2,1)S(1)}, u32[]{:S(2)}, u32[]{:S(2)}) collective-permute-start(bf16[256,256]{1,0:T(8,128)(2,1)S(1)} %add_convert_fusion.4.refs_2_), channel_id=1, source_target_pairs={{0,2},{1,3},{4,6},{5,7},{8,10},{9,11},{12,14},{13,15},{16,18},{17,... | collective-permute-start | bytes 393224 | tf_op jit(solution)/shard_map/ppermute | solution.py:53
  44.4 2.2 %collective-permute-start.20 = (bf16[256,256]{1,0:T(8,128)(2,1)S(1)}, bf16[256,256]{1,0:T(8,128)(2,1)S(1)}, u32[]{:S(2)}, u32[]{:S(2)}) collective-permute-start(bf16[256,256]{1,0:T(8,128)(2,1)S(1)} %add_convert_fusion.4.refs_2_), channel_id=1, source_target_pairs={{0,1},{1,2},{2,3},{4,5},{5,6},{6,7},{8,9},{9,10},{10,11},{12,13},{... | collective-permute-start | bytes 393224 | tf_op jit(solution)/shard_map/ppermute | solution.py:53
  46.8 2.9 %collective-permute-done.19.refs_0_ = bf16[256,256]{1,0:T(8,128)(2,1)S(1)} collective-permute-done((bf16[256,256]{1,0:T(8,128)(2,1)S(1)}, bf16[256,256]{1,0:T(8,128)(2,1)S(1)}, u32[]{:S(2)}, u32[]{:S(2)}) %collective-permute-start.19) | collective-permute-done | bytes 131104 | tf_op jit(solution)/shard_map/ppermute | solution.py:53
  50.2 4.1 %attend.1 = (bf16[256,512]{1,0:T(8,128)(2,1)}, bf16[256,512]{1,0:T(8,128)(2,1)S(1)}, f32[256,256]{1,0:T(8,128)S(1)}, bf16[512,256]{1,0:T(8,128)(2,1)S(1)}) custom-call(s32[8]{0:T(128)S(1)} %bitcast.25, f32[256,512]{1,0:T(8,128)S(1)} %get-tuple-element.54.q_ref, bf16[256,512]{1,0:T(8,128)(2,1)S(1)} %collective-permute-done.17.q_from_ref, ...), custom_call_target="tpu_custom_call" | custom-call | tf_op jit(solution)/shard_map/attend/pallas_call | solution.py:339
  54.3 1.3 %collective-permute-start.22 = (bf16[256,256]{1,0:T(8,128)(2,1)S(1)}, bf16[256,256]{1,0:T(8,128)(2,1)S(1)}, u32[]{:S(2)}, u32[]{:S(2)}) collective-permute-start(bf16[256,256]{1,0:T(8,128)(2,1)S(1)} %get-tuple-element.84), channel_id=1, source_target_pairs={{2,0},{3,1},{6,4},{7,5},{10,8},{11,9},{14,12},{15,13},{18,16},{19,... | collective-permute-start | bytes 393224 | tf_op jit(solution)/shard_map/ppermute | solution.py:53
  55.6 1.3 %collective-permute-start.21 = (bf16[256,256]{1,0:T(8,128)(2,1)S(1)}, bf16[256,256]{1,0:T(8,128)(2,1)S(1)}, u32[]{:S(2)}, u32[]{:S(2)}) collective-permute-start(bf16[256,256]{1,0:T(8,128)(2,1)S(1)} %get-tuple-element.83), channel_id=1, source_target_pairs={{1,0},{2,1},{3,2},{5,4},{6,5},{7,6},{9,8},{10,9},{11,10},{13,12},{... | collective-permute-start | bytes 393224 | tf_op jit(solution)/shard_map/ppermute | solution.py:53
  56.9 3.2 %collective-permute-start.24 = (bf16[256,512]{1,0:T(8,128)(2,1)S(1)}, bf16[256,512]{1,0:T(8,128)(2,1)S(1)}, u32[]{:S(2)}, u32[]{:S(2)}) collective-permute-start(bf16[256,512]{1,0:T(8,128)(2,1)S(1)} %get-tuple-element.63.dquery_ref.refs_6_), channel_id=1, source_target_pairs={{0,1},{1,0},{2,3},{3,2},{4,5},{5,4},{6,7},{7,6},{8,9},{9,8},{10,11... | collective-permute-start | bytes 786440 | tf_op jit(solution)/shard_map/ppermute | solution.py:28
  60.1 1.1 %collective-permute-done.22 = bf16[256,256]{1,0:T(8,128)(2,1)S(1)} collective-permute-done((bf16[256,256]{1,0:T(8,128)(2,1)S(1)}, bf16[256,256]{1,0:T(8,128)(2,1)S(1)}, u32[]{:S(2)}, u32[]{:S(2)}) %collective-permute-start.22) | collective-permute-done | bytes 131104 | tf_op jit(solution)/shard_map/ppermute | solution.py:53
  61.2 2.0 %collective-permute-done.21 = bf16[256,256]{1,0:T(8,128)(2,1)S(1)} collective-permute-done((bf16[256,256]{1,0:T(8,128)(2,1)S(1)}, bf16[256,256]{1,0:T(8,128)(2,1)S(1)}, u32[]{:S(2)}, u32[]{:S(2)}) %collective-permute-start.21) | collective-permute-done | bytes 131104 | tf_op jit(solution)/shard_map/ppermute | solution.py:53
  63.2 2.8 %collective-permute-start.25 = (bf16[256,256]{1,0:T(8,128)(2,1)S(1)}, bf16[256,256]{1,0:T(8,128)(2,1)S(1)}, u32[]{:S(2)}, u32[]{:S(2)}) collective-permute-start(bf16[256,256]{1,0:T(8,128)(2,1)S(1)} %add_convert_fusion.3.dpair_ref.refs_7_.refs_14_), channel_id=1, source_target_pairs={{0,1},{1,0},{2,3},{3,2},{4,5},{5,4},{6,7},{7,6},{8,9},{9,8},{10,11... | collective-permute-start | bytes 393224 | tf_op jit(solution)/shard_map/ppermute | solution.py:28
  66.0 0.7 collective-permute-done.24.dquery_ref.refs_8_
  66.7 2.2 %collective-permute-done.25.dpair_ref.refs_9_ = bf16[256,256]{1,0:T(8,128)(2,1)S(1)} collective-permute-done((bf16[256,256]{1,0:T(8,128)(2,1)S(1)}, bf16[256,256]{1,0:T(8,128)(2,1)S(1)}, u32[]{:S(2)}, u32[]{:S(2)}) %collective-permute-start.25) | collective-permute-done | bytes 131104 | tf_op jit(solution)/shard_map/ppermute | solution.py:28
  68.9 0.5 collective-permute-start.33
  69.4 0.8 collective-permute-done.31.refs_11_
  70.5 1.0 %weight_terms.3 = (bf16[256,768]{1,0:T(8,128)(2,1)S(1)}, f32[128,768]{1,0:T(8,128)S(1)}, bf16[128,768]{1,0:T(8,128)(2,1)S(1)}) custom-call(bf16[256,1024]{1,0:T(8,128)(2,1)S(1)} %copy-done, bf16[256,1536]{1,0:T(8,128)(2,1)S(1)} %collective-permute-done.6.refs_0_.refs_1_, bf16[256,512]{1,0:T(8,128)(2,1)S(1)} %collective-permute-done.23.refs_2_, ...), custom_call_target="tpu_custom_call" | custom-call | tf_op jit(solution)/shard_map/weight_terms/pallas_call | solution.py:256
  71.5 2.3 %collective-permute-start.36 = (bf16[128,768]{1,0:T(8,128)(2,1)S(1)}, bf16[128,768]{1,0:T(8,128)(2,1)S(1)}, u32[]{:S(2)}, u32[]{:S(2)}) collective-permute-start(bf16[128,768]{1,0:T(8,128)(2,1)S(1)} %get-tuple-element.72), channel_id=1, source_target_pairs={{0,2},{1,3},{2,0},{3,1},{4,6},{5,7},{6,4},{7,5},{8,10},{9,11},{10,... | collective-permute-start | bytes 589832 | tf_op jit(solution)/shard_map/ppermute | solution.py:35
  73.8 0.8 width_grad.3
  74.6 1.0 collective-permute-start.26
  75.5 3.9 %collective-permute-start.34 = (bf16[256,768]{1,0:T(8,128)(2,1)S(1)}, bf16[256,768]{1,0:T(8,128)(2,1)S(1)}, u32[]{:S(2)}, u32[]{:S(2)}) collective-permute-start(bf16[256,768]{1,0:T(8,128)(2,1)S(1)} %get-tuple-element.69), channel_id=1, source_target_pairs={{0,8},{4,12},{8,16},{12,20},{16,24},{20,28},{24,0},{28,4},{1,9},{5... | collective-permute-start | bytes 1179656 | tf_op jit(solution)/shard_map/ppermute | solution.py:47
  79.4 1.0 %weight_terms.2 = (f32[128,768]{1,0:T(8,128)S(1)}, bf16[128,768]{1,0:T(8,128)(2,1)S(1)}, f32[128,768]{1,0:T(8,128)S(1)}, bf16[128,768]{1,0:T(8,128)(2,1)S(1)}) custom-call(bf16[256,1024]{1,0:T(8,128)(2,1)S(1)} %copy-done, bf16[256,1536]{1,0:T(8,128)(2,1)S(1)} %collective-permute-done.6.refs_0_.refs_1_, bf16[256,512]{1,0:T(8,128)(2,1)S(1)} %collective-permute-done.23.refs_2_, ...), custom_call_target="tpu_custom_call" | custom-call | tf_op jit(solution)/shard_map/weight_terms/pallas_call | solution.py:256
  80.5 1.0 %collective-permute-start.38 = (bf16[128,768]{1,0:T(8,128)(2,1)S(1)}, bf16[128,768]{1,0:T(8,128)(2,1)S(1)}, u32[]{:S(2)}, u32[]{:S(2)}) collective-permute-start(bf16[128,768]{1,0:T(8,128)(2,1)S(1)} %get-tuple-element.74), channel_id=1, source_target_pairs={{0,2},{1,3},{2,0},{3,1},{4,6},{5,7},{6,4},{7,5},{8,10},{9,11},{10,... | collective-permute-start | bytes 589832 | tf_op jit(solution)/shard_map/ppermute | solution.py:35
  81.5 0.8 collective-permute-start.37
  82.3 4.5 %collective-permute-done.38 = bf16[128,768]{1,0:T(8,128)(2,1)S(1)} collective-permute-done((bf16[128,768]{1,0:T(8,128)(2,1)S(1)}, bf16[128,768]{1,0:T(8,128)(2,1)S(1)}, u32[]{:S(2)}, u32[]{:S(2)}) %collective-permute-start.38) | collective-permute-done | bytes 196640 | tf_op jit(solution)/shard_map/ppermute | solution.py:35
  87.2 2.2 %collective-permute-done.34 = bf16[256,768]{1,0:T(8,128)(2,1)S(1)} collective-permute-done((bf16[256,768]{1,0:T(8,128)(2,1)S(1)}, bf16[256,768]{1,0:T(8,128)(2,1)S(1)}, u32[]{:S(2)}, u32[]{:S(2)}) %collective-permute-start.34) | collective-permute-done | bytes 393248 | tf_op jit(solution)/shard_map/ppermute | solution.py:47
  89.5 1.0 %collective-permute-start.35 = (bf16[128,768]{1,0:T(8,128)(2,1)S(1)}, bf16[128,768]{1,0:T(8,128)(2,1)S(1)}, u32[]{:S(2)}, u32[]{:S(2)}) collective-permute-start(bf16[128,768]{1,0:T(8,128)(2,1)S(1)} %get-tuple-element.82), channel_id=1, source_target_pairs={{0,2},{1,3},{2,0},{3,1},{4,6},{5,7},{6,4},{7,5},{8,10},{9,11},{10,... | collective-permute-start | bytes 589832 | tf_op jit(solution)/shard_map/ppermute | solution.py:35
  90.5 1.6 %width_grad.2 = (bf16[256,2048]{1,0:T(8,128)(2,1)S(1)}, bf16[256,512]{1,0:T(8,128)(2,1)S(1)}, bf16[16,128]{1,0:T(8,128)(2,1)}) custom-call(bf16[256,512]{1,0:T(8,128)(2,1)S(1)} %get-tuple-element.63.dquery_ref.refs_6_, bf16[256,256]{1,0:T(8,128)(2,1)S(1)} %add_convert_fusion.3.dpair_ref.refs_7_.refs_14_, ...), custom_call_target="tpu_custom_call" | custom-call | tf_op jit(solution)/shard_map/width_grad/pallas_call | solution.py:209
  92.1 4.8 %collective-permute-done.37.refs_5_ = bf16[128,768]{1,0:T(8,128)(2,1)S(1)} collective-permute-done((bf16[128,768]{1,0:T(8,128)(2,1)S(1)}, bf16[128,768]{1,0:T(8,128)(2,1)S(1)}, u32[]{:S(2)}, u32[]{:S(2)}) %collective-permute-start.37) | collective-permute-done | bytes 196640 | tf_op jit(solution)/shard_map/ppermute | solution.py:47
  97.1 1.7 %finish.1 = (bf16[256,4096]{1,0:T(8,128)(2,1)}, f32[128,768]{1,0:T(8,128)}) custom-call(bf16[256,2048]{1,0:T(8,128)(2,1)S(1)} %get-tuple-element.61.refs_0_, bf16[256,1536]{1,0:T(8,128)(2,1)S(1)} %collective-permute-done.26.refs_1_, bf16[256,512]{1,0:T(8,128)(2,1)S(1)} %get-tuple-element.65.refs_2_, bf16[128,768]{1,0:T(8,128)(2,1)S(1)} %collective-permute-done.35.refs_3_, ...), custom_call_target="tpu_custom_call" | custom-call | tf_op jit(solution)/shard_map/finish/pallas_call | solution.py:145
  (70 shorter events, 3.3 us)
Async XLA Ops:
  0.6 32.2 %copy-start.4 = (bf16[512,768]{1,0:T(8,128)(2,1)S(1)}, bf16[512,768]{1,0:T(8,128)(2,1)}, u32[]{:S(2)}) copy-start(bf16[512,768]{1,0:T(8,128)(2,1)} %param.6) | copy-start | bytes 2359300
  0.6 21.0 %copy-start.3 = (s32[1,8]{1,0:T(1,128)S(1)}, s32[1,8]{1,0:T(1,128)}, u32[]{:S(2)}) copy-start(s32[1,8]{1,0:T(1,128)} %param.8) | copy-start | bytes 100
  0.7 32.1 %copy-start.6 = (s32[1,8]{1,0:T(1,128)S(1)}, s32[1,8]{1,0:T(1,128)}, u32[]{:S(2)}) copy-start(s32[1,8]{1,0:T(1,128)} %param.9) | copy-start | bytes 100
  1.7 10.0 %collective-permute-start.1 = (bf16[128,768]{1,0:T(8,128)(2,1)S(1)}, bf16[128,768]{1,0:T(8,128)(2,1)S(1)}, u32[]{:S(2)}, u32[]{:S(2)}) collective-permute-start(bf16[128,768]{1,0:T(8,128)(2,1)S(1)} %constant_dynamic-slice_fusion), channel_id=1, source_target_pairs={{0,8},{4,12},{8,16},{12,20},{16,24},{20,28},{24,0},{28,4},{1,9},{5... | collective-permute-start | bytes 589832 | tf_op jit(solution)/shard_map/ppermute | solution.py:47
  11.7 20.5 %collective-permute-start.6 = (bf16[256,1536]{1,0:T(8,128)(2,1)}, bf16[256,1536]{1,0:T(8,128)(2,1)S(1)}, u32[]{:S(2)}, u32[]{:S(2)}) collective-permute-start(bf16[256,1536]{1,0:T(8,128)(2,1)} %get-tuple-element.50), channel_id=1, source_target_pairs={{0,1},{1,0},{2,3},{3,2},{4,5},{5,4},{6,7},{7,6},{8,9},{9,8},{10,11... | collective-permute-start | bytes 2359304 | tf_op jit(solution)/shard_map/ppermute | solution.py:28
  13.2 6.9 %collective-permute-start.3 = (bf16[128,768]{1,0:T(8,128)(2,1)S(1)}, bf16[128,768]{1,0:T(8,128)(2,1)S(1)}, u32[]{:S(2)}, u32[]{:S(2)}) collective-permute-start(bf16[128,768]{1,0:T(8,128)(2,1)S(1)} %constant_dynamic-slice_fusion), channel_id=1, source_target_pairs={{0,24},{4,28},{8,0},{12,4},{16,8},{20,12},{24,16},{28,20},{1,25},{... | collective-permute-start | bytes 589832 | tf_op jit(solution)/shard_map/ppermute | solution.py:47
  14.9 11.5 %collective-permute-start = (bf16[128,768]{1,0:T(8,128)(2,1)S(1)}, bf16[128,768]{1,0:T(8,128)(2,1)S(1)}, u32[]{:S(2)}, u32[]{:S(2)}) collective-permute-start(bf16[128,768]{1,0:T(8,128)(2,1)S(1)} %constant_dynamic-slice_fusion), channel_id=1, source_target_pairs={{0,16},{4,20},{8,24},{12,28},{16,0},{20,4},{24,8},{28,12},{1,17},{... | collective-permute-start | bytes 589832 | tf_op jit(solution)/shard_map/ppermute | solution.py:47
  14.9 11.5 %collective-permute-start.2 = (bf16[128,768]{1,0:T(8,128)(2,1)S(1)}, bf16[128,768]{1,0:T(8,128)(2,1)S(1)}, u32[]{:S(2)}, u32[]{:S(2)}) collective-permute-start(bf16[128,768]{1,0:T(8,128)(2,1)S(1)} %collective-permute-done.1.refs_5_.refs_1_.refs_2_.refs_0_), channel_id=1, source_target_pairs={{0,2},{1,3},{2,0},{3,1},{4,6},{5,7},{6,4},{7,5},{8,10},{9,11},{10,... | collective-permute-start | bytes 589832 | tf_op jit(solution)/shard_map/ppermute | solution.py:35
  20.1 6.4 %collective-permute-start.4 = (bf16[128,768]{1,0:T(8,128)(2,1)S(1)}, bf16[128,768]{1,0:T(8,128)(2,1)S(1)}, u32[]{:S(2)}, u32[]{:S(2)}) collective-permute-start(bf16[128,768]{1,0:T(8,128)(2,1)S(1)} %collective-permute-done.3.refs_9_.refs_5_.refs_6_.refs_4_), channel_id=1, source_target_pairs={{0,2},{1,3},{2,0},{3,1},{4,6},{5,7},{6,4},{7,5},{8,10},{9,11},{10,... | collective-permute-start | bytes 589832 | tf_op jit(solution)/shard_map/ppermute | solution.py:35
  26.4 5.7 %collective-permute-start.5 = (bf16[128,768]{1,0:T(8,128)(2,1)S(1)}, bf16[128,768]{1,0:T(8,128)(2,1)S(1)}, u32[]{:S(2)}, u32[]{:S(2)}) collective-permute-start(bf16[128,768]{1,0:T(8,128)(2,1)S(1)} %collective-permute-done.refs_7_.refs_3_.refs_4_.refs_2_), channel_id=1, source_target_pairs={{0,2},{1,3},{2,0},{3,1},{4,6},{5,7},{6,4},{7,5},{8,10},{9,11},{10,... | collective-permute-start | bytes 589832 | tf_op jit(solution)/shard_map/ppermute | solution.py:35
  28.0 4.7 %collective-permute-start.9 = (bf16[128,768]{1,0:T(8,128)(2,1)S(1)}, bf16[128,768]{1,0:T(8,128)(2,1)S(1)}, u32[]{:S(2)}, u32[]{:S(2)}) collective-permute-start(bf16[128,768]{1,0:T(8,128)(2,1)S(1)} %collective-permute-done.1.refs_5_.refs_1_.refs_2_.refs_0_), channel_id=1, source_target_pairs={{0,4},{4,0},{8,12},{12,8},{16,20},{20,16},{24,28},{28,24},{1,5},{5... | collective-permute-start | bytes 589832 | tf_op jit(solution)/shard_map/ppermute | solution.py:40
  28.0 5.4 %collective-permute-start.11 = (bf16[128,768]{1,0:T(8,128)(2,1)S(1)}, bf16[128,768]{1,0:T(8,128)(2,1)S(1)}, u32[]{:S(2)}, u32[]{:S(2)}) collective-permute-start(bf16[128,768]{1,0:T(8,128)(2,1)S(1)} %collective-permute-done.refs_7_.refs_3_.refs_4_.refs_2_), channel_id=1, source_target_pairs={{0,4},{4,0},{8,12},{12,8},{16,20},{20,16},{24,28},{28,24},{1,5},{5... | collective-permute-start | bytes 589832 | tf_op jit(solution)/shard_map/ppermute | solution.py:40
  28.5 4.4 %collective-permute-start.10 = (bf16[128,768]{1,0:T(8,128)(2,1)S(1)}, bf16[128,768]{1,0:T(8,128)(2,1)S(1)}, u32[]{:S(2)}, u32[]{:S(2)}) collective-permute-start(bf16[128,768]{1,0:T(8,128)(2,1)S(1)} %collective-permute-done.2.refs_6_.refs_2_.refs_3_.refs_1_), channel_id=1, source_target_pairs={{0,4},{4,0},{8,12},{12,8},{16,20},{20,16},{24,28},{28,24},{1,5},{5... | collective-permute-start | bytes 589832 | tf_op jit(solution)/shard_map/ppermute | solution.py:40
  32.1 1.4 %collective-permute-start.13 = (bf16[128,768]{1,0:T(8,128)(2,1)S(1)}, bf16[128,768]{1,0:T(8,128)(2,1)S(1)}, u32[]{:S(2)}, u32[]{:S(2)}) collective-permute-start(bf16[128,768]{1,0:T(8,128)(2,1)S(1)} %collective-permute-done.3.refs_9_.refs_5_.refs_6_.refs_4_), channel_id=1, source_target_pairs={{0,4},{4,0},{8,12},{12,8},{16,20},{20,16},{24,28},{28,24},{1,5},{5... | collective-permute-start | bytes 589832 | tf_op jit(solution)/shard_map/ppermute | solution.py:40
  32.1 1.8 %collective-permute-start.14 = (bf16[128,768]{1,0:T(8,128)(2,1)S(1)}, bf16[128,768]{1,0:T(8,128)(2,1)S(1)}, u32[]{:S(2)}, u32[]{:S(2)}) collective-permute-start(bf16[128,768]{1,0:T(8,128)(2,1)S(1)} %collective-permute-done.4.refs_10_.refs_6_.refs_7_.refs_5_), channel_id=1, source_target_pairs={{0,4},{4,0},{8,12},{12,8},{16,20},{20,16},{24,28},{28,24},{1,5},{5... | collective-permute-start | bytes 589832 | tf_op jit(solution)/shard_map/ppermute | solution.py:40
  32.7 1.5 %collective-permute-start.12 = (bf16[128,768]{1,0:T(8,128)(2,1)S(1)}, bf16[128,768]{1,0:T(8,128)(2,1)S(1)}, u32[]{:S(2)}, u32[]{:S(2)}) collective-permute-start(bf16[128,768]{1,0:T(8,128)(2,1)S(1)} %collective-permute-done.5.refs_8_.refs_4_.refs_5_.refs_3_), channel_id=1, source_target_pairs={{0,4},{4,0},{8,12},{12,8},{16,20},{20,16},{24,28},{28,24},{1,5},{5... | collective-permute-start | bytes 589832 | tf_op jit(solution)/shard_map/ppermute | solution.py:40
  32.9 2.9 %collective-permute-start.7 = (bf16[128,768]{1,0:T(8,128)(2,1)S(1)}, bf16[128,768]{1,0:T(8,128)(2,1)S(1)}, u32[]{:S(2)}, u32[]{:S(2)}) collective-permute-start(bf16[128,768]{1,0:T(8,128)(2,1)S(1)} %get-tuple-element.80.refs_3_.refs_0_), channel_id=1, source_target_pairs={{0,4},{4,0},{8,12},{12,8},{16,20},{20,16},{24,28},{28,24},{1,5},{5... | collective-permute-start | bytes 589832 | tf_op jit(solution)/shard_map/ppermute | solution.py:40
  33.4 2.5 %collective-permute-start.8 = (bf16[128,768]{1,0:T(8,128)(2,1)S(1)}, bf16[128,768]{1,0:T(8,128)(2,1)S(1)}, u32[]{:S(2)}, u32[]{:S(2)}) collective-permute-start(bf16[128,768]{1,0:T(8,128)(2,1)S(1)} %get-tuple-element.79.refs_4_.refs_1_), channel_id=1, source_target_pairs={{0,4},{4,0},{8,12},{12,8},{16,20},{20,16},{24,28},{28,24},{1,5},{5... | collective-permute-start | bytes 589832 | tf_op jit(solution)/shard_map/ppermute | solution.py:40
  33.6 3.8 %collective-permute-start.15 = (bf16[128,768]{1,0:T(8,128)(2,1)S(1)}, bf16[128,768]{1,0:T(8,128)(2,1)S(1)}, u32[]{:S(2)}, u32[]{:S(2)}) collective-permute-start(bf16[128,768]{1,0:T(8,128)(2,1)S(1)} %get-tuple-element.78.refs_19_.refs_16_), channel_id=1, source_target_pairs={{0,4},{4,0},{8,12},{12,8},{16,20},{20,16},{24,28},{28,24},{1,5},{5... | collective-permute-start | bytes 589832 | tf_op jit(solution)/shard_map/ppermute | solution.py:40
  33.9 3.5 %collective-permute-start.16 = (bf16[128,768]{1,0:T(8,128)(2,1)S(1)}, bf16[128,768]{1,0:T(8,128)(2,1)S(1)}, u32[]{:S(2)}, u32[]{:S(2)}) collective-permute-start(bf16[128,768]{1,0:T(8,128)(2,1)S(1)} %get-tuple-element.77.refs_20_.refs_17_), channel_id=1, source_target_pairs={{0,4},{4,0},{8,12},{12,8},{16,20},{20,16},{24,28},{28,24},{1,5},{5... | collective-permute-start | bytes 589832 | tf_op jit(solution)/shard_map/ppermute | solution.py:40
  34.5 1.2 %copy-start.1 = (bf16[256,1024]{1,0:T(8,128)(2,1)S(1)}, bf16[256,1024]{1,0:T(8,128)(2,1)}, u32[]{:S(2)}) copy-start(bf16[256,1024]{1,0:T(8,128)(2,1)} %get-tuple-element.41.refs_1_) | copy-start | bytes 1572868
  34.5 2.9 %copy-start = (bf16[256,1024]{1,0:T(8,128)(2,1)S(1)}, bf16[256,1024]{1,0:T(8,128)(2,1)}, u32[]{:S(2)}) copy-start(bf16[256,1024]{1,0:T(8,128)(2,1)} %get-tuple-element.40.refs_0_) | copy-start | bytes 1572868
  34.5 2.9 %copy-start.2 = (bf16[256,512]{1,0:T(8,128)(2,1)S(1)}, bf16[256,512]{1,0:T(8,128)(2,1)}, u32[]{:S(2)}) copy-start(bf16[256,512]{1,0:T(8,128)(2,1)} %get-tuple-element.62.refs_2_) | copy-start | bytes 786436
  34.6 6.4 %collective-permute-start.18 = (bf16[256,256]{1,0:T(8,128)(2,1)S(1)}, bf16[256,256]{1,0:T(8,128)(2,1)S(1)}, u32[]{:S(2)}, u32[]{:S(2)}) collective-permute-start(bf16[256,256]{1,0:T(8,128)(2,1)S(1)} %project.5), channel_id=1, source_target_pairs={{0,1},{1,0},{2,3},{3,2},{4,5},{5,4},{6,7},{7,6},{8,9},{9,8},{10,11... | collective-permute-start | bytes 393224 | tf_op jit(solution)/shard_map/ppermute | solution.py:28
  35.8 30.2 %collective-permute-start.27 = (bf16[256,1024]{1,0:T(8,128)(2,1)S(1)}, bf16[256,1024]{1,0:T(8,128)(2,1)S(1)}, u32[]{:S(2)}, u32[]{:S(2)}) collective-permute-start(bf16[256,1024]{1,0:T(8,128)(2,1)S(1)} %copy-done.1), channel_id=1, source_target_pairs={{0,4},{4,0},{8,12},{12,8},{16,20},{20,16},{24,28},{28,24},{1,5},{5... | collective-permute-start | bytes 1572872 | tf_op jit(solution)/shard_map/ppermute | solution.py:40
  35.9 14.3 %collective-permute-start.17 = (bf16[256,512]{1,0:T(8,128)(2,1)S(1)}, bf16[256,512]{1,0:T(8,128)(2,1)S(1)}, u32[]{:S(2)}, u32[]{:S(2)}) collective-permute-start(bf16[256,512]{1,0:T(8,128)(2,1)S(1)} %project.4), channel_id=1, source_target_pairs={{0,1},{1,0},{2,3},{3,2},{4,5},{5,4},{6,7},{7,6},{8,9},{9,8},{10,11... | collective-permute-start | bytes 786440 | tf_op jit(solution)/shard_map/ppermute | solution.py:28
  37.4 9.2 %copy-start.5 = (bf16[1,256,512]{2,1,0:T(8,128)(2,1)S(1)}, bf16[1,256,512]{2,1,0:T(8,128)(2,1)}, u32[]{:S(2)}) copy-start(bf16[1,256,512]{2,1,0:T(8,128)(2,1)} %param.7) | copy-start | bytes 786436
  41.0 8.7 %collective-permute-start.19 = (bf16[256,256]{1,0:T(8,128)(2,1)S(1)}, bf16[256,256]{1,0:T(8,128)(2,1)S(1)}, u32[]{:S(2)}, u32[]{:S(2)}) collective-permute-start(bf16[256,256]{1,0:T(8,128)(2,1)S(1)} %add_convert_fusion.4.refs_2_), channel_id=1, source_target_pairs={{0,2},{1,3},{4,6},{5,7},{8,10},{9,11},{12,14},{13,15},{16,18},{17,... | collective-permute-start | bytes 393224 | tf_op jit(solution)/shard_map/ppermute | solution.py:53
  44.4 5.8 %collective-permute-start.20 = (bf16[256,256]{1,0:T(8,128)(2,1)S(1)}, bf16[256,256]{1,0:T(8,128)(2,1)S(1)}, u32[]{:S(2)}, u32[]{:S(2)}) collective-permute-start(bf16[256,256]{1,0:T(8,128)(2,1)S(1)} %add_convert_fusion.4.refs_2_), channel_id=1, source_target_pairs={{0,1},{1,2},{2,3},{4,5},{5,6},{6,7},{8,9},{9,10},{10,11},{12,13},{... | collective-permute-start | bytes 393224 | tf_op jit(solution)/shard_map/ppermute | solution.py:53
  46.7 23.6 %collective-permute-start.28 = (bf16[256,1536]{1,0:T(8,128)(2,1)S(1)}, bf16[256,1536]{1,0:T(8,128)(2,1)S(1)}, u32[]{:S(2)}, u32[]{:S(2)}) collective-permute-start(bf16[256,1536]{1,0:T(8,128)(2,1)S(1)} %collective-permute-done.6.refs_0_.refs_1_), channel_id=1, source_target_pairs={{0,4},{4,0},{8,12},{12,8},{16,20},{20,16},{24,28},{28,24},{1,5},{5... | collective-permute-start | bytes 2359304 | tf_op jit(solution)/shard_map/ppermute | solution.py:40
  49.7 7.2 %collective-permute-start.23 = (bf16[256,512]{1,0:T(8,128)(2,1)S(1)}, bf16[256,512]{1,0:T(8,128)(2,1)S(1)}, u32[]{:S(2)}, u32[]{:S(2)}) collective-permute-start(bf16[256,512]{1,0:T(8,128)(2,1)S(1)} %copy-done.2), channel_id=1, source_target_pairs={{0,1},{1,0},{2,3},{3,2},{4,5},{5,4},{6,7},{7,6},{8,9},{9,8},{10,11... | collective-permute-start | bytes 786440 | tf_op jit(solution)/shard_map/ppermute | solution.py:28
  54.3 6.9 %collective-permute-start.22 = (bf16[256,256]{1,0:T(8,128)(2,1)S(1)}, bf16[256,256]{1,0:T(8,128)(2,1)S(1)}, u32[]{:S(2)}, u32[]{:S(2)}) collective-permute-start(bf16[256,256]{1,0:T(8,128)(2,1)S(1)} %get-tuple-element.84), channel_id=1, source_target_pairs={{2,0},{3,1},{6,4},{7,5},{10,8},{11,9},{14,12},{15,13},{18,16},{19,... | collective-permute-start | bytes 393224 | tf_op jit(solution)/shard_map/ppermute | solution.py:53
  55.6 7.5 %collective-permute-start.21 = (bf16[256,256]{1,0:T(8,128)(2,1)S(1)}, bf16[256,256]{1,0:T(8,128)(2,1)S(1)}, u32[]{:S(2)}, u32[]{:S(2)}) collective-permute-start(bf16[256,256]{1,0:T(8,128)(2,1)S(1)} %get-tuple-element.83), channel_id=1, source_target_pairs={{1,0},{2,1},{3,2},{5,4},{6,5},{7,6},{9,8},{10,9},{11,10},{13,12},{... | collective-permute-start | bytes 393224 | tf_op jit(solution)/shard_map/ppermute | solution.py:53
  56.9 9.8 %collective-permute-start.24 = (bf16[256,512]{1,0:T(8,128)(2,1)S(1)}, bf16[256,512]{1,0:T(8,128)(2,1)S(1)}, u32[]{:S(2)}, u32[]{:S(2)}) collective-permute-start(bf16[256,512]{1,0:T(8,128)(2,1)S(1)} %get-tuple-element.63.dquery_ref.refs_6_), channel_id=1, source_target_pairs={{0,1},{1,0},{2,3},{3,2},{4,5},{5,4},{6,7},{7,6},{8,9},{9,8},{10,11... | collective-permute-start | bytes 786440 | tf_op jit(solution)/shard_map/ppermute | solution.py:28
  61.2 7.8 %collective-permute-start.30 = (bf16[256,512]{1,0:T(8,128)(2,1)S(1)}, bf16[256,512]{1,0:T(8,128)(2,1)S(1)}, u32[]{:S(2)}, u32[]{:S(2)}) collective-permute-start(bf16[256,512]{1,0:T(8,128)(2,1)S(1)} %get-tuple-element.63.dquery_ref.refs_6_), channel_id=1, source_target_pairs={{0,4},{4,0},{8,12},{12,8},{16,20},{20,16},{24,28},{28,24},{1,5},{5... | collective-permute-start | bytes 786440 | tf_op jit(solution)/shard_map/ppermute | solution.py:40
  63.2 5.7 %collective-permute-start.25 = (bf16[256,256]{1,0:T(8,128)(2,1)S(1)}, bf16[256,256]{1,0:T(8,128)(2,1)S(1)}, u32[]{:S(2)}, u32[]{:S(2)}) collective-permute-start(bf16[256,256]{1,0:T(8,128)(2,1)S(1)} %add_convert_fusion.3.dpair_ref.refs_7_.refs_14_), channel_id=1, source_target_pairs={{0,1},{1,0},{2,3},{3,2},{4,5},{5,4},{6,7},{7,6},{8,9},{9,8},{10,11... | collective-permute-start | bytes 393224 | tf_op jit(solution)/shard_map/ppermute | solution.py:28
  66.0 4.3 %collective-permute-start.29 = (bf16[256,512]{1,0:T(8,128)(2,1)S(1)}, bf16[256,512]{1,0:T(8,128)(2,1)S(1)}, u32[]{:S(2)}, u32[]{:S(2)}) collective-permute-start(bf16[256,512]{1,0:T(8,128)(2,1)S(1)} %collective-permute-done.23.refs_2_), channel_id=1, source_target_pairs={{0,4},{4,0},{8,12},{12,8},{16,20},{20,16},{24,28},{28,24},{1,5},{5... | collective-permute-start | bytes 786440 | tf_op jit(solution)/shard_map/ppermute | solution.py:40
  66.7 3.8 %collective-permute-start.32 = (bf16[256,512]{1,0:T(8,128)(2,1)S(1)}, bf16[256,512]{1,0:T(8,128)(2,1)S(1)}, u32[]{:S(2)}, u32[]{:S(2)}) collective-permute-start(bf16[256,512]{1,0:T(8,128)(2,1)S(1)} %collective-permute-done.24.dquery_ref.refs_8_), channel_id=1, source_target_pairs={{0,4},{4,0},{8,12},{12,8},{16,20},{20,16},{24,28},{28,24},{1,5},{5... | collective-permute-start | bytes 786440 | tf_op jit(solution)/shard_map/ppermute | solution.py:40
  68.9 1.3 %collective-permute-start.31 = (bf16[256,256]{1,0:T(8,128)(2,1)S(1)}, bf16[256,256]{1,0:T(8,128)(2,1)S(1)}, u32[]{:S(2)}, u32[]{:S(2)}) collective-permute-start(bf16[256,256]{1,0:T(8,128)(2,1)S(1)} %add_convert_fusion.3.dpair_ref.refs_7_.refs_14_), channel_id=1, source_target_pairs={{0,4},{4,0},{8,12},{12,8},{16,20},{20,16},{24,28},{28,24},{1,5},{5... | collective-permute-start | bytes 393224 | tf_op jit(solution)/shard_map/ppermute | solution.py:40
  68.9 1.5 %collective-permute-start.33 = (bf16[256,256]{1,0:T(8,128)(2,1)S(1)}, bf16[256,256]{1,0:T(8,128)(2,1)S(1)}, u32[]{:S(2)}, u32[]{:S(2)}) collective-permute-start(bf16[256,256]{1,0:T(8,128)(2,1)S(1)} %collective-permute-done.25.dpair_ref.refs_9_), channel_id=1, source_target_pairs={{0,4},{4,0},{8,12},{12,8},{16,20},{20,16},{24,28},{28,24},{1,5},{5... | collective-permute-start | bytes 393224 | tf_op jit(solution)/shard_map/ppermute | solution.py:40
  71.5 10.0 %collective-permute-start.36 = (bf16[128,768]{1,0:T(8,128)(2,1)S(1)}, bf16[128,768]{1,0:T(8,128)(2,1)S(1)}, u32[]{:S(2)}, u32[]{:S(2)}) collective-permute-start(bf16[128,768]{1,0:T(8,128)(2,1)S(1)} %get-tuple-element.72), channel_id=1, source_target_pairs={{0,2},{1,3},{2,0},{3,1},{4,6},{5,7},{6,4},{7,5},{8,10},{9,11},{10,... | collective-permute-start | bytes 589832 | tf_op jit(solution)/shard_map/ppermute | solution.py:35
  74.6 22.5 %collective-permute-start.26 = (bf16[256,1536]{1,0:T(8,128)(2,1)S(1)}, bf16[256,1536]{1,0:T(8,128)(2,1)S(1)}, u32[]{:S(2)}, u32[]{:S(2)}) collective-permute-start(bf16[256,1536]{1,0:T(8,128)(2,1)S(1)} %get-tuple-element.64), channel_id=1, source_target_pairs={{0,1},{1,0},{2,3},{3,2},{4,5},{5,4},{6,7},{7,6},{8,9},{9,8},{10,11... | collective-permute-start | bytes 2359304 | tf_op jit(solution)/shard_map/ppermute | solution.py:28
  75.5 13.9 %collective-permute-start.34 = (bf16[256,768]{1,0:T(8,128)(2,1)S(1)}, bf16[256,768]{1,0:T(8,128)(2,1)S(1)}, u32[]{:S(2)}, u32[]{:S(2)}) collective-permute-start(bf16[256,768]{1,0:T(8,128)(2,1)S(1)} %get-tuple-element.69), channel_id=1, source_target_pairs={{0,8},{4,12},{8,16},{12,20},{16,24},{20,28},{24,0},{28,4},{1,9},{5... | collective-permute-start | bytes 1179656 | tf_op jit(solution)/shard_map/ppermute | solution.py:47
  80.5 6.3 %collective-permute-start.38 = (bf16[128,768]{1,0:T(8,128)(2,1)S(1)}, bf16[128,768]{1,0:T(8,128)(2,1)S(1)}, u32[]{:S(2)}, u32[]{:S(2)}) collective-permute-start(bf16[128,768]{1,0:T(8,128)(2,1)S(1)} %get-tuple-element.74), channel_id=1, source_target_pairs={{0,2},{1,3},{2,0},{3,1},{4,6},{5,7},{6,4},{7,5},{8,10},{9,11},{10,... | collective-permute-start | bytes 589832 | tf_op jit(solution)/shard_map/ppermute | solution.py:35
  81.5 15.5 %collective-permute-start.37 = (bf16[128,768]{1,0:T(8,128)(2,1)S(1)}, bf16[128,768]{1,0:T(8,128)(2,1)S(1)}, u32[]{:S(2)}, u32[]{:S(2)}) collective-permute-start(bf16[128,768]{1,0:T(8,128)(2,1)S(1)} %add_convert_fusion.1), channel_id=1, source_target_pairs={{0,16},{4,20},{8,24},{12,28},{16,0},{20,4},{24,8},{28,12},{1,17},{... | collective-permute-start | bytes 589832 | tf_op jit(solution)/shard_map/ppermute | solution.py:47
  86.8 10.2 %collective-permute-start.39 = (bf16[128,768]{1,0:T(8,128)(2,1)S(1)}, bf16[128,768]{1,0:T(8,128)(2,1)S(1)}, u32[]{:S(2)}, u32[]{:S(2)}) collective-permute-start(bf16[128,768]{1,0:T(8,128)(2,1)S(1)} %add_convert_fusion), channel_id=1, source_target_pairs={{0,24},{4,28},{8,0},{12,4},{16,8},{20,12},{24,16},{28,20},{1,25},{... | collective-permute-start | bytes 589832 | tf_op jit(solution)/shard_map/ppermute | solution.py:47
  89.5 7.6 %collective-permute-start.35 = (bf16[128,768]{1,0:T(8,128)(2,1)S(1)}, bf16[128,768]{1,0:T(8,128)(2,1)S(1)}, u32[]{:S(2)}, u32[]{:S(2)}) collective-permute-start(bf16[128,768]{1,0:T(8,128)(2,1)S(1)} %get-tuple-element.82), channel_id=1, source_target_pairs={{0,2},{1,3},{2,0},{3,1},{4,6},{5,7},{6,4},{7,5},{8,10},{9,11},{10,... | collective-permute-start | bytes 589832 | tf_op jit(solution)/shard_map/ppermute | solution.py:35

commit v13 on v11

--- a/solution.py
+++ b/solution.py
@@ -315,9 +315,9 @@
         if h + 1 < heads:
             products(h + 1)
         outputs(h)
+        score_grads(h)
         if h:
             grads(h - 1)
-        score_grads(h)
     grads(heads - 1)
     both = jnp.concatenate([sums[0] * scale, sums[1]], axis=1)
     dpair_ref[...] = both[back * rows :]
@@ -399,7 +399,7 @@
     kept = kept_rows(doc_row, flag_row, positions)
     cot = jnp.where(kept[:, None] > 0, cotangent[0], jnp.zeros_like(cotangent[0]))
 
-    near, _ = lax.optimization_barrier((near, pair))
+    near, _ = lax.optimization_barrier((near, pair_from))
     near_other = swap_x(near)
     pairs = [shift_seq(pair, j) for j in range(back, 0, -1)] + [pair]
     attention, dquery, dpair, dback = attend(doc_row, query, query_from, cot, pairs)

time: 100 us -> 100 us (level)
  no operation moved by 1% of the time
where the time goes in v13:
time: 100 us
  starting transfers between devices  47.1 us (47%)
  waiting for transfers between devices  35 us (35%)
  Pallas kernels  15.3 us (15%)
  local copies, waits for them, and re-layouts  1.12 us (1%)
    ppermute x6, waiting for transfers between devices, shift_chip(): return lax.ppermute(array, 'dp', pairs)  16.4 us
    ppermute x6, starting transfers between devices, shift_chip(): return lax.ppermute(array, 'dp', pairs)  15.6 us
    ppermute x7, starting transfers between devices, swap_x(): return lax.ppermute(array, 'seq', [(i, i ^ 1) for i in range(count)])  10.6 us
    ppermute x7, starting transfers between devices, shift_rest(): return lax.ppermute(array, 'seq', pairs)  9.84 us
    ppermute x4, starting transfers between devices, shift_seq(): return lax.ppermute(array, 'seq', pairs)  8.18 us
    ppermute x4, waiting for transfers between devices, shift_seq(): return lax.ppermute(array, 'seq', pairs)  6.44 us
    ppermute x7, waiting for transfers between devices, shift_rest(): return lax.ppermute(array, 'seq', pairs)  5.74 us
    ppermute x7, waiting for transfers between devices, swap_x(): return lax.ppermute(array, 'seq', [(i, i ^ 1) for i in range(count)])  5.23 us
  transfers between devices with their start and end apart: 41, of which 17 were waited for; matrix products, arithmetic and copies ran while one was open for 1% of the time, Pallas kernels for 13%

profile of v13, /device:TPU:0, one launch (start us, length us, event | category | flops | bytes accessed | tf_op | source)
XLA Modules:
  0.0 100.0 jit_solution(12960428038746271938)
XLA Ops:
  0.7 1.0 %constant_dynamic-slice_fusion = bf16[128,768]{1,0:T(8,128)(2,1)S(1)} fusion(bf16[512,768]{1,0:T(8,128)(2,1)} %param.6, s32[]{:T(128)S(6)} %select_n.64), kind=kLoop, calls=%fused_computation.11 | loop fusion | bytes 393220 | tf_op jit(solution)/shard_map/dynamic_slice | solution.py:365
  1.7 3.1 %collective-permute-start.1 = (bf16[128,768]{1,0:T(8,128)(2,1)S(1)}, bf16[128,768]{1,0:T(8,128)(2,1)S(1)}, u32[]{:S(2)}, u32[]{:S(2)}) collective-permute-start(bf16[128,768]{1,0:T(8,128)(2,1)S(1)} %constant_dynamic-slice_fusion), channel_id=1, source_target_pairs={{0,8},{4,12},{8,16},{12,20},{16,24},{20,28},{24,0},{28,4},{1,9},{5... | collective-permute-start | bytes 589832 | tf_op jit(solution)/shard_map/ppermute | solution.py:47
  4.8 2.8 %split_tokens.1 = (bf16[256,1024]{1,0:T(8,128)(2,1)}, bf16[256,1024]{1,0:T(8,128)(2,1)}, bf16[256,1536]{1,0:T(8,128)(2,1)}, bf16[256,512]{1,0:T(8,128)(2,1)}) custom-call(bf16[256,4096]{1,0:T(8,128)(2,1)} %bitcast.26), custom_call_target="tpu_custom_call" | custom-call | tf_op jit(solution)/shard_map/split_tokens/pallas_call | solution.py:105
  7.6 4.1 %collective-permute-done.1.refs_5_.refs_1_.refs_2_.refs_0_ = bf16[128,768]{1,0:T(8,128)(2,1)S(1)} collective-permute-done((bf16[128,768]{1,0:T(8,128)(2,1)S(1)}, bf16[128,768]{1,0:T(8,128)(2,1)S(1)}, u32[]{:S(2)}, u32[]{:S(2)}) %collective-permute-start.1) | collective-permute-done | bytes 196640 | tf_op jit(solution)/shard_map/ppermute | solution.py:47
  11.7 1.5 %collective-permute-start.6 = (bf16[256,1536]{1,0:T(8,128)(2,1)}, bf16[256,1536]{1,0:T(8,128)(2,1)S(1)}, u32[]{:S(2)}, u32[]{:S(2)}) collective-permute-start(bf16[256,1536]{1,0:T(8,128)(2,1)} %get-tuple-element.51), channel_id=1, source_target_pairs={{0,1},{1,0},{2,3},{3,2},{4,5},{5,4},{6,7},{7,6},{8,9},{9,8},{10,11... | collective-permute-start | bytes 2359304 | tf_op jit(solution)/shard_map/ppermute | solution.py:28
  13.2 1.7 %collective-permute-start.3 = (bf16[128,768]{1,0:T(8,128)(2,1)S(1)}, bf16[128,768]{1,0:T(8,128)(2,1)S(1)}, u32[]{:S(2)}, u32[]{:S(2)}) collective-permute-start(bf16[128,768]{1,0:T(8,128)(2,1)S(1)} %constant_dynamic-slice_fusion), channel_id=1, source_target_pairs={{0,24},{4,28},{8,0},{12,4},{16,8},{20,12},{24,16},{28,20},{1,25},{... | collective-permute-start | bytes 589832 | tf_op jit(solution)/shard_map/ppermute | solution.py:47
  14.9 1.5 %collective-permute-start.2 = (bf16[128,768]{1,0:T(8,128)(2,1)S(1)}, bf16[128,768]{1,0:T(8,128)(2,1)S(1)}, u32[]{:S(2)}, u32[]{:S(2)}) collective-permute-start(bf16[128,768]{1,0:T(8,128)(2,1)S(1)} %collective-permute-done.1.refs_5_.refs_1_.refs_2_.refs_0_), channel_id=1, source_target_pairs={{0,2},{1,3},{2,0},{3,1},{4,6},{5,7},{6,4},{7,5},{8,10},{9,11},{10,... | collective-permute-start | bytes 589832 | tf_op jit(solution)/shard_map/ppermute | solution.py:35
  16.4 3.6 %collective-permute-done.3.refs_9_.refs_5_.refs_6_.refs_4_ = bf16[128,768]{1,0:T(8,128)(2,1)S(1)} collective-permute-done((bf16[128,768]{1,0:T(8,128)(2,1)S(1)}, bf16[128,768]{1,0:T(8,128)(2,1)S(1)}, u32[]{:S(2)}, u32[]{:S(2)}) %collective-permute-start.3) | collective-permute-done | bytes 196640 | tf_op jit(solution)/shard_map/ppermute | solution.py:47
  20.1 1.5 %collective-permute-start.4 = (bf16[128,768]{1,0:T(8,128)(2,1)S(1)}, bf16[128,768]{1,0:T(8,128)(2,1)S(1)}, u32[]{:S(2)}, u32[]{:S(2)}) collective-permute-start(bf16[128,768]{1,0:T(8,128)(2,1)S(1)} %collective-permute-done.3.refs_9_.refs_5_.refs_6_.refs_4_), channel_id=1, source_target_pairs={{0,2},{1,3},{2,0},{3,1},{4,6},{5,7},{6,4},{7,5},{8,10},{9,11},{10,... | collective-permute-start | bytes 589832 | tf_op jit(solution)/shard_map/ppermute | solution.py:35
  21.8 4.6 %collective-permute-done.refs_7_.refs_3_.refs_4_.refs_2_ = bf16[128,768]{1,0:T(8,128)(2,1)S(1)} collective-permute-done((bf16[128,768]{1,0:T(8,128)(2,1)S(1)}, bf16[128,768]{1,0:T(8,128)(2,1)S(1)}, u32[]{:S(2)}, u32[]{:S(2)}) %collective-permute-start) | collective-permute-done | bytes 196640 | tf_op jit(solution)/shard_map/ppermute | solution.py:47
  26.4 1.5 %collective-permute-start.5 = (bf16[128,768]{1,0:T(8,128)(2,1)S(1)}, bf16[128,768]{1,0:T(8,128)(2,1)S(1)}, u32[]{:S(2)}, u32[]{:S(2)}) collective-permute-start(bf16[128,768]{1,0:T(8,128)(2,1)S(1)} %collective-permute-done.refs_7_.refs_3_.refs_4_.refs_2_), channel_id=1, source_target_pairs={{0,2},{1,3},{2,0},{3,1},{4,6},{5,7},{6,4},{7,5},{8,10},{9,11},{10,... | collective-permute-start | bytes 589832 | tf_op jit(solution)/shard_map/ppermute | solution.py:35
  28.0 0.5 collective-permute-start.11
  28.5 3.7 %collective-permute-done.5.refs_8_.refs_4_.refs_5_.refs_3_ = bf16[128,768]{1,0:T(8,128)(2,1)S(1)} collective-permute-done((bf16[128,768]{1,0:T(8,128)(2,1)S(1)}, bf16[128,768]{1,0:T(8,128)(2,1)S(1)}, u32[]{:S(2)}, u32[]{:S(2)}) %collective-permute-start.5) | collective-permute-done | bytes 196640 | tf_op jit(solution)/shard_map/ppermute | solution.py:35
  32.1 0.5 collective-permute-start.14
  34.6 0.6 collective-permute-start.18
  35.2 0.6 project.4
  35.9 1.5 %collective-permute-start.17 = (bf16[256,512]{1,0:T(8,128)(2,1)S(1)}, bf16[256,512]{1,0:T(8,128)(2,1)S(1)}, u32[]{:S(2)}, u32[]{:S(2)}) collective-permute-start(bf16[256,512]{1,0:T(8,128)(2,1)S(1)} %project.4), channel_id=1, source_target_pairs={{0,1},{1,0},{2,3},{3,2},{4,5},{5,4},{6,7},{7,6},{8,9},{9,8},{10,11... | collective-permute-start | bytes 786440 | tf_op jit(solution)/shard_map/ppermute | solution.py:28
  37.4 1.2 %project.3 = (f32[256,512]{1,0:T(8,128)S(1)}, f32[256,256]{1,0:T(8,128)S(1)}) custom-call(bf16[256,1024]{1,0:T(8,128)(2,1)S(1)} %copy-done, bf16[256,1024]{1,0:T(8,128)(2,1)S(1)} %copy-done.1, bf16[256,512]{1,0:T(8,128)(2,1)S(1)} %copy-done.2, bf16[128,768]{1,0:T(8,128)(2,1)S(1)} %get-tuple-element.82.refs_3_.refs_0_, ...), custom_call_target="tpu_custom_call" | custom-call | tf_op jit(solution)/shard_map/project/pallas_call | solution.py:182
  38.7 2.3 %collective-permute-done.18 = bf16[256,256]{1,0:T(8,128)(2,1)S(1)} collective-permute-done((bf16[256,256]{1,0:T(8,128)(2,1)S(1)}, bf16[256,256]{1,0:T(8,128)(2,1)S(1)}, u32[]{:S(2)}, u32[]{:S(2)}) %collective-permute-start.18) | collective-permute-done | bytes 131104 | tf_op jit(solution)/shard_map/ppermute | solution.py:28
  41.0 3.4 %collective-permute-start.19 = (bf16[256,256]{1,0:T(8,128)(2,1)S(1)}, bf16[256,256]{1,0:T(8,128)(2,1)S(1)}, u32[]{:S(2)}, u32[]{:S(2)}) collective-permute-start(bf16[256,256]{1,0:T(8,128)(2,1)S(1)} %add_convert_fusion.4.refs_2_), channel_id=1, source_target_pairs={{0,2},{1,3},{4,6},{5,7},{8,10},{9,11},{12,14},{13,15},{16,18},{17,... | collective-permute-start | bytes 393224 | tf_op jit(solution)/shard_map/ppermute | solution.py:53
  44.4 2.2 %collective-permute-start.20 = (bf16[256,256]{1,0:T(8,128)(2,1)S(1)}, bf16[256,256]{1,0:T(8,128)(2,1)S(1)}, u32[]{:S(2)}, u32[]{:S(2)}) collective-permute-start(bf16[256,256]{1,0:T(8,128)(2,1)S(1)} %add_convert_fusion.4.refs_2_), channel_id=1, source_target_pairs={{0,1},{1,2},{2,3},{4,5},{5,6},{6,7},{8,9},{9,10},{10,11},{12,13},{... | collective-permute-start | bytes 393224 | tf_op jit(solution)/shard_map/ppermute | solution.py:53
  46.8 2.9 %collective-permute-done.19.refs_0_ = bf16[256,256]{1,0:T(8,128)(2,1)S(1)} collective-permute-done((bf16[256,256]{1,0:T(8,128)(2,1)S(1)}, bf16[256,256]{1,0:T(8,128)(2,1)S(1)}, u32[]{:S(2)}, u32[]{:S(2)}) %collective-permute-start.19) | collective-permute-done | bytes 131104 | tf_op jit(solution)/shard_map/ppermute | solution.py:53
  50.2 4.1 %attend.1 = (bf16[256,512]{1,0:T(8,128)(2,1)}, bf16[256,512]{1,0:T(8,128)(2,1)S(1)}, f32[256,256]{1,0:T(8,128)S(1)}, bf16[512,256]{1,0:T(8,128)(2,1)S(1)}) custom-call(s32[8]{0:T(128)S(1)} %bitcast.25, f32[256,512]{1,0:T(8,128)S(1)} %get-tuple-element.55.q_ref, bf16[256,512]{1,0:T(8,128)(2,1)S(1)} %collective-permute-done.17.q_from_ref, ...), custom_call_target="tpu_custom_call" | custom-call | tf_op jit(solution)/shard_map/attend/pallas_call | solution.py:331
  54.3 1.3 %collective-permute-start.22 = (bf16[256,256]{1,0:T(8,128)(2,1)S(1)}, bf16[256,256]{1,0:T(8,128)(2,1)S(1)}, u32[]{:S(2)}, u32[]{:S(2)}) collective-permute-start(bf16[256,256]{1,0:T(8,128)(2,1)S(1)} %get-tuple-element.84), channel_id=1, source_target_pairs={{2,0},{3,1},{6,4},{7,5},{10,8},{11,9},{14,12},{15,13},{18,16},{19,... | collective-permute-start | bytes 393224 | tf_op jit(solution)/shard_map/ppermute | solution.py:53
  55.6 1.3 %collective-permute-start.21 = (bf16[256,256]{1,0:T(8,128)(2,1)S(1)}, bf16[256,256]{1,0:T(8,128)(2,1)S(1)}, u32[]{:S(2)}, u32[]{:S(2)}) collective-permute-start(bf16[256,256]{1,0:T(8,128)(2,1)S(1)} %get-tuple-element.83), channel_id=1, source_target_pairs={{1,0},{2,1},{3,2},{5,4},{6,5},{7,6},{9,8},{10,9},{11,10},{13,12},{... | collective-permute-start | bytes 393224 | tf_op jit(solution)/shard_map/ppermute | solution.py:53
  56.9 3.2 %collective-permute-start.24 = (bf16[256,512]{1,0:T(8,128)(2,1)S(1)}, bf16[256,512]{1,0:T(8,128)(2,1)S(1)}, u32[]{:S(2)}, u32[]{:S(2)}) collective-permute-start(bf16[256,512]{1,0:T(8,128)(2,1)S(1)} %get-tuple-element.64.dquery_ref.refs_6_), channel_id=1, source_target_pairs={{0,1},{1,0},{2,3},{3,2},{4,5},{5,4},{6,7},{7,6},{8,9},{9,8},{10,11... | collective-permute-start | bytes 786440 | tf_op jit(solution)/shard_map/ppermute | solution.py:28
  60.1 1.1 %collective-permute-done.22 = bf16[256,256]{1,0:T(8,128)(2,1)S(1)} collective-permute-done((bf16[256,256]{1,0:T(8,128)(2,1)S(1)}, bf16[256,256]{1,0:T(8,128)(2,1)S(1)}, u32[]{:S(2)}, u32[]{:S(2)}) %collective-permute-start.22) | collective-permute-done | bytes 131104 | tf_op jit(solution)/shard_map/ppermute | solution.py:53
  61.2 2.0 %collective-permute-done.21 = bf16[256,256]{1,0:T(8,128)(2,1)S(1)} collective-permute-done((bf16[256,256]{1,0:T(8,128)(2,1)S(1)}, bf16[256,256]{1,0:T(8,128)(2,1)S(1)}, u32[]{:S(2)}, u32[]{:S(2)}) %collective-permute-start.21) | collective-permute-done | bytes 131104 | tf_op jit(solution)/shard_map/ppermute | solution.py:53
  63.2 2.8 %collective-permute-start.25 = (bf16[256,256]{1,0:T(8,128)(2,1)S(1)}, bf16[256,256]{1,0:T(8,128)(2,1)S(1)}, u32[]{:S(2)}, u32[]{:S(2)}) collective-permute-start(bf16[256,256]{1,0:T(8,128)(2,1)S(1)} %add_convert_fusion.3.dpair_ref.refs_7_.refs_14_), channel_id=1, source_target_pairs={{0,1},{1,0},{2,3},{3,2},{4,5},{5,4},{6,7},{7,6},{8,9},{9,8},{10,11... | collective-permute-start | bytes 393224 | tf_op jit(solution)/shard_map/ppermute | solution.py:28
  66.0 0.7 collective-permute-done.24.dquery_ref.refs_8_
  66.7 2.2 %collective-permute-done.25.dpair_ref.refs_9_ = bf16[256,256]{1,0:T(8,128)(2,1)S(1)} collective-permute-done((bf16[256,256]{1,0:T(8,128)(2,1)S(1)}, bf16[256,256]{1,0:T(8,128)(2,1)S(1)}, u32[]{:S(2)}, u32[]{:S(2)}) %collective-permute-start.25) | collective-permute-done | bytes 131104 | tf_op jit(solution)/shard_map/ppermute | solution.py:28
  68.9 0.5 collective-permute-start.33
  69.5 0.8 collective-permute-done.31.refs_11_
  70.5 0.6 weight_terms.2
  71.1 2.3 %collective-permute-start.34 = (bf16[128,768]{1,0:T(8,128)(2,1)S(1)}, bf16[128,768]{1,0:T(8,128)(2,1)S(1)}, u32[]{:S(2)}, u32[]{:S(2)}) collective-permute-start(bf16[128,768]{1,0:T(8,128)(2,1)S(1)} %get-tuple-element.69), channel_id=1, source_target_pairs={{0,2},{1,3},{2,0},{3,1},{4,6},{5,7},{6,4},{7,5},{8,10},{9,11},{10,... | collective-permute-start | bytes 589832 | tf_op jit(solution)/shard_map/ppermute | solution.py:35
  73.4 0.8 width_grad.3
  74.2 1.0 collective-permute-start.26
  75.2 1.5 %weight_terms.3 = (f32[128,768]{1,0:T(8,128)S(1)}, bf16[128,768]{1,0:T(8,128)(2,1)S(1)}, f32[128,768]{1,0:T(8,128)S(1)}, bf16[128,768]{1,0:T(8,128)(2,1)S(1)}, f...) custom-call(bf16[256,1024]{1,0:T(8,128)(2,1)S(1)} %copy-done, ...), custom_call_target="tpu_custom_call" | custom-call | tf_op jit(solution)/shard_map/weight_terms/pallas_call | solution.py:248
  76.7 1.0 collective-permute-start.36
  77.6 1.1 %collective-permute-start.38 = (bf16[128,768]{1,0:T(8,128)(2,1)S(1)}, bf16[128,768]{1,0:T(8,128)(2,1)S(1)}, u32[]{:S(2)}, u32[]{:S(2)}) collective-permute-start(bf16[128,768]{1,0:T(8,128)(2,1)S(1)} %get-tuple-element.74), channel_id=1, source_target_pairs={{0,2},{1,3},{2,0},{3,1},{4,6},{5,7},{6,4},{7,5},{8,10},{9,11},{10,... | collective-permute-start | bytes 589832 | tf_op jit(solution)/shard_map/ppermute | solution.py:35
  78.7 0.9 collective-permute-start.40
  79.7 3.1 %collective-permute-start.35 = (bf16[128,768]{1,0:T(8,128)(2,1)S(1)}, bf16[128,768]{1,0:T(8,128)(2,1)S(1)}, u32[]{:S(2)}, u32[]{:S(2)}) collective-permute-start(bf16[128,768]{1,0:T(8,128)(2,1)S(1)} %add_convert_fusion.2), channel_id=1, source_target_pairs={{0,16},{4,20},{8,24},{12,28},{16,0},{20,4},{24,8},{28,12},{1,17},{... | collective-permute-start | bytes 589832 | tf_op jit(solution)/shard_map/ppermute | solution.py:47
  82.8 1.7 %collective-permute-done.36 = bf16[128,768]{1,0:T(8,128)(2,1)S(1)} collective-permute-done((bf16[128,768]{1,0:T(8,128)(2,1)S(1)}, bf16[128,768]{1,0:T(8,128)(2,1)S(1)}, u32[]{:S(2)}, u32[]{:S(2)}) %collective-permute-start.36) | collective-permute-done | bytes 196640 | tf_op jit(solution)/shard_map/ppermute | solution.py:35
  84.6 3.8 %collective-permute-start.37 = (bf16[128,768]{1,0:T(8,128)(2,1)S(1)}, bf16[128,768]{1,0:T(8,128)(2,1)S(1)}, u32[]{:S(2)}, u32[]{:S(2)}) collective-permute-start(bf16[128,768]{1,0:T(8,128)(2,1)S(1)} %add_convert_fusion.1), channel_id=1, source_target_pairs={{0,24},{4,28},{8,0},{12,4},{16,8},{20,12},{24,16},{28,20},{1,25},{... | collective-permute-start | bytes 589832 | tf_op jit(solution)/shard_map/ppermute | solution.py:47
  88.8 3.9 %collective-permute-start.39 = (bf16[128,768]{1,0:T(8,128)(2,1)S(1)}, bf16[128,768]{1,0:T(8,128)(2,1)S(1)}, u32[]{:S(2)}, u32[]{:S(2)}) collective-permute-start(bf16[128,768]{1,0:T(8,128)(2,1)S(1)} %add_convert_fusion), channel_id=1, source_target_pairs={{0,8},{4,12},{8,16},{12,20},{16,24},{20,28},{24,0},{28,4},{1,9},{5... | collective-permute-start | bytes 589832 | tf_op jit(solution)/shard_map/ppermute | solution.py:47
  92.7 1.6 %width_grad.2 = (bf16[256,2048]{1,0:T(8,128)(2,1)S(1)}, bf16[256,512]{1,0:T(8,128)(2,1)S(1)}, bf16[16,128]{1,0:T(8,128)(2,1)}) custom-call(bf16[256,512]{1,0:T(8,128)(2,1)S(1)} %get-tuple-element.64.dquery_ref.refs_6_, bf16[256,256]{1,0:T(8,128)(2,1)S(1)} %add_convert_fusion.3.dpair_ref.refs_7_.refs_14_, ...), custom_call_target="tpu_custom_call" | custom-call | tf_op jit(solution)/shard_map/width_grad/pallas_call | solution.py:209
  94.3 4.0 %collective-permute-done.39.refs_5_ = bf16[128,768]{1,0:T(8,128)(2,1)S(1)} collective-permute-done((bf16[128,768]{1,0:T(8,128)(2,1)S(1)}, bf16[128,768]{1,0:T(8,128)(2,1)S(1)}, u32[]{:S(2)}, u32[]{:S(2)}) %collective-permute-start.39) | collective-permute-done | bytes 196640 | tf_op jit(solution)/shard_map/ppermute | solution.py:47
  98.3 1.7 %finish.1 = (bf16[256,4096]{1,0:T(8,128)(2,1)}, f32[128,768]{1,0:T(8,128)}) custom-call(bf16[256,2048]{1,0:T(8,128)(2,1)S(1)} %get-tuple-element.62.refs_0_, bf16[256,1536]{1,0:T(8,128)(2,1)S(1)} %collective-permute-done.26.refs_1_, bf16[256,512]{1,0:T(8,128)(2,1)S(1)} %get-tuple-element.66.refs_2_, bf16[128,768]{1,0:T(8,128)(2,1)S(1)} %collective-permute-done.35.refs_3_, ...), custom_call_target="tpu_custom_call" | custom-call | tf_op jit(solution)/shard_map/finish/pallas_call | solution.py:145
  (72 shorter events, 3.6 us)
Async XLA Ops:
  0.6 32.2 %copy-start.4 = (bf16[512,768]{1,0:T(8,128)(2,1)S(1)}, bf16[512,768]{1,0:T(8,128)(2,1)}, u32[]{:S(2)}) copy-start(bf16[512,768]{1,0:T(8,128)(2,1)} %param.6) | copy-start | bytes 2359300
  0.6 21.0 %copy-start.3 = (s32[1,8]{1,0:T(1,128)S(1)}, s32[1,8]{1,0:T(1,128)}, u32[]{:S(2)}) copy-start(s32[1,8]{1,0:T(1,128)} %param.8) | copy-start | bytes 100
  0.7 32.1 %copy-start.6 = (s32[1,8]{1,0:T(1,128)S(1)}, s32[1,8]{1,0:T(1,128)}, u32[]{:S(2)}) copy-start(s32[1,8]{1,0:T(1,128)} %param.9) | copy-start | bytes 100
  1.7 10.0 %collective-permute-start.1 = (bf16[128,768]{1,0:T(8,128)(2,1)S(1)}, bf16[128,768]{1,0:T(8,128)(2,1)S(1)}, u32[]{:S(2)}, u32[]{:S(2)}) collective-permute-start(bf16[128,768]{1,0:T(8,128)(2,1)S(1)} %constant_dynamic-slice_fusion), channel_id=1, source_target_pairs={{0,8},{4,12},{8,16},{12,20},{16,24},{20,28},{24,0},{28,4},{1,9},{5... | collective-permute-start | bytes 589832 | tf_op jit(solution)/shard_map/ppermute | solution.py:47
  11.7 20.5 %collective-permute-start.6 = (bf16[256,1536]{1,0:T(8,128)(2,1)}, bf16[256,1536]{1,0:T(8,128)(2,1)S(1)}, u32[]{:S(2)}, u32[]{:S(2)}) collective-permute-start(bf16[256,1536]{1,0:T(8,128)(2,1)} %get-tuple-element.51), channel_id=1, source_target_pairs={{0,1},{1,0},{2,3},{3,2},{4,5},{5,4},{6,7},{7,6},{8,9},{9,8},{10,11... | collective-permute-start | bytes 2359304 | tf_op jit(solution)/shard_map/ppermute | solution.py:28
  13.2 6.9 %collective-permute-start.3 = (bf16[128,768]{1,0:T(8,128)(2,1)S(1)}, bf16[128,768]{1,0:T(8,128)(2,1)S(1)}, u32[]{:S(2)}, u32[]{:S(2)}) collective-permute-start(bf16[128,768]{1,0:T(8,128)(2,1)S(1)} %constant_dynamic-slice_fusion), channel_id=1, source_target_pairs={{0,24},{4,28},{8,0},{12,4},{16,8},{20,12},{24,16},{28,20},{1,25},{... | collective-permute-start | bytes 589832 | tf_op jit(solution)/shard_map/ppermute | solution.py:47
  14.9 11.5 %collective-permute-start = (bf16[128,768]{1,0:T(8,128)(2,1)S(1)}, bf16[128,768]{1,0:T(8,128)(2,1)S(1)}, u32[]{:S(2)}, u32[]{:S(2)}) collective-permute-start(bf16[128,768]{1,0:T(8,128)(2,1)S(1)} %constant_dynamic-slice_fusion), channel_id=1, source_target_pairs={{0,16},{4,20},{8,24},{12,28},{16,0},{20,4},{24,8},{28,12},{1,17},{... | collective-permute-start | bytes 589832 | tf_op jit(solution)/shard_map/ppermute | solution.py:47
  14.9 11.5 %collective-permute-start.2 = (bf16[128,768]{1,0:T(8,128)(2,1)S(1)}, bf16[128,768]{1,0:T(8,128)(2,1)S(1)}, u32[]{:S(2)}, u32[]{:S(2)}) collective-permute-start(bf16[128,768]{1,0:T(8,128)(2,1)S(1)} %collective-permute-done.1.refs_5_.refs_1_.refs_2_.refs_0_), channel_id=1, source_target_pairs={{0,2},{1,3},{2,0},{3,1},{4,6},{5,7},{6,4},{7,5},{8,10},{9,11},{10,... | collective-permute-start | bytes 589832 | tf_op jit(solution)/shard_map/ppermute | solution.py:35
  20.1 6.4 %collective-permute-start.4 = (bf16[128,768]{1,0:T(8,128)(2,1)S(1)}, bf16[128,768]{1,0:T(8,128)(2,1)S(1)}, u32[]{:S(2)}, u32[]{:S(2)}) collective-permute-start(bf16[128,768]{1,0:T(8,128)(2,1)S(1)} %collective-permute-done.3.refs_9_.refs_5_.refs_6_.refs_4_), channel_id=1, source_target_pairs={{0,2},{1,3},{2,0},{3,1},{4,6},{5,7},{6,4},{7,5},{8,10},{9,11},{10,... | collective-permute-start | bytes 589832 | tf_op jit(solution)/shard_map/ppermute | solution.py:35
  26.4 5.7 %collective-permute-start.5 = (bf16[128,768]{1,0:T(8,128)(2,1)S(1)}, bf16[128,768]{1,0:T(8,128)(2,1)S(1)}, u32[]{:S(2)}, u32[]{:S(2)}) collective-permute-start(bf16[128,768]{1,0:T(8,128)(2,1)S(1)} %collective-permute-done.refs_7_.refs_3_.refs_4_.refs_2_), channel_id=1, source_target_pairs={{0,2},{1,3},{2,0},{3,1},{4,6},{5,7},{6,4},{7,5},{8,10},{9,11},{10,... | collective-permute-start | bytes 589832 | tf_op jit(solution)/shard_map/ppermute | solution.py:35
  28.0 4.7 %collective-permute-start.9 = (bf16[128,768]{1,0:T(8,128)(2,1)S(1)}, bf16[128,768]{1,0:T(8,128)(2,1)S(1)}, u32[]{:S(2)}, u32[]{:S(2)}) collective-permute-start(bf16[128,768]{1,0:T(8,128)(2,1)S(1)} %collective-permute-done.1.refs_5_.refs_1_.refs_2_.refs_0_), channel_id=1, source_target_pairs={{0,4},{4,0},{8,12},{12,8},{16,20},{20,16},{24,28},{28,24},{1,5},{5... | collective-permute-start | bytes 589832 | tf_op jit(solution)/shard_map/ppermute | solution.py:40
  28.0 5.4 %collective-permute-start.11 = (bf16[128,768]{1,0:T(8,128)(2,1)S(1)}, bf16[128,768]{1,0:T(8,128)(2,1)S(1)}, u32[]{:S(2)}, u32[]{:S(2)}) collective-permute-start(bf16[128,768]{1,0:T(8,128)(2,1)S(1)} %collective-permute-done.refs_7_.refs_3_.refs_4_.refs_2_), channel_id=1, source_target_pairs={{0,4},{4,0},{8,12},{12,8},{16,20},{20,16},{24,28},{28,24},{1,5},{5... | collective-permute-start | bytes 589832 | tf_op jit(solution)/shard_map/ppermute | solution.py:40
  28.5 4.4 %collective-permute-start.10 = (bf16[128,768]{1,0:T(8,128)(2,1)S(1)}, bf16[128,768]{1,0:T(8,128)(2,1)S(1)}, u32[]{:S(2)}, u32[]{:S(2)}) collective-permute-start(bf16[128,768]{1,0:T(8,128)(2,1)S(1)} %collective-permute-done.2.refs_6_.refs_2_.refs_3_.refs_1_), channel_id=1, source_target_pairs={{0,4},{4,0},{8,12},{12,8},{16,20},{20,16},{24,28},{28,24},{1,5},{5... | collective-permute-start | bytes 589832 | tf_op jit(solution)/shard_map/ppermute | solution.py:40
  32.1 1.4 %collective-permute-start.13 = (bf16[128,768]{1,0:T(8,128)(2,1)S(1)}, bf16[128,768]{1,0:T(8,128)(2,1)S(1)}, u32[]{:S(2)}, u32[]{:S(2)}) collective-permute-start(bf16[128,768]{1,0:T(8,128)(2,1)S(1)} %collective-permute-done.3.refs_9_.refs_5_.refs_6_.refs_4_), channel_id=1, source_target_pairs={{0,4},{4,0},{8,12},{12,8},{16,20},{20,16},{24,28},{28,24},{1,5},{5... | collective-permute-start | bytes 589832 | tf_op jit(solution)/shard_map/ppermute | solution.py:40
  32.1 1.8 %collective-permute-start.14 = (bf16[128,768]{1,0:T(8,128)(2,1)S(1)}, bf16[128,768]{1,0:T(8,128)(2,1)S(1)}, u32[]{:S(2)}, u32[]{:S(2)}) collective-permute-start(bf16[128,768]{1,0:T(8,128)(2,1)S(1)} %collective-permute-done.4.refs_10_.refs_6_.refs_7_.refs_5_), channel_id=1, source_target_pairs={{0,4},{4,0},{8,12},{12,8},{16,20},{20,16},{24,28},{28,24},{1,5},{5... | collective-permute-start | bytes 589832 | tf_op jit(solution)/shard_map/ppermute | solution.py:40
  32.7 1.5 %collective-permute-start.12 = (bf16[128,768]{1,0:T(8,128)(2,1)S(1)}, bf16[128,768]{1,0:T(8,128)(2,1)S(1)}, u32[]{:S(2)}, u32[]{:S(2)}) collective-permute-start(bf16[128,768]{1,0:T(8,128)(2,1)S(1)} %collective-permute-done.5.refs_8_.refs_4_.refs_5_.refs_3_), channel_id=1, source_target_pairs={{0,4},{4,0},{8,12},{12,8},{16,20},{20,16},{24,28},{28,24},{1,5},{5... | collective-permute-start | bytes 589832 | tf_op jit(solution)/shard_map/ppermute | solution.py:40
  32.9 2.9 %collective-permute-start.7 = (bf16[128,768]{1,0:T(8,128)(2,1)S(1)}, bf16[128,768]{1,0:T(8,128)(2,1)S(1)}, u32[]{:S(2)}, u32[]{:S(2)}) collective-permute-start(bf16[128,768]{1,0:T(8,128)(2,1)S(1)} %get-tuple-element.82.refs_3_.refs_0_), channel_id=1, source_target_pairs={{0,4},{4,0},{8,12},{12,8},{16,20},{20,16},{24,28},{28,24},{1,5},{5... | collective-permute-start | bytes 589832 | tf_op jit(solution)/shard_map/ppermute | solution.py:40
  33.4 2.5 %collective-permute-start.8 = (bf16[128,768]{1,0:T(8,128)(2,1)S(1)}, bf16[128,768]{1,0:T(8,128)(2,1)S(1)}, u32[]{:S(2)}, u32[]{:S(2)}) collective-permute-start(bf16[128,768]{1,0:T(8,128)(2,1)S(1)} %get-tuple-element.81.refs_4_.refs_1_), channel_id=1, source_target_pairs={{0,4},{4,0},{8,12},{12,8},{16,20},{20,16},{24,28},{28,24},{1,5},{5... | collective-permute-start | bytes 589832 | tf_op jit(solution)/shard_map/ppermute | solution.py:40
  33.6 3.8 %collective-permute-start.15 = (bf16[128,768]{1,0:T(8,128)(2,1)S(1)}, bf16[128,768]{1,0:T(8,128)(2,1)S(1)}, u32[]{:S(2)}, u32[]{:S(2)}) collective-permute-start(bf16[128,768]{1,0:T(8,128)(2,1)S(1)} %get-tuple-element.80.refs_19_.refs_16_), channel_id=1, source_target_pairs={{0,4},{4,0},{8,12},{12,8},{16,20},{20,16},{24,28},{28,24},{1,5},{5... | collective-permute-start | bytes 589832 | tf_op jit(solution)/shard_map/ppermute | solution.py:40
  33.9 3.5 %collective-permute-start.16 = (bf16[128,768]{1,0:T(8,128)(2,1)S(1)}, bf16[128,768]{1,0:T(8,128)(2,1)S(1)}, u32[]{:S(2)}, u32[]{:S(2)}) collective-permute-start(bf16[128,768]{1,0:T(8,128)(2,1)S(1)} %get-tuple-element.79.refs_20_.refs_17_), channel_id=1, source_target_pairs={{0,4},{4,0},{8,12},{12,8},{16,20},{20,16},{24,28},{28,24},{1,5},{5... | collective-permute-start | bytes 589832 | tf_op jit(solution)/shard_map/ppermute | solution.py:40
  34.5 1.2 %copy-start.1 = (bf16[256,1024]{1,0:T(8,128)(2,1)S(1)}, bf16[256,1024]{1,0:T(8,128)(2,1)}, u32[]{:S(2)}) copy-start(bf16[256,1024]{1,0:T(8,128)(2,1)} %get-tuple-element.42.refs_1_) | copy-start | bytes 1572868
  34.5 2.9 %copy-start = (bf16[256,1024]{1,0:T(8,128)(2,1)S(1)}, bf16[256,1024]{1,0:T(8,128)(2,1)}, u32[]{:S(2)}) copy-start(bf16[256,1024]{1,0:T(8,128)(2,1)} %get-tuple-element.41.refs_0_) | copy-start | bytes 1572868
  34.5 2.9 %copy-start.2 = (bf16[256,512]{1,0:T(8,128)(2,1)S(1)}, bf16[256,512]{1,0:T(8,128)(2,1)}, u32[]{:S(2)}) copy-start(bf16[256,512]{1,0:T(8,128)(2,1)} %get-tuple-element.63.refs_2_) | copy-start | bytes 786436
  34.6 6.4 %collective-permute-start.18 = (bf16[256,256]{1,0:T(8,128)(2,1)S(1)}, bf16[256,256]{1,0:T(8,128)(2,1)S(1)}, u32[]{:S(2)}, u32[]{:S(2)}) collective-permute-start(bf16[256,256]{1,0:T(8,128)(2,1)S(1)} %project.5), channel_id=1, source_target_pairs={{0,1},{1,0},{2,3},{3,2},{4,5},{5,4},{6,7},{7,6},{8,9},{9,8},{10,11... | collective-permute-start | bytes 393224 | tf_op jit(solution)/shard_map/ppermute | solution.py:28
  35.8 30.2 %collective-permute-start.27 = (bf16[256,1024]{1,0:T(8,128)(2,1)S(1)}, bf16[256,1024]{1,0:T(8,128)(2,1)S(1)}, u32[]{:S(2)}, u32[]{:S(2)}) collective-permute-start(bf16[256,1024]{1,0:T(8,128)(2,1)S(1)} %copy-done.1), channel_id=1, source_target_pairs={{0,4},{4,0},{8,12},{12,8},{16,20},{20,16},{24,28},{28,24},{1,5},{5... | collective-permute-start | bytes 1572872 | tf_op jit(solution)/shard_map/ppermute | solution.py:40
  35.9 14.3 %collective-permute-start.17 = (bf16[256,512]{1,0:T(8,128)(2,1)S(1)}, bf16[256,512]{1,0:T(8,128)(2,1)S(1)}, u32[]{:S(2)}, u32[]{:S(2)}) collective-permute-start(bf16[256,512]{1,0:T(8,128)(2,1)S(1)} %project.4), channel_id=1, source_target_pairs={{0,1},{1,0},{2,3},{3,2},{4,5},{5,4},{6,7},{7,6},{8,9},{9,8},{10,11... | collective-permute-start | bytes 786440 | tf_op jit(solution)/shard_map/ppermute | solution.py:28
  37.4 9.2 %copy-start.5 = (bf16[1,256,512]{2,1,0:T(8,128)(2,1)S(1)}, bf16[1,256,512]{2,1,0:T(8,128)(2,1)}, u32[]{:S(2)}) copy-start(bf16[1,256,512]{2,1,0:T(8,128)(2,1)} %param.7) | copy-start | bytes 786436
  41.0 8.7 %collective-permute-start.19 = (bf16[256,256]{1,0:T(8,128)(2,1)S(1)}, bf16[256,256]{1,0:T(8,128)(2,1)S(1)}, u32[]{:S(2)}, u32[]{:S(2)}) collective-permute-start(bf16[256,256]{1,0:T(8,128)(2,1)S(1)} %add_convert_fusion.4.refs_2_), channel_id=1, source_target_pairs={{0,2},{1,3},{4,6},{5,7},{8,10},{9,11},{12,14},{13,15},{16,18},{17,... | collective-permute-start | bytes 393224 | tf_op jit(solution)/shard_map/ppermute | solution.py:53
  44.4 5.8 %collective-permute-start.20 = (bf16[256,256]{1,0:T(8,128)(2,1)S(1)}, bf16[256,256]{1,0:T(8,128)(2,1)S(1)}, u32[]{:S(2)}, u32[]{:S(2)}) collective-permute-start(bf16[256,256]{1,0:T(8,128)(2,1)S(1)} %add_convert_fusion.4.refs_2_), channel_id=1, source_target_pairs={{0,1},{1,2},{2,3},{4,5},{5,6},{6,7},{8,9},{9,10},{10,11},{12,13},{... | collective-permute-start | bytes 393224 | tf_op jit(solution)/shard_map/ppermute | solution.py:53
  46.7 23.6 %collective-permute-start.28 = (bf16[256,1536]{1,0:T(8,128)(2,1)S(1)}, bf16[256,1536]{1,0:T(8,128)(2,1)S(1)}, u32[]{:S(2)}, u32[]{:S(2)}) collective-permute-start(bf16[256,1536]{1,0:T(8,128)(2,1)S(1)} %collective-permute-done.6.refs_0_.refs_1_), channel_id=1, source_target_pairs={{0,4},{4,0},{8,12},{12,8},{16,20},{20,16},{24,28},{28,24},{1,5},{5... | collective-permute-start | bytes 2359304 | tf_op jit(solution)/shard_map/ppermute | solution.py:40
  49.7 7.2 %collective-permute-start.23 = (bf16[256,512]{1,0:T(8,128)(2,1)S(1)}, bf16[256,512]{1,0:T(8,128)(2,1)S(1)}, u32[]{:S(2)}, u32[]{:S(2)}) collective-permute-start(bf16[256,512]{1,0:T(8,128)(2,1)S(1)} %copy-done.2), channel_id=1, source_target_pairs={{0,1},{1,0},{2,3},{3,2},{4,5},{5,4},{6,7},{7,6},{8,9},{9,8},{10,11... | collective-permute-start | bytes 786440 | tf_op jit(solution)/shard_map/ppermute | solution.py:28
  54.3 6.9 %collective-permute-start.22 = (bf16[256,256]{1,0:T(8,128)(2,1)S(1)}, bf16[256,256]{1,0:T(8,128)(2,1)S(1)}, u32[]{:S(2)}, u32[]{:S(2)}) collective-permute-start(bf16[256,256]{1,0:T(8,128)(2,1)S(1)} %get-tuple-element.84), channel_id=1, source_target_pairs={{2,0},{3,1},{6,4},{7,5},{10,8},{11,9},{14,12},{15,13},{18,16},{19,... | collective-permute-start | bytes 393224 | tf_op jit(solution)/shard_map/ppermute | solution.py:53
  55.6 7.5 %collective-permute-start.21 = (bf16[256,256]{1,0:T(8,128)(2,1)S(1)}, bf16[256,256]{1,0:T(8,128)(2,1)S(1)}, u32[]{:S(2)}, u32[]{:S(2)}) collective-permute-start(bf16[256,256]{1,0:T(8,128)(2,1)S(1)} %get-tuple-element.83), channel_id=1, source_target_pairs={{1,0},{2,1},{3,2},{5,4},{6,5},{7,6},{9,8},{10,9},{11,10},{13,12},{... | collective-permute-start | bytes 393224 | tf_op jit(solution)/shard_map/ppermute | solution.py:53
  56.9 9.8 %collective-permute-start.24 = (bf16[256,512]{1,0:T(8,128)(2,1)S(1)}, bf16[256,512]{1,0:T(8,128)(2,1)S(1)}, u32[]{:S(2)}, u32[]{:S(2)}) collective-permute-start(bf16[256,512]{1,0:T(8,128)(2,1)S(1)} %get-tuple-element.64.dquery_ref.refs_6_), channel_id=1, source_target_pairs={{0,1},{1,0},{2,3},{3,2},{4,5},{5,4},{6,7},{7,6},{8,9},{9,8},{10,11... | collective-permute-start | bytes 786440 | tf_op jit(solution)/shard_map/ppermute | solution.py:28
  61.2 7.8 %collective-permute-start.30 = (bf16[256,512]{1,0:T(8,128)(2,1)S(1)}, bf16[256,512]{1,0:T(8,128)(2,1)S(1)}, u32[]{:S(2)}, u32[]{:S(2)}) collective-permute-start(bf16[256,512]{1,0:T(8,128)(2,1)S(1)} %get-tuple-element.64.dquery_ref.refs_6_), channel_id=1, source_target_pairs={{0,4},{4,0},{8,12},{12,8},{16,20},{20,16},{24,28},{28,24},{1,5},{5... | collective-permute-start | bytes 786440 | tf_op jit(solution)/shard_map/ppermute | solution.py:40
  63.2 5.7 %collective-permute-start.25 = (bf16[256,256]{1,0:T(8,128)(2,1)S(1)}, bf16[256,256]{1,0:T(8,128)(2,1)S(1)}, u32[]{:S(2)}, u32[]{:S(2)}) collective-permute-start(bf16[256,256]{1,0:T(8,128)(2,1)S(1)} %add_convert_fusion.3.dpair_ref.refs_7_.refs_14_), channel_id=1, source_target_pairs={{0,1},{1,0},{2,3},{3,2},{4,5},{5,4},{6,7},{7,6},{8,9},{9,8},{10,11... | collective-permute-start | bytes 393224 | tf_op jit(solution)/shard_map/ppermute | solution.py:28
  66.0 4.3 %collective-permute-start.29 = (bf16[256,512]{1,0:T(8,128)(2,1)S(1)}, bf16[256,512]{1,0:T(8,128)(2,1)S(1)}, u32[]{:S(2)}, u32[]{:S(2)}) collective-permute-start(bf16[256,512]{1,0:T(8,128)(2,1)S(1)} %collective-permute-done.23.refs_2_), channel_id=1, source_target_pairs={{0,4},{4,0},{8,12},{12,8},{16,20},{20,16},{24,28},{28,24},{1,5},{5... | collective-permute-start | bytes 786440 | tf_op jit(solution)/shard_map/ppermute | solution.py:40
  66.7 3.8 %collective-permute-start.32 = (bf16[256,512]{1,0:T(8,128)(2,1)S(1)}, bf16[256,512]{1,0:T(8,128)(2,1)S(1)}, u32[]{:S(2)}, u32[]{:S(2)}) collective-permute-start(bf16[256,512]{1,0:T(8,128)(2,1)S(1)} %collective-permute-done.24.dquery_ref.refs_8_), channel_id=1, source_target_pairs={{0,4},{4,0},{8,12},{12,8},{16,20},{20,16},{24,28},{28,24},{1,5},{5... | collective-permute-start | bytes 786440 | tf_op jit(solution)/shard_map/ppermute | solution.py:40
  68.9 1.3 %collective-permute-start.31 = (bf16[256,256]{1,0:T(8,128)(2,1)S(1)}, bf16[256,256]{1,0:T(8,128)(2,1)S(1)}, u32[]{:S(2)}, u32[]{:S(2)}) collective-permute-start(bf16[256,256]{1,0:T(8,128)(2,1)S(1)} %add_convert_fusion.3.dpair_ref.refs_7_.refs_14_), channel_id=1, source_target_pairs={{0,4},{4,0},{8,12},{12,8},{16,20},{20,16},{24,28},{28,24},{1,5},{5... | collective-permute-start | bytes 393224 | tf_op jit(solution)/shard_map/ppermute | solution.py:40
  68.9 1.5 %collective-permute-start.33 = (bf16[256,256]{1,0:T(8,128)(2,1)S(1)}, bf16[256,256]{1,0:T(8,128)(2,1)S(1)}, u32[]{:S(2)}, u32[]{:S(2)}) collective-permute-start(bf16[256,256]{1,0:T(8,128)(2,1)S(1)} %collective-permute-done.25.dpair_ref.refs_9_), channel_id=1, source_target_pairs={{0,4},{4,0},{8,12},{12,8},{16,20},{20,16},{24,28},{28,24},{1,5},{5... | collective-permute-start | bytes 393224 | tf_op jit(solution)/shard_map/ppermute | solution.py:40
  71.1 8.5 %collective-permute-start.34 = (bf16[128,768]{1,0:T(8,128)(2,1)S(1)}, bf16[128,768]{1,0:T(8,128)(2,1)S(1)}, u32[]{:S(2)}, u32[]{:S(2)}) collective-permute-start(bf16[128,768]{1,0:T(8,128)(2,1)S(1)} %get-tuple-element.69), channel_id=1, source_target_pairs={{0,2},{1,3},{2,0},{3,1},{4,6},{5,7},{6,4},{7,5},{8,10},{9,11},{10,... | collective-permute-start | bytes 589832 | tf_op jit(solution)/shard_map/ppermute | solution.py:35
  74.2 24.1 %collective-permute-start.26 = (bf16[256,1536]{1,0:T(8,128)(2,1)S(1)}, bf16[256,1536]{1,0:T(8,128)(2,1)S(1)}, u32[]{:S(2)}, u32[]{:S(2)}) collective-permute-start(bf16[256,1536]{1,0:T(8,128)(2,1)S(1)} %get-tuple-element.65), channel_id=1, source_target_pairs={{0,1},{1,0},{2,3},{3,2},{4,5},{5,4},{6,7},{7,6},{8,9},{9,8},{10,11... | collective-permute-start | bytes 2359304 | tf_op jit(solution)/shard_map/ppermute | solution.py:28
  76.7 7.9 %collective-permute-start.36 = (bf16[128,768]{1,0:T(8,128)(2,1)S(1)}, bf16[128,768]{1,0:T(8,128)(2,1)S(1)}, u32[]{:S(2)}, u32[]{:S(2)}) collective-permute-start(bf16[128,768]{1,0:T(8,128)(2,1)S(1)} %get-tuple-element.72), channel_id=1, source_target_pairs={{0,2},{1,3},{2,0},{3,1},{4,6},{5,7},{6,4},{7,5},{8,10},{9,11},{10,... | collective-permute-start | bytes 589832 | tf_op jit(solution)/shard_map/ppermute | solution.py:35
  77.6 11.1 %collective-permute-start.38 = (bf16[128,768]{1,0:T(8,128)(2,1)S(1)}, bf16[128,768]{1,0:T(8,128)(2,1)S(1)}, u32[]{:S(2)}, u32[]{:S(2)}) collective-permute-start(bf16[128,768]{1,0:T(8,128)(2,1)S(1)} %get-tuple-element.74), channel_id=1, source_target_pairs={{0,2},{1,3},{2,0},{3,1},{4,6},{5,7},{6,4},{7,5},{8,10},{9,11},{10,... | collective-permute-start | bytes 589832 | tf_op jit(solution)/shard_map/ppermute | solution.py:35
  78.7 15.6 %collective-permute-start.40 = (bf16[128,768]{1,0:T(8,128)(2,1)S(1)}, bf16[128,768]{1,0:T(8,128)(2,1)S(1)}, u32[]{:S(2)}, u32[]{:S(2)}) collective-permute-start(bf16[128,768]{1,0:T(8,128)(2,1)S(1)} %get-tuple-element.76), channel_id=1, source_target_pairs={{0,2},{1,3},{2,0},{3,1},{4,6},{5,7},{6,4},{7,5},{8,10},{9,11},{10,... | collective-permute-start | bytes 589832 | tf_op jit(solution)/shard_map/ppermute | solution.py:35
  79.7 14.6 %collective-permute-start.35 = (bf16[128,768]{1,0:T(8,128)(2,1)S(1)}, bf16[128,768]{1,0:T(8,128)(2,1)S(1)}, u32[]{:S(2)}, u32[]{:S(2)}) collective-permute-start(bf16[128,768]{1,0:T(8,128)(2,1)S(1)} %add_convert_fusion.2), channel_id=1, source_target_pairs={{0,16},{4,20},{8,24},{12,28},{16,0},{20,4},{24,8},{28,12},{1,17},{... | collective-permute-start | bytes 589832 | tf_op jit(solution)/shard_map/ppermute | solution.py:47
  84.6 9.7 %collective-permute-start.37 = (bf16[128,768]{1,0:T(8,128)(2,1)S(1)}, bf16[128,768]{1,0:T(8,128)(2,1)S(1)}, u32[]{:S(2)}, u32[]{:S(2)}) collective-permute-start(bf16[128,768]{1,0:T(8,128)(2,1)S(1)} %add_convert_fusion.1), channel_id=1, source_target_pairs={{0,24},{4,28},{8,0},{12,4},{16,8},{20,12},{24,16},{28,20},{1,25},{... | collective-permute-start | bytes 589832 | tf_op jit(solution)/shard_map/ppermute | solution.py:47
  88.8 9.5 %collective-permute-start.39 = (bf16[128,768]{1,0:T(8,128)(2,1)S(1)}, bf16[128,768]{1,0:T(8,128)(2,1)S(1)}, u32[]{:S(2)}, u32[]{:S(2)}) collective-permute-start(bf16[128,768]{1,0:T(8,128)(2,1)S(1)} %add_convert_fusion), channel_id=1, source_target_pairs={{0,8},{4,12},{8,16},{12,20},{16,24},{20,28},{24,0},{28,4},{1,9},{5... | collective-permute-start | bytes 589832 | tf_op jit(solution)/shard_map/ppermute | solution.py:47
